TPU v7x, 32 devices: a whole 2x2x4 slice. The times are simulated.
32 devices in a mesh: slab: 8 (over z, x), col: 4 (over y, core).
Axes of the slice: x: 2, y: 2, z: 4, core: 2. Of those that a mesh axis runs over, the one named last changes fastest.
Arguments:
- basis: bfloat16 [3, 64, 16, 32, 128], P(None, None, 'slab', 'col')
- cell_map: int32 [16, 32, 128], P('slab', 'col'), may hold values from 0 to 7
- table: float32 [8, 27], replicated, may hold values from 0 to 1, as said below
Outputs:
- next_block: bfloat16 [64, 16, 32, 128], P(None, 'slab', 'col')
- projections: float32 [2, 192, 64], replicated
- triangles: float32 [2, 64, 64], replicated
Inputs may be any that keep to these rules, and one draw needn't show every extreme that they name: `table`: coefficients lie between 0 and 1; the centre one is the largest.
All inputs are finite; a program needn't handle non-finite values.
Results may differ from a plain program's by a relative error of at most 0.027.
Values may be sent and summed in bfloat16 or wider, within the bound.
No kernel may reach another device: no remote copies, remote signals or barrier semaphores. Data moves between devices by JAX's collectives and lax.ppermute only.
A program may use at most 64 MiB of HBM per device.

v0:
```python
import jax
import jax.numpy as jnp
from jax import lax
from jax.sharding import PartitionSpec as P


def extended(block, sides, width):
    for axis, dim in sides:
        count = lax.axis_size(axis)
        forward = [(i, i + 1) for i in range(count - 1)]
        backward = [(target, source) for source, target in forward]
        low = lax.ppermute(
            lax.slice_in_dim(block, block.shape[dim] - width, None, axis=dim), axis, forward
        )
        high = lax.ppermute(lax.slice_in_dim(block, 0, width, axis=dim), axis, backward)
        block = jnp.concatenate([low, block, high], axis=dim)
    return block


def apply_stencil(wide, coef):
    depth = wide.shape[3]
    rows_x = wide.shape[1] - 2
    rows_y = wide.shape[2] - 2
    padded = jnp.pad(wide, ((0, 0), (0, 0), (0, 0), (1, 1)))
    total = jnp.zeros((wide.shape[0], rows_x, rows_y, depth), jnp.float32)
    for dx in range(3):
        for dy in range(3):
            for dz in range(3):
                offset = 9 * dx + 3 * dy + dz
                piece = padded[:, dx : dx + rows_x, dy : dy + rows_y, dz : dz + depth].astype(
                    jnp.float32
                )
                total = total + coef[offset][None] * piece
    return total.astype(jnp.bfloat16)


def with_faces(block, coef):
    wide = extended(block, (("slab", 1), ("col", 2)), 1)
    return apply_stencil(wide, coef)


def lookup(cell_map, table):
    classes = table.shape[0]
    onehot = (cell_map[None] == jnp.arange(classes, dtype=jnp.int32)[:, None, None, None]).astype(
        jnp.float32
    )
    return jnp.einsum("ko,kxyz->oxyz", table, onehot, precision=lax.Precision.HIGHEST)


def gram_of(left, right, scale):
    return (
        lax.dot_general(left, right, (((1,), (1,)), ((), ())), preferred_element_type=jnp.float32)
        * scale
    )


def correct(stack, block, coeffs):
    moved = lax.dot_general(
        coeffs.astype(jnp.bfloat16),
        stack,
        (((0,), (0,)), ((), ())),
        preferred_element_type=jnp.float32,
    )
    return (block.astype(jnp.float32) - moved).astype(jnp.bfloat16)


def inner_part(flat, shape_wide):
    lead, span_x, span_y, depth = shape_wide
    cube = flat.reshape(lead, span_x, span_y, depth)
    return cube.reshape(lead, -1)


def orthonormalize(stack_wide, block_wide, shape_wide, scale):
    stack = inner_part(stack_wide, (stack_wide.shape[0],) + shape_wide[1:])
    block_inner = inner_part(block_wide, shape_wide)
    first = lax.psum(gram_of(stack, block_inner, 1.0), ("slab", "col")) * scale
    one_wide = correct(stack_wide, block_wide, first)
    second = (
        lax.psum(gram_of(stack, inner_part(one_wide, shape_wide), 1.0), ("slab", "col")) * scale
    )
    two_wide = correct(stack_wide, one_wide, second)
    two_inner = inner_part(two_wide, shape_wide)
    square = lax.psum(gram_of(two_inner, two_inner, 1.0), ("slab", "col")) * scale
    lower = jnp.linalg.cholesky(square)
    identity = jnp.eye(lower.shape[0], dtype=lower.dtype)
    inverse = lax.linalg.triangular_solve(lower, identity, left_side=True, lower=True)
    result = jnp.dot(
        inverse.astype(jnp.bfloat16), two_wide, preferred_element_type=jnp.float32
    ).astype(jnp.bfloat16)
    return (result, first + second, lower, None)


def shards(basis, cell_map, table):
    count_x, count_y, depth = cell_map.shape
    columns = basis.shape[1]
    devices_x = lax.axis_size("slab")
    devices_y = lax.axis_size("col")
    scale = 1.0 / (count_x * devices_x * count_y * devices_y * depth)
    coef = lookup(cell_map, table)
    flat = basis.reshape(3 * columns, count_x * count_y * depth)
    shape_inner = (columns, count_x, count_y, depth)
    image_first = with_faces(basis[2], coef)
    block_one, proj_one, lower_one, gram_one = orthonormalize(
        flat, image_first.reshape(columns, -1), shape_inner, scale
    )
    image = with_faces(block_one.reshape(shape_inner), coef)
    stack = jnp.concatenate([flat[columns:], block_one], axis=0)
    block_two, proj_two, lower_two, gram_two = orthonormalize(
        stack, image.reshape(columns, -1), shape_inner, scale
    )
    return (
        block_two.reshape(shape_inner),
        jnp.stack([proj_one, proj_two]),
        jnp.stack([lower_one, lower_two]),
    )


def solution(mesh):
    placed = (P(None, None, "slab", "col", None), P("slab", "col", None), P())
    return jax.shard_map(
        shards,
        mesh=mesh,
        in_specs=placed,
        out_specs=(P(None, "slab", "col", None), P(), P()),
        check_vma=False,
    )
```

profile of v0, /device:TPU:0, one launch (start us, length us, event | category | flops | bytes accessed | tf_op | source)
XLA Modules:
  0.0 326.8 jit_solution(6078061634676776645)
XLA Ops:
  0.6 0.0 copy-start
  0.6 0.0 copy-start.1
  0.7 1.0 slice_bitcast_fusion
  1.7 4.8 %collective-permute-start = (bf16[64,1,8,128]{3,2,1,0:T(8,128)(2,1)S(1)}, bf16[64,1,8,128]{3,2,1,0:T(8,128)(2,1)S(1)}, u32[]{:S(2)}, u32[]{:S(2)}) collective-permute-start(bf16[64,1,8,128]{3,2,1,0:T(8,128)(2,1)S(1)} %get-tuple-element.38), channel_id=1, source_target_pairs={{0,4},{4,8},{8,12},{12,16},{16,20},{20,24},{24,28},{1,5},{5,9},{9,... | collective-permute-start | bytes 393224 | tf_op jit(solution)/shard_map/ppermute | solution.py:12
  6.6 1.3 collective-permute-start.1
  7.9 0.0 copy-done
  7.9 1.0 convolution_bitcast_fusion
  8.9 0.1 fusion.47
  9.0 0.3 collective-permute-done
  9.3 4.1 %collective-permute-done.1 = bf16[64,1,8,128]{3,2,1,0:T(8,128)(2,1)S(1)} collective-permute-done((bf16[64,1,8,128]{3,2,1,0:T(8,128)(2,1)S(1)}, bf16[64,1,8,128]{3,2,1,0:T(8,128)(2,1)S(1)}, u32[]{:S(2)}, u32[]{:S(2)}) %collective-permute-start.1) | collective-permute-done | bytes 131104 | tf_op jit(solution)/shard_map/ppermute | solution.py:15
  13.4 0.2 pad_maximum_fusion.15
  13.6 1.3 collective-permute-start.2
  15.0 1.3 collective-permute-start.3
  16.3 0.3 reshape_reshape_reshape.2
  16.7 0.0 collective-permute-done.2
  16.7 3.3 %collective-permute-done.3 = bf16[64,4,1,128]{3,2,1,0:T(2,128)(2,1)S(1)} collective-permute-done((bf16[64,4,1,128]{3,2,1,0:T(2,128)(2,1)S(1)}, bf16[64,4,1,128]{3,2,1,0:T(2,128)(2,1)S(1)}, u32[]{:S(2)}, u32[]{:S(2)}) %collective-permute-start.3) | collective-permute-done | bytes 65568 | tf_op jit(solution)/shard_map/ppermute | solution.py:15
  19.9 2.8 fusion.11
  22.7 3.4 %add_convert_fusion.1 = bf16[64,2,8,128]{3,2,1,0:T(8,128)(2,1)S(1)} fusion(bf16[64,2,8,128]{3,2,1,0:T(8,128)(2,1)S(1)} %slice_bitcast_fusion, bf16[64,4,10,130]{3,2,1,0:T(8,128)(2,1)S(1)} %fusion.11, bf16[64,4,1,128]{3,2,1,0:T(2,128)(2,1)S(1)} %collective-permute-done.3, bf16[64,1,8,128]{3,2,1,0:T(8,128)(2,1)S(1)} %collective-permute-done.1, ...), kind=kLoop, calls=%fused_computation.32 | loop fusion | flops 16908288 | bytes 5857280 | tf_op jit(solution)/shard_map/convert_element_type | solution.py:34
  26.1 0.4 convolution_bitcast_fusion.2
  26.4 43.8 %psum.42 = f32[192,64]{0,1:T(8,128)S(1)} all-reduce(f32[192,64]{0,1:T(8,128)S(1)} %convolution_bitcast_fusion.2), channel_id=1, replica_groups=mesh['slab'=8,'col'=4] {'slab','col'}, use_global_device_ids=true, to_apply=%region_0.1 | all-reduce | flops 12288 | bytes 98304 | tf_op jit(solution)/shard_map/psum | solution.py:76
  70.2 0.3 fusion.1
  70.5 0.4 convolution_bitcast_fusion.1
  70.9 40.0 %psum.43 = f32[192,64]{0,1:T(8,128)S(1)} all-reduce(f32[192,64]{0,1:T(8,128)S(1)} %convolution_bitcast_fusion.1), channel_id=1, replica_groups=mesh['slab'=8,'col'=4] {'slab','col'}, use_global_device_ids=true, to_apply=%region_1.2 | all-reduce | flops 12288 | bytes 98304 | tf_op jit(solution)/shard_map/psum | solution.py:79
  110.9 0.3 fusion.2
  111.2 0.0 slice-start
  111.2 0.2 fusion.50
  111.4 40.4 %psum.44 = f32[64,64]{0,1:T(8,128)S(1)} all-reduce(f32[64,64]{0,1:T(8,128)S(1)} %fusion.50), channel_id=1, replica_groups=mesh['slab'=8,'col'=4] {'slab','col'}, use_global_device_ids=true, to_apply=%region_2.3 | all-reduce | flops 4096 | bytes 32768 | tf_op jit(solution)/shard_map/psum | solution.py:83
  151.8 0.1 copy.7
  151.9 5.8 %cholesky.44 = f32[64,64]{1,0:T(8,128)S(1)} custom-call(f32[64,64]{1,0:T(8,128)S(1)} %fusion.25), custom_call_target="Cholesky" | custom-call | tf_op jit(solution)/shard_map/jit(cholesky)/cholesky | solution.py:84
  157.8 0.6 compare_reduce_fusion.1
  158.5 0.7 fusion.38
  159.1 4.9 %custom-call.6 = f32[1,64,64]{1,2,0:T(8,128)S(1)} custom-call(f32[1,64,64]{2,1,0:T(8,128)S(1)} %get-tuple-element.41), custom_call_target="InvertDiagBlocksLowerTriangular" | custom-call | tf_op jit(solution)/shard_map/triangular_solve/custom-call.0 | solution.py:86
  164.0 0.3 convolution_convert_fusion.3
  164.3 0.2 convolution_convert_fusion.1
  164.6 4.2 %collective-permute-start.4 = (bf16[64,1,8,128]{3,2,1,0:T(8,128)(2,1)S(1)}, bf16[64,1,8,128]{3,2,1,0:T(8,128)(2,1)S(1)}, u32[]{:S(2)}, u32[]{:S(2)}) collective-permute-start(bf16[64,1,8,128]{3,2,1,0:T(8,128)(2,1)S(1)} %get-tuple-element.10), channel_id=1, source_target_pairs={{0,4},{4,8},{8,12},{12,16},{16,20},{20,24},{24,28},{1,5},{5,9},{9,... | collective-permute-start | bytes 393224 | tf_op jit(solution)/shard_map/ppermute | solution.py:12
  168.7 0.2 slice.434
  169.0 1.3 collective-permute-start.5
  170.3 2.3 collective-permute-done.4
  172.7 3.2 collective-permute-done.5
  175.9 0.2 fusion.45
  176.1 1.3 collective-permute-start.6
  177.4 1.5 collective-permute-start.7
  178.9 0.0 collective-permute-done.6
  178.9 2.3 collective-permute-done.7
  181.2 1.9 select_maximum_fusion
  183.1 3.3 %add_convert_fusion = bf16[64,2,8,128]{3,2,1,0:T(8,128)(2,1)S(1)} fusion(bf16[64,2,8,128]{3,2,1,0:T(8,128)(2,1)S(1)} %bitcast.105, bf16[64,4,10,130]{3,2,1,0:T(8,128)(2,1)S(1)} %select_maximum_fusion, bf16[64,4,1,128]{3,2,1,0:T(2,128)(2,1)S(1)} %collective-permute-done.7, bf16[64,4,8,128]{3,2,1,0:T(8,128)(2,1)S(1)} %constant_dynamic-update-slice_fusion, ...), kind=kLoop, calls=%fused_computation.31 | loop fusion | flops 13762560 | bytes 6381568 | tf_op jit(solution)/shard_map/convert_element_type | solution.py:34
  186.4 0.4 fusion.15
  186.8 43.6 %psum.45 = f32[192,64]{0,1:T(8,128)S(1)} all-reduce(f32[192,64]{0,1:T(8,128)S(1)} %fusion.15), channel_id=1, replica_groups=mesh['slab'=8,'col'=4] {'slab','col'}, use_global_device_ids=true, to_apply=%region_5.0 | all-reduce | flops 12288 | bytes 98304 | tf_op jit(solution)/shard_map/psum | solution.py:76
  230.4 0.3 fusion.3
  230.7 0.4 fusion.44
  231.1 39.1 %psum.46 = f32[192,64]{0,1:T(8,128)S(1)} all-reduce(f32[192,64]{0,1:T(8,128)S(1)} %fusion.44), channel_id=1, replica_groups=mesh['slab'=8,'col'=4] {'slab','col'}, use_global_device_ids=true, to_apply=%region_6.9 | all-reduce | flops 12288 | bytes 98304 | tf_op jit(solution)/shard_map/psum | solution.py:79
  270.2 0.3 fusion.4
  270.5 0.2 fusion.51
  270.7 41.3 %psum.47 = f32[64,64]{0,1:T(8,128)S(1)} all-reduce(f32[64,64]{0,1:T(8,128)S(1)} %fusion.51), channel_id=1, replica_groups=mesh['slab'=8,'col'=4] {'slab','col'}, use_global_device_ids=true, to_apply=%region_7.10 | all-reduce | flops 4096 | bytes 32768 | tf_op jit(solution)/shard_map/psum | solution.py:83
  312.1 0.1 copy.9
  312.2 5.8 %cholesky.55 = f32[64,64]{1,0:T(8,128)S(1)} custom-call(f32[64,64]{1,0:T(8,128)S(1)} %fusion.23), custom_call_target="Cholesky" | custom-call | tf_op jit(solution)/shard_map/jit(cholesky)/cholesky | solution.py:84
  318.1 0.6 compare_reduce_fusion
  318.7 0.7 fusion.37
  319.4 4.9 %custom-call.7 = f32[1,64,64]{1,2,0:T(8,128)S(1)} custom-call(f32[1,64,64]{2,1,0:T(8,128)S(1)} %get-tuple-element.43), custom_call_target="InvertDiagBlocksLowerTriangular" | custom-call | tf_op jit(solution)/shard_map/triangular_solve/custom-call.0 | solution.py:86
  324.3 0.3 convolution_convert_fusion.2
  324.5 0.2 fusion.14
  324.8 0.7 copy.16
  325.5 0.6 pad_maximum_fusion.17
  326.1 0.7 pad_maximum_fusion.16
  (17 shorter events, 0.3 us)
Async XLA Ops:
  0.6 7.3 %copy-start = (f32[8,27]{1,0:T(8,128)S(1)}, f32[8,27]{1,0:T(8,128)}, u32[]{:S(2)}) copy-start(f32[8,27]{1,0:T(8,128)} %param.8) | copy-start | bytes 2596
  0.6 15.7 %copy-start.1 = (bf16[3,64,2,8,128]{4,3,2,1,0:T(8,128)(2,1)S(1)}, bf16[3,64,2,8,128]{4,3,2,1,0:T(8,128)(2,1)}, u32[]{:S(2)}) copy-start(bf16[3,64,2,8,128]{4,3,2,1,0:T(8,128)(2,1)} %param.6) | copy-start | bytes 2359300
  1.7 7.6 %collective-permute-start = (bf16[64,1,8,128]{3,2,1,0:T(8,128)(2,1)S(1)}, bf16[64,1,8,128]{3,2,1,0:T(8,128)(2,1)S(1)}, u32[]{:S(2)}, u32[]{:S(2)}) collective-permute-start(bf16[64,1,8,128]{3,2,1,0:T(8,128)(2,1)S(1)} %get-tuple-element.38), channel_id=1, source_target_pairs={{0,4},{4,8},{8,12},{12,16},{16,20},{20,24},{24,28},{1,5},{5,9},{9,... | collective-permute-start | bytes 393224 | tf_op jit(solution)/shard_map/ppermute | solution.py:12
  6.6 6.9 %collective-permute-start.1 = (bf16[64,1,8,128]{3,2,1,0:T(8,128)(2,1)S(1)}, bf16[64,1,8,128]{3,2,1,0:T(8,128)(2,1)S(1)}, u32[]{:S(2)}, u32[]{:S(2)}) collective-permute-start(bf16[64,1,8,128]{3,2,1,0:T(8,128)(2,1)S(1)} %get-tuple-element.39), channel_id=1, source_target_pairs={{4,0},{8,4},{12,8},{16,12},{20,16},{24,20},{28,24},{5,1},{9,5},{13... | collective-permute-start | bytes 393224 | tf_op jit(solution)/shard_map/ppermute | solution.py:15
  13.6 3.0 collective-permute-start.2
  15.0 5.0 %collective-permute-start.3 = (bf16[64,4,1,128]{3,2,1,0:T(2,128)(2,1)S(1)}, bf16[64,4,1,128]{3,2,1,0:T(2,128)(2,1)S(1)}, u32[]{:S(2)}, u32[]{:S(2)}) collective-permute-start(bf16[64,4,1,128]{3,2,1,0:T(2,128)(2,1)S(1)} %get-tuple-element.8), channel_id=1, source_target_pairs={{1,0},{2,1},{3,2},{5,4},{6,5},{7,6},{9,8},{10,9},{11,10},{13,12},{... | collective-permute-start | bytes 196616 | tf_op jit(solution)/shard_map/ppermute | solution.py:15
  111.2 57.6 %slice-start = ((bf16[3,64,2,8,128]{4,3,2,1,0:T(8,128)(2,1)}), bf16[2,64,2,8,128]{4,3,2,1,0:T(8,128)(2,1)S(1)}, s32[]{:S(2)}) async-start(bf16[3,64,2,8,128]{4,3,2,1,0:T(8,128)(2,1)} %param.6), calls=%async_computation | async-start | bytes 1048576 | tf_op jit(solution)/shard_map/slice | solution.py:107
  164.6 8.0 %collective-permute-start.4 = (bf16[64,1,8,128]{3,2,1,0:T(8,128)(2,1)S(1)}, bf16[64,1,8,128]{3,2,1,0:T(8,128)(2,1)S(1)}, u32[]{:S(2)}, u32[]{:S(2)}) collective-permute-start(bf16[64,1,8,128]{3,2,1,0:T(8,128)(2,1)S(1)} %get-tuple-element.10), channel_id=1, source_target_pairs={{0,4},{4,8},{8,12},{12,16},{16,20},{20,24},{24,28},{1,5},{5,9},{9,... | collective-permute-start | bytes 393224 | tf_op jit(solution)/shard_map/ppermute | solution.py:12
  169.0 6.9 %collective-permute-start.5 = (bf16[64,1,8,128]{3,2,1,0:T(8,128)(2,1)S(1)}, bf16[64,1,8,128]{3,2,1,0:T(8,128)(2,1)S(1)}, u32[]{:S(2)}, u32[]{:S(2)}) collective-permute-start(bf16[64,1,8,128]{3,2,1,0:T(8,128)(2,1)S(1)} %get-tuple-element.9), channel_id=1, source_target_pairs={{4,0},{8,4},{12,8},{16,12},{20,16},{24,20},{28,24},{5,1},{9,5},{13... | collective-permute-start | bytes 393224 | tf_op jit(solution)/shard_map/ppermute | solution.py:15
  176.1 2.8 collective-permute-start.6
  177.4 3.8 %collective-permute-start.7 = (bf16[64,4,1,128]{3,2,1,0:T(2,128)(2,1)S(1)}, bf16[64,4,1,128]{3,2,1,0:T(2,128)(2,1)S(1)}, u32[]{:S(2)}, u32[]{:S(2)}) collective-permute-start(bf16[64,4,1,128]{3,2,1,0:T(2,128)(2,1)S(1)} %get-tuple-element.6), channel_id=1, source_target_pairs={{1,0},{2,1},{3,2},{5,4},{6,5},{7,6},{9,8},{10,9},{11,10},{13,12},{... | collective-permute-start | bytes 196616 | tf_op jit(solution)/shard_map/ppermute | solution.py:15
where the time goes:
time: 328 us; the launch traced here: 327 us
  blocking collectives  248 us (76%)
  other arithmetic  37 us (11%)
  starting transfers between devices  17 us (5%)
  waiting for transfers between devices  15.5 us (5%)
  matrix products  4.9 us (1%)
    psum x2, blocking collectives, orthonormalize(): first = lax.psum(gram_of(stack, block_inner, 1.0), ('slab', 'col')) * scale  87.4 us
    psum x2, blocking collectives, orthonormalize(): lax.psum(gram_of(two_inner, two_inner, 1.0), ('slab', 'col')) * scale  81.8 us
    psum x2, blocking collectives, orthonormalize(): lax.psum(gram_of(stack, inner_part(one_wide, shape_wide), 1.0), ('slab',...  79.2 us
    another operation x6, other arithmetic, orthonormalize(): lower = jnp.linalg.cholesky(square)  13 us
    ppermute x4, waiting for transfers between devices, extended(): lax.ppermute(lax.slice_in_dim(block, 0, width, axis=dim), axis, backward)  12.8 us
    ppermute x4, starting transfers between devices, extended(): lax.ppermute(lax.slice_in_dim(block, block.shape[dim] - width, None, axis...  11.6 us
    another operation x2, other arithmetic, orthonormalize(): lax.linalg.triangular_solve(lower, identity, left_side=True, lower=True)  9.79 us
    convert_element_type x2, other arithmetic, apply_stencil(): return total.astype(jnp.bfloat16)  6.68 us
  transfers between devices with their start and end apart: 8, of which 6 were waited for; matrix products, arithmetic and copies ran while one was open for 1% of the time, Pallas kernels for 0%

commit v1 on v0

v1 whole, which is shorter than its diff:
```python
import functools

import jax
import jax.numpy as jnp
from jax import lax
from jax.experimental import pallas as pl
from jax.experimental.pallas import tpu as pltpu
from jax.sharding import PartitionSpec as P

HIGHEST = lax.Precision.HIGHEST
NN = (((1,), (0,)), ((), ()))
NT = (((1,), (1,)), ((), ()))
ROWS = 16


def dot(left, right, dims=NN, precision=None):
    return lax.dot_general(
        left, right, dims, precision=precision, preferred_element_type=jnp.float32
    )


def exact(left, right, dims=NN):
    return dot(left, right, dims, HIGHEST)


def neighbours(block, span_x, span_y, depth):
    plane = span_y * depth

    def exchange(axis, upward, downward):
        count = lax.axis_size(axis)
        forward = [(i, i + 1) for i in range(count - 1)]
        backward = [(target, source) for source, target in forward]
        return lax.ppermute(upward, axis, forward), lax.ppermute(downward, axis, backward)

    xlo, xhi = exchange("slab", block[:, (span_x - 1) * plane :], block[:, :plane])

    def edge(row):
        at = row * depth
        parts = [xlo[:, at : at + depth]]
        parts += [block[:, x * plane + at : x * plane + at + depth] for x in range(span_x)]
        parts += [xhi[:, at : at + depth]]
        return jnp.concatenate(parts, axis=1)

    ylo, yhi = exchange("col", edge(span_y - 1), edge(0))
    return xlo, xhi, ylo, yhi


def coefficients_kernel(table, cells, coef):
    classes = table.shape[0]
    lanes = lax.broadcasted_iota(jnp.int32, cells.shape, 1)
    depth = cells.shape[1]
    here = cells[...]
    below = pltpu.roll(here, depth - 1, 1)
    above = pltpu.roll(here, 1, 1)
    maps = (below, here, above)
    keep = (lanes < depth - 1, None, lanes > 0)
    for dz in range(3):
        masks = [maps[dz] == k for k in range(1, classes)]
        for pair in range(9):
            offset = 3 * pair + dz
            value = jnp.full(cells.shape, table[0, offset], jnp.float32)
            for k in range(1, classes):
                value = jnp.where(masks[k - 1], table[k, offset], value)
            if keep[dz] is not None:
                value = jnp.where(keep[dz], value, 0.0)
            coef[offset] = value


def coefficients(table, cell_map):
    span_x, span_y, depth = cell_map.shape
    lines = span_x * span_y
    return pl.pallas_call(
        coefficients_kernel,
        out_shape=jax.ShapeDtypeStruct((27, lines, depth), jnp.float32),
        in_specs=[
            pl.BlockSpec(memory_space=pltpu.SMEM),
            pl.BlockSpec(memory_space=pltpu.VMEM),
        ],
        out_specs=pl.BlockSpec(memory_space=pltpu.VMEM),
        name="coefficients",
    )(table, cell_map.reshape(lines, depth))


def stencil_into(image, coef, block, xlo, xhi, ylo, yhi, span_x, span_y, depth):
    columns = block.shape[0]

    def tile(step, carry):
        rows = pl.ds(pl.multiple_of(step * ROWS, ROWS), ROWS)

        def line(x, y):
            if y < 0:
                ref, at = ylo, x + 1
            elif y >= span_y:
                ref, at = yhi, x + 1
            elif x < 0:
                ref, at = xlo, y
            elif x >= span_x:
                ref, at = xhi, y
            else:
                ref, at = block, x * span_y + y
            return ref[rows, at * depth : (at + 1) * depth].astype(jnp.float32)

        held = {y: [line(x, y) for x in range(-1, span_x + 1)] for y in (-1, 0)}
        for y in range(span_y):
            held[y + 1] = [line(x, y + 1) for x in range(-1, span_x + 1)]
            for x in range(span_x):
                at = x * span_y + y
                sums = [None, None, None]
                for dx in range(3):
                    for dy in range(3):
                        field = held[y + dy - 1][x + dx]
                        for dz in range(3):
                            term = coef[9 * dx + 3 * dy + dz, at : at + 1, :] * field
                            sums[dz] = term if sums[dz] is None else sums[dz] + term
                total = sums[1] + pltpu.roll(sums[0], 1, 1) + pltpu.roll(sums[2], depth - 1, 1)
                image[rows, at * depth : (at + 1) * depth] = total.astype(jnp.bfloat16)
            del held[y - 1]
        return carry

    lax.fori_loop(0, columns // ROWS, tile, 0)


def first_image_kernel(spans, coef, stack, xlo, xhi, ylo, yhi, image, cross, own):
    columns = image.shape[0]
    fields = stack.shape[0]
    block = stack.at[fields - columns : fields]
    stencil_into(image, coef, block, xlo, xhi, ylo, yhi, *spans)
    w = image[...]
    cross[:, :fields] = dot(w, stack[...], NT)
    cross[:, fields:] = dot(w, w, NT)
    own[...] = dot(stack[...], stack[...], NT)


def second_image_kernel(spans, coef, stack, block, xlo, xhi, ylo, yhi, image, cross):
    columns = image.shape[0]
    fields = stack.shape[0]
    stencil_into(image, coef, block, xlo, xhi, ylo, yhi, *spans)
    w = image[...]
    cross[:, : fields - columns] = dot(w, stack[columns:], NT)
    cross[:, fields - columns : fields] = dot(w, block[...], NT)
    cross[:, fields:] = dot(w, w, NT)


def factor(square):
    size = square.shape[0]
    lane = lax.broadcasted_iota(jnp.int32, (8, 2 * size), 1)
    sub = lax.broadcasted_iota(jnp.int32, (8, 2 * size), 0)
    blocks = []
    for b in range(size // 8):
        unit = (lax.broadcasted_iota(jnp.int32, (8, size), 1)
                == lax.broadcasted_iota(jnp.int32, (8, size), 0) + 8 * b).astype(jnp.float32)
        blocks.append(jnp.concatenate([square[8 * b : 8 * b + 8], unit], axis=1))
    for k in range(size):
        b, r = divmod(k, 8)
        row = blocks[b][r : r + 1, :]
        row = row * (1.0 / row[:, k : k + 1])
        for later in range(b, size // 8):
            column = blocks[later][:, k : k + 1]
            if later == b:
                column = jnp.where(sub[:, :1] > r, column, 0.0)
            blocks[later] = blocks[later] - column * row
    done = []
    for b, rows in enumerate(blocks):
        diagonal = jnp.sum(jnp.where(lane == sub + 8 * b, rows, 0.0), axis=1, keepdims=True)
        done.append(rows * lax.rsqrt(diagonal))
    whole = jnp.concatenate(done, axis=0)
    return whole[:, :size], whole[:, size:]


def project(cross, own, scale):
    fields = own.shape[0]
    first = cross[:, :fields] * scale
    square = cross[:, fields:] * scale
    first_low = first.astype(jnp.bfloat16)
    second = first - exact(first_low.astype(jnp.float32), own)
    second_low = second.astype(jnp.bfloat16)
    used = first_low.astype(jnp.float32) + second_low.astype(jnp.float32)
    rest = second - exact(second_low.astype(jnp.float32), own)
    square = square - exact(used, first, NT) - exact(rest, used, NT)
    return first_low, second_low, first + second, rest, square


def first_solve_kernel(scale, cross, own, stack, image, block, proj, low, own_next):
    columns = image.shape[0]
    gram = own[...] * scale
    first_low, second_low, both, rest, square = project(cross[...], gram, scale)
    proj[...] = both.T
    upper, inverse = factor(square)
    low[...] = upper.T
    inverse = inverse.astype(jnp.bfloat16)
    w = image[...].astype(jnp.float32) - dot(first_low, stack[...]) - dot(second_low, stack[...])
    block[...] = dot(inverse, w.astype(jnp.bfloat16)).astype(jnp.bfloat16)
    kept = stack.shape[0] - columns
    wide = inverse.astype(jnp.float32)
    mixed = exact(wide, rest[:, columns:])
    own_next[:kept, :kept] = gram[columns:, columns:]
    own_next[kept:, :kept] = mixed
    own_next[:kept, kept:] = mixed.T
    own_next[kept:, kept:] = exact(exact(wide, square), wide, NT)


def second_solve_kernel(scale, cross, own, stack, last, image, proj_in, low_in, block, proj, low):
    columns = image.shape[0]
    kept = stack.shape[0] - columns
    first_low, second_low, both, _, square = project(cross[...], own[...], scale)
    proj[0] = proj_in[...]
    proj[1] = both.T
    upper, inverse = factor(square)
    low[0] = low_in[...]
    low[1] = upper.T
    w = image[...].astype(jnp.float32)
    for part in (first_low, second_low):
        w = w - dot(part[:, :kept], stack[columns:]) - dot(part[:, kept:], last[...])
    block[...] = dot(inverse.astype(jnp.bfloat16), w.astype(jnp.bfloat16)).astype(jnp.bfloat16)


def whole_sum(parts):
    axes = ("slab", "col")
    count = lax.axis_size("slab") * lax.axis_size("col")
    flat = jnp.concatenate([part.reshape(count, -1) for part in parts], axis=1)
    shares = lax.all_to_all(flat, axes, 0, 0, tiled=True)
    share = jnp.sum(shares, axis=0, keepdims=True)
    flat = lax.all_to_all(jnp.broadcast_to(share, flat.shape), axes, 0, 0, tiled=True)
    done, at = [], 0
    for part in parts:
        width = part.size // count
        done.append(flat[:, at : at + width].reshape(part.shape))
        at += width
    return done


def call(kernel, name, outs, *args):
    return pl.pallas_call(
        kernel,
        out_shape=[jax.ShapeDtypeStruct(shape, dtype) for shape, dtype in outs],
        in_specs=[pl.BlockSpec(memory_space=pltpu.VMEM)] * len(args),
        out_specs=[pl.BlockSpec(memory_space=pltpu.VMEM)] * len(outs),
        compiler_params=pltpu.CompilerParams(vmem_limit_bytes=24 * 1024 * 1024),
        name=name,
    )(*args)


def shards(basis, cell_map, table):
    span_x, span_y, depth = cell_map.shape
    blocks, columns = basis.shape[:2]
    cells = span_x * span_y * depth
    fields = blocks * columns
    scale = 1.0 / (cells * lax.axis_size("slab") * lax.axis_size("col"))
    spans = (span_x, span_y, depth)
    f32, bf16 = jnp.float32, jnp.bfloat16

    stack = basis.reshape(fields, cells)
    coef = coefficients(table, cell_map)
    around = neighbours(stack[fields - columns :], *spans)
    image, cross, own = call(
        functools.partial(first_image_kernel, spans),
        "first_image",
        [((columns, cells), bf16), ((columns, fields + columns), f32), ((fields, fields), f32)],
        coef, stack, *around,
    )
    cross, own = whole_sum([cross, own])
    block, proj, low, own = call(
        functools.partial(first_solve_kernel, scale),
        "first_solve",
        [((columns, cells), bf16), ((fields, columns), f32), ((columns, columns), f32),
         ((fields, fields), f32)],
        cross, own, stack, image,
    )
    around = neighbours(block, *spans)
    image, cross = call(
        functools.partial(second_image_kernel, spans),
        "second_image",
        [((columns, cells), bf16), ((columns, fields + columns), f32)],
        coef, stack, block, *around,
    )
    (cross,) = whole_sum([cross])
    block, proj, low = call(
        functools.partial(second_solve_kernel, scale),
        "second_solve",
        [((columns, cells), bf16), ((2, fields, columns), f32), ((2, columns, columns), f32)],
        cross, own, stack, block, image, proj, low,
    )
    return block.reshape(columns, *spans), proj, low


def solution(mesh):
    placed = (P(None, None, "slab", "col", None), P("slab", "col", None), P())
    return jax.shard_map(
        shards,
        mesh=mesh,
        in_specs=placed,
        out_specs=(P(None, "slab", "col", None), P(), P()),
        check_vma=False,
    )
```

time: 328 us -> 106 us (0.32)
  blocking collectives: 248 us -> 50.8 us
  other arithmetic: 37 us -> 0.42 us
  Pallas kernels: 0 us -> 18.6 us
  matrix products: 4.9 us -> 0 us
  waiting for transfers between devices: 15.5 us -> 11.9 us
    psum x6 -> x0, blocking collectives: 248 us -> none  [the longest x2 87.4 us: orthonormalize(): first = lax.psum(gram_of(stack, block_inner, 1.0), ('slab', 'col')) * scale]
    all_to_all x0 -> x4, blocking collectives: none -> 50.8 us  [the longest x2 29.9 us: whole_sum(): shares = lax.all_to_all(flat, axes, 0, 0, tiled=True)]
    another operation x14 -> x0, other arithmetic: 25.5 us -> none  [the longest x6 13 us: orthonormalize(): lower = jnp.linalg.cholesky(square)]
    pallas_call x0 -> x5, Pallas kernels: none -> 18.6 us  [the longest x4 17.1 us: call(): pl.pallas_call(kernel, out_shape=[jax.ShapeDtypeStruct(shape, dtype) for...]
    convert_element_type x2 -> x0, other arithmetic: 6.68 us -> none  [apply_stencil(): return total.astype(jnp.bfloat16)]
    concatenate x2 -> x5, other arithmetic: 4.66 us -> 0.06 us  [the longest x4 0.05 us: edge(): return jnp.concatenate(parts, axis=1)]
    dot_general x13 -> x0, matrix products: 4.39 us -> none  [the longest x6 1.93 us: gram_of(): lax.dot_general(left, right, (((1,), (1,)), ((), ())), preferred_element_...]
    ppermute x8, waiting for transfers between devices: 15.5 us -> 11.9 us  [the longest x4 7.57 us: exchange(): lax.ppermute(downward, axis, backward)]
  transfers between devices with their start and end apart: 8 -> 8, of which waited for: 6 -> 6; matrix products, arithmetic and copies ran while one was open for 1% -> 0% of each run, Pallas kernels for 0% -> 1%
where the time goes in v1:
time: 106 us
  blocking collectives  50.8 us (48%)
  starting transfers between devices  18.6 us (18%)
  Pallas kernels  18.6 us (18%)
  waiting for transfers between devices  11.9 us (11%)
  local copies, waits for them, and re-layouts  4.62 us (4%)
    all_to_all x2, blocking collectives, whole_sum(): shares = lax.all_to_all(flat, axes, 0, 0, tiled=True)  29.9 us
    all_to_all x2, blocking collectives, whole_sum(): lax.all_to_all(jnp.broadcast_to(share, flat.shape), axes, 0, 0, tiled=True)  20.9 us
    pallas_call x4, Pallas kernels, call(): pl.pallas_call(kernel, out_shape=[jax.ShapeDtypeStruct(shape, dtype) for...  17.1 us
    ppermute x4, starting transfers between devices, exchange(): lax.ppermute(upward, axis, forward)  13.3 us
    ppermute x4, waiting for transfers between devices, exchange(): lax.ppermute(downward, axis, backward)  7.57 us
    ppermute x4, starting transfers between devices, exchange(): lax.ppermute(downward, axis, backward)  5.3 us
    ppermute x4, waiting for transfers between devices, exchange(): lax.ppermute(upward, axis, forward)  4.28 us
    unnamed x9, local copies, waits for them, and re-layouts  2.48 us
  transfers between devices with their start and end apart: 8, of which 6 were waited for; matrix products, arithmetic and copies ran while one was open for 0% of the time, Pallas kernels for 1%

profile of v1, /device:TPU:0, one launch (start us, length us, event | category | flops | bytes accessed | tf_op | source)
XLA Modules:
  0.0 105.7 jit_solution(11824320293525840168)
XLA Ops:
  0.6 0.0 slice-start
  0.6 0.9 slice-done
  1.6 0.0 copy-start.2
  1.6 0.1 slice.73
  1.7 1.4 %collective-permute-start.1 = (bf16[64,1024]{1,0:T(8,128)(2,1)S(1)}, bf16[64,1024]{1,0:T(8,128)(2,1)S(1)}, u32[]{:S(2)}, u32[]{:S(2)}) collective-permute-start(bf16[64,1024]{1,0:T(8,128)(2,1)S(1)} %get-tuple-element.43), channel_id=1, source_target_pairs={{4,0},{8,4},{12,8},{16,12},{20,16},{24,20},{28,24},{5,1},{9,5},{13... | collective-permute-start | bytes 393224 | tf_op jit(solution)/shard_map/ppermute | solution.py:33
  3.2 5.5 %collective-permute-start = (bf16[64,1024]{1,0:T(8,128)(2,1)S(1)}, bf16[64,1024]{1,0:T(8,128)(2,1)S(1)}, u32[]{:S(2)}, u32[]{:S(2)}) collective-permute-start(bf16[64,1024]{1,0:T(8,128)(2,1)S(1)} %get-tuple-element.44), channel_id=1, source_target_pairs={{0,4},{4,8},{8,12},{12,16},{16,20},{20,24},{24,28},{1,5},{5,9},{9,... | collective-permute-start | bytes 393224 | tf_op jit(solution)/shard_map/ppermute | solution.py:33
  8.7 1.5 %collective-permute-done.1.xhi = bf16[64,1024]{1,0:T(8,128)(2,1)S(1)} collective-permute-done((bf16[64,1024]{1,0:T(8,128)(2,1)S(1)}, bf16[64,1024]{1,0:T(8,128)(2,1)S(1)}, u32[]{:S(2)}, u32[]{:S(2)}) %collective-permute-start.1) | collective-permute-done | bytes 131104 | tf_op jit(solution)/shard_map/ppermute | solution.py:33
  10.2 3.0 %collective-permute-done.xlo = bf16[64,1024]{1,0:T(8,128)(2,1)S(1)} collective-permute-done((bf16[64,1024]{1,0:T(8,128)(2,1)S(1)}, bf16[64,1024]{1,0:T(8,128)(2,1)S(1)}, u32[]{:S(2)}, u32[]{:S(2)}) %collective-permute-start) | collective-permute-done | bytes 131104 | tf_op jit(solution)/shard_map/ppermute | solution.py:33
  13.2 1.9 %collective-permute-start.2 = (bf16[64,512]{1,0:T(8,128)(2,1)S(1)}, bf16[64,512]{1,0:T(8,128)(2,1)S(1)}, u32[]{:S(2)}, u32[]{:S(2)}) collective-permute-start(bf16[64,512]{1,0:T(8,128)(2,1)S(1)} %pad_maximum_fusion.1), channel_id=1, source_target_pairs={{0,1},{1,2},{2,3},{4,5},{5,6},{6,7},{8,9},{9,10},{10,11},{12,13},{... | collective-permute-start | bytes 196616 | tf_op jit(solution)/shard_map/ppermute | solution.py:33
  15.1 1.3 %collective-permute-start.3 = (bf16[64,512]{1,0:T(8,128)(2,1)S(1)}, bf16[64,512]{1,0:T(8,128)(2,1)S(1)}, u32[]{:S(2)}, u32[]{:S(2)}) collective-permute-start(bf16[64,512]{1,0:T(8,128)(2,1)S(1)} %pad_maximum_fusion.2), channel_id=1, source_target_pairs={{1,0},{2,1},{3,2},{5,4},{6,5},{7,6},{9,8},{10,9},{11,10},{13,12},{... | collective-permute-start | bytes 196616 | tf_op jit(solution)/shard_map/ppermute | solution.py:33
  16.4 0.0 copy-done.2
  16.4 0.3 reshape.51.stack
  16.8 1.6 %coefficients.1.coef = f32[27,16,128]{2,1,0:T(8,128)} custom-call(f32[8,27]{1,0:T(8,128)} %table.1, s32[16,128]{1,0:T(8,128)} %bitcast.15), custom_call_target="tpu_custom_call" | custom-call | tf_op jit(solution)/shard_map/coefficients/pallas_call | solution.py:72
  18.3 0.0 collective-permute-done.2.ylo
  18.3 1.0 collective-permute-done.3.yhi
  19.4 0.0 copy-start
  19.4 0.9 copy-done
  20.3 1.7 %first_image.1 = (bf16[64,2048]{1,0:T(8,128)(2,1)S(1)}, f32[64,256]{1,0:T(8,128)S(1)}, f32[192,192]{1,0:T(8,128)S(1)}) custom-call(f32[27,16,128]{2,1,0:T(8,128)S(1)} %copy-done, bf16[192,2048]{1,0:T(8,128)(2,1)S(1)} %reshape.51.stack, bf16[64,1024]{1,0:T(8,128)(2,1)S(1)} %collective-permute-done.xlo, bf16[64,1024]{1,0:T(8,128)(2,1)S(1)} %collective-permute-done.1.xhi, ...), custom_call_target="tpu_custom_call" | custom-call | tf_op jit(solution)/shard_map/first_image/pallas_call | solution.py:233
  22.0 0.1 reshape.53
  22.1 0.1 all_to_all.22
  22.3 16.9 %all_to_all.34 = f32[32,1,1664]{2,1,0:T(1,128)S(1)} all-to-all(f32[32,1,1664]{2,1,0:T(1,128)S(1)} %all_to_all.22), channel_id=1, replica_groups=mesh['slab'=8,'col'=4] {'slab','col'}, dimensions={0} | all-to-all | bytes 425984 | tf_op jit(solution)/shard_map/all_to_all | solution.py:221
  39.2 0.1 reduce_sum.18
  39.3 0.1 broadcast_in_dim.4
  39.5 11.8 %all_to_all.35 = f32[32,1,1664]{2,1,0:T(1,128)S(1)} all-to-all(f32[32,1,1664]{2,1,0:T(1,128)S(1)} %broadcast_in_dim.4), channel_id=1, replica_groups=mesh['slab'=8,'col'=4] {'slab','col'}, dimensions={0} | all-to-all | bytes 425984 | tf_op jit(solution)/shard_map/all_to_all | solution.py:223
  51.3 0.1 reshape.55.own
  51.4 6.8 %first_solve.1 = (bf16[64,2048]{1,0:T(8,128)(2,1)S(1)}, f32[192,64]{1,0:T(8,128)S(1)}, f32[64,64]{1,0:T(8,128)S(1)}, f32[192,192]{1,0:T(8,128)S(1)}) custom-call(f32[64,256]{1,0:T(8,128)S(1)} %reshape.54.cross, f32[192,192]{1,0:T(8,128)S(1)} %reshape.55.own, bf16[192,2048]{1,0:T(8,128)(2,1)S(1)} %reshape.51.stack, bf16[64,2048]{1,0:T(8,128)(2,1)S(1)} %get-tuple-element.17.image), custom_call_target="tpu_custom_call" | custom-call | tf_op jit(solution)/shard_map/first_solve/pallas_call | solution.py:233
  58.2 1.3 %collective-permute-start.5 = (bf16[64,1024]{1,0:T(8,128)(2,1)S(1)}, bf16[64,1024]{1,0:T(8,128)(2,1)S(1)}, u32[]{:S(2)}, u32[]{:S(2)}) collective-permute-start(bf16[64,1024]{1,0:T(8,128)(2,1)S(1)} %get-tuple-element.37), channel_id=1, source_target_pairs={{4,0},{8,4},{12,8},{16,12},{20,16},{24,20},{28,24},{5,1},{9,5},{13... | collective-permute-start | bytes 393224 | tf_op jit(solution)/shard_map/ppermute | solution.py:33
  59.5 4.6 %collective-permute-start.4 = (bf16[64,1024]{1,0:T(8,128)(2,1)S(1)}, bf16[64,1024]{1,0:T(8,128)(2,1)S(1)}, u32[]{:S(2)}, u32[]{:S(2)}) collective-permute-start(bf16[64,1024]{1,0:T(8,128)(2,1)S(1)} %get-tuple-element.38), channel_id=1, source_target_pairs={{0,4},{4,8},{8,12},{12,16},{16,20},{20,24},{24,28},{1,5},{5,9},{9,... | collective-permute-start | bytes 393224 | tf_op jit(solution)/shard_map/ppermute | solution.py:33
  64.1 0.0 copy-start.1
  64.1 1.8 %collective-permute-done.5.xhi = bf16[64,1024]{1,0:T(8,128)(2,1)S(1)} collective-permute-done((bf16[64,1024]{1,0:T(8,128)(2,1)S(1)}, bf16[64,1024]{1,0:T(8,128)(2,1)S(1)}, u32[]{:S(2)}, u32[]{:S(2)}) %collective-permute-start.5) | collective-permute-done | bytes 131104 | tf_op jit(solution)/shard_map/ppermute | solution.py:33
  65.9 1.3 %collective-permute-done.4.xlo = bf16[64,1024]{1,0:T(8,128)(2,1)S(1)} collective-permute-done((bf16[64,1024]{1,0:T(8,128)(2,1)S(1)}, bf16[64,1024]{1,0:T(8,128)(2,1)S(1)}, u32[]{:S(2)}, u32[]{:S(2)}) %collective-permute-start.4) | collective-permute-done | bytes 131104 | tf_op jit(solution)/shard_map/ppermute | solution.py:33
  67.2 1.3 %collective-permute-start.6 = (bf16[64,512]{1,0:T(8,128)(2,1)S(1)}, bf16[64,512]{1,0:T(8,128)(2,1)S(1)}, u32[]{:S(2)}, u32[]{:S(2)}) collective-permute-start(bf16[64,512]{1,0:T(8,128)(2,1)S(1)} %pad_maximum_fusion.3), channel_id=1, source_target_pairs={{0,1},{1,2},{2,3},{4,5},{5,6},{6,7},{8,9},{9,10},{10,11},{12,13},{... | collective-permute-start | bytes 196616 | tf_op jit(solution)/shard_map/ppermute | solution.py:33
  68.5 1.3 %collective-permute-start.7 = (bf16[64,512]{1,0:T(8,128)(2,1)S(1)}, bf16[64,512]{1,0:T(8,128)(2,1)S(1)}, u32[]{:S(2)}, u32[]{:S(2)}) collective-permute-start(bf16[64,512]{1,0:T(8,128)(2,1)S(1)} %pad_maximum_fusion.4), channel_id=1, source_target_pairs={{1,0},{2,1},{3,2},{5,4},{6,5},{7,6},{9,8},{10,9},{11,10},{13,12},{... | collective-permute-start | bytes 196616 | tf_op jit(solution)/shard_map/ppermute | solution.py:33
  69.8 0.0 collective-permute-done.6.ylo
  69.8 3.2 %collective-permute-done.7.yhi = bf16[64,512]{1,0:T(8,128)(2,1)S(1)} collective-permute-done((bf16[64,512]{1,0:T(8,128)(2,1)S(1)}, bf16[64,512]{1,0:T(8,128)(2,1)S(1)}, u32[]{:S(2)}, u32[]{:S(2)}) %collective-permute-start.7) | collective-permute-done | bytes 65568 | tf_op jit(solution)/shard_map/ppermute | solution.py:33
  73.1 0.0 copy-done.1
  73.1 1.5 %second_image.1 = (bf16[64,2048]{1,0:T(8,128)(2,1)S(1)}, f32[64,256]{1,0:T(8,128)S(1)}) custom-call(f32[27,16,128]{2,1,0:T(8,128)S(1)} %copy-done.1, bf16[192,2048]{1,0:T(8,128)(2,1)S(1)} %reshape.51.stack, bf16[64,2048]{1,0:T(8,128)(2,1)S(1)} %get-tuple-element.18.block.last, bf16[64,1024]{1,0:T(8,128)(2,1)S(1)} %collective-permute-done.4.xlo, ...), custom_call_target="tpu_custom_call" | custom-call | tf_op jit(solution)/shard_map/second_image/pallas_call | solution.py:233
  74.6 0.1 all_to_all.29
  74.7 13.0 %all_to_all.36 = f32[32,1,512]{2,1,0:T(1,128)S(1)} all-to-all(f32[32,1,512]{2,1,0:T(1,128)S(1)} %all_to_all.29), channel_id=1, replica_groups=mesh['slab'=8,'col'=4] {'slab','col'}, dimensions={0} | all-to-all | bytes 131072 | tf_op jit(solution)/shard_map/all_to_all | solution.py:221
  87.7 0.1 reduce_sum.19
  87.8 9.1 %all_to_all.37 = f32[32,1,512]{2,1,0:T(1,128)S(1)} all-to-all(f32[32,1,512]{2,1,0:T(1,128)S(1)} %broadcast_in_dim.5), channel_id=1, replica_groups=mesh['slab'=8,'col'=4] {'slab','col'}, dimensions={0} | all-to-all | bytes 131072 | tf_op jit(solution)/shard_map/all_to_all | solution.py:223
  96.9 0.2 reduce.2
  97.1 7.1 %second_solve.1 = (bf16[64,2048]{1,0:T(8,128)(2,1)S(1)}, f32[2,192,64]{2,1,0:T(8,128)S(1)}, f32[2,64,64]{2,1,0:T(8,128)}) custom-call(f32[64,256]{1,0:T(8,128)S(1)} %reshape.56.cross, f32[192,192]{1,0:T(8,128)S(1)} %get-tuple-element.20.own, bf16[192,2048]{1,0:T(8,128)(2,1)S(1)} %reshape.51.stack, bf16[64,2048]{1,0:T(8,128)(2,1)S(1)} %get-tuple-element.18.block.last, ...), custom_call_target="tpu_custom_call" | custom-call | tf_op jit(solution)/shard_map/second_solve/pallas_call | solution.py:233
  104.2 0.7 copy.10
  105.0 0.8 copy.8
  (20 shorter events, 0.3 us)
Async XLA Ops:
  0.6 1.0 slice-start
  1.6 14.8 %copy-start.2 = (bf16[3,64,2,8,128]{4,3,2,1,0:T(8,128)(2,1)S(1)}, bf16[3,64,2,8,128]{4,3,2,1,0:T(8,128)(2,1)}, u32[]{:S(2)}) copy-start(bf16[3,64,2,8,128]{4,3,2,1,0:T(8,128)(2,1)} %param.3) | copy-start | bytes 2359300
  1.7 8.5 %collective-permute-start.1 = (bf16[64,1024]{1,0:T(8,128)(2,1)S(1)}, bf16[64,1024]{1,0:T(8,128)(2,1)S(1)}, u32[]{:S(2)}, u32[]{:S(2)}) collective-permute-start(bf16[64,1024]{1,0:T(8,128)(2,1)S(1)} %get-tuple-element.43), channel_id=1, source_target_pairs={{4,0},{8,4},{12,8},{16,12},{20,16},{24,20},{28,24},{5,1},{9,5},{13... | collective-permute-start | bytes 393224 | tf_op jit(solution)/shard_map/ppermute | solution.py:33
  3.2 10.0 %collective-permute-start = (bf16[64,1024]{1,0:T(8,128)(2,1)S(1)}, bf16[64,1024]{1,0:T(8,128)(2,1)S(1)}, u32[]{:S(2)}, u32[]{:S(2)}) collective-permute-start(bf16[64,1024]{1,0:T(8,128)(2,1)S(1)} %get-tuple-element.44), channel_id=1, source_target_pairs={{0,4},{4,8},{8,12},{12,16},{16,20},{20,24},{24,28},{1,5},{5,9},{9,... | collective-permute-start | bytes 393224 | tf_op jit(solution)/shard_map/ppermute | solution.py:33
  13.2 5.2 %collective-permute-start.2 = (bf16[64,512]{1,0:T(8,128)(2,1)S(1)}, bf16[64,512]{1,0:T(8,128)(2,1)S(1)}, u32[]{:S(2)}, u32[]{:S(2)}) collective-permute-start(bf16[64,512]{1,0:T(8,128)(2,1)S(1)} %pad_maximum_fusion.1), channel_id=1, source_target_pairs={{0,1},{1,2},{2,3},{4,5},{5,6},{6,7},{8,9},{9,10},{10,11},{12,13},{... | collective-permute-start | bytes 196616 | tf_op jit(solution)/shard_map/ppermute | solution.py:33
  15.1 4.3 %collective-permute-start.3 = (bf16[64,512]{1,0:T(8,128)(2,1)S(1)}, bf16[64,512]{1,0:T(8,128)(2,1)S(1)}, u32[]{:S(2)}, u32[]{:S(2)}) collective-permute-start(bf16[64,512]{1,0:T(8,128)(2,1)S(1)} %pad_maximum_fusion.2), channel_id=1, source_target_pairs={{1,0},{2,1},{3,2},{5,4},{6,5},{7,6},{9,8},{10,9},{11,10},{13,12},{... | collective-permute-start | bytes 196616 | tf_op jit(solution)/shard_map/ppermute | solution.py:33
  19.4 0.9 copy-start
  58.2 7.7 %collective-permute-start.5 = (bf16[64,1024]{1,0:T(8,128)(2,1)S(1)}, bf16[64,1024]{1,0:T(8,128)(2,1)S(1)}, u32[]{:S(2)}, u32[]{:S(2)}) collective-permute-start(bf16[64,1024]{1,0:T(8,128)(2,1)S(1)} %get-tuple-element.37), channel_id=1, source_target_pairs={{4,0},{8,4},{12,8},{16,12},{20,16},{24,20},{28,24},{5,1},{9,5},{13... | collective-permute-start | bytes 393224 | tf_op jit(solution)/shard_map/ppermute | solution.py:33
  59.5 7.7 %collective-permute-start.4 = (bf16[64,1024]{1,0:T(8,128)(2,1)S(1)}, bf16[64,1024]{1,0:T(8,128)(2,1)S(1)}, u32[]{:S(2)}, u32[]{:S(2)}) collective-permute-start(bf16[64,1024]{1,0:T(8,128)(2,1)S(1)} %get-tuple-element.38), channel_id=1, source_target_pairs={{0,4},{4,8},{8,12},{12,16},{16,20},{20,24},{24,28},{1,5},{5,9},{9,... | collective-permute-start | bytes 393224 | tf_op jit(solution)/shard_map/ppermute | solution.py:33
  64.1 9.0 %copy-start.1 = (f32[27,16,128]{2,1,0:T(8,128)S(1)}, f32[27,16,128]{2,1,0:T(8,128)}, u32[]{:S(2)}) copy-start(f32[27,16,128]{2,1,0:T(8,128)} %coefficients.1.coef) | copy-start | bytes 663556
  67.2 2.6 %collective-permute-start.6 = (bf16[64,512]{1,0:T(8,128)(2,1)S(1)}, bf16[64,512]{1,0:T(8,128)(2,1)S(1)}, u32[]{:S(2)}, u32[]{:S(2)}) collective-permute-start(bf16[64,512]{1,0:T(8,128)(2,1)S(1)} %pad_maximum_fusion.3), channel_id=1, source_target_pairs={{0,1},{1,2},{2,3},{4,5},{5,6},{6,7},{8,9},{9,10},{10,11},{12,13},{... | collective-permute-start | bytes 196616 | tf_op jit(solution)/shard_map/ppermute | solution.py:33
  68.5 4.6 %collective-permute-start.7 = (bf16[64,512]{1,0:T(8,128)(2,1)S(1)}, bf16[64,512]{1,0:T(8,128)(2,1)S(1)}, u32[]{:S(2)}, u32[]{:S(2)}) collective-permute-start(bf16[64,512]{1,0:T(8,128)(2,1)S(1)} %pad_maximum_fusion.4), channel_id=1, source_target_pairs={{1,0},{2,1},{3,2},{5,4},{6,5},{7,6},{9,8},{10,9},{11,10},{13,12},{... | collective-permute-start | bytes 196616 | tf_op jit(solution)/shard_map/ppermute | solution.py:33

commit v2 on v1

--- a/solution.py
+++ b/solution.py
@@ -120,15 +120,19 @@
     lax.fori_loop(0, columns // ROWS, tile, 0)
 
 
-def first_image_kernel(spans, coef, stack, xlo, xhi, ylo, yhi, image, cross, own):
+def first_image_kernel(spans, coef, stack, xlo, xhi, ylo, yhi, image, cross):
     columns = image.shape[0]
     fields = stack.shape[0]
     block = stack.at[fields - columns : fields]
     stencil_into(image, coef, block, xlo, xhi, ylo, yhi, *spans)
     w = image[...]
     cross[:, :fields] = dot(w, stack[...], NT)
-    cross[:, fields:] = dot(w, w, NT)
-    own[...] = dot(stack[...], stack[...], NT)
+    cross[:, fields : fields + columns] = dot(w, w, NT)
+    at = fields + columns
+    for b in range(0, fields, columns):
+        width = fields - b
+        cross[:, at : at + width] = dot(stack[b : b + columns], stack[b:], NT)
+        at += width
 
 
 def second_image_kernel(spans, coef, stack, block, xlo, xhi, ylo, yhi, image, cross):
@@ -180,11 +184,26 @@
     return first_low, second_low, first + second, rest, square
 
 
-def first_solve_kernel(scale, cross, own, stack, image, block, proj, low, own_next):
+def unpacked(upper, columns, fields):
+    rows, at = [], 0
+    for b in range(0, fields, columns):
+        rows.append((b, upper[:, at : at + fields - b]))
+        at += fields - b
+    whole = []
+    for b, row in rows:
+        left = [above[:, b - a : b - a + columns].T for a, above in rows if a < b]
+        whole.append(jnp.concatenate(left + [row], axis=1))
+    return jnp.concatenate(whole, axis=0)
+
+
+def first_solve_kernel(scale, cross, stack, image, block, proj, low, own_next):
     columns = image.shape[0]
-    gram = own[...] * scale
-    first_low, second_low, both, rest, square = project(cross[...], gram, scale)
-    proj[...] = both.T
+    fields = stack.shape[0]
+    gram = unpacked(cross[:, fields + columns :] * scale, columns, fields)
+    first_low, second_low, both, rest, square = project(
+        cross[:, : fields + columns], gram, scale
+    )
+    proj[...] = both
     upper, inverse = factor(square)
     low[...] = upper.T
     inverse = inverse.astype(jnp.bfloat16)
@@ -204,7 +223,7 @@
     kept = stack.shape[0] - columns
     first_low, second_low, both, _, square = project(cross[...], own[...], scale)
     proj[0] = proj_in[...]
-    proj[1] = both.T
+    proj[1] = both
     upper, inverse = factor(square)
     low[0] = low_in[...]
     low[1] = upper.T
@@ -214,19 +233,18 @@
     block[...] = dot(inverse.astype(jnp.bfloat16), w.astype(jnp.bfloat16)).astype(jnp.bfloat16)
 
 
-def whole_sum(parts):
-    axes = ("slab", "col")
-    count = lax.axis_size("slab") * lax.axis_size("col")
-    flat = jnp.concatenate([part.reshape(count, -1) for part in parts], axis=1)
-    shares = lax.all_to_all(flat, axes, 0, 0, tiled=True)
-    share = jnp.sum(shares, axis=0, keepdims=True)
-    flat = lax.all_to_all(jnp.broadcast_to(share, flat.shape), axes, 0, 0, tiled=True)
-    done, at = [], 0
-    for part in parts:
-        width = part.size // count
-        done.append(flat[:, at : at + width].reshape(part.shape))
-        at += width
-    return done
+def exchange_shares(shares, axis):
+    return lax.all_to_all(shares, axis, 0, 0, tiled=True)
+
+
+def whole_sum(part):
+    slabs, cols = lax.axis_size("slab"), lax.axis_size("col")
+    rows, width = part.shape
+    shape = (rows // slabs, width) if rows % slabs == 0 else (1, rows * width // slabs)
+    share = jnp.sum(exchange_shares(part.reshape(slabs, *shape), "slab"), axis=0)
+    share = jnp.sum(exchange_shares(jnp.broadcast_to(share, (cols, *shape)), "col"), axis=0)
+    whole = exchange_shares(jnp.broadcast_to(share, (slabs, *shape)), "slab")
+    return whole.reshape(part.shape)
 
 
 def call(kernel, name, outs, *args):
@@ -252,19 +270,19 @@
     stack = basis.reshape(fields, cells)
     coef = coefficients(table, cell_map)
     around = neighbours(stack[fields - columns :], *spans)
-    image, cross, own = call(
+    packed = fields + columns + columns * blocks * (blocks + 1) // 2
+    image, cross = call(
         functools.partial(first_image_kernel, spans),
         "first_image",
-        [((columns, cells), bf16), ((columns, fields + columns), f32), ((fields, fields), f32)],
+        [((columns, cells), bf16), ((columns, packed), f32)],
         coef, stack, *around,
     )
-    cross, own = whole_sum([cross, own])
     block, proj, low, own = call(
         functools.partial(first_solve_kernel, scale),
         "first_solve",
-        [((columns, cells), bf16), ((fields, columns), f32), ((columns, columns), f32),
+        [((columns, cells), bf16), ((columns, fields), f32), ((columns, columns), f32),
          ((fields, fields), f32)],
-        cross, own, stack, image,
+        whole_sum(cross), stack, image,
     )
     around = neighbours(block, *spans)
     image, cross = call(
@@ -273,14 +291,13 @@
         [((columns, cells), bf16), ((columns, fields + columns), f32)],
         coef, stack, block, *around,
     )
-    (cross,) = whole_sum([cross])
     block, proj, low = call(
         functools.partial(second_solve_kernel, scale),
         "second_solve",
-        [((columns, cells), bf16), ((2, fields, columns), f32), ((2, columns, columns), f32)],
-        cross, own, stack, block, image, proj, low,
-    )
-    return block.reshape(columns, *spans), proj, low
+        [((columns, cells), bf16), ((2, columns, fields), f32), ((2, columns, columns), f32)],
+        whole_sum(cross), own, stack, block, image, proj, low,
+    )
+    return block.reshape(columns, *spans), jnp.swapaxes(proj, 1, 2), low
 
 
 def solution(mesh):

time: 106 us -> 113 us (1.066)
  blocking collectives: 50.8 us -> 60.1 us
  local copies, waits for them, and re-layouts: 4.62 us -> 3.21 us
  waiting for transfers between devices: 11.9 us -> 10.7 us
    all_to_all x4 -> x6, blocking collectives: 50.8 us -> 60.1 us  [exchange_shares(): return lax.all_to_all(shares, axis, 0, 0, tiled=True)]
    ppermute x4, waiting for transfers between devices: 7.57 us -> 6.22 us  [exchange(): lax.ppermute(downward, axis, backward)]
    unnamed x9 -> x7, local copies, waits for them, and re-layouts: 2.48 us -> 1.69 us
where the time goes in v2:
time: 113 us; the launch traced here: 112 us
  blocking collectives  60.1 us (53%)
  Pallas kernels  19 us (17%)
  starting transfers between devices  18.6 us (16%)
  waiting for transfers between devices  10.7 us (9%)
  local copies, waits for them, and re-layouts  3.21 us (3%)
    all_to_all x6, blocking collectives, exchange_shares(): return lax.all_to_all(shares, axis, 0, 0, tiled=True)  60.1 us
    pallas_call x4, Pallas kernels, call(): pl.pallas_call(kernel, out_shape=[jax.ShapeDtypeStruct(shape, dtype) for...  17.4 us
    ppermute x4, starting transfers between devices, exchange(): lax.ppermute(upward, axis, forward)  13.2 us
    ppermute x4, waiting for transfers between devices, exchange(): lax.ppermute(downward, axis, backward)  6.22 us
    ppermute x4, starting transfers between devices, exchange(): lax.ppermute(downward, axis, backward)  5.3 us
    ppermute x4, waiting for transfers between devices, exchange(): lax.ppermute(upward, axis, forward)  4.45 us
  transfers between devices with their start and end apart: 8, of which 6 were waited for; matrix products, arithmetic and copies ran while one was open for 0% of the time, Pallas kernels for 1%

profile of v2, /device:TPU:0, one launch (start us, length us, event | category | flops | bytes accessed | tf_op | source)
XLA Modules:
  0.0 112.4 jit_solution(8204569489059750009)
XLA Ops:
  0.6 0.0 slice-start
  0.6 0.9 slice-done
  1.6 0.0 copy-start.2
  1.6 0.1 slice.67
  1.7 1.4 %collective-permute-start.1 = (bf16[64,1024]{1,0:T(8,128)(2,1)S(1)}, bf16[64,1024]{1,0:T(8,128)(2,1)S(1)}, u32[]{:S(2)}, u32[]{:S(2)}) collective-permute-start(bf16[64,1024]{1,0:T(8,128)(2,1)S(1)} %get-tuple-element.35), channel_id=1, source_target_pairs={{4,0},{8,4},{12,8},{16,12},{20,16},{24,20},{28,24},{5,1},{9,5},{13... | collective-permute-start | bytes 393224 | tf_op jit(solution)/shard_map/ppermute | solution.py:33
  3.2 5.5 %collective-permute-start = (bf16[64,1024]{1,0:T(8,128)(2,1)S(1)}, bf16[64,1024]{1,0:T(8,128)(2,1)S(1)}, u32[]{:S(2)}, u32[]{:S(2)}) collective-permute-start(bf16[64,1024]{1,0:T(8,128)(2,1)S(1)} %get-tuple-element.36), channel_id=1, source_target_pairs={{0,4},{4,8},{8,12},{12,16},{16,20},{20,24},{24,28},{1,5},{5,9},{9,... | collective-permute-start | bytes 393224 | tf_op jit(solution)/shard_map/ppermute | solution.py:33
  8.7 1.5 %collective-permute-done.1.xhi = bf16[64,1024]{1,0:T(8,128)(2,1)S(1)} collective-permute-done((bf16[64,1024]{1,0:T(8,128)(2,1)S(1)}, bf16[64,1024]{1,0:T(8,128)(2,1)S(1)}, u32[]{:S(2)}, u32[]{:S(2)}) %collective-permute-start.1) | collective-permute-done | bytes 131104 | tf_op jit(solution)/shard_map/ppermute | solution.py:33
  10.2 3.0 %collective-permute-done.xlo = bf16[64,1024]{1,0:T(8,128)(2,1)S(1)} collective-permute-done((bf16[64,1024]{1,0:T(8,128)(2,1)S(1)}, bf16[64,1024]{1,0:T(8,128)(2,1)S(1)}, u32[]{:S(2)}, u32[]{:S(2)}) %collective-permute-start) | collective-permute-done | bytes 131104 | tf_op jit(solution)/shard_map/ppermute | solution.py:33
  13.2 1.9 %collective-permute-start.2 = (bf16[64,512]{1,0:T(8,128)(2,1)S(1)}, bf16[64,512]{1,0:T(8,128)(2,1)S(1)}, u32[]{:S(2)}, u32[]{:S(2)}) collective-permute-start(bf16[64,512]{1,0:T(8,128)(2,1)S(1)} %pad_maximum_fusion), channel_id=1, source_target_pairs={{0,1},{1,2},{2,3},{4,5},{5,6},{6,7},{8,9},{9,10},{10,11},{12,13},{... | collective-permute-start | bytes 196616 | tf_op jit(solution)/shard_map/ppermute | solution.py:33
  15.1 1.3 %collective-permute-start.3 = (bf16[64,512]{1,0:T(8,128)(2,1)S(1)}, bf16[64,512]{1,0:T(8,128)(2,1)S(1)}, u32[]{:S(2)}, u32[]{:S(2)}) collective-permute-start(bf16[64,512]{1,0:T(8,128)(2,1)S(1)} %pad_maximum_fusion.1), channel_id=1, source_target_pairs={{1,0},{2,1},{3,2},{5,4},{6,5},{7,6},{9,8},{10,9},{11,10},{13,12},{... | collective-permute-start | bytes 196616 | tf_op jit(solution)/shard_map/ppermute | solution.py:33
  16.4 0.0 copy-done.2
  16.4 0.3 reshape.29.stack
  16.8 1.6 %coefficients.1.coef = f32[27,16,128]{2,1,0:T(8,128)} custom-call(f32[8,27]{1,0:T(8,128)} %table.1, s32[16,128]{1,0:T(8,128)} %bitcast.19), custom_call_target="tpu_custom_call" | custom-call | tf_op jit(solution)/shard_map/coefficients/pallas_call | solution.py:72
  18.3 0.0 collective-permute-done.2.ylo
  18.3 1.0 collective-permute-done.3.yhi
  19.4 0.0 copy-start
  19.4 0.9 copy-done
  20.3 1.9 %first_image.1 = (bf16[64,2048]{1,0:T(8,128)(2,1)S(1)}, f32[64,640]{1,0:T(8,128)S(1)}) custom-call(f32[27,16,128]{2,1,0:T(8,128)S(1)} %copy-done, bf16[192,2048]{1,0:T(8,128)(2,1)S(1)} %reshape.29.stack, bf16[64,1024]{1,0:T(8,128)(2,1)S(1)} %collective-permute-done.xlo, bf16[64,1024]{1,0:T(8,128)(2,1)S(1)} %collective-permute-done.1.xhi, ...), custom_call_target="tpu_custom_call" | custom-call | tf_op jit(solution)/shard_map/first_image/pallas_call | solution.py:251
  22.3 13.5 %all_to_all.30 = f32[8,8,640]{2,1,0:T(8,128)S(1)} all-to-all(f32[8,8,640]{2,1,0:T(8,128)S(1)} %bitcast.16), channel_id=1, replica_groups=mesh['slab'=8,'col'=4] {'slab'}, dimensions={0} | all-to-all | bytes 327680 | tf_op jit(solution)/shard_map/all_to_all | solution.py:237
  35.8 8.0 %all_to_all.31 = f32[4,8,640]{2,1,0:T(8,128)S(1)} all-to-all(f32[4,8,640]{2,1,0:T(8,128)S(1)} %broadcast_in_dim.12), channel_id=1, replica_groups=mesh['slab'=8,'col'=4] {'col'}, dimensions={0} | all-to-all | bytes 163840 | tf_op jit(solution)/shard_map/all_to_all | solution.py:237
  43.9 10.0 %all_to_all.32 = f32[8,8,640]{2,1,0:T(8,128)S(1)} all-to-all(f32[8,8,640]{2,1,0:T(8,128)S(1)} %broadcast_in_dim.13), channel_id=1, replica_groups=mesh['slab'=8,'col'=4] {'slab'}, dimensions={0} | all-to-all | bytes 327680 | tf_op jit(solution)/shard_map/all_to_all | solution.py:237
  53.9 7.0 %first_solve.1 = (bf16[64,2048]{1,0:T(8,128)(2,1)S(1)}, f32[64,192]{1,0:T(8,128)S(1)}, f32[64,64]{1,0:T(8,128)S(1)}, f32[192,192]{1,0:T(8,128)S(1)}) custom-call(f32[64,640]{1,0:T(8,128)S(1)} %bitcast.13, bf16[192,2048]{1,0:T(8,128)(2,1)S(1)} %reshape.29.stack, bf16[64,2048]{1,0:T(8,128)(2,1)S(1)} %get-tuple-element.15.image), custom_call_target="tpu_custom_call" | custom-call | tf_op jit(solution)/shard_map/first_solve/pallas_call | solution.py:251
  60.8 1.3 %collective-permute-start.5 = (bf16[64,1024]{1,0:T(8,128)(2,1)S(1)}, bf16[64,1024]{1,0:T(8,128)(2,1)S(1)}, u32[]{:S(2)}, u32[]{:S(2)}) collective-permute-start(bf16[64,1024]{1,0:T(8,128)(2,1)S(1)} %get-tuple-element.29), channel_id=1, source_target_pairs={{4,0},{8,4},{12,8},{16,12},{20,16},{24,20},{28,24},{5,1},{9,5},{13... | collective-permute-start | bytes 393224 | tf_op jit(solution)/shard_map/ppermute | solution.py:33
  62.1 4.6 %collective-permute-start.4 = (bf16[64,1024]{1,0:T(8,128)(2,1)S(1)}, bf16[64,1024]{1,0:T(8,128)(2,1)S(1)}, u32[]{:S(2)}, u32[]{:S(2)}) collective-permute-start(bf16[64,1024]{1,0:T(8,128)(2,1)S(1)} %get-tuple-element.30), channel_id=1, source_target_pairs={{0,4},{4,8},{8,12},{12,16},{16,20},{20,24},{24,28},{1,5},{5,9},{9,... | collective-permute-start | bytes 393224 | tf_op jit(solution)/shard_map/ppermute | solution.py:33
  66.7 0.0 copy-start.1
  66.7 1.0 collective-permute-done.5.xhi
  67.7 1.5 %collective-permute-done.4.xlo = bf16[64,1024]{1,0:T(8,128)(2,1)S(1)} collective-permute-done((bf16[64,1024]{1,0:T(8,128)(2,1)S(1)}, bf16[64,1024]{1,0:T(8,128)(2,1)S(1)}, u32[]{:S(2)}, u32[]{:S(2)}) %collective-permute-start.4) | collective-permute-done | bytes 131104 | tf_op jit(solution)/shard_map/ppermute | solution.py:33
  69.2 1.3 %collective-permute-start.6 = (bf16[64,512]{1,0:T(8,128)(2,1)S(1)}, bf16[64,512]{1,0:T(8,128)(2,1)S(1)}, u32[]{:S(2)}, u32[]{:S(2)}) collective-permute-start(bf16[64,512]{1,0:T(8,128)(2,1)S(1)} %pad_maximum_fusion.2), channel_id=1, source_target_pairs={{0,1},{1,2},{2,3},{4,5},{5,6},{6,7},{8,9},{9,10},{10,11},{12,13},{... | collective-permute-start | bytes 196616 | tf_op jit(solution)/shard_map/ppermute | solution.py:33
  70.5 1.3 %collective-permute-start.7 = (bf16[64,512]{1,0:T(8,128)(2,1)S(1)}, bf16[64,512]{1,0:T(8,128)(2,1)S(1)}, u32[]{:S(2)}, u32[]{:S(2)}) collective-permute-start(bf16[64,512]{1,0:T(8,128)(2,1)S(1)} %pad_maximum_fusion.3), channel_id=1, source_target_pairs={{1,0},{2,1},{3,2},{5,4},{6,5},{7,6},{9,8},{10,9},{11,10},{13,12},{... | collective-permute-start | bytes 196616 | tf_op jit(solution)/shard_map/ppermute | solution.py:33
  71.8 0.0 collective-permute-done.6.ylo
  71.8 2.7 %collective-permute-done.7.yhi = bf16[64,512]{1,0:T(8,128)(2,1)S(1)} collective-permute-done((bf16[64,512]{1,0:T(8,128)(2,1)S(1)}, bf16[64,512]{1,0:T(8,128)(2,1)S(1)}, u32[]{:S(2)}, u32[]{:S(2)}) %collective-permute-start.7) | collective-permute-done | bytes 65568 | tf_op jit(solution)/shard_map/ppermute | solution.py:33
  74.5 0.0 copy-done.1
  74.5 1.5 %second_image.1 = (bf16[64,2048]{1,0:T(8,128)(2,1)S(1)}, f32[64,256]{1,0:T(8,128)S(1)}) custom-call(f32[27,16,128]{2,1,0:T(8,128)S(1)} %copy-done.1, bf16[192,2048]{1,0:T(8,128)(2,1)S(1)} %reshape.29.stack, bf16[64,2048]{1,0:T(8,128)(2,1)S(1)} %get-tuple-element.16.block.last, bf16[64,1024]{1,0:T(8,128)(2,1)S(1)} %collective-permute-done.4.xlo, ...), custom_call_target="tpu_custom_call" | custom-call | tf_op jit(solution)/shard_map/second_image/pallas_call | solution.py:251
  76.0 11.5 %all_to_all.33 = f32[8,8,256]{2,1,0:T(8,128)S(1)} all-to-all(f32[8,8,256]{2,1,0:T(8,128)S(1)} %bitcast.17), channel_id=1, replica_groups=mesh['slab'=8,'col'=4] {'slab'}, dimensions={0} | all-to-all | bytes 131072 | tf_op jit(solution)/shard_map/all_to_all | solution.py:237
  87.5 7.8 %all_to_all.34 = f32[4,8,256]{2,1,0:T(8,128)S(1)} all-to-all(f32[4,8,256]{2,1,0:T(8,128)S(1)} %broadcast_in_dim.14), channel_id=1, replica_groups=mesh['slab'=8,'col'=4] {'col'}, dimensions={0} | all-to-all | bytes 65536 | tf_op jit(solution)/shard_map/all_to_all | solution.py:237
  95.3 9.3 %all_to_all.35 = f32[8,8,256]{2,1,0:T(8,128)S(1)} all-to-all(f32[8,8,256]{2,1,0:T(8,128)S(1)} %broadcast_in_dim.15), channel_id=1, replica_groups=mesh['slab'=8,'col'=4] {'slab'}, dimensions={0} | all-to-all | bytes 131072 | tf_op jit(solution)/shard_map/all_to_all | solution.py:237
  104.6 7.1 %second_solve.1 = (bf16[64,2048]{1,0:T(8,128)(2,1)S(1)}, f32[2,64,192]{2,1,0:T(8,128)}, f32[2,64,64]{2,1,0:T(8,128)}) custom-call(f32[64,256]{1,0:T(8,128)S(1)} %bitcast.14, f32[192,192]{1,0:T(8,128)S(1)} %get-tuple-element.18.own, bf16[192,2048]{1,0:T(8,128)(2,1)S(1)} %reshape.29.stack, bf16[64,2048]{1,0:T(8,128)(2,1)S(1)} %get-tuple-element.16.block.last, ...), custom_call_target="tpu_custom_call" | custom-call | tf_op jit(solution)/shard_map/second_solve/pallas_call | solution.py:251
  111.7 0.7 copy.6
  (20 shorter events, 0.2 us)
Async XLA Ops:
  0.6 1.0 slice-start
  1.6 14.8 %copy-start.2 = (bf16[3,64,2,8,128]{4,3,2,1,0:T(8,128)(2,1)S(1)}, bf16[3,64,2,8,128]{4,3,2,1,0:T(8,128)(2,1)}, u32[]{:S(2)}) copy-start(bf16[3,64,2,8,128]{4,3,2,1,0:T(8,128)(2,1)} %param.3) | copy-start | bytes 2359300
  1.7 8.5 %collective-permute-start.1 = (bf16[64,1024]{1,0:T(8,128)(2,1)S(1)}, bf16[64,1024]{1,0:T(8,128)(2,1)S(1)}, u32[]{:S(2)}, u32[]{:S(2)}) collective-permute-start(bf16[64,1024]{1,0:T(8,128)(2,1)S(1)} %get-tuple-element.35), channel_id=1, source_target_pairs={{4,0},{8,4},{12,8},{16,12},{20,16},{24,20},{28,24},{5,1},{9,5},{13... | collective-permute-start | bytes 393224 | tf_op jit(solution)/shard_map/ppermute | solution.py:33
  3.2 10.0 %collective-permute-start = (bf16[64,1024]{1,0:T(8,128)(2,1)S(1)}, bf16[64,1024]{1,0:T(8,128)(2,1)S(1)}, u32[]{:S(2)}, u32[]{:S(2)}) collective-permute-start(bf16[64,1024]{1,0:T(8,128)(2,1)S(1)} %get-tuple-element.36), channel_id=1, source_target_pairs={{0,4},{4,8},{8,12},{12,16},{16,20},{20,24},{24,28},{1,5},{5,9},{9,... | collective-permute-start | bytes 393224 | tf_op jit(solution)/shard_map/ppermute | solution.py:33
  13.2 5.2 %collective-permute-start.2 = (bf16[64,512]{1,0:T(8,128)(2,1)S(1)}, bf16[64,512]{1,0:T(8,128)(2,1)S(1)}, u32[]{:S(2)}, u32[]{:S(2)}) collective-permute-start(bf16[64,512]{1,0:T(8,128)(2,1)S(1)} %pad_maximum_fusion), channel_id=1, source_target_pairs={{0,1},{1,2},{2,3},{4,5},{5,6},{6,7},{8,9},{9,10},{10,11},{12,13},{... | collective-permute-start | bytes 196616 | tf_op jit(solution)/shard_map/ppermute | solution.py:33
  15.1 4.3 %collective-permute-start.3 = (bf16[64,512]{1,0:T(8,128)(2,1)S(1)}, bf16[64,512]{1,0:T(8,128)(2,1)S(1)}, u32[]{:S(2)}, u32[]{:S(2)}) collective-permute-start(bf16[64,512]{1,0:T(8,128)(2,1)S(1)} %pad_maximum_fusion.1), channel_id=1, source_target_pairs={{1,0},{2,1},{3,2},{5,4},{6,5},{7,6},{9,8},{10,9},{11,10},{13,12},{... | collective-permute-start | bytes 196616 | tf_op jit(solution)/shard_map/ppermute | solution.py:33
  19.4 0.9 copy-start
  60.8 6.9 %collective-permute-start.5 = (bf16[64,1024]{1,0:T(8,128)(2,1)S(1)}, bf16[64,1024]{1,0:T(8,128)(2,1)S(1)}, u32[]{:S(2)}, u32[]{:S(2)}) collective-permute-start(bf16[64,1024]{1,0:T(8,128)(2,1)S(1)} %get-tuple-element.29), channel_id=1, source_target_pairs={{4,0},{8,4},{12,8},{16,12},{20,16},{24,20},{28,24},{5,1},{9,5},{13... | collective-permute-start | bytes 393224 | tf_op jit(solution)/shard_map/ppermute | solution.py:33
  62.1 7.1 %collective-permute-start.4 = (bf16[64,1024]{1,0:T(8,128)(2,1)S(1)}, bf16[64,1024]{1,0:T(8,128)(2,1)S(1)}, u32[]{:S(2)}, u32[]{:S(2)}) collective-permute-start(bf16[64,1024]{1,0:T(8,128)(2,1)S(1)} %get-tuple-element.30), channel_id=1, source_target_pairs={{0,4},{4,8},{8,12},{12,16},{16,20},{20,24},{24,28},{1,5},{5,9},{9,... | collective-permute-start | bytes 393224 | tf_op jit(solution)/shard_map/ppermute | solution.py:33
  66.7 7.8 %copy-start.1 = (f32[27,16,128]{2,1,0:T(8,128)S(1)}, f32[27,16,128]{2,1,0:T(8,128)}, u32[]{:S(2)}) copy-start(f32[27,16,128]{2,1,0:T(8,128)} %coefficients.1.coef) | copy-start | bytes 663556
  69.2 2.6 %collective-permute-start.6 = (bf16[64,512]{1,0:T(8,128)(2,1)S(1)}, bf16[64,512]{1,0:T(8,128)(2,1)S(1)}, u32[]{:S(2)}, u32[]{:S(2)}) collective-permute-start(bf16[64,512]{1,0:T(8,128)(2,1)S(1)} %pad_maximum_fusion.2), channel_id=1, source_target_pairs={{0,1},{1,2},{2,3},{4,5},{5,6},{6,7},{8,9},{9,10},{10,11},{12,13},{... | collective-permute-start | bytes 196616 | tf_op jit(solution)/shard_map/ppermute | solution.py:33
  70.5 4.0 %collective-permute-start.7 = (bf16[64,512]{1,0:T(8,128)(2,1)S(1)}, bf16[64,512]{1,0:T(8,128)(2,1)S(1)}, u32[]{:S(2)}, u32[]{:S(2)}) collective-permute-start(bf16[64,512]{1,0:T(8,128)(2,1)S(1)} %pad_maximum_fusion.3), channel_id=1, source_target_pairs={{1,0},{2,1},{3,2},{5,4},{6,5},{7,6},{9,8},{10,9},{11,10},{13,12},{... | collective-permute-start | bytes 196616 | tf_op jit(solution)/shard_map/ppermute | solution.py:33

commit v3 on v2

--- a/solution.py
+++ b/solution.py
@@ -233,18 +233,12 @@
     block[...] = dot(inverse.astype(jnp.bfloat16), w.astype(jnp.bfloat16)).astype(jnp.bfloat16)
 
 
-def exchange_shares(shares, axis):
-    return lax.all_to_all(shares, axis, 0, 0, tiled=True)
-
-
 def whole_sum(part):
-    slabs, cols = lax.axis_size("slab"), lax.axis_size("col")
-    rows, width = part.shape
-    shape = (rows // slabs, width) if rows % slabs == 0 else (1, rows * width // slabs)
-    share = jnp.sum(exchange_shares(part.reshape(slabs, *shape), "slab"), axis=0)
-    share = jnp.sum(exchange_shares(jnp.broadcast_to(share, (cols, *shape)), "col"), axis=0)
-    whole = exchange_shares(jnp.broadcast_to(share, (slabs, *shape)), "slab")
-    return whole.reshape(part.shape)
+    axes = ("slab", "col")
+    count = lax.axis_size("slab") * lax.axis_size("col")
+    shares = lax.all_to_all(part.reshape(count, -1), axes, 0, 0, tiled=True)
+    share = jnp.sum(shares, axis=0, keepdims=True)
+    return lax.all_gather(share, axes, axis=0, tiled=True).reshape(part.shape)
 
 
 def call(kernel, name, outs, *args):

time: 113 us -> 159 us (1.41)
  blocking collectives: 60.1 us -> 105 us
    all_gather x0 -> x2, blocking collectives: none -> 76.2 us  [whole_sum(): return lax.all_gather(share, axes, axis=0, tiled=True).reshape(part.shape)]
    all_to_all x6 -> x2, blocking collectives: 60.1 us -> 28.7 us  [whole_sum(): shares = lax.all_to_all(part.reshape(count, -1), axes, 0, 0, tiled=True)]
where the time goes in v3:
time: 159 us; the launch traced here: 158 us
  blocking collectives  105 us (66%)
  Pallas kernels  19 us (12%)
  starting transfers between devices  18.5 us (12%)
  waiting for transfers between devices  10.6 us (7%)
  local copies, waits for them, and re-layouts  3.46 us (2%)
    all_gather x2, blocking collectives, whole_sum(): return lax.all_gather(share, axes, axis=0, tiled=True).reshape(part.shape)  76.2 us
    all_to_all x2, blocking collectives, whole_sum(): shares = lax.all_to_all(part.reshape(count, -1), axes, 0, 0, tiled=True)  28.7 us
    pallas_call x4, Pallas kernels, call(): pl.pallas_call(kernel, out_shape=[jax.ShapeDtypeStruct(shape, dtype) for...  17.5 us
    ppermute x4, starting transfers between devices, exchange(): lax.ppermute(upward, axis, forward)  13.2 us
    ppermute x4, waiting for transfers between devices, exchange(): lax.ppermute(downward, axis, backward)  6.48 us
    ppermute x4, starting transfers between devices, exchange(): lax.ppermute(downward, axis, backward)  5.3 us
    ppermute x4, waiting for transfers between devices, exchange(): lax.ppermute(upward, axis, forward)  4.13 us
  transfers between devices with their start and end apart: 8, of which 6 were waited for; matrix products, arithmetic and copies ran while one was open for 0% of the time, Pallas kernels for 1%

profile of v3, /device:TPU:0, one launch (start us, length us, event | category | flops | bytes accessed | tf_op | source)
XLA Modules:
  0.0 158.1 jit_solution(15869259117327617635)
XLA Ops:
  0.6 0.0 slice-start
  0.6 0.9 slice-done
  1.6 0.0 copy-start.2
  1.6 0.1 slice.67
  1.7 1.4 collective-permute-start.1
  3.2 5.5 %collective-permute-start = (bf16[64,1024]{1,0:T(8,128)(2,1)S(1)}, bf16[64,1024]{1,0:T(8,128)(2,1)S(1)}, u32[]{:S(2)}, u32[]{:S(2)}) collective-permute-start(bf16[64,1024]{1,0:T(8,128)(2,1)S(1)} %get-tuple-element.36), channel_id=1, source_target_pairs={{0,4},{4,8},{8,12},{12,16},{16,20},{20,24},{24,28},{1,5},{5,9},{9,... | collective-permute-start | bytes 393224 | tf_op jit(solution)/shard_map/ppermute | solution.py:33
  8.7 1.5 collective-permute-done.1.xhi
  10.2 3.0 %collective-permute-done.xlo = bf16[64,1024]{1,0:T(8,128)(2,1)S(1)} collective-permute-done((bf16[64,1024]{1,0:T(8,128)(2,1)S(1)}, bf16[64,1024]{1,0:T(8,128)(2,1)S(1)}, u32[]{:S(2)}, u32[]{:S(2)}) %collective-permute-start) | collective-permute-done | bytes 131104 | tf_op jit(solution)/shard_map/ppermute | solution.py:33
  13.2 1.9 %collective-permute-start.2 = (bf16[64,512]{1,0:T(8,128)(2,1)S(1)}, bf16[64,512]{1,0:T(8,128)(2,1)S(1)}, u32[]{:S(2)}, u32[]{:S(2)}) collective-permute-start(bf16[64,512]{1,0:T(8,128)(2,1)S(1)} %pad_maximum_fusion), channel_id=1, source_target_pairs={{0,1},{1,2},{2,3},{4,5},{5,6},{6,7},{8,9},{9,10},{10,11},{12,13},{... | collective-permute-start | bytes 196616 | tf_op jit(solution)/shard_map/ppermute | solution.py:33
  15.1 1.3 collective-permute-start.3
  16.4 0.0 copy-done.2
  16.4 0.3 reshape.31.stack
  16.8 1.6 coefficients.1.coef
  18.3 0.0 collective-permute-done.2.ylo
  18.3 1.0 collective-permute-done.3.yhi
  19.4 0.0 copy-start
  19.4 0.9 copy-done
  20.3 1.9 %first_image.1 = (bf16[64,2048]{1,0:T(8,128)(2,1)S(1)}, f32[64,640]{1,0:T(8,128)S(1)}) custom-call(f32[27,16,128]{2,1,0:T(8,128)S(1)} %copy-done, bf16[192,2048]{1,0:T(8,128)(2,1)S(1)} %reshape.31.stack, bf16[64,1024]{1,0:T(8,128)(2,1)S(1)} %collective-permute-done.xlo, bf16[64,1024]{1,0:T(8,128)(2,1)S(1)} %collective-permute-done.1.xhi, ...), custom_call_target="tpu_custom_call" | custom-call | tf_op jit(solution)/shard_map/first_image/pallas_call | solution.py:245
  22.3 0.2 all_to_all.16
  22.4 16.1 %all_to_all.20 = f32[32,1,1280]{2,1,0:T(1,128)S(1)} all-to-all(f32[32,1,1280]{2,1,0:T(1,128)S(1)} %all_to_all.16), channel_id=1, replica_groups=mesh['slab'=8,'col'=4] {'slab','col'}, dimensions={0} | all-to-all | bytes 327680 | tf_op jit(solution)/shard_map/all_to_all | solution.py:239
  38.5 0.1 reduce_sum.18
  38.6 38.7 %all-gather.2 = f32[32,1,1280]{2,1,0:T(1,128)S(1)} all-gather(f32[1,1,1280]{2,1,0:T(1,128)S(1)} %reshape.39), channel_id=2, replica_groups=mesh['slab'=8,'col'=4] {'slab','col'}, dimensions={0}, use_global_device_ids=true | all-gather | bytes 168960 | tf_op jit(solution)/shard_map/all_gather | solution.py:241
  77.3 0.4 reduce.2
  77.8 7.0 %first_solve.1 = (bf16[64,2048]{1,0:T(8,128)(2,1)S(1)}, f32[64,192]{1,0:T(8,128)S(1)}, f32[64,64]{1,0:T(8,128)S(1)}, f32[192,192]{1,0:T(8,128)S(1)}) custom-call(f32[64,640]{1,0:T(8,128)S(1)} %reshape.32.cross, bf16[192,2048]{1,0:T(8,128)(2,1)S(1)} %reshape.31.stack, bf16[64,2048]{1,0:T(8,128)(2,1)S(1)} %get-tuple-element.15.image), custom_call_target="tpu_custom_call" | custom-call | tf_op jit(solution)/shard_map/first_solve/pallas_call | solution.py:245
  84.8 1.3 collective-permute-start.5
  86.1 4.6 %collective-permute-start.4 = (bf16[64,1024]{1,0:T(8,128)(2,1)S(1)}, bf16[64,1024]{1,0:T(8,128)(2,1)S(1)}, u32[]{:S(2)}, u32[]{:S(2)}) collective-permute-start(bf16[64,1024]{1,0:T(8,128)(2,1)S(1)} %get-tuple-element.30), channel_id=1, source_target_pairs={{0,4},{4,8},{8,12},{12,16},{16,20},{20,24},{24,28},{1,5},{5,9},{9,... | collective-permute-start | bytes 393224 | tf_op jit(solution)/shard_map/ppermute | solution.py:33
  90.6 0.0 copy-start.1
  90.6 1.7 %collective-permute-done.5.xhi = bf16[64,1024]{1,0:T(8,128)(2,1)S(1)} collective-permute-done((bf16[64,1024]{1,0:T(8,128)(2,1)S(1)}, bf16[64,1024]{1,0:T(8,128)(2,1)S(1)}, u32[]{:S(2)}, u32[]{:S(2)}) %collective-permute-start.5) | collective-permute-done | bytes 131104 | tf_op jit(solution)/shard_map/ppermute | solution.py:33
  92.4 1.2 collective-permute-done.4.xlo
  93.6 1.3 collective-permute-start.6
  94.9 1.3 collective-permute-start.7
  96.2 0.0 collective-permute-done.6.ylo
  96.2 2.2 %collective-permute-done.7.yhi = bf16[64,512]{1,0:T(8,128)(2,1)S(1)} collective-permute-done((bf16[64,512]{1,0:T(8,128)(2,1)S(1)}, bf16[64,512]{1,0:T(8,128)(2,1)S(1)}, u32[]{:S(2)}, u32[]{:S(2)}) %collective-permute-start.7) | collective-permute-done | bytes 65568 | tf_op jit(solution)/shard_map/ppermute | solution.py:33
  98.4 0.0 copy-done.1
  98.4 1.5 second_image.1
  99.9 0.1 all_to_all.17
  100.0 12.6 %all_to_all.21 = f32[32,1,512]{2,1,0:T(1,128)S(1)} all-to-all(f32[32,1,512]{2,1,0:T(1,128)S(1)} %all_to_all.17), channel_id=1, replica_groups=mesh['slab'=8,'col'=4] {'slab','col'}, dimensions={0} | all-to-all | bytes 131072 | tf_op jit(solution)/shard_map/all_to_all | solution.py:239
  112.6 0.1 reduce_sum.19
  112.6 37.5 %all-gather.3 = f32[32,1,512]{2,1,0:T(1,128)S(1)} all-gather(f32[1,1,512]{2,1,0:T(1,128)S(1)} %bitcast.13), channel_id=3, replica_groups=mesh['slab'=8,'col'=4] {'slab','col'}, dimensions={0}, use_global_device_ids=true | all-gather | bytes 67584 | tf_op jit(solution)/shard_map/all_gather | solution.py:241
  150.1 0.2 reduce.3
  150.3 7.1 %second_solve.1 = (bf16[64,2048]{1,0:T(8,128)(2,1)S(1)}, f32[2,64,192]{2,1,0:T(8,128)}, f32[2,64,64]{2,1,0:T(8,128)}) custom-call(f32[64,256]{1,0:T(8,128)S(1)} %reshape.33.cross, f32[192,192]{1,0:T(8,128)S(1)} %get-tuple-element.18.own, bf16[192,2048]{1,0:T(8,128)(2,1)S(1)} %reshape.31.stack, bf16[64,2048]{1,0:T(8,128)(2,1)S(1)} %get-tuple-element.16.block.last, ...), custom_call_target="tpu_custom_call" | custom-call | tf_op jit(solution)/shard_map/second_solve/pallas_call | solution.py:245
  157.4 0.7 copy.8
  (15 shorter events, 0.2 us)
Async XLA Ops:
  0.6 1.0 slice-start
  1.6 14.8 %copy-start.2 = (bf16[3,64,2,8,128]{4,3,2,1,0:T(8,128)(2,1)S(1)}, bf16[3,64,2,8,128]{4,3,2,1,0:T(8,128)(2,1)}, u32[]{:S(2)}) copy-start(bf16[3,64,2,8,128]{4,3,2,1,0:T(8,128)(2,1)} %param.3) | copy-start | bytes 2359300
  1.7 8.5 %collective-permute-start.1 = (bf16[64,1024]{1,0:T(8,128)(2,1)S(1)}, bf16[64,1024]{1,0:T(8,128)(2,1)S(1)}, u32[]{:S(2)}, u32[]{:S(2)}) collective-permute-start(bf16[64,1024]{1,0:T(8,128)(2,1)S(1)} %get-tuple-element.35), channel_id=1, source_target_pairs={{4,0},{8,4},{12,8},{16,12},{20,16},{24,20},{28,24},{5,1},{9,5},{13... | collective-permute-start | bytes 393224 | tf_op jit(solution)/shard_map/ppermute | solution.py:33
  3.2 10.0 %collective-permute-start = (bf16[64,1024]{1,0:T(8,128)(2,1)S(1)}, bf16[64,1024]{1,0:T(8,128)(2,1)S(1)}, u32[]{:S(2)}, u32[]{:S(2)}) collective-permute-start(bf16[64,1024]{1,0:T(8,128)(2,1)S(1)} %get-tuple-element.36), channel_id=1, source_target_pairs={{0,4},{4,8},{8,12},{12,16},{16,20},{20,24},{24,28},{1,5},{5,9},{9,... | collective-permute-start | bytes 393224 | tf_op jit(solution)/shard_map/ppermute | solution.py:33
  13.2 5.2 %collective-permute-start.2 = (bf16[64,512]{1,0:T(8,128)(2,1)S(1)}, bf16[64,512]{1,0:T(8,128)(2,1)S(1)}, u32[]{:S(2)}, u32[]{:S(2)}) collective-permute-start(bf16[64,512]{1,0:T(8,128)(2,1)S(1)} %pad_maximum_fusion), channel_id=1, source_target_pairs={{0,1},{1,2},{2,3},{4,5},{5,6},{6,7},{8,9},{9,10},{10,11},{12,13},{... | collective-permute-start | bytes 196616 | tf_op jit(solution)/shard_map/ppermute | solution.py:33
  15.1 4.3 %collective-permute-start.3 = (bf16[64,512]{1,0:T(8,128)(2,1)S(1)}, bf16[64,512]{1,0:T(8,128)(2,1)S(1)}, u32[]{:S(2)}, u32[]{:S(2)}) collective-permute-start(bf16[64,512]{1,0:T(8,128)(2,1)S(1)} %pad_maximum_fusion.1), channel_id=1, source_target_pairs={{1,0},{2,1},{3,2},{5,4},{6,5},{7,6},{9,8},{10,9},{11,10},{13,12},{... | collective-permute-start | bytes 196616 | tf_op jit(solution)/shard_map/ppermute | solution.py:33
  19.4 0.9 copy-start
  84.8 7.6 %collective-permute-start.5 = (bf16[64,1024]{1,0:T(8,128)(2,1)S(1)}, bf16[64,1024]{1,0:T(8,128)(2,1)S(1)}, u32[]{:S(2)}, u32[]{:S(2)}) collective-permute-start(bf16[64,1024]{1,0:T(8,128)(2,1)S(1)} %get-tuple-element.29), channel_id=1, source_target_pairs={{4,0},{8,4},{12,8},{16,12},{20,16},{24,20},{28,24},{5,1},{9,5},{13... | collective-permute-start | bytes 393224 | tf_op jit(solution)/shard_map/ppermute | solution.py:33
  86.1 7.5 %collective-permute-start.4 = (bf16[64,1024]{1,0:T(8,128)(2,1)S(1)}, bf16[64,1024]{1,0:T(8,128)(2,1)S(1)}, u32[]{:S(2)}, u32[]{:S(2)}) collective-permute-start(bf16[64,1024]{1,0:T(8,128)(2,1)S(1)} %get-tuple-element.30), channel_id=1, source_target_pairs={{0,4},{4,8},{8,12},{12,16},{16,20},{20,24},{24,28},{1,5},{5,9},{9,... | collective-permute-start | bytes 393224 | tf_op jit(solution)/shard_map/ppermute | solution.py:33
  90.6 7.8 %copy-start.1 = (f32[27,16,128]{2,1,0:T(8,128)S(1)}, f32[27,16,128]{2,1,0:T(8,128)}, u32[]{:S(2)}) copy-start(f32[27,16,128]{2,1,0:T(8,128)} %coefficients.1.coef) | copy-start | bytes 663556
  93.6 2.6 %collective-permute-start.6 = (bf16[64,512]{1,0:T(8,128)(2,1)S(1)}, bf16[64,512]{1,0:T(8,128)(2,1)S(1)}, u32[]{:S(2)}, u32[]{:S(2)}) collective-permute-start(bf16[64,512]{1,0:T(8,128)(2,1)S(1)} %pad_maximum_fusion.2), channel_id=1, source_target_pairs={{0,1},{1,2},{2,3},{4,5},{5,6},{6,7},{8,9},{9,10},{10,11},{12,13},{... | collective-permute-start | bytes 196616 | tf_op jit(solution)/shard_map/ppermute | solution.py:33
  94.9 3.5 %collective-permute-start.7 = (bf16[64,512]{1,0:T(8,128)(2,1)S(1)}, bf16[64,512]{1,0:T(8,128)(2,1)S(1)}, u32[]{:S(2)}, u32[]{:S(2)}) collective-permute-start(bf16[64,512]{1,0:T(8,128)(2,1)S(1)} %pad_maximum_fusion.3), channel_id=1, source_target_pairs={{1,0},{2,1},{3,2},{5,4},{6,5},{7,6},{9,8},{10,9},{11,10},{13,12},{... | collective-permute-start | bytes 196616 | tf_op jit(solution)/shard_map/ppermute | solution.py:33

commit v4 on v3

--- a/solution.py
+++ b/solution.py
@@ -233,12 +233,31 @@
     block[...] = dot(inverse.astype(jnp.bfloat16), w.astype(jnp.bfloat16)).astype(jnp.bfloat16)
 
 
-def whole_sum(part):
-    axes = ("slab", "col")
-    count = lax.axis_size("slab") * lax.axis_size("col")
-    shares = lax.all_to_all(part.reshape(count, -1), axes, 0, 0, tiled=True)
-    share = jnp.sum(shares, axis=0, keepdims=True)
-    return lax.all_gather(share, axes, axis=0, tiled=True).reshape(part.shape)
+def partner(part, axis, bit):
+    count = lax.axis_size(axis)
+    return lax.ppermute(part, axis, [(i, i ^ bit) for i in range(count)])
+
+
+def bits(axis, first=1):
+    while first < lax.axis_size(axis):
+        yield axis, first
+        first *= 2
+
+
+def whole_sum(part, split):
+    if split:
+        half = part.shape[0] // 2
+        upper = lax.axis_index("col") % 2 == 1
+        low, high = part[:half], part[half:]
+        given = partner(jnp.where(upper, low, high), "col", 1)
+        part = jnp.where(upper, high, low) + given
+    for axis, bit in (*bits("col", 2 if split else 1), *bits("slab")):
+        part = part + partner(part, axis, bit)
+    if split:
+        other = partner(part, "col", 1)
+        low, high = jnp.where(upper, other, part), jnp.where(upper, part, other)
+        part = jnp.concatenate([low, high], axis=0)
+    return part
 
 
 def call(kernel, name, outs, *args):
@@ -276,7 +295,7 @@
         "first_solve",
         [((columns, cells), bf16), ((columns, fields), f32), ((columns, columns), f32),
          ((fields, fields), f32)],
-        whole_sum(cross), stack, image,
+        whole_sum(cross, True), stack, image,
     )
     around = neighbours(block, *spans)
     image, cross = call(
@@ -289,7 +308,7 @@
         functools.partial(second_solve_kernel, scale),
         "second_solve",
         [((columns, cells), bf16), ((2, columns, fields), f32), ((2, columns, columns), f32)],
-        whole_sum(cross), own, stack, block, image, proj, low,
+        whole_sum(cross, False), own, stack, block, image, proj, low,
     )
     return block.reshape(columns, *spans), jnp.swapaxes(proj, 1, 2), low
 

time: 159 us -> 103 us (0.65)
  blocking collectives: 105 us -> 0 us
  waiting for transfers between devices: 10.6 us -> 37.2 us
  starting transfers between devices: 18.5 us -> 42.1 us
    all_gather x2 -> x0, blocking collectives: 76.2 us -> none  [whole_sum(): return lax.all_gather(share, axes, axis=0, tiled=True).reshape(part.shape)]
    all_to_all x2 -> x0, blocking collectives: 28.7 us -> none  [whole_sum(): shares = lax.all_to_all(part.reshape(count, -1), axes, 0, 0, tiled=True)]
    ppermute x0 -> x11, waiting for transfers between devices: none -> 25.7 us  [partner(): return lax.ppermute(part, axis, [(i, i ^ bit) for i in range(count)])]
    ppermute x0 -> x11, starting transfers between devices: none -> 22.9 us  [partner(): return lax.ppermute(part, axis, [(i, i ^ bit) for i in range(count)])]
  transfers between devices with their start and end apart: 8 -> 19, of which waited for: 6 -> 17; matrix products, arithmetic and copies ran while one was open for 0% -> 0% of each run, Pallas kernels for 1% -> 2%
where the time goes in v4:
time: 103 us
  starting transfers between devices  42.1 us (41%)
  waiting for transfers between devices  37.2 us (36%)
  Pallas kernels  19 us (18%)
  local copies, waits for them, and re-layouts  3.17 us (3%)
    ppermute x11, waiting for transfers between devices, partner(): return lax.ppermute(part, axis, [(i, i ^ bit) for i in range(count)])  25.7 us
    ppermute x11, starting transfers between devices, partner(): return lax.ppermute(part, axis, [(i, i ^ bit) for i in range(count)])  22.9 us
    pallas_call x4, Pallas kernels, call(): pl.pallas_call(kernel, out_shape=[jax.ShapeDtypeStruct(shape, dtype) for...  17.5 us
    ppermute x4, starting transfers between devices, exchange(): lax.ppermute(upward, axis, forward)  13.9 us
    ppermute x4, waiting for transfers between devices, exchange(): lax.ppermute(downward, axis, backward)  5.96 us
    ppermute x4, waiting for transfers between devices, exchange(): lax.ppermute(upward, axis, forward)  5.57 us
    ppermute x4, starting transfers between devices, exchange(): lax.ppermute(downward, axis, backward)  5.3 us
  transfers between devices with their start and end apart: 19, of which 17 were waited for; matrix products, arithmetic and copies ran while one was open for 0% of the time, Pallas kernels for 2%

profile of v4, /device:TPU:0, one launch (start us, length us, event | category | flops | bytes accessed | tf_op | source)
XLA Modules:
  0.0 102.6 jit_solution(11987262358990108414)
XLA Ops:
  0.6 0.0 slice-start
  0.6 0.9 slice-done
  1.6 0.0 copy-start.1
  1.6 0.1 slice.73
  1.7 1.4 %collective-permute-start.1 = (bf16[64,1024]{1,0:T(8,128)(2,1)S(1)}, bf16[64,1024]{1,0:T(8,128)(2,1)S(1)}, u32[]{:S(2)}, u32[]{:S(2)}) collective-permute-start(bf16[64,1024]{1,0:T(8,128)(2,1)S(1)} %get-tuple-element.35), channel_id=1, source_target_pairs={{4,0},{8,4},{12,8},{16,12},{20,16},{24,20},{28,24},{5,1},{9,5},{13... | collective-permute-start | bytes 393224 | tf_op jit(solution)/shard_map/ppermute | solution.py:33
  3.2 5.5 %collective-permute-start = (bf16[64,1024]{1,0:T(8,128)(2,1)S(1)}, bf16[64,1024]{1,0:T(8,128)(2,1)S(1)}, u32[]{:S(2)}, u32[]{:S(2)}) collective-permute-start(bf16[64,1024]{1,0:T(8,128)(2,1)S(1)} %get-tuple-element.36), channel_id=1, source_target_pairs={{0,4},{4,8},{8,12},{12,16},{16,20},{20,24},{24,28},{1,5},{5,9},{9,... | collective-permute-start | bytes 393224 | tf_op jit(solution)/shard_map/ppermute | solution.py:33
  8.7 1.5 %collective-permute-done.1.xhi = bf16[64,1024]{1,0:T(8,128)(2,1)S(1)} collective-permute-done((bf16[64,1024]{1,0:T(8,128)(2,1)S(1)}, bf16[64,1024]{1,0:T(8,128)(2,1)S(1)}, u32[]{:S(2)}, u32[]{:S(2)}) %collective-permute-start.1) | collective-permute-done | bytes 131104 | tf_op jit(solution)/shard_map/ppermute | solution.py:33
  10.2 3.0 %collective-permute-done.xlo = bf16[64,1024]{1,0:T(8,128)(2,1)S(1)} collective-permute-done((bf16[64,1024]{1,0:T(8,128)(2,1)S(1)}, bf16[64,1024]{1,0:T(8,128)(2,1)S(1)}, u32[]{:S(2)}, u32[]{:S(2)}) %collective-permute-start) | collective-permute-done | bytes 131104 | tf_op jit(solution)/shard_map/ppermute | solution.py:33
  13.2 1.9 %collective-permute-start.2 = (bf16[64,512]{1,0:T(8,128)(2,1)S(1)}, bf16[64,512]{1,0:T(8,128)(2,1)S(1)}, u32[]{:S(2)}, u32[]{:S(2)}) collective-permute-start(bf16[64,512]{1,0:T(8,128)(2,1)S(1)} %pad_maximum_fusion.1), channel_id=1, source_target_pairs={{0,1},{1,2},{2,3},{4,5},{5,6},{6,7},{8,9},{9,10},{10,11},{12,13},{... | collective-permute-start | bytes 196616 | tf_op jit(solution)/shard_map/ppermute | solution.py:33
  15.1 1.3 %collective-permute-start.3 = (bf16[64,512]{1,0:T(8,128)(2,1)S(1)}, bf16[64,512]{1,0:T(8,128)(2,1)S(1)}, u32[]{:S(2)}, u32[]{:S(2)}) collective-permute-start(bf16[64,512]{1,0:T(8,128)(2,1)S(1)} %pad_maximum_fusion.2), channel_id=1, source_target_pairs={{1,0},{2,1},{3,2},{5,4},{6,5},{7,6},{9,8},{10,9},{11,10},{13,12},{... | collective-permute-start | bytes 196616 | tf_op jit(solution)/shard_map/ppermute | solution.py:33
  16.4 0.0 copy-done.1
  16.4 0.3 reshape.17.stack
  16.8 1.6 %coefficients.1.coef = f32[27,16,128]{2,1,0:T(8,128)} custom-call(f32[8,27]{1,0:T(8,128)} %table.1, s32[16,128]{1,0:T(8,128)} %bitcast.11), custom_call_target="tpu_custom_call" | custom-call | tf_op jit(solution)/shard_map/coefficients/pallas_call | solution.py:72
  18.4 0.0 collective-permute-done.2.ylo
  18.4 1.0 %collective-permute-done.3.yhi = bf16[64,512]{1,0:T(8,128)(2,1)S(1)} collective-permute-done((bf16[64,512]{1,0:T(8,128)(2,1)S(1)}, bf16[64,512]{1,0:T(8,128)(2,1)S(1)}, u32[]{:S(2)}, u32[]{:S(2)}) %collective-permute-start.3) | collective-permute-done | bytes 65568 | tf_op jit(solution)/shard_map/ppermute | solution.py:33
  19.4 0.0 copy-start
  19.4 0.9 copy-done
  20.3 1.9 %first_image.1 = (bf16[64,2048]{1,0:T(8,128)(2,1)S(1)}, f32[64,640]{1,0:T(8,128)S(1)}) custom-call(f32[27,16,128]{2,1,0:T(8,128)S(1)} %copy-done, bf16[192,2048]{1,0:T(8,128)(2,1)S(1)} %reshape.17.stack, bf16[64,1024]{1,0:T(8,128)(2,1)S(1)} %collective-permute-done.xlo, bf16[64,1024]{1,0:T(8,128)(2,1)S(1)} %collective-permute-done.1.xhi, ...), custom_call_target="tpu_custom_call" | custom-call | tf_op jit(solution)/shard_map/first_image/pallas_call | solution.py:264
  22.3 3.0 %collective-permute-start.4 = (f32[32,640]{1,0:T(8,128)S(1)}, f32[32,640]{1,0:T(8,128)S(1)}, u32[]{:S(2)}, u32[]{:S(2)}) collective-permute-start(f32[32,640]{1,0:T(8,128)S(1)} %slice_select_fusion), channel_id=1, source_target_pairs={{0,1},{1,0},{2,3},{3,2},{4,5},{5,4},{6,7},{7,6},{8,9},{9,8},{10,11... | collective-permute-start | bytes 245768 | tf_op jit(solution)/shard_map/ppermute | solution.py:238
  25.3 0.9 collective-permute-done.4
  26.2 0.3 collective-permute-start.5
  26.6 4.4 %collective-permute-done.5 = f32[32,640]{1,0:T(8,128)S(1)} collective-permute-done((f32[32,640]{1,0:T(8,128)S(1)}, f32[32,640]{1,0:T(8,128)S(1)}, u32[]{:S(2)}, u32[]{:S(2)}) %collective-permute-start.5) | collective-permute-done | bytes 81952 | tf_op jit(solution)/shard_map/ppermute | solution.py:238
  31.0 2.6 %collective-permute-start.6 = (f32[32,640]{1,0:T(8,128)S(1)}, f32[32,640]{1,0:T(8,128)S(1)}, u32[]{:S(2)}, u32[]{:S(2)}) collective-permute-start(f32[32,640]{1,0:T(8,128)S(1)} %add.36), channel_id=1, source_target_pairs={{0,4},{4,0},{8,12},{12,8},{16,20},{20,16},{24,28},{28,24},{1,5},{5... | collective-permute-start | bytes 245768 | tf_op jit(solution)/shard_map/ppermute | solution.py:238
  33.6 2.4 %collective-permute-done.6 = f32[32,640]{1,0:T(8,128)S(1)} collective-permute-done((f32[32,640]{1,0:T(8,128)S(1)}, f32[32,640]{1,0:T(8,128)S(1)}, u32[]{:S(2)}, u32[]{:S(2)}) %collective-permute-start.6) | collective-permute-done | bytes 81952 | tf_op jit(solution)/shard_map/ppermute | solution.py:238
  36.0 2.4 %collective-permute-start.7 = (f32[32,640]{1,0:T(8,128)S(1)}, f32[32,640]{1,0:T(8,128)S(1)}, u32[]{:S(2)}, u32[]{:S(2)}) collective-permute-start(f32[32,640]{1,0:T(8,128)S(1)} %add.37), channel_id=1, source_target_pairs={{0,8},{4,12},{8,0},{12,4},{16,24},{20,28},{24,16},{28,20},{1,9},{5... | collective-permute-start | bytes 245768 | tf_op jit(solution)/shard_map/ppermute | solution.py:238
  38.4 2.4 %collective-permute-done.7 = f32[32,640]{1,0:T(8,128)S(1)} collective-permute-done((f32[32,640]{1,0:T(8,128)S(1)}, f32[32,640]{1,0:T(8,128)S(1)}, u32[]{:S(2)}, u32[]{:S(2)}) %collective-permute-start.7) | collective-permute-done | bytes 81952 | tf_op jit(solution)/shard_map/ppermute | solution.py:238
  40.8 3.3 %collective-permute-start.8 = (f32[32,640]{1,0:T(8,128)S(1)}, f32[32,640]{1,0:T(8,128)S(1)}, u32[]{:S(2)}, u32[]{:S(2)}) collective-permute-start(f32[32,640]{1,0:T(8,128)S(1)} %add.38), channel_id=1, source_target_pairs={{0,16},{4,20},{8,24},{12,28},{16,0},{20,4},{24,8},{28,12},{1,17},{... | collective-permute-start | bytes 245768 | tf_op jit(solution)/shard_map/ppermute | solution.py:238
  44.1 2.4 %collective-permute-done.8 = f32[32,640]{1,0:T(8,128)S(1)} collective-permute-done((f32[32,640]{1,0:T(8,128)S(1)}, f32[32,640]{1,0:T(8,128)S(1)}, u32[]{:S(2)}, u32[]{:S(2)}) %collective-permute-start.8) | collective-permute-done | bytes 81952 | tf_op jit(solution)/shard_map/ppermute | solution.py:238
  46.6 0.1 collective-permute-start.9
  46.7 1.3 %collective-permute-done.9 = f32[32,640]{1,0:T(8,128)S(1)} collective-permute-done((f32[32,640]{1,0:T(8,128)S(1)}, f32[32,640]{1,0:T(8,128)S(1)}, u32[]{:S(2)}, u32[]{:S(2)}) %collective-permute-start.9) | collective-permute-done | bytes 81952 | tf_op jit(solution)/shard_map/ppermute | solution.py:238
  48.0 7.0 %first_solve.1 = (bf16[64,2048]{1,0:T(8,128)(2,1)S(1)}, f32[64,192]{1,0:T(8,128)S(1)}, f32[64,64]{1,0:T(8,128)S(1)}, f32[192,192]{1,0:T(8,128)S(1)}) custom-call(f32[64,640]{1,0:T(8,128)S(1)} %pad_maximum_fusion.cross, bf16[192,2048]{1,0:T(8,128)(2,1)S(1)} %reshape.17.stack, bf16[64,2048]{1,0:T(8,128)(2,1)S(1)} %get-tuple-element.15.image), custom_call_target="tpu_custom_call" | custom-call | tf_op jit(solution)/shard_map/first_solve/pallas_call | solution.py:264
  55.0 1.3 %collective-permute-start.11 = (bf16[64,1024]{1,0:T(8,128)(2,1)S(1)}, bf16[64,1024]{1,0:T(8,128)(2,1)S(1)}, u32[]{:S(2)}, u32[]{:S(2)}) collective-permute-start(bf16[64,1024]{1,0:T(8,128)(2,1)S(1)} %get-tuple-element.29), channel_id=1, source_target_pairs={{4,0},{8,4},{12,8},{16,12},{20,16},{24,20},{28,24},{5,1},{9,5},{13... | collective-permute-start | bytes 393224 | tf_op jit(solution)/shard_map/ppermute | solution.py:33
  56.3 4.6 %collective-permute-start.10 = (bf16[64,1024]{1,0:T(8,128)(2,1)S(1)}, bf16[64,1024]{1,0:T(8,128)(2,1)S(1)}, u32[]{:S(2)}, u32[]{:S(2)}) collective-permute-start(bf16[64,1024]{1,0:T(8,128)(2,1)S(1)} %get-tuple-element.30), channel_id=1, source_target_pairs={{0,4},{4,8},{8,12},{12,16},{16,20},{20,24},{24,28},{1,5},{5,9},{9,... | collective-permute-start | bytes 393224 | tf_op jit(solution)/shard_map/ppermute | solution.py:33
  60.8 1.6 %collective-permute-done.11.xhi = bf16[64,1024]{1,0:T(8,128)(2,1)S(1)} collective-permute-done((bf16[64,1024]{1,0:T(8,128)(2,1)S(1)}, bf16[64,1024]{1,0:T(8,128)(2,1)S(1)}, u32[]{:S(2)}, u32[]{:S(2)}) %collective-permute-start.11) | collective-permute-done | bytes 131104 | tf_op jit(solution)/shard_map/ppermute | solution.py:33
  62.4 2.6 %collective-permute-done.10.xlo = bf16[64,1024]{1,0:T(8,128)(2,1)S(1)} collective-permute-done((bf16[64,1024]{1,0:T(8,128)(2,1)S(1)}, bf16[64,1024]{1,0:T(8,128)(2,1)S(1)}, u32[]{:S(2)}, u32[]{:S(2)}) %collective-permute-start.10) | collective-permute-done | bytes 131104 | tf_op jit(solution)/shard_map/ppermute | solution.py:33
  65.0 1.9 %collective-permute-start.12 = (bf16[64,512]{1,0:T(8,128)(2,1)S(1)}, bf16[64,512]{1,0:T(8,128)(2,1)S(1)}, u32[]{:S(2)}, u32[]{:S(2)}) collective-permute-start(bf16[64,512]{1,0:T(8,128)(2,1)S(1)} %pad_maximum_fusion.3), channel_id=1, source_target_pairs={{0,1},{1,2},{2,3},{4,5},{5,6},{6,7},{8,9},{9,10},{10,11},{12,13},{... | collective-permute-start | bytes 196616 | tf_op jit(solution)/shard_map/ppermute | solution.py:33
  67.0 1.3 %collective-permute-start.13 = (bf16[64,512]{1,0:T(8,128)(2,1)S(1)}, bf16[64,512]{1,0:T(8,128)(2,1)S(1)}, u32[]{:S(2)}, u32[]{:S(2)}) collective-permute-start(bf16[64,512]{1,0:T(8,128)(2,1)S(1)} %pad_maximum_fusion.4), channel_id=1, source_target_pairs={{1,0},{2,1},{3,2},{5,4},{6,5},{7,6},{9,8},{10,9},{11,10},{13,12},{... | collective-permute-start | bytes 196616 | tf_op jit(solution)/shard_map/ppermute | solution.py:33
  68.3 0.0 collective-permute-done.12.ylo
  68.3 1.8 %collective-permute-done.13.yhi = bf16[64,512]{1,0:T(8,128)(2,1)S(1)} collective-permute-done((bf16[64,512]{1,0:T(8,128)(2,1)S(1)}, bf16[64,512]{1,0:T(8,128)(2,1)S(1)}, u32[]{:S(2)}, u32[]{:S(2)}) %collective-permute-start.13) | collective-permute-done | bytes 65568 | tf_op jit(solution)/shard_map/ppermute | solution.py:33
  70.1 1.5 %second_image.1 = (bf16[64,2048]{1,0:T(8,128)(2,1)S(1)}, f32[64,256]{1,0:T(8,128)S(1)}) custom-call(f32[27,16,128]{2,1,0:T(8,128)S(1)} %copy-done, bf16[192,2048]{1,0:T(8,128)(2,1)S(1)} %reshape.17.stack, bf16[64,2048]{1,0:T(8,128)(2,1)S(1)} %get-tuple-element.16.block.last, bf16[64,1024]{1,0:T(8,128)(2,1)S(1)} %collective-permute-done.10.xlo, ...), custom_call_target="tpu_custom_call" | custom-call | tf_op jit(solution)/shard_map/second_image/pallas_call | solution.py:264
  71.6 2.9 %collective-permute-start.14 = (f32[64,256]{1,0:T(8,128)S(1)}, f32[64,256]{1,0:T(8,128)S(1)}, u32[]{:S(2)}, u32[]{:S(2)}) collective-permute-start(f32[64,256]{1,0:T(8,128)S(1)} %get-tuple-element.17), channel_id=1, source_target_pairs={{0,1},{1,0},{2,3},{3,2},{4,5},{5,4},{6,7},{7,6},{8,9},{9,8},{10,11... | collective-permute-start | bytes 196616 | tf_op jit(solution)/shard_map/ppermute | solution.py:238
  74.5 0.9 collective-permute-done.14
  75.4 0.2 collective-permute-start.15
  75.7 4.2 %collective-permute-done.15 = f32[64,256]{1,0:T(8,128)S(1)} collective-permute-done((f32[64,256]{1,0:T(8,128)S(1)}, f32[64,256]{1,0:T(8,128)S(1)}, u32[]{:S(2)}, u32[]{:S(2)}) %collective-permute-start.15) | collective-permute-done | bytes 65568 | tf_op jit(solution)/shard_map/ppermute | solution.py:238
  79.9 2.5 %collective-permute-start.16 = (f32[64,256]{1,0:T(8,128)S(1)}, f32[64,256]{1,0:T(8,128)S(1)}, u32[]{:S(2)}, u32[]{:S(2)}) collective-permute-start(f32[64,256]{1,0:T(8,128)S(1)} %add.41), channel_id=1, source_target_pairs={{0,4},{4,0},{8,12},{12,8},{16,20},{20,16},{24,28},{28,24},{1,5},{5... | collective-permute-start | bytes 196616 | tf_op jit(solution)/shard_map/ppermute | solution.py:238
  82.4 2.2 %collective-permute-done.16 = f32[64,256]{1,0:T(8,128)S(1)} collective-permute-done((f32[64,256]{1,0:T(8,128)S(1)}, f32[64,256]{1,0:T(8,128)S(1)}, u32[]{:S(2)}, u32[]{:S(2)}) %collective-permute-start.16) | collective-permute-done | bytes 65568 | tf_op jit(solution)/shard_map/ppermute | solution.py:238
  84.6 2.4 %collective-permute-start.17 = (f32[64,256]{1,0:T(8,128)S(1)}, f32[64,256]{1,0:T(8,128)S(1)}, u32[]{:S(2)}, u32[]{:S(2)}) collective-permute-start(f32[64,256]{1,0:T(8,128)S(1)} %add.42), channel_id=1, source_target_pairs={{0,8},{4,12},{8,0},{12,4},{16,24},{20,28},{24,16},{28,20},{1,9},{5... | collective-permute-start | bytes 196616 | tf_op jit(solution)/shard_map/ppermute | solution.py:238
  87.0 2.2 %collective-permute-done.17 = f32[64,256]{1,0:T(8,128)S(1)} collective-permute-done((f32[64,256]{1,0:T(8,128)S(1)}, f32[64,256]{1,0:T(8,128)S(1)}, u32[]{:S(2)}, u32[]{:S(2)}) %collective-permute-start.17) | collective-permute-done | bytes 65568 | tf_op jit(solution)/shard_map/ppermute | solution.py:238
  89.3 3.2 %collective-permute-start.18 = (f32[64,256]{1,0:T(8,128)S(1)}, f32[64,256]{1,0:T(8,128)S(1)}, u32[]{:S(2)}, u32[]{:S(2)}) collective-permute-start(f32[64,256]{1,0:T(8,128)S(1)} %add.43), channel_id=1, source_target_pairs={{0,16},{4,20},{8,24},{12,28},{16,0},{20,4},{24,8},{28,12},{1,17},{... | collective-permute-start | bytes 196616 | tf_op jit(solution)/shard_map/ppermute | solution.py:238
  92.5 2.2 %collective-permute-done.18 = f32[64,256]{1,0:T(8,128)S(1)} collective-permute-done((f32[64,256]{1,0:T(8,128)S(1)}, f32[64,256]{1,0:T(8,128)S(1)}, u32[]{:S(2)}, u32[]{:S(2)}) %collective-permute-start.18) | collective-permute-done | bytes 65568 | tf_op jit(solution)/shard_map/ppermute | solution.py:238
  94.7 7.1 %second_solve.1 = (bf16[64,2048]{1,0:T(8,128)(2,1)S(1)}, f32[2,64,192]{2,1,0:T(8,128)}, f32[2,64,64]{2,1,0:T(8,128)}) custom-call(f32[64,256]{1,0:T(8,128)S(1)} %add.44.cross, f32[192,192]{1,0:T(8,128)S(1)} %get-tuple-element.18.own, bf16[192,2048]{1,0:T(8,128)(2,1)S(1)} %reshape.17.stack, bf16[64,2048]{1,0:T(8,128)(2,1)S(1)} %get-tuple-element.16.block.last, ...), custom_call_target="tpu_custom_call" | custom-call | tf_op jit(solution)/shard_map/second_solve/pallas_call | solution.py:264
  101.8 0.7 copy.6
  (25 shorter events, 0.3 us)
Async XLA Ops:
  0.6 1.0 slice-start
  1.6 14.9 %copy-start.1 = (bf16[3,64,2,8,128]{4,3,2,1,0:T(8,128)(2,1)S(1)}, bf16[3,64,2,8,128]{4,3,2,1,0:T(8,128)(2,1)}, u32[]{:S(2)}) copy-start(bf16[3,64,2,8,128]{4,3,2,1,0:T(8,128)(2,1)} %param.3) | copy-start | bytes 2359300
  1.7 8.5 %collective-permute-start.1 = (bf16[64,1024]{1,0:T(8,128)(2,1)S(1)}, bf16[64,1024]{1,0:T(8,128)(2,1)S(1)}, u32[]{:S(2)}, u32[]{:S(2)}) collective-permute-start(bf16[64,1024]{1,0:T(8,128)(2,1)S(1)} %get-tuple-element.35), channel_id=1, source_target_pairs={{4,0},{8,4},{12,8},{16,12},{20,16},{24,20},{28,24},{5,1},{9,5},{13... | collective-permute-start | bytes 393224 | tf_op jit(solution)/shard_map/ppermute | solution.py:33
  3.2 10.0 %collective-permute-start = (bf16[64,1024]{1,0:T(8,128)(2,1)S(1)}, bf16[64,1024]{1,0:T(8,128)(2,1)S(1)}, u32[]{:S(2)}, u32[]{:S(2)}) collective-permute-start(bf16[64,1024]{1,0:T(8,128)(2,1)S(1)} %get-tuple-element.36), channel_id=1, source_target_pairs={{0,4},{4,8},{8,12},{12,16},{16,20},{20,24},{24,28},{1,5},{5,9},{9,... | collective-permute-start | bytes 393224 | tf_op jit(solution)/shard_map/ppermute | solution.py:33
  13.2 5.2 %collective-permute-start.2 = (bf16[64,512]{1,0:T(8,128)(2,1)S(1)}, bf16[64,512]{1,0:T(8,128)(2,1)S(1)}, u32[]{:S(2)}, u32[]{:S(2)}) collective-permute-start(bf16[64,512]{1,0:T(8,128)(2,1)S(1)} %pad_maximum_fusion.1), channel_id=1, source_target_pairs={{0,1},{1,2},{2,3},{4,5},{5,6},{6,7},{8,9},{9,10},{10,11},{12,13},{... | collective-permute-start | bytes 196616 | tf_op jit(solution)/shard_map/ppermute | solution.py:33
  15.1 4.3 %collective-permute-start.3 = (bf16[64,512]{1,0:T(8,128)(2,1)S(1)}, bf16[64,512]{1,0:T(8,128)(2,1)S(1)}, u32[]{:S(2)}, u32[]{:S(2)}) collective-permute-start(bf16[64,512]{1,0:T(8,128)(2,1)S(1)} %pad_maximum_fusion.2), channel_id=1, source_target_pairs={{1,0},{2,1},{3,2},{5,4},{6,5},{7,6},{9,8},{10,9},{11,10},{13,12},{... | collective-permute-start | bytes 196616 | tf_op jit(solution)/shard_map/ppermute | solution.py:33
  19.4 0.9 copy-start
  22.3 3.9 %collective-permute-start.4 = (f32[32,640]{1,0:T(8,128)S(1)}, f32[32,640]{1,0:T(8,128)S(1)}, u32[]{:S(2)}, u32[]{:S(2)}) collective-permute-start(f32[32,640]{1,0:T(8,128)S(1)} %slice_select_fusion), channel_id=1, source_target_pairs={{0,1},{1,0},{2,3},{3,2},{4,5},{5,4},{6,7},{7,6},{8,9},{9,8},{10,11... | collective-permute-start | bytes 245768 | tf_op jit(solution)/shard_map/ppermute | solution.py:238
  26.2 4.8 %collective-permute-start.5 = (f32[32,640]{1,0:T(8,128)S(1)}, f32[32,640]{1,0:T(8,128)S(1)}, u32[]{:S(2)}, u32[]{:S(2)}) collective-permute-start(f32[32,640]{1,0:T(8,128)S(1)} %select_add_fusion), channel_id=1, source_target_pairs={{0,2},{1,3},{2,0},{3,1},{4,6},{5,7},{6,4},{7,5},{8,10},{9,11},{10,... | collective-permute-start | bytes 245768 | tf_op jit(solution)/shard_map/ppermute | solution.py:238
  31.0 5.0 %collective-permute-start.6 = (f32[32,640]{1,0:T(8,128)S(1)}, f32[32,640]{1,0:T(8,128)S(1)}, u32[]{:S(2)}, u32[]{:S(2)}) collective-permute-start(f32[32,640]{1,0:T(8,128)S(1)} %add.36), channel_id=1, source_target_pairs={{0,4},{4,0},{8,12},{12,8},{16,20},{20,16},{24,28},{28,24},{1,5},{5... | collective-permute-start | bytes 245768 | tf_op jit(solution)/shard_map/ppermute | solution.py:238
  36.0 4.8 %collective-permute-start.7 = (f32[32,640]{1,0:T(8,128)S(1)}, f32[32,640]{1,0:T(8,128)S(1)}, u32[]{:S(2)}, u32[]{:S(2)}) collective-permute-start(f32[32,640]{1,0:T(8,128)S(1)} %add.37), channel_id=1, source_target_pairs={{0,8},{4,12},{8,0},{12,4},{16,24},{20,28},{24,16},{28,20},{1,9},{5... | collective-permute-start | bytes 245768 | tf_op jit(solution)/shard_map/ppermute | solution.py:238
  40.8 5.7 %collective-permute-start.8 = (f32[32,640]{1,0:T(8,128)S(1)}, f32[32,640]{1,0:T(8,128)S(1)}, u32[]{:S(2)}, u32[]{:S(2)}) collective-permute-start(f32[32,640]{1,0:T(8,128)S(1)} %add.38), channel_id=1, source_target_pairs={{0,16},{4,20},{8,24},{12,28},{16,0},{20,4},{24,8},{28,12},{1,17},{... | collective-permute-start | bytes 245768 | tf_op jit(solution)/shard_map/ppermute | solution.py:238
  46.6 1.3 %collective-permute-start.9 = (f32[32,640]{1,0:T(8,128)S(1)}, f32[32,640]{1,0:T(8,128)S(1)}, u32[]{:S(2)}, u32[]{:S(2)}) collective-permute-start(f32[32,640]{1,0:T(8,128)S(1)} %add.39), channel_id=1, source_target_pairs={{0,1},{1,0},{2,3},{3,2},{4,5},{5,4},{6,7},{7,6},{8,9},{9,8},{10,11... | collective-permute-start | bytes 245768 | tf_op jit(solution)/shard_map/ppermute | solution.py:238
  55.0 7.5 %collective-permute-start.11 = (bf16[64,1024]{1,0:T(8,128)(2,1)S(1)}, bf16[64,1024]{1,0:T(8,128)(2,1)S(1)}, u32[]{:S(2)}, u32[]{:S(2)}) collective-permute-start(bf16[64,1024]{1,0:T(8,128)(2,1)S(1)} %get-tuple-element.29), channel_id=1, source_target_pairs={{4,0},{8,4},{12,8},{16,12},{20,16},{24,20},{28,24},{5,1},{9,5},{13... | collective-permute-start | bytes 393224 | tf_op jit(solution)/shard_map/ppermute | solution.py:33
  56.3 8.8 %collective-permute-start.10 = (bf16[64,1024]{1,0:T(8,128)(2,1)S(1)}, bf16[64,1024]{1,0:T(8,128)(2,1)S(1)}, u32[]{:S(2)}, u32[]{:S(2)}) collective-permute-start(bf16[64,1024]{1,0:T(8,128)(2,1)S(1)} %get-tuple-element.30), channel_id=1, source_target_pairs={{0,4},{4,8},{8,12},{12,16},{16,20},{20,24},{24,28},{1,5},{5,9},{9,... | collective-permute-start | bytes 393224 | tf_op jit(solution)/shard_map/ppermute | solution.py:33
  65.0 3.3 %collective-permute-start.12 = (bf16[64,512]{1,0:T(8,128)(2,1)S(1)}, bf16[64,512]{1,0:T(8,128)(2,1)S(1)}, u32[]{:S(2)}, u32[]{:S(2)}) collective-permute-start(bf16[64,512]{1,0:T(8,128)(2,1)S(1)} %pad_maximum_fusion.3), channel_id=1, source_target_pairs={{0,1},{1,2},{2,3},{4,5},{5,6},{6,7},{8,9},{9,10},{10,11},{12,13},{... | collective-permute-start | bytes 196616 | tf_op jit(solution)/shard_map/ppermute | solution.py:33
  67.0 3.1 %collective-permute-start.13 = (bf16[64,512]{1,0:T(8,128)(2,1)S(1)}, bf16[64,512]{1,0:T(8,128)(2,1)S(1)}, u32[]{:S(2)}, u32[]{:S(2)}) collective-permute-start(bf16[64,512]{1,0:T(8,128)(2,1)S(1)} %pad_maximum_fusion.4), channel_id=1, source_target_pairs={{1,0},{2,1},{3,2},{5,4},{6,5},{7,6},{9,8},{10,9},{11,10},{13,12},{... | collective-permute-start | bytes 196616 | tf_op jit(solution)/shard_map/ppermute | solution.py:33
  71.6 3.8 %collective-permute-start.14 = (f32[64,256]{1,0:T(8,128)S(1)}, f32[64,256]{1,0:T(8,128)S(1)}, u32[]{:S(2)}, u32[]{:S(2)}) collective-permute-start(f32[64,256]{1,0:T(8,128)S(1)} %get-tuple-element.17), channel_id=1, source_target_pairs={{0,1},{1,0},{2,3},{3,2},{4,5},{5,4},{6,7},{7,6},{8,9},{9,8},{10,11... | collective-permute-start | bytes 196616 | tf_op jit(solution)/shard_map/ppermute | solution.py:238
  75.4 4.4 %collective-permute-start.15 = (f32[64,256]{1,0:T(8,128)S(1)}, f32[64,256]{1,0:T(8,128)S(1)}, u32[]{:S(2)}, u32[]{:S(2)}) collective-permute-start(f32[64,256]{1,0:T(8,128)S(1)} %add.40), channel_id=1, source_target_pairs={{0,2},{1,3},{2,0},{3,1},{4,6},{5,7},{6,4},{7,5},{8,10},{9,11},{10,... | collective-permute-start | bytes 196616 | tf_op jit(solution)/shard_map/ppermute | solution.py:238
  79.9 4.8 %collective-permute-start.16 = (f32[64,256]{1,0:T(8,128)S(1)}, f32[64,256]{1,0:T(8,128)S(1)}, u32[]{:S(2)}, u32[]{:S(2)}) collective-permute-start(f32[64,256]{1,0:T(8,128)S(1)} %add.41), channel_id=1, source_target_pairs={{0,4},{4,0},{8,12},{12,8},{16,20},{20,16},{24,28},{28,24},{1,5},{5... | collective-permute-start | bytes 196616 | tf_op jit(solution)/shard_map/ppermute | solution.py:238
  84.6 4.6 %collective-permute-start.17 = (f32[64,256]{1,0:T(8,128)S(1)}, f32[64,256]{1,0:T(8,128)S(1)}, u32[]{:S(2)}, u32[]{:S(2)}) collective-permute-start(f32[64,256]{1,0:T(8,128)S(1)} %add.42), channel_id=1, source_target_pairs={{0,8},{4,12},{8,0},{12,4},{16,24},{20,28},{24,16},{28,20},{1,9},{5... | collective-permute-start | bytes 196616 | tf_op jit(solution)/shard_map/ppermute | solution.py:238
  89.3 5.4 %collective-permute-start.18 = (f32[64,256]{1,0:T(8,128)S(1)}, f32[64,256]{1,0:T(8,128)S(1)}, u32[]{:S(2)}, u32[]{:S(2)}) collective-permute-start(f32[64,256]{1,0:T(8,128)S(1)} %add.43), channel_id=1, source_target_pairs={{0,16},{4,20},{8,24},{12,28},{16,0},{20,4},{24,8},{28,12},{1,17},{... | collective-permute-start | bytes 196616 | tf_op jit(solution)/shard_map/ppermute | solution.py:238

commit v5 on v3

--- a/solution.py
+++ b/solution.py
@@ -28,9 +28,12 @@
 
     def exchange(axis, upward, downward):
         count = lax.axis_size(axis)
-        forward = [(i, i + 1) for i in range(count - 1)]
-        backward = [(target, source) for source, target in forward]
-        return lax.ppermute(upward, axis, forward), lax.ppermute(downward, axis, backward)
+        odd = lax.axis_index(axis) % 2 == 1
+        pairs = [[(i, i + 1) for i in range(first, count - 1, 2)] for first in (0, 1)]
+        swaps = [pair + [(b, a) for a, b in pair] for pair in pairs]
+        inner = lax.ppermute(jnp.where(odd, downward, upward), axis, swaps[0])
+        outer = lax.ppermute(jnp.where(odd, upward, downward), axis, swaps[1])
+        return jnp.where(odd, inner, outer), jnp.where(odd, outer, inner)
 
     xlo, xhi = exchange("slab", block[:, (span_x - 1) * plane :], block[:, :plane])
 
@@ -233,12 +236,28 @@
     block[...] = dot(inverse.astype(jnp.bfloat16), w.astype(jnp.bfloat16)).astype(jnp.bfloat16)
 
 
-def whole_sum(part):
+def partner(part, mask):
     axes = ("slab", "col")
     count = lax.axis_size("slab") * lax.axis_size("col")
-    shares = lax.all_to_all(part.reshape(count, -1), axes, 0, 0, tiled=True)
-    share = jnp.sum(shares, axis=0, keepdims=True)
-    return lax.all_gather(share, axes, axis=0, tiled=True).reshape(part.shape)
+    return lax.ppermute(part, axes, [(i, i ^ mask) for i in range(count)])
+
+
+def whole_sum(part):
+    count = lax.axis_size("slab") * lax.axis_size("col")
+    half = part.shape[0] // 2
+    upper = lax.axis_index("col") % 2 == 1
+    low, high = part[:half], part[half:]
+    part = jnp.where(upper, high, low) + partner(jnp.where(upper, low, high), 1)
+    bit = 2
+    while bit < count:
+        if 2 * bit < count:
+            one, two, both = (partner(part, mask) for mask in (bit, 2 * bit, 3 * bit))
+            part = (part + one) + (two + both)
+        else:
+            part = part + partner(part, bit)
+        bit *= 4
+    other = partner(part, 1)
+    return jnp.concatenate([jnp.where(upper, other, part), jnp.where(upper, part, other)], axis=0)
 
 
 def call(kernel, name, outs, *args):

time: 159 us -> 92 us (0.58)
  blocking collectives: 105 us -> 0 us
  waiting for transfers between devices: 10.6 us -> 31.3 us
  starting transfers between devices: 18.5 us -> 36.9 us
    all_gather x2 -> x0, blocking collectives: 76.2 us -> none  [whole_sum(): return lax.all_gather(share, axes, axis=0, tiled=True).reshape(part.shape)]
    all_to_all x2 -> x0, blocking collectives: 28.7 us -> none  [whole_sum(): shares = lax.all_to_all(part.reshape(count, -1), axes, 0, 0, tiled=True)]
    ppermute x8 -> x24, waiting for transfers between devices: 10.6 us -> 31.3 us  [the longest x16 20 us: partner(): return lax.ppermute(part, axes, [(i, i ^ mask) for i in range(count)])]
    ppermute x8 -> x24, starting transfers between devices: 18.5 us -> 36.9 us  [the longest x16 19.8 us: partner(): return lax.ppermute(part, axes, [(i, i ^ mask) for i in range(count)])]
  transfers between devices with their start and end apart: 8 -> 24, of which waited for: 6 -> 16; matrix products, arithmetic and copies ran while one was open for 0% -> 0% of each run, Pallas kernels for 1% -> 2%
where the time goes in v5:
time: 92 us; the launch traced here: 91.7 us
  starting transfers between devices  36.9 us (40%)
  waiting for transfers between devices  31.3 us (34%)
  Pallas kernels  19.2 us (21%)
  local copies, waits for them, and re-layouts  3.1 us (3%)
    ppermute x16, waiting for transfers between devices, partner(): return lax.ppermute(part, axes, [(i, i ^ mask) for i in range(count)])  20 us
    ppermute x16, starting transfers between devices, partner(): return lax.ppermute(part, axes, [(i, i ^ mask) for i in range(count)])  19.8 us
    pallas_call x4, Pallas kernels, call(): pl.pallas_call(kernel, out_shape=[jax.ShapeDtypeStruct(shape, dtype) for...  17.6 us
    ppermute x4, starting transfers between devices, exchange(): inner = lax.ppermute(jnp.where(odd, downward, upward), axis, swaps[0])  14.3 us
    ppermute x4, waiting for transfers between devices, exchange(): inner = lax.ppermute(jnp.where(odd, downward, upward), axis, swaps[0])  11.3 us
    ppermute x4, starting transfers between devices, exchange(): outer = lax.ppermute(jnp.where(odd, upward, downward), axis, swaps[1])  2.8 us
  transfers between devices with their start and end apart: 24, of which 16 were waited for; matrix products, arithmetic and copies ran while one was open for 0% of the time, Pallas kernels for 2%

profile of v5, /device:TPU:0, one launch (start us, length us, event | category | flops | bytes accessed | tf_op | source)
XLA Modules:
  0.0 91.7 jit_solution(6543139081266583458)
XLA Ops:
  0.6 0.0 slice-start
  0.7 0.9 %slice-done = bf16[1,64,2,8,128]{4,3,2,1,0:T(8,128)(2,1)S(1)} async-done(((bf16[3,64,2,8,128]{4,3,2,1,0:T(8,128)(2,1)}), bf16[1,64,2,8,128]{4,3,2,1,0:T(8,128)(2,1)S(1)}, s32[]{:S(2)}) %slice-start) | async-done | bytes 262168 | tf_op jit(solution)/shard_map/slice | solution.py:285
  1.6 0.1 slice.79
  1.7 0.0 copy-start.1
  1.8 0.8 collective-permute-start.1
  2.6 5.8 %collective-permute-start = (bf16[64,1024]{1,0:T(8,128)(2,1)S(1)}, bf16[64,1024]{1,0:T(8,128)(2,1)S(1)}, u32[]{:S(2)}, u32[]{:S(2)}) collective-permute-start(bf16[64,1024]{1,0:T(8,128)(2,1)S(1)} %get-tuple-element.40), channel_id=1, source_target_pairs={{0,4},{8,12},{16,20},{24,28},{4,0},{12,8},{20,16},{28,24},{1,5},{9... | collective-permute-start | bytes 393224 | tf_op jit(solution)/shard_map/ppermute | solution.py:34
  8.4 0.0 collective-permute-done.1
  8.4 4.8 %collective-permute-done = bf16[64,1024]{1,0:T(8,128)(2,1)S(1)} collective-permute-done((bf16[64,1024]{1,0:T(8,128)(2,1)S(1)}, bf16[64,1024]{1,0:T(8,128)(2,1)S(1)}, u32[]{:S(2)}, u32[]{:S(2)}) %collective-permute-start) | collective-permute-done | bytes 131104 | tf_op jit(solution)/shard_map/ppermute | solution.py:34
  13.3 0.7 collective-permute-start.3
  13.9 2.9 %collective-permute-start.2 = (bf16[64,512]{1,0:T(8,128)(2,1)S(1)}, bf16[64,512]{1,0:T(8,128)(2,1)S(1)}, u32[]{:S(2)}, u32[]{:S(2)}) collective-permute-start(bf16[64,512]{1,0:T(8,128)(2,1)S(1)} %get-tuple-element.54), channel_id=1, source_target_pairs={{0,1},{2,3},{1,0},{3,2},{4,5},{6,7},{5,4},{7,6},{8,9},{10,11},{9,8... | collective-permute-start | bytes 196616 | tf_op jit(solution)/shard_map/ppermute | solution.py:34
  16.9 0.0 copy-done.1
  16.9 0.3 reshape.17.stack
  17.2 1.6 %coefficients.1.coef = f32[27,16,128]{2,1,0:T(8,128)} custom-call(f32[8,27]{1,0:T(8,128)} %table.1, s32[16,128]{1,0:T(8,128)} %bitcast.11), custom_call_target="tpu_custom_call" | custom-call | tf_op jit(solution)/shard_map/coefficients/pallas_call | solution.py:75
  18.8 0.0 copy-start
  18.8 0.0 collective-permute-done.3
  18.8 0.0 collective-permute-done.2
  18.8 0.9 copy-done
  19.7 2.0 %first_image.1 = (bf16[64,2048]{1,0:T(8,128)(2,1)S(1)}, f32[64,640]{1,0:T(8,128)S(1)}) custom-call(f32[27,16,128]{2,1,0:T(8,128)S(1)} %copy-done, bf16[192,2048]{1,0:T(8,128)(2,1)S(1)} %reshape.17.stack, bf16[64,1024]{1,0:T(8,128)(2,1)S(1)} %get-tuple-element.38.xlo, bf16[64,1024]{1,0:T(8,128)(2,1)S(1)} %get-tuple-element.37.xhi, ...), custom_call_target="tpu_custom_call" | custom-call | tf_op jit(solution)/shard_map/first_image/pallas_call | solution.py:264
  21.8 0.1 collective-permute-start.4
  21.9 1.2 %collective-permute-done.4 = f32[32,640]{1,0:T(8,128)S(1)} collective-permute-done((f32[32,640]{1,0:T(8,128)S(1)}, f32[32,640]{1,0:T(8,128)S(1)}, u32[]{:S(2)}, u32[]{:S(2)}) %collective-permute-start.4) | collective-permute-done | bytes 81952 | tf_op jit(solution)/shard_map/ppermute | solution.py:242
  23.1 2.7 %collective-permute-start.7 = (f32[32,640]{1,0:T(8,128)S(1)}, f32[32,640]{1,0:T(8,128)S(1)}, u32[]{:S(2)}, u32[]{:S(2)}) collective-permute-start(f32[32,640]{1,0:T(8,128)S(1)} %select_add_fusion), channel_id=1, source_target_pairs={{0,6},{1,7},{2,4},{3,5},{4,2},{5,3},{6,0},{7,1},{8,14},{9,15},{10,... | collective-permute-start | bytes 245768 | tf_op jit(solution)/shard_map/ppermute | solution.py:242
  25.8 0.0 collective-permute-start.6
  25.8 1.3 %collective-permute-start.5 = (f32[32,640]{1,0:T(8,128)S(1)}, f32[32,640]{1,0:T(8,128)S(1)}, u32[]{:S(2)}, u32[]{:S(2)}) collective-permute-start(f32[32,640]{1,0:T(8,128)S(1)} %select_add_fusion), channel_id=1, source_target_pairs={{0,2},{1,3},{2,0},{3,1},{4,6},{5,7},{6,4},{7,5},{8,10},{9,11},{10,... | collective-permute-start | bytes 245768 | tf_op jit(solution)/shard_map/ppermute | solution.py:242
  27.2 1.5 %collective-permute-done.7 = f32[32,640]{1,0:T(8,128)S(1)} collective-permute-done((f32[32,640]{1,0:T(8,128)S(1)}, f32[32,640]{1,0:T(8,128)S(1)}, u32[]{:S(2)}, u32[]{:S(2)}) %collective-permute-start.7) | collective-permute-done | bytes 81952 | tf_op jit(solution)/shard_map/ppermute | solution.py:242
  28.6 1.6 %collective-permute-done.6 = f32[32,640]{1,0:T(8,128)S(1)} collective-permute-done((f32[32,640]{1,0:T(8,128)S(1)}, f32[32,640]{1,0:T(8,128)S(1)}, u32[]{:S(2)}, u32[]{:S(2)}) %collective-permute-start.6) | collective-permute-done | bytes 81952 | tf_op jit(solution)/shard_map/ppermute | solution.py:242
  30.2 0.1 collective-permute-done.5
  30.4 4.7 %collective-permute-start.10 = (f32[32,640]{1,0:T(8,128)S(1)}, f32[32,640]{1,0:T(8,128)S(1)}, u32[]{:S(2)}, u32[]{:S(2)}) collective-permute-start(f32[32,640]{1,0:T(8,128)S(1)} %add_add_fusion.1), channel_id=1, source_target_pairs={{0,24},{1,25},{2,26},{3,27},{4,28},{5,29},{6,30},{7,31},{8,16},{9,... | collective-permute-start | bytes 245768 | tf_op jit(solution)/shard_map/ppermute | solution.py:242
  35.1 0.0 collective-permute-start.9
  35.1 0.6 collective-permute-start.8
  35.7 2.4 %collective-permute-done.10 = f32[32,640]{1,0:T(8,128)S(1)} collective-permute-done((f32[32,640]{1,0:T(8,128)S(1)}, f32[32,640]{1,0:T(8,128)S(1)}, u32[]{:S(2)}, u32[]{:S(2)}) %collective-permute-start.10) | collective-permute-done | bytes 81952 | tf_op jit(solution)/shard_map/ppermute | solution.py:242
  38.1 3.6 %collective-permute-done.9 = f32[32,640]{1,0:T(8,128)S(1)} collective-permute-done((f32[32,640]{1,0:T(8,128)S(1)}, f32[32,640]{1,0:T(8,128)S(1)}, u32[]{:S(2)}, u32[]{:S(2)}) %collective-permute-start.9) | collective-permute-done | bytes 81952 | tf_op jit(solution)/shard_map/ppermute | solution.py:242
  41.7 0.0 collective-permute-done.8
  41.7 0.1 collective-permute-start.11
  41.8 1.3 %collective-permute-done.11 = f32[32,640]{1,0:T(8,128)S(1)} collective-permute-done((f32[32,640]{1,0:T(8,128)S(1)}, f32[32,640]{1,0:T(8,128)S(1)}, u32[]{:S(2)}, u32[]{:S(2)}) %collective-permute-start.11) | collective-permute-done | bytes 81952 | tf_op jit(solution)/shard_map/ppermute | solution.py:242
  43.1 7.0 %first_solve.1 = (bf16[64,2048]{1,0:T(8,128)(2,1)S(1)}, f32[64,192]{1,0:T(8,128)S(1)}, f32[64,64]{1,0:T(8,128)S(1)}, f32[192,192]{1,0:T(8,128)S(1)}) custom-call(f32[64,640]{1,0:T(8,128)S(1)} %pad_maximum_fusion.cross, bf16[192,2048]{1,0:T(8,128)(2,1)S(1)} %reshape.17.stack, bf16[64,2048]{1,0:T(8,128)(2,1)S(1)} %get-tuple-element.15.image), custom_call_target="tpu_custom_call" | custom-call | tf_op jit(solution)/shard_map/first_solve/pallas_call | solution.py:264
  50.1 0.7 collective-permute-start.13
  50.8 3.5 %collective-permute-start.12 = (bf16[64,1024]{1,0:T(8,128)(2,1)S(1)}, bf16[64,1024]{1,0:T(8,128)(2,1)S(1)}, u32[]{:S(2)}, u32[]{:S(2)}) collective-permute-start(bf16[64,1024]{1,0:T(8,128)(2,1)S(1)} %get-tuple-element.32), channel_id=1, source_target_pairs={{0,4},{8,12},{16,20},{24,28},{4,0},{12,8},{20,16},{28,24},{1,5},{9... | collective-permute-start | bytes 393224 | tf_op jit(solution)/shard_map/ppermute | solution.py:34
  54.3 0.0 collective-permute-done.13
  54.3 5.6 %collective-permute-done.12 = bf16[64,1024]{1,0:T(8,128)(2,1)S(1)} collective-permute-done((bf16[64,1024]{1,0:T(8,128)(2,1)S(1)}, bf16[64,1024]{1,0:T(8,128)(2,1)S(1)}, u32[]{:S(2)}, u32[]{:S(2)}) %collective-permute-start.12) | collective-permute-done | bytes 131104 | tf_op jit(solution)/shard_map/ppermute | solution.py:34
  60.0 0.7 collective-permute-start.15
  60.7 2.1 %collective-permute-start.14 = (bf16[64,512]{1,0:T(8,128)(2,1)S(1)}, bf16[64,512]{1,0:T(8,128)(2,1)S(1)}, u32[]{:S(2)}, u32[]{:S(2)}) collective-permute-start(bf16[64,512]{1,0:T(8,128)(2,1)S(1)} %get-tuple-element.46), channel_id=1, source_target_pairs={{0,1},{2,3},{1,0},{3,2},{4,5},{6,7},{5,4},{7,6},{8,9},{10,11},{9,8... | collective-permute-start | bytes 196616 | tf_op jit(solution)/shard_map/ppermute | solution.py:34
  62.8 0.0 collective-permute-done.15
  62.8 0.9 collective-permute-done.14
  63.7 1.6 %second_image.1 = (bf16[64,2048]{1,0:T(8,128)(2,1)S(1)}, f32[64,256]{1,0:T(8,128)S(1)}) custom-call(f32[27,16,128]{2,1,0:T(8,128)S(1)} %copy-done, bf16[192,2048]{1,0:T(8,128)(2,1)S(1)} %reshape.17.stack, bf16[64,2048]{1,0:T(8,128)(2,1)S(1)} %get-tuple-element.16.block.last, bf16[64,1024]{1,0:T(8,128)(2,1)S(1)} %get-tuple-element.30.xlo, ...), custom_call_target="tpu_custom_call" | custom-call | tf_op jit(solution)/shard_map/second_image/pallas_call | solution.py:264
  65.3 1.8 %collective-permute-start.16 = (f32[32,256]{1,0:T(8,128)S(1)}, f32[32,256]{1,0:T(8,128)S(1)}, u32[]{:S(2)}, u32[]{:S(2)}) collective-permute-start(f32[32,256]{1,0:T(8,128)S(1)} %slice_select_fusion.1), channel_id=1, source_target_pairs={{0,1},{1,0},{2,3},{3,2},{4,5},{5,4},{6,7},{7,6},{8,9},{9,8},{10,11... | collective-permute-start | bytes 98312 | tf_op jit(solution)/shard_map/ppermute | solution.py:242
  67.1 0.9 collective-permute-done.16
  67.9 3.1 %collective-permute-start.19 = (f32[32,256]{1,0:T(8,128)S(1)}, f32[32,256]{1,0:T(8,128)S(1)}, u32[]{:S(2)}, u32[]{:S(2)}) collective-permute-start(f32[32,256]{1,0:T(8,128)S(1)} %select_add_fusion.1), channel_id=1, source_target_pairs={{0,6},{1,7},{2,4},{3,5},{4,2},{5,3},{6,0},{7,1},{8,14},{9,15},{10,... | collective-permute-start | bytes 98312 | tf_op jit(solution)/shard_map/ppermute | solution.py:242
  71.0 0.0 collective-permute-start.18
  71.0 0.8 collective-permute-start.17
  71.9 1.1 %collective-permute-done.19 = f32[32,256]{1,0:T(8,128)S(1)} collective-permute-done((f32[32,256]{1,0:T(8,128)S(1)}, f32[32,256]{1,0:T(8,128)S(1)}, u32[]{:S(2)}, u32[]{:S(2)}) %collective-permute-start.19) | collective-permute-done | bytes 32800 | tf_op jit(solution)/shard_map/ppermute | solution.py:242
  72.9 2.0 %collective-permute-done.18 = f32[32,256]{1,0:T(8,128)S(1)} collective-permute-done((f32[32,256]{1,0:T(8,128)S(1)}, f32[32,256]{1,0:T(8,128)S(1)}, u32[]{:S(2)}, u32[]{:S(2)}) %collective-permute-start.18) | collective-permute-done | bytes 32800 | tf_op jit(solution)/shard_map/ppermute | solution.py:242
  75.0 0.0 collective-permute-done.17
  75.0 2.7 %collective-permute-start.22 = (f32[32,256]{1,0:T(8,128)S(1)}, f32[32,256]{1,0:T(8,128)S(1)}, u32[]{:S(2)}, u32[]{:S(2)}) collective-permute-start(f32[32,256]{1,0:T(8,128)S(1)} %add_add_fusion.3), channel_id=1, source_target_pairs={{0,24},{1,25},{2,26},{3,27},{4,28},{5,29},{6,30},{7,31},{8,16},{9,... | collective-permute-start | bytes 98312 | tf_op jit(solution)/shard_map/ppermute | solution.py:242
  77.7 0.4 collective-permute-start.21
  78.2 1.3 %collective-permute-start.20 = (f32[32,256]{1,0:T(8,128)S(1)}, f32[32,256]{1,0:T(8,128)S(1)}, u32[]{:S(2)}, u32[]{:S(2)}) collective-permute-start(f32[32,256]{1,0:T(8,128)S(1)} %add_add_fusion.3), channel_id=1, source_target_pairs={{0,8},{1,9},{2,10},{3,11},{4,12},{5,13},{6,14},{7,15},{8,0},{9,1},... | collective-permute-start | bytes 98312 | tf_op jit(solution)/shard_map/ppermute | solution.py:242
  79.4 1.5 %collective-permute-done.22 = f32[32,256]{1,0:T(8,128)S(1)} collective-permute-done((f32[32,256]{1,0:T(8,128)S(1)}, f32[32,256]{1,0:T(8,128)S(1)}, u32[]{:S(2)}, u32[]{:S(2)}) %collective-permute-start.22) | collective-permute-done | bytes 32800 | tf_op jit(solution)/shard_map/ppermute | solution.py:242
  80.9 1.6 %collective-permute-done.21 = f32[32,256]{1,0:T(8,128)S(1)} collective-permute-done((f32[32,256]{1,0:T(8,128)S(1)}, f32[32,256]{1,0:T(8,128)S(1)}, u32[]{:S(2)}, u32[]{:S(2)}) %collective-permute-start.21) | collective-permute-done | bytes 32800 | tf_op jit(solution)/shard_map/ppermute | solution.py:242
  82.5 0.0 collective-permute-done.20
  82.5 0.1 collective-permute-start.23
  82.6 1.2 %collective-permute-done.23 = f32[32,256]{1,0:T(8,128)S(1)} collective-permute-done((f32[32,256]{1,0:T(8,128)S(1)}, f32[32,256]{1,0:T(8,128)S(1)}, u32[]{:S(2)}, u32[]{:S(2)}) %collective-permute-start.23) | collective-permute-done | bytes 32800 | tf_op jit(solution)/shard_map/ppermute | solution.py:242
  83.8 7.1 %second_solve.1 = (bf16[64,2048]{1,0:T(8,128)(2,1)S(1)}, f32[2,64,192]{2,1,0:T(8,128)}, f32[2,64,64]{2,1,0:T(8,128)}) custom-call(f32[64,256]{1,0:T(8,128)S(1)} %pad_maximum_fusion.5.cross, f32[192,192]{1,0:T(8,128)S(1)} %get-tuple-element.18.own, bf16[192,2048]{1,0:T(8,128)(2,1)S(1)} %reshape.17.stack, bf16[64,2048]{1,0:T(8,128)(2,1)S(1)} %get-tuple-element.16.block.last, ...), custom_call_target="tpu_custom_call" | custom-call | tf_op jit(solution)/shard_map/second_solve/pallas_call | solution.py:264
  90.9 0.7 copy.6
  (25 shorter events, 0.4 us)
Async XLA Ops:
  0.6 1.0 %slice-start = ((bf16[3,64,2,8,128]{4,3,2,1,0:T(8,128)(2,1)}), bf16[1,64,2,8,128]{4,3,2,1,0:T(8,128)(2,1)S(1)}, s32[]{:S(2)}) async-start(bf16[3,64,2,8,128]{4,3,2,1,0:T(8,128)(2,1)} %param.3), calls=%async_computation | async-start | bytes 524288 | tf_op jit(solution)/shard_map/slice | solution.py:285
  1.7 15.2 %copy-start.1 = (bf16[3,64,2,8,128]{4,3,2,1,0:T(8,128)(2,1)S(1)}, bf16[3,64,2,8,128]{4,3,2,1,0:T(8,128)(2,1)}, u32[]{:S(2)}) copy-start(bf16[3,64,2,8,128]{4,3,2,1,0:T(8,128)(2,1)} %param.3) | copy-start | bytes 2359300
  1.8 6.6 %collective-permute-start.1 = (bf16[64,1024]{1,0:T(8,128)(2,1)S(1)}, bf16[64,1024]{1,0:T(8,128)(2,1)S(1)}, u32[]{:S(2)}, u32[]{:S(2)}) collective-permute-start(bf16[64,1024]{1,0:T(8,128)(2,1)S(1)} %get-tuple-element.39), channel_id=1, source_target_pairs={{4,8},{12,16},{20,24},{8,4},{16,12},{24,20},{5,9},{13,17},{21,25},... | collective-permute-start | bytes 393224 | tf_op jit(solution)/shard_map/ppermute | solution.py:35
  2.6 10.6 %collective-permute-start = (bf16[64,1024]{1,0:T(8,128)(2,1)S(1)}, bf16[64,1024]{1,0:T(8,128)(2,1)S(1)}, u32[]{:S(2)}, u32[]{:S(2)}) collective-permute-start(bf16[64,1024]{1,0:T(8,128)(2,1)S(1)} %get-tuple-element.40), channel_id=1, source_target_pairs={{0,4},{8,12},{16,20},{24,28},{4,0},{12,8},{20,16},{28,24},{1,5},{9... | collective-permute-start | bytes 393224 | tf_op jit(solution)/shard_map/ppermute | solution.py:34
  13.3 5.5 %collective-permute-start.3 = (bf16[64,512]{1,0:T(8,128)(2,1)S(1)}, bf16[64,512]{1,0:T(8,128)(2,1)S(1)}, u32[]{:S(2)}, u32[]{:S(2)}) collective-permute-start(bf16[64,512]{1,0:T(8,128)(2,1)S(1)} %get-tuple-element.53), channel_id=1, source_target_pairs={{1,2},{2,1},{5,6},{6,5},{9,10},{10,9},{13,14},{14,13},{17,18},{18,... | collective-permute-start | bytes 196616 | tf_op jit(solution)/shard_map/ppermute | solution.py:35
  13.9 4.9 %collective-permute-start.2 = (bf16[64,512]{1,0:T(8,128)(2,1)S(1)}, bf16[64,512]{1,0:T(8,128)(2,1)S(1)}, u32[]{:S(2)}, u32[]{:S(2)}) collective-permute-start(bf16[64,512]{1,0:T(8,128)(2,1)S(1)} %get-tuple-element.54), channel_id=1, source_target_pairs={{0,1},{2,3},{1,0},{3,2},{4,5},{6,7},{5,4},{7,6},{8,9},{10,11},{9,8... | collective-permute-start | bytes 196616 | tf_op jit(solution)/shard_map/ppermute | solution.py:34
  18.8 0.9 %copy-start = (f32[27,16,128]{2,1,0:T(8,128)S(1)}, f32[27,16,128]{2,1,0:T(8,128)}, u32[]{:S(2)}) copy-start(f32[27,16,128]{2,1,0:T(8,128)} %coefficients.1.coef) | copy-start | bytes 663556
  21.8 1.3 %collective-permute-start.4 = (f32[32,640]{1,0:T(8,128)S(1)}, f32[32,640]{1,0:T(8,128)S(1)}, u32[]{:S(2)}, u32[]{:S(2)}) collective-permute-start(f32[32,640]{1,0:T(8,128)S(1)} %slice_select_fusion), channel_id=1, source_target_pairs={{0,1},{1,0},{2,3},{3,2},{4,5},{5,4},{6,7},{7,6},{8,9},{9,8},{10,11... | collective-permute-start | bytes 245768 | tf_op jit(solution)/shard_map/ppermute | solution.py:242
  23.1 5.5 %collective-permute-start.7 = (f32[32,640]{1,0:T(8,128)S(1)}, f32[32,640]{1,0:T(8,128)S(1)}, u32[]{:S(2)}, u32[]{:S(2)}) collective-permute-start(f32[32,640]{1,0:T(8,128)S(1)} %select_add_fusion), channel_id=1, source_target_pairs={{0,6},{1,7},{2,4},{3,5},{4,2},{5,3},{6,0},{7,1},{8,14},{9,15},{10,... | collective-permute-start | bytes 245768 | tf_op jit(solution)/shard_map/ppermute | solution.py:242
  25.8 4.4 %collective-permute-start.6 = (f32[32,640]{1,0:T(8,128)S(1)}, f32[32,640]{1,0:T(8,128)S(1)}, u32[]{:S(2)}, u32[]{:S(2)}) collective-permute-start(f32[32,640]{1,0:T(8,128)S(1)} %select_add_fusion), channel_id=1, source_target_pairs={{0,4},{1,5},{2,6},{3,7},{4,0},{5,1},{6,2},{7,3},{8,12},{9,13},{10,... | collective-permute-start | bytes 245768 | tf_op jit(solution)/shard_map/ppermute | solution.py:242
  25.8 4.6 %collective-permute-start.5 = (f32[32,640]{1,0:T(8,128)S(1)}, f32[32,640]{1,0:T(8,128)S(1)}, u32[]{:S(2)}, u32[]{:S(2)}) collective-permute-start(f32[32,640]{1,0:T(8,128)S(1)} %select_add_fusion), channel_id=1, source_target_pairs={{0,2},{1,3},{2,0},{3,1},{4,6},{5,7},{6,4},{7,5},{8,10},{9,11},{10,... | collective-permute-start | bytes 245768 | tf_op jit(solution)/shard_map/ppermute | solution.py:242
  30.4 7.7 %collective-permute-start.10 = (f32[32,640]{1,0:T(8,128)S(1)}, f32[32,640]{1,0:T(8,128)S(1)}, u32[]{:S(2)}, u32[]{:S(2)}) collective-permute-start(f32[32,640]{1,0:T(8,128)S(1)} %add_add_fusion.1), channel_id=1, source_target_pairs={{0,24},{1,25},{2,26},{3,27},{4,28},{5,29},{6,30},{7,31},{8,16},{9,... | collective-permute-start | bytes 245768 | tf_op jit(solution)/shard_map/ppermute | solution.py:242
  35.1 6.7 %collective-permute-start.9 = (f32[32,640]{1,0:T(8,128)S(1)}, f32[32,640]{1,0:T(8,128)S(1)}, u32[]{:S(2)}, u32[]{:S(2)}) collective-permute-start(f32[32,640]{1,0:T(8,128)S(1)} %add_add_fusion.1), channel_id=1, source_target_pairs={{0,16},{1,17},{2,18},{3,19},{4,20},{5,21},{6,22},{7,23},{8,24},{9,... | collective-permute-start | bytes 245768 | tf_op jit(solution)/shard_map/ppermute | solution.py:242
  35.1 6.7 %collective-permute-start.8 = (f32[32,640]{1,0:T(8,128)S(1)}, f32[32,640]{1,0:T(8,128)S(1)}, u32[]{:S(2)}, u32[]{:S(2)}) collective-permute-start(f32[32,640]{1,0:T(8,128)S(1)} %add_add_fusion.1), channel_id=1, source_target_pairs={{0,8},{1,9},{2,10},{3,11},{4,12},{5,13},{6,14},{7,15},{8,0},{9,1},... | collective-permute-start | bytes 245768 | tf_op jit(solution)/shard_map/ppermute | solution.py:242
  41.7 1.3 %collective-permute-start.11 = (f32[32,640]{1,0:T(8,128)S(1)}, f32[32,640]{1,0:T(8,128)S(1)}, u32[]{:S(2)}, u32[]{:S(2)}) collective-permute-start(f32[32,640]{1,0:T(8,128)S(1)} %add_add_fusion), channel_id=1, source_target_pairs={{0,1},{1,0},{2,3},{3,2},{4,5},{5,4},{6,7},{7,6},{8,9},{9,8},{10,11... | collective-permute-start | bytes 245768 | tf_op jit(solution)/shard_map/ppermute | solution.py:242
  50.1 4.2 %collective-permute-start.13 = (bf16[64,1024]{1,0:T(8,128)(2,1)S(1)}, bf16[64,1024]{1,0:T(8,128)(2,1)S(1)}, u32[]{:S(2)}, u32[]{:S(2)}) collective-permute-start(bf16[64,1024]{1,0:T(8,128)(2,1)S(1)} %get-tuple-element.31), channel_id=1, source_target_pairs={{4,8},{12,16},{20,24},{8,4},{16,12},{24,20},{5,9},{13,17},{21,25},... | collective-permute-start | bytes 393224 | tf_op jit(solution)/shard_map/ppermute | solution.py:35
  50.8 9.1 %collective-permute-start.12 = (bf16[64,1024]{1,0:T(8,128)(2,1)S(1)}, bf16[64,1024]{1,0:T(8,128)(2,1)S(1)}, u32[]{:S(2)}, u32[]{:S(2)}) collective-permute-start(bf16[64,1024]{1,0:T(8,128)(2,1)S(1)} %get-tuple-element.32), channel_id=1, source_target_pairs={{0,4},{8,12},{16,20},{24,28},{4,0},{12,8},{20,16},{28,24},{1,5},{9... | collective-permute-start | bytes 393224 | tf_op jit(solution)/shard_map/ppermute | solution.py:34
  60.0 2.7 %collective-permute-start.15 = (bf16[64,512]{1,0:T(8,128)(2,1)S(1)}, bf16[64,512]{1,0:T(8,128)(2,1)S(1)}, u32[]{:S(2)}, u32[]{:S(2)}) collective-permute-start(bf16[64,512]{1,0:T(8,128)(2,1)S(1)} %get-tuple-element.45), channel_id=1, source_target_pairs={{1,2},{2,1},{5,6},{6,5},{9,10},{10,9},{13,14},{14,13},{17,18},{18,... | collective-permute-start | bytes 196616 | tf_op jit(solution)/shard_map/ppermute | solution.py:35
  60.7 3.0 %collective-permute-start.14 = (bf16[64,512]{1,0:T(8,128)(2,1)S(1)}, bf16[64,512]{1,0:T(8,128)(2,1)S(1)}, u32[]{:S(2)}, u32[]{:S(2)}) collective-permute-start(bf16[64,512]{1,0:T(8,128)(2,1)S(1)} %get-tuple-element.46), channel_id=1, source_target_pairs={{0,1},{2,3},{1,0},{3,2},{4,5},{6,7},{5,4},{7,6},{8,9},{10,11},{9,8... | collective-permute-start | bytes 196616 | tf_op jit(solution)/shard_map/ppermute | solution.py:34
  65.3 2.7 %collective-permute-start.16 = (f32[32,256]{1,0:T(8,128)S(1)}, f32[32,256]{1,0:T(8,128)S(1)}, u32[]{:S(2)}, u32[]{:S(2)}) collective-permute-start(f32[32,256]{1,0:T(8,128)S(1)} %slice_select_fusion.1), channel_id=1, source_target_pairs={{0,1},{1,0},{2,3},{3,2},{4,5},{5,4},{6,7},{7,6},{8,9},{9,8},{10,11... | collective-permute-start | bytes 98312 | tf_op jit(solution)/shard_map/ppermute | solution.py:242
  67.9 5.0 %collective-permute-start.19 = (f32[32,256]{1,0:T(8,128)S(1)}, f32[32,256]{1,0:T(8,128)S(1)}, u32[]{:S(2)}, u32[]{:S(2)}) collective-permute-start(f32[32,256]{1,0:T(8,128)S(1)} %select_add_fusion.1), channel_id=1, source_target_pairs={{0,6},{1,7},{2,4},{3,5},{4,2},{5,3},{6,0},{7,1},{8,14},{9,15},{10,... | collective-permute-start | bytes 98312 | tf_op jit(solution)/shard_map/ppermute | solution.py:242
  71.0 3.9 %collective-permute-start.18 = (f32[32,256]{1,0:T(8,128)S(1)}, f32[32,256]{1,0:T(8,128)S(1)}, u32[]{:S(2)}, u32[]{:S(2)}) collective-permute-start(f32[32,256]{1,0:T(8,128)S(1)} %select_add_fusion.1), channel_id=1, source_target_pairs={{0,4},{1,5},{2,6},{3,7},{4,0},{5,1},{6,2},{7,3},{8,12},{9,13},{10,... | collective-permute-start | bytes 98312 | tf_op jit(solution)/shard_map/ppermute | solution.py:242
  71.0 3.9 %collective-permute-start.17 = (f32[32,256]{1,0:T(8,128)S(1)}, f32[32,256]{1,0:T(8,128)S(1)}, u32[]{:S(2)}, u32[]{:S(2)}) collective-permute-start(f32[32,256]{1,0:T(8,128)S(1)} %select_add_fusion.1), channel_id=1, source_target_pairs={{0,2},{1,3},{2,0},{3,1},{4,6},{5,7},{6,4},{7,5},{8,10},{9,11},{10,... | collective-permute-start | bytes 98312 | tf_op jit(solution)/shard_map/ppermute | solution.py:242
  75.0 6.0 %collective-permute-start.22 = (f32[32,256]{1,0:T(8,128)S(1)}, f32[32,256]{1,0:T(8,128)S(1)}, u32[]{:S(2)}, u32[]{:S(2)}) collective-permute-start(f32[32,256]{1,0:T(8,128)S(1)} %add_add_fusion.3), channel_id=1, source_target_pairs={{0,24},{1,25},{2,26},{3,27},{4,28},{5,29},{6,30},{7,31},{8,16},{9,... | collective-permute-start | bytes 98312 | tf_op jit(solution)/shard_map/ppermute | solution.py:242
  77.7 4.8 %collective-permute-start.21 = (f32[32,256]{1,0:T(8,128)S(1)}, f32[32,256]{1,0:T(8,128)S(1)}, u32[]{:S(2)}, u32[]{:S(2)}) collective-permute-start(f32[32,256]{1,0:T(8,128)S(1)} %add_add_fusion.3), channel_id=1, source_target_pairs={{0,16},{1,17},{2,18},{3,19},{4,20},{5,21},{6,22},{7,23},{8,24},{9,... | collective-permute-start | bytes 98312 | tf_op jit(solution)/shard_map/ppermute | solution.py:242
  78.2 4.4 %collective-permute-start.20 = (f32[32,256]{1,0:T(8,128)S(1)}, f32[32,256]{1,0:T(8,128)S(1)}, u32[]{:S(2)}, u32[]{:S(2)}) collective-permute-start(f32[32,256]{1,0:T(8,128)S(1)} %add_add_fusion.3), channel_id=1, source_target_pairs={{0,8},{1,9},{2,10},{3,11},{4,12},{5,13},{6,14},{7,15},{8,0},{9,1},... | collective-permute-start | bytes 98312 | tf_op jit(solution)/shard_map/ppermute | solution.py:242
  82.5 1.3 %collective-permute-start.23 = (f32[32,256]{1,0:T(8,128)S(1)}, f32[32,256]{1,0:T(8,128)S(1)}, u32[]{:S(2)}, u32[]{:S(2)}) collective-permute-start(f32[32,256]{1,0:T(8,128)S(1)} %add_add_fusion.2), channel_id=1, source_target_pairs={{0,1},{1,0},{2,3},{3,2},{4,5},{5,4},{6,7},{7,6},{8,9},{9,8},{10,11... | collective-permute-start | bytes 98312 | tf_op jit(solution)/shard_map/ppermute | solution.py:242

commit v6 on v5

--- a/solution.py
+++ b/solution.py
@@ -80,6 +80,7 @@
             pl.BlockSpec(memory_space=pltpu.VMEM),
         ],
         out_specs=pl.BlockSpec(memory_space=pltpu.VMEM),
+        compiler_params=pltpu.CompilerParams(vmem_limit_bytes=4 * 1024 * 1024),
         name="coefficients",
     )(table, cell_map.reshape(lines, depth))
 
@@ -236,28 +237,24 @@
     block[...] = dot(inverse.astype(jnp.bfloat16), w.astype(jnp.bfloat16)).astype(jnp.bfloat16)
 
 
-def partner(part, mask):
-    axes = ("slab", "col")
-    count = lax.axis_size("slab") * lax.axis_size("col")
-    return lax.ppermute(part, axes, [(i, i ^ mask) for i in range(count)])
+def moved(part, pairs):
+    return lax.ppermute(part, ("slab", "col"), pairs)
 
 
 def whole_sum(part):
     count = lax.axis_size("slab") * lax.axis_size("col")
-    half = part.shape[0] // 2
-    upper = lax.axis_index("col") % 2 == 1
-    low, high = part[:half], part[half:]
-    part = jnp.where(upper, high, low) + partner(jnp.where(upper, low, high), 1)
+    second = range(1, count, 2)
+    part = part + moved(part, [(i - 1, i) for i in second])
     bit = 2
     while bit < count:
-        if 2 * bit < count:
-            one, two, both = (partner(part, mask) for mask in (bit, 2 * bit, 3 * bit))
-            part = (part + one) + (two + both)
-        else:
-            part = part + partner(part, bit)
+        masks = [mask for mask in (bit, 2 * bit, 3 * bit) if mask < count]
+        given = [moved(part, [(i, i ^ mask) for i in second]) for mask in masks]
+        part = part + given[0]
+        if len(given) == 3:
+            part = part + (given[1] + given[2])
         bit *= 4
-    other = partner(part, 1)
-    return jnp.concatenate([jnp.where(upper, other, part), jnp.where(upper, part, other)], axis=0)
+    back = moved(part, [(i, i - 1) for i in second])
+    return jnp.where(lax.axis_index("col") % 2 == 1, part, back)
 
 
 def call(kernel, name, outs, *args):

time: 92 us -> 113 us (1.23)
  waiting for transfers between devices: 31.3 us -> 57.7 us
  starting transfers between devices: 36.9 us -> 32.7 us
    ppermute x16, waiting for transfers between devices: 20 us -> 46.4 us  [moved(): return lax.ppermute(part, ('slab', 'col'), pairs)]
    ppermute x16, starting transfers between devices: 19.8 us -> 16 us  [moved(): return lax.ppermute(part, ('slab', 'col'), pairs)]
  transfers between devices with their start and end apart: 24 -> 24, of which waited for: 16 -> 7; matrix products, arithmetic and copies ran while one was open for 0% -> 0% of each run, Pallas kernels for 2% -> 1%
where the time goes in v6:
time: 113 us
  waiting for transfers between devices  57.7 us (51%)
  starting transfers between devices  32.7 us (29%)
  Pallas kernels  18.4 us (16%)
  local copies, waits for them, and re-layouts  2.55 us (2%)
    ppermute x16, waiting for transfers between devices, moved(): return lax.ppermute(part, ('slab', 'col'), pairs)  46.4 us
    pallas_call x4, Pallas kernels, call(): pl.pallas_call(kernel, out_shape=[jax.ShapeDtypeStruct(shape, dtype) for...  17.6 us
    ppermute x16, starting transfers between devices, moved(): return lax.ppermute(part, ('slab', 'col'), pairs)  16 us
    ppermute x4, starting transfers between devices, exchange(): inner = lax.ppermute(jnp.where(odd, downward, upward), axis, swaps[0])  13.9 us
    ppermute x4, waiting for transfers between devices, exchange(): inner = lax.ppermute(jnp.where(odd, downward, upward), axis, swaps[0])  11.3 us
    ppermute x4, starting transfers between devices, exchange(): outer = lax.ppermute(jnp.where(odd, upward, downward), axis, swaps[1])  2.8 us
  transfers between devices with their start and end apart: 24, of which 7 were waited for; matrix products, arithmetic and copies ran while one was open for 0% of the time, Pallas kernels for 1%

profile of v6, /device:TPU:0, one launch (start us, length us, event | category | flops | bytes accessed | tf_op | source)
XLA Modules:
  0.0 112.8 jit_solution(13157985205591247554)
XLA Ops:
  0.6 0.0 slice-start
  0.7 0.9 slice-done
  1.6 0.1 slice.67
  1.7 0.0 copy-start.2
  1.8 0.8 collective-permute-start.1
  2.6 5.8 %collective-permute-start = (bf16[64,1024]{1,0:T(8,128)(2,1)S(1)}, bf16[64,1024]{1,0:T(8,128)(2,1)S(1)}, u32[]{:S(2)}, u32[]{:S(2)}) collective-permute-start(bf16[64,1024]{1,0:T(8,128)(2,1)S(1)} %get-tuple-element.40), channel_id=1, source_target_pairs={{0,4},{8,12},{16,20},{24,28},{4,0},{12,8},{20,16},{28,24},{1,5},{9... | collective-permute-start | bytes 393224 | tf_op jit(solution)/shard_map/ppermute | solution.py:34
  8.4 0.0 collective-permute-done.1
  8.4 4.8 %collective-permute-done = bf16[64,1024]{1,0:T(8,128)(2,1)S(1)} collective-permute-done((bf16[64,1024]{1,0:T(8,128)(2,1)S(1)}, bf16[64,1024]{1,0:T(8,128)(2,1)S(1)}, u32[]{:S(2)}, u32[]{:S(2)}) %collective-permute-start) | collective-permute-done | bytes 131104 | tf_op jit(solution)/shard_map/ppermute | solution.py:34
  13.3 0.7 collective-permute-start.3
  13.9 0.0 copy-start
  14.0 2.9 %collective-permute-start.2 = (bf16[64,512]{1,0:T(8,128)(2,1)S(1)}, bf16[64,512]{1,0:T(8,128)(2,1)S(1)}, u32[]{:S(2)}, u32[]{:S(2)}) collective-permute-start(bf16[64,512]{1,0:T(8,128)(2,1)S(1)} %get-tuple-element.52), channel_id=1, source_target_pairs={{0,1},{2,3},{1,0},{3,2},{4,5},{6,7},{5,4},{7,6},{8,9},{10,11},{9,8... | collective-permute-start | bytes 196616 | tf_op jit(solution)/shard_map/ppermute | solution.py:34
  16.9 0.0 copy-done.2
  16.9 0.0 copy-start.1
  16.9 0.3 reshape.17.stack
  17.2 0.0 copy-done
  17.3 0.3 copy-done.1
  17.6 0.8 coefficients.1.coef
  18.4 0.0 collective-permute-done.3
  18.4 0.0 collective-permute-done.2
  18.4 2.0 %first_image.1 = (bf16[64,2048]{1,0:T(8,128)(2,1)S(1)}, f32[64,640]{1,0:T(8,128)S(1)}) custom-call(f32[27,16,128]{2,1,0:T(8,128)S(1)} %coefficients.1.coef, bf16[192,2048]{1,0:T(8,128)(2,1)S(1)} %reshape.17.stack, bf16[64,1024]{1,0:T(8,128)(2,1)S(1)} %get-tuple-element.38.xlo, bf16[64,1024]{1,0:T(8,128)(2,1)S(1)} %get-tuple-element.37.xhi, ...), custom_call_target="tpu_custom_call" | custom-call | tf_op jit(solution)/shard_map/first_image/pallas_call | solution.py:261
  20.4 2.4 %collective-permute-start.4 = (f32[64,640]{1,0:T(8,128)S(1)}, f32[64,640]{1,0:T(8,128)S(1)}, u32[]{:S(2)}, u32[]{:S(2)}) collective-permute-start(f32[64,640]{1,0:T(8,128)S(1)} %get-tuple-element.14), channel_id=1, source_target_pairs={{0,1},{2,3},{4,5},{6,7},{8,9},{10,11},{12,13},{14,15},{16,17},{18,... | collective-permute-start | bytes 491528 | tf_op jit(solution)/shard_map/ppermute | solution.py:241
  22.8 1.0 collective-permute-done.4
  23.9 0.7 collective-permute-start.7
  24.6 0.7 collective-permute-start.6
  25.2 0.7 collective-permute-start.5
  25.9 0.0 collective-permute-done.7
  25.9 0.0 collective-permute-done.6
  25.9 0.0 collective-permute-done.5
  26.0 0.7 collective-permute-start.10
  26.7 0.7 collective-permute-start.9
  27.3 0.7 collective-permute-start.8
  28.0 0.0 collective-permute-done.10
  28.0 0.0 collective-permute-done.9
  28.0 0.0 collective-permute-done.8
  28.1 1.3 %collective-permute-start.11 = (f32[64,640]{1,0:T(8,128)S(1)}, f32[64,640]{1,0:T(8,128)S(1)}, u32[]{:S(2)}, u32[]{:S(2)}) collective-permute-start(f32[64,640]{1,0:T(8,128)S(1)} %add_add_fusion), channel_id=1, source_target_pairs={{1,0},{3,2},{5,4},{7,6},{9,8},{11,10},{13,12},{15,14},{17,16},{19,... | collective-permute-start | bytes 491528 | tf_op jit(solution)/shard_map/ppermute | solution.py:241
  29.4 24.5 %collective-permute-done.11 = f32[64,640]{1,0:T(8,128)S(1)} collective-permute-done((f32[64,640]{1,0:T(8,128)S(1)}, f32[64,640]{1,0:T(8,128)S(1)}, u32[]{:S(2)}, u32[]{:S(2)}) %collective-permute-start.11) | collective-permute-done | bytes 163872 | tf_op jit(solution)/shard_map/ppermute | solution.py:241
  53.9 7.0 %first_solve.1 = (bf16[64,2048]{1,0:T(8,128)(2,1)S(1)}, f32[64,192]{1,0:T(8,128)S(1)}, f32[64,64]{1,0:T(8,128)S(1)}, f32[192,192]{1,0:T(8,128)S(1)}) custom-call(f32[64,640]{1,0:T(8,128)S(1)} %broadcast_select_fusion.8.cross, bf16[192,2048]{1,0:T(8,128)(2,1)S(1)} %reshape.17.stack, bf16[64,2048]{1,0:T(8,128)(2,1)S(1)} %get-tuple-element.15.image), custom_call_target="tpu_custom_call" | custom-call | tf_op jit(solution)/shard_map/first_solve/pallas_call | solution.py:261
  60.9 0.7 collective-permute-start.13
  61.6 2.6 %collective-permute-start.12 = (bf16[64,1024]{1,0:T(8,128)(2,1)S(1)}, bf16[64,1024]{1,0:T(8,128)(2,1)S(1)}, u32[]{:S(2)}, u32[]{:S(2)}) collective-permute-start(bf16[64,1024]{1,0:T(8,128)(2,1)S(1)} %get-tuple-element.32), channel_id=1, source_target_pairs={{0,4},{8,12},{16,20},{24,28},{4,0},{12,8},{20,16},{28,24},{1,5},{9... | collective-permute-start | bytes 393224 | tf_op jit(solution)/shard_map/ppermute | solution.py:34
  64.2 0.0 collective-permute-done.13
  64.2 5.6 %collective-permute-done.12 = bf16[64,1024]{1,0:T(8,128)(2,1)S(1)} collective-permute-done((bf16[64,1024]{1,0:T(8,128)(2,1)S(1)}, bf16[64,1024]{1,0:T(8,128)(2,1)S(1)}, u32[]{:S(2)}, u32[]{:S(2)}) %collective-permute-start.12) | collective-permute-done | bytes 131104 | tf_op jit(solution)/shard_map/ppermute | solution.py:34
  69.9 0.7 collective-permute-start.15
  70.5 2.6 %collective-permute-start.14 = (bf16[64,512]{1,0:T(8,128)(2,1)S(1)}, bf16[64,512]{1,0:T(8,128)(2,1)S(1)}, u32[]{:S(2)}, u32[]{:S(2)}) collective-permute-start(bf16[64,512]{1,0:T(8,128)(2,1)S(1)} %get-tuple-element.44), channel_id=1, source_target_pairs={{0,1},{2,3},{1,0},{3,2},{4,5},{6,7},{5,4},{7,6},{8,9},{10,11},{9,8... | collective-permute-start | bytes 196616 | tf_op jit(solution)/shard_map/ppermute | solution.py:34
  73.1 0.0 collective-permute-done.15
  73.1 0.9 collective-permute-done.14
  74.0 1.6 %second_image.1 = (bf16[64,2048]{1,0:T(8,128)(2,1)S(1)}, f32[64,256]{1,0:T(8,128)S(1)}) custom-call(f32[27,16,128]{2,1,0:T(8,128)S(1)} %coefficients.1.coef, bf16[192,2048]{1,0:T(8,128)(2,1)S(1)} %reshape.17.stack, bf16[64,2048]{1,0:T(8,128)(2,1)S(1)} %get-tuple-element.16.block.last, bf16[64,1024]{1,0:T(8,128)(2,1)S(1)} %get-tuple-element.30.xlo, ...), custom_call_target="tpu_custom_call" | custom-call | tf_op jit(solution)/shard_map/second_image/pallas_call | solution.py:261
  75.6 3.0 %collective-permute-start.16 = (f32[64,256]{1,0:T(8,128)S(1)}, f32[64,256]{1,0:T(8,128)S(1)}, u32[]{:S(2)}, u32[]{:S(2)}) collective-permute-start(f32[64,256]{1,0:T(8,128)S(1)} %get-tuple-element.17), channel_id=1, source_target_pairs={{0,1},{2,3},{4,5},{6,7},{8,9},{10,11},{12,13},{14,15},{16,17},{18,... | collective-permute-start | bytes 196616 | tf_op jit(solution)/shard_map/ppermute | solution.py:241
  78.5 0.9 collective-permute-done.16
  79.4 0.7 collective-permute-start.19
  80.1 0.7 collective-permute-start.18
  80.8 0.7 collective-permute-start.17
  81.5 0.0 collective-permute-done.19
  81.5 0.0 collective-permute-done.18
  81.5 0.0 collective-permute-done.17
  81.5 0.7 collective-permute-start.22
  82.2 0.7 collective-permute-start.21
  82.9 0.7 collective-permute-start.20
  83.5 0.0 collective-permute-done.22
  83.5 0.0 collective-permute-done.21
  83.6 0.0 collective-permute-done.20
  83.6 1.3 %collective-permute-start.23 = (f32[64,256]{1,0:T(8,128)S(1)}, f32[64,256]{1,0:T(8,128)S(1)}, u32[]{:S(2)}, u32[]{:S(2)}) collective-permute-start(f32[64,256]{1,0:T(8,128)S(1)} %add_add_fusion.2), channel_id=1, source_target_pairs={{1,0},{3,2},{5,4},{7,6},{9,8},{11,10},{13,12},{15,14},{17,16},{19,... | collective-permute-start | bytes 196616 | tf_op jit(solution)/shard_map/ppermute | solution.py:241
  84.9 20.0 %collective-permute-done.23 = f32[64,256]{1,0:T(8,128)S(1)} collective-permute-done((f32[64,256]{1,0:T(8,128)S(1)}, f32[64,256]{1,0:T(8,128)S(1)}, u32[]{:S(2)}, u32[]{:S(2)}) %collective-permute-start.23) | collective-permute-done | bytes 65568 | tf_op jit(solution)/shard_map/ppermute | solution.py:241
  104.9 7.1 %second_solve.1 = (bf16[64,2048]{1,0:T(8,128)(2,1)S(1)}, f32[2,64,192]{2,1,0:T(8,128)}, f32[2,64,64]{2,1,0:T(8,128)}) custom-call(f32[64,256]{1,0:T(8,128)S(1)} %broadcast_select_fusion.17.cross, f32[192,192]{1,0:T(8,128)S(1)} %get-tuple-element.18.own, bf16[192,2048]{1,0:T(8,128)(2,1)S(1)} %reshape.17.stack, ...), custom_call_target="tpu_custom_call" | custom-call | tf_op jit(solution)/shard_map/second_solve/pallas_call | solution.py:261
  112.0 0.7 copy.6
  (21 shorter events, 0.4 us)
Async XLA Ops:
  0.6 1.0 slice-start
  1.7 15.2 %copy-start.2 = (bf16[3,64,2,8,128]{4,3,2,1,0:T(8,128)(2,1)S(1)}, bf16[3,64,2,8,128]{4,3,2,1,0:T(8,128)(2,1)}, u32[]{:S(2)}) copy-start(bf16[3,64,2,8,128]{4,3,2,1,0:T(8,128)(2,1)} %param.3) | copy-start | bytes 2359300
  1.8 6.6 %collective-permute-start.1 = (bf16[64,1024]{1,0:T(8,128)(2,1)S(1)}, bf16[64,1024]{1,0:T(8,128)(2,1)S(1)}, u32[]{:S(2)}, u32[]{:S(2)}) collective-permute-start(bf16[64,1024]{1,0:T(8,128)(2,1)S(1)} %get-tuple-element.39), channel_id=1, source_target_pairs={{4,8},{12,16},{20,24},{8,4},{16,12},{24,20},{5,9},{13,17},{21,25},... | collective-permute-start | bytes 393224 | tf_op jit(solution)/shard_map/ppermute | solution.py:35
  2.6 10.6 %collective-permute-start = (bf16[64,1024]{1,0:T(8,128)(2,1)S(1)}, bf16[64,1024]{1,0:T(8,128)(2,1)S(1)}, u32[]{:S(2)}, u32[]{:S(2)}) collective-permute-start(bf16[64,1024]{1,0:T(8,128)(2,1)S(1)} %get-tuple-element.40), channel_id=1, source_target_pairs={{0,4},{8,12},{16,20},{24,28},{4,0},{12,8},{20,16},{28,24},{1,5},{9... | collective-permute-start | bytes 393224 | tf_op jit(solution)/shard_map/ppermute | solution.py:34
  13.3 5.1 %collective-permute-start.3 = (bf16[64,512]{1,0:T(8,128)(2,1)S(1)}, bf16[64,512]{1,0:T(8,128)(2,1)S(1)}, u32[]{:S(2)}, u32[]{:S(2)}) collective-permute-start(bf16[64,512]{1,0:T(8,128)(2,1)S(1)} %get-tuple-element.51), channel_id=1, source_target_pairs={{1,2},{2,1},{5,6},{6,5},{9,10},{10,9},{13,14},{14,13},{17,18},{18,... | collective-permute-start | bytes 196616 | tf_op jit(solution)/shard_map/ppermute | solution.py:35
  13.9 3.3 %copy-start = (s32[2,8,128]{2,1,0:T(8,128)S(1)}, s32[2,8,128]{2,1,0:T(8,128)}, u32[]{:S(2)}) copy-start(s32[2,8,128]{2,1,0:T(8,128)} %param.4) | copy-start | bytes 24580
  14.0 4.4 %collective-permute-start.2 = (bf16[64,512]{1,0:T(8,128)(2,1)S(1)}, bf16[64,512]{1,0:T(8,128)(2,1)S(1)}, u32[]{:S(2)}, u32[]{:S(2)}) collective-permute-start(bf16[64,512]{1,0:T(8,128)(2,1)S(1)} %get-tuple-element.52), channel_id=1, source_target_pairs={{0,1},{2,3},{1,0},{3,2},{4,5},{6,7},{5,4},{7,6},{8,9},{10,11},{9,8... | collective-permute-start | bytes 196616 | tf_op jit(solution)/shard_map/ppermute | solution.py:34
  16.9 0.7 copy-start.1
  20.4 3.4 %collective-permute-start.4 = (f32[64,640]{1,0:T(8,128)S(1)}, f32[64,640]{1,0:T(8,128)S(1)}, u32[]{:S(2)}, u32[]{:S(2)}) collective-permute-start(f32[64,640]{1,0:T(8,128)S(1)} %get-tuple-element.14), channel_id=1, source_target_pairs={{0,1},{2,3},{4,5},{6,7},{8,9},{10,11},{12,13},{14,15},{16,17},{18,... | collective-permute-start | bytes 491528 | tf_op jit(solution)/shard_map/ppermute | solution.py:241
  23.9 2.0 %collective-permute-start.7 = (f32[64,640]{1,0:T(8,128)S(1)}, f32[64,640]{1,0:T(8,128)S(1)}, u32[]{:S(2)}, u32[]{:S(2)}) collective-permute-start(f32[64,640]{1,0:T(8,128)S(1)} %add.55), channel_id=1, source_target_pairs={{1,7},{3,5},{5,3},{7,1},{9,15},{11,13},{13,11},{15,9},{17,23},{19,... | collective-permute-start | bytes 491528 | tf_op jit(solution)/shard_map/ppermute | solution.py:241
  24.6 1.4 %collective-permute-start.6 = (f32[64,640]{1,0:T(8,128)S(1)}, f32[64,640]{1,0:T(8,128)S(1)}, u32[]{:S(2)}, u32[]{:S(2)}) collective-permute-start(f32[64,640]{1,0:T(8,128)S(1)} %add.55), channel_id=1, source_target_pairs={{1,5},{3,7},{5,1},{7,3},{9,13},{11,15},{13,9},{15,11},{17,21},{19,... | collective-permute-start | bytes 491528 | tf_op jit(solution)/shard_map/ppermute | solution.py:241
  25.2 0.7 collective-permute-start.5
  26.0 2.0 %collective-permute-start.10 = (f32[64,640]{1,0:T(8,128)S(1)}, f32[64,640]{1,0:T(8,128)S(1)}, u32[]{:S(2)}, u32[]{:S(2)}) collective-permute-start(f32[64,640]{1,0:T(8,128)S(1)} %add_add_fusion.1), channel_id=1, source_target_pairs={{1,25},{3,27},{5,29},{7,31},{9,17},{11,19},{13,21},{15,23},{17,9},... | collective-permute-start | bytes 491528 | tf_op jit(solution)/shard_map/ppermute | solution.py:241
  26.7 1.4 %collective-permute-start.9 = (f32[64,640]{1,0:T(8,128)S(1)}, f32[64,640]{1,0:T(8,128)S(1)}, u32[]{:S(2)}, u32[]{:S(2)}) collective-permute-start(f32[64,640]{1,0:T(8,128)S(1)} %add_add_fusion.1), channel_id=1, source_target_pairs={{1,17},{3,19},{5,21},{7,23},{9,25},{11,27},{13,29},{15,31},{17,1},... | collective-permute-start | bytes 491528 | tf_op jit(solution)/shard_map/ppermute | solution.py:241
  27.3 0.7 collective-permute-start.8
  28.1 25.8 %collective-permute-start.11 = (f32[64,640]{1,0:T(8,128)S(1)}, f32[64,640]{1,0:T(8,128)S(1)}, u32[]{:S(2)}, u32[]{:S(2)}) collective-permute-start(f32[64,640]{1,0:T(8,128)S(1)} %add_add_fusion), channel_id=1, source_target_pairs={{1,0},{3,2},{5,4},{7,6},{9,8},{11,10},{13,12},{15,14},{17,16},{19,... | collective-permute-start | bytes 491528 | tf_op jit(solution)/shard_map/ppermute | solution.py:241
  60.9 3.3 %collective-permute-start.13 = (bf16[64,1024]{1,0:T(8,128)(2,1)S(1)}, bf16[64,1024]{1,0:T(8,128)(2,1)S(1)}, u32[]{:S(2)}, u32[]{:S(2)}) collective-permute-start(bf16[64,1024]{1,0:T(8,128)(2,1)S(1)} %get-tuple-element.31), channel_id=1, source_target_pairs={{4,8},{12,16},{20,24},{8,4},{16,12},{24,20},{5,9},{13,17},{21,25},... | collective-permute-start | bytes 393224 | tf_op jit(solution)/shard_map/ppermute | solution.py:35
  61.6 8.2 %collective-permute-start.12 = (bf16[64,1024]{1,0:T(8,128)(2,1)S(1)}, bf16[64,1024]{1,0:T(8,128)(2,1)S(1)}, u32[]{:S(2)}, u32[]{:S(2)}) collective-permute-start(bf16[64,1024]{1,0:T(8,128)(2,1)S(1)} %get-tuple-element.32), channel_id=1, source_target_pairs={{0,4},{8,12},{16,20},{24,28},{4,0},{12,8},{20,16},{28,24},{1,5},{9... | collective-permute-start | bytes 393224 | tf_op jit(solution)/shard_map/ppermute | solution.py:34
  69.9 3.2 %collective-permute-start.15 = (bf16[64,512]{1,0:T(8,128)(2,1)S(1)}, bf16[64,512]{1,0:T(8,128)(2,1)S(1)}, u32[]{:S(2)}, u32[]{:S(2)}) collective-permute-start(bf16[64,512]{1,0:T(8,128)(2,1)S(1)} %get-tuple-element.43), channel_id=1, source_target_pairs={{1,2},{2,1},{5,6},{6,5},{9,10},{10,9},{13,14},{14,13},{17,18},{18,... | collective-permute-start | bytes 196616 | tf_op jit(solution)/shard_map/ppermute | solution.py:35
  70.5 3.5 %collective-permute-start.14 = (bf16[64,512]{1,0:T(8,128)(2,1)S(1)}, bf16[64,512]{1,0:T(8,128)(2,1)S(1)}, u32[]{:S(2)}, u32[]{:S(2)}) collective-permute-start(bf16[64,512]{1,0:T(8,128)(2,1)S(1)} %get-tuple-element.44), channel_id=1, source_target_pairs={{0,1},{2,3},{1,0},{3,2},{4,5},{6,7},{5,4},{7,6},{8,9},{10,11},{9,8... | collective-permute-start | bytes 196616 | tf_op jit(solution)/shard_map/ppermute | solution.py:34
  75.6 3.9 %collective-permute-start.16 = (f32[64,256]{1,0:T(8,128)S(1)}, f32[64,256]{1,0:T(8,128)S(1)}, u32[]{:S(2)}, u32[]{:S(2)}) collective-permute-start(f32[64,256]{1,0:T(8,128)S(1)} %get-tuple-element.17), channel_id=1, source_target_pairs={{0,1},{2,3},{4,5},{6,7},{8,9},{10,11},{12,13},{14,15},{16,17},{18,... | collective-permute-start | bytes 196616 | tf_op jit(solution)/shard_map/ppermute | solution.py:241
  79.4 2.0 %collective-permute-start.19 = (f32[64,256]{1,0:T(8,128)S(1)}, f32[64,256]{1,0:T(8,128)S(1)}, u32[]{:S(2)}, u32[]{:S(2)}) collective-permute-start(f32[64,256]{1,0:T(8,128)S(1)} %add.62), channel_id=1, source_target_pairs={{1,7},{3,5},{5,3},{7,1},{9,15},{11,13},{13,11},{15,9},{17,23},{19,... | collective-permute-start | bytes 196616 | tf_op jit(solution)/shard_map/ppermute | solution.py:241
  80.1 1.4 %collective-permute-start.18 = (f32[64,256]{1,0:T(8,128)S(1)}, f32[64,256]{1,0:T(8,128)S(1)}, u32[]{:S(2)}, u32[]{:S(2)}) collective-permute-start(f32[64,256]{1,0:T(8,128)S(1)} %add.62), channel_id=1, source_target_pairs={{1,5},{3,7},{5,1},{7,3},{9,13},{11,15},{13,9},{15,11},{17,21},{19,... | collective-permute-start | bytes 196616 | tf_op jit(solution)/shard_map/ppermute | solution.py:241
  80.8 0.7 collective-permute-start.17
  81.5 2.0 %collective-permute-start.22 = (f32[64,256]{1,0:T(8,128)S(1)}, f32[64,256]{1,0:T(8,128)S(1)}, u32[]{:S(2)}, u32[]{:S(2)}) collective-permute-start(f32[64,256]{1,0:T(8,128)S(1)} %add_add_fusion.3), channel_id=1, source_target_pairs={{1,25},{3,27},{5,29},{7,31},{9,17},{11,19},{13,21},{15,23},{17,9},... | collective-permute-start | bytes 196616 | tf_op jit(solution)/shard_map/ppermute | solution.py:241
  82.2 1.4 %collective-permute-start.21 = (f32[64,256]{1,0:T(8,128)S(1)}, f32[64,256]{1,0:T(8,128)S(1)}, u32[]{:S(2)}, u32[]{:S(2)}) collective-permute-start(f32[64,256]{1,0:T(8,128)S(1)} %add_add_fusion.3), channel_id=1, source_target_pairs={{1,17},{3,19},{5,21},{7,23},{9,25},{11,27},{13,29},{15,31},{17,1},... | collective-permute-start | bytes 196616 | tf_op jit(solution)/shard_map/ppermute | solution.py:241
  82.9 0.7 collective-permute-start.20
  83.6 21.3 %collective-permute-start.23 = (f32[64,256]{1,0:T(8,128)S(1)}, f32[64,256]{1,0:T(8,128)S(1)}, u32[]{:S(2)}, u32[]{:S(2)}) collective-permute-start(f32[64,256]{1,0:T(8,128)S(1)} %add_add_fusion.2), channel_id=1, source_target_pairs={{1,0},{3,2},{5,4},{7,6},{9,8},{11,10},{13,12},{15,14},{17,16},{19,... | collective-permute-start | bytes 196616 | tf_op jit(solution)/shard_map/ppermute | solution.py:241

commit v7 on v6

--- a/solution.py
+++ b/solution.py
@@ -1,4 +1,5 @@
 import functools
+import math
 
 import jax
 import jax.numpy as jnp
@@ -28,11 +29,15 @@
 
     def exchange(axis, upward, downward):
         count = lax.axis_size(axis)
-        odd = lax.axis_index(axis) % 2 == 1
-        pairs = [[(i, i + 1) for i in range(first, count - 1, 2)] for first in (0, 1)]
-        swaps = [pair + [(b, a) for a, b in pair] for pair in pairs]
-        inner = lax.ppermute(jnp.where(odd, downward, upward), axis, swaps[0])
-        outer = lax.ppermute(jnp.where(odd, upward, downward), axis, swaps[1])
+        me = lax.axis_index(axis)
+        odd = me % 2 == 1
+        inner = swapped(jnp.where(odd, downward, upward), (axis,), lambda i: i ^ 1)
+        outer = swapped(
+            jnp.where(odd, upward, downward),
+            (axis,),
+            lambda i: i if i in (0, count - 1) else (i - 1 ^ 1) + 1,
+        )
+        outer = jnp.where((me == 0) | (me == count - 1), 0, outer)
         return jnp.where(odd, inner, outer), jnp.where(odd, outer, inner)
 
     xlo, xhi = exchange("slab", block[:, (span_x - 1) * plane :], block[:, :plane])
@@ -237,24 +242,26 @@
     block[...] = dot(inverse.astype(jnp.bfloat16), w.astype(jnp.bfloat16)).astype(jnp.bfloat16)
 
 
-def moved(part, pairs):
-    return lax.ppermute(part, ("slab", "col"), pairs)
+def swapped(part, axis, partner):
+    count = math.prod(lax.axis_size(name) for name in axis)
+    return lax.ppermute(part, axis, [(i, partner(i)) for i in range(count)])
 
 
 def whole_sum(part):
+    axes = ("slab", "col")
     count = lax.axis_size("slab") * lax.axis_size("col")
-    second = range(1, count, 2)
-    part = part + moved(part, [(i - 1, i) for i in second])
+    part = part + swapped(part, axes, lambda i: i ^ 1)
     bit = 2
     while bit < count:
         masks = [mask for mask in (bit, 2 * bit, 3 * bit) if mask < count]
-        given = [moved(part, [(i, i ^ mask) for i in second]) for mask in masks]
+        given = [swapped(part, axes, lambda i: i ^ mask if i % 2 else i) for mask in masks]
         part = part + given[0]
         if len(given) == 3:
             part = part + (given[1] + given[2])
         bit *= 4
-    back = moved(part, [(i, i - 1) for i in second])
-    return jnp.where(lax.axis_index("col") % 2 == 1, part, back)
+    return jnp.where(
+        lax.axis_index("col") % 2 == 1, part, swapped(part, axes, lambda i: i ^ 1)
+    )
 
 
 def call(kernel, name, outs, *args):

time: 113 us -> 109 us (0.965)
  waiting for transfers between devices: 57.7 us -> 15.6 us
  starting transfers between devices: 32.7 us -> 69.7 us
    ppermute x24, waiting for transfers between devices: 57.7 us -> 15.6 us  [swapped(): return lax.ppermute(part, axis, [(i, partner(i)) for i in range(count)])]
    ppermute x24, starting transfers between devices: 32.7 us -> 69.7 us  [swapped(): return lax.ppermute(part, axis, [(i, partner(i)) for i in range(count)])]
where the time goes in v7:
time: 109 us; the launch traced here: 108 us
  starting transfers between devices  69.7 us (64%)
  Pallas kernels  18.4 us (17%)
  waiting for transfers between devices  15.6 us (14%)
  local copies, waits for them, and re-layouts  2.88 us (3%)
    ppermute x24, starting transfers between devices, swapped(): return lax.ppermute(part, axis, [(i, partner(i)) for i in range(count)])  69.7 us
    pallas_call x4, Pallas kernels, call(): pl.pallas_call(kernel, out_shape=[jax.ShapeDtypeStruct(shape, dtype) for...  17.6 us
    ppermute x24, waiting for transfers between devices, swapped(): return lax.ppermute(part, axis, [(i, partner(i)) for i in range(count)])  15.6 us
  transfers between devices with their start and end apart: 24, of which 7 were waited for; matrix products, arithmetic and copies ran while one was open for 0% of the time, Pallas kernels for 1%

profile of v7, /device:TPU:0, one launch (start us, length us, event | category | flops | bytes accessed | tf_op | source)
XLA Modules:
  0.0 108.0 jit_solution(10293440448262552801)
XLA Ops:
  0.6 0.0 slice-start
  0.7 0.9 slice-done
  1.6 0.1 slice.67
  1.7 0.0 copy-start.2
  1.8 0.8 collective-permute-start.1
  2.6 5.8 %collective-permute-start = (bf16[64,1024]{1,0:T(8,128)(2,1)S(1)}, bf16[64,1024]{1,0:T(8,128)(2,1)S(1)}, u32[]{:S(2)}, u32[]{:S(2)}) collective-permute-start(bf16[64,1024]{1,0:T(8,128)(2,1)S(1)} %get-tuple-element.40), channel_id=1, source_target_pairs={{0,4},{4,0},{8,12},{12,8},{16,20},{20,16},{24,28},{28,24},{1,5},{5... | collective-permute-start | bytes 393224 | tf_op jit(solution)/shard_map/ppermute | solution.py:247
  8.4 0.0 collective-permute-done.1
  8.4 4.8 %collective-permute-done = bf16[64,1024]{1,0:T(8,128)(2,1)S(1)} collective-permute-done((bf16[64,1024]{1,0:T(8,128)(2,1)S(1)}, bf16[64,1024]{1,0:T(8,128)(2,1)S(1)}, u32[]{:S(2)}, u32[]{:S(2)}) %collective-permute-start) | collective-permute-done | bytes 131104 | tf_op jit(solution)/shard_map/ppermute | solution.py:247
  13.3 0.7 collective-permute-start.3
  13.9 2.9 %collective-permute-start.2 = (bf16[64,512]{1,0:T(8,128)(2,1)S(1)}, bf16[64,512]{1,0:T(8,128)(2,1)S(1)}, u32[]{:S(2)}, u32[]{:S(2)}) collective-permute-start(bf16[64,512]{1,0:T(8,128)(2,1)S(1)} %get-tuple-element.52), channel_id=1, source_target_pairs={{0,1},{1,0},{2,3},{3,2},{4,5},{5,4},{6,7},{7,6},{8,9},{9,8},{10,11... | collective-permute-start | bytes 196616 | tf_op jit(solution)/shard_map/ppermute | solution.py:247
  16.9 0.0 copy-done.2
  16.9 0.0 copy-start
  16.9 0.3 reshape.17.stack
  17.2 0.0 copy-start.1
  17.3 0.3 copy-done
  17.6 0.3 copy-done.1
  17.9 0.8 coefficients.1.coef
  18.7 0.0 collective-permute-done.3
  18.7 0.0 collective-permute-done.2
  18.7 2.0 %first_image.1 = (bf16[64,2048]{1,0:T(8,128)(2,1)S(1)}, f32[64,640]{1,0:T(8,128)S(1)}) custom-call(f32[27,16,128]{2,1,0:T(8,128)S(1)} %coefficients.1.coef, bf16[192,2048]{1,0:T(8,128)(2,1)S(1)} %reshape.17.stack, bf16[64,1024]{1,0:T(8,128)(2,1)S(1)} %get-tuple-element.38.xlo, bf16[64,1024]{1,0:T(8,128)(2,1)S(1)} %get-tuple-element.37.xhi, ...), custom_call_target="tpu_custom_call" | custom-call | tf_op jit(solution)/shard_map/first_image/pallas_call | solution.py:268
  20.8 0.2 collective-permute-start.4
  21.0 1.2 %collective-permute-done.4 = f32[64,640]{1,0:T(8,128)S(1)} collective-permute-done((f32[64,640]{1,0:T(8,128)S(1)}, f32[64,640]{1,0:T(8,128)S(1)}, u32[]{:S(2)}, u32[]{:S(2)}) %collective-permute-start.4) | collective-permute-done | bytes 163872 | tf_op jit(solution)/shard_map/ppermute | solution.py:247
  22.3 0.7 collective-permute-start.7
  22.9 0.7 collective-permute-start.6
  23.6 0.7 collective-permute-start.5
  24.3 0.0 collective-permute-done.7
  24.3 0.0 collective-permute-done.6
  24.3 0.0 collective-permute-done.5
  24.4 0.7 collective-permute-start.10
  25.0 0.7 collective-permute-start.9
  25.7 0.7 collective-permute-start.8
  26.4 0.0 collective-permute-done.10
  26.4 0.0 collective-permute-done.9
  26.4 0.0 collective-permute-done.8
  26.5 24.2 %collective-permute-start.11 = (f32[64,640]{1,0:T(8,128)S(1)}, f32[64,640]{1,0:T(8,128)S(1)}, u32[]{:S(2)}, u32[]{:S(2)}) collective-permute-start(f32[64,640]{1,0:T(8,128)S(1)} %add_add_fusion), channel_id=1, source_target_pairs={{0,1},{1,0},{2,3},{3,2},{4,5},{5,4},{6,7},{7,6},{8,9},{9,8},{10,11... | collective-permute-start | bytes 491528 | tf_op jit(solution)/shard_map/ppermute | solution.py:247
  50.7 1.0 collective-permute-done.11
  51.7 7.0 %first_solve.1 = (bf16[64,2048]{1,0:T(8,128)(2,1)S(1)}, f32[64,192]{1,0:T(8,128)S(1)}, f32[64,64]{1,0:T(8,128)S(1)}, f32[192,192]{1,0:T(8,128)S(1)}) custom-call(f32[64,640]{1,0:T(8,128)S(1)} %broadcast_select_fusion.10.cross, bf16[192,2048]{1,0:T(8,128)(2,1)S(1)} %reshape.17.stack, bf16[64,2048]{1,0:T(8,128)(2,1)S(1)} %get-tuple-element.15.image), custom_call_target="tpu_custom_call" | custom-call | tf_op jit(solution)/shard_map/first_solve/pallas_call | solution.py:268
  58.7 0.7 collective-permute-start.13
  59.4 2.6 %collective-permute-start.12 = (bf16[64,1024]{1,0:T(8,128)(2,1)S(1)}, bf16[64,1024]{1,0:T(8,128)(2,1)S(1)}, u32[]{:S(2)}, u32[]{:S(2)}) collective-permute-start(bf16[64,1024]{1,0:T(8,128)(2,1)S(1)} %get-tuple-element.32), channel_id=1, source_target_pairs={{0,4},{4,0},{8,12},{12,8},{16,20},{20,16},{24,28},{28,24},{1,5},{5... | collective-permute-start | bytes 393224 | tf_op jit(solution)/shard_map/ppermute | solution.py:247
  62.1 0.0 collective-permute-done.13
  62.1 5.8 %collective-permute-done.12 = bf16[64,1024]{1,0:T(8,128)(2,1)S(1)} collective-permute-done((bf16[64,1024]{1,0:T(8,128)(2,1)S(1)}, bf16[64,1024]{1,0:T(8,128)(2,1)S(1)}, u32[]{:S(2)}, u32[]{:S(2)}) %collective-permute-start.12) | collective-permute-done | bytes 131104 | tf_op jit(solution)/shard_map/ppermute | solution.py:247
  67.9 0.7 collective-permute-start.15
  68.6 1.8 %collective-permute-start.14 = (bf16[64,512]{1,0:T(8,128)(2,1)S(1)}, bf16[64,512]{1,0:T(8,128)(2,1)S(1)}, u32[]{:S(2)}, u32[]{:S(2)}) collective-permute-start(bf16[64,512]{1,0:T(8,128)(2,1)S(1)} %get-tuple-element.44), channel_id=1, source_target_pairs={{0,1},{1,0},{2,3},{3,2},{4,5},{5,4},{6,7},{7,6},{8,9},{9,8},{10,11... | collective-permute-start | bytes 196616 | tf_op jit(solution)/shard_map/ppermute | solution.py:247
  70.4 0.0 collective-permute-done.15
  70.4 0.9 collective-permute-done.14
  71.3 1.5 %second_image.1 = (bf16[64,2048]{1,0:T(8,128)(2,1)S(1)}, f32[64,256]{1,0:T(8,128)S(1)}) custom-call(f32[27,16,128]{2,1,0:T(8,128)S(1)} %coefficients.1.coef, bf16[192,2048]{1,0:T(8,128)(2,1)S(1)} %reshape.17.stack, bf16[64,2048]{1,0:T(8,128)(2,1)S(1)} %get-tuple-element.16.block.last, bf16[64,1024]{1,0:T(8,128)(2,1)S(1)} %get-tuple-element.30.xlo, ...), custom_call_target="tpu_custom_call" | custom-call | tf_op jit(solution)/shard_map/second_image/pallas_call | solution.py:268
  72.9 1.9 %collective-permute-start.16 = (f32[64,256]{1,0:T(8,128)S(1)}, f32[64,256]{1,0:T(8,128)S(1)}, u32[]{:S(2)}, u32[]{:S(2)}) collective-permute-start(f32[64,256]{1,0:T(8,128)S(1)} %get-tuple-element.17), channel_id=1, source_target_pairs={{0,1},{1,0},{2,3},{3,2},{4,5},{5,4},{6,7},{7,6},{8,9},{9,8},{10,11... | collective-permute-start | bytes 196616 | tf_op jit(solution)/shard_map/ppermute | solution.py:247
  74.8 0.9 collective-permute-done.16
  75.7 0.7 collective-permute-start.19
  76.3 0.7 collective-permute-start.18
  77.0 0.7 collective-permute-start.17
  77.7 0.0 collective-permute-done.19
  77.7 0.0 collective-permute-done.18
  77.7 0.0 collective-permute-done.17
  77.7 0.7 collective-permute-start.22
  78.4 0.7 collective-permute-start.21
  79.1 0.7 collective-permute-start.20
  79.8 0.0 collective-permute-done.22
  79.8 0.0 collective-permute-done.21
  79.8 0.0 collective-permute-done.20
  79.8 19.4 %collective-permute-start.23 = (f32[64,256]{1,0:T(8,128)S(1)}, f32[64,256]{1,0:T(8,128)S(1)}, u32[]{:S(2)}, u32[]{:S(2)}) collective-permute-start(f32[64,256]{1,0:T(8,128)S(1)} %add_add_fusion.2), channel_id=1, source_target_pairs={{0,1},{1,0},{2,3},{3,2},{4,5},{5,4},{6,7},{7,6},{8,9},{9,8},{10,11... | collective-permute-start | bytes 196616 | tf_op jit(solution)/shard_map/ppermute | solution.py:247
  99.2 0.9 collective-permute-done.23
  100.1 7.1 %second_solve.1 = (bf16[64,2048]{1,0:T(8,128)(2,1)S(1)}, f32[2,64,192]{2,1,0:T(8,128)}, f32[2,64,64]{2,1,0:T(8,128)}) custom-call(f32[64,256]{1,0:T(8,128)S(1)} %broadcast_select_fusion.21.cross, f32[192,192]{1,0:T(8,128)S(1)} %get-tuple-element.18.own, bf16[192,2048]{1,0:T(8,128)(2,1)S(1)} %reshape.17.stack, ...), custom_call_target="tpu_custom_call" | custom-call | tf_op jit(solution)/shard_map/second_solve/pallas_call | solution.py:268
  107.2 0.7 copy.6
  (21 shorter events, 0.4 us)
Async XLA Ops:
  0.6 1.0 slice-start
  1.7 15.2 %copy-start.2 = (bf16[3,64,2,8,128]{4,3,2,1,0:T(8,128)(2,1)S(1)}, bf16[3,64,2,8,128]{4,3,2,1,0:T(8,128)(2,1)}, u32[]{:S(2)}) copy-start(bf16[3,64,2,8,128]{4,3,2,1,0:T(8,128)(2,1)} %param.3) | copy-start | bytes 2359300
  1.8 6.6 %collective-permute-start.1 = (bf16[64,1024]{1,0:T(8,128)(2,1)S(1)}, bf16[64,1024]{1,0:T(8,128)(2,1)S(1)}, u32[]{:S(2)}, u32[]{:S(2)}) collective-permute-start(bf16[64,1024]{1,0:T(8,128)(2,1)S(1)} %get-tuple-element.39), channel_id=1, source_target_pairs={{0,0},{4,8},{8,4},{12,16},{16,12},{20,24},{24,20},{28,28},{1,1},{5... | collective-permute-start | bytes 393224 | tf_op jit(solution)/shard_map/ppermute | solution.py:247
  2.6 10.6 %collective-permute-start = (bf16[64,1024]{1,0:T(8,128)(2,1)S(1)}, bf16[64,1024]{1,0:T(8,128)(2,1)S(1)}, u32[]{:S(2)}, u32[]{:S(2)}) collective-permute-start(bf16[64,1024]{1,0:T(8,128)(2,1)S(1)} %get-tuple-element.40), channel_id=1, source_target_pairs={{0,4},{4,0},{8,12},{12,8},{16,20},{20,16},{24,28},{28,24},{1,5},{5... | collective-permute-start | bytes 393224 | tf_op jit(solution)/shard_map/ppermute | solution.py:247
  13.3 5.4 %collective-permute-start.3 = (bf16[64,512]{1,0:T(8,128)(2,1)S(1)}, bf16[64,512]{1,0:T(8,128)(2,1)S(1)}, u32[]{:S(2)}, u32[]{:S(2)}) collective-permute-start(bf16[64,512]{1,0:T(8,128)(2,1)S(1)} %get-tuple-element.51), channel_id=1, source_target_pairs={{0,0},{1,2},{2,1},{3,3},{4,4},{5,6},{6,5},{7,7},{8,8},{9,10},{10,9... | collective-permute-start | bytes 196616 | tf_op jit(solution)/shard_map/ppermute | solution.py:247
  13.9 4.8 %collective-permute-start.2 = (bf16[64,512]{1,0:T(8,128)(2,1)S(1)}, bf16[64,512]{1,0:T(8,128)(2,1)S(1)}, u32[]{:S(2)}, u32[]{:S(2)}) collective-permute-start(bf16[64,512]{1,0:T(8,128)(2,1)S(1)} %get-tuple-element.52), channel_id=1, source_target_pairs={{0,1},{1,0},{2,3},{3,2},{4,5},{5,4},{6,7},{7,6},{8,9},{9,8},{10,11... | collective-permute-start | bytes 196616 | tf_op jit(solution)/shard_map/ppermute | solution.py:247
  16.9 0.7 copy-start
  17.2 0.7 copy-start.1
  20.8 1.5 %collective-permute-start.4 = (f32[64,640]{1,0:T(8,128)S(1)}, f32[64,640]{1,0:T(8,128)S(1)}, u32[]{:S(2)}, u32[]{:S(2)}) collective-permute-start(f32[64,640]{1,0:T(8,128)S(1)} %get-tuple-element.14), channel_id=1, source_target_pairs={{0,1},{1,0},{2,3},{3,2},{4,5},{5,4},{6,7},{7,6},{8,9},{9,8},{10,11... | collective-permute-start | bytes 491528 | tf_op jit(solution)/shard_map/ppermute | solution.py:247
  22.3 2.0 %collective-permute-start.7 = (f32[64,640]{1,0:T(8,128)S(1)}, f32[64,640]{1,0:T(8,128)S(1)}, u32[]{:S(2)}, u32[]{:S(2)}) collective-permute-start(f32[64,640]{1,0:T(8,128)S(1)} %add.55), channel_id=1, source_target_pairs={{0,0},{1,7},{2,2},{3,5},{4,4},{5,3},{6,6},{7,1},{8,8},{9,15},{10,1... | collective-permute-start | bytes 491528 | tf_op jit(solution)/shard_map/ppermute | solution.py:247
  22.9 1.4 %collective-permute-start.6 = (f32[64,640]{1,0:T(8,128)S(1)}, f32[64,640]{1,0:T(8,128)S(1)}, u32[]{:S(2)}, u32[]{:S(2)}) collective-permute-start(f32[64,640]{1,0:T(8,128)S(1)} %add.55), channel_id=1, source_target_pairs={{0,0},{1,5},{2,2},{3,7},{4,4},{5,1},{6,6},{7,3},{8,8},{9,13},{10,1... | collective-permute-start | bytes 491528 | tf_op jit(solution)/shard_map/ppermute | solution.py:247
  23.6 0.7 collective-permute-start.5
  24.4 2.0 %collective-permute-start.10 = (f32[64,640]{1,0:T(8,128)S(1)}, f32[64,640]{1,0:T(8,128)S(1)}, u32[]{:S(2)}, u32[]{:S(2)}) collective-permute-start(f32[64,640]{1,0:T(8,128)S(1)} %add_add_fusion.1), channel_id=1, source_target_pairs={{0,0},{1,25},{2,2},{3,27},{4,4},{5,29},{6,6},{7,31},{8,8},{9,17},{... | collective-permute-start | bytes 491528 | tf_op jit(solution)/shard_map/ppermute | solution.py:247
  25.0 1.4 %collective-permute-start.9 = (f32[64,640]{1,0:T(8,128)S(1)}, f32[64,640]{1,0:T(8,128)S(1)}, u32[]{:S(2)}, u32[]{:S(2)}) collective-permute-start(f32[64,640]{1,0:T(8,128)S(1)} %add_add_fusion.1), channel_id=1, source_target_pairs={{0,0},{1,17},{2,2},{3,19},{4,4},{5,21},{6,6},{7,23},{8,8},{9,25},{... | collective-permute-start | bytes 491528 | tf_op jit(solution)/shard_map/ppermute | solution.py:247
  25.7 0.7 collective-permute-start.8
  26.5 25.2 %collective-permute-start.11 = (f32[64,640]{1,0:T(8,128)S(1)}, f32[64,640]{1,0:T(8,128)S(1)}, u32[]{:S(2)}, u32[]{:S(2)}) collective-permute-start(f32[64,640]{1,0:T(8,128)S(1)} %add_add_fusion), channel_id=1, source_target_pairs={{0,1},{1,0},{2,3},{3,2},{4,5},{5,4},{6,7},{7,6},{8,9},{9,8},{10,11... | collective-permute-start | bytes 491528 | tf_op jit(solution)/shard_map/ppermute | solution.py:247
  58.7 3.3 %collective-permute-start.13 = (bf16[64,1024]{1,0:T(8,128)(2,1)S(1)}, bf16[64,1024]{1,0:T(8,128)(2,1)S(1)}, u32[]{:S(2)}, u32[]{:S(2)}) collective-permute-start(bf16[64,1024]{1,0:T(8,128)(2,1)S(1)} %get-tuple-element.31), channel_id=1, source_target_pairs={{0,0},{4,8},{8,4},{12,16},{16,12},{20,24},{24,20},{28,28},{1,1},{5... | collective-permute-start | bytes 393224 | tf_op jit(solution)/shard_map/ppermute | solution.py:247
  59.4 8.4 %collective-permute-start.12 = (bf16[64,1024]{1,0:T(8,128)(2,1)S(1)}, bf16[64,1024]{1,0:T(8,128)(2,1)S(1)}, u32[]{:S(2)}, u32[]{:S(2)}) collective-permute-start(bf16[64,1024]{1,0:T(8,128)(2,1)S(1)} %get-tuple-element.32), channel_id=1, source_target_pairs={{0,4},{4,0},{8,12},{12,8},{16,20},{20,16},{24,28},{28,24},{1,5},{5... | collective-permute-start | bytes 393224 | tf_op jit(solution)/shard_map/ppermute | solution.py:247
  67.9 2.5 %collective-permute-start.15 = (bf16[64,512]{1,0:T(8,128)(2,1)S(1)}, bf16[64,512]{1,0:T(8,128)(2,1)S(1)}, u32[]{:S(2)}, u32[]{:S(2)}) collective-permute-start(bf16[64,512]{1,0:T(8,128)(2,1)S(1)} %get-tuple-element.43), channel_id=1, source_target_pairs={{0,0},{1,2},{2,1},{3,3},{4,4},{5,6},{6,5},{7,7},{8,8},{9,10},{10,9... | collective-permute-start | bytes 196616 | tf_op jit(solution)/shard_map/ppermute | solution.py:247
  68.6 2.7 %collective-permute-start.14 = (bf16[64,512]{1,0:T(8,128)(2,1)S(1)}, bf16[64,512]{1,0:T(8,128)(2,1)S(1)}, u32[]{:S(2)}, u32[]{:S(2)}) collective-permute-start(bf16[64,512]{1,0:T(8,128)(2,1)S(1)} %get-tuple-element.44), channel_id=1, source_target_pairs={{0,1},{1,0},{2,3},{3,2},{4,5},{5,4},{6,7},{7,6},{8,9},{9,8},{10,11... | collective-permute-start | bytes 196616 | tf_op jit(solution)/shard_map/ppermute | solution.py:247
  72.9 2.8 %collective-permute-start.16 = (f32[64,256]{1,0:T(8,128)S(1)}, f32[64,256]{1,0:T(8,128)S(1)}, u32[]{:S(2)}, u32[]{:S(2)}) collective-permute-start(f32[64,256]{1,0:T(8,128)S(1)} %get-tuple-element.17), channel_id=1, source_target_pairs={{0,1},{1,0},{2,3},{3,2},{4,5},{5,4},{6,7},{7,6},{8,9},{9,8},{10,11... | collective-permute-start | bytes 196616 | tf_op jit(solution)/shard_map/ppermute | solution.py:247
  75.7 2.0 %collective-permute-start.19 = (f32[64,256]{1,0:T(8,128)S(1)}, f32[64,256]{1,0:T(8,128)S(1)}, u32[]{:S(2)}, u32[]{:S(2)}) collective-permute-start(f32[64,256]{1,0:T(8,128)S(1)} %add.62), channel_id=1, source_target_pairs={{0,0},{1,7},{2,2},{3,5},{4,4},{5,3},{6,6},{7,1},{8,8},{9,15},{10,1... | collective-permute-start | bytes 196616 | tf_op jit(solution)/shard_map/ppermute | solution.py:247
  76.3 1.4 %collective-permute-start.18 = (f32[64,256]{1,0:T(8,128)S(1)}, f32[64,256]{1,0:T(8,128)S(1)}, u32[]{:S(2)}, u32[]{:S(2)}) collective-permute-start(f32[64,256]{1,0:T(8,128)S(1)} %add.62), channel_id=1, source_target_pairs={{0,0},{1,5},{2,2},{3,7},{4,4},{5,1},{6,6},{7,3},{8,8},{9,13},{10,1... | collective-permute-start | bytes 196616 | tf_op jit(solution)/shard_map/ppermute | solution.py:247
  77.0 0.7 collective-permute-start.17
  77.7 2.0 %collective-permute-start.22 = (f32[64,256]{1,0:T(8,128)S(1)}, f32[64,256]{1,0:T(8,128)S(1)}, u32[]{:S(2)}, u32[]{:S(2)}) collective-permute-start(f32[64,256]{1,0:T(8,128)S(1)} %add_add_fusion.3), channel_id=1, source_target_pairs={{0,0},{1,25},{2,2},{3,27},{4,4},{5,29},{6,6},{7,31},{8,8},{9,17},{... | collective-permute-start | bytes 196616 | tf_op jit(solution)/shard_map/ppermute | solution.py:247
  78.4 1.4 %collective-permute-start.21 = (f32[64,256]{1,0:T(8,128)S(1)}, f32[64,256]{1,0:T(8,128)S(1)}, u32[]{:S(2)}, u32[]{:S(2)}) collective-permute-start(f32[64,256]{1,0:T(8,128)S(1)} %add_add_fusion.3), channel_id=1, source_target_pairs={{0,0},{1,17},{2,2},{3,19},{4,4},{5,21},{6,6},{7,23},{8,8},{9,25},{... | collective-permute-start | bytes 196616 | tf_op jit(solution)/shard_map/ppermute | solution.py:247
  79.1 0.7 collective-permute-start.20
  79.8 20.3 %collective-permute-start.23 = (f32[64,256]{1,0:T(8,128)S(1)}, f32[64,256]{1,0:T(8,128)S(1)}, u32[]{:S(2)}, u32[]{:S(2)}) collective-permute-start(f32[64,256]{1,0:T(8,128)S(1)} %add_add_fusion.2), channel_id=1, source_target_pairs={{0,1},{1,0},{2,3},{3,2},{4,5},{5,4},{6,7},{7,6},{8,9},{9,8},{10,11... | collective-permute-start | bytes 196616 | tf_op jit(solution)/shard_map/ppermute | solution.py:247

commit v8 on v5

--- a/solution.py
+++ b/solution.py
@@ -7,20 +7,13 @@
 from jax.experimental.pallas import tpu as pltpu
 from jax.sharding import PartitionSpec as P
 
-HIGHEST = lax.Precision.HIGHEST
 NN = (((1,), (0,)), ((), ()))
 NT = (((1,), (1,)), ((), ()))
 ROWS = 16
 
 
-def dot(left, right, dims=NN, precision=None):
-    return lax.dot_general(
-        left, right, dims, precision=precision, preferred_element_type=jnp.float32
-    )
-
-
-def exact(left, right, dims=NN):
-    return dot(left, right, dims, HIGHEST)
+def dot(left, right, dims=NN):
+    return lax.dot_general(left, right, dims, preferred_element_type=jnp.float32)
 
 
 def neighbours(block, span_x, span_y, depth):
@@ -80,6 +73,7 @@
             pl.BlockSpec(memory_space=pltpu.VMEM),
         ],
         out_specs=pl.BlockSpec(memory_space=pltpu.VMEM),
+        compiler_params=pltpu.CompilerParams(vmem_limit_bytes=4 * 1024 * 1024),
         name="coefficients",
     )(table, cell_map.reshape(lines, depth))
 
@@ -148,43 +142,64 @@
     cross[:, fields:] = dot(w, w, NT)
 
 
+def split(values):
+    high = values.astype(jnp.bfloat16)
+    return high, (values - high.astype(jnp.float32)).astype(jnp.bfloat16)
+
+
+def dots(lefts, rights, dims=NN):
+    return sum(dot(left, right, dims) for left in lefts for right in rights)
+
+
 def factor(square):
     size = square.shape[0]
-    lane = lax.broadcasted_iota(jnp.int32, (8, 2 * size), 1)
+    f32 = jnp.float32
+    unit = lax.broadcasted_iota(jnp.int32, (size, size), 0) == lax.broadcasted_iota(
+        jnp.int32, (size, size), 1
+    )
+    diagonal = jnp.where(unit, square, 0.0)
+    down = lax.rsqrt(jnp.sum(diagonal, axis=1, keepdims=True))
+    across_squared = jnp.sum(diagonal, axis=0, keepdims=True)
+    across = lax.rsqrt(across_squared)
+    whole = jnp.concatenate([square * down * across, unit.astype(f32)], axis=1)
     sub = lax.broadcasted_iota(jnp.int32, (8, 2 * size), 0)
-    blocks = []
-    for b in range(size // 8):
-        unit = (lax.broadcasted_iota(jnp.int32, (8, size), 1)
-                == lax.broadcasted_iota(jnp.int32, (8, size), 0) + 8 * b).astype(jnp.float32)
-        blocks.append(jnp.concatenate([square[8 * b : 8 * b + 8], unit], axis=1))
-    for k in range(size):
+    blocks = [whole[8 * b : 8 * b + 8] for b in range(size // 8)]
+    done = [jnp.zeros((8, 2 * size), f32) for _ in blocks]
+    for k in range(0, size, 2):
         b, r = divmod(k, 8)
-        row = blocks[b][r : r + 1, :]
-        row = row * (1.0 / row[:, k : k + 1])
+        here = blocks[b]
+        row, next_row = here[r : r + 1, :], here[r + 1 : r + 2, :]
+        first, mixed = row[:, k : k + 1], next_row[:, k : k + 1]
+        last = next_row[:, k + 1 : k + 2]
+        inverse = 1.0 / (first * last - mixed * mixed)
+        left = (last * row - mixed * next_row) * inverse
+        right = (first * next_row - mixed * row) * inverse
         for later in range(b, size // 8):
-            column = blocks[later][:, k : k + 1]
+            one, two = blocks[later][:, k : k + 1], blocks[later][:, k + 1 : k + 2]
+            change = one * left + two * right
             if later == b:
-                column = jnp.where(sub[:, :1] > r, column, 0.0)
-            blocks[later] = blocks[later] - column * row
-    done = []
-    for b, rows in enumerate(blocks):
-        diagonal = jnp.sum(jnp.where(lane == sub + 8 * b, rows, 0.0), axis=1, keepdims=True)
-        done.append(rows * lax.rsqrt(diagonal))
-    whole = jnp.concatenate(done, axis=0)
-    return whole[:, :size], whole[:, size:]
+                change = jnp.where(sub > r + 1, change, 0.0)
+            blocks[later] = blocks[later] - change
+        ratio = mixed * (1.0 / first)
+        done[b] = jnp.where(sub == r, row * lax.rsqrt(first), done[b])
+        rest = (next_row - ratio * row) * lax.rsqrt(last - ratio * mixed)
+        done[b] = jnp.where(sub == r + 1, rest, done[b])
+    done = jnp.concatenate(done, axis=0)
+    return done[:, :size] * (across_squared * across), done[:, size:] * across
 
 
 def project(cross, own, scale):
-    fields = own.shape[0]
+    fields = own[0].shape[0]
     first = cross[:, :fields] * scale
-    square = cross[:, fields:] * scale
-    first_low = first.astype(jnp.bfloat16)
-    second = first - exact(first_low.astype(jnp.float32), own)
+    first_parts = split(first)
+    first_low = first_parts[0]
+    second = first - dots((first_low,), own)
     second_low = second.astype(jnp.bfloat16)
-    used = first_low.astype(jnp.float32) + second_low.astype(jnp.float32)
-    rest = second - exact(second_low.astype(jnp.float32), own)
-    square = square - exact(used, first, NT) - exact(rest, used, NT)
-    return first_low, second_low, first + second, rest, square
+    used = (first_low, second_low)
+    square = cross[:, fields:] * scale - dots(used, first_parts, NT)
+    rest = second - dots((second_low,), own)
+    square = square - dots(split(rest), used, NT)
+    return used, first + second, rest, square
 
 
 def unpacked(upper, columns, fields):
@@ -199,41 +214,55 @@
     return jnp.concatenate(whole, axis=0)
 
 
-def first_solve_kernel(scale, cross, stack, image, block, proj, low, own_next):
+def first_solve_kernel(scale, cross, stack, image, block, proj, low, rest, square, inverse):
     columns = image.shape[0]
     fields = stack.shape[0]
     gram = unpacked(cross[:, fields + columns :] * scale, columns, fields)
-    first_low, second_low, both, rest, square = project(
-        cross[:, : fields + columns], gram, scale
-    )
-    proj[...] = both
-    upper, inverse = factor(square)
+    used, proj[...], rest[...], square_here = project(
+        cross[:, : fields + columns], split(gram), scale
+    )
+    square[...] = square_here
+    w = image[...].astype(jnp.float32) - dots(used, (stack[...],))
+    block[...] = w.astype(jnp.bfloat16)
+    upper, inverse_here = factor(square_here)
     low[...] = upper.T
-    inverse = inverse.astype(jnp.bfloat16)
-    w = image[...].astype(jnp.float32) - dot(first_low, stack[...]) - dot(second_low, stack[...])
-    block[...] = dot(inverse, w.astype(jnp.bfloat16)).astype(jnp.bfloat16)
-    kept = stack.shape[0] - columns
-    wide = inverse.astype(jnp.float32)
-    mixed = exact(wide, rest[:, columns:])
-    own_next[:kept, :kept] = gram[columns:, columns:]
-    own_next[kept:, :kept] = mixed
-    own_next[:kept, kept:] = mixed.T
-    own_next[kept:, kept:] = exact(exact(wide, square), wide, NT)
-
-
-def second_solve_kernel(scale, cross, own, stack, last, image, proj_in, low_in, block, proj, low):
+    inverse_here = inverse_here.astype(jnp.bfloat16)
+    inverse[...] = inverse_here
+    block[...] = dot(inverse_here, block[...]).astype(jnp.bfloat16)
+
+
+def next_gram_kernel(scale, cross, rest, square, inverse, high, low):
+    columns = square.shape[0]
+    fields = rest.shape[1]
+    kept = fields - columns
+    gram = unpacked(cross[:, fields + columns :] * scale, columns, fields)
+    mixed = dots((inverse[...],), split(rest[:, columns:]))
+    corner = dots((inverse[...],), split(square[...]))
+    corner = dots(split(corner), (inverse[...],), NT)
+    for part, (old, side, end) in zip(
+        (high, low), zip(split(gram[columns:, columns:]), split(mixed), split(corner))
+    ):
+        part[:kept, :kept] = old
+        part[kept:, :kept] = side
+        part[:kept, kept:] = side.T
+        part[kept:, kept:] = end
+
+
+def second_solve_kernel(
+    scale, cross, own_high, own_low, stack, last, image, proj_in, low_in, block, proj, low
+):
     columns = image.shape[0]
     kept = stack.shape[0] - columns
-    first_low, second_low, both, _, square = project(cross[...], own[...], scale)
+    used, proj[1], _, square = project(cross[...], (own_high[...], own_low[...]), scale)
     proj[0] = proj_in[...]
-    proj[1] = both
+    low[0] = low_in[...]
+    w = image[...].astype(jnp.float32)
+    w = w - dots([part[:, :kept] for part in used], (stack[columns:],))
+    w = w - dots([part[:, kept:] for part in used], (last[...],))
+    block[...] = w.astype(jnp.bfloat16)
     upper, inverse = factor(square)
-    low[0] = low_in[...]
     low[1] = upper.T
-    w = image[...].astype(jnp.float32)
-    for part in (first_low, second_low):
-        w = w - dot(part[:, :kept], stack[columns:]) - dot(part[:, kept:], last[...])
-    block[...] = dot(inverse.astype(jnp.bfloat16), w.astype(jnp.bfloat16)).astype(jnp.bfloat16)
+    block[...] = dot(inverse.astype(jnp.bfloat16), block[...]).astype(jnp.bfloat16)
 
 
 def partner(part, mask):
@@ -243,18 +272,24 @@
 
 
 def whole_sum(part):
-    count = lax.axis_size("slab") * lax.axis_size("col")
+    cols = lax.axis_size("col")
+    count = lax.axis_size("slab") * cols
+    index = lax.axis_index("slab") * cols + lax.axis_index("col")
+    bit, upper = 1, 0
+    while bit < count:
+        upper = upper ^ (index // bit % 2)
+        bit *= 2
+    upper = upper == 1
     half = part.shape[0] // 2
-    upper = lax.axis_index("col") % 2 == 1
     low, high = part[:half], part[half:]
     part = jnp.where(upper, high, low) + partner(jnp.where(upper, low, high), 1)
     bit = 2
     while bit < count:
         if 2 * bit < count:
-            one, two, both = (partner(part, mask) for mask in (bit, 2 * bit, 3 * bit))
+            one, two, both = (partner(part, mask) for mask in (bit + 1, 2 * bit + 1, 3 * bit))
             part = (part + one) + (two + both)
         else:
-            part = part + partner(part, bit)
+            part = part + partner(part, bit + 1)
         bit *= 4
     other = partner(part, 1)
     return jnp.concatenate([jnp.where(upper, other, part), jnp.where(upper, part, other)], axis=0)
@@ -290,12 +325,19 @@
         [((columns, cells), bf16), ((columns, packed), f32)],
         coef, stack, *around,
     )
-    block, proj, low, own = call(
+    cross = whole_sum(cross)
+    block, proj, low, rest, square, inverse = call(
         functools.partial(first_solve_kernel, scale),
         "first_solve",
         [((columns, cells), bf16), ((columns, fields), f32), ((columns, columns), f32),
-         ((fields, fields), f32)],
-        whole_sum(cross), stack, image,
+         ((columns, fields), f32), ((columns, columns), f32), ((columns, columns), bf16)],
+        cross, stack, image,
+    )
+    own = call(
+        functools.partial(next_gram_kernel, scale),
+        "next_gram",
+        [((fields, fields), bf16)] * 2,
+        cross, rest, square, inverse,
     )
     around = neighbours(block, *spans)
     image, cross = call(
@@ -308,7 +350,7 @@
         functools.partial(second_solve_kernel, scale),
         "second_solve",
         [((columns, cells), bf16), ((2, columns, fields), f32), ((2, columns, columns), f32)],
-        whole_sum(cross), own, stack, block, image, proj, low,
+        whole_sum(cross), *own, stack, block, image, proj, low,
     )
     return block.reshape(columns, *spans), jnp.swapaxes(proj, 1, 2), low
 

time: 92 us -> 90.2 us (0.980)
  Pallas kernels: 19.2 us -> 17.7 us
    ppermute x16, starting transfers between devices: 19.8 us -> 18.6 us  [partner(): return lax.ppermute(part, axes, [(i, i ^ mask) for i in range(count)])]
    pallas_call x4 -> x5, Pallas kernels: 17.6 us -> 16.9 us  [call(): pl.pallas_call(kernel, out_shape=[jax.ShapeDtypeStruct(shape, dtype) for...]
  transfers between devices with their start and end apart: 24 -> 24, of which waited for: 16 -> 16; matrix products, arithmetic and copies ran while one was open for 0% -> 0% of each run, Pallas kernels for 2% -> 1%
where the time goes in v8:
time: 90.2 us; the launch traced here: 89.9 us
  starting transfers between devices  36.4 us (40%)
  waiting for transfers between devices  31.6 us (35%)
  Pallas kernels  17.7 us (20%)
  local copies, waits for them, and re-layouts  2.88 us (3%)
  between operations  0.98 us (1%)
    ppermute x16, waiting for transfers between devices, partner(): return lax.ppermute(part, axes, [(i, i ^ mask) for i in range(count)])  20.1 us
    ppermute x16, starting transfers between devices, partner(): return lax.ppermute(part, axes, [(i, i ^ mask) for i in range(count)])  18.6 us
    pallas_call x5, Pallas kernels, call(): pl.pallas_call(kernel, out_shape=[jax.ShapeDtypeStruct(shape, dtype) for...  16.9 us
    ppermute x4, starting transfers between devices, exchange(): inner = lax.ppermute(jnp.where(odd, downward, upward), axis, swaps[0])  15 us
    ppermute x4, waiting for transfers between devices, exchange(): inner = lax.ppermute(jnp.where(odd, downward, upward), axis, swaps[0])  11.5 us
    ppermute x4, starting transfers between devices, exchange(): outer = lax.ppermute(jnp.where(odd, upward, downward), axis, swaps[1])  2.8 us
  transfers between devices with their start and end apart: 24, of which 16 were waited for; matrix products, arithmetic and copies ran while one was open for 0% of the time, Pallas kernels for 1%

profile of v8, /device:TPU:0, one launch (start us, length us, event | category | flops | bytes accessed | tf_op | source)
XLA Modules:
  0.0 89.9 jit_solution(4631932258792376440)
XLA Ops:
  0.6 0.0 slice-start
  0.7 0.9 %slice-done = bf16[1,64,2,8,128]{4,3,2,1,0:T(8,128)(2,1)S(1)} async-done(((bf16[3,64,2,8,128]{4,3,2,1,0:T(8,128)(2,1)}), bf16[1,64,2,8,128]{4,3,2,1,0:T(8,128)(2,1)S(1)}, s32[]{:S(2)}) %slice-start) | async-done | bytes 262168 | tf_op jit(solution)/shard_map/slice | solution.py:320
  1.6 0.1 slice.79
  1.7 0.0 copy-start.2
  1.8 0.8 collective-permute-start.1
  2.6 5.8 %collective-permute-start = (bf16[64,1024]{1,0:T(8,128)(2,1)S(1)}, bf16[64,1024]{1,0:T(8,128)(2,1)S(1)}, u32[]{:S(2)}, u32[]{:S(2)}) collective-permute-start(bf16[64,1024]{1,0:T(8,128)(2,1)S(1)} %get-tuple-element.48), channel_id=1, source_target_pairs={{0,4},{8,12},{16,20},{24,28},{4,0},{12,8},{20,16},{28,24},{1,5},{9... | collective-permute-start | bytes 393224 | tf_op jit(solution)/shard_map/ppermute | solution.py:27
  8.4 0.0 collective-permute-done.1
  8.4 4.8 %collective-permute-done = bf16[64,1024]{1,0:T(8,128)(2,1)S(1)} collective-permute-done((bf16[64,1024]{1,0:T(8,128)(2,1)S(1)}, bf16[64,1024]{1,0:T(8,128)(2,1)S(1)}, u32[]{:S(2)}, u32[]{:S(2)}) %collective-permute-start) | collective-permute-done | bytes 131104 | tf_op jit(solution)/shard_map/ppermute | solution.py:27
  13.3 0.7 collective-permute-start.3
  13.9 2.9 %collective-permute-start.2 = (bf16[64,512]{1,0:T(8,128)(2,1)S(1)}, bf16[64,512]{1,0:T(8,128)(2,1)S(1)}, u32[]{:S(2)}, u32[]{:S(2)}) collective-permute-start(bf16[64,512]{1,0:T(8,128)(2,1)S(1)} %get-tuple-element.62), channel_id=1, source_target_pairs={{0,1},{2,3},{1,0},{3,2},{4,5},{6,7},{5,4},{7,6},{8,9},{10,11},{9,8... | collective-permute-start | bytes 196616 | tf_op jit(solution)/shard_map/ppermute | solution.py:27
  16.9 0.3 reshape.17.stack
  17.3 0.0 copy-start
  17.3 0.0 copy-start.1
  17.3 0.7 copy-done
  18.0 0.0 copy-done.1
  18.0 0.8 coefficients.1.coef
  18.7 0.0 collective-permute-done.3
  18.8 0.0 collective-permute-done.2
  18.8 2.0 %first_image.1 = (bf16[64,2048]{1,0:T(8,128)(2,1)S(1)}, f32[64,640]{1,0:T(8,128)S(1)}) custom-call(f32[27,16,128]{2,1,0:T(8,128)S(1)} %coefficients.1.coef, bf16[192,2048]{1,0:T(8,128)(2,1)S(1)} %reshape.17.stack, bf16[64,1024]{1,0:T(8,128)(2,1)S(1)} %get-tuple-element.46.xlo, bf16[64,1024]{1,0:T(8,128)(2,1)S(1)} %get-tuple-element.45.xhi, ...), custom_call_target="tpu_custom_call" | custom-call | tf_op jit(solution)/shard_map/first_image/pallas_call | solution.py:299
  20.8 0.2 collective-permute-start.4
  21.0 1.2 %collective-permute-done.4 = f32[32,640]{1,0:T(8,128)S(1)} collective-permute-done((f32[32,640]{1,0:T(8,128)S(1)}, f32[32,640]{1,0:T(8,128)S(1)}, u32[]{:S(2)}, u32[]{:S(2)}) %collective-permute-start.4) | collective-permute-done | bytes 81952 | tf_op jit(solution)/shard_map/ppermute | solution.py:271
  22.2 3.6 %collective-permute-start.7 = (f32[32,640]{1,0:T(8,128)S(1)}, f32[32,640]{1,0:T(8,128)S(1)}, u32[]{:S(2)}, u32[]{:S(2)}) collective-permute-start(f32[32,640]{1,0:T(8,128)S(1)} %select_add_fusion), channel_id=1, source_target_pairs={{0,6},{1,7},{2,4},{3,5},{4,2},{5,3},{6,0},{7,1},{8,14},{9,15},{10,... | collective-permute-start | bytes 245768 | tf_op jit(solution)/shard_map/ppermute | solution.py:271
  25.8 0.0 collective-permute-start.6
  25.8 0.4 collective-permute-start.5
  26.2 2.4 %collective-permute-done.7 = f32[32,640]{1,0:T(8,128)S(1)} collective-permute-done((f32[32,640]{1,0:T(8,128)S(1)}, f32[32,640]{1,0:T(8,128)S(1)}, u32[]{:S(2)}, u32[]{:S(2)}) %collective-permute-start.7) | collective-permute-done | bytes 81952 | tf_op jit(solution)/shard_map/ppermute | solution.py:271
  28.6 1.9 %collective-permute-done.6 = f32[32,640]{1,0:T(8,128)S(1)} collective-permute-done((f32[32,640]{1,0:T(8,128)S(1)}, f32[32,640]{1,0:T(8,128)S(1)}, u32[]{:S(2)}, u32[]{:S(2)}) %collective-permute-start.6) | collective-permute-done | bytes 81952 | tf_op jit(solution)/shard_map/ppermute | solution.py:271
  30.5 0.0 collective-permute-done.5
  30.5 3.6 %collective-permute-start.10 = (f32[32,640]{1,0:T(8,128)S(1)}, f32[32,640]{1,0:T(8,128)S(1)}, u32[]{:S(2)}, u32[]{:S(2)}) collective-permute-start(f32[32,640]{1,0:T(8,128)S(1)} %add_add_fusion.1), channel_id=1, source_target_pairs={{0,24},{1,25},{2,26},{3,27},{4,28},{5,29},{6,30},{7,31},{8,16},{9,... | collective-permute-start | bytes 245768 | tf_op jit(solution)/shard_map/ppermute | solution.py:271
  34.1 0.0 collective-permute-start.9
  34.1 0.6 collective-permute-start.8
  34.7 2.4 %collective-permute-done.10 = f32[32,640]{1,0:T(8,128)S(1)} collective-permute-done((f32[32,640]{1,0:T(8,128)S(1)}, f32[32,640]{1,0:T(8,128)S(1)}, u32[]{:S(2)}, u32[]{:S(2)}) %collective-permute-start.10) | collective-permute-done | bytes 81952 | tf_op jit(solution)/shard_map/ppermute | solution.py:271
  37.1 3.5 %collective-permute-done.9 = f32[32,640]{1,0:T(8,128)S(1)} collective-permute-done((f32[32,640]{1,0:T(8,128)S(1)}, f32[32,640]{1,0:T(8,128)S(1)}, u32[]{:S(2)}, u32[]{:S(2)}) %collective-permute-start.9) | collective-permute-done | bytes 81952 | tf_op jit(solution)/shard_map/ppermute | solution.py:271
  40.6 0.0 collective-permute-done.8
  40.7 0.6 collective-permute-start.11
  41.3 0.9 %collective-permute-done.11 = f32[32,640]{1,0:T(8,128)S(1)} collective-permute-done((f32[32,640]{1,0:T(8,128)S(1)}, f32[32,640]{1,0:T(8,128)S(1)}, u32[]{:S(2)}, u32[]{:S(2)}) %collective-permute-start.11) | collective-permute-done | bytes 81952 | tf_op jit(solution)/shard_map/ppermute | solution.py:271
  42.2 6.3 %first_solve.1 = (bf16[64,2048]{1,0:T(8,128)(2,1)S(1)}, f32[64,192]{1,0:T(8,128)S(1)}, f32[64,64]{1,0:T(8,128)S(1)}, f32[64,192]{1,0:T(8,128)S(1)}, f32[64,64]{1,0:T(8,128)S(1)}, /*index=5*/bf16[64,64]{1,0:T(8,128)(2,1)S(1)}) custom-call(f32[64,640]{1,0:T(8,128)S(1)} %pad_maximum_fusion.cross, bf16[192,2048]{1,0:T(8,128)(2,1)S(1)} %reshape.17.stack, ...), custom_call_target="tpu_custom_call" | custom-call | tf_op jit(solution)/shard_map/first_solve/pallas_call | solution.py:299
  48.6 0.7 collective-permute-start.13
  49.3 3.7 %collective-permute-start.12 = (bf16[64,1024]{1,0:T(8,128)(2,1)S(1)}, bf16[64,1024]{1,0:T(8,128)(2,1)S(1)}, u32[]{:S(2)}, u32[]{:S(2)}) collective-permute-start(bf16[64,1024]{1,0:T(8,128)(2,1)S(1)} %get-tuple-element.40), channel_id=1, source_target_pairs={{0,4},{8,12},{16,20},{24,28},{4,0},{12,8},{20,16},{28,24},{1,5},{9... | collective-permute-start | bytes 393224 | tf_op jit(solution)/shard_map/ppermute | solution.py:27
  53.0 0.0 collective-permute-done.13
  53.0 5.8 %collective-permute-done.12 = bf16[64,1024]{1,0:T(8,128)(2,1)S(1)} collective-permute-done((bf16[64,1024]{1,0:T(8,128)(2,1)S(1)}, bf16[64,1024]{1,0:T(8,128)(2,1)S(1)}, u32[]{:S(2)}, u32[]{:S(2)}) %collective-permute-start.12) | collective-permute-done | bytes 131104 | tf_op jit(solution)/shard_map/ppermute | solution.py:27
  58.9 0.7 collective-permute-start.15
  59.6 2.6 %collective-permute-start.14 = (bf16[64,512]{1,0:T(8,128)(2,1)S(1)}, bf16[64,512]{1,0:T(8,128)(2,1)S(1)}, u32[]{:S(2)}, u32[]{:S(2)}) collective-permute-start(bf16[64,512]{1,0:T(8,128)(2,1)S(1)} %get-tuple-element.54), channel_id=1, source_target_pairs={{0,1},{2,3},{1,0},{3,2},{4,5},{6,7},{5,4},{7,6},{8,9},{10,11},{9,8... | collective-permute-start | bytes 196616 | tf_op jit(solution)/shard_map/ppermute | solution.py:27
  62.2 0.0 collective-permute-done.15
  62.2 0.9 collective-permute-done.14
  63.1 1.6 %second_image.1 = (bf16[64,2048]{1,0:T(8,128)(2,1)S(1)}, f32[64,256]{1,0:T(8,128)S(1)}) custom-call(f32[27,16,128]{2,1,0:T(8,128)S(1)} %coefficients.1.coef, bf16[192,2048]{1,0:T(8,128)(2,1)S(1)} %reshape.17.stack, bf16[64,2048]{1,0:T(8,128)(2,1)S(1)} %get-tuple-element.20.block.last, bf16[64,1024]{1,0:T(8,128)(2,1)S(1)} %get-tuple-element.38.xlo, ...), custom_call_target="tpu_custom_call" | custom-call | tf_op jit(solution)/shard_map/second_image/pallas_call | solution.py:299
  64.7 1.3 %collective-permute-start.16 = (f32[32,256]{1,0:T(8,128)S(1)}, f32[32,256]{1,0:T(8,128)S(1)}, u32[]{:S(2)}, u32[]{:S(2)}) collective-permute-start(f32[32,256]{1,0:T(8,128)S(1)} %slice_select_fusion.1), channel_id=1, source_target_pairs={{0,1},{1,0},{2,3},{3,2},{4,5},{5,4},{6,7},{7,6},{8,9},{9,8},{10,11... | collective-permute-start | bytes 98312 | tf_op jit(solution)/shard_map/ppermute | solution.py:271
  65.9 0.9 collective-permute-done.16
  66.8 3.7 %collective-permute-start.19 = (f32[32,256]{1,0:T(8,128)S(1)}, f32[32,256]{1,0:T(8,128)S(1)}, u32[]{:S(2)}, u32[]{:S(2)}) collective-permute-start(f32[32,256]{1,0:T(8,128)S(1)} %select_add_fusion.1), channel_id=1, source_target_pairs={{0,6},{1,7},{2,4},{3,5},{4,2},{5,3},{6,0},{7,1},{8,14},{9,15},{10,... | collective-permute-start | bytes 98312 | tf_op jit(solution)/shard_map/ppermute | solution.py:271
  70.5 0.0 collective-permute-start.18
  70.5 0.4 collective-permute-start.17
  70.8 1.5 %collective-permute-done.19 = f32[32,256]{1,0:T(8,128)S(1)} collective-permute-done((f32[32,256]{1,0:T(8,128)S(1)}, f32[32,256]{1,0:T(8,128)S(1)}, u32[]{:S(2)}, u32[]{:S(2)}) %collective-permute-start.19) | collective-permute-done | bytes 32800 | tf_op jit(solution)/shard_map/ppermute | solution.py:271
  72.4 1.7 %collective-permute-done.18 = f32[32,256]{1,0:T(8,128)S(1)} collective-permute-done((f32[32,256]{1,0:T(8,128)S(1)}, f32[32,256]{1,0:T(8,128)S(1)}, u32[]{:S(2)}, u32[]{:S(2)}) %collective-permute-start.18) | collective-permute-done | bytes 32800 | tf_op jit(solution)/shard_map/ppermute | solution.py:271
  74.1 0.0 collective-permute-done.17
  74.1 1.9 %collective-permute-start.22 = (f32[32,256]{1,0:T(8,128)S(1)}, f32[32,256]{1,0:T(8,128)S(1)}, u32[]{:S(2)}, u32[]{:S(2)}) collective-permute-start(f32[32,256]{1,0:T(8,128)S(1)} %add_add_fusion.3), channel_id=1, source_target_pairs={{0,24},{1,25},{2,26},{3,27},{4,28},{5,29},{6,30},{7,31},{8,16},{9,... | collective-permute-start | bytes 98312 | tf_op jit(solution)/shard_map/ppermute | solution.py:271
  76.0 0.4 collective-permute-start.21
  76.4 1.8 %collective-permute-start.20 = (f32[32,256]{1,0:T(8,128)S(1)}, f32[32,256]{1,0:T(8,128)S(1)}, u32[]{:S(2)}, u32[]{:S(2)}) collective-permute-start(f32[32,256]{1,0:T(8,128)S(1)} %add_add_fusion.3), channel_id=1, source_target_pairs={{0,9},{1,8},{2,11},{3,10},{4,13},{5,12},{6,15},{7,14},{8,1},{9,0},... | collective-permute-start | bytes 98312 | tf_op jit(solution)/shard_map/ppermute | solution.py:271
  78.3 1.7 %collective-permute-done.22 = f32[32,256]{1,0:T(8,128)S(1)} collective-permute-done((f32[32,256]{1,0:T(8,128)S(1)}, f32[32,256]{1,0:T(8,128)S(1)}, u32[]{:S(2)}, u32[]{:S(2)}) %collective-permute-start.22) | collective-permute-done | bytes 32800 | tf_op jit(solution)/shard_map/ppermute | solution.py:271
  80.0 0.8 collective-permute-done.21
  80.8 0.4 collective-permute-done.20
  81.2 0.2 collective-permute-start.23
  81.4 0.4 next_gram.1
  81.8 0.7 collective-permute-done.23
  82.5 6.7 %second_solve.1 = (bf16[64,2048]{1,0:T(8,128)(2,1)S(1)}, f32[2,64,192]{2,1,0:T(8,128)}, f32[2,64,64]{2,1,0:T(8,128)}) custom-call(f32[64,256]{1,0:T(8,128)S(1)} %pad_maximum_fusion.5.cross, bf16[192,192]{1,0:T(8,128)(2,1)S(1)} %get-tuple-element.25.own_high, bf16[192,192]{1,0:T(8,128)(2,1)S(1)} %get-tuple-element.26.own_low, ...), custom_call_target="tpu_custom_call" | custom-call | tf_op jit(solution)/shard_map/second_solve/pallas_call | solution.py:299
  89.2 0.7 copy.6
  (26 shorter events, 0.4 us)
Async XLA Ops:
  0.6 1.0 %slice-start = ((bf16[3,64,2,8,128]{4,3,2,1,0:T(8,128)(2,1)}), bf16[1,64,2,8,128]{4,3,2,1,0:T(8,128)(2,1)S(1)}, s32[]{:S(2)}) async-start(bf16[3,64,2,8,128]{4,3,2,1,0:T(8,128)(2,1)} %param.3), calls=%async_computation | async-start | bytes 524288 | tf_op jit(solution)/shard_map/slice | solution.py:320
  1.7 15.2 %copy-start.2 = (bf16[3,64,2,8,128]{4,3,2,1,0:T(8,128)(2,1)S(1)}, bf16[3,64,2,8,128]{4,3,2,1,0:T(8,128)(2,1)}, u32[]{:S(2)}) copy-start(bf16[3,64,2,8,128]{4,3,2,1,0:T(8,128)(2,1)} %param.3) | copy-start | bytes 2359300
  1.8 6.6 %collective-permute-start.1 = (bf16[64,1024]{1,0:T(8,128)(2,1)S(1)}, bf16[64,1024]{1,0:T(8,128)(2,1)S(1)}, u32[]{:S(2)}, u32[]{:S(2)}) collective-permute-start(bf16[64,1024]{1,0:T(8,128)(2,1)S(1)} %get-tuple-element.47), channel_id=1, source_target_pairs={{4,8},{12,16},{20,24},{8,4},{16,12},{24,20},{5,9},{13,17},{21,25},... | collective-permute-start | bytes 393224 | tf_op jit(solution)/shard_map/ppermute | solution.py:28
  2.6 10.6 %collective-permute-start = (bf16[64,1024]{1,0:T(8,128)(2,1)S(1)}, bf16[64,1024]{1,0:T(8,128)(2,1)S(1)}, u32[]{:S(2)}, u32[]{:S(2)}) collective-permute-start(bf16[64,1024]{1,0:T(8,128)(2,1)S(1)} %get-tuple-element.48), channel_id=1, source_target_pairs={{0,4},{8,12},{16,20},{24,28},{4,0},{12,8},{20,16},{28,24},{1,5},{9... | collective-permute-start | bytes 393224 | tf_op jit(solution)/shard_map/ppermute | solution.py:27
  13.3 5.5 %collective-permute-start.3 = (bf16[64,512]{1,0:T(8,128)(2,1)S(1)}, bf16[64,512]{1,0:T(8,128)(2,1)S(1)}, u32[]{:S(2)}, u32[]{:S(2)}) collective-permute-start(bf16[64,512]{1,0:T(8,128)(2,1)S(1)} %get-tuple-element.61), channel_id=1, source_target_pairs={{1,2},{2,1},{5,6},{6,5},{9,10},{10,9},{13,14},{14,13},{17,18},{18,... | collective-permute-start | bytes 196616 | tf_op jit(solution)/shard_map/ppermute | solution.py:28
  13.9 4.8 %collective-permute-start.2 = (bf16[64,512]{1,0:T(8,128)(2,1)S(1)}, bf16[64,512]{1,0:T(8,128)(2,1)S(1)}, u32[]{:S(2)}, u32[]{:S(2)}) collective-permute-start(bf16[64,512]{1,0:T(8,128)(2,1)S(1)} %get-tuple-element.62), channel_id=1, source_target_pairs={{0,1},{2,3},{1,0},{3,2},{4,5},{6,7},{5,4},{7,6},{8,9},{10,11},{9,8... | collective-permute-start | bytes 196616 | tf_op jit(solution)/shard_map/ppermute | solution.py:27
  17.3 0.7 copy-start
  17.3 0.7 copy-start.1
  20.8 1.3 %collective-permute-start.4 = (f32[32,640]{1,0:T(8,128)S(1)}, f32[32,640]{1,0:T(8,128)S(1)}, u32[]{:S(2)}, u32[]{:S(2)}) collective-permute-start(f32[32,640]{1,0:T(8,128)S(1)} %slice_select_fusion), channel_id=1, source_target_pairs={{0,1},{1,0},{2,3},{3,2},{4,5},{5,4},{6,7},{7,6},{8,9},{9,8},{10,11... | collective-permute-start | bytes 245768 | tf_op jit(solution)/shard_map/ppermute | solution.py:271
  22.2 6.4 %collective-permute-start.7 = (f32[32,640]{1,0:T(8,128)S(1)}, f32[32,640]{1,0:T(8,128)S(1)}, u32[]{:S(2)}, u32[]{:S(2)}) collective-permute-start(f32[32,640]{1,0:T(8,128)S(1)} %select_add_fusion), channel_id=1, source_target_pairs={{0,6},{1,7},{2,4},{3,5},{4,2},{5,3},{6,0},{7,1},{8,14},{9,15},{10,... | collective-permute-start | bytes 245768 | tf_op jit(solution)/shard_map/ppermute | solution.py:271
  25.8 4.7 %collective-permute-start.6 = (f32[32,640]{1,0:T(8,128)S(1)}, f32[32,640]{1,0:T(8,128)S(1)}, u32[]{:S(2)}, u32[]{:S(2)}) collective-permute-start(f32[32,640]{1,0:T(8,128)S(1)} %select_add_fusion), channel_id=1, source_target_pairs={{0,5},{1,4},{2,7},{3,6},{4,1},{5,0},{6,3},{7,2},{8,13},{9,12},{10,... | collective-permute-start | bytes 245768 | tf_op jit(solution)/shard_map/ppermute | solution.py:271
  25.8 4.7 %collective-permute-start.5 = (f32[32,640]{1,0:T(8,128)S(1)}, f32[32,640]{1,0:T(8,128)S(1)}, u32[]{:S(2)}, u32[]{:S(2)}) collective-permute-start(f32[32,640]{1,0:T(8,128)S(1)} %select_add_fusion), channel_id=1, source_target_pairs={{0,3},{1,2},{2,1},{3,0},{4,7},{5,6},{6,5},{7,4},{8,11},{9,10},{10,... | collective-permute-start | bytes 245768 | tf_op jit(solution)/shard_map/ppermute | solution.py:271
  30.5 6.6 %collective-permute-start.10 = (f32[32,640]{1,0:T(8,128)S(1)}, f32[32,640]{1,0:T(8,128)S(1)}, u32[]{:S(2)}, u32[]{:S(2)}) collective-permute-start(f32[32,640]{1,0:T(8,128)S(1)} %add_add_fusion.1), channel_id=1, source_target_pairs={{0,24},{1,25},{2,26},{3,27},{4,28},{5,29},{6,30},{7,31},{8,16},{9,... | collective-permute-start | bytes 245768 | tf_op jit(solution)/shard_map/ppermute | solution.py:271
  34.1 6.5 %collective-permute-start.9 = (f32[32,640]{1,0:T(8,128)S(1)}, f32[32,640]{1,0:T(8,128)S(1)}, u32[]{:S(2)}, u32[]{:S(2)}) collective-permute-start(f32[32,640]{1,0:T(8,128)S(1)} %add_add_fusion.1), channel_id=1, source_target_pairs={{0,17},{1,16},{2,19},{3,18},{4,21},{5,20},{6,23},{7,22},{8,25},{9,... | collective-permute-start | bytes 245768 | tf_op jit(solution)/shard_map/ppermute | solution.py:271
  34.1 6.5 %collective-permute-start.8 = (f32[32,640]{1,0:T(8,128)S(1)}, f32[32,640]{1,0:T(8,128)S(1)}, u32[]{:S(2)}, u32[]{:S(2)}) collective-permute-start(f32[32,640]{1,0:T(8,128)S(1)} %add_add_fusion.1), channel_id=1, source_target_pairs={{0,9},{1,8},{2,11},{3,10},{4,13},{5,12},{6,15},{7,14},{8,1},{9,0},... | collective-permute-start | bytes 245768 | tf_op jit(solution)/shard_map/ppermute | solution.py:271
  40.7 1.5 %collective-permute-start.11 = (f32[32,640]{1,0:T(8,128)S(1)}, f32[32,640]{1,0:T(8,128)S(1)}, u32[]{:S(2)}, u32[]{:S(2)}) collective-permute-start(f32[32,640]{1,0:T(8,128)S(1)} %add_add_fusion), channel_id=1, source_target_pairs={{0,1},{1,0},{2,3},{3,2},{4,5},{5,4},{6,7},{7,6},{8,9},{9,8},{10,11... | collective-permute-start | bytes 245768 | tf_op jit(solution)/shard_map/ppermute | solution.py:271
  48.6 4.4 %collective-permute-start.13 = (bf16[64,1024]{1,0:T(8,128)(2,1)S(1)}, bf16[64,1024]{1,0:T(8,128)(2,1)S(1)}, u32[]{:S(2)}, u32[]{:S(2)}) collective-permute-start(bf16[64,1024]{1,0:T(8,128)(2,1)S(1)} %get-tuple-element.39), channel_id=1, source_target_pairs={{4,8},{12,16},{20,24},{8,4},{16,12},{24,20},{5,9},{13,17},{21,25},... | collective-permute-start | bytes 393224 | tf_op jit(solution)/shard_map/ppermute | solution.py:28
  49.3 9.5 %collective-permute-start.12 = (bf16[64,1024]{1,0:T(8,128)(2,1)S(1)}, bf16[64,1024]{1,0:T(8,128)(2,1)S(1)}, u32[]{:S(2)}, u32[]{:S(2)}) collective-permute-start(bf16[64,1024]{1,0:T(8,128)(2,1)S(1)} %get-tuple-element.40), channel_id=1, source_target_pairs={{0,4},{8,12},{16,20},{24,28},{4,0},{12,8},{20,16},{28,24},{1,5},{9... | collective-permute-start | bytes 393224 | tf_op jit(solution)/shard_map/ppermute | solution.py:27
  58.9 3.3 %collective-permute-start.15 = (bf16[64,512]{1,0:T(8,128)(2,1)S(1)}, bf16[64,512]{1,0:T(8,128)(2,1)S(1)}, u32[]{:S(2)}, u32[]{:S(2)}) collective-permute-start(bf16[64,512]{1,0:T(8,128)(2,1)S(1)} %get-tuple-element.53), channel_id=1, source_target_pairs={{1,2},{2,1},{5,6},{6,5},{9,10},{10,9},{13,14},{14,13},{17,18},{18,... | collective-permute-start | bytes 196616 | tf_op jit(solution)/shard_map/ppermute | solution.py:28
  59.6 3.5 %collective-permute-start.14 = (bf16[64,512]{1,0:T(8,128)(2,1)S(1)}, bf16[64,512]{1,0:T(8,128)(2,1)S(1)}, u32[]{:S(2)}, u32[]{:S(2)}) collective-permute-start(bf16[64,512]{1,0:T(8,128)(2,1)S(1)} %get-tuple-element.54), channel_id=1, source_target_pairs={{0,1},{2,3},{1,0},{3,2},{4,5},{6,7},{5,4},{7,6},{8,9},{10,11},{9,8... | collective-permute-start | bytes 196616 | tf_op jit(solution)/shard_map/ppermute | solution.py:27
  64.7 2.1 %collective-permute-start.16 = (f32[32,256]{1,0:T(8,128)S(1)}, f32[32,256]{1,0:T(8,128)S(1)}, u32[]{:S(2)}, u32[]{:S(2)}) collective-permute-start(f32[32,256]{1,0:T(8,128)S(1)} %slice_select_fusion.1), channel_id=1, source_target_pairs={{0,1},{1,0},{2,3},{3,2},{4,5},{5,4},{6,7},{7,6},{8,9},{9,8},{10,11... | collective-permute-start | bytes 98312 | tf_op jit(solution)/shard_map/ppermute | solution.py:271
  66.8 5.6 %collective-permute-start.19 = (f32[32,256]{1,0:T(8,128)S(1)}, f32[32,256]{1,0:T(8,128)S(1)}, u32[]{:S(2)}, u32[]{:S(2)}) collective-permute-start(f32[32,256]{1,0:T(8,128)S(1)} %select_add_fusion.1), channel_id=1, source_target_pairs={{0,6},{1,7},{2,4},{3,5},{4,2},{5,3},{6,0},{7,1},{8,14},{9,15},{10,... | collective-permute-start | bytes 98312 | tf_op jit(solution)/shard_map/ppermute | solution.py:271
  70.5 3.6 %collective-permute-start.18 = (f32[32,256]{1,0:T(8,128)S(1)}, f32[32,256]{1,0:T(8,128)S(1)}, u32[]{:S(2)}, u32[]{:S(2)}) collective-permute-start(f32[32,256]{1,0:T(8,128)S(1)} %select_add_fusion.1), channel_id=1, source_target_pairs={{0,5},{1,4},{2,7},{3,6},{4,1},{5,0},{6,3},{7,2},{8,13},{9,12},{10,... | collective-permute-start | bytes 98312 | tf_op jit(solution)/shard_map/ppermute | solution.py:271
  70.5 3.6 %collective-permute-start.17 = (f32[32,256]{1,0:T(8,128)S(1)}, f32[32,256]{1,0:T(8,128)S(1)}, u32[]{:S(2)}, u32[]{:S(2)}) collective-permute-start(f32[32,256]{1,0:T(8,128)S(1)} %select_add_fusion.1), channel_id=1, source_target_pairs={{0,3},{1,2},{2,1},{3,0},{4,7},{5,6},{6,5},{7,4},{8,11},{9,10},{10,... | collective-permute-start | bytes 98312 | tf_op jit(solution)/shard_map/ppermute | solution.py:271
  74.1 5.9 %collective-permute-start.22 = (f32[32,256]{1,0:T(8,128)S(1)}, f32[32,256]{1,0:T(8,128)S(1)}, u32[]{:S(2)}, u32[]{:S(2)}) collective-permute-start(f32[32,256]{1,0:T(8,128)S(1)} %add_add_fusion.3), channel_id=1, source_target_pairs={{0,24},{1,25},{2,26},{3,27},{4,28},{5,29},{6,30},{7,31},{8,16},{9,... | collective-permute-start | bytes 98312 | tf_op jit(solution)/shard_map/ppermute | solution.py:271
  76.0 4.8 %collective-permute-start.21 = (f32[32,256]{1,0:T(8,128)S(1)}, f32[32,256]{1,0:T(8,128)S(1)}, u32[]{:S(2)}, u32[]{:S(2)}) collective-permute-start(f32[32,256]{1,0:T(8,128)S(1)} %add_add_fusion.3), channel_id=1, source_target_pairs={{0,17},{1,16},{2,19},{3,18},{4,21},{5,20},{6,23},{7,22},{8,25},{9,... | collective-permute-start | bytes 98312 | tf_op jit(solution)/shard_map/ppermute | solution.py:271
  76.4 4.7 %collective-permute-start.20 = (f32[32,256]{1,0:T(8,128)S(1)}, f32[32,256]{1,0:T(8,128)S(1)}, u32[]{:S(2)}, u32[]{:S(2)}) collective-permute-start(f32[32,256]{1,0:T(8,128)S(1)} %add_add_fusion.3), channel_id=1, source_target_pairs={{0,9},{1,8},{2,11},{3,10},{4,13},{5,12},{6,15},{7,14},{8,1},{9,0},... | collective-permute-start | bytes 98312 | tf_op jit(solution)/shard_map/ppermute | solution.py:271
  81.2 1.3 %collective-permute-start.23 = (f32[32,256]{1,0:T(8,128)S(1)}, f32[32,256]{1,0:T(8,128)S(1)}, u32[]{:S(2)}, u32[]{:S(2)}) collective-permute-start(f32[32,256]{1,0:T(8,128)S(1)} %add_add_fusion.2), channel_id=1, source_target_pairs={{0,1},{1,0},{2,3},{3,2},{4,5},{5,4},{6,7},{7,6},{8,9},{9,8},{10,11... | collective-permute-start | bytes 98312 | tf_op jit(solution)/shard_map/ppermute | solution.py:271

commit v9 on v8

--- a/solution.py
+++ b/solution.py
@@ -16,7 +16,7 @@
     return lax.dot_general(left, right, dims, preferred_element_type=jnp.float32)
 
 
-def neighbours(block, span_x, span_y, depth):
+def neighbours(block, span_x, span_y, depth, meanwhile=()):
     plane = span_y * depth
 
     def exchange(axis, upward, downward):
@@ -30,6 +30,8 @@
 
     xlo, xhi = exchange("slab", block[:, (span_x - 1) * plane :], block[:, :plane])
 
+    xlo, xhi, meanwhile = lax.optimization_barrier((xlo, xhi, meanwhile))
+
     def edge(row):
         at = row * depth
         parts = [xlo[:, at : at + depth]]
@@ -38,7 +40,7 @@
         return jnp.concatenate(parts, axis=1)
 
     ylo, yhi = exchange("col", edge(span_y - 1), edge(0))
-    return xlo, xhi, ylo, yhi
+    return (xlo, xhi, ylo, yhi), meanwhile
 
 
 def coefficients_kernel(table, cells, coef):
@@ -117,7 +119,15 @@
     lax.fori_loop(0, columns // ROWS, tile, 0)
 
 
-def first_image_kernel(spans, coef, stack, xlo, xhi, ylo, yhi, image, cross):
+def stack_gram_kernel(columns, stack, own):
+    at = 0
+    for b in range(0, stack.shape[0], columns):
+        width = stack.shape[0] - b
+        own[:, at : at + width] = dot(stack[b : b + columns], stack[b:], NT)
+        at += width
+
+
+def first_image_kernel(spans, coef, stack, own, xlo, xhi, ylo, yhi, image, cross):
     columns = image.shape[0]
     fields = stack.shape[0]
     block = stack.at[fields - columns : fields]
@@ -125,11 +135,7 @@
     w = image[...]
     cross[:, :fields] = dot(w, stack[...], NT)
     cross[:, fields : fields + columns] = dot(w, w, NT)
-    at = fields + columns
-    for b in range(0, fields, columns):
-        width = fields - b
-        cross[:, at : at + width] = dot(stack[b : b + columns], stack[b:], NT)
-        at += width
+    cross[:, fields + columns :] = own[...]
 
 
 def second_image_kernel(spans, coef, stack, block, xlo, xhi, ylo, yhi, image, cross):
@@ -153,39 +159,50 @@
 
 def factor(square):
     size = square.shape[0]
-    f32 = jnp.float32
+    shape = (8, 2 * size)
+    sub = lax.broadcasted_iota(jnp.int32, shape, 0)
     unit = lax.broadcasted_iota(jnp.int32, (size, size), 0) == lax.broadcasted_iota(
         jnp.int32, (size, size), 1
     )
-    diagonal = jnp.where(unit, square, 0.0)
-    down = lax.rsqrt(jnp.sum(diagonal, axis=1, keepdims=True))
-    across_squared = jnp.sum(diagonal, axis=0, keepdims=True)
-    across = lax.rsqrt(across_squared)
-    whole = jnp.concatenate([square * down * across, unit.astype(f32)], axis=1)
-    sub = lax.broadcasted_iota(jnp.int32, (8, 2 * size), 0)
-    blocks = [whole[8 * b : 8 * b + 8] for b in range(size // 8)]
-    done = [jnp.zeros((8, 2 * size), f32) for _ in blocks]
-    for k in range(0, size, 2):
-        b, r = divmod(k, 8)
-        here = blocks[b]
-        row, next_row = here[r : r + 1, :], here[r + 1 : r + 2, :]
-        first, mixed = row[:, k : k + 1], next_row[:, k : k + 1]
-        last = next_row[:, k + 1 : k + 2]
-        inverse = 1.0 / (first * last - mixed * mixed)
-        left = (last * row - mixed * next_row) * inverse
-        right = (first * next_row - mixed * row) * inverse
-        for later in range(b, size // 8):
-            one, two = blocks[later][:, k : k + 1], blocks[later][:, k + 1 : k + 2]
-            change = one * left + two * right
-            if later == b:
-                change = jnp.where(sub > r + 1, change, 0.0)
-            blocks[later] = blocks[later] - change
-        ratio = mixed * (1.0 / first)
-        done[b] = jnp.where(sub == r, row * lax.rsqrt(first), done[b])
-        rest = (next_row - ratio * row) * lax.rsqrt(last - ratio * mixed)
-        done[b] = jnp.where(sub == r + 1, rest, done[b])
+    whole = jnp.concatenate([square, unit.astype(jnp.float32)], axis=1)
+    blocks = [whole[b : b + 8] for b in range(0, size, 8)]
+    done = []
+
+    def row_of(values, at):
+        return jnp.broadcast_to(values[at : at + 1, :], shape)
+
+    def column_of(values, at):
+        return jnp.broadcast_to(values[:, at : at + 1], shape)
+
+    for b, here in enumerate(blocks):
+        columns = [column_of(here, 8 * b + j) for j in range(8)]
+        entry = {(i, j): row_of(columns[j], i) for j in range(8) for i in range(j + 1)}
+        rows = [row_of(here, i) for i in range(8)]
+        inverse, ratio = [], {}
+        for r in range(8):
+            inverse.append(1.0 / entry[r, r])
+            for j in range(r + 1, 8):
+                ratio[r, j] = entry[r, j] * inverse[r]
+            for i in range(r + 1, 8):
+                for j in range(i, 8):
+                    entry[i, j] = entry[i, j] - entry[r, i] * ratio[r, j]
+                rows[i] = rows[i] - ratio[r, i] * rows[r]
+        solved = {}
+        for r in reversed(range(8)):
+            solved[r] = rows[r] * inverse[r]
+            for j in range(r + 1, 8):
+                solved[r] = solved[r] - ratio[r, j] * solved[j]
+        for later in range(b + 1, len(blocks)):
+            for j in range(8):
+                change = column_of(blocks[later], 8 * b + j) * solved[j]
+                total = change if j == 0 else total + change
+            blocks[later] = blocks[later] - total
+        scaled = jnp.zeros(shape, jnp.float32)
+        for r in range(8):
+            scaled = jnp.where(sub == r, rows[r] * lax.rsqrt(entry[r, r]), scaled)
+        done.append(scaled)
     done = jnp.concatenate(done, axis=0)
-    return done[:, :size] * (across_squared * across), done[:, size:] * across
+    return done[:, :size], done[:, size:]
 
 
 def project(cross, own, scale):
@@ -285,12 +302,8 @@
     part = jnp.where(upper, high, low) + partner(jnp.where(upper, low, high), 1)
     bit = 2
     while bit < count:
-        if 2 * bit < count:
-            one, two, both = (partner(part, mask) for mask in (bit + 1, 2 * bit + 1, 3 * bit))
-            part = (part + one) + (two + both)
-        else:
-            part = part + partner(part, bit + 1)
-        bit *= 4
+        part = part + partner(part, bit + 1)
+        bit *= 2
     other = partner(part, 1)
     return jnp.concatenate([jnp.where(upper, other, part), jnp.where(upper, part, other)], axis=0)
 
@@ -317,13 +330,21 @@
 
     stack = basis.reshape(fields, cells)
     coef = coefficients(table, cell_map)
-    around = neighbours(stack[fields - columns :], *spans)
-    packed = fields + columns + columns * blocks * (blocks + 1) // 2
+    (own,) = call(
+        functools.partial(stack_gram_kernel, columns),
+        "stack_gram",
+        [((columns, columns * blocks * (blocks + 1) // 2), f32)],
+        stack,
+    )
+    around, (coef, stack, own) = neighbours(
+        basis[blocks - 1].reshape(columns, cells), *spans, (coef, stack, own)
+    )
+    packed = fields + columns + own.shape[1]
     image, cross = call(
         functools.partial(first_image_kernel, spans),
         "first_image",
         [((columns, cells), bf16), ((columns, packed), f32)],
-        coef, stack, *around,
+        coef, stack, own, *around,
     )
     cross = whole_sum(cross)
     block, proj, low, rest, square, inverse = call(
@@ -339,7 +360,7 @@
         [((fields, fields), bf16)] * 2,
         cross, rest, square, inverse,
     )
-    around = neighbours(block, *spans)
+    around, _ = neighbours(block, *spans)
     image, cross = call(
         functools.partial(second_image_kernel, spans),
         "second_image",

time: 90.2 us -> 88.2 us (0.978)
  Pallas kernels: 17.7 us -> 12.7 us
  starting transfers between devices: 36.4 us -> 39.6 us
    pallas_call x5 -> x6, Pallas kernels: 16.9 us -> 12 us  [call(): pl.pallas_call(kernel, out_shape=[jax.ShapeDtypeStruct(shape, dtype) for...]
    ppermute x16 -> x12, starting transfers between devices: 18.6 us -> 20.4 us  [partner(): return lax.ppermute(part, axes, [(i, i ^ mask) for i in range(count)])]
    ppermute x16 -> x12, waiting for transfers between devices: 20.1 us -> 21.5 us  [partner(): return lax.ppermute(part, axes, [(i, i ^ mask) for i in range(count)])]
    ppermute x4, starting transfers between devices: 15 us -> 16.5 us  [exchange(): inner = lax.ppermute(jnp.where(odd, downward, upward), axis, swaps[0])]
    ppermute x4, waiting for transfers between devices: 11.5 us -> 10.3 us  [exchange(): inner = lax.ppermute(jnp.where(odd, downward, upward), axis, swaps[0])]
  transfers between devices with their start and end apart: 24 -> 20, of which waited for: 16 -> 16; matrix products, arithmetic and copies ran while one was open for 0% -> 0% of each run, Pallas kernels for 1% -> 2%
where the time goes in v9:
time: 88.2 us; the launch traced here: 87.7 us
  starting transfers between devices  39.6 us (45%)
  waiting for transfers between devices  31.9 us (36%)
  Pallas kernels  12.7 us (14%)
  local copies, waits for them, and re-layouts  2.25 us (3%)
  between operations  0.91 us (1%)
    ppermute x12, waiting for transfers between devices, partner(): return lax.ppermute(part, axes, [(i, i ^ mask) for i in range(count)])  21.5 us
    ppermute x12, starting transfers between devices, partner(): return lax.ppermute(part, axes, [(i, i ^ mask) for i in range(count)])  20.4 us
    ppermute x4, starting transfers between devices, exchange(): inner = lax.ppermute(jnp.where(odd, downward, upward), axis, swaps[0])  16.5 us
    pallas_call x6, Pallas kernels, call(): pl.pallas_call(kernel, out_shape=[jax.ShapeDtypeStruct(shape, dtype) for...  12 us
    ppermute x4, waiting for transfers between devices, exchange(): inner = lax.ppermute(jnp.where(odd, downward, upward), axis, swaps[0])  10.3 us
    ppermute x4, starting transfers between devices, exchange(): outer = lax.ppermute(jnp.where(odd, upward, downward), axis, swaps[1])  2.67 us
  transfers between devices with their start and end apart: 20, of which 16 were waited for; matrix products, arithmetic and copies ran while one was open for 0% of the time, Pallas kernels for 2%

profile of v9, /device:TPU:0, one launch (start us, length us, event | category | flops | bytes accessed | tf_op | source)
XLA Modules:
  0.0 87.7 jit_solution(9597624447672040606)
XLA Ops:
  0.6 0.0 slice-start
  0.7 0.0 copy-start.2
  0.7 0.9 %slice-done = bf16[1,64,2,8,128]{4,3,2,1,0:T(8,128)(2,1)S(1)} async-done(((bf16[3,64,2,8,128]{4,3,2,1,0:T(8,128)(2,1)}), bf16[1,64,2,8,128]{4,3,2,1,0:T(8,128)(2,1)S(1)}, s32[]{:S(2)}) %slice-start) | async-done | bytes 262168 | tf_op jit(solution)/shard_map/slice | solution.py:340
  1.6 0.1 reshape_squeeze.3
  1.7 0.7 collective-permute-start.1
  2.4 5.8 %collective-permute-start = (bf16[64,1024]{1,0:T(8,128)(2,1)S(1)}, bf16[64,1024]{1,0:T(8,128)(2,1)S(1)}, u32[]{:S(2)}, u32[]{:S(2)}) collective-permute-start(bf16[64,1024]{1,0:T(8,128)(2,1)S(1)} %get-tuple-element.62), channel_id=1, source_target_pairs={{0,4},{8,12},{16,20},{24,28},{4,0},{12,8},{20,16},{28,24},{1,5},{9... | collective-permute-start | bytes 393224 | tf_op jit(solution)/shard_map/ppermute | solution.py:27
  8.2 0.0 copy-done.2
  8.2 0.3 reshape.16.stack
  8.6 0.0 copy-start
  8.6 0.0 copy-start.1
  8.6 0.6 stack_gram.1.own
  9.2 0.0 copy-done
  9.3 0.0 copy-done.1
  9.3 0.8 coefficients.1.coef
  10.1 0.0 collective-permute-done.1
  10.1 3.0 %collective-permute-done = bf16[64,1024]{1,0:T(8,128)(2,1)S(1)} collective-permute-done((bf16[64,1024]{1,0:T(8,128)(2,1)S(1)}, bf16[64,1024]{1,0:T(8,128)(2,1)S(1)}, u32[]{:S(2)}, u32[]{:S(2)}) %collective-permute-start) | collective-permute-done | bytes 131104 | tf_op jit(solution)/shard_map/ppermute | solution.py:27
  13.1 0.7 collective-permute-start.3
  13.8 2.9 %collective-permute-start.2 = (bf16[64,512]{1,0:T(8,128)(2,1)S(1)}, bf16[64,512]{1,0:T(8,128)(2,1)S(1)}, u32[]{:S(2)}, u32[]{:S(2)}) collective-permute-start(bf16[64,512]{1,0:T(8,128)(2,1)S(1)} %get-tuple-element.76), channel_id=1, source_target_pairs={{0,1},{2,3},{1,0},{3,2},{4,5},{6,7},{5,4},{7,6},{8,9},{10,11},{9,8... | collective-permute-start | bytes 196616 | tf_op jit(solution)/shard_map/ppermute | solution.py:27
  16.7 0.0 collective-permute-done.3
  16.7 0.9 %collective-permute-done.2 = bf16[64,512]{1,0:T(8,128)(2,1)S(1)} collective-permute-done((bf16[64,512]{1,0:T(8,128)(2,1)S(1)}, bf16[64,512]{1,0:T(8,128)(2,1)S(1)}, u32[]{:S(2)}, u32[]{:S(2)}) %collective-permute-start.2) | collective-permute-done | bytes 65568 | tf_op jit(solution)/shard_map/ppermute | solution.py:27
  17.7 1.5 %first_image.1 = (bf16[64,2048]{1,0:T(8,128)(2,1)S(1)}, f32[64,640]{1,0:T(8,128)S(1)}) custom-call(f32[27,16,128]{2,1,0:T(8,128)S(1)} %coefficients.1.coef, bf16[192,2048]{1,0:T(8,128)(2,1)S(1)} %reshape.16.stack, f32[64,384]{1,0:T(8,128)S(1)} %stack_gram.1.own, bf16[64,1024]{1,0:T(8,128)(2,1)S(1)} %get-tuple-element.28.xlo, ...), custom_call_target="tpu_custom_call" | custom-call | tf_op jit(solution)/shard_map/first_image/pallas_call | solution.py:312
  19.2 1.2 %collective-permute-start.4 = (f32[32,640]{1,0:T(8,128)S(1)}, f32[32,640]{1,0:T(8,128)S(1)}, u32[]{:S(2)}, u32[]{:S(2)}) collective-permute-start(f32[32,640]{1,0:T(8,128)S(1)} %slice_select_fusion), channel_id=1, source_target_pairs={{0,1},{1,0},{2,3},{3,2},{4,5},{5,4},{6,7},{7,6},{8,9},{9,8},{10,11... | collective-permute-start | bytes 245768 | tf_op jit(solution)/shard_map/ppermute | solution.py:288
  20.3 0.9 %collective-permute-done.4 = f32[32,640]{1,0:T(8,128)S(1)} collective-permute-done((f32[32,640]{1,0:T(8,128)S(1)}, f32[32,640]{1,0:T(8,128)S(1)}, u32[]{:S(2)}, u32[]{:S(2)}) %collective-permute-start.4) | collective-permute-done | bytes 81952 | tf_op jit(solution)/shard_map/ppermute | solution.py:288
  21.3 1.7 %collective-permute-start.5 = (f32[32,640]{1,0:T(8,128)S(1)}, f32[32,640]{1,0:T(8,128)S(1)}, u32[]{:S(2)}, u32[]{:S(2)}) collective-permute-start(f32[32,640]{1,0:T(8,128)S(1)} %select_add_fusion), channel_id=1, source_target_pairs={{0,3},{1,2},{2,1},{3,0},{4,7},{5,6},{6,5},{7,4},{8,11},{9,10},{10,... | collective-permute-start | bytes 245768 | tf_op jit(solution)/shard_map/ppermute | solution.py:288
  23.0 2.7 %collective-permute-done.5 = f32[32,640]{1,0:T(8,128)S(1)} collective-permute-done((f32[32,640]{1,0:T(8,128)S(1)}, f32[32,640]{1,0:T(8,128)S(1)}, u32[]{:S(2)}, u32[]{:S(2)}) %collective-permute-start.5) | collective-permute-done | bytes 81952 | tf_op jit(solution)/shard_map/ppermute | solution.py:288
  25.6 2.4 %collective-permute-start.6 = (f32[32,640]{1,0:T(8,128)S(1)}, f32[32,640]{1,0:T(8,128)S(1)}, u32[]{:S(2)}, u32[]{:S(2)}) collective-permute-start(f32[32,640]{1,0:T(8,128)S(1)} %add.77), channel_id=1, source_target_pairs={{0,5},{1,4},{2,7},{3,6},{4,1},{5,0},{6,3},{7,2},{8,13},{9,12},{10,... | collective-permute-start | bytes 245768 | tf_op jit(solution)/shard_map/ppermute | solution.py:288
  28.1 2.7 %collective-permute-done.6 = f32[32,640]{1,0:T(8,128)S(1)} collective-permute-done((f32[32,640]{1,0:T(8,128)S(1)}, f32[32,640]{1,0:T(8,128)S(1)}, u32[]{:S(2)}, u32[]{:S(2)}) %collective-permute-start.6) | collective-permute-done | bytes 81952 | tf_op jit(solution)/shard_map/ppermute | solution.py:288
  30.8 1.7 %collective-permute-start.7 = (f32[32,640]{1,0:T(8,128)S(1)}, f32[32,640]{1,0:T(8,128)S(1)}, u32[]{:S(2)}, u32[]{:S(2)}) collective-permute-start(f32[32,640]{1,0:T(8,128)S(1)} %add.78), channel_id=1, source_target_pairs={{0,9},{1,8},{2,11},{3,10},{4,13},{5,12},{6,15},{7,14},{8,1},{9,0},... | collective-permute-start | bytes 245768 | tf_op jit(solution)/shard_map/ppermute | solution.py:288
  32.5 2.8 %collective-permute-done.7 = f32[32,640]{1,0:T(8,128)S(1)} collective-permute-done((f32[32,640]{1,0:T(8,128)S(1)}, f32[32,640]{1,0:T(8,128)S(1)}, u32[]{:S(2)}, u32[]{:S(2)}) %collective-permute-start.7) | collective-permute-done | bytes 81952 | tf_op jit(solution)/shard_map/ppermute | solution.py:288
  35.3 2.7 %collective-permute-start.8 = (f32[32,640]{1,0:T(8,128)S(1)}, f32[32,640]{1,0:T(8,128)S(1)}, u32[]{:S(2)}, u32[]{:S(2)}) collective-permute-start(f32[32,640]{1,0:T(8,128)S(1)} %add.79), channel_id=1, source_target_pairs={{0,17},{1,16},{2,19},{3,18},{4,21},{5,20},{6,23},{7,22},{8,25},{9,... | collective-permute-start | bytes 245768 | tf_op jit(solution)/shard_map/ppermute | solution.py:288
  38.0 2.6 %collective-permute-done.8 = f32[32,640]{1,0:T(8,128)S(1)} collective-permute-done((f32[32,640]{1,0:T(8,128)S(1)}, f32[32,640]{1,0:T(8,128)S(1)}, u32[]{:S(2)}, u32[]{:S(2)}) %collective-permute-start.8) | collective-permute-done | bytes 81952 | tf_op jit(solution)/shard_map/ppermute | solution.py:288
  40.5 2.1 %collective-permute-start.9 = (f32[32,640]{1,0:T(8,128)S(1)}, f32[32,640]{1,0:T(8,128)S(1)}, u32[]{:S(2)}, u32[]{:S(2)}) collective-permute-start(f32[32,640]{1,0:T(8,128)S(1)} %add.80), channel_id=1, source_target_pairs={{0,1},{1,0},{2,3},{3,2},{4,5},{5,4},{6,7},{7,6},{8,9},{9,8},{10,11... | collective-permute-start | bytes 245768 | tf_op jit(solution)/shard_map/ppermute | solution.py:288
  42.6 0.9 %collective-permute-done.9 = f32[32,640]{1,0:T(8,128)S(1)} collective-permute-done((f32[32,640]{1,0:T(8,128)S(1)}, f32[32,640]{1,0:T(8,128)S(1)}, u32[]{:S(2)}, u32[]{:S(2)}) %collective-permute-start.9) | collective-permute-done | bytes 81952 | tf_op jit(solution)/shard_map/ppermute | solution.py:288
  43.6 3.8 %first_solve.1 = (bf16[64,2048]{1,0:T(8,128)(2,1)S(1)}, f32[64,192]{1,0:T(8,128)S(1)}, f32[64,64]{1,0:T(8,128)S(1)}, f32[64,192]{1,0:T(8,128)S(1)}, f32[64,64]{1,0:T(8,128)S(1)}, /*index=5*/bf16[64,64]{1,0:T(8,128)(2,1)S(1)}) custom-call(f32[64,640]{1,0:T(8,128)S(1)} %pad_maximum_fusion.cross, bf16[192,2048]{1,0:T(8,128)(2,1)S(1)} %reshape.16.stack, ...), custom_call_target="tpu_custom_call" | custom-call | tf_op jit(solution)/shard_map/first_solve/pallas_call | solution.py:312
  47.5 0.7 collective-permute-start.11
  48.1 4.3 %collective-permute-start.10 = (bf16[64,1024]{1,0:T(8,128)(2,1)S(1)}, bf16[64,1024]{1,0:T(8,128)(2,1)S(1)}, u32[]{:S(2)}, u32[]{:S(2)}) collective-permute-start(bf16[64,1024]{1,0:T(8,128)(2,1)S(1)} %get-tuple-element.54), channel_id=1, source_target_pairs={{0,4},{8,12},{16,20},{24,28},{4,0},{12,8},{20,16},{28,24},{1,5},{9... | collective-permute-start | bytes 393224 | tf_op jit(solution)/shard_map/ppermute | solution.py:27
  52.4 0.0 collective-permute-done.11
  52.5 5.6 %collective-permute-done.10 = bf16[64,1024]{1,0:T(8,128)(2,1)S(1)} collective-permute-done((bf16[64,1024]{1,0:T(8,128)(2,1)S(1)}, bf16[64,1024]{1,0:T(8,128)(2,1)S(1)}, u32[]{:S(2)}, u32[]{:S(2)}) %collective-permute-start.10) | collective-permute-done | bytes 131104 | tf_op jit(solution)/shard_map/ppermute | solution.py:27
  58.1 0.7 collective-permute-start.13
  58.8 3.4 %collective-permute-start.12 = (bf16[64,512]{1,0:T(8,128)(2,1)S(1)}, bf16[64,512]{1,0:T(8,128)(2,1)S(1)}, u32[]{:S(2)}, u32[]{:S(2)}) collective-permute-start(bf16[64,512]{1,0:T(8,128)(2,1)S(1)} %get-tuple-element.68), channel_id=1, source_target_pairs={{0,1},{2,3},{1,0},{3,2},{4,5},{6,7},{5,4},{7,6},{8,9},{10,11},{9,8... | collective-permute-start | bytes 196616 | tf_op jit(solution)/shard_map/ppermute | solution.py:27
  62.2 0.0 collective-permute-done.13
  62.2 0.9 %collective-permute-done.12 = bf16[64,512]{1,0:T(8,128)(2,1)S(1)} collective-permute-done((bf16[64,512]{1,0:T(8,128)(2,1)S(1)}, bf16[64,512]{1,0:T(8,128)(2,1)S(1)}, u32[]{:S(2)}, u32[]{:S(2)}) %collective-permute-start.12) | collective-permute-done | bytes 65568 | tf_op jit(solution)/shard_map/ppermute | solution.py:27
  63.2 1.5 %second_image.1 = (bf16[64,2048]{1,0:T(8,128)(2,1)S(1)}, f32[64,256]{1,0:T(8,128)S(1)}) custom-call(f32[27,16,128]{2,1,0:T(8,128)S(1)} %coefficients.1.coef, bf16[192,2048]{1,0:T(8,128)(2,1)S(1)} %reshape.16.stack, bf16[64,2048]{1,0:T(8,128)(2,1)S(1)} %get-tuple-element.32.block.last, bf16[64,1024]{1,0:T(8,128)(2,1)S(1)} %get-tuple-element.33.xlo, ...), custom_call_target="tpu_custom_call" | custom-call | tf_op jit(solution)/shard_map/second_image/pallas_call | solution.py:312
  64.7 1.0 %collective-permute-start.14 = (f32[32,256]{1,0:T(8,128)S(1)}, f32[32,256]{1,0:T(8,128)S(1)}, u32[]{:S(2)}, u32[]{:S(2)}) collective-permute-start(f32[32,256]{1,0:T(8,128)S(1)} %slice_select_fusion.1), channel_id=1, source_target_pairs={{0,1},{1,0},{2,3},{3,2},{4,5},{5,4},{6,7},{7,6},{8,9},{9,8},{10,11... | collective-permute-start | bytes 98312 | tf_op jit(solution)/shard_map/ppermute | solution.py:288
  65.7 0.9 collective-permute-done.14
  66.6 1.7 %collective-permute-start.15 = (f32[32,256]{1,0:T(8,128)S(1)}, f32[32,256]{1,0:T(8,128)S(1)}, u32[]{:S(2)}, u32[]{:S(2)}) collective-permute-start(f32[32,256]{1,0:T(8,128)S(1)} %select_add_fusion.1), channel_id=1, source_target_pairs={{0,3},{1,2},{2,1},{3,0},{4,7},{5,6},{6,5},{7,4},{8,11},{9,10},{10,... | collective-permute-start | bytes 98312 | tf_op jit(solution)/shard_map/ppermute | solution.py:288
  68.3 1.6 %collective-permute-done.15 = f32[32,256]{1,0:T(8,128)S(1)} collective-permute-done((f32[32,256]{1,0:T(8,128)S(1)}, f32[32,256]{1,0:T(8,128)S(1)}, u32[]{:S(2)}, u32[]{:S(2)}) %collective-permute-start.15) | collective-permute-done | bytes 32800 | tf_op jit(solution)/shard_map/ppermute | solution.py:288
  69.9 2.4 %collective-permute-start.16 = (f32[32,256]{1,0:T(8,128)S(1)}, f32[32,256]{1,0:T(8,128)S(1)}, u32[]{:S(2)}, u32[]{:S(2)}) collective-permute-start(f32[32,256]{1,0:T(8,128)S(1)} %add.82), channel_id=1, source_target_pairs={{0,5},{1,4},{2,7},{3,6},{4,1},{5,0},{6,3},{7,2},{8,13},{9,12},{10,... | collective-permute-start | bytes 98312 | tf_op jit(solution)/shard_map/ppermute | solution.py:288
  72.4 1.6 %collective-permute-done.16 = f32[32,256]{1,0:T(8,128)S(1)} collective-permute-done((f32[32,256]{1,0:T(8,128)S(1)}, f32[32,256]{1,0:T(8,128)S(1)}, u32[]{:S(2)}, u32[]{:S(2)}) %collective-permute-start.16) | collective-permute-done | bytes 32800 | tf_op jit(solution)/shard_map/ppermute | solution.py:288
  74.0 1.4 %collective-permute-start.17 = (f32[32,256]{1,0:T(8,128)S(1)}, f32[32,256]{1,0:T(8,128)S(1)}, u32[]{:S(2)}, u32[]{:S(2)}) collective-permute-start(f32[32,256]{1,0:T(8,128)S(1)} %add.83), channel_id=1, source_target_pairs={{0,9},{1,8},{2,11},{3,10},{4,13},{5,12},{6,15},{7,14},{8,1},{9,0},... | collective-permute-start | bytes 98312 | tf_op jit(solution)/shard_map/ppermute | solution.py:288
  75.3 2.0 %collective-permute-done.17 = f32[32,256]{1,0:T(8,128)S(1)} collective-permute-done((f32[32,256]{1,0:T(8,128)S(1)}, f32[32,256]{1,0:T(8,128)S(1)}, u32[]{:S(2)}, u32[]{:S(2)}) %collective-permute-start.17) | collective-permute-done | bytes 32800 | tf_op jit(solution)/shard_map/ppermute | solution.py:288
  77.3 1.9 %collective-permute-start.18 = (f32[32,256]{1,0:T(8,128)S(1)}, f32[32,256]{1,0:T(8,128)S(1)}, u32[]{:S(2)}, u32[]{:S(2)}) collective-permute-start(f32[32,256]{1,0:T(8,128)S(1)} %add.84), channel_id=1, source_target_pairs={{0,17},{1,16},{2,19},{3,18},{4,21},{5,20},{6,23},{7,22},{8,25},{9,... | collective-permute-start | bytes 98312 | tf_op jit(solution)/shard_map/ppermute | solution.py:288
  79.2 2.3 %collective-permute-done.18 = f32[32,256]{1,0:T(8,128)S(1)} collective-permute-done((f32[32,256]{1,0:T(8,128)S(1)}, f32[32,256]{1,0:T(8,128)S(1)}, u32[]{:S(2)}, u32[]{:S(2)}) %collective-permute-start.18) | collective-permute-done | bytes 32800 | tf_op jit(solution)/shard_map/ppermute | solution.py:288
  81.6 0.2 collective-permute-start.19
  81.7 0.4 next_gram.1
  82.1 0.7 collective-permute-done.19
  82.8 4.2 %second_solve.1 = (bf16[64,2048]{1,0:T(8,128)(2,1)S(1)}, f32[2,64,192]{2,1,0:T(8,128)}, f32[2,64,64]{2,1,0:T(8,128)}) custom-call(f32[64,256]{1,0:T(8,128)S(1)} %pad_maximum_fusion.5.cross, bf16[192,192]{1,0:T(8,128)(2,1)S(1)} %get-tuple-element.39.own_high, bf16[192,192]{1,0:T(8,128)(2,1)S(1)} %get-tuple-element.40.own_low, ...), custom_call_target="tpu_custom_call" | custom-call | tf_op jit(solution)/shard_map/second_solve/pallas_call | solution.py:312
  86.9 0.7 copy.6
  (29 shorter events, 0.4 us)
Async XLA Ops:
  0.6 1.0 %slice-start = ((bf16[3,64,2,8,128]{4,3,2,1,0:T(8,128)(2,1)}), bf16[1,64,2,8,128]{4,3,2,1,0:T(8,128)(2,1)S(1)}, s32[]{:S(2)}) async-start(bf16[3,64,2,8,128]{4,3,2,1,0:T(8,128)(2,1)} %param.3), calls=%async_computation | async-start | bytes 524288 | tf_op jit(solution)/shard_map/slice | solution.py:340
  0.7 7.6 %copy-start.2 = (bf16[3,64,2,8,128]{4,3,2,1,0:T(8,128)(2,1)S(1)}, bf16[3,64,2,8,128]{4,3,2,1,0:T(8,128)(2,1)}, u32[]{:S(2)}) copy-start(bf16[3,64,2,8,128]{4,3,2,1,0:T(8,128)(2,1)} %param.3) | copy-start | bytes 2359300
  1.7 8.3 %collective-permute-start.1 = (bf16[64,1024]{1,0:T(8,128)(2,1)S(1)}, bf16[64,1024]{1,0:T(8,128)(2,1)S(1)}, u32[]{:S(2)}, u32[]{:S(2)}) collective-permute-start(bf16[64,1024]{1,0:T(8,128)(2,1)S(1)} %get-tuple-element.61), channel_id=1, source_target_pairs={{4,8},{12,16},{20,24},{8,4},{16,12},{24,20},{5,9},{13,17},{21,25},... | collective-permute-start | bytes 393224 | tf_op jit(solution)/shard_map/ppermute | solution.py:28
  2.4 10.6 %collective-permute-start = (bf16[64,1024]{1,0:T(8,128)(2,1)S(1)}, bf16[64,1024]{1,0:T(8,128)(2,1)S(1)}, u32[]{:S(2)}, u32[]{:S(2)}) collective-permute-start(bf16[64,1024]{1,0:T(8,128)(2,1)S(1)} %get-tuple-element.62), channel_id=1, source_target_pairs={{0,4},{8,12},{16,20},{24,28},{4,0},{12,8},{20,16},{28,24},{1,5},{9... | collective-permute-start | bytes 393224 | tf_op jit(solution)/shard_map/ppermute | solution.py:27
  8.6 0.7 copy-start
  8.6 0.7 copy-start.1
  13.1 3.6 %collective-permute-start.3 = (bf16[64,512]{1,0:T(8,128)(2,1)S(1)}, bf16[64,512]{1,0:T(8,128)(2,1)S(1)}, u32[]{:S(2)}, u32[]{:S(2)}) collective-permute-start(bf16[64,512]{1,0:T(8,128)(2,1)S(1)} %get-tuple-element.75), channel_id=1, source_target_pairs={{1,2},{2,1},{5,6},{6,5},{9,10},{10,9},{13,14},{14,13},{17,18},{18,... | collective-permute-start | bytes 196616 | tf_op jit(solution)/shard_map/ppermute | solution.py:28
  13.8 3.8 %collective-permute-start.2 = (bf16[64,512]{1,0:T(8,128)(2,1)S(1)}, bf16[64,512]{1,0:T(8,128)(2,1)S(1)}, u32[]{:S(2)}, u32[]{:S(2)}) collective-permute-start(bf16[64,512]{1,0:T(8,128)(2,1)S(1)} %get-tuple-element.76), channel_id=1, source_target_pairs={{0,1},{2,3},{1,0},{3,2},{4,5},{6,7},{5,4},{7,6},{8,9},{10,11},{9,8... | collective-permute-start | bytes 196616 | tf_op jit(solution)/shard_map/ppermute | solution.py:27
  19.2 2.1 %collective-permute-start.4 = (f32[32,640]{1,0:T(8,128)S(1)}, f32[32,640]{1,0:T(8,128)S(1)}, u32[]{:S(2)}, u32[]{:S(2)}) collective-permute-start(f32[32,640]{1,0:T(8,128)S(1)} %slice_select_fusion), channel_id=1, source_target_pairs={{0,1},{1,0},{2,3},{3,2},{4,5},{5,4},{6,7},{7,6},{8,9},{9,8},{10,11... | collective-permute-start | bytes 245768 | tf_op jit(solution)/shard_map/ppermute | solution.py:288
  21.3 4.3 %collective-permute-start.5 = (f32[32,640]{1,0:T(8,128)S(1)}, f32[32,640]{1,0:T(8,128)S(1)}, u32[]{:S(2)}, u32[]{:S(2)}) collective-permute-start(f32[32,640]{1,0:T(8,128)S(1)} %select_add_fusion), channel_id=1, source_target_pairs={{0,3},{1,2},{2,1},{3,0},{4,7},{5,6},{6,5},{7,4},{8,11},{9,10},{10,... | collective-permute-start | bytes 245768 | tf_op jit(solution)/shard_map/ppermute | solution.py:288
  25.6 5.1 %collective-permute-start.6 = (f32[32,640]{1,0:T(8,128)S(1)}, f32[32,640]{1,0:T(8,128)S(1)}, u32[]{:S(2)}, u32[]{:S(2)}) collective-permute-start(f32[32,640]{1,0:T(8,128)S(1)} %add.77), channel_id=1, source_target_pairs={{0,5},{1,4},{2,7},{3,6},{4,1},{5,0},{6,3},{7,2},{8,13},{9,12},{10,... | collective-permute-start | bytes 245768 | tf_op jit(solution)/shard_map/ppermute | solution.py:288
  30.8 4.5 %collective-permute-start.7 = (f32[32,640]{1,0:T(8,128)S(1)}, f32[32,640]{1,0:T(8,128)S(1)}, u32[]{:S(2)}, u32[]{:S(2)}) collective-permute-start(f32[32,640]{1,0:T(8,128)S(1)} %add.78), channel_id=1, source_target_pairs={{0,9},{1,8},{2,11},{3,10},{4,13},{5,12},{6,15},{7,14},{8,1},{9,0},... | collective-permute-start | bytes 245768 | tf_op jit(solution)/shard_map/ppermute | solution.py:288
  35.3 5.2 %collective-permute-start.8 = (f32[32,640]{1,0:T(8,128)S(1)}, f32[32,640]{1,0:T(8,128)S(1)}, u32[]{:S(2)}, u32[]{:S(2)}) collective-permute-start(f32[32,640]{1,0:T(8,128)S(1)} %add.79), channel_id=1, source_target_pairs={{0,17},{1,16},{2,19},{3,18},{4,21},{5,20},{6,23},{7,22},{8,25},{9,... | collective-permute-start | bytes 245768 | tf_op jit(solution)/shard_map/ppermute | solution.py:288
  40.5 3.0 %collective-permute-start.9 = (f32[32,640]{1,0:T(8,128)S(1)}, f32[32,640]{1,0:T(8,128)S(1)}, u32[]{:S(2)}, u32[]{:S(2)}) collective-permute-start(f32[32,640]{1,0:T(8,128)S(1)} %add.80), channel_id=1, source_target_pairs={{0,1},{1,0},{2,3},{3,2},{4,5},{5,4},{6,7},{7,6},{8,9},{9,8},{10,11... | collective-permute-start | bytes 245768 | tf_op jit(solution)/shard_map/ppermute | solution.py:288
  47.5 5.0 %collective-permute-start.11 = (bf16[64,1024]{1,0:T(8,128)(2,1)S(1)}, bf16[64,1024]{1,0:T(8,128)(2,1)S(1)}, u32[]{:S(2)}, u32[]{:S(2)}) collective-permute-start(bf16[64,1024]{1,0:T(8,128)(2,1)S(1)} %get-tuple-element.53), channel_id=1, source_target_pairs={{4,8},{12,16},{20,24},{8,4},{16,12},{24,20},{5,9},{13,17},{21,25},... | collective-permute-start | bytes 393224 | tf_op jit(solution)/shard_map/ppermute | solution.py:28
  48.1 9.9 %collective-permute-start.10 = (bf16[64,1024]{1,0:T(8,128)(2,1)S(1)}, bf16[64,1024]{1,0:T(8,128)(2,1)S(1)}, u32[]{:S(2)}, u32[]{:S(2)}) collective-permute-start(bf16[64,1024]{1,0:T(8,128)(2,1)S(1)} %get-tuple-element.54), channel_id=1, source_target_pairs={{0,4},{8,12},{16,20},{24,28},{4,0},{12,8},{20,16},{28,24},{1,5},{9... | collective-permute-start | bytes 393224 | tf_op jit(solution)/shard_map/ppermute | solution.py:27
  58.1 4.1 %collective-permute-start.13 = (bf16[64,512]{1,0:T(8,128)(2,1)S(1)}, bf16[64,512]{1,0:T(8,128)(2,1)S(1)}, u32[]{:S(2)}, u32[]{:S(2)}) collective-permute-start(bf16[64,512]{1,0:T(8,128)(2,1)S(1)} %get-tuple-element.67), channel_id=1, source_target_pairs={{1,2},{2,1},{5,6},{6,5},{9,10},{10,9},{13,14},{14,13},{17,18},{18,... | collective-permute-start | bytes 196616 | tf_op jit(solution)/shard_map/ppermute | solution.py:28
  58.8 4.3 %collective-permute-start.12 = (bf16[64,512]{1,0:T(8,128)(2,1)S(1)}, bf16[64,512]{1,0:T(8,128)(2,1)S(1)}, u32[]{:S(2)}, u32[]{:S(2)}) collective-permute-start(bf16[64,512]{1,0:T(8,128)(2,1)S(1)} %get-tuple-element.68), channel_id=1, source_target_pairs={{0,1},{2,3},{1,0},{3,2},{4,5},{6,7},{5,4},{7,6},{8,9},{10,11},{9,8... | collective-permute-start | bytes 196616 | tf_op jit(solution)/shard_map/ppermute | solution.py:27
  64.7 1.9 %collective-permute-start.14 = (f32[32,256]{1,0:T(8,128)S(1)}, f32[32,256]{1,0:T(8,128)S(1)}, u32[]{:S(2)}, u32[]{:S(2)}) collective-permute-start(f32[32,256]{1,0:T(8,128)S(1)} %slice_select_fusion.1), channel_id=1, source_target_pairs={{0,1},{1,0},{2,3},{3,2},{4,5},{5,4},{6,7},{7,6},{8,9},{9,8},{10,11... | collective-permute-start | bytes 98312 | tf_op jit(solution)/shard_map/ppermute | solution.py:288
  66.6 3.3 %collective-permute-start.15 = (f32[32,256]{1,0:T(8,128)S(1)}, f32[32,256]{1,0:T(8,128)S(1)}, u32[]{:S(2)}, u32[]{:S(2)}) collective-permute-start(f32[32,256]{1,0:T(8,128)S(1)} %select_add_fusion.1), channel_id=1, source_target_pairs={{0,3},{1,2},{2,1},{3,0},{4,7},{5,6},{6,5},{7,4},{8,11},{9,10},{10,... | collective-permute-start | bytes 98312 | tf_op jit(solution)/shard_map/ppermute | solution.py:288
  69.9 4.0 %collective-permute-start.16 = (f32[32,256]{1,0:T(8,128)S(1)}, f32[32,256]{1,0:T(8,128)S(1)}, u32[]{:S(2)}, u32[]{:S(2)}) collective-permute-start(f32[32,256]{1,0:T(8,128)S(1)} %add.82), channel_id=1, source_target_pairs={{0,5},{1,4},{2,7},{3,6},{4,1},{5,0},{6,3},{7,2},{8,13},{9,12},{10,... | collective-permute-start | bytes 98312 | tf_op jit(solution)/shard_map/ppermute | solution.py:288
  74.0 3.3 %collective-permute-start.17 = (f32[32,256]{1,0:T(8,128)S(1)}, f32[32,256]{1,0:T(8,128)S(1)}, u32[]{:S(2)}, u32[]{:S(2)}) collective-permute-start(f32[32,256]{1,0:T(8,128)S(1)} %add.83), channel_id=1, source_target_pairs={{0,9},{1,8},{2,11},{3,10},{4,13},{5,12},{6,15},{7,14},{8,1},{9,0},... | collective-permute-start | bytes 98312 | tf_op jit(solution)/shard_map/ppermute | solution.py:288
  77.3 4.2 %collective-permute-start.18 = (f32[32,256]{1,0:T(8,128)S(1)}, f32[32,256]{1,0:T(8,128)S(1)}, u32[]{:S(2)}, u32[]{:S(2)}) collective-permute-start(f32[32,256]{1,0:T(8,128)S(1)} %add.84), channel_id=1, source_target_pairs={{0,17},{1,16},{2,19},{3,18},{4,21},{5,20},{6,23},{7,22},{8,25},{9,... | collective-permute-start | bytes 98312 | tf_op jit(solution)/shard_map/ppermute | solution.py:288
  81.6 1.2 %collective-permute-start.19 = (f32[32,256]{1,0:T(8,128)S(1)}, f32[32,256]{1,0:T(8,128)S(1)}, u32[]{:S(2)}, u32[]{:S(2)}) collective-permute-start(f32[32,256]{1,0:T(8,128)S(1)} %add.85), channel_id=1, source_target_pairs={{0,1},{1,0},{2,3},{3,2},{4,5},{5,4},{6,7},{7,6},{8,9},{9,8},{10,11... | collective-permute-start | bytes 98312 | tf_op jit(solution)/shard_map/ppermute | solution.py:288

commit v10 on v9

--- a/solution.py
+++ b/solution.py
@@ -19,16 +19,22 @@
 def neighbours(block, span_x, span_y, depth, meanwhile=()):
     plane = span_y * depth
 
-    def exchange(axis, upward, downward):
+    def exchange(axis, upward, downward, closed):
         count = lax.axis_size(axis)
-        odd = lax.axis_index(axis) % 2 == 1
-        pairs = [[(i, i + 1) for i in range(first, count - 1, 2)] for first in (0, 1)]
-        swaps = [pair + [(b, a) for a, b in pair] for pair in pairs]
-        inner = lax.ppermute(jnp.where(odd, downward, upward), axis, swaps[0])
-        outer = lax.ppermute(jnp.where(odd, upward, downward), axis, swaps[1])
+        me = lax.axis_index(axis)
+        odd = me % 2 == 1
+        pairs = [(i, (i - 1 ^ 1) + 1) for i in range(1, count - 1)]
+        if closed:
+            pairs += [(0, count - 1), (count - 1, 0)]
+        outer = lax.ppermute(jnp.where(odd, upward, downward), axis, pairs)
+        inner = lax.ppermute(
+            jnp.where(odd, downward, upward), axis, [(i, i ^ 1) for i in range(count)]
+        )
+        if closed:
+            outer = jnp.where((me == 0) | (me == count - 1), 0, outer)
         return jnp.where(odd, inner, outer), jnp.where(odd, outer, inner)
 
-    xlo, xhi = exchange("slab", block[:, (span_x - 1) * plane :], block[:, :plane])
+    xlo, xhi = exchange("slab", block[:, (span_x - 1) * plane :], block[:, :plane], False)
 
     xlo, xhi, meanwhile = lax.optimization_barrier((xlo, xhi, meanwhile))
 
@@ -39,7 +45,7 @@
         parts += [xhi[:, at : at + depth]]
         return jnp.concatenate(parts, axis=1)
 
-    ylo, yhi = exchange("col", edge(span_y - 1), edge(0))
+    ylo, yhi = exchange("col", edge(span_y - 1), edge(0), True)
     return (xlo, xhi, ylo, yhi), meanwhile
 
 
@@ -80,43 +86,71 @@
     )(table, cell_map.reshape(lines, depth))
 
 
-def stencil_into(image, coef, block, xlo, xhi, ylo, yhi, span_x, span_y, depth):
-    columns = block.shape[0]
+def stencil(coef, spans, columns, line, inner, write):
+    span_x, span_y, depth = spans
 
     def tile(step, carry):
         rows = pl.ds(pl.multiple_of(step * ROWS, ROWS), ROWS)
-
-        def line(x, y):
-            if y < 0:
-                ref, at = ylo, x + 1
-            elif y >= span_y:
-                ref, at = yhi, x + 1
-            elif x < 0:
-                ref, at = xlo, y
-            elif x >= span_x:
-                ref, at = xhi, y
-            else:
-                ref, at = block, x * span_y + y
-            return ref[rows, at * depth : (at + 1) * depth].astype(jnp.float32)
-
-        held = {y: [line(x, y) for x in range(-1, span_x + 1)] for y in (-1, 0)}
+        held = {}
         for y in range(span_y):
-            held[y + 1] = [line(x, y + 1) for x in range(-1, span_x + 1)]
             for x in range(span_x):
-                at = x * span_y + y
                 sums = [None, None, None]
-                for dx in range(3):
-                    for dy in range(3):
-                        field = held[y + dy - 1][x + dx]
-                        for dz in range(3):
-                            term = coef[9 * dx + 3 * dy + dz, at : at + 1, :] * field
-                            sums[dz] = term if sums[dz] is None else sums[dz] + term
-                total = sums[1] + pltpu.roll(sums[0], 1, 1) + pltpu.roll(sums[2], depth - 1, 1)
-                image[rows, at * depth : (at + 1) * depth] = total.astype(jnp.bfloat16)
-            del held[y - 1]
+                for pair in range(9):
+                    x_there, y_there = x + pair // 3 - 1, y + pair % 3 - 1
+                    inside = 0 <= x_there < span_x and 0 <= y_there < span_y
+                    if inside != inner:
+                        continue
+                    if (x_there, y_there) not in held:
+                        held[x_there, y_there] = line(rows, x_there, y_there)
+                    for dz in range(3):
+                        at = x * span_y + y
+                        term = coef[3 * pair + dz, at : at + 1, :] * held[x_there, y_there]
+                        sums[dz] = term if sums[dz] is None else sums[dz] + term
+                total = None
+                if sums[0] is not None:
+                    total = pltpu.roll(sums[0], 1, 1) + pltpu.roll(sums[2], depth - 1, 1)
+                    total = sums[1] + total
+                write(rows, x, y, total)
         return carry
 
     lax.fori_loop(0, columns // ROWS, tile, 0)
+
+
+def inner_image_kernel(spans, coef, fields, partial):
+    _, span_y, depth = spans
+    columns = partial.shape[0]
+    block = fields.at[fields.shape[0] - columns :]
+
+    def here(x, y):
+        return pl.ds((x * span_y + y) * depth, depth)
+
+    def write(rows, x, y, total):
+        partial[rows, here(x, y)] = total
+
+    def line(rows, x, y):
+        return block[rows, here(x, y)].astype(jnp.float32)
+
+    stencil(coef, spans, columns, line, True, write)
+
+
+def complete(image, partial, coef, spans, xlo, xhi, ylo, yhi):
+    span_x, span_y, depth = spans
+
+    def line(rows, x, y):
+        if y < 0:
+            ref, at = ylo, x + 1
+        elif y >= span_y:
+            ref, at = yhi, x + 1
+        else:
+            ref, at = (xlo, y) if x < 0 else (xhi, y)
+        return ref[rows, at * depth : (at + 1) * depth].astype(jnp.float32)
+
+    def write(rows, x, y, total):
+        there = pl.ds((x * span_y + y) * depth, depth)
+        known = partial[rows, there]
+        image[rows, there] = (known if total is None else known + total).astype(jnp.bfloat16)
+
+    stencil(coef, spans, image.shape[0], line, False, write)
 
 
 def stack_gram_kernel(columns, stack, own):
@@ -127,21 +161,20 @@
         at += width
 
 
-def first_image_kernel(spans, coef, stack, own, xlo, xhi, ylo, yhi, image, cross):
+def first_image_kernel(spans, coef, stack, own, partial, xlo, xhi, ylo, yhi, image, cross):
     columns = image.shape[0]
     fields = stack.shape[0]
-    block = stack.at[fields - columns : fields]
-    stencil_into(image, coef, block, xlo, xhi, ylo, yhi, *spans)
+    complete(image, partial, coef, spans, xlo, xhi, ylo, yhi)
     w = image[...]
     cross[:, :fields] = dot(w, stack[...], NT)
     cross[:, fields : fields + columns] = dot(w, w, NT)
     cross[:, fields + columns :] = own[...]
 
 
-def second_image_kernel(spans, coef, stack, block, xlo, xhi, ylo, yhi, image, cross):
+def second_image_kernel(spans, coef, stack, block, partial, xlo, xhi, ylo, yhi, image, cross):
     columns = image.shape[0]
     fields = stack.shape[0]
-    stencil_into(image, coef, block, xlo, xhi, ylo, yhi, *spans)
+    complete(image, partial, coef, spans, xlo, xhi, ylo, yhi)
     w = image[...]
     cross[:, : fields - columns] = dot(w, stack[columns:], NT)
     cross[:, fields - columns : fields] = dot(w, block[...], NT)
@@ -239,7 +272,8 @@
         cross[:, : fields + columns], split(gram), scale
     )
     square[...] = square_here
-    w = image[...].astype(jnp.float32) - dots(used, (stack[...],))
+    moved = dot(jnp.concatenate(used, axis=0), stack[...])
+    w = image[...].astype(jnp.float32) - moved[:columns] - moved[columns:]
     block[...] = w.astype(jnp.bfloat16)
     upper, inverse_here = factor(square_here)
     low[...] = upper.T
@@ -273,9 +307,9 @@
     used, proj[1], _, square = project(cross[...], (own_high[...], own_low[...]), scale)
     proj[0] = proj_in[...]
     low[0] = low_in[...]
-    w = image[...].astype(jnp.float32)
-    w = w - dots([part[:, :kept] for part in used], (stack[columns:],))
-    w = w - dots([part[:, kept:] for part in used], (last[...],))
+    both = jnp.concatenate(used, axis=0)
+    moved = dot(both[:, :kept], stack[columns:]) + dot(both[:, kept:], last[...])
+    w = image[...].astype(jnp.float32) - moved[:columns] - moved[columns:]
     block[...] = w.astype(jnp.bfloat16)
     upper, inverse = factor(square)
     low[1] = upper.T
@@ -302,8 +336,12 @@
     part = jnp.where(upper, high, low) + partner(jnp.where(upper, low, high), 1)
     bit = 2
     while bit < count:
-        part = part + partner(part, bit + 1)
-        bit *= 2
+        if 2 * bit < count:
+            one, two, both = (partner(part, mask) for mask in (bit + 1, 2 * bit + 1, 3 * bit))
+            part = (part + one) + (two + both)
+        else:
+            part = part + partner(part, bit + 1)
+        bit *= 4
     other = partner(part, 1)
     return jnp.concatenate([jnp.where(upper, other, part), jnp.where(upper, part, other)], axis=0)
 
@@ -336,15 +374,22 @@
         [((columns, columns * blocks * (blocks + 1) // 2), f32)],
         stack,
     )
-    around, (coef, stack, own) = neighbours(
-        basis[blocks - 1].reshape(columns, cells), *spans, (coef, stack, own)
+    inner_image = functools.partial(
+        call,
+        functools.partial(inner_image_kernel, spans),
+        "inner_image",
+        [((columns, cells), f32)],
+        coef,
+    )
+    around, (coef, stack, own, partial) = neighbours(
+        basis[blocks - 1].reshape(columns, cells), *spans, (coef, stack, own, *inner_image(stack))
     )
     packed = fields + columns + own.shape[1]
     image, cross = call(
         functools.partial(first_image_kernel, spans),
         "first_image",
         [((columns, cells), bf16), ((columns, packed), f32)],
-        coef, stack, own, *around,
+        coef, stack, own, partial, *around,
     )
     cross = whole_sum(cross)
     block, proj, low, rest, square, inverse = call(
@@ -360,12 +405,12 @@
         [((fields, fields), bf16)] * 2,
         cross, rest, square, inverse,
     )
-    around, _ = neighbours(block, *spans)
+    around, (partial,) = neighbours(block, *spans, tuple(inner_image(block)))
     image, cross = call(
         functools.partial(second_image_kernel, spans),
         "second_image",
         [((columns, cells), bf16), ((columns, fields + columns), f32)],
-        coef, stack, block, *around,
+        coef, stack, block, partial, *around,
     )
     block, proj, low = call(
         functools.partial(second_solve_kernel, scale),

time: 88.2 us -> 81.8 us (0.927)
  starting transfers between devices: 39.6 us -> 30.6 us
  waiting for transfers between devices: 31.9 us -> 34.1 us
    ppermute x8, starting transfers between devices: 19.1 us -> 13.9 us  [the longest x4 10.8 us: exchange(): lax.ppermute(jnp.where(odd, downward, upward), axis, [(i, i ^ 1) for i in...]
    ppermute x12 -> x16, starting transfers between devices: 20.4 us -> 16.7 us  [partner(): return lax.ppermute(part, axes, [(i, i ^ mask) for i in range(count)])]
    ppermute x8, waiting for transfers between devices: 10.4 us -> 13.8 us  [the longest x4 8.08 us: exchange(): lax.ppermute(jnp.where(odd, downward, upward), axis, [(i, i ^ 1) for i in...]
    ppermute x12 -> x16, waiting for transfers between devices: 21.5 us -> 20.3 us  [partner(): return lax.ppermute(part, axes, [(i, i ^ mask) for i in range(count)])]
    pallas_call x6 -> x8, Pallas kernels: 12 us -> 12.6 us  [call(): pl.pallas_call(kernel, out_shape=[jax.ShapeDtypeStruct(shape, dtype) for...]
  transfers between devices with their start and end apart: 20 -> 24, of which waited for: 16 -> 17; matrix products, arithmetic and copies ran while one was open for 0% -> 0% of each run, Pallas kernels for 2% -> 3%
where the time goes in v10:
time: 81.8 us; the launch traced here: 81.5 us
  waiting for transfers between devices  34.1 us (42%)
  starting transfers between devices  30.6 us (37%)
  Pallas kernels  13.3 us (16%)
  local copies, waits for them, and re-layouts  2.25 us (3%)
  between operations  0.91 us (1%)
    ppermute x16, waiting for transfers between devices, partner(): return lax.ppermute(part, axes, [(i, i ^ mask) for i in range(count)])  20.3 us
    ppermute x16, starting transfers between devices, partner(): return lax.ppermute(part, axes, [(i, i ^ mask) for i in range(count)])  16.7 us
    pallas_call x8, Pallas kernels, call(): pl.pallas_call(kernel, out_shape=[jax.ShapeDtypeStruct(shape, dtype) for...  12.6 us
    ppermute x4, starting transfers between devices, exchange(): lax.ppermute(jnp.where(odd, downward, upward), axis, [(i, i ^ 1) for i in...  10.8 us
    ppermute x4, waiting for transfers between devices, exchange(): lax.ppermute(jnp.where(odd, downward, upward), axis, [(i, i ^ 1) for i in...  8.08 us
    ppermute x4, waiting for transfers between devices, exchange(): outer = lax.ppermute(jnp.where(odd, upward, downward), axis, pairs)  5.69 us
    ppermute x4, starting transfers between devices, exchange(): outer = lax.ppermute(jnp.where(odd, upward, downward), axis, pairs)  3.08 us
  transfers between devices with their start and end apart: 24, of which 17 were waited for; matrix products, arithmetic and copies ran while one was open for 0% of the time, Pallas kernels for 3%

profile of v10, /device:TPU:0, one launch (start us, length us, event | category | flops | bytes accessed | tf_op | source)
XLA Modules:
  0.0 81.5 jit_solution(8502720239928910780)
XLA Ops:
  0.6 0.0 slice-start
  0.7 0.9 %slice-done = bf16[1,64,2,8,128]{4,3,2,1,0:T(8,128)(2,1)S(1)} async-done(((bf16[3,64,2,8,128]{4,3,2,1,0:T(8,128)(2,1)}), bf16[1,64,2,8,128]{4,3,2,1,0:T(8,128)(2,1)S(1)}, s32[]{:S(2)}) %slice-start) | async-done | bytes 262168 | tf_op jit(solution)/shard_map/slice | solution.py:385
  1.6 0.1 reshape_squeeze.3
  1.7 0.7 collective-permute-start.1
  2.4 5.8 %collective-permute-start = (bf16[64,1024]{1,0:T(8,128)(2,1)S(1)}, bf16[64,1024]{1,0:T(8,128)(2,1)S(1)}, u32[]{:S(2)}, u32[]{:S(2)}) collective-permute-start(bf16[64,1024]{1,0:T(8,128)(2,1)S(1)} %get-tuple-element.66), channel_id=1, source_target_pairs={{0,4},{4,0},{8,12},{12,8},{16,20},{20,16},{24,28},{28,24},{1,5},{5... | collective-permute-start | bytes 393224 | tf_op jit(solution)/shard_map/ppermute | solution.py:30
  8.2 0.3 reshape.16.stack.fields
  8.6 0.0 copy-start
  8.6 0.0 copy-start.1
  8.6 0.6 stack_gram.1.own
  9.2 0.0 copy-done
  9.3 0.0 copy-done.1
  9.3 0.8 coefficients.1.coef
  10.0 0.7 inner_image.2.partial
  10.7 0.0 collective-permute-done.1
  10.7 2.3 %collective-permute-done = bf16[64,1024]{1,0:T(8,128)(2,1)S(1)} collective-permute-done((bf16[64,1024]{1,0:T(8,128)(2,1)S(1)}, bf16[64,1024]{1,0:T(8,128)(2,1)S(1)}, u32[]{:S(2)}, u32[]{:S(2)}) %collective-permute-start) | collective-permute-done | bytes 131104 | tf_op jit(solution)/shard_map/ppermute | solution.py:30
  13.1 1.2 %collective-permute-start.3 = (bf16[64,512]{1,0:T(8,128)(2,1)S(1)}, bf16[64,512]{1,0:T(8,128)(2,1)S(1)}, u32[]{:S(2)}, u32[]{:S(2)}) collective-permute-start(bf16[64,512]{1,0:T(8,128)(2,1)S(1)} %get-tuple-element.79), channel_id=1, source_target_pairs={{1,2},{2,1},{0,3},{3,0},{5,6},{6,5},{4,7},{7,4},{9,10},{10,9},{8,1... | collective-permute-start | bytes 196616 | tf_op jit(solution)/shard_map/ppermute | solution.py:29
  14.3 0.5 collective-permute-start.2
  14.8 2.6 %collective-permute-done.3 = bf16[64,512]{1,0:T(8,128)(2,1)S(1)} collective-permute-done((bf16[64,512]{1,0:T(8,128)(2,1)S(1)}, bf16[64,512]{1,0:T(8,128)(2,1)S(1)}, u32[]{:S(2)}, u32[]{:S(2)}) %collective-permute-start.3) | collective-permute-done | bytes 65568 | tf_op jit(solution)/shard_map/ppermute | solution.py:29
  17.4 0.0 collective-permute-done.2
  17.4 1.1 %first_image.1 = (bf16[64,2048]{1,0:T(8,128)(2,1)S(1)}, f32[64,640]{1,0:T(8,128)S(1)}) custom-call(f32[27,16,128]{2,1,0:T(8,128)S(1)} %coefficients.1.coef, bf16[192,2048]{1,0:T(8,128)(2,1)S(1)} %reshape.16.stack.fields, f32[64,384]{1,0:T(8,128)S(1)} %stack_gram.1.own, f32[64,2048]{1,0:T(8,128)S(1)} %inner_image.2.partial, ...), custom_call_target="tpu_custom_call" | custom-call | tf_op jit(solution)/shard_map/first_image/pallas_call | solution.py:350
  18.5 0.2 collective-permute-start.4
  18.7 1.2 %collective-permute-done.4 = f32[32,640]{1,0:T(8,128)S(1)} collective-permute-done((f32[32,640]{1,0:T(8,128)S(1)}, f32[32,640]{1,0:T(8,128)S(1)}, u32[]{:S(2)}, u32[]{:S(2)}) %collective-permute-start.4) | collective-permute-done | bytes 81952 | tf_op jit(solution)/shard_map/ppermute | solution.py:322
  19.9 3.5 %collective-permute-start.7 = (f32[32,640]{1,0:T(8,128)S(1)}, f32[32,640]{1,0:T(8,128)S(1)}, u32[]{:S(2)}, u32[]{:S(2)}) collective-permute-start(f32[32,640]{1,0:T(8,128)S(1)} %select_add_fusion), channel_id=1, source_target_pairs={{0,6},{1,7},{2,4},{3,5},{4,2},{5,3},{6,0},{7,1},{8,14},{9,15},{10,... | collective-permute-start | bytes 245768 | tf_op jit(solution)/shard_map/ppermute | solution.py:322
  23.4 0.0 collective-permute-start.6
  23.4 0.4 collective-permute-start.5
  23.8 2.4 %collective-permute-done.7 = f32[32,640]{1,0:T(8,128)S(1)} collective-permute-done((f32[32,640]{1,0:T(8,128)S(1)}, f32[32,640]{1,0:T(8,128)S(1)}, u32[]{:S(2)}, u32[]{:S(2)}) %collective-permute-start.7) | collective-permute-done | bytes 81952 | tf_op jit(solution)/shard_map/ppermute | solution.py:322
  26.2 1.9 %collective-permute-done.6 = f32[32,640]{1,0:T(8,128)S(1)} collective-permute-done((f32[32,640]{1,0:T(8,128)S(1)}, f32[32,640]{1,0:T(8,128)S(1)}, u32[]{:S(2)}, u32[]{:S(2)}) %collective-permute-start.6) | collective-permute-done | bytes 81952 | tf_op jit(solution)/shard_map/ppermute | solution.py:322
  28.1 0.0 collective-permute-done.5
  28.1 3.7 %collective-permute-start.10 = (f32[32,640]{1,0:T(8,128)S(1)}, f32[32,640]{1,0:T(8,128)S(1)}, u32[]{:S(2)}, u32[]{:S(2)}) collective-permute-start(f32[32,640]{1,0:T(8,128)S(1)} %add_add_fusion.1), channel_id=1, source_target_pairs={{0,24},{1,25},{2,26},{3,27},{4,28},{5,29},{6,30},{7,31},{8,16},{9,... | collective-permute-start | bytes 245768 | tf_op jit(solution)/shard_map/ppermute | solution.py:322
  31.8 0.0 collective-permute-start.9
  31.8 0.5 collective-permute-start.8
  32.3 2.4 %collective-permute-done.10 = f32[32,640]{1,0:T(8,128)S(1)} collective-permute-done((f32[32,640]{1,0:T(8,128)S(1)}, f32[32,640]{1,0:T(8,128)S(1)}, u32[]{:S(2)}, u32[]{:S(2)}) %collective-permute-start.10) | collective-permute-done | bytes 81952 | tf_op jit(solution)/shard_map/ppermute | solution.py:322
  34.8 3.5 %collective-permute-done.9 = f32[32,640]{1,0:T(8,128)S(1)} collective-permute-done((f32[32,640]{1,0:T(8,128)S(1)}, f32[32,640]{1,0:T(8,128)S(1)}, u32[]{:S(2)}, u32[]{:S(2)}) %collective-permute-start.9) | collective-permute-done | bytes 81952 | tf_op jit(solution)/shard_map/ppermute | solution.py:322
  38.3 0.0 collective-permute-done.8
  38.3 0.6 collective-permute-start.11
  38.9 0.9 %collective-permute-done.11 = f32[32,640]{1,0:T(8,128)S(1)} collective-permute-done((f32[32,640]{1,0:T(8,128)S(1)}, f32[32,640]{1,0:T(8,128)S(1)}, u32[]{:S(2)}, u32[]{:S(2)}) %collective-permute-start.11) | collective-permute-done | bytes 81952 | tf_op jit(solution)/shard_map/ppermute | solution.py:322
  39.8 3.8 %first_solve.1 = (bf16[64,2048]{1,0:T(8,128)(2,1)S(1)}, f32[64,192]{1,0:T(8,128)S(1)}, f32[64,64]{1,0:T(8,128)S(1)}, f32[64,192]{1,0:T(8,128)S(1)}, f32[64,64]{1,0:T(8,128)S(1)}, /*index=5*/bf16[64,64]{1,0:T(8,128)(2,1)S(1)}) custom-call(f32[64,640]{1,0:T(8,128)S(1)} %pad_maximum_fusion.cross, bf16[192,2048]{1,0:T(8,128)(2,1)S(1)} %reshape.16.stack.fields, ...), custom_call_target="tpu_custom_call" | custom-call | tf_op jit(solution)/shard_map/first_solve/pallas_call | solution.py:350
  43.7 0.7 inner_image.3.partial
  44.4 0.7 collective-permute-start.13
  45.0 3.8 %collective-permute-start.12 = (bf16[64,1024]{1,0:T(8,128)(2,1)S(1)}, bf16[64,1024]{1,0:T(8,128)(2,1)S(1)}, u32[]{:S(2)}, u32[]{:S(2)}) collective-permute-start(bf16[64,1024]{1,0:T(8,128)(2,1)S(1)} %get-tuple-element.58), channel_id=1, source_target_pairs={{0,4},{4,0},{8,12},{12,8},{16,20},{20,16},{24,28},{28,24},{1,5},{5... | collective-permute-start | bytes 393224 | tf_op jit(solution)/shard_map/ppermute | solution.py:30
  48.8 5.8 %collective-permute-done.12 = bf16[64,1024]{1,0:T(8,128)(2,1)S(1)} collective-permute-done((bf16[64,1024]{1,0:T(8,128)(2,1)S(1)}, bf16[64,1024]{1,0:T(8,128)(2,1)S(1)}, u32[]{:S(2)}, u32[]{:S(2)}) %collective-permute-start.12) | collective-permute-done | bytes 131104 | tf_op jit(solution)/shard_map/ppermute | solution.py:30
  54.7 0.5 collective-permute-start.15
  55.2 0.7 collective-permute-start.14
  56.0 3.1 %collective-permute-done.15 = bf16[64,512]{1,0:T(8,128)(2,1)S(1)} collective-permute-done((bf16[64,512]{1,0:T(8,128)(2,1)S(1)}, bf16[64,512]{1,0:T(8,128)(2,1)S(1)}, u32[]{:S(2)}, u32[]{:S(2)}) %collective-permute-start.15) | collective-permute-done | bytes 65568 | tf_op jit(solution)/shard_map/ppermute | solution.py:29
  59.1 0.0 collective-permute-done.14
  59.1 1.1 %second_image.1 = (bf16[64,2048]{1,0:T(8,128)(2,1)S(1)}, f32[64,256]{1,0:T(8,128)S(1)}) custom-call(f32[27,16,128]{2,1,0:T(8,128)S(1)} %coefficients.1.coef, bf16[192,2048]{1,0:T(8,128)(2,1)S(1)} %reshape.16.stack.fields, bf16[64,2048]{1,0:T(8,128)(2,1)S(1)} %get-tuple-element.35.fields.block.last, f32[64,2048]{1,0:T(8,128)S(1)} %inner_image.3.partial, ...), custom_call_target="tpu_custom_call" | custom-call | tf_op jit(solution)/shard_map/second_image/pallas_call | solution.py:350
  60.2 0.1 collective-permute-start.16
  60.4 1.1 %collective-permute-done.16 = f32[32,256]{1,0:T(8,128)S(1)} collective-permute-done((f32[32,256]{1,0:T(8,128)S(1)}, f32[32,256]{1,0:T(8,128)S(1)}, u32[]{:S(2)}, u32[]{:S(2)}) %collective-permute-start.16) | collective-permute-done | bytes 32800 | tf_op jit(solution)/shard_map/ppermute | solution.py:322
  61.5 3.0 %collective-permute-start.19 = (f32[32,256]{1,0:T(8,128)S(1)}, f32[32,256]{1,0:T(8,128)S(1)}, u32[]{:S(2)}, u32[]{:S(2)}) collective-permute-start(f32[32,256]{1,0:T(8,128)S(1)} %select_add_fusion.1), channel_id=1, source_target_pairs={{0,6},{1,7},{2,4},{3,5},{4,2},{5,3},{6,0},{7,1},{8,14},{9,15},{10,... | collective-permute-start | bytes 98312 | tf_op jit(solution)/shard_map/ppermute | solution.py:322
  64.5 0.0 collective-permute-start.18
  64.5 0.4 collective-permute-start.17
  64.9 1.5 %collective-permute-done.19 = f32[32,256]{1,0:T(8,128)S(1)} collective-permute-done((f32[32,256]{1,0:T(8,128)S(1)}, f32[32,256]{1,0:T(8,128)S(1)}, u32[]{:S(2)}, u32[]{:S(2)}) %collective-permute-start.19) | collective-permute-done | bytes 32800 | tf_op jit(solution)/shard_map/ppermute | solution.py:322
  66.4 1.7 %collective-permute-done.18 = f32[32,256]{1,0:T(8,128)S(1)} collective-permute-done((f32[32,256]{1,0:T(8,128)S(1)}, f32[32,256]{1,0:T(8,128)S(1)}, u32[]{:S(2)}, u32[]{:S(2)}) %collective-permute-start.18) | collective-permute-done | bytes 32800 | tf_op jit(solution)/shard_map/ppermute | solution.py:322
  68.2 2.0 %collective-permute-start.22 = (f32[32,256]{1,0:T(8,128)S(1)}, f32[32,256]{1,0:T(8,128)S(1)}, u32[]{:S(2)}, u32[]{:S(2)}) collective-permute-start(f32[32,256]{1,0:T(8,128)S(1)} %add_add_fusion.3), channel_id=1, source_target_pairs={{0,24},{1,25},{2,26},{3,27},{4,28},{5,29},{6,30},{7,31},{8,16},{9,... | collective-permute-start | bytes 98312 | tf_op jit(solution)/shard_map/ppermute | solution.py:322
  70.2 0.2 collective-permute-start.21
  70.3 2.0 %collective-permute-start.20 = (f32[32,256]{1,0:T(8,128)S(1)}, f32[32,256]{1,0:T(8,128)S(1)}, u32[]{:S(2)}, u32[]{:S(2)}) collective-permute-start(f32[32,256]{1,0:T(8,128)S(1)} %add_add_fusion.3), channel_id=1, source_target_pairs={{0,9},{1,8},{2,11},{3,10},{4,13},{5,12},{6,15},{7,14},{8,1},{9,0},... | collective-permute-start | bytes 98312 | tf_op jit(solution)/shard_map/ppermute | solution.py:322
  72.3 1.7 %collective-permute-done.22 = f32[32,256]{1,0:T(8,128)S(1)} collective-permute-done((f32[32,256]{1,0:T(8,128)S(1)}, f32[32,256]{1,0:T(8,128)S(1)}, u32[]{:S(2)}, u32[]{:S(2)}) %collective-permute-start.22) | collective-permute-done | bytes 32800 | tf_op jit(solution)/shard_map/ppermute | solution.py:322
  74.1 1.0 %collective-permute-done.21 = f32[32,256]{1,0:T(8,128)S(1)} collective-permute-done((f32[32,256]{1,0:T(8,128)S(1)}, f32[32,256]{1,0:T(8,128)S(1)}, u32[]{:S(2)}, u32[]{:S(2)}) %collective-permute-start.21) | collective-permute-done | bytes 32800 | tf_op jit(solution)/shard_map/ppermute | solution.py:322
  75.0 0.2 collective-permute-done.20
  75.2 0.2 collective-permute-start.23
  75.4 0.4 next_gram.1
  75.8 0.7 collective-permute-done.23
  76.5 4.2 %second_solve.1 = (bf16[64,2048]{1,0:T(8,128)(2,1)S(1)}, f32[2,64,192]{2,1,0:T(8,128)}, f32[2,64,64]{2,1,0:T(8,128)}) custom-call(f32[64,256]{1,0:T(8,128)S(1)} %pad_maximum_fusion.5.cross, bf16[192,192]{1,0:T(8,128)(2,1)S(1)} %get-tuple-element.43.own_high, bf16[192,192]{1,0:T(8,128)(2,1)S(1)} %get-tuple-element.44.own_low, ...), custom_call_target="tpu_custom_call" | custom-call | tf_op jit(solution)/shard_map/second_solve/pallas_call | solution.py:350
  80.8 0.7 copy.6
  (29 shorter events, 0.4 us)
Async XLA Ops:
  0.6 1.0 %slice-start = ((bf16[3,64,2,8,128]{4,3,2,1,0:T(8,128)(2,1)}), bf16[1,64,2,8,128]{4,3,2,1,0:T(8,128)(2,1)S(1)}, s32[]{:S(2)}) async-start(bf16[3,64,2,8,128]{4,3,2,1,0:T(8,128)(2,1)} %param.3), calls=%async_computation | async-start | bytes 524288 | tf_op jit(solution)/shard_map/slice | solution.py:385
  0.7 7.6 %copy-start.2 = (bf16[3,64,2,8,128]{4,3,2,1,0:T(8,128)(2,1)S(1)}, bf16[3,64,2,8,128]{4,3,2,1,0:T(8,128)(2,1)}, u32[]{:S(2)}) copy-start(bf16[3,64,2,8,128]{4,3,2,1,0:T(8,128)(2,1)} %param.3) | copy-start | bytes 2359300
  1.7 9.0 %collective-permute-start.1 = (bf16[64,1024]{1,0:T(8,128)(2,1)S(1)}, bf16[64,1024]{1,0:T(8,128)(2,1)S(1)}, u32[]{:S(2)}, u32[]{:S(2)}) collective-permute-start(bf16[64,1024]{1,0:T(8,128)(2,1)S(1)} %get-tuple-element.65), channel_id=1, source_target_pairs={{4,8},{8,4},{12,16},{16,12},{20,24},{24,20},{5,9},{9,5},{13,17},{1... | collective-permute-start | bytes 393224 | tf_op jit(solution)/shard_map/ppermute | solution.py:29
  2.4 10.6 %collective-permute-start = (bf16[64,1024]{1,0:T(8,128)(2,1)S(1)}, bf16[64,1024]{1,0:T(8,128)(2,1)S(1)}, u32[]{:S(2)}, u32[]{:S(2)}) collective-permute-start(bf16[64,1024]{1,0:T(8,128)(2,1)S(1)} %get-tuple-element.66), channel_id=1, source_target_pairs={{0,4},{4,0},{8,12},{12,8},{16,20},{20,16},{24,28},{28,24},{1,5},{5... | collective-permute-start | bytes 393224 | tf_op jit(solution)/shard_map/ppermute | solution.py:30
  8.6 0.7 copy-start
  8.6 0.7 copy-start.1
  13.1 4.3 %collective-permute-start.3 = (bf16[64,512]{1,0:T(8,128)(2,1)S(1)}, bf16[64,512]{1,0:T(8,128)(2,1)S(1)}, u32[]{:S(2)}, u32[]{:S(2)}) collective-permute-start(bf16[64,512]{1,0:T(8,128)(2,1)S(1)} %get-tuple-element.79), channel_id=1, source_target_pairs={{1,2},{2,1},{0,3},{3,0},{5,6},{6,5},{4,7},{7,4},{9,10},{10,9},{8,1... | collective-permute-start | bytes 196616 | tf_op jit(solution)/shard_map/ppermute | solution.py:29
  14.3 3.1 %collective-permute-start.2 = (bf16[64,512]{1,0:T(8,128)(2,1)S(1)}, bf16[64,512]{1,0:T(8,128)(2,1)S(1)}, u32[]{:S(2)}, u32[]{:S(2)}) collective-permute-start(bf16[64,512]{1,0:T(8,128)(2,1)S(1)} %get-tuple-element.80), channel_id=1, source_target_pairs={{0,1},{1,0},{2,3},{3,2},{4,5},{5,4},{6,7},{7,6},{8,9},{9,8},{10,11... | collective-permute-start | bytes 196616 | tf_op jit(solution)/shard_map/ppermute | solution.py:30
  18.5 1.3 %collective-permute-start.4 = (f32[32,640]{1,0:T(8,128)S(1)}, f32[32,640]{1,0:T(8,128)S(1)}, u32[]{:S(2)}, u32[]{:S(2)}) collective-permute-start(f32[32,640]{1,0:T(8,128)S(1)} %slice_select_fusion), channel_id=1, source_target_pairs={{0,1},{1,0},{2,3},{3,2},{4,5},{5,4},{6,7},{7,6},{8,9},{9,8},{10,11... | collective-permute-start | bytes 245768 | tf_op jit(solution)/shard_map/ppermute | solution.py:322
  19.9 6.3 %collective-permute-start.7 = (f32[32,640]{1,0:T(8,128)S(1)}, f32[32,640]{1,0:T(8,128)S(1)}, u32[]{:S(2)}, u32[]{:S(2)}) collective-permute-start(f32[32,640]{1,0:T(8,128)S(1)} %select_add_fusion), channel_id=1, source_target_pairs={{0,6},{1,7},{2,4},{3,5},{4,2},{5,3},{6,0},{7,1},{8,14},{9,15},{10,... | collective-permute-start | bytes 245768 | tf_op jit(solution)/shard_map/ppermute | solution.py:322
  23.4 4.7 %collective-permute-start.6 = (f32[32,640]{1,0:T(8,128)S(1)}, f32[32,640]{1,0:T(8,128)S(1)}, u32[]{:S(2)}, u32[]{:S(2)}) collective-permute-start(f32[32,640]{1,0:T(8,128)S(1)} %select_add_fusion), channel_id=1, source_target_pairs={{0,5},{1,4},{2,7},{3,6},{4,1},{5,0},{6,3},{7,2},{8,13},{9,12},{10,... | collective-permute-start | bytes 245768 | tf_op jit(solution)/shard_map/ppermute | solution.py:322
  23.4 4.7 %collective-permute-start.5 = (f32[32,640]{1,0:T(8,128)S(1)}, f32[32,640]{1,0:T(8,128)S(1)}, u32[]{:S(2)}, u32[]{:S(2)}) collective-permute-start(f32[32,640]{1,0:T(8,128)S(1)} %select_add_fusion), channel_id=1, source_target_pairs={{0,3},{1,2},{2,1},{3,0},{4,7},{5,6},{6,5},{7,4},{8,11},{9,10},{10,... | collective-permute-start | bytes 245768 | tf_op jit(solution)/shard_map/ppermute | solution.py:322
  28.1 6.6 %collective-permute-start.10 = (f32[32,640]{1,0:T(8,128)S(1)}, f32[32,640]{1,0:T(8,128)S(1)}, u32[]{:S(2)}, u32[]{:S(2)}) collective-permute-start(f32[32,640]{1,0:T(8,128)S(1)} %add_add_fusion.1), channel_id=1, source_target_pairs={{0,24},{1,25},{2,26},{3,27},{4,28},{5,29},{6,30},{7,31},{8,16},{9,... | collective-permute-start | bytes 245768 | tf_op jit(solution)/shard_map/ppermute | solution.py:322
  31.8 6.5 %collective-permute-start.9 = (f32[32,640]{1,0:T(8,128)S(1)}, f32[32,640]{1,0:T(8,128)S(1)}, u32[]{:S(2)}, u32[]{:S(2)}) collective-permute-start(f32[32,640]{1,0:T(8,128)S(1)} %add_add_fusion.1), channel_id=1, source_target_pairs={{0,17},{1,16},{2,19},{3,18},{4,21},{5,20},{6,23},{7,22},{8,25},{9,... | collective-permute-start | bytes 245768 | tf_op jit(solution)/shard_map/ppermute | solution.py:322
  31.8 6.5 %collective-permute-start.8 = (f32[32,640]{1,0:T(8,128)S(1)}, f32[32,640]{1,0:T(8,128)S(1)}, u32[]{:S(2)}, u32[]{:S(2)}) collective-permute-start(f32[32,640]{1,0:T(8,128)S(1)} %add_add_fusion.1), channel_id=1, source_target_pairs={{0,9},{1,8},{2,11},{3,10},{4,13},{5,12},{6,15},{7,14},{8,1},{9,0},... | collective-permute-start | bytes 245768 | tf_op jit(solution)/shard_map/ppermute | solution.py:322
  38.3 1.5 %collective-permute-start.11 = (f32[32,640]{1,0:T(8,128)S(1)}, f32[32,640]{1,0:T(8,128)S(1)}, u32[]{:S(2)}, u32[]{:S(2)}) collective-permute-start(f32[32,640]{1,0:T(8,128)S(1)} %add_add_fusion), channel_id=1, source_target_pairs={{0,1},{1,0},{2,3},{3,2},{4,5},{5,4},{6,7},{7,6},{8,9},{9,8},{10,11... | collective-permute-start | bytes 245768 | tf_op jit(solution)/shard_map/ppermute | solution.py:322
  44.4 4.5 %collective-permute-start.13 = (bf16[64,1024]{1,0:T(8,128)(2,1)S(1)}, bf16[64,1024]{1,0:T(8,128)(2,1)S(1)}, u32[]{:S(2)}, u32[]{:S(2)}) collective-permute-start(bf16[64,1024]{1,0:T(8,128)(2,1)S(1)} %get-tuple-element.57), channel_id=1, source_target_pairs={{4,8},{8,4},{12,16},{16,12},{20,24},{24,20},{5,9},{9,5},{13,17},{1... | collective-permute-start | bytes 393224 | tf_op jit(solution)/shard_map/ppermute | solution.py:29
  45.0 9.6 %collective-permute-start.12 = (bf16[64,1024]{1,0:T(8,128)(2,1)S(1)}, bf16[64,1024]{1,0:T(8,128)(2,1)S(1)}, u32[]{:S(2)}, u32[]{:S(2)}) collective-permute-start(bf16[64,1024]{1,0:T(8,128)(2,1)S(1)} %get-tuple-element.58), channel_id=1, source_target_pairs={{0,4},{4,0},{8,12},{12,8},{16,20},{20,16},{24,28},{28,24},{1,5},{5... | collective-permute-start | bytes 393224 | tf_op jit(solution)/shard_map/ppermute | solution.py:30
  54.7 4.4 %collective-permute-start.15 = (bf16[64,512]{1,0:T(8,128)(2,1)S(1)}, bf16[64,512]{1,0:T(8,128)(2,1)S(1)}, u32[]{:S(2)}, u32[]{:S(2)}) collective-permute-start(bf16[64,512]{1,0:T(8,128)(2,1)S(1)} %get-tuple-element.71), channel_id=1, source_target_pairs={{1,2},{2,1},{0,3},{3,0},{5,6},{6,5},{4,7},{7,4},{9,10},{10,9},{8,1... | collective-permute-start | bytes 196616 | tf_op jit(solution)/shard_map/ppermute | solution.py:29
  55.2 3.9 %collective-permute-start.14 = (bf16[64,512]{1,0:T(8,128)(2,1)S(1)}, bf16[64,512]{1,0:T(8,128)(2,1)S(1)}, u32[]{:S(2)}, u32[]{:S(2)}) collective-permute-start(bf16[64,512]{1,0:T(8,128)(2,1)S(1)} %get-tuple-element.72), channel_id=1, source_target_pairs={{0,1},{1,0},{2,3},{3,2},{4,5},{5,4},{6,7},{7,6},{8,9},{9,8},{10,11... | collective-permute-start | bytes 196616 | tf_op jit(solution)/shard_map/ppermute | solution.py:30
  60.2 1.3 %collective-permute-start.16 = (f32[32,256]{1,0:T(8,128)S(1)}, f32[32,256]{1,0:T(8,128)S(1)}, u32[]{:S(2)}, u32[]{:S(2)}) collective-permute-start(f32[32,256]{1,0:T(8,128)S(1)} %slice_select_fusion.1), channel_id=1, source_target_pairs={{0,1},{1,0},{2,3},{3,2},{4,5},{5,4},{6,7},{7,6},{8,9},{9,8},{10,11... | collective-permute-start | bytes 98312 | tf_op jit(solution)/shard_map/ppermute | solution.py:322
  61.5 4.9 %collective-permute-start.19 = (f32[32,256]{1,0:T(8,128)S(1)}, f32[32,256]{1,0:T(8,128)S(1)}, u32[]{:S(2)}, u32[]{:S(2)}) collective-permute-start(f32[32,256]{1,0:T(8,128)S(1)} %select_add_fusion.1), channel_id=1, source_target_pairs={{0,6},{1,7},{2,4},{3,5},{4,2},{5,3},{6,0},{7,1},{8,14},{9,15},{10,... | collective-permute-start | bytes 98312 | tf_op jit(solution)/shard_map/ppermute | solution.py:322
  64.5 3.6 %collective-permute-start.18 = (f32[32,256]{1,0:T(8,128)S(1)}, f32[32,256]{1,0:T(8,128)S(1)}, u32[]{:S(2)}, u32[]{:S(2)}) collective-permute-start(f32[32,256]{1,0:T(8,128)S(1)} %select_add_fusion.1), channel_id=1, source_target_pairs={{0,5},{1,4},{2,7},{3,6},{4,1},{5,0},{6,3},{7,2},{8,13},{9,12},{10,... | collective-permute-start | bytes 98312 | tf_op jit(solution)/shard_map/ppermute | solution.py:322
  64.5 3.6 %collective-permute-start.17 = (f32[32,256]{1,0:T(8,128)S(1)}, f32[32,256]{1,0:T(8,128)S(1)}, u32[]{:S(2)}, u32[]{:S(2)}) collective-permute-start(f32[32,256]{1,0:T(8,128)S(1)} %select_add_fusion.1), channel_id=1, source_target_pairs={{0,3},{1,2},{2,1},{3,0},{4,7},{5,6},{6,5},{7,4},{8,11},{9,10},{10,... | collective-permute-start | bytes 98312 | tf_op jit(solution)/shard_map/ppermute | solution.py:322
  68.2 5.9 %collective-permute-start.22 = (f32[32,256]{1,0:T(8,128)S(1)}, f32[32,256]{1,0:T(8,128)S(1)}, u32[]{:S(2)}, u32[]{:S(2)}) collective-permute-start(f32[32,256]{1,0:T(8,128)S(1)} %add_add_fusion.3), channel_id=1, source_target_pairs={{0,24},{1,25},{2,26},{3,27},{4,28},{5,29},{6,30},{7,31},{8,16},{9,... | collective-permute-start | bytes 98312 | tf_op jit(solution)/shard_map/ppermute | solution.py:322
  70.2 4.9 %collective-permute-start.21 = (f32[32,256]{1,0:T(8,128)S(1)}, f32[32,256]{1,0:T(8,128)S(1)}, u32[]{:S(2)}, u32[]{:S(2)}) collective-permute-start(f32[32,256]{1,0:T(8,128)S(1)} %add_add_fusion.3), channel_id=1, source_target_pairs={{0,17},{1,16},{2,19},{3,18},{4,21},{5,20},{6,23},{7,22},{8,25},{9,... | collective-permute-start | bytes 98312 | tf_op jit(solution)/shard_map/ppermute | solution.py:322
  70.3 4.9 %collective-permute-start.20 = (f32[32,256]{1,0:T(8,128)S(1)}, f32[32,256]{1,0:T(8,128)S(1)}, u32[]{:S(2)}, u32[]{:S(2)}) collective-permute-start(f32[32,256]{1,0:T(8,128)S(1)} %add_add_fusion.3), channel_id=1, source_target_pairs={{0,9},{1,8},{2,11},{3,10},{4,13},{5,12},{6,15},{7,14},{8,1},{9,0},... | collective-permute-start | bytes 98312 | tf_op jit(solution)/shard_map/ppermute | solution.py:322
  75.2 1.3 %collective-permute-start.23 = (f32[32,256]{1,0:T(8,128)S(1)}, f32[32,256]{1,0:T(8,128)S(1)}, u32[]{:S(2)}, u32[]{:S(2)}) collective-permute-start(f32[32,256]{1,0:T(8,128)S(1)} %add_add_fusion.2), channel_id=1, source_target_pairs={{0,1},{1,0},{2,3},{3,2},{4,5},{5,4},{6,7},{7,6},{8,9},{9,8},{10,11... | collective-permute-start | bytes 98312 | tf_op jit(solution)/shard_map/ppermute | solution.py:322

commit v11 on v10

--- a/solution.py
+++ b/solution.py
@@ -1,4 +1,5 @@
 import functools
+import math
 
 import jax
 import jax.numpy as jnp
@@ -16,27 +17,35 @@
     return lax.dot_general(left, right, dims, preferred_element_type=jnp.float32)
 
 
-def neighbours(block, span_x, span_y, depth, meanwhile=()):
-    plane = span_y * depth
-
-    def exchange(axis, upward, downward, closed):
-        count = lax.axis_size(axis)
-        me = lax.axis_index(axis)
-        odd = me % 2 == 1
-        pairs = [(i, (i - 1 ^ 1) + 1) for i in range(1, count - 1)]
-        if closed:
-            pairs += [(0, count - 1), (count - 1, 0)]
-        outer = lax.ppermute(jnp.where(odd, upward, downward), axis, pairs)
-        inner = lax.ppermute(
-            jnp.where(odd, downward, upward), axis, [(i, i ^ 1) for i in range(count)]
-        )
+def swaps(axis, upward, downward, closed):
+    count = lax.axis_size(axis)
+    me = lax.axis_index(axis)
+    odd = me % 2 == 1
+    pairs = [(i, (i - 1 ^ 1) + 1) for i in range(1, count - 1)]
+    if closed:
+        pairs += [(0, count - 1), (count - 1, 0)]
+    inner = lax.ppermute(
+        jnp.where(odd, downward, upward), axis, [(i, i ^ 1) for i in range(count)]
+    )
+    outer = lax.ppermute(jnp.where(odd, upward, downward), axis, pairs)
+
+    def sort(inner, outer):
         if closed:
             outer = jnp.where((me == 0) | (me == count - 1), 0, outer)
         return jnp.where(odd, inner, outer), jnp.where(odd, outer, inner)
 
-    xlo, xhi = exchange("slab", block[:, (span_x - 1) * plane :], block[:, :plane], False)
-
-    xlo, xhi, meanwhile = lax.optimization_barrier((xlo, xhi, meanwhile))
+    return inner, outer, sort
+
+
+def neighbours(block, span_x, span_y, depth, inner_image, meanwhile=()):
+    plane = span_y * depth
+    inner, outer, sort = swaps(
+        "slab", block[:, (span_x - 1) * plane :], block[:, :plane], False
+    )
+    inner, tied = lax.optimization_barrier((inner, block))
+    partial = inner_image(tied)
+    inner, outer, partial, meanwhile = lax.optimization_barrier((inner, outer, partial, meanwhile))
+    xlo, xhi = sort(inner, outer)
 
     def edge(row):
         at = row * depth
@@ -45,8 +54,8 @@
         parts += [xhi[:, at : at + depth]]
         return jnp.concatenate(parts, axis=1)
 
-    ylo, yhi = exchange("col", edge(span_y - 1), edge(0), True)
-    return (xlo, xhi, ylo, yhi), meanwhile
+    inner, outer, sort = swaps("col", edge(span_y - 1), edge(0), True)
+    return (xlo, xhi, *sort(inner, outer)), partial, meanwhile
 
 
 def coefficients_kernel(table, cells, coef):
@@ -300,7 +309,7 @@
 
 
 def second_solve_kernel(
-    scale, cross, own_high, own_low, stack, last, image, proj_in, low_in, block, proj, low
+    scale, cross, own_high, own_low, stack, last, image, proj_in, low_in, result, proj, low, block
 ):
     columns = image.shape[0]
     kept = stack.shape[0] - columns
@@ -313,7 +322,12 @@
     block[...] = w.astype(jnp.bfloat16)
     upper, inverse = factor(square)
     low[1] = upper.T
-    block[...] = dot(inverse.astype(jnp.bfloat16), block[...]).astype(jnp.bfloat16)
+    inverse = inverse.astype(jnp.bfloat16)
+    _, span_x, span_y, depth = result.shape
+    plane = span_y * depth
+    for x in range(span_x):
+        part = dot(inverse, block[:, x * plane : (x + 1) * plane])
+        result[:, x] = part.reshape(columns, span_y, depth).astype(jnp.bfloat16)
 
 
 def partner(part, mask):
@@ -322,7 +336,7 @@
     return lax.ppermute(part, axes, [(i, i ^ mask) for i in range(count)])
 
 
-def whole_sum(part):
+def whole_sum(part, grouped):
     cols = lax.axis_size("col")
     count = lax.axis_size("slab") * cols
     index = lax.axis_index("slab") * cols + lax.axis_index("col")
@@ -336,23 +350,28 @@
     part = jnp.where(upper, high, low) + partner(jnp.where(upper, low, high), 1)
     bit = 2
     while bit < count:
-        if 2 * bit < count:
+        if 2 * bit < count and (grouped or bit == 2):
             one, two, both = (partner(part, mask) for mask in (bit + 1, 2 * bit + 1, 3 * bit))
             part = (part + one) + (two + both)
+            bit *= 4
         else:
             part = part + partner(part, bit + 1)
-        bit *= 4
+            bit *= 2
     other = partner(part, 1)
     return jnp.concatenate([jnp.where(upper, other, part), jnp.where(upper, part, other)], axis=0)
 
 
-def call(kernel, name, outs, *args):
+def call(kernel, name, outs, *args, flops=0, scratch=()):
+    moved = sum(math.prod(arg.shape) * arg.dtype.itemsize for arg in args)
+    moved += sum(math.prod(shape) * jnp.dtype(dtype).itemsize for shape, dtype in outs)
     return pl.pallas_call(
         kernel,
         out_shape=[jax.ShapeDtypeStruct(shape, dtype) for shape, dtype in outs],
         in_specs=[pl.BlockSpec(memory_space=pltpu.VMEM)] * len(args),
         out_specs=[pl.BlockSpec(memory_space=pltpu.VMEM)] * len(outs),
+        scratch_shapes=scratch,
         compiler_params=pltpu.CompilerParams(vmem_limit_bytes=24 * 1024 * 1024),
+        cost_estimate=pl.CostEstimate(flops=flops, bytes_accessed=moved, transcendentals=0),
         name=name,
     )(*args)
 
@@ -373,25 +392,28 @@
         "stack_gram",
         [((columns, columns * blocks * (blocks + 1) // 2), f32)],
         stack,
-    )
-    inner_image = functools.partial(
-        call,
-        functools.partial(inner_image_kernel, spans),
-        "inner_image",
-        [((columns, cells), f32)],
-        coef,
-    )
-    around, (coef, stack, own, partial) = neighbours(
-        basis[blocks - 1].reshape(columns, cells), *spans, (coef, stack, own, *inner_image(stack))
+        flops=2 * fields * fields * cells,
+    )
+    def inner_image(block):
+        return call(
+            functools.partial(inner_image_kernel, spans),
+            "inner_image",
+            [((columns, cells), f32)],
+            coef, block,
+            flops=2 * 27 * columns * cells,
+        )[0]
+
+    around, partial, (coef_ready, stack, own) = neighbours(
+        basis[blocks - 1].reshape(columns, cells), *spans, inner_image, (coef, stack, own)
     )
     packed = fields + columns + own.shape[1]
     image, cross = call(
         functools.partial(first_image_kernel, spans),
         "first_image",
         [((columns, cells), bf16), ((columns, packed), f32)],
-        coef, stack, own, partial, *around,
-    )
-    cross = whole_sum(cross)
+        coef_ready, stack, own, partial, *around,
+    )
+    cross = whole_sum(cross, False)
     block, proj, low, rest, square, inverse = call(
         functools.partial(first_solve_kernel, scale),
         "first_solve",
@@ -405,7 +427,7 @@
         [((fields, fields), bf16)] * 2,
         cross, rest, square, inverse,
     )
-    around, (partial,) = neighbours(block, *spans, tuple(inner_image(block)))
+    around, partial, _ = neighbours(block, *spans, inner_image)
     image, cross = call(
         functools.partial(second_image_kernel, spans),
         "second_image",
@@ -415,10 +437,11 @@
     block, proj, low = call(
         functools.partial(second_solve_kernel, scale),
         "second_solve",
-        [((columns, cells), bf16), ((2, columns, fields), f32), ((2, columns, columns), f32)],
-        whole_sum(cross), *own, stack, block, image, proj, low,
-    )
-    return block.reshape(columns, *spans), jnp.swapaxes(proj, 1, 2), low
+        [((columns, *spans), bf16), ((2, columns, fields), f32), ((2, columns, columns), f32)],
+        whole_sum(cross, True), *own, stack, block, image, proj, low,
+        scratch=[pltpu.VMEM((columns, cells), bf16)],
+    )
+    return block, jnp.swapaxes(proj, 1, 2), low
 
 
 def solution(mesh):

time: 81.8 us -> 82.9 us (1.013)
  waiting for transfers between devices: 34.1 us -> 36.3 us
    ppermute x16 -> x15, waiting for transfers between devices: 20.3 us -> 22.2 us  [partner(): return lax.ppermute(part, axes, [(i, i ^ mask) for i in range(count)])]
    ppermute x16 -> x15, starting transfers between devices: 16.7 us -> 16.1 us  [partner(): return lax.ppermute(part, axes, [(i, i ^ mask) for i in range(count)])]
  transfers between devices with their start and end apart: 24 -> 23, of which waited for: 17 -> 16; matrix products, arithmetic and copies ran while one was open for 0% -> 0% of each run, Pallas kernels for 3% -> 4%
where the time goes in v11:
time: 82.9 us; the launch traced here: 82.6 us
  waiting for transfers between devices  36.3 us (44%)
  starting transfers between devices  30.1 us (36%)
  Pallas kernels  13.5 us (16%)
  local copies, waits for them, and re-layouts  1.5 us (2%)
  between operations  0.92 us (1%)
    ppermute x15, waiting for transfers between devices, partner(): return lax.ppermute(part, axes, [(i, i ^ mask) for i in range(count)])  22.2 us
    ppermute x15, starting transfers between devices, partner(): return lax.ppermute(part, axes, [(i, i ^ mask) for i in range(count)])  16.1 us
    pallas_call x8, Pallas kernels, call(): pl.pallas_call(kernel, out_shape=[jax.ShapeDtypeStruct(shape, dtype) for...  12.7 us
    ppermute x4, starting transfers between devices, swaps(): lax.ppermute(jnp.where(odd, downward, upward), axis, [(i, i ^ 1) for i in...  10.6 us
    ppermute x4, waiting for transfers between devices, swaps(): lax.ppermute(jnp.where(odd, downward, upward), axis, [(i, i ^ 1) for i in...  8.58 us
    ppermute x4, waiting for transfers between devices, swaps(): outer = lax.ppermute(jnp.where(odd, upward, downward), axis, pairs)  5.49 us
    ppermute x4, starting transfers between devices, swaps(): outer = lax.ppermute(jnp.where(odd, upward, downward), axis, pairs)  3.48 us
  transfers between devices with their start and end apart: 23, of which 16 were waited for; matrix products, arithmetic and copies ran while one was open for 0% of the time, Pallas kernels for 4%

profile of v11, /device:TPU:0, one launch (start us, length us, event | category | flops | bytes accessed | tf_op | source)
XLA Modules:
  0.0 82.6 jit_solution(2730486099378529169)
XLA Ops:
  0.6 0.0 slice-start
  0.7 0.0 copy-start.2
  0.7 0.9 %slice-done = bf16[1,64,2,8,128]{4,3,2,1,0:T(8,128)(2,1)S(1)} async-done(((bf16[3,64,2,8,128]{4,3,2,1,0:T(8,128)(2,1)}), bf16[1,64,2,8,128]{4,3,2,1,0:T(8,128)(2,1)S(1)}, s32[]{:S(2)}) %slice-start) | async-done | bytes 262168 | tf_op jit(solution)/shard_map/slice | solution.py:407
  1.6 0.1 reshape_squeeze.3.fields
  1.7 0.7 collective-permute-start.1
  2.4 5.8 %collective-permute-start = (bf16[64,1024]{1,0:T(8,128)(2,1)S(1)}, bf16[64,1024]{1,0:T(8,128)(2,1)S(1)}, u32[]{:S(2)}, u32[]{:S(2)}) collective-permute-start(bf16[64,1024]{1,0:T(8,128)(2,1)S(1)} %get-tuple-element.74), channel_id=1, source_target_pairs={{0,4},{4,0},{8,12},{12,8},{16,20},{20,16},{24,28},{28,24},{1,5},{5... | collective-permute-start | bytes 393224 | tf_op jit(solution)/shard_map/ppermute | solution.py:27
  8.2 0.3 reshape.13.stack
  8.6 0.0 copy-start
  8.6 0.0 copy-start.1
  8.6 0.6 stack_gram.1.own
  9.2 0.0 copy-done
  9.3 0.0 copy-done.1
  9.3 0.8 coefficients.1.coef
  10.1 3.0 %collective-permute-done = bf16[64,1024]{1,0:T(8,128)(2,1)S(1)} collective-permute-done((bf16[64,1024]{1,0:T(8,128)(2,1)S(1)}, bf16[64,1024]{1,0:T(8,128)(2,1)S(1)}, u32[]{:S(2)}, u32[]{:S(2)}) %collective-permute-start) | collective-permute-done | bytes 131104 | tf_op jit(solution)/shard_map/ppermute | solution.py:27
  13.0 0.7 inner_image.2.partial
  13.7 0.0 collective-permute-done.1
  13.8 1.2 %collective-permute-start.3 = (bf16[64,512]{1,0:T(8,128)(2,1)S(1)}, bf16[64,512]{1,0:T(8,128)(2,1)S(1)}, u32[]{:S(2)}, u32[]{:S(2)}) collective-permute-start(bf16[64,512]{1,0:T(8,128)(2,1)S(1)} %get-tuple-element.87), channel_id=1, source_target_pairs={{1,2},{2,1},{0,3},{3,0},{5,6},{6,5},{4,7},{7,4},{9,10},{10,9},{8,1... | collective-permute-start | bytes 196616 | tf_op jit(solution)/shard_map/ppermute | solution.py:30
  15.0 0.5 collective-permute-start.2
  15.5 2.6 %collective-permute-done.3 = bf16[64,512]{1,0:T(8,128)(2,1)S(1)} collective-permute-done((bf16[64,512]{1,0:T(8,128)(2,1)S(1)}, bf16[64,512]{1,0:T(8,128)(2,1)S(1)}, u32[]{:S(2)}, u32[]{:S(2)}) %collective-permute-start.3) | collective-permute-done | bytes 65568 | tf_op jit(solution)/shard_map/ppermute | solution.py:30
  18.1 0.0 collective-permute-done.2
  18.1 1.1 %first_image.1 = (bf16[64,2048]{1,0:T(8,128)(2,1)S(1)}, f32[64,640]{1,0:T(8,128)S(1)}) custom-call(f32[27,16,128]{2,1,0:T(8,128)S(1)} %coefficients.1.coef, bf16[192,2048]{1,0:T(8,128)(2,1)S(1)} %reshape.13.stack, f32[64,384]{1,0:T(8,128)S(1)} %stack_gram.1.own, f32[64,2048]{1,0:T(8,128)S(1)} %inner_image.2.partial, ...), custom_call_target="tpu_custom_call" | custom-call | bytes 2449408 | tf_op jit(solution)/shard_map/first_image/pallas_call | solution.py:367
  19.2 0.2 collective-permute-start.4
  19.4 1.2 %collective-permute-done.4 = f32[32,640]{1,0:T(8,128)S(1)} collective-permute-done((f32[32,640]{1,0:T(8,128)S(1)}, f32[32,640]{1,0:T(8,128)S(1)}, u32[]{:S(2)}, u32[]{:S(2)}) %collective-permute-start.4) | collective-permute-done | bytes 81952 | tf_op jit(solution)/shard_map/ppermute | solution.py:336
  20.6 3.5 %collective-permute-start.7 = (f32[32,640]{1,0:T(8,128)S(1)}, f32[32,640]{1,0:T(8,128)S(1)}, u32[]{:S(2)}, u32[]{:S(2)}) collective-permute-start(f32[32,640]{1,0:T(8,128)S(1)} %select_add_fusion), channel_id=1, source_target_pairs={{0,6},{1,7},{2,4},{3,5},{4,2},{5,3},{6,0},{7,1},{8,14},{9,15},{10,... | collective-permute-start | bytes 245768 | tf_op jit(solution)/shard_map/ppermute | solution.py:336
  24.1 0.0 collective-permute-start.6
  24.1 0.4 collective-permute-start.5
  24.5 2.4 %collective-permute-done.7 = f32[32,640]{1,0:T(8,128)S(1)} collective-permute-done((f32[32,640]{1,0:T(8,128)S(1)}, f32[32,640]{1,0:T(8,128)S(1)}, u32[]{:S(2)}, u32[]{:S(2)}) %collective-permute-start.7) | collective-permute-done | bytes 81952 | tf_op jit(solution)/shard_map/ppermute | solution.py:336
  26.9 1.9 %collective-permute-done.6 = f32[32,640]{1,0:T(8,128)S(1)} collective-permute-done((f32[32,640]{1,0:T(8,128)S(1)}, f32[32,640]{1,0:T(8,128)S(1)}, u32[]{:S(2)}, u32[]{:S(2)}) %collective-permute-start.6) | collective-permute-done | bytes 81952 | tf_op jit(solution)/shard_map/ppermute | solution.py:336
  28.8 0.0 collective-permute-done.5
  28.8 1.4 %collective-permute-start.8 = (f32[32,640]{1,0:T(8,128)S(1)}, f32[32,640]{1,0:T(8,128)S(1)}, u32[]{:S(2)}, u32[]{:S(2)}) collective-permute-start(f32[32,640]{1,0:T(8,128)S(1)} %add_add_fusion), channel_id=1, source_target_pairs={{0,9},{1,8},{2,11},{3,10},{4,13},{5,12},{6,15},{7,14},{8,1},{9,0},... | collective-permute-start | bytes 245768 | tf_op jit(solution)/shard_map/ppermute | solution.py:336
  30.2 3.1 %collective-permute-done.8 = f32[32,640]{1,0:T(8,128)S(1)} collective-permute-done((f32[32,640]{1,0:T(8,128)S(1)}, f32[32,640]{1,0:T(8,128)S(1)}, u32[]{:S(2)}, u32[]{:S(2)}) %collective-permute-start.8) | collective-permute-done | bytes 81952 | tf_op jit(solution)/shard_map/ppermute | solution.py:336
  33.3 2.4 %collective-permute-start.9 = (f32[32,640]{1,0:T(8,128)S(1)}, f32[32,640]{1,0:T(8,128)S(1)}, u32[]{:S(2)}, u32[]{:S(2)}) collective-permute-start(f32[32,640]{1,0:T(8,128)S(1)} %add.89), channel_id=1, source_target_pairs={{0,17},{1,16},{2,19},{3,18},{4,21},{5,20},{6,23},{7,22},{8,25},{9,... | collective-permute-start | bytes 245768 | tf_op jit(solution)/shard_map/ppermute | solution.py:336
  35.7 4.7 %collective-permute-done.9 = f32[32,640]{1,0:T(8,128)S(1)} collective-permute-done((f32[32,640]{1,0:T(8,128)S(1)}, f32[32,640]{1,0:T(8,128)S(1)}, u32[]{:S(2)}, u32[]{:S(2)}) %collective-permute-start.9) | collective-permute-done | bytes 81952 | tf_op jit(solution)/shard_map/ppermute | solution.py:336
  40.5 0.2 collective-permute-start.10
  40.7 1.2 %collective-permute-done.10 = f32[32,640]{1,0:T(8,128)S(1)} collective-permute-done((f32[32,640]{1,0:T(8,128)S(1)}, f32[32,640]{1,0:T(8,128)S(1)}, u32[]{:S(2)}, u32[]{:S(2)}) %collective-permute-start.10) | collective-permute-done | bytes 81952 | tf_op jit(solution)/shard_map/ppermute | solution.py:336
  41.9 3.8 %first_solve.1 = (bf16[64,2048]{1,0:T(8,128)(2,1)S(1)}, f32[64,192]{1,0:T(8,128)S(1)}, f32[64,64]{1,0:T(8,128)S(1)}, f32[64,192]{1,0:T(8,128)S(1)}, f32[64,64]{1,0:T(8,128)S(1)}, /*index=5*/bf16[64,64]{1,0:T(8,128)(2,1)S(1)}) custom-call(f32[64,640]{1,0:T(8,128)S(1)} %pad_maximum_fusion.cross, bf16[192,2048]{1,0:T(8,128)(2,1)S(1)} %reshape.13.stack, ...), custom_call_target="tpu_custom_call" | custom-call | bytes 1613824 | tf_op jit(solution)/shard_map/first_solve/pallas_call | solution.py:367
  45.7 0.7 collective-permute-start.12
  46.4 3.8 %collective-permute-start.11 = (bf16[64,1024]{1,0:T(8,128)(2,1)S(1)}, bf16[64,1024]{1,0:T(8,128)(2,1)S(1)}, u32[]{:S(2)}, u32[]{:S(2)}) collective-permute-start(bf16[64,1024]{1,0:T(8,128)(2,1)S(1)} %get-tuple-element.66), channel_id=1, source_target_pairs={{0,4},{4,0},{8,12},{12,8},{16,20},{20,16},{24,28},{28,24},{1,5},{5... | collective-permute-start | bytes 393224 | tf_op jit(solution)/shard_map/ppermute | solution.py:27
  50.2 5.6 %collective-permute-done.11 = bf16[64,1024]{1,0:T(8,128)(2,1)S(1)} collective-permute-done((bf16[64,1024]{1,0:T(8,128)(2,1)S(1)}, bf16[64,1024]{1,0:T(8,128)(2,1)S(1)}, u32[]{:S(2)}, u32[]{:S(2)}) %collective-permute-start.11) | collective-permute-done | bytes 131104 | tf_op jit(solution)/shard_map/ppermute | solution.py:27
  55.8 0.7 inner_image.3.partial
  56.5 0.0 collective-permute-done.12
  56.6 0.9 %collective-permute-start.14 = (bf16[64,512]{1,0:T(8,128)(2,1)S(1)}, bf16[64,512]{1,0:T(8,128)(2,1)S(1)}, u32[]{:S(2)}, u32[]{:S(2)}) collective-permute-start(bf16[64,512]{1,0:T(8,128)(2,1)S(1)} %get-tuple-element.79), channel_id=1, source_target_pairs={{1,2},{2,1},{0,3},{3,0},{5,6},{6,5},{4,7},{7,4},{9,10},{10,9},{8,1... | collective-permute-start | bytes 196616 | tf_op jit(solution)/shard_map/ppermute | solution.py:30
  57.5 0.5 collective-permute-start.13
  58.0 2.9 %collective-permute-done.14 = bf16[64,512]{1,0:T(8,128)(2,1)S(1)} collective-permute-done((bf16[64,512]{1,0:T(8,128)(2,1)S(1)}, bf16[64,512]{1,0:T(8,128)(2,1)S(1)}, u32[]{:S(2)}, u32[]{:S(2)}) %collective-permute-start.14) | collective-permute-done | bytes 65568 | tf_op jit(solution)/shard_map/ppermute | solution.py:30
  61.0 0.0 collective-permute-done.13
  61.0 1.1 %second_image.1 = (bf16[64,2048]{1,0:T(8,128)(2,1)S(1)}, f32[64,256]{1,0:T(8,128)S(1)}) custom-call(f32[27,16,128]{2,1,0:T(8,128)S(1)} %coefficients.1.coef, bf16[192,2048]{1,0:T(8,128)(2,1)S(1)} %reshape.13.stack, bf16[64,2048]{1,0:T(8,128)(2,1)S(1)} %get-tuple-element.43.fields.block.last, f32[64,2048]{1,0:T(8,128)S(1)} %inner_image.3.partial, ...), custom_call_target="tpu_custom_call" | custom-call | bytes 2514944 | tf_op jit(solution)/shard_map/second_image/pallas_call | solution.py:367
  62.1 0.2 collective-permute-start.15
  62.3 1.1 %collective-permute-done.15 = f32[32,256]{1,0:T(8,128)S(1)} collective-permute-done((f32[32,256]{1,0:T(8,128)S(1)}, f32[32,256]{1,0:T(8,128)S(1)}, u32[]{:S(2)}, u32[]{:S(2)}) %collective-permute-start.15) | collective-permute-done | bytes 32800 | tf_op jit(solution)/shard_map/ppermute | solution.py:336
  63.4 3.1 %collective-permute-start.18 = (f32[32,256]{1,0:T(8,128)S(1)}, f32[32,256]{1,0:T(8,128)S(1)}, u32[]{:S(2)}, u32[]{:S(2)}) collective-permute-start(f32[32,256]{1,0:T(8,128)S(1)} %select_add_fusion.1), channel_id=1, source_target_pairs={{0,6},{1,7},{2,4},{3,5},{4,2},{5,3},{6,0},{7,1},{8,14},{9,15},{10,... | collective-permute-start | bytes 98312 | tf_op jit(solution)/shard_map/ppermute | solution.py:336
  66.4 0.0 collective-permute-start.17
  66.5 0.4 collective-permute-start.16
  66.8 1.5 %collective-permute-done.18 = f32[32,256]{1,0:T(8,128)S(1)} collective-permute-done((f32[32,256]{1,0:T(8,128)S(1)}, f32[32,256]{1,0:T(8,128)S(1)}, u32[]{:S(2)}, u32[]{:S(2)}) %collective-permute-start.18) | collective-permute-done | bytes 32800 | tf_op jit(solution)/shard_map/ppermute | solution.py:336
  68.3 1.7 %collective-permute-done.17 = f32[32,256]{1,0:T(8,128)S(1)} collective-permute-done((f32[32,256]{1,0:T(8,128)S(1)}, f32[32,256]{1,0:T(8,128)S(1)}, u32[]{:S(2)}, u32[]{:S(2)}) %collective-permute-start.17) | collective-permute-done | bytes 32800 | tf_op jit(solution)/shard_map/ppermute | solution.py:336
  70.1 0.0 collective-permute-done.16
  70.1 2.4 %collective-permute-start.21 = (f32[32,256]{1,0:T(8,128)S(1)}, f32[32,256]{1,0:T(8,128)S(1)}, u32[]{:S(2)}, u32[]{:S(2)}) collective-permute-start(f32[32,256]{1,0:T(8,128)S(1)} %add_add_fusion.2), channel_id=1, source_target_pairs={{0,24},{1,25},{2,26},{3,27},{4,28},{5,29},{6,30},{7,31},{8,16},{9,... | collective-permute-start | bytes 98312 | tf_op jit(solution)/shard_map/ppermute | solution.py:336
  72.5 0.0 collective-permute-start.20
  72.5 1.8 %collective-permute-start.19 = (f32[32,256]{1,0:T(8,128)S(1)}, f32[32,256]{1,0:T(8,128)S(1)}, u32[]{:S(2)}, u32[]{:S(2)}) collective-permute-start(f32[32,256]{1,0:T(8,128)S(1)} %add_add_fusion.2), channel_id=1, source_target_pairs={{0,9},{1,8},{2,11},{3,10},{4,13},{5,12},{6,15},{7,14},{8,1},{9,0},... | collective-permute-start | bytes 98312 | tf_op jit(solution)/shard_map/ppermute | solution.py:336
  74.3 1.8 %collective-permute-done.21 = f32[32,256]{1,0:T(8,128)S(1)} collective-permute-done((f32[32,256]{1,0:T(8,128)S(1)}, f32[32,256]{1,0:T(8,128)S(1)}, u32[]{:S(2)}, u32[]{:S(2)}) %collective-permute-start.21) | collective-permute-done | bytes 32800 | tf_op jit(solution)/shard_map/ppermute | solution.py:336
  76.1 0.8 collective-permute-done.20
  76.9 0.0 collective-permute-done.19
  76.9 0.2 collective-permute-start.22
  77.2 0.4 next_gram.1
  77.6 0.7 collective-permute-done.22
  78.2 4.4 %second_solve.1 = (bf16[64,2,8,128]{3,2,1,0:T(8,128)(2,1)}, f32[2,64,192]{2,1,0:T(8,128)}, f32[2,64,64]{2,1,0:T(8,128)}) custom-call(f32[64,256]{1,0:T(8,128)S(1)} %pad_maximum_fusion.5.cross, bf16[192,192]{1,0:T(8,128)(2,1)S(1)} %get-tuple-element.51.own_high, bf16[192,192]{1,0:T(8,128)(2,1)S(1)} %get-tuple-element.52.own_low, ...), custom_call_target="tpu_custom_call" | custom-call | bytes 1982464 | tf_op jit(solution)/shard_map/second_solve/pallas_call | solution.py:367
  (27 shorter events, 0.4 us)
Async XLA Ops:
  0.6 1.0 %slice-start = ((bf16[3,64,2,8,128]{4,3,2,1,0:T(8,128)(2,1)}), bf16[1,64,2,8,128]{4,3,2,1,0:T(8,128)(2,1)S(1)}, s32[]{:S(2)}) async-start(bf16[3,64,2,8,128]{4,3,2,1,0:T(8,128)(2,1)} %param.3), calls=%async_computation | async-start | bytes 524288 | tf_op jit(solution)/shard_map/slice | solution.py:407
  0.7 7.6 %copy-start.2 = (bf16[3,64,2,8,128]{4,3,2,1,0:T(8,128)(2,1)S(1)}, bf16[3,64,2,8,128]{4,3,2,1,0:T(8,128)(2,1)}, u32[]{:S(2)}) copy-start(bf16[3,64,2,8,128]{4,3,2,1,0:T(8,128)(2,1)} %param.3) | copy-start | bytes 2359300
  1.7 12.0 %collective-permute-start.1 = (bf16[64,1024]{1,0:T(8,128)(2,1)S(1)}, bf16[64,1024]{1,0:T(8,128)(2,1)S(1)}, u32[]{:S(2)}, u32[]{:S(2)}) collective-permute-start(bf16[64,1024]{1,0:T(8,128)(2,1)S(1)} %get-tuple-element.73), channel_id=1, source_target_pairs={{4,8},{8,4},{12,16},{16,12},{20,24},{24,20},{5,9},{9,5},{13,17},{1... | collective-permute-start | bytes 393224 | tf_op jit(solution)/shard_map/ppermute | solution.py:30
  2.4 10.6 %collective-permute-start = (bf16[64,1024]{1,0:T(8,128)(2,1)S(1)}, bf16[64,1024]{1,0:T(8,128)(2,1)S(1)}, u32[]{:S(2)}, u32[]{:S(2)}) collective-permute-start(bf16[64,1024]{1,0:T(8,128)(2,1)S(1)} %get-tuple-element.74), channel_id=1, source_target_pairs={{0,4},{4,0},{8,12},{12,8},{16,20},{20,16},{24,28},{28,24},{1,5},{5... | collective-permute-start | bytes 393224 | tf_op jit(solution)/shard_map/ppermute | solution.py:27
  8.6 0.7 copy-start
  8.6 0.7 copy-start.1
  13.8 4.3 %collective-permute-start.3 = (bf16[64,512]{1,0:T(8,128)(2,1)S(1)}, bf16[64,512]{1,0:T(8,128)(2,1)S(1)}, u32[]{:S(2)}, u32[]{:S(2)}) collective-permute-start(bf16[64,512]{1,0:T(8,128)(2,1)S(1)} %get-tuple-element.87), channel_id=1, source_target_pairs={{1,2},{2,1},{0,3},{3,0},{5,6},{6,5},{4,7},{7,4},{9,10},{10,9},{8,1... | collective-permute-start | bytes 196616 | tf_op jit(solution)/shard_map/ppermute | solution.py:30
  15.0 3.1 %collective-permute-start.2 = (bf16[64,512]{1,0:T(8,128)(2,1)S(1)}, bf16[64,512]{1,0:T(8,128)(2,1)S(1)}, u32[]{:S(2)}, u32[]{:S(2)}) collective-permute-start(bf16[64,512]{1,0:T(8,128)(2,1)S(1)} %get-tuple-element.88), channel_id=1, source_target_pairs={{0,1},{1,0},{2,3},{3,2},{4,5},{5,4},{6,7},{7,6},{8,9},{9,8},{10,11... | collective-permute-start | bytes 196616 | tf_op jit(solution)/shard_map/ppermute | solution.py:27
  19.2 1.3 %collective-permute-start.4 = (f32[32,640]{1,0:T(8,128)S(1)}, f32[32,640]{1,0:T(8,128)S(1)}, u32[]{:S(2)}, u32[]{:S(2)}) collective-permute-start(f32[32,640]{1,0:T(8,128)S(1)} %slice_select_fusion), channel_id=1, source_target_pairs={{0,1},{1,0},{2,3},{3,2},{4,5},{5,4},{6,7},{7,6},{8,9},{9,8},{10,11... | collective-permute-start | bytes 245768 | tf_op jit(solution)/shard_map/ppermute | solution.py:336
  20.6 6.3 %collective-permute-start.7 = (f32[32,640]{1,0:T(8,128)S(1)}, f32[32,640]{1,0:T(8,128)S(1)}, u32[]{:S(2)}, u32[]{:S(2)}) collective-permute-start(f32[32,640]{1,0:T(8,128)S(1)} %select_add_fusion), channel_id=1, source_target_pairs={{0,6},{1,7},{2,4},{3,5},{4,2},{5,3},{6,0},{7,1},{8,14},{9,15},{10,... | collective-permute-start | bytes 245768 | tf_op jit(solution)/shard_map/ppermute | solution.py:336
  24.1 4.7 %collective-permute-start.6 = (f32[32,640]{1,0:T(8,128)S(1)}, f32[32,640]{1,0:T(8,128)S(1)}, u32[]{:S(2)}, u32[]{:S(2)}) collective-permute-start(f32[32,640]{1,0:T(8,128)S(1)} %select_add_fusion), channel_id=1, source_target_pairs={{0,5},{1,4},{2,7},{3,6},{4,1},{5,0},{6,3},{7,2},{8,13},{9,12},{10,... | collective-permute-start | bytes 245768 | tf_op jit(solution)/shard_map/ppermute | solution.py:336
  24.1 4.7 %collective-permute-start.5 = (f32[32,640]{1,0:T(8,128)S(1)}, f32[32,640]{1,0:T(8,128)S(1)}, u32[]{:S(2)}, u32[]{:S(2)}) collective-permute-start(f32[32,640]{1,0:T(8,128)S(1)} %select_add_fusion), channel_id=1, source_target_pairs={{0,3},{1,2},{2,1},{3,0},{4,7},{5,6},{6,5},{7,4},{8,11},{9,10},{10,... | collective-permute-start | bytes 245768 | tf_op jit(solution)/shard_map/ppermute | solution.py:336
  28.8 4.5 %collective-permute-start.8 = (f32[32,640]{1,0:T(8,128)S(1)}, f32[32,640]{1,0:T(8,128)S(1)}, u32[]{:S(2)}, u32[]{:S(2)}) collective-permute-start(f32[32,640]{1,0:T(8,128)S(1)} %add_add_fusion), channel_id=1, source_target_pairs={{0,9},{1,8},{2,11},{3,10},{4,13},{5,12},{6,15},{7,14},{8,1},{9,0},... | collective-permute-start | bytes 245768 | tf_op jit(solution)/shard_map/ppermute | solution.py:336
  33.3 7.2 %collective-permute-start.9 = (f32[32,640]{1,0:T(8,128)S(1)}, f32[32,640]{1,0:T(8,128)S(1)}, u32[]{:S(2)}, u32[]{:S(2)}) collective-permute-start(f32[32,640]{1,0:T(8,128)S(1)} %add.89), channel_id=1, source_target_pairs={{0,17},{1,16},{2,19},{3,18},{4,21},{5,20},{6,23},{7,22},{8,25},{9,... | collective-permute-start | bytes 245768 | tf_op jit(solution)/shard_map/ppermute | solution.py:336
  40.5 1.3 %collective-permute-start.10 = (f32[32,640]{1,0:T(8,128)S(1)}, f32[32,640]{1,0:T(8,128)S(1)}, u32[]{:S(2)}, u32[]{:S(2)}) collective-permute-start(f32[32,640]{1,0:T(8,128)S(1)} %add.90), channel_id=1, source_target_pairs={{0,1},{1,0},{2,3},{3,2},{4,5},{5,4},{6,7},{7,6},{8,9},{9,8},{10,11... | collective-permute-start | bytes 245768 | tf_op jit(solution)/shard_map/ppermute | solution.py:336
  45.7 10.8 %collective-permute-start.12 = (bf16[64,1024]{1,0:T(8,128)(2,1)S(1)}, bf16[64,1024]{1,0:T(8,128)(2,1)S(1)}, u32[]{:S(2)}, u32[]{:S(2)}) collective-permute-start(bf16[64,1024]{1,0:T(8,128)(2,1)S(1)} %get-tuple-element.65), channel_id=1, source_target_pairs={{4,8},{8,4},{12,16},{16,12},{20,24},{24,20},{5,9},{9,5},{13,17},{1... | collective-permute-start | bytes 393224 | tf_op jit(solution)/shard_map/ppermute | solution.py:30
  46.4 9.4 %collective-permute-start.11 = (bf16[64,1024]{1,0:T(8,128)(2,1)S(1)}, bf16[64,1024]{1,0:T(8,128)(2,1)S(1)}, u32[]{:S(2)}, u32[]{:S(2)}) collective-permute-start(bf16[64,1024]{1,0:T(8,128)(2,1)S(1)} %get-tuple-element.66), channel_id=1, source_target_pairs={{0,4},{4,0},{8,12},{12,8},{16,20},{20,16},{24,28},{28,24},{1,5},{5... | collective-permute-start | bytes 393224 | tf_op jit(solution)/shard_map/ppermute | solution.py:27
  56.6 4.4 %collective-permute-start.14 = (bf16[64,512]{1,0:T(8,128)(2,1)S(1)}, bf16[64,512]{1,0:T(8,128)(2,1)S(1)}, u32[]{:S(2)}, u32[]{:S(2)}) collective-permute-start(bf16[64,512]{1,0:T(8,128)(2,1)S(1)} %get-tuple-element.79), channel_id=1, source_target_pairs={{1,2},{2,1},{0,3},{3,0},{5,6},{6,5},{4,7},{7,4},{9,10},{10,9},{8,1... | collective-permute-start | bytes 196616 | tf_op jit(solution)/shard_map/ppermute | solution.py:30
  57.5 3.4 %collective-permute-start.13 = (bf16[64,512]{1,0:T(8,128)(2,1)S(1)}, bf16[64,512]{1,0:T(8,128)(2,1)S(1)}, u32[]{:S(2)}, u32[]{:S(2)}) collective-permute-start(bf16[64,512]{1,0:T(8,128)(2,1)S(1)} %get-tuple-element.80), channel_id=1, source_target_pairs={{0,1},{1,0},{2,3},{3,2},{4,5},{5,4},{6,7},{7,6},{8,9},{9,8},{10,11... | collective-permute-start | bytes 196616 | tf_op jit(solution)/shard_map/ppermute | solution.py:27
  62.1 1.3 %collective-permute-start.15 = (f32[32,256]{1,0:T(8,128)S(1)}, f32[32,256]{1,0:T(8,128)S(1)}, u32[]{:S(2)}, u32[]{:S(2)}) collective-permute-start(f32[32,256]{1,0:T(8,128)S(1)} %slice_select_fusion.1), channel_id=1, source_target_pairs={{0,1},{1,0},{2,3},{3,2},{4,5},{5,4},{6,7},{7,6},{8,9},{9,8},{10,11... | collective-permute-start | bytes 98312 | tf_op jit(solution)/shard_map/ppermute | solution.py:336
  63.4 5.0 %collective-permute-start.18 = (f32[32,256]{1,0:T(8,128)S(1)}, f32[32,256]{1,0:T(8,128)S(1)}, u32[]{:S(2)}, u32[]{:S(2)}) collective-permute-start(f32[32,256]{1,0:T(8,128)S(1)} %select_add_fusion.1), channel_id=1, source_target_pairs={{0,6},{1,7},{2,4},{3,5},{4,2},{5,3},{6,0},{7,1},{8,14},{9,15},{10,... | collective-permute-start | bytes 98312 | tf_op jit(solution)/shard_map/ppermute | solution.py:336
  66.4 3.6 %collective-permute-start.17 = (f32[32,256]{1,0:T(8,128)S(1)}, f32[32,256]{1,0:T(8,128)S(1)}, u32[]{:S(2)}, u32[]{:S(2)}) collective-permute-start(f32[32,256]{1,0:T(8,128)S(1)} %select_add_fusion.1), channel_id=1, source_target_pairs={{0,5},{1,4},{2,7},{3,6},{4,1},{5,0},{6,3},{7,2},{8,13},{9,12},{10,... | collective-permute-start | bytes 98312 | tf_op jit(solution)/shard_map/ppermute | solution.py:336
  66.5 3.6 %collective-permute-start.16 = (f32[32,256]{1,0:T(8,128)S(1)}, f32[32,256]{1,0:T(8,128)S(1)}, u32[]{:S(2)}, u32[]{:S(2)}) collective-permute-start(f32[32,256]{1,0:T(8,128)S(1)} %select_add_fusion.1), channel_id=1, source_target_pairs={{0,3},{1,2},{2,1},{3,0},{4,7},{5,6},{6,5},{7,4},{8,11},{9,10},{10,... | collective-permute-start | bytes 98312 | tf_op jit(solution)/shard_map/ppermute | solution.py:336
  70.1 6.0 %collective-permute-start.21 = (f32[32,256]{1,0:T(8,128)S(1)}, f32[32,256]{1,0:T(8,128)S(1)}, u32[]{:S(2)}, u32[]{:S(2)}) collective-permute-start(f32[32,256]{1,0:T(8,128)S(1)} %add_add_fusion.2), channel_id=1, source_target_pairs={{0,24},{1,25},{2,26},{3,27},{4,28},{5,29},{6,30},{7,31},{8,16},{9,... | collective-permute-start | bytes 98312 | tf_op jit(solution)/shard_map/ppermute | solution.py:336
  72.5 4.4 %collective-permute-start.20 = (f32[32,256]{1,0:T(8,128)S(1)}, f32[32,256]{1,0:T(8,128)S(1)}, u32[]{:S(2)}, u32[]{:S(2)}) collective-permute-start(f32[32,256]{1,0:T(8,128)S(1)} %add_add_fusion.2), channel_id=1, source_target_pairs={{0,17},{1,16},{2,19},{3,18},{4,21},{5,20},{6,23},{7,22},{8,25},{9,... | collective-permute-start | bytes 98312 | tf_op jit(solution)/shard_map/ppermute | solution.py:336
  72.5 4.4 %collective-permute-start.19 = (f32[32,256]{1,0:T(8,128)S(1)}, f32[32,256]{1,0:T(8,128)S(1)}, u32[]{:S(2)}, u32[]{:S(2)}) collective-permute-start(f32[32,256]{1,0:T(8,128)S(1)} %add_add_fusion.2), channel_id=1, source_target_pairs={{0,9},{1,8},{2,11},{3,10},{4,13},{5,12},{6,15},{7,14},{8,1},{9,0},... | collective-permute-start | bytes 98312 | tf_op jit(solution)/shard_map/ppermute | solution.py:336
  76.9 1.3 %collective-permute-start.22 = (f32[32,256]{1,0:T(8,128)S(1)}, f32[32,256]{1,0:T(8,128)S(1)}, u32[]{:S(2)}, u32[]{:S(2)}) collective-permute-start(f32[32,256]{1,0:T(8,128)S(1)} %add_add_fusion.1), channel_id=1, source_target_pairs={{0,1},{1,0},{2,3},{3,2},{4,5},{5,4},{6,7},{7,6},{8,9},{9,8},{10,11... | collective-permute-start | bytes 98312 | tf_op jit(solution)/shard_map/ppermute | solution.py:336

commit v12 on v11

--- a/solution.py
+++ b/solution.py
@@ -17,35 +17,28 @@
     return lax.dot_general(left, right, dims, preferred_element_type=jnp.float32)
 
 
-def swaps(axis, upward, downward, closed):
+def swaps(axis, upward, downward, closed, beside=None):
     count = lax.axis_size(axis)
     me = lax.axis_index(axis)
     odd = me % 2 == 1
     pairs = [(i, (i - 1 ^ 1) + 1) for i in range(1, count - 1)]
     if closed:
         pairs += [(0, count - 1), (count - 1, 0)]
-    inner = lax.ppermute(
-        jnp.where(odd, downward, upward), axis, [(i, i ^ 1) for i in range(count)]
-    )
-    outer = lax.ppermute(jnp.where(odd, upward, downward), axis, pairs)
-
-    def sort(inner, outer):
-        if closed:
-            outer = jnp.where((me == 0) | (me == count - 1), 0, outer)
-        return jnp.where(odd, inner, outer), jnp.where(odd, outer, inner)
-
-    return inner, outer, sort
-
-
-def neighbours(block, span_x, span_y, depth, inner_image, meanwhile=()):
+    near, far = jnp.where(odd, downward, upward), jnp.where(odd, upward, downward)
+    inner = lax.ppermute(near, axis, [(i, i ^ 1) for i in range(count)])
+    far, beside = lax.optimization_barrier((far, beside))
+    outer = lax.ppermute(far, axis, pairs)
+    if closed:
+        outer = jnp.where((me == 0) | (me == count - 1), 0, outer)
+    return jnp.where(odd, inner, outer), jnp.where(odd, outer, inner), beside
+
+
+def neighbours(block, span_x, span_y, depth, beside=None, meanwhile=None):
     plane = span_y * depth
-    inner, outer, sort = swaps(
-        "slab", block[:, (span_x - 1) * plane :], block[:, :plane], False
-    )
-    inner, tied = lax.optimization_barrier((inner, block))
-    partial = inner_image(tied)
-    inner, outer, partial, meanwhile = lax.optimization_barrier((inner, outer, partial, meanwhile))
-    xlo, xhi = sort(inner, outer)
+    xlo, xhi, beside = swaps(
+        "slab", block[:, (span_x - 1) * plane :], block[:, :plane], False, beside
+    )
+    xlo, xhi, meanwhile = lax.optimization_barrier((xlo, xhi, meanwhile))
 
     def edge(row):
         at = row * depth
@@ -54,8 +47,8 @@
         parts += [xhi[:, at : at + depth]]
         return jnp.concatenate(parts, axis=1)
 
-    inner, outer, sort = swaps("col", edge(span_y - 1), edge(0), True)
-    return (xlo, xhi, *sort(inner, outer)), partial, meanwhile
+    ylo, yhi, _ = swaps("col", edge(span_y - 1), edge(0), True)
+    return (xlo, xhi, ylo, yhi), beside, meanwhile
 
 
 def coefficients_kernel(table, cells, coef):
@@ -336,7 +329,7 @@
     return lax.ppermute(part, axes, [(i, i ^ mask) for i in range(count)])
 
 
-def whole_sum(part, grouped):
+def whole_sum(part):
     cols = lax.axis_size("col")
     count = lax.axis_size("slab") * cols
     index = lax.axis_index("slab") * cols + lax.axis_index("col")
@@ -350,7 +343,7 @@
     part = jnp.where(upper, high, low) + partner(jnp.where(upper, low, high), 1)
     bit = 2
     while bit < count:
-        if 2 * bit < count and (grouped or bit == 2):
+        if 2 * bit < count:
             one, two, both = (partner(part, mask) for mask in (bit + 1, 2 * bit + 1, 3 * bit))
             part = (part + one) + (two + both)
             bit *= 4
@@ -403,17 +396,16 @@
             flops=2 * 27 * columns * cells,
         )[0]
 
-    around, partial, (coef_ready, stack, own) = neighbours(
-        basis[blocks - 1].reshape(columns, cells), *spans, inner_image, (coef, stack, own)
-    )
+    last = basis[blocks - 1].reshape(columns, cells)
+    around, partial, (stack, own) = neighbours(last, *spans, inner_image(last), (stack, own))
     packed = fields + columns + own.shape[1]
     image, cross = call(
         functools.partial(first_image_kernel, spans),
         "first_image",
         [((columns, cells), bf16), ((columns, packed), f32)],
-        coef_ready, stack, own, partial, *around,
-    )
-    cross = whole_sum(cross, False)
+        coef, stack, own, partial, *around,
+    )
+    cross = whole_sum(cross)
     block, proj, low, rest, square, inverse = call(
         functools.partial(first_solve_kernel, scale),
         "first_solve",
@@ -427,18 +419,18 @@
         [((fields, fields), bf16)] * 2,
         cross, rest, square, inverse,
     )
-    around, partial, _ = neighbours(block, *spans, inner_image)
+    around, _, _ = neighbours(block, *spans)
     image, cross = call(
         functools.partial(second_image_kernel, spans),
         "second_image",
         [((columns, cells), bf16), ((columns, fields + columns), f32)],
-        coef, stack, block, partial, *around,
+        coef, stack, block, inner_image(block), *around,
     )
     block, proj, low = call(
         functools.partial(second_solve_kernel, scale),
         "second_solve",
         [((columns, *spans), bf16), ((2, columns, fields), f32), ((2, columns, columns), f32)],
-        whole_sum(cross, True), *own, stack, block, image, proj, low,
+        whole_sum(cross), *own, stack, block, image, proj, low,
         scratch=[pltpu.VMEM((columns, cells), bf16)],
     )
     return block, jnp.swapaxes(proj, 1, 2), low

time: 82.9 us -> 79.1 us (0.954)
  waiting for transfers between devices: 36.3 us -> 29.8 us
  starting transfers between devices: 30.1 us -> 33 us
    ppermute x15 -> x16, starting transfers between devices: 16.1 us -> 21.9 us  [partner(): return lax.ppermute(part, axes, [(i, i ^ mask) for i in range(count)])]
    ppermute x8, waiting for transfers between devices: 14.1 us -> 10.3 us  [the longest x4 5.61 us: swaps(): inner = lax.ppermute(near, axis, [(i, i ^ 1) for i in range(count)])]
    ppermute x8, starting transfers between devices: 14.1 us -> 11.1 us  [the longest x4 8.72 us: swaps(): inner = lax.ppermute(near, axis, [(i, i ^ 1) for i in range(count)])]
    ppermute x15 -> x16, waiting for transfers between devices: 22.2 us -> 19.5 us  [partner(): return lax.ppermute(part, axes, [(i, i ^ mask) for i in range(count)])]
  transfers between devices with their start and end apart: 23 -> 24, of which waited for: 16 -> 16; matrix products, arithmetic and copies ran while one was open for 0% -> 0% of each run, Pallas kernels for 4% -> 4%
where the time goes in v12:
time: 79.1 us; the launch traced here: 78.9 us
  starting transfers between devices  33 us (42%)
  waiting for transfers between devices  29.8 us (38%)
  Pallas kernels  13.5 us (17%)
  local copies, waits for them, and re-layouts  1.47 us (2%)
  between operations  0.92 us (1%)
    ppermute x16, starting transfers between devices, partner(): return lax.ppermute(part, axes, [(i, i ^ mask) for i in range(count)])  21.9 us
    ppermute x16, waiting for transfers between devices, partner(): return lax.ppermute(part, axes, [(i, i ^ mask) for i in range(count)])  19.5 us
    pallas_call x8, Pallas kernels, call(): pl.pallas_call(kernel, out_shape=[jax.ShapeDtypeStruct(shape, dtype) for...  12.7 us
    ppermute x4, starting transfers between devices, swaps(): inner = lax.ppermute(near, axis, [(i, i ^ 1) for i in range(count)])  8.72 us
    ppermute x4, waiting for transfers between devices, swaps(): inner = lax.ppermute(near, axis, [(i, i ^ 1) for i in range(count)])  5.61 us
    ppermute x4, waiting for transfers between devices, swaps(): outer = lax.ppermute(far, axis, pairs)  4.69 us
    ppermute x4, starting transfers between devices, swaps(): outer = lax.ppermute(far, axis, pairs)  2.35 us
  transfers between devices with their start and end apart: 24, of which 16 were waited for; matrix products, arithmetic and copies ran while one was open for 0% of the time, Pallas kernels for 4%

profile of v12, /device:TPU:0, one launch (start us, length us, event | category | flops | bytes accessed | tf_op | source)
XLA Modules:
  0.0 78.9 jit_solution(16378090607211498397)
XLA Ops:
  0.6 0.0 slice-start
  0.7 0.9 %slice-done = bf16[1,64,2,8,128]{4,3,2,1,0:T(8,128)(2,1)S(1)} async-done(((bf16[3,64,2,8,128]{4,3,2,1,0:T(8,128)(2,1)}), bf16[1,64,2,8,128]{4,3,2,1,0:T(8,128)(2,1)S(1)}, s32[]{:S(2)}) %slice-start) | async-done | bytes 262168 | tf_op jit(solution)/shard_map/slice | solution.py:399
  1.6 0.1 reshape_squeeze.3.fields
  1.7 0.0 copy-start
  1.7 0.0 copy-start.1
  1.7 0.0 copy-start.2
  1.8 3.0 %collective-permute-start = (bf16[64,1024]{1,0:T(8,128)(2,1)S(1)}, bf16[64,1024]{1,0:T(8,128)(2,1)S(1)}, u32[]{:S(2)}, u32[]{:S(2)}) collective-permute-start(bf16[64,1024]{1,0:T(8,128)(2,1)S(1)} %get-tuple-element.64), channel_id=1, source_target_pairs={{0,4},{4,0},{8,12},{12,8},{16,20},{20,16},{24,28},{28,24},{1,5},{5... | collective-permute-start | bytes 393224 | tf_op jit(solution)/shard_map/ppermute | solution.py:28
  4.8 0.8 coefficients.1.coef
  5.6 0.7 inner_image.2.partial
  6.2 0.7 collective-permute-start.1
  6.9 0.3 reshape.13.stack
  7.3 0.6 stack_gram.1.own
  7.9 0.4 collective-permute-done
  8.3 0.0 collective-permute-done.1
  8.4 0.4 collective-permute-start.3
  8.8 1.5 %collective-permute-start.2 = (bf16[64,512]{1,0:T(8,128)(2,1)S(1)}, bf16[64,512]{1,0:T(8,128)(2,1)S(1)}, u32[]{:S(2)}, u32[]{:S(2)}) collective-permute-start(bf16[64,512]{1,0:T(8,128)(2,1)S(1)} %get-tuple-element.78), channel_id=1, source_target_pairs={{0,1},{1,0},{2,3},{3,2},{4,5},{5,4},{6,7},{7,6},{8,9},{9,8},{10,11... | collective-permute-start | bytes 196616 | tf_op jit(solution)/shard_map/ppermute | solution.py:28
  10.3 2.2 %collective-permute-done.3 = bf16[64,512]{1,0:T(8,128)(2,1)S(1)} collective-permute-done((bf16[64,512]{1,0:T(8,128)(2,1)S(1)}, bf16[64,512]{1,0:T(8,128)(2,1)S(1)}, u32[]{:S(2)}, u32[]{:S(2)}) %collective-permute-start.3) | collective-permute-done | bytes 65568 | tf_op jit(solution)/shard_map/ppermute | solution.py:30
  12.5 0.0 collective-permute-done.2
  12.5 1.1 %first_image.1 = (bf16[64,2048]{1,0:T(8,128)(2,1)S(1)}, f32[64,640]{1,0:T(8,128)S(1)}) custom-call(f32[27,16,128]{2,1,0:T(8,128)S(1)} %coefficients.1.coef, bf16[192,2048]{1,0:T(8,128)(2,1)S(1)} %reshape.13.stack, f32[64,384]{1,0:T(8,128)S(1)} %stack_gram.1.own, f32[64,2048]{1,0:T(8,128)S(1)} %inner_image.2.partial, ...), custom_call_target="tpu_custom_call" | custom-call | bytes 2449408 | tf_op jit(solution)/shard_map/first_image/pallas_call | solution.py:360
  13.7 0.2 collective-permute-start.4
  13.9 1.1 %collective-permute-done.4 = f32[32,640]{1,0:T(8,128)S(1)} collective-permute-done((f32[32,640]{1,0:T(8,128)S(1)}, f32[32,640]{1,0:T(8,128)S(1)}, u32[]{:S(2)}, u32[]{:S(2)}) %collective-permute-start.4) | collective-permute-done | bytes 81952 | tf_op jit(solution)/shard_map/ppermute | solution.py:329
  15.0 7.2 %collective-permute-start.7 = (f32[32,640]{1,0:T(8,128)S(1)}, f32[32,640]{1,0:T(8,128)S(1)}, u32[]{:S(2)}, u32[]{:S(2)}) collective-permute-start(f32[32,640]{1,0:T(8,128)S(1)} %select_add_fusion), channel_id=1, source_target_pairs={{0,6},{1,7},{2,4},{3,5},{4,2},{5,3},{6,0},{7,1},{8,14},{9,15},{10,... | collective-permute-start | bytes 245768 | tf_op jit(solution)/shard_map/ppermute | solution.py:329
  22.2 0.0 collective-permute-start.6
  22.2 0.6 collective-permute-start.5
  22.8 2.2 %collective-permute-done.7 = f32[32,640]{1,0:T(8,128)S(1)} collective-permute-done((f32[32,640]{1,0:T(8,128)S(1)}, f32[32,640]{1,0:T(8,128)S(1)}, u32[]{:S(2)}, u32[]{:S(2)}) %collective-permute-start.7) | collective-permute-done | bytes 81952 | tf_op jit(solution)/shard_map/ppermute | solution.py:329
  25.0 1.9 %collective-permute-done.6 = f32[32,640]{1,0:T(8,128)S(1)} collective-permute-done((f32[32,640]{1,0:T(8,128)S(1)}, f32[32,640]{1,0:T(8,128)S(1)}, u32[]{:S(2)}, u32[]{:S(2)}) %collective-permute-start.6) | collective-permute-done | bytes 81952 | tf_op jit(solution)/shard_map/ppermute | solution.py:329
  26.9 0.0 collective-permute-done.5
  26.9 4.7 %collective-permute-start.10 = (f32[32,640]{1,0:T(8,128)S(1)}, f32[32,640]{1,0:T(8,128)S(1)}, u32[]{:S(2)}, u32[]{:S(2)}) collective-permute-start(f32[32,640]{1,0:T(8,128)S(1)} %add_add_fusion.1), channel_id=1, source_target_pairs={{0,24},{1,25},{2,26},{3,27},{4,28},{5,29},{6,30},{7,31},{8,16},{9,... | collective-permute-start | bytes 245768 | tf_op jit(solution)/shard_map/ppermute | solution.py:329
  31.6 0.0 collective-permute-start.9
  31.6 0.4 collective-permute-start.8
  32.0 2.5 %collective-permute-done.10 = f32[32,640]{1,0:T(8,128)S(1)} collective-permute-done((f32[32,640]{1,0:T(8,128)S(1)}, f32[32,640]{1,0:T(8,128)S(1)}, u32[]{:S(2)}, u32[]{:S(2)}) %collective-permute-start.10) | collective-permute-done | bytes 81952 | tf_op jit(solution)/shard_map/ppermute | solution.py:329
  34.5 3.5 %collective-permute-done.9 = f32[32,640]{1,0:T(8,128)S(1)} collective-permute-done((f32[32,640]{1,0:T(8,128)S(1)}, f32[32,640]{1,0:T(8,128)S(1)}, u32[]{:S(2)}, u32[]{:S(2)}) %collective-permute-start.9) | collective-permute-done | bytes 81952 | tf_op jit(solution)/shard_map/ppermute | solution.py:329
  38.1 0.0 collective-permute-done.8
  38.1 0.6 collective-permute-start.11
  38.7 0.9 %collective-permute-done.11 = f32[32,640]{1,0:T(8,128)S(1)} collective-permute-done((f32[32,640]{1,0:T(8,128)S(1)}, f32[32,640]{1,0:T(8,128)S(1)}, u32[]{:S(2)}, u32[]{:S(2)}) %collective-permute-start.11) | collective-permute-done | bytes 81952 | tf_op jit(solution)/shard_map/ppermute | solution.py:329
  39.7 3.8 %first_solve.1 = (bf16[64,2048]{1,0:T(8,128)(2,1)S(1)}, f32[64,192]{1,0:T(8,128)S(1)}, f32[64,64]{1,0:T(8,128)S(1)}, f32[64,192]{1,0:T(8,128)S(1)}, f32[64,64]{1,0:T(8,128)S(1)}, /*index=5*/bf16[64,64]{1,0:T(8,128)(2,1)S(1)}) custom-call(f32[64,640]{1,0:T(8,128)S(1)} %pad_maximum_fusion.cross, bf16[192,2048]{1,0:T(8,128)(2,1)S(1)} %reshape.13.stack, ...), custom_call_target="tpu_custom_call" | custom-call | bytes 1613824 | tf_op jit(solution)/shard_map/first_solve/pallas_call | solution.py:360
  43.5 0.7 collective-permute-start.13
  44.2 3.7 %collective-permute-start.12 = (bf16[64,1024]{1,0:T(8,128)(2,1)S(1)}, bf16[64,1024]{1,0:T(8,128)(2,1)S(1)}, u32[]{:S(2)}, u32[]{:S(2)}) collective-permute-start(bf16[64,1024]{1,0:T(8,128)(2,1)S(1)} %get-tuple-element.56), channel_id=1, source_target_pairs={{0,4},{4,0},{8,12},{12,8},{16,20},{20,16},{24,28},{28,24},{1,5},{5... | collective-permute-start | bytes 393224 | tf_op jit(solution)/shard_map/ppermute | solution.py:28
  47.9 0.0 collective-permute-done.13
  47.9 5.2 %collective-permute-done.12 = bf16[64,1024]{1,0:T(8,128)(2,1)S(1)} collective-permute-done((bf16[64,1024]{1,0:T(8,128)(2,1)S(1)}, bf16[64,1024]{1,0:T(8,128)(2,1)S(1)}, u32[]{:S(2)}, u32[]{:S(2)}) %collective-permute-start.12) | collective-permute-done | bytes 131104 | tf_op jit(solution)/shard_map/ppermute | solution.py:28
  53.3 0.6 collective-permute-start.15
  53.9 0.5 collective-permute-start.14
  54.3 0.7 inner_image.3.partial
  55.0 2.5 %collective-permute-done.15 = bf16[64,512]{1,0:T(8,128)(2,1)S(1)} collective-permute-done((bf16[64,512]{1,0:T(8,128)(2,1)S(1)}, bf16[64,512]{1,0:T(8,128)(2,1)S(1)}, u32[]{:S(2)}, u32[]{:S(2)}) %collective-permute-start.15) | collective-permute-done | bytes 65568 | tf_op jit(solution)/shard_map/ppermute | solution.py:30
  57.5 0.0 collective-permute-done.14
  57.5 1.1 %second_image.1 = (bf16[64,2048]{1,0:T(8,128)(2,1)S(1)}, f32[64,256]{1,0:T(8,128)S(1)}) custom-call(f32[27,16,128]{2,1,0:T(8,128)S(1)} %coefficients.1.coef, bf16[192,2048]{1,0:T(8,128)(2,1)S(1)} %reshape.13.stack, bf16[64,2048]{1,0:T(8,128)(2,1)S(1)} %get-tuple-element.34.fields.block.last, f32[64,2048]{1,0:T(8,128)S(1)} %inner_image.3.partial, ...), custom_call_target="tpu_custom_call" | custom-call | bytes 2514944 | tf_op jit(solution)/shard_map/second_image/pallas_call | solution.py:360
  58.6 0.2 collective-permute-start.16
  58.8 1.1 %collective-permute-done.16 = f32[32,256]{1,0:T(8,128)S(1)} collective-permute-done((f32[32,256]{1,0:T(8,128)S(1)}, f32[32,256]{1,0:T(8,128)S(1)}, u32[]{:S(2)}, u32[]{:S(2)}) %collective-permute-start.16) | collective-permute-done | bytes 32800 | tf_op jit(solution)/shard_map/ppermute | solution.py:329
  59.9 2.8 %collective-permute-start.19 = (f32[32,256]{1,0:T(8,128)S(1)}, f32[32,256]{1,0:T(8,128)S(1)}, u32[]{:S(2)}, u32[]{:S(2)}) collective-permute-start(f32[32,256]{1,0:T(8,128)S(1)} %select_add_fusion.1), channel_id=1, source_target_pairs={{0,6},{1,7},{2,4},{3,5},{4,2},{5,3},{6,0},{7,1},{8,14},{9,15},{10,... | collective-permute-start | bytes 98312 | tf_op jit(solution)/shard_map/ppermute | solution.py:329
  62.7 0.0 collective-permute-start.18
  62.7 0.6 collective-permute-start.17
  63.4 1.4 %collective-permute-done.19 = f32[32,256]{1,0:T(8,128)S(1)} collective-permute-done((f32[32,256]{1,0:T(8,128)S(1)}, f32[32,256]{1,0:T(8,128)S(1)}, u32[]{:S(2)}, u32[]{:S(2)}) %collective-permute-start.19) | collective-permute-done | bytes 32800 | tf_op jit(solution)/shard_map/ppermute | solution.py:329
  64.7 1.6 %collective-permute-done.18 = f32[32,256]{1,0:T(8,128)S(1)} collective-permute-done((f32[32,256]{1,0:T(8,128)S(1)}, f32[32,256]{1,0:T(8,128)S(1)}, u32[]{:S(2)}, u32[]{:S(2)}) %collective-permute-start.18) | collective-permute-done | bytes 32800 | tf_op jit(solution)/shard_map/ppermute | solution.py:329
  66.4 0.0 collective-permute-done.17
  66.4 2.2 %collective-permute-start.22 = (f32[32,256]{1,0:T(8,128)S(1)}, f32[32,256]{1,0:T(8,128)S(1)}, u32[]{:S(2)}, u32[]{:S(2)}) collective-permute-start(f32[32,256]{1,0:T(8,128)S(1)} %add_add_fusion.3), channel_id=1, source_target_pairs={{0,24},{1,25},{2,26},{3,27},{4,28},{5,29},{6,30},{7,31},{8,16},{9,... | collective-permute-start | bytes 98312 | tf_op jit(solution)/shard_map/ppermute | solution.py:329
  68.6 0.8 collective-permute-start.21
  69.4 1.2 %collective-permute-start.20 = (f32[32,256]{1,0:T(8,128)S(1)}, f32[32,256]{1,0:T(8,128)S(1)}, u32[]{:S(2)}, u32[]{:S(2)}) collective-permute-start(f32[32,256]{1,0:T(8,128)S(1)} %add_add_fusion.3), channel_id=1, source_target_pairs={{0,9},{1,8},{2,11},{3,10},{4,13},{5,12},{6,15},{7,14},{8,1},{9,0},... | collective-permute-start | bytes 98312 | tf_op jit(solution)/shard_map/ppermute | solution.py:329
  70.6 1.8 %collective-permute-done.22 = f32[32,256]{1,0:T(8,128)S(1)} collective-permute-done((f32[32,256]{1,0:T(8,128)S(1)}, f32[32,256]{1,0:T(8,128)S(1)}, u32[]{:S(2)}, u32[]{:S(2)}) %collective-permute-start.22) | collective-permute-done | bytes 32800 | tf_op jit(solution)/shard_map/ppermute | solution.py:329
  72.4 0.8 %collective-permute-done.21 = f32[32,256]{1,0:T(8,128)S(1)} collective-permute-done((f32[32,256]{1,0:T(8,128)S(1)}, f32[32,256]{1,0:T(8,128)S(1)}, u32[]{:S(2)}, u32[]{:S(2)}) %collective-permute-start.21) | collective-permute-done | bytes 32800 | tf_op jit(solution)/shard_map/ppermute | solution.py:329
  73.2 0.0 collective-permute-done.20
  73.2 0.4 collective-permute-start.23
  73.7 0.4 next_gram.1
  74.1 0.5 collective-permute-done.23
  74.6 4.4 %second_solve.1 = (bf16[64,2,8,128]{3,2,1,0:T(8,128)(2,1)}, f32[2,64,192]{2,1,0:T(8,128)}, f32[2,64,64]{2,1,0:T(8,128)}) custom-call(f32[64,256]{1,0:T(8,128)S(1)} %pad_maximum_fusion.5.cross, bf16[192,192]{1,0:T(8,128)(2,1)S(1)} %get-tuple-element.41.own_high, bf16[192,192]{1,0:T(8,128)(2,1)S(1)} %get-tuple-element.42.own_low, ...), custom_call_target="tpu_custom_call" | custom-call | bytes 1982464 | tf_op jit(solution)/shard_map/second_solve/pallas_call | solution.py:360
  (28 shorter events, 0.4 us)
Async XLA Ops:
  0.6 1.0 %slice-start = ((bf16[3,64,2,8,128]{4,3,2,1,0:T(8,128)(2,1)}), bf16[1,64,2,8,128]{4,3,2,1,0:T(8,128)(2,1)S(1)}, s32[]{:S(2)}) async-start(bf16[3,64,2,8,128]{4,3,2,1,0:T(8,128)(2,1)} %param.3), calls=%async_computation | async-start | bytes 524288 | tf_op jit(solution)/shard_map/slice | solution.py:399
  1.7 3.1 %copy-start = (s32[2,8,128]{2,1,0:T(8,128)S(1)}, s32[2,8,128]{2,1,0:T(8,128)}, u32[]{:S(2)}) copy-start(s32[2,8,128]{2,1,0:T(8,128)} %param.4) | copy-start | bytes 24580
  1.7 3.1 %copy-start.1 = (f32[8,27]{1,0:T(8,128)S(1)}, f32[8,27]{1,0:T(8,128)}, u32[]{:S(2)}) copy-start(f32[8,27]{1,0:T(8,128)} %table.1) | copy-start | bytes 2596
  1.7 5.2 %copy-start.2 = (bf16[3,64,2,8,128]{4,3,2,1,0:T(8,128)(2,1)S(1)}, bf16[3,64,2,8,128]{4,3,2,1,0:T(8,128)(2,1)}, u32[]{:S(2)}) copy-start(bf16[3,64,2,8,128]{4,3,2,1,0:T(8,128)(2,1)} %param.3) | copy-start | bytes 2359300
  1.8 6.5 %collective-permute-start = (bf16[64,1024]{1,0:T(8,128)(2,1)S(1)}, bf16[64,1024]{1,0:T(8,128)(2,1)S(1)}, u32[]{:S(2)}, u32[]{:S(2)}) collective-permute-start(bf16[64,1024]{1,0:T(8,128)(2,1)S(1)} %get-tuple-element.64), channel_id=1, source_target_pairs={{0,4},{4,0},{8,12},{12,8},{16,20},{20,16},{24,28},{28,24},{1,5},{5... | collective-permute-start | bytes 393224 | tf_op jit(solution)/shard_map/ppermute | solution.py:28
  6.2 2.1 %collective-permute-start.1 = (bf16[64,1024]{1,0:T(8,128)(2,1)S(1)}, bf16[64,1024]{1,0:T(8,128)(2,1)S(1)}, u32[]{:S(2)}, u32[]{:S(2)}) collective-permute-start(bf16[64,1024]{1,0:T(8,128)(2,1)S(1)} %get-tuple-element.26), channel_id=1, source_target_pairs={{4,8},{8,4},{12,16},{16,12},{20,24},{24,20},{5,9},{9,5},{13,17},{1... | collective-permute-start | bytes 393224 | tf_op jit(solution)/shard_map/ppermute | solution.py:30
  8.4 4.1 %collective-permute-start.3 = (bf16[64,512]{1,0:T(8,128)(2,1)S(1)}, bf16[64,512]{1,0:T(8,128)(2,1)S(1)}, u32[]{:S(2)}, u32[]{:S(2)}) collective-permute-start(bf16[64,512]{1,0:T(8,128)(2,1)S(1)} %get-tuple-element.77), channel_id=1, source_target_pairs={{1,2},{2,1},{0,3},{3,0},{5,6},{6,5},{4,7},{7,4},{9,10},{10,9},{8,1... | collective-permute-start | bytes 196616 | tf_op jit(solution)/shard_map/ppermute | solution.py:30
  8.8 3.7 %collective-permute-start.2 = (bf16[64,512]{1,0:T(8,128)(2,1)S(1)}, bf16[64,512]{1,0:T(8,128)(2,1)S(1)}, u32[]{:S(2)}, u32[]{:S(2)}) collective-permute-start(bf16[64,512]{1,0:T(8,128)(2,1)S(1)} %get-tuple-element.78), channel_id=1, source_target_pairs={{0,1},{1,0},{2,3},{3,2},{4,5},{5,4},{6,7},{7,6},{8,9},{9,8},{10,11... | collective-permute-start | bytes 196616 | tf_op jit(solution)/shard_map/ppermute | solution.py:28
  13.7 1.3 %collective-permute-start.4 = (f32[32,640]{1,0:T(8,128)S(1)}, f32[32,640]{1,0:T(8,128)S(1)}, u32[]{:S(2)}, u32[]{:S(2)}) collective-permute-start(f32[32,640]{1,0:T(8,128)S(1)} %slice_select_fusion), channel_id=1, source_target_pairs={{0,1},{1,0},{2,3},{3,2},{4,5},{5,4},{6,7},{7,6},{8,9},{9,8},{10,11... | collective-permute-start | bytes 245768 | tf_op jit(solution)/shard_map/ppermute | solution.py:329
  15.0 10.0 %collective-permute-start.7 = (f32[32,640]{1,0:T(8,128)S(1)}, f32[32,640]{1,0:T(8,128)S(1)}, u32[]{:S(2)}, u32[]{:S(2)}) collective-permute-start(f32[32,640]{1,0:T(8,128)S(1)} %select_add_fusion), channel_id=1, source_target_pairs={{0,6},{1,7},{2,4},{3,5},{4,2},{5,3},{6,0},{7,1},{8,14},{9,15},{10,... | collective-permute-start | bytes 245768 | tf_op jit(solution)/shard_map/ppermute | solution.py:329
  22.2 4.7 %collective-permute-start.6 = (f32[32,640]{1,0:T(8,128)S(1)}, f32[32,640]{1,0:T(8,128)S(1)}, u32[]{:S(2)}, u32[]{:S(2)}) collective-permute-start(f32[32,640]{1,0:T(8,128)S(1)} %select_add_fusion), channel_id=1, source_target_pairs={{0,5},{1,4},{2,7},{3,6},{4,1},{5,0},{6,3},{7,2},{8,13},{9,12},{10,... | collective-permute-start | bytes 245768 | tf_op jit(solution)/shard_map/ppermute | solution.py:329
  22.2 4.7 %collective-permute-start.5 = (f32[32,640]{1,0:T(8,128)S(1)}, f32[32,640]{1,0:T(8,128)S(1)}, u32[]{:S(2)}, u32[]{:S(2)}) collective-permute-start(f32[32,640]{1,0:T(8,128)S(1)} %select_add_fusion), channel_id=1, source_target_pairs={{0,3},{1,2},{2,1},{3,0},{4,7},{5,6},{6,5},{7,4},{8,11},{9,10},{10,... | collective-permute-start | bytes 245768 | tf_op jit(solution)/shard_map/ppermute | solution.py:329
  26.9 7.6 %collective-permute-start.10 = (f32[32,640]{1,0:T(8,128)S(1)}, f32[32,640]{1,0:T(8,128)S(1)}, u32[]{:S(2)}, u32[]{:S(2)}) collective-permute-start(f32[32,640]{1,0:T(8,128)S(1)} %add_add_fusion.1), channel_id=1, source_target_pairs={{0,24},{1,25},{2,26},{3,27},{4,28},{5,29},{6,30},{7,31},{8,16},{9,... | collective-permute-start | bytes 245768 | tf_op jit(solution)/shard_map/ppermute | solution.py:329
  31.6 6.4 %collective-permute-start.9 = (f32[32,640]{1,0:T(8,128)S(1)}, f32[32,640]{1,0:T(8,128)S(1)}, u32[]{:S(2)}, u32[]{:S(2)}) collective-permute-start(f32[32,640]{1,0:T(8,128)S(1)} %add_add_fusion.1), channel_id=1, source_target_pairs={{0,17},{1,16},{2,19},{3,18},{4,21},{5,20},{6,23},{7,22},{8,25},{9,... | collective-permute-start | bytes 245768 | tf_op jit(solution)/shard_map/ppermute | solution.py:329
  31.6 6.4 %collective-permute-start.8 = (f32[32,640]{1,0:T(8,128)S(1)}, f32[32,640]{1,0:T(8,128)S(1)}, u32[]{:S(2)}, u32[]{:S(2)}) collective-permute-start(f32[32,640]{1,0:T(8,128)S(1)} %add_add_fusion.1), channel_id=1, source_target_pairs={{0,9},{1,8},{2,11},{3,10},{4,13},{5,12},{6,15},{7,14},{8,1},{9,0},... | collective-permute-start | bytes 245768 | tf_op jit(solution)/shard_map/ppermute | solution.py:329
  38.1 1.5 %collective-permute-start.11 = (f32[32,640]{1,0:T(8,128)S(1)}, f32[32,640]{1,0:T(8,128)S(1)}, u32[]{:S(2)}, u32[]{:S(2)}) collective-permute-start(f32[32,640]{1,0:T(8,128)S(1)} %add_add_fusion), channel_id=1, source_target_pairs={{0,1},{1,0},{2,3},{3,2},{4,5},{5,4},{6,7},{7,6},{8,9},{9,8},{10,11... | collective-permute-start | bytes 245768 | tf_op jit(solution)/shard_map/ppermute | solution.py:329
  43.5 4.4 %collective-permute-start.13 = (bf16[64,1024]{1,0:T(8,128)(2,1)S(1)}, bf16[64,1024]{1,0:T(8,128)(2,1)S(1)}, u32[]{:S(2)}, u32[]{:S(2)}) collective-permute-start(bf16[64,1024]{1,0:T(8,128)(2,1)S(1)} %get-tuple-element.55), channel_id=1, source_target_pairs={{4,8},{8,4},{12,16},{16,12},{20,24},{24,20},{5,9},{9,5},{13,17},{1... | collective-permute-start | bytes 393224 | tf_op jit(solution)/shard_map/ppermute | solution.py:30
  44.2 9.0 %collective-permute-start.12 = (bf16[64,1024]{1,0:T(8,128)(2,1)S(1)}, bf16[64,1024]{1,0:T(8,128)(2,1)S(1)}, u32[]{:S(2)}, u32[]{:S(2)}) collective-permute-start(bf16[64,1024]{1,0:T(8,128)(2,1)S(1)} %get-tuple-element.56), channel_id=1, source_target_pairs={{0,4},{4,0},{8,12},{12,8},{16,20},{20,16},{24,28},{28,24},{1,5},{5... | collective-permute-start | bytes 393224 | tf_op jit(solution)/shard_map/ppermute | solution.py:28
  53.3 4.2 %collective-permute-start.15 = (bf16[64,512]{1,0:T(8,128)(2,1)S(1)}, bf16[64,512]{1,0:T(8,128)(2,1)S(1)}, u32[]{:S(2)}, u32[]{:S(2)}) collective-permute-start(bf16[64,512]{1,0:T(8,128)(2,1)S(1)} %get-tuple-element.69), channel_id=1, source_target_pairs={{1,2},{2,1},{0,3},{3,0},{5,6},{6,5},{4,7},{7,4},{9,10},{10,9},{8,1... | collective-permute-start | bytes 196616 | tf_op jit(solution)/shard_map/ppermute | solution.py:30
  53.9 3.7 %collective-permute-start.14 = (bf16[64,512]{1,0:T(8,128)(2,1)S(1)}, bf16[64,512]{1,0:T(8,128)(2,1)S(1)}, u32[]{:S(2)}, u32[]{:S(2)}) collective-permute-start(bf16[64,512]{1,0:T(8,128)(2,1)S(1)} %get-tuple-element.70), channel_id=1, source_target_pairs={{0,1},{1,0},{2,3},{3,2},{4,5},{5,4},{6,7},{7,6},{8,9},{9,8},{10,11... | collective-permute-start | bytes 196616 | tf_op jit(solution)/shard_map/ppermute | solution.py:28
  58.6 1.3 %collective-permute-start.16 = (f32[32,256]{1,0:T(8,128)S(1)}, f32[32,256]{1,0:T(8,128)S(1)}, u32[]{:S(2)}, u32[]{:S(2)}) collective-permute-start(f32[32,256]{1,0:T(8,128)S(1)} %slice_select_fusion.1), channel_id=1, source_target_pairs={{0,1},{1,0},{2,3},{3,2},{4,5},{5,4},{6,7},{7,6},{8,9},{9,8},{10,11... | collective-permute-start | bytes 98312 | tf_op jit(solution)/shard_map/ppermute | solution.py:329
  59.9 4.8 %collective-permute-start.19 = (f32[32,256]{1,0:T(8,128)S(1)}, f32[32,256]{1,0:T(8,128)S(1)}, u32[]{:S(2)}, u32[]{:S(2)}) collective-permute-start(f32[32,256]{1,0:T(8,128)S(1)} %select_add_fusion.1), channel_id=1, source_target_pairs={{0,6},{1,7},{2,4},{3,5},{4,2},{5,3},{6,0},{7,1},{8,14},{9,15},{10,... | collective-permute-start | bytes 98312 | tf_op jit(solution)/shard_map/ppermute | solution.py:329
  62.7 3.6 %collective-permute-start.18 = (f32[32,256]{1,0:T(8,128)S(1)}, f32[32,256]{1,0:T(8,128)S(1)}, u32[]{:S(2)}, u32[]{:S(2)}) collective-permute-start(f32[32,256]{1,0:T(8,128)S(1)} %select_add_fusion.1), channel_id=1, source_target_pairs={{0,5},{1,4},{2,7},{3,6},{4,1},{5,0},{6,3},{7,2},{8,13},{9,12},{10,... | collective-permute-start | bytes 98312 | tf_op jit(solution)/shard_map/ppermute | solution.py:329
  62.7 3.6 %collective-permute-start.17 = (f32[32,256]{1,0:T(8,128)S(1)}, f32[32,256]{1,0:T(8,128)S(1)}, u32[]{:S(2)}, u32[]{:S(2)}) collective-permute-start(f32[32,256]{1,0:T(8,128)S(1)} %select_add_fusion.1), channel_id=1, source_target_pairs={{0,3},{1,2},{2,1},{3,0},{4,7},{5,6},{6,5},{7,4},{8,11},{9,10},{10,... | collective-permute-start | bytes 98312 | tf_op jit(solution)/shard_map/ppermute | solution.py:329
  66.4 6.0 %collective-permute-start.22 = (f32[32,256]{1,0:T(8,128)S(1)}, f32[32,256]{1,0:T(8,128)S(1)}, u32[]{:S(2)}, u32[]{:S(2)}) collective-permute-start(f32[32,256]{1,0:T(8,128)S(1)} %add_add_fusion.3), channel_id=1, source_target_pairs={{0,24},{1,25},{2,26},{3,27},{4,28},{5,29},{6,30},{7,31},{8,16},{9,... | collective-permute-start | bytes 98312 | tf_op jit(solution)/shard_map/ppermute | solution.py:329
  68.6 4.6 %collective-permute-start.21 = (f32[32,256]{1,0:T(8,128)S(1)}, f32[32,256]{1,0:T(8,128)S(1)}, u32[]{:S(2)}, u32[]{:S(2)}) collective-permute-start(f32[32,256]{1,0:T(8,128)S(1)} %add_add_fusion.3), channel_id=1, source_target_pairs={{0,17},{1,16},{2,19},{3,18},{4,21},{5,20},{6,23},{7,22},{8,25},{9,... | collective-permute-start | bytes 98312 | tf_op jit(solution)/shard_map/ppermute | solution.py:329
  69.4 3.9 %collective-permute-start.20 = (f32[32,256]{1,0:T(8,128)S(1)}, f32[32,256]{1,0:T(8,128)S(1)}, u32[]{:S(2)}, u32[]{:S(2)}) collective-permute-start(f32[32,256]{1,0:T(8,128)S(1)} %add_add_fusion.3), channel_id=1, source_target_pairs={{0,9},{1,8},{2,11},{3,10},{4,13},{5,12},{6,15},{7,14},{8,1},{9,0},... | collective-permute-start | bytes 98312 | tf_op jit(solution)/shard_map/ppermute | solution.py:329
  73.2 1.3 %collective-permute-start.23 = (f32[32,256]{1,0:T(8,128)S(1)}, f32[32,256]{1,0:T(8,128)S(1)}, u32[]{:S(2)}, u32[]{:S(2)}) collective-permute-start(f32[32,256]{1,0:T(8,128)S(1)} %add_add_fusion.2), channel_id=1, source_target_pairs={{0,1},{1,0},{2,3},{3,2},{4,5},{5,4},{6,7},{7,6},{8,9},{9,8},{10,11... | collective-permute-start | bytes 98312 | tf_op jit(solution)/shard_map/ppermute | solution.py:329

commit v13 on v12

--- a/solution.py
+++ b/solution.py
@@ -302,25 +302,36 @@
 
 
 def second_solve_kernel(
-    scale, cross, own_high, own_low, stack, last, image, proj_in, low_in, result, proj, low, block
+    scale, cross, own_high, own_low, stack, last, image, proj_in, low_in, result_out, proj_out,
+    low_out, block, result, proj, low, done,
 ):
     columns = image.shape[0]
     kept = stack.shape[0] - columns
     used, proj[1], _, square = project(cross[...], (own_high[...], own_low[...]), scale)
     proj[0] = proj_in[...]
-    low[0] = low_in[...]
+    copies = [pltpu.make_async_copy(proj, proj_out, done.at[0])]
+    copies[0].start()
     both = jnp.concatenate(used, axis=0)
     moved = dot(both[:, :kept], stack[columns:]) + dot(both[:, kept:], last[...])
     w = image[...].astype(jnp.float32) - moved[:columns] - moved[columns:]
     block[...] = w.astype(jnp.bfloat16)
     upper, inverse = factor(square)
-    low[1] = upper.T
     inverse = inverse.astype(jnp.bfloat16)
     _, span_x, span_y, depth = result.shape
     plane = span_y * depth
     for x in range(span_x):
         part = dot(inverse, block[:, x * plane : (x + 1) * plane])
         result[:, x] = part.reshape(columns, span_y, depth).astype(jnp.bfloat16)
+        copies.append(
+            pltpu.make_async_copy(result.at[:, x], result_out.at[:, x], done.at[2 + x])
+        )
+        copies[-1].start()
+    low[0] = low_in[...]
+    low[1] = upper.T
+    copies.append(pltpu.make_async_copy(low, low_out, done.at[1]))
+    copies[-1].start()
+    for copy in copies:
+        copy.wait()
 
 
 def partner(part, mask):
@@ -329,7 +340,7 @@
     return lax.ppermute(part, axes, [(i, i ^ mask) for i in range(count)])
 
 
-def whole_sum(part):
+def whole_sum(part, scattered):
     cols = lax.axis_size("col")
     count = lax.axis_size("slab") * cols
     index = lax.axis_index("slab") * cols + lax.axis_index("col")
@@ -341,27 +352,42 @@
     half = part.shape[0] // 2
     low, high = part[:half], part[half:]
     part = jnp.where(upper, high, low) + partner(jnp.where(upper, low, high), 1)
+
+    def by_place(four):
+        odd, later = index // 2 % 2 == 1, index // 4 % 2 == 1
+        four = [jnp.where(odd, four[i ^ 1], four[i]) for i in range(4)]
+        return [jnp.where(later, four[i ^ 2], four[i]) for i in range(4)]
+
+    def group(four, bit):
+        return [partner(four[i], mask) for i, mask in ((1, bit + 1), (2, 2 * bit + 1), (3, 3 * bit))]
+
     bit = 2
+    if scattered:
+        mine = by_place(jnp.split(part, 4, axis=0))
+        one, two, both = group(mine, bit)
+        part = (mine[0] + one) + (two + both)
+        bit = 8
     while bit < count:
         if 2 * bit < count:
-            one, two, both = (partner(part, mask) for mask in (bit + 1, 2 * bit + 1, 3 * bit))
+            one, two, both = group([part] * 4, bit)
             part = (part + one) + (two + both)
-            bit *= 4
         else:
             part = part + partner(part, bit + 1)
-            bit *= 2
+        bit *= 4
+    if scattered:
+        part = jnp.concatenate(by_place([part, *group([part] * 4, 2)]), axis=0)
     other = partner(part, 1)
     return jnp.concatenate([jnp.where(upper, other, part), jnp.where(upper, part, other)], axis=0)
 
 
-def call(kernel, name, outs, *args, flops=0, scratch=()):
+def call(kernel, name, outs, *args, flops=0, scratch=(), place=pltpu.VMEM):
     moved = sum(math.prod(arg.shape) * arg.dtype.itemsize for arg in args)
     moved += sum(math.prod(shape) * jnp.dtype(dtype).itemsize for shape, dtype in outs)
     return pl.pallas_call(
         kernel,
         out_shape=[jax.ShapeDtypeStruct(shape, dtype) for shape, dtype in outs],
         in_specs=[pl.BlockSpec(memory_space=pltpu.VMEM)] * len(args),
-        out_specs=[pl.BlockSpec(memory_space=pltpu.VMEM)] * len(outs),
+        out_specs=[pl.BlockSpec(memory_space=place)] * len(outs),
         scratch_shapes=scratch,
         compiler_params=pltpu.CompilerParams(vmem_limit_bytes=24 * 1024 * 1024),
         cost_estimate=pl.CostEstimate(flops=flops, bytes_accessed=moved, transcendentals=0),
@@ -405,7 +431,7 @@
         [((columns, cells), bf16), ((columns, packed), f32)],
         coef, stack, own, partial, *around,
     )
-    cross = whole_sum(cross)
+    cross = whole_sum(cross, True)
     block, proj, low, rest, square, inverse = call(
         functools.partial(first_solve_kernel, scale),
         "first_solve",
@@ -426,12 +452,18 @@
         [((columns, cells), bf16), ((columns, fields + columns), f32)],
         coef, stack, block, inner_image(block), *around,
     )
+    outs = [((columns, *spans), bf16), ((2, columns, fields), f32), ((2, columns, columns), f32)]
     block, proj, low = call(
         functools.partial(second_solve_kernel, scale),
         "second_solve",
-        [((columns, *spans), bf16), ((2, columns, fields), f32), ((2, columns, columns), f32)],
-        whole_sum(cross), *own, stack, block, image, proj, low,
-        scratch=[pltpu.VMEM((columns, cells), bf16)],
+        outs,
+        whole_sum(cross, False), *own, stack, block, image, proj, low,
+        place=pl.ANY,
+        scratch=[
+            pltpu.VMEM((columns, cells), bf16),
+            *(pltpu.VMEM(shape, dtype) for shape, dtype in outs),
+            pltpu.SemaphoreType.DMA((2 + span_x,)),
+        ],
     )
     return block, jnp.swapaxes(proj, 1, 2), low
 

time: 79.1 us -> 82.1 us (1.038)
  waiting for transfers between devices: 29.8 us -> 32 us
    ppermute x16 -> x19, starting transfers between devices: 21.9 us -> 24 us  [partner(): return lax.ppermute(part, axes, [(i, i ^ mask) for i in range(count)])]
    ppermute x16 -> x19, waiting for transfers between devices: 19.5 us -> 21.3 us  [partner(): return lax.ppermute(part, axes, [(i, i ^ mask) for i in range(count)])]
    ppermute x4, starting transfers between devices: 8.72 us -> 7.47 us  [swaps(): inner = lax.ppermute(near, axis, [(i, i ^ 1) for i in range(count)])]
  transfers between devices with their start and end apart: 24 -> 27, of which waited for: 16 -> 19; matrix products, arithmetic and copies ran while one was open for 0% -> 0% of each run, Pallas kernels for 4% -> 4%
where the time goes in v13:
time: 82.1 us; the launch traced here: 82 us
  starting transfers between devices  33.7 us (41%)
  waiting for transfers between devices  32 us (39%)
  Pallas kernels  13.5 us (16%)
  local copies, waits for them, and re-layouts  1.47 us (2%)
  between operations  0.95 us (1%)
    ppermute x19, starting transfers between devices, partner(): return lax.ppermute(part, axes, [(i, i ^ mask) for i in range(count)])  24 us
    ppermute x19, waiting for transfers between devices, partner(): return lax.ppermute(part, axes, [(i, i ^ mask) for i in range(count)])  21.3 us
    pallas_call x8, Pallas kernels, call(): pl.pallas_call(kernel, out_shape=[jax.ShapeDtypeStruct(shape, dtype) for...  12.7 us
    ppermute x4, starting transfers between devices, swaps(): inner = lax.ppermute(near, axis, [(i, i ^ 1) for i in range(count)])  7.47 us
    ppermute x4, waiting for transfers between devices, swaps(): inner = lax.ppermute(near, axis, [(i, i ^ 1) for i in range(count)])  5.94 us
    ppermute x4, waiting for transfers between devices, swaps(): outer = lax.ppermute(far, axis, pairs)  4.72 us
    ppermute x4, starting transfers between devices, swaps(): outer = lax.ppermute(far, axis, pairs)  2.32 us
  transfers between devices with their start and end apart: 27, of which 19 were waited for; matrix products, arithmetic and copies ran while one was open for 0% of the time, Pallas kernels for 4%

profile of v13, /device:TPU:0, one launch (start us, length us, event | category | flops | bytes accessed | tf_op | source)
XLA Modules:
  0.0 82.0 jit_solution(3791764533863569195)
XLA Ops:
  0.6 0.0 slice-start
  0.7 0.9 %slice-done = bf16[1,64,2,8,128]{4,3,2,1,0:T(8,128)(2,1)S(1)} async-done(((bf16[3,64,2,8,128]{4,3,2,1,0:T(8,128)(2,1)}), bf16[1,64,2,8,128]{4,3,2,1,0:T(8,128)(2,1)S(1)}, s32[]{:S(2)}) %slice-start) | async-done | bytes 262168 | tf_op jit(solution)/shard_map/slice | solution.py:425
  1.6 0.1 reshape_squeeze.3.fields
  1.7 0.0 copy-start
  1.7 0.0 copy-start.1
  1.7 0.0 copy-start.2
  1.8 3.0 %collective-permute-start = (bf16[64,1024]{1,0:T(8,128)(2,1)S(1)}, bf16[64,1024]{1,0:T(8,128)(2,1)S(1)}, u32[]{:S(2)}, u32[]{:S(2)}) collective-permute-start(bf16[64,1024]{1,0:T(8,128)(2,1)S(1)} %get-tuple-element.64), channel_id=1, source_target_pairs={{0,4},{4,0},{8,12},{12,8},{16,20},{20,16},{24,28},{28,24},{1,5},{5... | collective-permute-start | bytes 393224 | tf_op jit(solution)/shard_map/ppermute | solution.py:28
  4.8 0.8 coefficients.1.coef
  5.6 0.7 inner_image.2.partial
  6.2 0.7 collective-permute-start.1
  6.9 0.3 reshape.13.stack
  7.3 0.6 stack_gram.1.own
  7.9 0.4 collective-permute-done
  8.3 0.0 collective-permute-done.1
  8.4 0.4 collective-permute-start.3
  8.8 1.5 %collective-permute-start.2 = (bf16[64,512]{1,0:T(8,128)(2,1)S(1)}, bf16[64,512]{1,0:T(8,128)(2,1)S(1)}, u32[]{:S(2)}, u32[]{:S(2)}) collective-permute-start(bf16[64,512]{1,0:T(8,128)(2,1)S(1)} %get-tuple-element.78), channel_id=1, source_target_pairs={{0,1},{1,0},{2,3},{3,2},{4,5},{5,4},{6,7},{7,6},{8,9},{9,8},{10,11... | collective-permute-start | bytes 196616 | tf_op jit(solution)/shard_map/ppermute | solution.py:28
  10.3 2.2 %collective-permute-done.3 = bf16[64,512]{1,0:T(8,128)(2,1)S(1)} collective-permute-done((bf16[64,512]{1,0:T(8,128)(2,1)S(1)}, bf16[64,512]{1,0:T(8,128)(2,1)S(1)}, u32[]{:S(2)}, u32[]{:S(2)}) %collective-permute-start.3) | collective-permute-done | bytes 65568 | tf_op jit(solution)/shard_map/ppermute | solution.py:30
  12.5 0.0 collective-permute-done.2
  12.5 1.1 %first_image.1 = (bf16[64,2048]{1,0:T(8,128)(2,1)S(1)}, f32[64,640]{1,0:T(8,128)S(1)}) custom-call(f32[27,16,128]{2,1,0:T(8,128)S(1)} %coefficients.1.coef, bf16[192,2048]{1,0:T(8,128)(2,1)S(1)} %reshape.13.stack, f32[64,384]{1,0:T(8,128)S(1)} %stack_gram.1.own, f32[64,2048]{1,0:T(8,128)S(1)} %inner_image.2.partial, ...), custom_call_target="tpu_custom_call" | custom-call | bytes 2449408 | tf_op jit(solution)/shard_map/first_image/pallas_call | solution.py:386
  13.7 0.2 collective-permute-start.4
  13.9 1.1 %collective-permute-done.4 = f32[32,640]{1,0:T(8,128)S(1)} collective-permute-done((f32[32,640]{1,0:T(8,128)S(1)}, f32[32,640]{1,0:T(8,128)S(1)}, u32[]{:S(2)}, u32[]{:S(2)}) %collective-permute-start.4) | collective-permute-done | bytes 81952 | tf_op jit(solution)/shard_map/ppermute | solution.py:340
  15.0 1.2 %collective-permute-start.5 = (f32[8,640]{1,0:T(8,128)S(1)}, f32[8,640]{1,0:T(8,128)S(1)}, u32[]{:S(2)}, u32[]{:S(2)}) collective-permute-start(f32[8,640]{1,0:T(8,128)S(1)} %get-tuple-element.87), channel_id=1, source_target_pairs={{0,3},{1,2},{2,1},{3,0},{4,7},{5,6},{6,5},{7,4},{8,11},{9,10},{10,... | collective-permute-start | bytes 61448 | tf_op jit(solution)/shard_map/ppermute | solution.py:340
  16.3 6.3 %collective-permute-start.6 = (f32[8,640]{1,0:T(8,128)S(1)}, f32[8,640]{1,0:T(8,128)S(1)}, u32[]{:S(2)}, u32[]{:S(2)}) collective-permute-start(f32[8,640]{1,0:T(8,128)S(1)} %get-tuple-element.88), channel_id=1, source_target_pairs={{0,5},{1,4},{2,7},{3,6},{4,1},{5,0},{6,3},{7,2},{8,13},{9,12},{10,... | collective-permute-start | bytes 61448 | tf_op jit(solution)/shard_map/ppermute | solution.py:340
  22.5 0.6 collective-permute-start.7
  23.1 0.9 %collective-permute-done.6 = f32[8,640]{1,0:T(8,128)S(1)} collective-permute-done((f32[8,640]{1,0:T(8,128)S(1)}, f32[8,640]{1,0:T(8,128)S(1)}, u32[]{:S(2)}, u32[]{:S(2)}) %collective-permute-start.6) | collective-permute-done | bytes 20512 | tf_op jit(solution)/shard_map/ppermute | solution.py:340
  24.0 3.2 %collective-permute-done.7 = f32[8,640]{1,0:T(8,128)S(1)} collective-permute-done((f32[8,640]{1,0:T(8,128)S(1)}, f32[8,640]{1,0:T(8,128)S(1)}, u32[]{:S(2)}, u32[]{:S(2)}) %collective-permute-start.7) | collective-permute-done | bytes 20512 | tf_op jit(solution)/shard_map/ppermute | solution.py:340
  27.2 2.9 %collective-permute-start.10 = (f32[8,640]{1,0:T(8,128)S(1)}, f32[8,640]{1,0:T(8,128)S(1)}, u32[]{:S(2)}, u32[]{:S(2)}) collective-permute-start(f32[8,640]{1,0:T(8,128)S(1)} %add_add_fusion.3), channel_id=1, source_target_pairs={{0,24},{1,25},{2,26},{3,27},{4,28},{5,29},{6,30},{7,31},{8,16},{9,... | collective-permute-start | bytes 61448 | tf_op jit(solution)/shard_map/ppermute | solution.py:340
  30.1 1.3 %collective-permute-start.8 = (f32[8,640]{1,0:T(8,128)S(1)}, f32[8,640]{1,0:T(8,128)S(1)}, u32[]{:S(2)}, u32[]{:S(2)}) collective-permute-start(f32[8,640]{1,0:T(8,128)S(1)} %add_add_fusion.3), channel_id=1, source_target_pairs={{0,9},{1,8},{2,11},{3,10},{4,13},{5,12},{6,15},{7,14},{8,1},{9,0},... | collective-permute-start | bytes 61448 | tf_op jit(solution)/shard_map/ppermute | solution.py:340
  31.4 1.5 %collective-permute-done.10 = f32[8,640]{1,0:T(8,128)S(1)} collective-permute-done((f32[8,640]{1,0:T(8,128)S(1)}, f32[8,640]{1,0:T(8,128)S(1)}, u32[]{:S(2)}, u32[]{:S(2)}) %collective-permute-start.10) | collective-permute-done | bytes 20512 | tf_op jit(solution)/shard_map/ppermute | solution.py:340
  32.9 1.3 %collective-permute-done.9 = f32[8,640]{1,0:T(8,128)S(1)} collective-permute-done((f32[8,640]{1,0:T(8,128)S(1)}, f32[8,640]{1,0:T(8,128)S(1)}, u32[]{:S(2)}, u32[]{:S(2)}) %collective-permute-start.9) | collective-permute-done | bytes 20512 | tf_op jit(solution)/shard_map/ppermute | solution.py:340
  34.2 0.0 collective-permute-done.8
  34.2 0.5 collective-permute-start.13
  34.7 2.4 %collective-permute-start.12 = (f32[8,640]{1,0:T(8,128)S(1)}, f32[8,640]{1,0:T(8,128)S(1)}, u32[]{:S(2)}, u32[]{:S(2)}) collective-permute-start(f32[8,640]{1,0:T(8,128)S(1)} %add_add_fusion.2), channel_id=1, source_target_pairs={{0,5},{1,4},{2,7},{3,6},{4,1},{5,0},{6,3},{7,2},{8,13},{9,12},{10,... | collective-permute-start | bytes 61448 | tf_op jit(solution)/shard_map/ppermute | solution.py:340
  37.1 0.4 collective-permute-start.11
  37.5 0.1 collective-permute-done.13
  37.6 1.0 %collective-permute-done.12 = f32[8,640]{1,0:T(8,128)S(1)} collective-permute-done((f32[8,640]{1,0:T(8,128)S(1)}, f32[8,640]{1,0:T(8,128)S(1)}, u32[]{:S(2)}, u32[]{:S(2)}) %collective-permute-start.12) | collective-permute-done | bytes 20512 | tf_op jit(solution)/shard_map/ppermute | solution.py:340
  38.6 3.2 %collective-permute-done.11 = f32[8,640]{1,0:T(8,128)S(1)} collective-permute-done((f32[8,640]{1,0:T(8,128)S(1)}, f32[8,640]{1,0:T(8,128)S(1)}, u32[]{:S(2)}, u32[]{:S(2)}) %collective-permute-start.11) | collective-permute-done | bytes 20512 | tf_op jit(solution)/shard_map/ppermute | solution.py:340
  41.8 0.1 collective-permute-start.14
  41.9 1.3 %collective-permute-done.14 = f32[32,640]{1,0:T(8,128)S(1)} collective-permute-done((f32[32,640]{1,0:T(8,128)S(1)}, f32[32,640]{1,0:T(8,128)S(1)}, u32[]{:S(2)}, u32[]{:S(2)}) %collective-permute-start.14) | collective-permute-done | bytes 81952 | tf_op jit(solution)/shard_map/ppermute | solution.py:340
  43.2 3.8 %first_solve.1 = (bf16[64,2048]{1,0:T(8,128)(2,1)S(1)}, f32[64,192]{1,0:T(8,128)S(1)}, f32[64,64]{1,0:T(8,128)S(1)}, f32[64,192]{1,0:T(8,128)S(1)}, f32[64,64]{1,0:T(8,128)S(1)}, /*index=5*/bf16[64,64]{1,0:T(8,128)(2,1)S(1)}) custom-call(f32[64,640]{1,0:T(8,128)S(1)} %pad_maximum_fusion.cross, bf16[192,2048]{1,0:T(8,128)(2,1)S(1)} %reshape.13.stack, ...), custom_call_target="tpu_custom_call" | custom-call | bytes 1613824 | tf_op jit(solution)/shard_map/first_solve/pallas_call | solution.py:386
  47.0 0.7 collective-permute-start.16
  47.7 2.4 %collective-permute-start.15 = (bf16[64,1024]{1,0:T(8,128)(2,1)S(1)}, bf16[64,1024]{1,0:T(8,128)(2,1)S(1)}, u32[]{:S(2)}, u32[]{:S(2)}) collective-permute-start(bf16[64,1024]{1,0:T(8,128)(2,1)S(1)} %get-tuple-element.56), channel_id=1, source_target_pairs={{0,4},{4,0},{8,12},{12,8},{16,20},{20,16},{24,28},{28,24},{1,5},{5... | collective-permute-start | bytes 393224 | tf_op jit(solution)/shard_map/ppermute | solution.py:28
  50.2 5.6 %collective-permute-done.15 = bf16[64,1024]{1,0:T(8,128)(2,1)S(1)} collective-permute-done((bf16[64,1024]{1,0:T(8,128)(2,1)S(1)}, bf16[64,1024]{1,0:T(8,128)(2,1)S(1)}, u32[]{:S(2)}, u32[]{:S(2)}) %collective-permute-start.15) | collective-permute-done | bytes 131104 | tf_op jit(solution)/shard_map/ppermute | solution.py:28
  55.8 0.6 collective-permute-start.18
  56.4 0.5 collective-permute-start.17
  56.9 0.7 inner_image.3.partial
  57.6 2.5 %collective-permute-done.18 = bf16[64,512]{1,0:T(8,128)(2,1)S(1)} collective-permute-done((bf16[64,512]{1,0:T(8,128)(2,1)S(1)}, bf16[64,512]{1,0:T(8,128)(2,1)S(1)}, u32[]{:S(2)}, u32[]{:S(2)}) %collective-permute-start.18) | collective-permute-done | bytes 65568 | tf_op jit(solution)/shard_map/ppermute | solution.py:30
  60.1 0.0 collective-permute-done.17
  60.1 1.1 %second_image.1 = (bf16[64,2048]{1,0:T(8,128)(2,1)S(1)}, f32[64,256]{1,0:T(8,128)S(1)}) custom-call(f32[27,16,128]{2,1,0:T(8,128)S(1)} %coefficients.1.coef, bf16[192,2048]{1,0:T(8,128)(2,1)S(1)} %reshape.13.stack, bf16[64,2048]{1,0:T(8,128)(2,1)S(1)} %get-tuple-element.34.fields.block.last, f32[64,2048]{1,0:T(8,128)S(1)} %inner_image.3.partial, ...), custom_call_target="tpu_custom_call" | custom-call | bytes 2514944 | tf_op jit(solution)/shard_map/second_image/pallas_call | solution.py:386
  61.3 0.2 collective-permute-start.19
  61.4 1.1 %collective-permute-done.19 = f32[32,256]{1,0:T(8,128)S(1)} collective-permute-done((f32[32,256]{1,0:T(8,128)S(1)}, f32[32,256]{1,0:T(8,128)S(1)}, u32[]{:S(2)}, u32[]{:S(2)}) %collective-permute-start.19) | collective-permute-done | bytes 32800 | tf_op jit(solution)/shard_map/ppermute | solution.py:340
  62.5 2.8 %collective-permute-start.22 = (f32[32,256]{1,0:T(8,128)S(1)}, f32[32,256]{1,0:T(8,128)S(1)}, u32[]{:S(2)}, u32[]{:S(2)}) collective-permute-start(f32[32,256]{1,0:T(8,128)S(1)} %select_add_fusion.1), channel_id=1, source_target_pairs={{0,6},{1,7},{2,4},{3,5},{4,2},{5,3},{6,0},{7,1},{8,14},{9,15},{10,... | collective-permute-start | bytes 98312 | tf_op jit(solution)/shard_map/ppermute | solution.py:340
  65.3 0.0 collective-permute-start.21
  65.3 0.6 collective-permute-start.20
  66.0 1.4 %collective-permute-done.22 = f32[32,256]{1,0:T(8,128)S(1)} collective-permute-done((f32[32,256]{1,0:T(8,128)S(1)}, f32[32,256]{1,0:T(8,128)S(1)}, u32[]{:S(2)}, u32[]{:S(2)}) %collective-permute-start.22) | collective-permute-done | bytes 32800 | tf_op jit(solution)/shard_map/ppermute | solution.py:340
  67.3 1.6 %collective-permute-done.21 = f32[32,256]{1,0:T(8,128)S(1)} collective-permute-done((f32[32,256]{1,0:T(8,128)S(1)}, f32[32,256]{1,0:T(8,128)S(1)}, u32[]{:S(2)}, u32[]{:S(2)}) %collective-permute-start.21) | collective-permute-done | bytes 32800 | tf_op jit(solution)/shard_map/ppermute | solution.py:340
  69.0 3.0 %collective-permute-start.25 = (f32[32,256]{1,0:T(8,128)S(1)}, f32[32,256]{1,0:T(8,128)S(1)}, u32[]{:S(2)}, u32[]{:S(2)}) collective-permute-start(f32[32,256]{1,0:T(8,128)S(1)} %add_add_fusion.1), channel_id=1, source_target_pairs={{0,24},{1,25},{2,26},{3,27},{4,28},{5,29},{6,30},{7,31},{8,16},{9,... | collective-permute-start | bytes 98312 | tf_op jit(solution)/shard_map/ppermute | solution.py:340
  72.0 1.2 %collective-permute-start.23 = (f32[32,256]{1,0:T(8,128)S(1)}, f32[32,256]{1,0:T(8,128)S(1)}, u32[]{:S(2)}, u32[]{:S(2)}) collective-permute-start(f32[32,256]{1,0:T(8,128)S(1)} %add_add_fusion.1), channel_id=1, source_target_pairs={{0,9},{1,8},{2,11},{3,10},{4,13},{5,12},{6,15},{7,14},{8,1},{9,0},... | collective-permute-start | bytes 98312 | tf_op jit(solution)/shard_map/ppermute | solution.py:340
  73.2 1.6 %collective-permute-done.25 = f32[32,256]{1,0:T(8,128)S(1)} collective-permute-done((f32[32,256]{1,0:T(8,128)S(1)}, f32[32,256]{1,0:T(8,128)S(1)}, u32[]{:S(2)}, u32[]{:S(2)}) %collective-permute-start.25) | collective-permute-done | bytes 32800 | tf_op jit(solution)/shard_map/ppermute | solution.py:340
  74.8 1.5 %collective-permute-done.24 = f32[32,256]{1,0:T(8,128)S(1)} collective-permute-done((f32[32,256]{1,0:T(8,128)S(1)}, f32[32,256]{1,0:T(8,128)S(1)}, u32[]{:S(2)}, u32[]{:S(2)}) %collective-permute-start.24) | collective-permute-done | bytes 32800 | tf_op jit(solution)/shard_map/ppermute | solution.py:340
  76.3 0.4 collective-permute-start.26
  76.6 0.4 next_gram.1
  77.0 0.5 collective-permute-done.26
  77.6 4.4 %second_solve.1 = (bf16[64,2,8,128]{3,2,1,0:T(8,128)(2,1)}, f32[2,64,192]{2,1,0:T(8,128)}, f32[2,64,64]{2,1,0:T(8,128)}) custom-call(f32[64,256]{1,0:T(8,128)S(1)} %pad_maximum_fusion.6.cross, bf16[192,192]{1,0:T(8,128)(2,1)S(1)} %get-tuple-element.41.own_high, bf16[192,192]{1,0:T(8,128)(2,1)S(1)} %get-tuple-element.42.own_low, ...), custom_call_target="tpu_custom_call" | custom-call | bytes 1982464 | tf_op jit(solution)/shard_map/second_solve/pallas_call | solution.py:386
  (37 shorter events, 0.4 us)
Async XLA Ops:
  0.6 1.0 %slice-start = ((bf16[3,64,2,8,128]{4,3,2,1,0:T(8,128)(2,1)}), bf16[1,64,2,8,128]{4,3,2,1,0:T(8,128)(2,1)S(1)}, s32[]{:S(2)}) async-start(bf16[3,64,2,8,128]{4,3,2,1,0:T(8,128)(2,1)} %param.3), calls=%async_computation | async-start | bytes 524288 | tf_op jit(solution)/shard_map/slice | solution.py:425
  1.7 3.1 %copy-start = (s32[2,8,128]{2,1,0:T(8,128)S(1)}, s32[2,8,128]{2,1,0:T(8,128)}, u32[]{:S(2)}) copy-start(s32[2,8,128]{2,1,0:T(8,128)} %param.4) | copy-start | bytes 24580
  1.7 3.1 %copy-start.1 = (f32[8,27]{1,0:T(8,128)S(1)}, f32[8,27]{1,0:T(8,128)}, u32[]{:S(2)}) copy-start(f32[8,27]{1,0:T(8,128)} %table.1) | copy-start | bytes 2596
  1.7 5.2 %copy-start.2 = (bf16[3,64,2,8,128]{4,3,2,1,0:T(8,128)(2,1)S(1)}, bf16[3,64,2,8,128]{4,3,2,1,0:T(8,128)(2,1)}, u32[]{:S(2)}) copy-start(bf16[3,64,2,8,128]{4,3,2,1,0:T(8,128)(2,1)} %param.3) | copy-start | bytes 2359300
  1.8 6.5 %collective-permute-start = (bf16[64,1024]{1,0:T(8,128)(2,1)S(1)}, bf16[64,1024]{1,0:T(8,128)(2,1)S(1)}, u32[]{:S(2)}, u32[]{:S(2)}) collective-permute-start(bf16[64,1024]{1,0:T(8,128)(2,1)S(1)} %get-tuple-element.64), channel_id=1, source_target_pairs={{0,4},{4,0},{8,12},{12,8},{16,20},{20,16},{24,28},{28,24},{1,5},{5... | collective-permute-start | bytes 393224 | tf_op jit(solution)/shard_map/ppermute | solution.py:28
  6.2 2.1 %collective-permute-start.1 = (bf16[64,1024]{1,0:T(8,128)(2,1)S(1)}, bf16[64,1024]{1,0:T(8,128)(2,1)S(1)}, u32[]{:S(2)}, u32[]{:S(2)}) collective-permute-start(bf16[64,1024]{1,0:T(8,128)(2,1)S(1)} %get-tuple-element.26), channel_id=1, source_target_pairs={{4,8},{8,4},{12,16},{16,12},{20,24},{24,20},{5,9},{9,5},{13,17},{1... | collective-permute-start | bytes 393224 | tf_op jit(solution)/shard_map/ppermute | solution.py:30
  8.4 4.1 %collective-permute-start.3 = (bf16[64,512]{1,0:T(8,128)(2,1)S(1)}, bf16[64,512]{1,0:T(8,128)(2,1)S(1)}, u32[]{:S(2)}, u32[]{:S(2)}) collective-permute-start(bf16[64,512]{1,0:T(8,128)(2,1)S(1)} %get-tuple-element.77), channel_id=1, source_target_pairs={{1,2},{2,1},{0,3},{3,0},{5,6},{6,5},{4,7},{7,4},{9,10},{10,9},{8,1... | collective-permute-start | bytes 196616 | tf_op jit(solution)/shard_map/ppermute | solution.py:30
  8.8 3.7 %collective-permute-start.2 = (bf16[64,512]{1,0:T(8,128)(2,1)S(1)}, bf16[64,512]{1,0:T(8,128)(2,1)S(1)}, u32[]{:S(2)}, u32[]{:S(2)}) collective-permute-start(bf16[64,512]{1,0:T(8,128)(2,1)S(1)} %get-tuple-element.78), channel_id=1, source_target_pairs={{0,1},{1,0},{2,3},{3,2},{4,5},{5,4},{6,7},{7,6},{8,9},{9,8},{10,11... | collective-permute-start | bytes 196616 | tf_op jit(solution)/shard_map/ppermute | solution.py:28
  13.7 1.3 %collective-permute-start.4 = (f32[32,640]{1,0:T(8,128)S(1)}, f32[32,640]{1,0:T(8,128)S(1)}, u32[]{:S(2)}, u32[]{:S(2)}) collective-permute-start(f32[32,640]{1,0:T(8,128)S(1)} %slice_select_fusion), channel_id=1, source_target_pairs={{0,1},{1,0},{2,3},{3,2},{4,5},{5,4},{6,7},{7,6},{8,9},{9,8},{10,11... | collective-permute-start | bytes 245768 | tf_op jit(solution)/shard_map/ppermute | solution.py:340
  15.0 8.1 %collective-permute-start.5 = (f32[8,640]{1,0:T(8,128)S(1)}, f32[8,640]{1,0:T(8,128)S(1)}, u32[]{:S(2)}, u32[]{:S(2)}) collective-permute-start(f32[8,640]{1,0:T(8,128)S(1)} %get-tuple-element.87), channel_id=1, source_target_pairs={{0,3},{1,2},{2,1},{3,0},{4,7},{5,6},{6,5},{7,4},{8,11},{9,10},{10,... | collective-permute-start | bytes 61448 | tf_op jit(solution)/shard_map/ppermute | solution.py:340
  16.3 7.8 %collective-permute-start.6 = (f32[8,640]{1,0:T(8,128)S(1)}, f32[8,640]{1,0:T(8,128)S(1)}, u32[]{:S(2)}, u32[]{:S(2)}) collective-permute-start(f32[8,640]{1,0:T(8,128)S(1)} %get-tuple-element.88), channel_id=1, source_target_pairs={{0,5},{1,4},{2,7},{3,6},{4,1},{5,0},{6,3},{7,2},{8,13},{9,12},{10,... | collective-permute-start | bytes 61448 | tf_op jit(solution)/shard_map/ppermute | solution.py:340
  22.5 4.7 %collective-permute-start.7 = (f32[8,640]{1,0:T(8,128)S(1)}, f32[8,640]{1,0:T(8,128)S(1)}, u32[]{:S(2)}, u32[]{:S(2)}) collective-permute-start(f32[8,640]{1,0:T(8,128)S(1)} %get-tuple-element.89), channel_id=1, source_target_pairs={{0,6},{1,7},{2,4},{3,5},{4,2},{5,3},{6,0},{7,1},{8,14},{9,15},{10,... | collective-permute-start | bytes 61448 | tf_op jit(solution)/shard_map/ppermute | solution.py:340
  27.2 5.6 %collective-permute-start.10 = (f32[8,640]{1,0:T(8,128)S(1)}, f32[8,640]{1,0:T(8,128)S(1)}, u32[]{:S(2)}, u32[]{:S(2)}) collective-permute-start(f32[8,640]{1,0:T(8,128)S(1)} %add_add_fusion.3), channel_id=1, source_target_pairs={{0,24},{1,25},{2,26},{3,27},{4,28},{5,29},{6,30},{7,31},{8,16},{9,... | collective-permute-start | bytes 61448 | tf_op jit(solution)/shard_map/ppermute | solution.py:340
  30.1 4.1 %collective-permute-start.9 = (f32[8,640]{1,0:T(8,128)S(1)}, f32[8,640]{1,0:T(8,128)S(1)}, u32[]{:S(2)}, u32[]{:S(2)}) collective-permute-start(f32[8,640]{1,0:T(8,128)S(1)} %add_add_fusion.3), channel_id=1, source_target_pairs={{0,17},{1,16},{2,19},{3,18},{4,21},{5,20},{6,23},{7,22},{8,25},{9,... | collective-permute-start | bytes 61448 | tf_op jit(solution)/shard_map/ppermute | solution.py:340
  30.1 4.1 %collective-permute-start.8 = (f32[8,640]{1,0:T(8,128)S(1)}, f32[8,640]{1,0:T(8,128)S(1)}, u32[]{:S(2)}, u32[]{:S(2)}) collective-permute-start(f32[8,640]{1,0:T(8,128)S(1)} %add_add_fusion.3), channel_id=1, source_target_pairs={{0,9},{1,8},{2,11},{3,10},{4,13},{5,12},{6,15},{7,14},{8,1},{9,0},... | collective-permute-start | bytes 61448 | tf_op jit(solution)/shard_map/ppermute | solution.py:340
  34.2 3.4 %collective-permute-start.13 = (f32[8,640]{1,0:T(8,128)S(1)}, f32[8,640]{1,0:T(8,128)S(1)}, u32[]{:S(2)}, u32[]{:S(2)}) collective-permute-start(f32[8,640]{1,0:T(8,128)S(1)} %add_add_fusion.2), channel_id=1, source_target_pairs={{0,3},{1,2},{2,1},{3,0},{4,7},{5,6},{6,5},{7,4},{8,11},{9,10},{10,... | collective-permute-start | bytes 61448 | tf_op jit(solution)/shard_map/ppermute | solution.py:340
  34.7 3.9 %collective-permute-start.12 = (f32[8,640]{1,0:T(8,128)S(1)}, f32[8,640]{1,0:T(8,128)S(1)}, u32[]{:S(2)}, u32[]{:S(2)}) collective-permute-start(f32[8,640]{1,0:T(8,128)S(1)} %add_add_fusion.2), channel_id=1, source_target_pairs={{0,5},{1,4},{2,7},{3,6},{4,1},{5,0},{6,3},{7,2},{8,13},{9,12},{10,... | collective-permute-start | bytes 61448 | tf_op jit(solution)/shard_map/ppermute | solution.py:340
  37.1 4.7 %collective-permute-start.11 = (f32[8,640]{1,0:T(8,128)S(1)}, f32[8,640]{1,0:T(8,128)S(1)}, u32[]{:S(2)}, u32[]{:S(2)}) collective-permute-start(f32[8,640]{1,0:T(8,128)S(1)} %add_add_fusion.2), channel_id=1, source_target_pairs={{0,6},{1,7},{2,4},{3,5},{4,2},{5,3},{6,0},{7,1},{8,14},{9,15},{10,... | collective-permute-start | bytes 61448 | tf_op jit(solution)/shard_map/ppermute | solution.py:340
  41.8 1.3 %collective-permute-start.14 = (f32[32,640]{1,0:T(8,128)S(1)}, f32[32,640]{1,0:T(8,128)S(1)}, u32[]{:S(2)}, u32[]{:S(2)}) collective-permute-start(f32[32,640]{1,0:T(8,128)S(1)} %pad_maximum_fusion.1), channel_id=1, source_target_pairs={{0,1},{1,0},{2,3},{3,2},{4,5},{5,4},{6,7},{7,6},{8,9},{9,8},{10,11... | collective-permute-start | bytes 245768 | tf_op jit(solution)/shard_map/ppermute | solution.py:340
  47.0 3.1 %collective-permute-start.16 = (bf16[64,1024]{1,0:T(8,128)(2,1)S(1)}, bf16[64,1024]{1,0:T(8,128)(2,1)S(1)}, u32[]{:S(2)}, u32[]{:S(2)}) collective-permute-start(bf16[64,1024]{1,0:T(8,128)(2,1)S(1)} %get-tuple-element.55), channel_id=1, source_target_pairs={{4,8},{8,4},{12,16},{16,12},{20,24},{24,20},{5,9},{9,5},{13,17},{1... | collective-permute-start | bytes 393224 | tf_op jit(solution)/shard_map/ppermute | solution.py:30
  47.7 8.0 %collective-permute-start.15 = (bf16[64,1024]{1,0:T(8,128)(2,1)S(1)}, bf16[64,1024]{1,0:T(8,128)(2,1)S(1)}, u32[]{:S(2)}, u32[]{:S(2)}) collective-permute-start(bf16[64,1024]{1,0:T(8,128)(2,1)S(1)} %get-tuple-element.56), channel_id=1, source_target_pairs={{0,4},{4,0},{8,12},{12,8},{16,20},{20,16},{24,28},{28,24},{1,5},{5... | collective-permute-start | bytes 393224 | tf_op jit(solution)/shard_map/ppermute | solution.py:28
  55.8 4.3 %collective-permute-start.18 = (bf16[64,512]{1,0:T(8,128)(2,1)S(1)}, bf16[64,512]{1,0:T(8,128)(2,1)S(1)}, u32[]{:S(2)}, u32[]{:S(2)}) collective-permute-start(bf16[64,512]{1,0:T(8,128)(2,1)S(1)} %get-tuple-element.69), channel_id=1, source_target_pairs={{1,2},{2,1},{0,3},{3,0},{5,6},{6,5},{4,7},{7,4},{9,10},{10,9},{8,1... | collective-permute-start | bytes 196616 | tf_op jit(solution)/shard_map/ppermute | solution.py:30
  56.4 3.7 %collective-permute-start.17 = (bf16[64,512]{1,0:T(8,128)(2,1)S(1)}, bf16[64,512]{1,0:T(8,128)(2,1)S(1)}, u32[]{:S(2)}, u32[]{:S(2)}) collective-permute-start(bf16[64,512]{1,0:T(8,128)(2,1)S(1)} %get-tuple-element.70), channel_id=1, source_target_pairs={{0,1},{1,0},{2,3},{3,2},{4,5},{5,4},{6,7},{7,6},{8,9},{9,8},{10,11... | collective-permute-start | bytes 196616 | tf_op jit(solution)/shard_map/ppermute | solution.py:28
  61.3 1.3 %collective-permute-start.19 = (f32[32,256]{1,0:T(8,128)S(1)}, f32[32,256]{1,0:T(8,128)S(1)}, u32[]{:S(2)}, u32[]{:S(2)}) collective-permute-start(f32[32,256]{1,0:T(8,128)S(1)} %slice_select_fusion.1), channel_id=1, source_target_pairs={{0,1},{1,0},{2,3},{3,2},{4,5},{5,4},{6,7},{7,6},{8,9},{9,8},{10,11... | collective-permute-start | bytes 98312 | tf_op jit(solution)/shard_map/ppermute | solution.py:340
  62.5 4.8 %collective-permute-start.22 = (f32[32,256]{1,0:T(8,128)S(1)}, f32[32,256]{1,0:T(8,128)S(1)}, u32[]{:S(2)}, u32[]{:S(2)}) collective-permute-start(f32[32,256]{1,0:T(8,128)S(1)} %select_add_fusion.1), channel_id=1, source_target_pairs={{0,6},{1,7},{2,4},{3,5},{4,2},{5,3},{6,0},{7,1},{8,14},{9,15},{10,... | collective-permute-start | bytes 98312 | tf_op jit(solution)/shard_map/ppermute | solution.py:340
  65.3 3.6 %collective-permute-start.21 = (f32[32,256]{1,0:T(8,128)S(1)}, f32[32,256]{1,0:T(8,128)S(1)}, u32[]{:S(2)}, u32[]{:S(2)}) collective-permute-start(f32[32,256]{1,0:T(8,128)S(1)} %select_add_fusion.1), channel_id=1, source_target_pairs={{0,5},{1,4},{2,7},{3,6},{4,1},{5,0},{6,3},{7,2},{8,13},{9,12},{10,... | collective-permute-start | bytes 98312 | tf_op jit(solution)/shard_map/ppermute | solution.py:340
  65.3 3.6 %collective-permute-start.20 = (f32[32,256]{1,0:T(8,128)S(1)}, f32[32,256]{1,0:T(8,128)S(1)}, u32[]{:S(2)}, u32[]{:S(2)}) collective-permute-start(f32[32,256]{1,0:T(8,128)S(1)} %select_add_fusion.1), channel_id=1, source_target_pairs={{0,3},{1,2},{2,1},{3,0},{4,7},{5,6},{6,5},{7,4},{8,11},{9,10},{10,... | collective-permute-start | bytes 98312 | tf_op jit(solution)/shard_map/ppermute | solution.py:340
  69.0 5.8 %collective-permute-start.25 = (f32[32,256]{1,0:T(8,128)S(1)}, f32[32,256]{1,0:T(8,128)S(1)}, u32[]{:S(2)}, u32[]{:S(2)}) collective-permute-start(f32[32,256]{1,0:T(8,128)S(1)} %add_add_fusion.1), channel_id=1, source_target_pairs={{0,24},{1,25},{2,26},{3,27},{4,28},{5,29},{6,30},{7,31},{8,16},{9,... | collective-permute-start | bytes 98312 | tf_op jit(solution)/shard_map/ppermute | solution.py:340
  72.0 4.3 %collective-permute-start.24 = (f32[32,256]{1,0:T(8,128)S(1)}, f32[32,256]{1,0:T(8,128)S(1)}, u32[]{:S(2)}, u32[]{:S(2)}) collective-permute-start(f32[32,256]{1,0:T(8,128)S(1)} %add_add_fusion.1), channel_id=1, source_target_pairs={{0,17},{1,16},{2,19},{3,18},{4,21},{5,20},{6,23},{7,22},{8,25},{9,... | collective-permute-start | bytes 98312 | tf_op jit(solution)/shard_map/ppermute | solution.py:340
  72.0 4.3 %collective-permute-start.23 = (f32[32,256]{1,0:T(8,128)S(1)}, f32[32,256]{1,0:T(8,128)S(1)}, u32[]{:S(2)}, u32[]{:S(2)}) collective-permute-start(f32[32,256]{1,0:T(8,128)S(1)} %add_add_fusion.1), channel_id=1, source_target_pairs={{0,9},{1,8},{2,11},{3,10},{4,13},{5,12},{6,15},{7,14},{8,1},{9,0},... | collective-permute-start | bytes 98312 | tf_op jit(solution)/shard_map/ppermute | solution.py:340
  76.3 1.3 %collective-permute-start.26 = (f32[32,256]{1,0:T(8,128)S(1)}, f32[32,256]{1,0:T(8,128)S(1)}, u32[]{:S(2)}, u32[]{:S(2)}) collective-permute-start(f32[32,256]{1,0:T(8,128)S(1)} %add_add_fusion), channel_id=1, source_target_pairs={{0,1},{1,0},{2,3},{3,2},{4,5},{5,4},{6,7},{7,6},{8,9},{9,8},{10,11... | collective-permute-start | bytes 98312 | tf_op jit(solution)/shard_map/ppermute | solution.py:340

commit v14 on v12

--- a/solution.py
+++ b/solution.py
@@ -192,13 +192,15 @@
     return sum(dot(left, right, dims) for left in lefts for right in rights)
 
 
-def factor(square):
+def factor(square, sizes, across):
     size = square.shape[0]
     shape = (8, 2 * size)
     sub = lax.broadcasted_iota(jnp.int32, shape, 0)
     unit = lax.broadcasted_iota(jnp.int32, (size, size), 0) == lax.broadcasted_iota(
         jnp.int32, (size, size), 1
     )
+    scale = lax.rsqrt(across)
+    square = square * lax.rsqrt(sizes) * scale
     whole = jnp.concatenate([square, unit.astype(jnp.float32)], axis=1)
     blocks = [whole[b : b + 8] for b in range(0, size, 8)]
     done = []
@@ -206,38 +208,62 @@
     def row_of(values, at):
         return jnp.broadcast_to(values[at : at + 1, :], shape)
 
-    def column_of(values, at):
-        return jnp.broadcast_to(values[:, at : at + 1], shape)
+    def columns_of(values, first):
+        return [
+            jnp.broadcast_to(values[:, at : at + 1], shape) for at in range(first, first + 8)
+        ]
 
     for b, here in enumerate(blocks):
-        columns = [column_of(here, 8 * b + j) for j in range(8)]
+        columns = columns_of(here, 8 * b)
         entry = {(i, j): row_of(columns[j], i) for j in range(8) for i in range(j + 1)}
         rows = [row_of(here, i) for i in range(8)]
-        inverse, ratio = [], {}
-        for r in range(8):
-            inverse.append(1.0 / entry[r, r])
-            for j in range(r + 1, 8):
-                ratio[r, j] = entry[r, j] * inverse[r]
-            for i in range(r + 1, 8):
+        scaled = jnp.zeros(shape, jnp.float32)
+        solved, ratio = [], {}
+        if b + 1 < len(blocks):
+            below = columns_of(blocks[b + 1], 8 * b)
+        for p in range(0, 8, 2):
+            q = p + 1
+            first, mixed, last = entry[p, p], entry[p, q], entry[q, q]
+            inverse = 1.0 / (first * last - mixed * mixed)
+
+            def solve(one, two):
+                return (
+                    (last * one - mixed * two) * inverse,
+                    (first * two - mixed * one) * inverse,
+                )
+
+            for j in range(p + 2, 8):
+                ratio[p, j], ratio[q, j] = solve(entry[p, j], entry[q, j])
+            for i in range(p + 2, 8):
                 for j in range(i, 8):
-                    entry[i, j] = entry[i, j] - entry[r, i] * ratio[r, j]
-                rows[i] = rows[i] - ratio[r, i] * rows[r]
-        solved = {}
-        for r in reversed(range(8)):
-            solved[r] = rows[r] * inverse[r]
-            for j in range(r + 1, 8):
-                solved[r] = solved[r] - ratio[r, j] * solved[j]
-        for later in range(b + 1, len(blocks)):
-            for j in range(8):
-                change = column_of(blocks[later], 8 * b + j) * solved[j]
-                total = change if j == 0 else total + change
-            blocks[later] = blocks[later] - total
-        scaled = jnp.zeros(shape, jnp.float32)
-        for r in range(8):
-            scaled = jnp.where(sub == r, rows[r] * lax.rsqrt(entry[r, r]), scaled)
+                    change = entry[p, i] * ratio[p, j] + entry[q, i] * ratio[q, j]
+                    entry[i, j] = entry[i, j] - change
+                rows[i] = rows[i] - (ratio[p, i] * rows[p] + ratio[q, i] * rows[q])
+            solved += solve(rows[p], rows[q])
+            if b + 1 < len(blocks):
+                change = below[p] * solved[p] + below[q] * solved[q]
+                blocks[b + 1] = blocks[b + 1] - change
+                for j in range(p + 2, 8):
+                    below[j] = below[j] - (below[p] * ratio[p, j] + below[q] * ratio[q, j])
+            part = mixed * (1.0 / first)
+            scaled = jnp.where(sub == p, rows[p] * lax.rsqrt(first), scaled)
+            rest = (rows[q] - part * rows[p]) * lax.rsqrt(last - part * mixed)
+            scaled = jnp.where(sub == q, rest, scaled)
         done.append(scaled)
+        for p in (4, 2, 0):
+            for r in (p, p + 1):
+                for j in range(p + 2, 8):
+                    solved[r] = solved[r] - ratio[r, j] * solved[j]
+        for later in range(b + 2, len(blocks)):
+            parts = [one * two for one, two in zip(columns_of(blocks[later], 8 * b), solved)]
+            while len(parts) > 1:
+                parts = [one + two for one, two in zip(parts[::2], parts[1::2])]
+            blocks[later] = blocks[later] - parts[0]
     done = jnp.concatenate(done, axis=0)
-    return done[:, :size], done[:, size:]
+    above = lax.broadcasted_iota(jnp.int32, (size, size), 0) <= lax.broadcasted_iota(
+        jnp.int32, (size, size), 1
+    )
+    return jnp.where(above, done[:, :size] * (across * scale), 0.0), done[:, size:] * scale
 
 
 def project(cross, own, scale):
@@ -248,10 +274,18 @@
     second = first - dots((first_low,), own)
     second_low = second.astype(jnp.bfloat16)
     used = (first_low, second_low)
-    square = cross[:, fields:] * scale - dots(used, first_parts, NT)
+    square = cross[:, fields:] * scale
+    diagonal = jnp.where(
+        lax.broadcasted_iota(jnp.int32, square.shape, 0)
+        == lax.broadcasted_iota(jnp.int32, square.shape, 1),
+        square,
+        0.0,
+    )
+    sizes = [jnp.sum(diagonal, axis=axis, keepdims=True) for axis in (1, 0)]
+    square = square - dots(used, first_parts, NT)
     rest = second - dots((second_low,), own)
     square = square - dots(split(rest), used, NT)
-    return used, first + second, rest, square
+    return used, first + second, rest, square, sizes
 
 
 def unpacked(upper, columns, fields):
@@ -270,14 +304,14 @@
     columns = image.shape[0]
     fields = stack.shape[0]
     gram = unpacked(cross[:, fields + columns :] * scale, columns, fields)
-    used, proj[...], rest[...], square_here = project(
+    used, proj[...], rest[...], square_here, sizes = project(
         cross[:, : fields + columns], split(gram), scale
     )
     square[...] = square_here
     moved = dot(jnp.concatenate(used, axis=0), stack[...])
     w = image[...].astype(jnp.float32) - moved[:columns] - moved[columns:]
     block[...] = w.astype(jnp.bfloat16)
-    upper, inverse_here = factor(square_here)
+    upper, inverse_here = factor(square_here, *sizes)
     low[...] = upper.T
     inverse_here = inverse_here.astype(jnp.bfloat16)
     inverse[...] = inverse_here
@@ -306,14 +340,14 @@
 ):
     columns = image.shape[0]
     kept = stack.shape[0] - columns
-    used, proj[1], _, square = project(cross[...], (own_high[...], own_low[...]), scale)
+    used, proj[1], _, square, sizes = project(cross[...], (own_high[...], own_low[...]), scale)
     proj[0] = proj_in[...]
     low[0] = low_in[...]
     both = jnp.concatenate(used, axis=0)
     moved = dot(both[:, :kept], stack[columns:]) + dot(both[:, kept:], last[...])
     w = image[...].astype(jnp.float32) - moved[:columns] - moved[columns:]
     block[...] = w.astype(jnp.bfloat16)
-    upper, inverse = factor(square)
+    upper, inverse = factor(square, *sizes)
     low[1] = upper.T
     inverse = inverse.astype(jnp.bfloat16)
     _, span_x, span_y, depth = result.shape

time: 79.1 us -> 77.6 us (0.981)
  Pallas kernels: 13.5 us -> 12 us
    pallas_call x8, Pallas kernels: 12.7 us -> 11.2 us  [call(): pl.pallas_call(kernel, out_shape=[jax.ShapeDtypeStruct(shape, dtype) for...]
where the time goes in v14:
time: 77.6 us; the launch traced here: 77.5 us
  starting transfers between devices  32.9 us (42%)
  waiting for transfers between devices  29.8 us (38%)
  Pallas kernels  12 us (15%)
  local copies, waits for them, and re-layouts  1.47 us (2%)
  between operations  0.92 us (1%)
    ppermute x16, starting transfers between devices, partner(): return lax.ppermute(part, axes, [(i, i ^ mask) for i in range(count)])  21.9 us
    ppermute x16, waiting for transfers between devices, partner(): return lax.ppermute(part, axes, [(i, i ^ mask) for i in range(count)])  19.5 us
    pallas_call x8, Pallas kernels, call(): pl.pallas_call(kernel, out_shape=[jax.ShapeDtypeStruct(shape, dtype) for...  11.2 us
    ppermute x4, starting transfers between devices, swaps(): inner = lax.ppermute(near, axis, [(i, i ^ 1) for i in range(count)])  8.72 us
    ppermute x4, waiting for transfers between devices, swaps(): inner = lax.ppermute(near, axis, [(i, i ^ 1) for i in range(count)])  5.61 us
    ppermute x4, waiting for transfers between devices, swaps(): outer = lax.ppermute(far, axis, pairs)  4.69 us
    ppermute x4, starting transfers between devices, swaps(): outer = lax.ppermute(far, axis, pairs)  2.35 us
  transfers between devices with their start and end apart: 24, of which 16 were waited for; matrix products, arithmetic and copies ran while one was open for 0% of the time, Pallas kernels for 4%

profile of v14, /device:TPU:0, one launch (start us, length us, event | category | flops | bytes accessed | tf_op | source)
XLA Modules:
  0.0 77.5 jit_solution(7028277647411584815)
XLA Ops:
  0.6 0.0 slice-start
  0.7 0.9 %slice-done = bf16[1,64,2,8,128]{4,3,2,1,0:T(8,128)(2,1)S(1)} async-done(((bf16[3,64,2,8,128]{4,3,2,1,0:T(8,128)(2,1)}), bf16[1,64,2,8,128]{4,3,2,1,0:T(8,128)(2,1)S(1)}, s32[]{:S(2)}) %slice-start) | async-done | bytes 262168 | tf_op jit(solution)/shard_map/slice | solution.py:433
  1.6 0.1 reshape_squeeze.3.fields
  1.7 0.0 copy-start
  1.7 0.0 copy-start.1
  1.7 0.0 copy-start.2
  1.8 3.0 %collective-permute-start = (bf16[64,1024]{1,0:T(8,128)(2,1)S(1)}, bf16[64,1024]{1,0:T(8,128)(2,1)S(1)}, u32[]{:S(2)}, u32[]{:S(2)}) collective-permute-start(bf16[64,1024]{1,0:T(8,128)(2,1)S(1)} %get-tuple-element.64), channel_id=1, source_target_pairs={{0,4},{4,0},{8,12},{12,8},{16,20},{20,16},{24,28},{28,24},{1,5},{5... | collective-permute-start | bytes 393224 | tf_op jit(solution)/shard_map/ppermute | solution.py:28
  4.8 0.8 coefficients.1.coef
  5.6 0.7 inner_image.2.partial
  6.2 0.7 collective-permute-start.1
  6.9 0.3 reshape.13.stack
  7.3 0.6 stack_gram.1.own
  7.9 0.4 collective-permute-done
  8.3 0.0 collective-permute-done.1
  8.4 0.4 collective-permute-start.3
  8.8 1.5 %collective-permute-start.2 = (bf16[64,512]{1,0:T(8,128)(2,1)S(1)}, bf16[64,512]{1,0:T(8,128)(2,1)S(1)}, u32[]{:S(2)}, u32[]{:S(2)}) collective-permute-start(bf16[64,512]{1,0:T(8,128)(2,1)S(1)} %get-tuple-element.78), channel_id=1, source_target_pairs={{0,1},{1,0},{2,3},{3,2},{4,5},{5,4},{6,7},{7,6},{8,9},{9,8},{10,11... | collective-permute-start | bytes 196616 | tf_op jit(solution)/shard_map/ppermute | solution.py:28
  10.3 2.2 %collective-permute-done.3 = bf16[64,512]{1,0:T(8,128)(2,1)S(1)} collective-permute-done((bf16[64,512]{1,0:T(8,128)(2,1)S(1)}, bf16[64,512]{1,0:T(8,128)(2,1)S(1)}, u32[]{:S(2)}, u32[]{:S(2)}) %collective-permute-start.3) | collective-permute-done | bytes 65568 | tf_op jit(solution)/shard_map/ppermute | solution.py:30
  12.5 0.0 collective-permute-done.2
  12.5 1.1 %first_image.1 = (bf16[64,2048]{1,0:T(8,128)(2,1)S(1)}, f32[64,640]{1,0:T(8,128)S(1)}) custom-call(f32[27,16,128]{2,1,0:T(8,128)S(1)} %coefficients.1.coef, bf16[192,2048]{1,0:T(8,128)(2,1)S(1)} %reshape.13.stack, f32[64,384]{1,0:T(8,128)S(1)} %stack_gram.1.own, f32[64,2048]{1,0:T(8,128)S(1)} %inner_image.2.partial, ...), custom_call_target="tpu_custom_call" | custom-call | bytes 2449408 | tf_op jit(solution)/shard_map/first_image/pallas_call | solution.py:394
  13.7 0.2 collective-permute-start.4
  13.9 1.1 %collective-permute-done.4 = f32[32,640]{1,0:T(8,128)S(1)} collective-permute-done((f32[32,640]{1,0:T(8,128)S(1)}, f32[32,640]{1,0:T(8,128)S(1)}, u32[]{:S(2)}, u32[]{:S(2)}) %collective-permute-start.4) | collective-permute-done | bytes 81952 | tf_op jit(solution)/shard_map/ppermute | solution.py:363
  15.0 7.2 %collective-permute-start.7 = (f32[32,640]{1,0:T(8,128)S(1)}, f32[32,640]{1,0:T(8,128)S(1)}, u32[]{:S(2)}, u32[]{:S(2)}) collective-permute-start(f32[32,640]{1,0:T(8,128)S(1)} %select_add_fusion), channel_id=1, source_target_pairs={{0,6},{1,7},{2,4},{3,5},{4,2},{5,3},{6,0},{7,1},{8,14},{9,15},{10,... | collective-permute-start | bytes 245768 | tf_op jit(solution)/shard_map/ppermute | solution.py:363
  22.2 0.0 collective-permute-start.6
  22.2 0.6 collective-permute-start.5
  22.8 2.2 %collective-permute-done.7 = f32[32,640]{1,0:T(8,128)S(1)} collective-permute-done((f32[32,640]{1,0:T(8,128)S(1)}, f32[32,640]{1,0:T(8,128)S(1)}, u32[]{:S(2)}, u32[]{:S(2)}) %collective-permute-start.7) | collective-permute-done | bytes 81952 | tf_op jit(solution)/shard_map/ppermute | solution.py:363
  25.0 1.9 %collective-permute-done.6 = f32[32,640]{1,0:T(8,128)S(1)} collective-permute-done((f32[32,640]{1,0:T(8,128)S(1)}, f32[32,640]{1,0:T(8,128)S(1)}, u32[]{:S(2)}, u32[]{:S(2)}) %collective-permute-start.6) | collective-permute-done | bytes 81952 | tf_op jit(solution)/shard_map/ppermute | solution.py:363
  26.9 0.0 collective-permute-done.5
  26.9 4.7 %collective-permute-start.10 = (f32[32,640]{1,0:T(8,128)S(1)}, f32[32,640]{1,0:T(8,128)S(1)}, u32[]{:S(2)}, u32[]{:S(2)}) collective-permute-start(f32[32,640]{1,0:T(8,128)S(1)} %add_add_fusion.1), channel_id=1, source_target_pairs={{0,24},{1,25},{2,26},{3,27},{4,28},{5,29},{6,30},{7,31},{8,16},{9,... | collective-permute-start | bytes 245768 | tf_op jit(solution)/shard_map/ppermute | solution.py:363
  31.6 0.0 collective-permute-start.9
  31.6 0.4 collective-permute-start.8
  32.0 2.5 %collective-permute-done.10 = f32[32,640]{1,0:T(8,128)S(1)} collective-permute-done((f32[32,640]{1,0:T(8,128)S(1)}, f32[32,640]{1,0:T(8,128)S(1)}, u32[]{:S(2)}, u32[]{:S(2)}) %collective-permute-start.10) | collective-permute-done | bytes 81952 | tf_op jit(solution)/shard_map/ppermute | solution.py:363
  34.5 3.5 %collective-permute-done.9 = f32[32,640]{1,0:T(8,128)S(1)} collective-permute-done((f32[32,640]{1,0:T(8,128)S(1)}, f32[32,640]{1,0:T(8,128)S(1)}, u32[]{:S(2)}, u32[]{:S(2)}) %collective-permute-start.9) | collective-permute-done | bytes 81952 | tf_op jit(solution)/shard_map/ppermute | solution.py:363
  38.1 0.0 collective-permute-done.8
  38.1 0.6 collective-permute-start.11
  38.7 0.9 %collective-permute-done.11 = f32[32,640]{1,0:T(8,128)S(1)} collective-permute-done((f32[32,640]{1,0:T(8,128)S(1)}, f32[32,640]{1,0:T(8,128)S(1)}, u32[]{:S(2)}, u32[]{:S(2)}) %collective-permute-start.11) | collective-permute-done | bytes 81952 | tf_op jit(solution)/shard_map/ppermute | solution.py:363
  39.7 3.1 %first_solve.1 = (bf16[64,2048]{1,0:T(8,128)(2,1)S(1)}, f32[64,192]{1,0:T(8,128)S(1)}, f32[64,64]{1,0:T(8,128)S(1)}, f32[64,192]{1,0:T(8,128)S(1)}, f32[64,64]{1,0:T(8,128)S(1)}, /*index=5*/bf16[64,64]{1,0:T(8,128)(2,1)S(1)}) custom-call(f32[64,640]{1,0:T(8,128)S(1)} %pad_maximum_fusion.cross, bf16[192,2048]{1,0:T(8,128)(2,1)S(1)} %reshape.13.stack, ...), custom_call_target="tpu_custom_call" | custom-call | bytes 1613824 | tf_op jit(solution)/shard_map/first_solve/pallas_call | solution.py:394
  42.8 0.7 collective-permute-start.13
  43.4 3.7 %collective-permute-start.12 = (bf16[64,1024]{1,0:T(8,128)(2,1)S(1)}, bf16[64,1024]{1,0:T(8,128)(2,1)S(1)}, u32[]{:S(2)}, u32[]{:S(2)}) collective-permute-start(bf16[64,1024]{1,0:T(8,128)(2,1)S(1)} %get-tuple-element.56), channel_id=1, source_target_pairs={{0,4},{4,0},{8,12},{12,8},{16,20},{20,16},{24,28},{28,24},{1,5},{5... | collective-permute-start | bytes 393224 | tf_op jit(solution)/shard_map/ppermute | solution.py:28
  47.1 0.0 collective-permute-done.13
  47.2 5.3 %collective-permute-done.12 = bf16[64,1024]{1,0:T(8,128)(2,1)S(1)} collective-permute-done((bf16[64,1024]{1,0:T(8,128)(2,1)S(1)}, bf16[64,1024]{1,0:T(8,128)(2,1)S(1)}, u32[]{:S(2)}, u32[]{:S(2)}) %collective-permute-start.12) | collective-permute-done | bytes 131104 | tf_op jit(solution)/shard_map/ppermute | solution.py:28
  52.5 0.6 collective-permute-start.15
  53.1 0.5 collective-permute-start.14
  53.6 0.7 inner_image.3.partial
  54.3 2.5 %collective-permute-done.15 = bf16[64,512]{1,0:T(8,128)(2,1)S(1)} collective-permute-done((bf16[64,512]{1,0:T(8,128)(2,1)S(1)}, bf16[64,512]{1,0:T(8,128)(2,1)S(1)}, u32[]{:S(2)}, u32[]{:S(2)}) %collective-permute-start.15) | collective-permute-done | bytes 65568 | tf_op jit(solution)/shard_map/ppermute | solution.py:30
  56.8 0.0 collective-permute-done.14
  56.8 1.1 %second_image.1 = (bf16[64,2048]{1,0:T(8,128)(2,1)S(1)}, f32[64,256]{1,0:T(8,128)S(1)}) custom-call(f32[27,16,128]{2,1,0:T(8,128)S(1)} %coefficients.1.coef, bf16[192,2048]{1,0:T(8,128)(2,1)S(1)} %reshape.13.stack, bf16[64,2048]{1,0:T(8,128)(2,1)S(1)} %get-tuple-element.34.fields.block.last, f32[64,2048]{1,0:T(8,128)S(1)} %inner_image.3.partial, ...), custom_call_target="tpu_custom_call" | custom-call | bytes 2514944 | tf_op jit(solution)/shard_map/second_image/pallas_call | solution.py:394
  57.9 0.2 collective-permute-start.16
  58.1 1.1 %collective-permute-done.16 = f32[32,256]{1,0:T(8,128)S(1)} collective-permute-done((f32[32,256]{1,0:T(8,128)S(1)}, f32[32,256]{1,0:T(8,128)S(1)}, u32[]{:S(2)}, u32[]{:S(2)}) %collective-permute-start.16) | collective-permute-done | bytes 32800 | tf_op jit(solution)/shard_map/ppermute | solution.py:363
  59.2 2.8 %collective-permute-start.19 = (f32[32,256]{1,0:T(8,128)S(1)}, f32[32,256]{1,0:T(8,128)S(1)}, u32[]{:S(2)}, u32[]{:S(2)}) collective-permute-start(f32[32,256]{1,0:T(8,128)S(1)} %select_add_fusion.1), channel_id=1, source_target_pairs={{0,6},{1,7},{2,4},{3,5},{4,2},{5,3},{6,0},{7,1},{8,14},{9,15},{10,... | collective-permute-start | bytes 98312 | tf_op jit(solution)/shard_map/ppermute | solution.py:363
  62.0 0.0 collective-permute-start.18
  62.0 0.6 collective-permute-start.17
  62.6 1.4 %collective-permute-done.19 = f32[32,256]{1,0:T(8,128)S(1)} collective-permute-done((f32[32,256]{1,0:T(8,128)S(1)}, f32[32,256]{1,0:T(8,128)S(1)}, u32[]{:S(2)}, u32[]{:S(2)}) %collective-permute-start.19) | collective-permute-done | bytes 32800 | tf_op jit(solution)/shard_map/ppermute | solution.py:363
  64.0 1.6 %collective-permute-done.18 = f32[32,256]{1,0:T(8,128)S(1)} collective-permute-done((f32[32,256]{1,0:T(8,128)S(1)}, f32[32,256]{1,0:T(8,128)S(1)}, u32[]{:S(2)}, u32[]{:S(2)}) %collective-permute-start.18) | collective-permute-done | bytes 32800 | tf_op jit(solution)/shard_map/ppermute | solution.py:363
  65.6 0.0 collective-permute-done.17
  65.6 2.2 %collective-permute-start.22 = (f32[32,256]{1,0:T(8,128)S(1)}, f32[32,256]{1,0:T(8,128)S(1)}, u32[]{:S(2)}, u32[]{:S(2)}) collective-permute-start(f32[32,256]{1,0:T(8,128)S(1)} %add_add_fusion.3), channel_id=1, source_target_pairs={{0,24},{1,25},{2,26},{3,27},{4,28},{5,29},{6,30},{7,31},{8,16},{9,... | collective-permute-start | bytes 98312 | tf_op jit(solution)/shard_map/ppermute | solution.py:363
  67.8 0.8 %collective-permute-start.21 = (f32[32,256]{1,0:T(8,128)S(1)}, f32[32,256]{1,0:T(8,128)S(1)}, u32[]{:S(2)}, u32[]{:S(2)}) collective-permute-start(f32[32,256]{1,0:T(8,128)S(1)} %add_add_fusion.3), channel_id=1, source_target_pairs={{0,17},{1,16},{2,19},{3,18},{4,21},{5,20},{6,23},{7,22},{8,25},{9,... | collective-permute-start | bytes 98312 | tf_op jit(solution)/shard_map/ppermute | solution.py:363
  68.6 1.2 %collective-permute-start.20 = (f32[32,256]{1,0:T(8,128)S(1)}, f32[32,256]{1,0:T(8,128)S(1)}, u32[]{:S(2)}, u32[]{:S(2)}) collective-permute-start(f32[32,256]{1,0:T(8,128)S(1)} %add_add_fusion.3), channel_id=1, source_target_pairs={{0,9},{1,8},{2,11},{3,10},{4,13},{5,12},{6,15},{7,14},{8,1},{9,0},... | collective-permute-start | bytes 98312 | tf_op jit(solution)/shard_map/ppermute | solution.py:363
  69.8 1.8 %collective-permute-done.22 = f32[32,256]{1,0:T(8,128)S(1)} collective-permute-done((f32[32,256]{1,0:T(8,128)S(1)}, f32[32,256]{1,0:T(8,128)S(1)}, u32[]{:S(2)}, u32[]{:S(2)}) %collective-permute-start.22) | collective-permute-done | bytes 32800 | tf_op jit(solution)/shard_map/ppermute | solution.py:363
  71.6 0.9 %collective-permute-done.21 = f32[32,256]{1,0:T(8,128)S(1)} collective-permute-done((f32[32,256]{1,0:T(8,128)S(1)}, f32[32,256]{1,0:T(8,128)S(1)}, u32[]{:S(2)}, u32[]{:S(2)}) %collective-permute-start.21) | collective-permute-done | bytes 32800 | tf_op jit(solution)/shard_map/ppermute | solution.py:363
  72.5 0.0 collective-permute-done.20
  72.5 0.4 collective-permute-start.23
  72.9 0.4 next_gram.1
  73.3 0.5 collective-permute-done.23
  73.8 3.6 %second_solve.1 = (bf16[64,2,8,128]{3,2,1,0:T(8,128)(2,1)}, f32[2,64,192]{2,1,0:T(8,128)}, f32[2,64,64]{2,1,0:T(8,128)}) custom-call(f32[64,256]{1,0:T(8,128)S(1)} %pad_maximum_fusion.5.cross, bf16[192,192]{1,0:T(8,128)(2,1)S(1)} %get-tuple-element.41.own_high, bf16[192,192]{1,0:T(8,128)(2,1)S(1)} %get-tuple-element.42.own_low, ...), custom_call_target="tpu_custom_call" | custom-call | bytes 1982464 | tf_op jit(solution)/shard_map/second_solve/pallas_call | solution.py:394
  (28 shorter events, 0.4 us)
Async XLA Ops:
  0.6 1.0 %slice-start = ((bf16[3,64,2,8,128]{4,3,2,1,0:T(8,128)(2,1)}), bf16[1,64,2,8,128]{4,3,2,1,0:T(8,128)(2,1)S(1)}, s32[]{:S(2)}) async-start(bf16[3,64,2,8,128]{4,3,2,1,0:T(8,128)(2,1)} %param.3), calls=%async_computation | async-start | bytes 524288 | tf_op jit(solution)/shard_map/slice | solution.py:433
  1.7 3.1 %copy-start = (s32[2,8,128]{2,1,0:T(8,128)S(1)}, s32[2,8,128]{2,1,0:T(8,128)}, u32[]{:S(2)}) copy-start(s32[2,8,128]{2,1,0:T(8,128)} %param.4) | copy-start | bytes 24580
  1.7 3.1 %copy-start.1 = (f32[8,27]{1,0:T(8,128)S(1)}, f32[8,27]{1,0:T(8,128)}, u32[]{:S(2)}) copy-start(f32[8,27]{1,0:T(8,128)} %table.1) | copy-start | bytes 2596
  1.7 5.2 %copy-start.2 = (bf16[3,64,2,8,128]{4,3,2,1,0:T(8,128)(2,1)S(1)}, bf16[3,64,2,8,128]{4,3,2,1,0:T(8,128)(2,1)}, u32[]{:S(2)}) copy-start(bf16[3,64,2,8,128]{4,3,2,1,0:T(8,128)(2,1)} %param.3) | copy-start | bytes 2359300
  1.8 6.5 %collective-permute-start = (bf16[64,1024]{1,0:T(8,128)(2,1)S(1)}, bf16[64,1024]{1,0:T(8,128)(2,1)S(1)}, u32[]{:S(2)}, u32[]{:S(2)}) collective-permute-start(bf16[64,1024]{1,0:T(8,128)(2,1)S(1)} %get-tuple-element.64), channel_id=1, source_target_pairs={{0,4},{4,0},{8,12},{12,8},{16,20},{20,16},{24,28},{28,24},{1,5},{5... | collective-permute-start | bytes 393224 | tf_op jit(solution)/shard_map/ppermute | solution.py:28
  6.2 2.1 %collective-permute-start.1 = (bf16[64,1024]{1,0:T(8,128)(2,1)S(1)}, bf16[64,1024]{1,0:T(8,128)(2,1)S(1)}, u32[]{:S(2)}, u32[]{:S(2)}) collective-permute-start(bf16[64,1024]{1,0:T(8,128)(2,1)S(1)} %get-tuple-element.26), channel_id=1, source_target_pairs={{4,8},{8,4},{12,16},{16,12},{20,24},{24,20},{5,9},{9,5},{13,17},{1... | collective-permute-start | bytes 393224 | tf_op jit(solution)/shard_map/ppermute | solution.py:30
  8.4 4.1 %collective-permute-start.3 = (bf16[64,512]{1,0:T(8,128)(2,1)S(1)}, bf16[64,512]{1,0:T(8,128)(2,1)S(1)}, u32[]{:S(2)}, u32[]{:S(2)}) collective-permute-start(bf16[64,512]{1,0:T(8,128)(2,1)S(1)} %get-tuple-element.77), channel_id=1, source_target_pairs={{1,2},{2,1},{0,3},{3,0},{5,6},{6,5},{4,7},{7,4},{9,10},{10,9},{8,1... | collective-permute-start | bytes 196616 | tf_op jit(solution)/shard_map/ppermute | solution.py:30
  8.8 3.7 %collective-permute-start.2 = (bf16[64,512]{1,0:T(8,128)(2,1)S(1)}, bf16[64,512]{1,0:T(8,128)(2,1)S(1)}, u32[]{:S(2)}, u32[]{:S(2)}) collective-permute-start(bf16[64,512]{1,0:T(8,128)(2,1)S(1)} %get-tuple-element.78), channel_id=1, source_target_pairs={{0,1},{1,0},{2,3},{3,2},{4,5},{5,4},{6,7},{7,6},{8,9},{9,8},{10,11... | collective-permute-start | bytes 196616 | tf_op jit(solution)/shard_map/ppermute | solution.py:28
  13.7 1.3 %collective-permute-start.4 = (f32[32,640]{1,0:T(8,128)S(1)}, f32[32,640]{1,0:T(8,128)S(1)}, u32[]{:S(2)}, u32[]{:S(2)}) collective-permute-start(f32[32,640]{1,0:T(8,128)S(1)} %slice_select_fusion), channel_id=1, source_target_pairs={{0,1},{1,0},{2,3},{3,2},{4,5},{5,4},{6,7},{7,6},{8,9},{9,8},{10,11... | collective-permute-start | bytes 245768 | tf_op jit(solution)/shard_map/ppermute | solution.py:363
  15.0 10.0 %collective-permute-start.7 = (f32[32,640]{1,0:T(8,128)S(1)}, f32[32,640]{1,0:T(8,128)S(1)}, u32[]{:S(2)}, u32[]{:S(2)}) collective-permute-start(f32[32,640]{1,0:T(8,128)S(1)} %select_add_fusion), channel_id=1, source_target_pairs={{0,6},{1,7},{2,4},{3,5},{4,2},{5,3},{6,0},{7,1},{8,14},{9,15},{10,... | collective-permute-start | bytes 245768 | tf_op jit(solution)/shard_map/ppermute | solution.py:363
  22.2 4.7 %collective-permute-start.6 = (f32[32,640]{1,0:T(8,128)S(1)}, f32[32,640]{1,0:T(8,128)S(1)}, u32[]{:S(2)}, u32[]{:S(2)}) collective-permute-start(f32[32,640]{1,0:T(8,128)S(1)} %select_add_fusion), channel_id=1, source_target_pairs={{0,5},{1,4},{2,7},{3,6},{4,1},{5,0},{6,3},{7,2},{8,13},{9,12},{10,... | collective-permute-start | bytes 245768 | tf_op jit(solution)/shard_map/ppermute | solution.py:363
  22.2 4.7 %collective-permute-start.5 = (f32[32,640]{1,0:T(8,128)S(1)}, f32[32,640]{1,0:T(8,128)S(1)}, u32[]{:S(2)}, u32[]{:S(2)}) collective-permute-start(f32[32,640]{1,0:T(8,128)S(1)} %select_add_fusion), channel_id=1, source_target_pairs={{0,3},{1,2},{2,1},{3,0},{4,7},{5,6},{6,5},{7,4},{8,11},{9,10},{10,... | collective-permute-start | bytes 245768 | tf_op jit(solution)/shard_map/ppermute | solution.py:363
  26.9 7.6 %collective-permute-start.10 = (f32[32,640]{1,0:T(8,128)S(1)}, f32[32,640]{1,0:T(8,128)S(1)}, u32[]{:S(2)}, u32[]{:S(2)}) collective-permute-start(f32[32,640]{1,0:T(8,128)S(1)} %add_add_fusion.1), channel_id=1, source_target_pairs={{0,24},{1,25},{2,26},{3,27},{4,28},{5,29},{6,30},{7,31},{8,16},{9,... | collective-permute-start | bytes 245768 | tf_op jit(solution)/shard_map/ppermute | solution.py:363
  31.6 6.4 %collective-permute-start.9 = (f32[32,640]{1,0:T(8,128)S(1)}, f32[32,640]{1,0:T(8,128)S(1)}, u32[]{:S(2)}, u32[]{:S(2)}) collective-permute-start(f32[32,640]{1,0:T(8,128)S(1)} %add_add_fusion.1), channel_id=1, source_target_pairs={{0,17},{1,16},{2,19},{3,18},{4,21},{5,20},{6,23},{7,22},{8,25},{9,... | collective-permute-start | bytes 245768 | tf_op jit(solution)/shard_map/ppermute | solution.py:363
  31.6 6.4 %collective-permute-start.8 = (f32[32,640]{1,0:T(8,128)S(1)}, f32[32,640]{1,0:T(8,128)S(1)}, u32[]{:S(2)}, u32[]{:S(2)}) collective-permute-start(f32[32,640]{1,0:T(8,128)S(1)} %add_add_fusion.1), channel_id=1, source_target_pairs={{0,9},{1,8},{2,11},{3,10},{4,13},{5,12},{6,15},{7,14},{8,1},{9,0},... | collective-permute-start | bytes 245768 | tf_op jit(solution)/shard_map/ppermute | solution.py:363
  38.1 1.5 %collective-permute-start.11 = (f32[32,640]{1,0:T(8,128)S(1)}, f32[32,640]{1,0:T(8,128)S(1)}, u32[]{:S(2)}, u32[]{:S(2)}) collective-permute-start(f32[32,640]{1,0:T(8,128)S(1)} %add_add_fusion), channel_id=1, source_target_pairs={{0,1},{1,0},{2,3},{3,2},{4,5},{5,4},{6,7},{7,6},{8,9},{9,8},{10,11... | collective-permute-start | bytes 245768 | tf_op jit(solution)/shard_map/ppermute | solution.py:363
  42.8 4.4 %collective-permute-start.13 = (bf16[64,1024]{1,0:T(8,128)(2,1)S(1)}, bf16[64,1024]{1,0:T(8,128)(2,1)S(1)}, u32[]{:S(2)}, u32[]{:S(2)}) collective-permute-start(bf16[64,1024]{1,0:T(8,128)(2,1)S(1)} %get-tuple-element.55), channel_id=1, source_target_pairs={{4,8},{8,4},{12,16},{16,12},{20,24},{24,20},{5,9},{9,5},{13,17},{1... | collective-permute-start | bytes 393224 | tf_op jit(solution)/shard_map/ppermute | solution.py:30
  43.4 9.0 %collective-permute-start.12 = (bf16[64,1024]{1,0:T(8,128)(2,1)S(1)}, bf16[64,1024]{1,0:T(8,128)(2,1)S(1)}, u32[]{:S(2)}, u32[]{:S(2)}) collective-permute-start(bf16[64,1024]{1,0:T(8,128)(2,1)S(1)} %get-tuple-element.56), channel_id=1, source_target_pairs={{0,4},{4,0},{8,12},{12,8},{16,20},{20,16},{24,28},{28,24},{1,5},{5... | collective-permute-start | bytes 393224 | tf_op jit(solution)/shard_map/ppermute | solution.py:28
  52.5 4.2 %collective-permute-start.15 = (bf16[64,512]{1,0:T(8,128)(2,1)S(1)}, bf16[64,512]{1,0:T(8,128)(2,1)S(1)}, u32[]{:S(2)}, u32[]{:S(2)}) collective-permute-start(bf16[64,512]{1,0:T(8,128)(2,1)S(1)} %get-tuple-element.69), channel_id=1, source_target_pairs={{1,2},{2,1},{0,3},{3,0},{5,6},{6,5},{4,7},{7,4},{9,10},{10,9},{8,1... | collective-permute-start | bytes 196616 | tf_op jit(solution)/shard_map/ppermute | solution.py:30
  53.1 3.7 %collective-permute-start.14 = (bf16[64,512]{1,0:T(8,128)(2,1)S(1)}, bf16[64,512]{1,0:T(8,128)(2,1)S(1)}, u32[]{:S(2)}, u32[]{:S(2)}) collective-permute-start(bf16[64,512]{1,0:T(8,128)(2,1)S(1)} %get-tuple-element.70), channel_id=1, source_target_pairs={{0,1},{1,0},{2,3},{3,2},{4,5},{5,4},{6,7},{7,6},{8,9},{9,8},{10,11... | collective-permute-start | bytes 196616 | tf_op jit(solution)/shard_map/ppermute | solution.py:28
  57.9 1.3 %collective-permute-start.16 = (f32[32,256]{1,0:T(8,128)S(1)}, f32[32,256]{1,0:T(8,128)S(1)}, u32[]{:S(2)}, u32[]{:S(2)}) collective-permute-start(f32[32,256]{1,0:T(8,128)S(1)} %slice_select_fusion.1), channel_id=1, source_target_pairs={{0,1},{1,0},{2,3},{3,2},{4,5},{5,4},{6,7},{7,6},{8,9},{9,8},{10,11... | collective-permute-start | bytes 98312 | tf_op jit(solution)/shard_map/ppermute | solution.py:363
  59.2 4.8 %collective-permute-start.19 = (f32[32,256]{1,0:T(8,128)S(1)}, f32[32,256]{1,0:T(8,128)S(1)}, u32[]{:S(2)}, u32[]{:S(2)}) collective-permute-start(f32[32,256]{1,0:T(8,128)S(1)} %select_add_fusion.1), channel_id=1, source_target_pairs={{0,6},{1,7},{2,4},{3,5},{4,2},{5,3},{6,0},{7,1},{8,14},{9,15},{10,... | collective-permute-start | bytes 98312 | tf_op jit(solution)/shard_map/ppermute | solution.py:363
  62.0 3.6 %collective-permute-start.18 = (f32[32,256]{1,0:T(8,128)S(1)}, f32[32,256]{1,0:T(8,128)S(1)}, u32[]{:S(2)}, u32[]{:S(2)}) collective-permute-start(f32[32,256]{1,0:T(8,128)S(1)} %select_add_fusion.1), channel_id=1, source_target_pairs={{0,5},{1,4},{2,7},{3,6},{4,1},{5,0},{6,3},{7,2},{8,13},{9,12},{10,... | collective-permute-start | bytes 98312 | tf_op jit(solution)/shard_map/ppermute | solution.py:363
  62.0 3.6 %collective-permute-start.17 = (f32[32,256]{1,0:T(8,128)S(1)}, f32[32,256]{1,0:T(8,128)S(1)}, u32[]{:S(2)}, u32[]{:S(2)}) collective-permute-start(f32[32,256]{1,0:T(8,128)S(1)} %select_add_fusion.1), channel_id=1, source_target_pairs={{0,3},{1,2},{2,1},{3,0},{4,7},{5,6},{6,5},{7,4},{8,11},{9,10},{10,... | collective-permute-start | bytes 98312 | tf_op jit(solution)/shard_map/ppermute | solution.py:363
  65.6 6.0 %collective-permute-start.22 = (f32[32,256]{1,0:T(8,128)S(1)}, f32[32,256]{1,0:T(8,128)S(1)}, u32[]{:S(2)}, u32[]{:S(2)}) collective-permute-start(f32[32,256]{1,0:T(8,128)S(1)} %add_add_fusion.3), channel_id=1, source_target_pairs={{0,24},{1,25},{2,26},{3,27},{4,28},{5,29},{6,30},{7,31},{8,16},{9,... | collective-permute-start | bytes 98312 | tf_op jit(solution)/shard_map/ppermute | solution.py:363
  67.8 4.7 %collective-permute-start.21 = (f32[32,256]{1,0:T(8,128)S(1)}, f32[32,256]{1,0:T(8,128)S(1)}, u32[]{:S(2)}, u32[]{:S(2)}) collective-permute-start(f32[32,256]{1,0:T(8,128)S(1)} %add_add_fusion.3), channel_id=1, source_target_pairs={{0,17},{1,16},{2,19},{3,18},{4,21},{5,20},{6,23},{7,22},{8,25},{9,... | collective-permute-start | bytes 98312 | tf_op jit(solution)/shard_map/ppermute | solution.py:363
  68.6 3.9 %collective-permute-start.20 = (f32[32,256]{1,0:T(8,128)S(1)}, f32[32,256]{1,0:T(8,128)S(1)}, u32[]{:S(2)}, u32[]{:S(2)}) collective-permute-start(f32[32,256]{1,0:T(8,128)S(1)} %add_add_fusion.3), channel_id=1, source_target_pairs={{0,9},{1,8},{2,11},{3,10},{4,13},{5,12},{6,15},{7,14},{8,1},{9,0},... | collective-permute-start | bytes 98312 | tf_op jit(solution)/shard_map/ppermute | solution.py:363
  72.5 1.3 %collective-permute-start.23 = (f32[32,256]{1,0:T(8,128)S(1)}, f32[32,256]{1,0:T(8,128)S(1)}, u32[]{:S(2)}, u32[]{:S(2)}) collective-permute-start(f32[32,256]{1,0:T(8,128)S(1)} %add_add_fusion.2), channel_id=1, source_target_pairs={{0,1},{1,0},{2,3},{3,2},{4,5},{5,4},{6,7},{7,6},{8,9},{9,8},{10,11... | collective-permute-start | bytes 98312 | tf_op jit(solution)/shard_map/ppermute | solution.py:363

commit v15 on v14

--- a/solution.py
+++ b/solution.py
@@ -155,22 +155,67 @@
     stencil(coef, spans, image.shape[0], line, False, write)
 
 
-def stack_gram_kernel(columns, stack, own):
-    at = 0
-    for b in range(0, stack.shape[0], columns):
-        width = stack.shape[0] - b
-        own[:, at : at + width] = dot(stack[b : b + columns], stack[b:], NT)
-        at += width
-
-
-def first_image_kernel(spans, coef, stack, own, partial, xlo, xhi, ylo, yhi, image, cross):
+def places(size):
+    return [lax.broadcasted_iota(jnp.int32, (size, size), dim) for dim in (0, 1)]
+
+
+def diagonal_of(square, axis):
+    row, column = places(square.shape[0])
+    return jnp.sum(jnp.where(row == column, square, 0.0), axis=axis, keepdims=True)
+
+
+def two_in_one(one, two):
+    row, column = places(one.shape[0])
+    return jnp.where(row >= column, one, two), diagonal_of(two, 0)
+
+
+def both_of(packed, diagonal):
+    row, column = places(packed.shape[0])
+    turned = packed.T
+    two = jnp.where(row < column, packed, turned)
+    return jnp.where(row >= column, packed, turned), jnp.where(row == column, diagonal, two)
+
+
+def stack_gram_kernel(columns, stack, sides, pair, last, diagonal):
+    parts = [stack[b * columns : (b + 1) * columns] for b in range(3)]
+    sides[0] = dot(parts[0], parts[1], NT)
+    sides[1] = dot(parts[0], parts[2], NT)
+    sides[2] = dot(parts[1], parts[2], NT)
+    pair[...], diagonal[...] = two_in_one(dot(parts[0], parts[0], NT), dot(parts[1], parts[1], NT))
+    last[...] = dot(parts[2], parts[2], NT)
+
+
+def first_image_kernel(
+    spans, coef, stack, sides, pair, last, diagonal, partial, xlo, xhi, ylo, yhi, image, cross
+):
     columns = image.shape[0]
-    fields = stack.shape[0]
     complete(image, partial, coef, spans, xlo, xhi, ylo, yhi)
     w = image[...]
-    cross[:, :fields] = dot(w, stack[...], NT)
-    cross[:, fields : fields + columns] = dot(w, w, NT)
-    cross[:, fields + columns :] = own[...]
+    first = dot(w, stack[...], NT)
+    corner, own_diagonal = two_in_one(last[...], dot(w, w, NT))
+    rows = [
+        first[:, : 2 * columns],
+        jnp.concatenate([first[:, 2 * columns :], sides[0]], axis=1),
+        jnp.concatenate([sides[1], sides[2]], axis=1),
+        jnp.concatenate([pair[...], corner], axis=1),
+    ]
+    for i, row in enumerate(rows):
+        cross[i * columns : (i + 1) * columns] = row
+    rest = jnp.concatenate([diagonal[...], own_diagonal], axis=1)
+    rest = jnp.broadcast_to(rest, (cross.shape[0] - 4 * columns, 2 * columns))
+    cross[4 * columns :] = rest
+
+
+def opened(cross, columns, scale):
+    parts = [cross[i * columns : (i + 1) * columns] * scale for i in range(4)]
+    diagonals = cross[4 * columns : 4 * columns + 1] * scale
+    first = jnp.concatenate([parts[0], parts[1][:, :columns]], axis=1)
+    side = parts[1][:, columns:], parts[2][:, :columns], parts[2][:, columns:]
+    one, two = both_of(parts[3][:, :columns], diagonals[:, :columns])
+    three, square = both_of(parts[3][:, columns:], diagonals[:, columns:])
+    gram = [[one, side[0], side[1]], [side[0].T, two, side[2]], [side[1].T, side[2].T, three]]
+    gram = jnp.concatenate([jnp.concatenate(row, axis=1) for row in gram], axis=0)
+    return first, square, gram
 
 
 def second_image_kernel(spans, coef, stack, block, partial, xlo, xhi, ylo, yhi, image, cross):
@@ -266,47 +311,23 @@
     return jnp.where(above, done[:, :size] * (across * scale), 0.0), done[:, size:] * scale
 
 
-def project(cross, own, scale):
-    fields = own[0].shape[0]
-    first = cross[:, :fields] * scale
+def project(first, square, own):
     first_parts = split(first)
     first_low = first_parts[0]
     second = first - dots((first_low,), own)
     second_low = second.astype(jnp.bfloat16)
     used = (first_low, second_low)
-    square = cross[:, fields:] * scale
-    diagonal = jnp.where(
-        lax.broadcasted_iota(jnp.int32, square.shape, 0)
-        == lax.broadcasted_iota(jnp.int32, square.shape, 1),
-        square,
-        0.0,
-    )
-    sizes = [jnp.sum(diagonal, axis=axis, keepdims=True) for axis in (1, 0)]
+    sizes = [diagonal_of(square, axis) for axis in (1, 0)]
     square = square - dots(used, first_parts, NT)
     rest = second - dots((second_low,), own)
     square = square - dots(split(rest), used, NT)
     return used, first + second, rest, square, sizes
 
 
-def unpacked(upper, columns, fields):
-    rows, at = [], 0
-    for b in range(0, fields, columns):
-        rows.append((b, upper[:, at : at + fields - b]))
-        at += fields - b
-    whole = []
-    for b, row in rows:
-        left = [above[:, b - a : b - a + columns].T for a, above in rows if a < b]
-        whole.append(jnp.concatenate(left + [row], axis=1))
-    return jnp.concatenate(whole, axis=0)
-
-
 def first_solve_kernel(scale, cross, stack, image, block, proj, low, rest, square, inverse):
     columns = image.shape[0]
-    fields = stack.shape[0]
-    gram = unpacked(cross[:, fields + columns :] * scale, columns, fields)
-    used, proj[...], rest[...], square_here, sizes = project(
-        cross[:, : fields + columns], split(gram), scale
-    )
+    first, own_square, gram = opened(cross, columns, scale)
+    used, proj[...], rest[...], square_here, sizes = project(first, own_square, split(gram))
     square[...] = square_here
     moved = dot(jnp.concatenate(used, axis=0), stack[...])
     w = image[...].astype(jnp.float32) - moved[:columns] - moved[columns:]
@@ -320,9 +341,8 @@
 
 def next_gram_kernel(scale, cross, rest, square, inverse, high, low):
     columns = square.shape[0]
-    fields = rest.shape[1]
-    kept = fields - columns
-    gram = unpacked(cross[:, fields + columns :] * scale, columns, fields)
+    kept = rest.shape[1] - columns
+    _, _, gram = opened(cross, columns, scale)
     mixed = dots((inverse[...],), split(rest[:, columns:]))
     corner = dots((inverse[...],), split(square[...]))
     corner = dots(split(corner), (inverse[...],), NT)
@@ -340,7 +360,11 @@
 ):
     columns = image.shape[0]
     kept = stack.shape[0] - columns
-    used, proj[1], _, square, sizes = project(cross[...], (own_high[...], own_low[...]), scale)
+    fields = stack.shape[0]
+    sums = cross[...] * scale
+    used, proj[1], _, square, sizes = project(
+        sums[:, :fields], sums[:, fields:], (own_high[...], own_low[...])
+    )
     proj[0] = proj_in[...]
     low[0] = low_in[...]
     both = jnp.concatenate(used, axis=0)
@@ -414,13 +438,15 @@
 
     stack = basis.reshape(fields, cells)
     coef = coefficients(table, cell_map)
-    (own,) = call(
+    own = call(
         functools.partial(stack_gram_kernel, columns),
         "stack_gram",
-        [((columns, columns * blocks * (blocks + 1) // 2), f32)],
+        [((blocks, columns, columns), f32), ((columns, columns), f32), ((columns, columns), f32),
+         ((1, columns), f32)],
         stack,
         flops=2 * fields * fields * cells,
     )
+
     def inner_image(block):
         return call(
             functools.partial(inner_image_kernel, spans),
@@ -432,12 +458,11 @@
 
     last = basis[blocks - 1].reshape(columns, cells)
     around, partial, (stack, own) = neighbours(last, *spans, inner_image(last), (stack, own))
-    packed = fields + columns + own.shape[1]
     image, cross = call(
         functools.partial(first_image_kernel, spans),
         "first_image",
-        [((columns, cells), bf16), ((columns, packed), f32)],
-        coef, stack, own, partial, *around,
+        [((columns, cells), bf16), ((4 * columns + 16, 2 * columns), f32)],
+        coef, stack, *own, partial, *around,
     )
     cross = whole_sum(cross)
     block, proj, low, rest, square, inverse = call(

time: 77.6 us -> 76.7 us (0.988)
  no operation moved by 1% of the time
where the time goes in v15:
time: 76.7 us; the launch traced here: 76.5 us
  starting transfers between devices  32.2 us (42%)
  waiting for transfers between devices  29.5 us (38%)
  Pallas kernels  12.1 us (16%)
  local copies, waits for them, and re-layouts  1.47 us (2%)
  between operations  0.93 us (1%)
    ppermute x16, starting transfers between devices, partner(): return lax.ppermute(part, axes, [(i, i ^ mask) for i in range(count)])  21.1 us
    ppermute x16, waiting for transfers between devices, partner(): return lax.ppermute(part, axes, [(i, i ^ mask) for i in range(count)])  19.4 us
    pallas_call x8, Pallas kernels, call(): pl.pallas_call(kernel, out_shape=[jax.ShapeDtypeStruct(shape, dtype) for...  11.3 us
    ppermute x4, starting transfers between devices, swaps(): inner = lax.ppermute(near, axis, [(i, i ^ 1) for i in range(count)])  8.73 us
    ppermute x4, waiting for transfers between devices, swaps(): inner = lax.ppermute(near, axis, [(i, i ^ 1) for i in range(count)])  5.46 us
    ppermute x4, waiting for transfers between devices, swaps(): outer = lax.ppermute(far, axis, pairs)  4.72 us
    ppermute x4, starting transfers between devices, swaps(): outer = lax.ppermute(far, axis, pairs)  2.31 us
  transfers between devices with their start and end apart: 24, of which 16 were waited for; matrix products, arithmetic and copies ran while one was open for 0% of the time, Pallas kernels for 4%

profile of v15, /device:TPU:0, one launch (start us, length us, event | category | flops | bytes accessed | tf_op | source)
XLA Modules:
  0.0 76.5 jit_solution(13621684650825931535)
XLA Ops:
  0.6 0.0 slice-start
  0.7 0.9 %slice-done = bf16[1,64,2,8,128]{4,3,2,1,0:T(8,128)(2,1)S(1)} async-done(((bf16[3,64,2,8,128]{4,3,2,1,0:T(8,128)(2,1)}), bf16[1,64,2,8,128]{4,3,2,1,0:T(8,128)(2,1)S(1)}, s32[]{:S(2)}) %slice-start) | async-done | bytes 262168 | tf_op jit(solution)/shard_map/slice | solution.py:459
  1.6 0.1 reshape_squeeze.3.fields
  1.7 0.0 copy-start
  1.7 0.0 copy-start.1
  1.7 0.0 copy-start.2
  1.8 3.0 %collective-permute-start = (bf16[64,1024]{1,0:T(8,128)(2,1)S(1)}, bf16[64,1024]{1,0:T(8,128)(2,1)S(1)}, u32[]{:S(2)}, u32[]{:S(2)}) collective-permute-start(bf16[64,1024]{1,0:T(8,128)(2,1)S(1)} %get-tuple-element.78), channel_id=1, source_target_pairs={{0,4},{4,0},{8,12},{12,8},{16,20},{20,16},{24,28},{28,24},{1,5},{5... | collective-permute-start | bytes 393224 | tf_op jit(solution)/shard_map/ppermute | solution.py:28
  4.8 0.8 coefficients.1.coef
  5.6 0.7 inner_image.2.partial
  6.2 0.7 collective-permute-start.1
  6.9 0.3 reshape.13.stack
  7.3 0.6 stack_gram.1
  7.9 0.4 collective-permute-done
  8.3 0.0 collective-permute-done.1
  8.4 0.4 collective-permute-start.3
  8.8 1.5 %collective-permute-start.2 = (bf16[64,512]{1,0:T(8,128)(2,1)S(1)}, bf16[64,512]{1,0:T(8,128)(2,1)S(1)}, u32[]{:S(2)}, u32[]{:S(2)}) collective-permute-start(bf16[64,512]{1,0:T(8,128)(2,1)S(1)} %get-tuple-element.92), channel_id=1, source_target_pairs={{0,1},{1,0},{2,3},{3,2},{4,5},{5,4},{6,7},{7,6},{8,9},{9,8},{10,11... | collective-permute-start | bytes 196616 | tf_op jit(solution)/shard_map/ppermute | solution.py:28
  10.3 2.2 %collective-permute-done.3 = bf16[64,512]{1,0:T(8,128)(2,1)S(1)} collective-permute-done((bf16[64,512]{1,0:T(8,128)(2,1)S(1)}, bf16[64,512]{1,0:T(8,128)(2,1)S(1)}, u32[]{:S(2)}, u32[]{:S(2)}) %collective-permute-start.3) | collective-permute-done | bytes 65568 | tf_op jit(solution)/shard_map/ppermute | solution.py:30
  12.5 0.0 collective-permute-done.2
  12.5 1.1 %first_image.1 = (bf16[64,2048]{1,0:T(8,128)(2,1)S(1)}, f32[272,128]{1,0:T(8,128)S(1)}) custom-call(f32[27,16,128]{2,1,0:T(8,128)S(1)} %coefficients.1.coef, bf16[192,2048]{1,0:T(8,128)(2,1)S(1)} %reshape.13.stack, f32[3,64,64]{2,1,0:T(8,128)S(1)} %get-tuple-element.39.sides, f32[64,64]{1,0:T(8,128)S(1)} %get-tuple-element.40.pair, ...), custom_call_target="tpu_custom_call" | custom-call | bytes 2408704 | tf_op jit(solution)/shard_map/first_image/pallas_call | solution.py:418
  13.7 0.2 collective-permute-start.4
  13.9 1.1 %collective-permute-done.4 = f32[136,128]{1,0:T(8,128)S(1)} collective-permute-done((f32[136,128]{1,0:T(8,128)S(1)}, f32[136,128]{1,0:T(8,128)S(1)}, u32[]{:S(2)}, u32[]{:S(2)}) %collective-permute-start.4) | collective-permute-done | bytes 69664 | tf_op jit(solution)/shard_map/ppermute | solution.py:387
  15.0 7.2 %collective-permute-start.7 = (f32[136,128]{1,0:T(8,128)S(1)}, f32[136,128]{1,0:T(8,128)S(1)}, u32[]{:S(2)}, u32[]{:S(2)}) collective-permute-start(f32[136,128]{1,0:T(8,128)S(1)} %select_add_fusion), channel_id=1, source_target_pairs={{0,6},{1,7},{2,4},{3,5},{4,2},{5,3},{6,0},{7,1},{8,14},{9,15},{10,... | collective-permute-start | bytes 208904 | tf_op jit(solution)/shard_map/ppermute | solution.py:387
  22.2 0.0 collective-permute-start.6
  22.2 0.6 collective-permute-start.5
  22.8 1.9 %collective-permute-done.7 = f32[136,128]{1,0:T(8,128)S(1)} collective-permute-done((f32[136,128]{1,0:T(8,128)S(1)}, f32[136,128]{1,0:T(8,128)S(1)}, u32[]{:S(2)}, u32[]{:S(2)}) %collective-permute-start.7) | collective-permute-done | bytes 69664 | tf_op jit(solution)/shard_map/ppermute | solution.py:387
  24.7 1.9 %collective-permute-done.6 = f32[136,128]{1,0:T(8,128)S(1)} collective-permute-done((f32[136,128]{1,0:T(8,128)S(1)}, f32[136,128]{1,0:T(8,128)S(1)}, u32[]{:S(2)}, u32[]{:S(2)}) %collective-permute-start.6) | collective-permute-done | bytes 69664 | tf_op jit(solution)/shard_map/ppermute | solution.py:387
  26.6 0.0 collective-permute-done.5
  26.6 4.6 %collective-permute-start.10 = (f32[136,128]{1,0:T(8,128)S(1)}, f32[136,128]{1,0:T(8,128)S(1)}, u32[]{:S(2)}, u32[]{:S(2)}) collective-permute-start(f32[136,128]{1,0:T(8,128)S(1)} %add_add_fusion.1), channel_id=1, source_target_pairs={{0,24},{1,25},{2,26},{3,27},{4,28},{5,29},{6,30},{7,31},{8,16},{9,... | collective-permute-start | bytes 208904 | tf_op jit(solution)/shard_map/ppermute | solution.py:387
  31.2 0.0 collective-permute-start.9
  31.2 0.4 collective-permute-start.8
  31.6 2.3 %collective-permute-done.10 = f32[136,128]{1,0:T(8,128)S(1)} collective-permute-done((f32[136,128]{1,0:T(8,128)S(1)}, f32[136,128]{1,0:T(8,128)S(1)}, u32[]{:S(2)}, u32[]{:S(2)}) %collective-permute-start.10) | collective-permute-done | bytes 69664 | tf_op jit(solution)/shard_map/ppermute | solution.py:387
  33.9 3.2 %collective-permute-done.9 = f32[136,128]{1,0:T(8,128)S(1)} collective-permute-done((f32[136,128]{1,0:T(8,128)S(1)}, f32[136,128]{1,0:T(8,128)S(1)}, u32[]{:S(2)}, u32[]{:S(2)}) %collective-permute-start.9) | collective-permute-done | bytes 69664 | tf_op jit(solution)/shard_map/ppermute | solution.py:387
  37.1 0.0 collective-permute-done.8
  37.1 0.2 collective-permute-start.11
  37.3 1.1 %collective-permute-done.11 = f32[136,128]{1,0:T(8,128)S(1)} collective-permute-done((f32[136,128]{1,0:T(8,128)S(1)}, f32[136,128]{1,0:T(8,128)S(1)}, u32[]{:S(2)}, u32[]{:S(2)}) %collective-permute-start.11) | collective-permute-done | bytes 69664 | tf_op jit(solution)/shard_map/ppermute | solution.py:387
  38.4 3.1 %first_solve.1 = (bf16[64,2048]{1,0:T(8,128)(2,1)S(1)}, f32[64,192]{1,0:T(8,128)S(1)}, f32[64,64]{1,0:T(8,128)S(1)}, f32[64,192]{1,0:T(8,128)S(1)}, f32[64,64]{1,0:T(8,128)S(1)}, /*index=5*/bf16[64,64]{1,0:T(8,128)(2,1)S(1)}) custom-call(f32[272,128]{1,0:T(8,128)S(1)} %pad_maximum_fusion.cross, bf16[192,2048]{1,0:T(8,128)(2,1)S(1)} %reshape.13.stack, ...), custom_call_target="tpu_custom_call" | custom-call | bytes 1589248 | tf_op jit(solution)/shard_map/first_solve/pallas_call | solution.py:418
  41.6 0.7 collective-permute-start.13
  42.3 3.7 %collective-permute-start.12 = (bf16[64,1024]{1,0:T(8,128)(2,1)S(1)}, bf16[64,1024]{1,0:T(8,128)(2,1)S(1)}, u32[]{:S(2)}, u32[]{:S(2)}) collective-permute-start(bf16[64,1024]{1,0:T(8,128)(2,1)S(1)} %get-tuple-element.70), channel_id=1, source_target_pairs={{0,4},{4,0},{8,12},{12,8},{16,20},{20,16},{24,28},{28,24},{1,5},{5... | collective-permute-start | bytes 393224 | tf_op jit(solution)/shard_map/ppermute | solution.py:28
  46.0 0.0 collective-permute-done.13
  46.0 5.0 %collective-permute-done.12 = bf16[64,1024]{1,0:T(8,128)(2,1)S(1)} collective-permute-done((bf16[64,1024]{1,0:T(8,128)(2,1)S(1)}, bf16[64,1024]{1,0:T(8,128)(2,1)S(1)}, u32[]{:S(2)}, u32[]{:S(2)}) %collective-permute-start.12) | collective-permute-done | bytes 131104 | tf_op jit(solution)/shard_map/ppermute | solution.py:28
  51.2 0.6 collective-permute-start.15
  51.7 0.5 collective-permute-start.14
  52.2 0.7 inner_image.3.partial
  52.9 2.5 %collective-permute-done.15 = bf16[64,512]{1,0:T(8,128)(2,1)S(1)} collective-permute-done((bf16[64,512]{1,0:T(8,128)(2,1)S(1)}, bf16[64,512]{1,0:T(8,128)(2,1)S(1)}, u32[]{:S(2)}, u32[]{:S(2)}) %collective-permute-start.15) | collective-permute-done | bytes 65568 | tf_op jit(solution)/shard_map/ppermute | solution.py:30
  55.4 0.0 collective-permute-done.14
  55.4 1.1 %second_image.1 = (bf16[64,2048]{1,0:T(8,128)(2,1)S(1)}, f32[64,256]{1,0:T(8,128)S(1)}) custom-call(f32[27,16,128]{2,1,0:T(8,128)S(1)} %coefficients.1.coef, bf16[192,2048]{1,0:T(8,128)(2,1)S(1)} %reshape.13.stack, bf16[64,2048]{1,0:T(8,128)(2,1)S(1)} %get-tuple-element.48.fields.block.last, f32[64,2048]{1,0:T(8,128)S(1)} %inner_image.3.partial, ...), custom_call_target="tpu_custom_call" | custom-call | bytes 2514944 | tf_op jit(solution)/shard_map/second_image/pallas_call | solution.py:418
  56.5 0.2 collective-permute-start.16
  56.7 1.1 %collective-permute-done.16 = f32[32,256]{1,0:T(8,128)S(1)} collective-permute-done((f32[32,256]{1,0:T(8,128)S(1)}, f32[32,256]{1,0:T(8,128)S(1)}, u32[]{:S(2)}, u32[]{:S(2)}) %collective-permute-start.16) | collective-permute-done | bytes 32800 | tf_op jit(solution)/shard_map/ppermute | solution.py:387
  57.8 2.8 %collective-permute-start.19 = (f32[32,256]{1,0:T(8,128)S(1)}, f32[32,256]{1,0:T(8,128)S(1)}, u32[]{:S(2)}, u32[]{:S(2)}) collective-permute-start(f32[32,256]{1,0:T(8,128)S(1)} %select_add_fusion.1), channel_id=1, source_target_pairs={{0,6},{1,7},{2,4},{3,5},{4,2},{5,3},{6,0},{7,1},{8,14},{9,15},{10,... | collective-permute-start | bytes 98312 | tf_op jit(solution)/shard_map/ppermute | solution.py:387
  60.6 0.0 collective-permute-start.18
  60.6 0.6 collective-permute-start.17
  61.3 1.4 %collective-permute-done.19 = f32[32,256]{1,0:T(8,128)S(1)} collective-permute-done((f32[32,256]{1,0:T(8,128)S(1)}, f32[32,256]{1,0:T(8,128)S(1)}, u32[]{:S(2)}, u32[]{:S(2)}) %collective-permute-start.19) | collective-permute-done | bytes 32800 | tf_op jit(solution)/shard_map/ppermute | solution.py:387
  62.6 1.6 %collective-permute-done.18 = f32[32,256]{1,0:T(8,128)S(1)} collective-permute-done((f32[32,256]{1,0:T(8,128)S(1)}, f32[32,256]{1,0:T(8,128)S(1)}, u32[]{:S(2)}, u32[]{:S(2)}) %collective-permute-start.18) | collective-permute-done | bytes 32800 | tf_op jit(solution)/shard_map/ppermute | solution.py:387
  64.2 0.0 collective-permute-done.17
  64.3 2.1 %collective-permute-start.22 = (f32[32,256]{1,0:T(8,128)S(1)}, f32[32,256]{1,0:T(8,128)S(1)}, u32[]{:S(2)}, u32[]{:S(2)}) collective-permute-start(f32[32,256]{1,0:T(8,128)S(1)} %add_add_fusion.3), channel_id=1, source_target_pairs={{0,24},{1,25},{2,26},{3,27},{4,28},{5,29},{6,30},{7,31},{8,16},{9,... | collective-permute-start | bytes 98312 | tf_op jit(solution)/shard_map/ppermute | solution.py:387
  66.4 1.1 %collective-permute-start.21 = (f32[32,256]{1,0:T(8,128)S(1)}, f32[32,256]{1,0:T(8,128)S(1)}, u32[]{:S(2)}, u32[]{:S(2)}) collective-permute-start(f32[32,256]{1,0:T(8,128)S(1)} %add_add_fusion.3), channel_id=1, source_target_pairs={{0,17},{1,16},{2,19},{3,18},{4,21},{5,20},{6,23},{7,22},{8,25},{9,... | collective-permute-start | bytes 98312 | tf_op jit(solution)/shard_map/ppermute | solution.py:387
  67.5 0.9 %collective-permute-start.20 = (f32[32,256]{1,0:T(8,128)S(1)}, f32[32,256]{1,0:T(8,128)S(1)}, u32[]{:S(2)}, u32[]{:S(2)}) collective-permute-start(f32[32,256]{1,0:T(8,128)S(1)} %add_add_fusion.3), channel_id=1, source_target_pairs={{0,9},{1,8},{2,11},{3,10},{4,13},{5,12},{6,15},{7,14},{8,1},{9,0},... | collective-permute-start | bytes 98312 | tf_op jit(solution)/shard_map/ppermute | solution.py:387
  68.4 1.6 %collective-permute-done.22 = f32[32,256]{1,0:T(8,128)S(1)} collective-permute-done((f32[32,256]{1,0:T(8,128)S(1)}, f32[32,256]{1,0:T(8,128)S(1)}, u32[]{:S(2)}, u32[]{:S(2)}) %collective-permute-start.22) | collective-permute-done | bytes 32800 | tf_op jit(solution)/shard_map/ppermute | solution.py:387
  70.1 1.4 %collective-permute-done.21 = f32[32,256]{1,0:T(8,128)S(1)} collective-permute-done((f32[32,256]{1,0:T(8,128)S(1)}, f32[32,256]{1,0:T(8,128)S(1)}, u32[]{:S(2)}, u32[]{:S(2)}) %collective-permute-start.21) | collective-permute-done | bytes 32800 | tf_op jit(solution)/shard_map/ppermute | solution.py:387
  71.5 0.0 collective-permute-done.20
  71.5 0.2 collective-permute-start.23
  71.8 0.4 next_gram.1
  72.2 0.6 collective-permute-done.23
  72.8 3.6 %second_solve.1 = (bf16[64,2,8,128]{3,2,1,0:T(8,128)(2,1)}, f32[2,64,192]{2,1,0:T(8,128)}, f32[2,64,64]{2,1,0:T(8,128)}) custom-call(f32[64,256]{1,0:T(8,128)S(1)} %pad_maximum_fusion.5.cross, bf16[192,192]{1,0:T(8,128)(2,1)S(1)} %get-tuple-element.55.own_high, bf16[192,192]{1,0:T(8,128)(2,1)S(1)} %get-tuple-element.56.own_low, ...), custom_call_target="tpu_custom_call" | custom-call | bytes 1982464 | tf_op jit(solution)/shard_map/second_solve/pallas_call | solution.py:418
  (28 shorter events, 0.4 us)
Async XLA Ops:
  0.6 1.0 %slice-start = ((bf16[3,64,2,8,128]{4,3,2,1,0:T(8,128)(2,1)}), bf16[1,64,2,8,128]{4,3,2,1,0:T(8,128)(2,1)S(1)}, s32[]{:S(2)}) async-start(bf16[3,64,2,8,128]{4,3,2,1,0:T(8,128)(2,1)} %param.3), calls=%async_computation | async-start | bytes 524288 | tf_op jit(solution)/shard_map/slice | solution.py:459
  1.7 3.1 %copy-start = (s32[2,8,128]{2,1,0:T(8,128)S(1)}, s32[2,8,128]{2,1,0:T(8,128)}, u32[]{:S(2)}) copy-start(s32[2,8,128]{2,1,0:T(8,128)} %param.4) | copy-start | bytes 24580
  1.7 3.1 %copy-start.1 = (f32[8,27]{1,0:T(8,128)S(1)}, f32[8,27]{1,0:T(8,128)}, u32[]{:S(2)}) copy-start(f32[8,27]{1,0:T(8,128)} %table.1) | copy-start | bytes 2596
  1.7 5.2 %copy-start.2 = (bf16[3,64,2,8,128]{4,3,2,1,0:T(8,128)(2,1)S(1)}, bf16[3,64,2,8,128]{4,3,2,1,0:T(8,128)(2,1)}, u32[]{:S(2)}) copy-start(bf16[3,64,2,8,128]{4,3,2,1,0:T(8,128)(2,1)} %param.3) | copy-start | bytes 2359300
  1.8 6.5 %collective-permute-start = (bf16[64,1024]{1,0:T(8,128)(2,1)S(1)}, bf16[64,1024]{1,0:T(8,128)(2,1)S(1)}, u32[]{:S(2)}, u32[]{:S(2)}) collective-permute-start(bf16[64,1024]{1,0:T(8,128)(2,1)S(1)} %get-tuple-element.78), channel_id=1, source_target_pairs={{0,4},{4,0},{8,12},{12,8},{16,20},{20,16},{24,28},{28,24},{1,5},{5... | collective-permute-start | bytes 393224 | tf_op jit(solution)/shard_map/ppermute | solution.py:28
  6.2 2.1 %collective-permute-start.1 = (bf16[64,1024]{1,0:T(8,128)(2,1)S(1)}, bf16[64,1024]{1,0:T(8,128)(2,1)S(1)}, u32[]{:S(2)}, u32[]{:S(2)}) collective-permute-start(bf16[64,1024]{1,0:T(8,128)(2,1)S(1)} %get-tuple-element.33), channel_id=1, source_target_pairs={{4,8},{8,4},{12,16},{16,12},{20,24},{24,20},{5,9},{9,5},{13,17},{1... | collective-permute-start | bytes 393224 | tf_op jit(solution)/shard_map/ppermute | solution.py:30
  8.4 4.1 %collective-permute-start.3 = (bf16[64,512]{1,0:T(8,128)(2,1)S(1)}, bf16[64,512]{1,0:T(8,128)(2,1)S(1)}, u32[]{:S(2)}, u32[]{:S(2)}) collective-permute-start(bf16[64,512]{1,0:T(8,128)(2,1)S(1)} %get-tuple-element.91), channel_id=1, source_target_pairs={{1,2},{2,1},{0,3},{3,0},{5,6},{6,5},{4,7},{7,4},{9,10},{10,9},{8,1... | collective-permute-start | bytes 196616 | tf_op jit(solution)/shard_map/ppermute | solution.py:30
  8.8 3.7 %collective-permute-start.2 = (bf16[64,512]{1,0:T(8,128)(2,1)S(1)}, bf16[64,512]{1,0:T(8,128)(2,1)S(1)}, u32[]{:S(2)}, u32[]{:S(2)}) collective-permute-start(bf16[64,512]{1,0:T(8,128)(2,1)S(1)} %get-tuple-element.92), channel_id=1, source_target_pairs={{0,1},{1,0},{2,3},{3,2},{4,5},{5,4},{6,7},{7,6},{8,9},{9,8},{10,11... | collective-permute-start | bytes 196616 | tf_op jit(solution)/shard_map/ppermute | solution.py:28
  13.7 1.3 %collective-permute-start.4 = (f32[136,128]{1,0:T(8,128)S(1)}, f32[136,128]{1,0:T(8,128)S(1)}, u32[]{:S(2)}, u32[]{:S(2)}) collective-permute-start(f32[136,128]{1,0:T(8,128)S(1)} %slice_select_fusion), channel_id=1, source_target_pairs={{0,1},{1,0},{2,3},{3,2},{4,5},{5,4},{6,7},{7,6},{8,9},{9,8},{10,11... | collective-permute-start | bytes 208904 | tf_op jit(solution)/shard_map/ppermute | solution.py:387
  15.0 9.7 %collective-permute-start.7 = (f32[136,128]{1,0:T(8,128)S(1)}, f32[136,128]{1,0:T(8,128)S(1)}, u32[]{:S(2)}, u32[]{:S(2)}) collective-permute-start(f32[136,128]{1,0:T(8,128)S(1)} %select_add_fusion), channel_id=1, source_target_pairs={{0,6},{1,7},{2,4},{3,5},{4,2},{5,3},{6,0},{7,1},{8,14},{9,15},{10,... | collective-permute-start | bytes 208904 | tf_op jit(solution)/shard_map/ppermute | solution.py:387
  22.2 4.4 %collective-permute-start.6 = (f32[136,128]{1,0:T(8,128)S(1)}, f32[136,128]{1,0:T(8,128)S(1)}, u32[]{:S(2)}, u32[]{:S(2)}) collective-permute-start(f32[136,128]{1,0:T(8,128)S(1)} %select_add_fusion), channel_id=1, source_target_pairs={{0,5},{1,4},{2,7},{3,6},{4,1},{5,0},{6,3},{7,2},{8,13},{9,12},{10,... | collective-permute-start | bytes 208904 | tf_op jit(solution)/shard_map/ppermute | solution.py:387
  22.2 4.4 %collective-permute-start.5 = (f32[136,128]{1,0:T(8,128)S(1)}, f32[136,128]{1,0:T(8,128)S(1)}, u32[]{:S(2)}, u32[]{:S(2)}) collective-permute-start(f32[136,128]{1,0:T(8,128)S(1)} %select_add_fusion), channel_id=1, source_target_pairs={{0,3},{1,2},{2,1},{3,0},{4,7},{5,6},{6,5},{7,4},{8,11},{9,10},{10,... | collective-permute-start | bytes 208904 | tf_op jit(solution)/shard_map/ppermute | solution.py:387
  26.6 7.2 %collective-permute-start.10 = (f32[136,128]{1,0:T(8,128)S(1)}, f32[136,128]{1,0:T(8,128)S(1)}, u32[]{:S(2)}, u32[]{:S(2)}) collective-permute-start(f32[136,128]{1,0:T(8,128)S(1)} %add_add_fusion.1), channel_id=1, source_target_pairs={{0,24},{1,25},{2,26},{3,27},{4,28},{5,29},{6,30},{7,31},{8,16},{9,... | collective-permute-start | bytes 208904 | tf_op jit(solution)/shard_map/ppermute | solution.py:387
  31.2 5.8 %collective-permute-start.9 = (f32[136,128]{1,0:T(8,128)S(1)}, f32[136,128]{1,0:T(8,128)S(1)}, u32[]{:S(2)}, u32[]{:S(2)}) collective-permute-start(f32[136,128]{1,0:T(8,128)S(1)} %add_add_fusion.1), channel_id=1, source_target_pairs={{0,17},{1,16},{2,19},{3,18},{4,21},{5,20},{6,23},{7,22},{8,25},{9,... | collective-permute-start | bytes 208904 | tf_op jit(solution)/shard_map/ppermute | solution.py:387
  31.2 5.8 %collective-permute-start.8 = (f32[136,128]{1,0:T(8,128)S(1)}, f32[136,128]{1,0:T(8,128)S(1)}, u32[]{:S(2)}, u32[]{:S(2)}) collective-permute-start(f32[136,128]{1,0:T(8,128)S(1)} %add_add_fusion.1), channel_id=1, source_target_pairs={{0,9},{1,8},{2,11},{3,10},{4,13},{5,12},{6,15},{7,14},{8,1},{9,0},... | collective-permute-start | bytes 208904 | tf_op jit(solution)/shard_map/ppermute | solution.py:387
  37.1 1.3 %collective-permute-start.11 = (f32[136,128]{1,0:T(8,128)S(1)}, f32[136,128]{1,0:T(8,128)S(1)}, u32[]{:S(2)}, u32[]{:S(2)}) collective-permute-start(f32[136,128]{1,0:T(8,128)S(1)} %add_add_fusion), channel_id=1, source_target_pairs={{0,1},{1,0},{2,3},{3,2},{4,5},{5,4},{6,7},{7,6},{8,9},{9,8},{10,11... | collective-permute-start | bytes 208904 | tf_op jit(solution)/shard_map/ppermute | solution.py:387
  41.6 4.4 %collective-permute-start.13 = (bf16[64,1024]{1,0:T(8,128)(2,1)S(1)}, bf16[64,1024]{1,0:T(8,128)(2,1)S(1)}, u32[]{:S(2)}, u32[]{:S(2)}) collective-permute-start(bf16[64,1024]{1,0:T(8,128)(2,1)S(1)} %get-tuple-element.69), channel_id=1, source_target_pairs={{4,8},{8,4},{12,16},{16,12},{20,24},{24,20},{5,9},{9,5},{13,17},{1... | collective-permute-start | bytes 393224 | tf_op jit(solution)/shard_map/ppermute | solution.py:30
  42.3 8.8 %collective-permute-start.12 = (bf16[64,1024]{1,0:T(8,128)(2,1)S(1)}, bf16[64,1024]{1,0:T(8,128)(2,1)S(1)}, u32[]{:S(2)}, u32[]{:S(2)}) collective-permute-start(bf16[64,1024]{1,0:T(8,128)(2,1)S(1)} %get-tuple-element.70), channel_id=1, source_target_pairs={{0,4},{4,0},{8,12},{12,8},{16,20},{20,16},{24,28},{28,24},{1,5},{5... | collective-permute-start | bytes 393224 | tf_op jit(solution)/shard_map/ppermute | solution.py:28
  51.2 4.2 %collective-permute-start.15 = (bf16[64,512]{1,0:T(8,128)(2,1)S(1)}, bf16[64,512]{1,0:T(8,128)(2,1)S(1)}, u32[]{:S(2)}, u32[]{:S(2)}) collective-permute-start(bf16[64,512]{1,0:T(8,128)(2,1)S(1)} %get-tuple-element.83), channel_id=1, source_target_pairs={{1,2},{2,1},{0,3},{3,0},{5,6},{6,5},{4,7},{7,4},{9,10},{10,9},{8,1... | collective-permute-start | bytes 196616 | tf_op jit(solution)/shard_map/ppermute | solution.py:30
  51.7 3.7 %collective-permute-start.14 = (bf16[64,512]{1,0:T(8,128)(2,1)S(1)}, bf16[64,512]{1,0:T(8,128)(2,1)S(1)}, u32[]{:S(2)}, u32[]{:S(2)}) collective-permute-start(bf16[64,512]{1,0:T(8,128)(2,1)S(1)} %get-tuple-element.84), channel_id=1, source_target_pairs={{0,1},{1,0},{2,3},{3,2},{4,5},{5,4},{6,7},{7,6},{8,9},{9,8},{10,11... | collective-permute-start | bytes 196616 | tf_op jit(solution)/shard_map/ppermute | solution.py:28
  56.5 1.3 %collective-permute-start.16 = (f32[32,256]{1,0:T(8,128)S(1)}, f32[32,256]{1,0:T(8,128)S(1)}, u32[]{:S(2)}, u32[]{:S(2)}) collective-permute-start(f32[32,256]{1,0:T(8,128)S(1)} %slice_select_fusion.1), channel_id=1, source_target_pairs={{0,1},{1,0},{2,3},{3,2},{4,5},{5,4},{6,7},{7,6},{8,9},{9,8},{10,11... | collective-permute-start | bytes 98312 | tf_op jit(solution)/shard_map/ppermute | solution.py:387
  57.8 4.8 %collective-permute-start.19 = (f32[32,256]{1,0:T(8,128)S(1)}, f32[32,256]{1,0:T(8,128)S(1)}, u32[]{:S(2)}, u32[]{:S(2)}) collective-permute-start(f32[32,256]{1,0:T(8,128)S(1)} %select_add_fusion.1), channel_id=1, source_target_pairs={{0,6},{1,7},{2,4},{3,5},{4,2},{5,3},{6,0},{7,1},{8,14},{9,15},{10,... | collective-permute-start | bytes 98312 | tf_op jit(solution)/shard_map/ppermute | solution.py:387
  60.6 3.6 %collective-permute-start.18 = (f32[32,256]{1,0:T(8,128)S(1)}, f32[32,256]{1,0:T(8,128)S(1)}, u32[]{:S(2)}, u32[]{:S(2)}) collective-permute-start(f32[32,256]{1,0:T(8,128)S(1)} %select_add_fusion.1), channel_id=1, source_target_pairs={{0,5},{1,4},{2,7},{3,6},{4,1},{5,0},{6,3},{7,2},{8,13},{9,12},{10,... | collective-permute-start | bytes 98312 | tf_op jit(solution)/shard_map/ppermute | solution.py:387
  60.6 3.6 %collective-permute-start.17 = (f32[32,256]{1,0:T(8,128)S(1)}, f32[32,256]{1,0:T(8,128)S(1)}, u32[]{:S(2)}, u32[]{:S(2)}) collective-permute-start(f32[32,256]{1,0:T(8,128)S(1)} %select_add_fusion.1), channel_id=1, source_target_pairs={{0,3},{1,2},{2,1},{3,0},{4,7},{5,6},{6,5},{7,4},{8,11},{9,10},{10,... | collective-permute-start | bytes 98312 | tf_op jit(solution)/shard_map/ppermute | solution.py:387
  64.3 5.8 %collective-permute-start.22 = (f32[32,256]{1,0:T(8,128)S(1)}, f32[32,256]{1,0:T(8,128)S(1)}, u32[]{:S(2)}, u32[]{:S(2)}) collective-permute-start(f32[32,256]{1,0:T(8,128)S(1)} %add_add_fusion.3), channel_id=1, source_target_pairs={{0,24},{1,25},{2,26},{3,27},{4,28},{5,29},{6,30},{7,31},{8,16},{9,... | collective-permute-start | bytes 98312 | tf_op jit(solution)/shard_map/ppermute | solution.py:387
  66.4 5.1 %collective-permute-start.21 = (f32[32,256]{1,0:T(8,128)S(1)}, f32[32,256]{1,0:T(8,128)S(1)}, u32[]{:S(2)}, u32[]{:S(2)}) collective-permute-start(f32[32,256]{1,0:T(8,128)S(1)} %add_add_fusion.3), channel_id=1, source_target_pairs={{0,17},{1,16},{2,19},{3,18},{4,21},{5,20},{6,23},{7,22},{8,25},{9,... | collective-permute-start | bytes 98312 | tf_op jit(solution)/shard_map/ppermute | solution.py:387
  67.5 4.1 %collective-permute-start.20 = (f32[32,256]{1,0:T(8,128)S(1)}, f32[32,256]{1,0:T(8,128)S(1)}, u32[]{:S(2)}, u32[]{:S(2)}) collective-permute-start(f32[32,256]{1,0:T(8,128)S(1)} %add_add_fusion.3), channel_id=1, source_target_pairs={{0,9},{1,8},{2,11},{3,10},{4,13},{5,12},{6,15},{7,14},{8,1},{9,0},... | collective-permute-start | bytes 98312 | tf_op jit(solution)/shard_map/ppermute | solution.py:387
  71.5 1.3 %collective-permute-start.23 = (f32[32,256]{1,0:T(8,128)S(1)}, f32[32,256]{1,0:T(8,128)S(1)}, u32[]{:S(2)}, u32[]{:S(2)}) collective-permute-start(f32[32,256]{1,0:T(8,128)S(1)} %add_add_fusion.2), channel_id=1, source_target_pairs={{0,1},{1,0},{2,3},{3,2},{4,5},{5,4},{6,7},{7,6},{8,9},{9,8},{10,11... | collective-permute-start | bytes 98312 | tf_op jit(solution)/shard_map/ppermute | solution.py:387

commit v16 on v15

--- a/solution.py
+++ b/solution.py
@@ -17,27 +17,45 @@
     return lax.dot_general(left, right, dims, preferred_element_type=jnp.float32)
 
 
-def swaps(axis, upward, downward, closed, beside=None):
+def swaps(axis, near, far, closed):
     count = lax.axis_size(axis)
     me = lax.axis_index(axis)
     odd = me % 2 == 1
     pairs = [(i, (i - 1 ^ 1) + 1) for i in range(1, count - 1)]
     if closed:
         pairs += [(0, count - 1), (count - 1, 0)]
-    near, far = jnp.where(odd, downward, upward), jnp.where(odd, upward, downward)
     inner = lax.ppermute(near, axis, [(i, i ^ 1) for i in range(count)])
-    far, beside = lax.optimization_barrier((far, beside))
     outer = lax.ppermute(far, axis, pairs)
     if closed:
         outer = jnp.where((me == 0) | (me == count - 1), 0, outer)
-    return jnp.where(odd, inner, outer), jnp.where(odd, outer, inner), beside
-
-
-def neighbours(block, span_x, span_y, depth, beside=None, meanwhile=None):
+    return jnp.where(odd, inner, outer), jnp.where(odd, outer, inner)
+
+
+def cut_kernel(start, block, part):
+    part[...] = block[:, pl.ds(pl.multiple_of(start[0], 128), part.shape[1])]
+
+
+def cut(block, start, width):
+    return pl.pallas_call(
+        cut_kernel,
+        out_shape=jax.ShapeDtypeStruct((block.shape[0], width), block.dtype),
+        in_specs=[
+            pl.BlockSpec(memory_space=pltpu.SMEM),
+            pl.BlockSpec(memory_space=pltpu.VMEM),
+        ],
+        out_specs=pl.BlockSpec(memory_space=pltpu.VMEM),
+        compiler_params=pltpu.CompilerParams(vmem_limit_bytes=4 * 1024 * 1024),
+        name="cut",
+    )(start.reshape(1), block)
+
+
+def neighbours(block, span_x, span_y, depth, meanwhile=None):
     plane = span_y * depth
-    xlo, xhi, beside = swaps(
-        "slab", block[:, (span_x - 1) * plane :], block[:, :plane], False, beside
-    )
+    top = (span_x - 1) * plane
+    odd = lax.axis_index("slab") % 2 == 1
+    near = jnp.where(odd, block[:, :plane], block[:, top:])
+    far = cut(block, jnp.where(odd, top, 0), plane)
+    xlo, xhi = swaps("slab", near, far, False)
     xlo, xhi, meanwhile = lax.optimization_barrier((xlo, xhi, meanwhile))
 
     def edge(row):
@@ -47,8 +65,12 @@
         parts += [xhi[:, at : at + depth]]
         return jnp.concatenate(parts, axis=1)
 
-    ylo, yhi, _ = swaps("col", edge(span_y - 1), edge(0), True)
-    return (xlo, xhi, ylo, yhi), beside, meanwhile
+    odd = lax.axis_index("col") % 2 == 1
+    upward, downward = edge(span_y - 1), edge(0)
+    ylo, yhi = swaps(
+        "col", jnp.where(odd, downward, upward), jnp.where(odd, upward, downward), True
+    )
+    return (xlo, xhi, ylo, yhi), meanwhile
 
 
 def coefficients_kernel(table, cells, coef):
@@ -457,7 +479,7 @@
         )[0]
 
     last = basis[blocks - 1].reshape(columns, cells)
-    around, partial, (stack, own) = neighbours(last, *spans, inner_image(last), (stack, own))
+    around, (stack, own, partial) = neighbours(last, *spans, (stack, own, inner_image(last)))
     image, cross = call(
         functools.partial(first_image_kernel, spans),
         "first_image",
@@ -478,7 +500,7 @@
         [((fields, fields), bf16)] * 2,
         cross, rest, square, inverse,
     )
-    around, _, _ = neighbours(block, *spans)
+    around, _ = neighbours(block, *spans)
     image, cross = call(
         functools.partial(second_image_kernel, spans),
         "second_image",

time: 76.7 us -> 73.3 us (0.956)
  starting transfers between devices: 32.2 us -> 28.3 us
    ppermute x4, starting transfers between devices: 8.73 us -> 5.46 us  [swaps(): inner = lax.ppermute(near, axis, [(i, i ^ 1) for i in range(count)])]
    ppermute x4, waiting for transfers between devices: 5.46 us -> 4.56 us  [swaps(): inner = lax.ppermute(near, axis, [(i, i ^ 1) for i in range(count)])]
where the time goes in v16:
time: 73.3 us; the launch traced here: 73.1 us
  waiting for transfers between devices  29.3 us (40%)
  starting transfers between devices  28.3 us (39%)
  Pallas kernels  12.1 us (17%)
  local copies, waits for them, and re-layouts  2.13 us (3%)
  between operations  0.97 us (1%)
    ppermute x16, starting transfers between devices, partner(): return lax.ppermute(part, axes, [(i, i ^ mask) for i in range(count)])  20.7 us
    ppermute x16, waiting for transfers between devices, partner(): return lax.ppermute(part, axes, [(i, i ^ mask) for i in range(count)])  19.9 us
    pallas_call x8, Pallas kernels, call(): pl.pallas_call(kernel, out_shape=[jax.ShapeDtypeStruct(shape, dtype) for...  11.3 us
    ppermute x4, starting transfers between devices, swaps(): inner = lax.ppermute(near, axis, [(i, i ^ 1) for i in range(count)])  5.46 us
    ppermute x4, waiting for transfers between devices, swaps(): outer = lax.ppermute(far, axis, pairs)  4.84 us
    ppermute x4, waiting for transfers between devices, swaps(): inner = lax.ppermute(near, axis, [(i, i ^ 1) for i in range(count)])  4.56 us
    ppermute x4, starting transfers between devices, swaps(): outer = lax.ppermute(far, axis, pairs)  2.14 us
  transfers between devices with their start and end apart: 24, of which 16 were waited for; matrix products, arithmetic and copies ran while one was open for 0% of the time, Pallas kernels for 4%

profile of v16, /device:TPU:0, one launch (start us, length us, event | category | flops | bytes accessed | tf_op | source)
XLA Modules:
  0.0 73.1 jit_solution(16116780904009637672)
XLA Ops:
  0.6 0.0 slice-start
  0.7 0.9 %slice-done = bf16[1,64,2,8,128]{4,3,2,1,0:T(8,128)(2,1)S(1)} async-done(((bf16[3,64,2,8,128]{4,3,2,1,0:T(8,128)(2,1)}), bf16[1,64,2,8,128]{4,3,2,1,0:T(8,128)(2,1)S(1)}, s32[]{:S(2)}) %slice-start) | async-done | bytes 262168 | tf_op jit(solution)/shard_map/slice | solution.py:481
  1.6 0.1 reshape_squeeze.3.block.fields
  1.7 3.0 %collective-permute-start = (bf16[64,1024]{1,0:T(8,128)(2,1)S(1)}, bf16[64,1024]{1,0:T(8,128)(2,1)S(1)}, u32[]{:S(2)}, u32[]{:S(2)}) collective-permute-start(bf16[64,1024]{1,0:T(8,128)(2,1)S(1)} %slice_select_fusion), channel_id=1, source_target_pairs={{0,4},{4,0},{8,12},{12,8},{16,20},{20,16},{24,28},{28,24},{1,5},{5... | collective-permute-start | bytes 393224 | tf_op jit(solution)/shard_map/ppermute | solution.py:27
  4.8 0.7 collective-permute-start.1
  5.5 0.0 copy-start
  5.5 0.3 reshape.18.stack
  5.8 0.0 copy-start.1
  5.8 0.3 copy-done
  6.2 0.3 copy-done.1
  6.5 0.8 %coefficients.1.coef = f32[27,16,128]{2,1,0:T(8,128)S(1)} custom-call(f32[8,27]{1,0:T(8,128)S(1)} %copy-done.1, s32[16,128]{1,0:T(8,128)S(1)} %bitcast.7), custom_call_target="tpu_custom_call" | custom-call | tf_op jit(solution)/shard_map/coefficients/pallas_call | solution.py:100
  7.3 0.7 inner_image.2.partial
  7.9 0.6 stack_gram.1
  8.5 0.0 collective-permute-done
  8.5 0.0 collective-permute-done.1
  8.6 0.7 %collective-permute-start.3 = (bf16[64,512]{1,0:T(8,128)(2,1)S(1)}, bf16[64,512]{1,0:T(8,128)(2,1)S(1)}, u32[]{:S(2)}, u32[]{:S(2)}) collective-permute-start(bf16[64,512]{1,0:T(8,128)(2,1)S(1)} %get-tuple-element.85), channel_id=1, source_target_pairs={{1,2},{2,1},{0,3},{3,0},{5,6},{6,5},{4,7},{7,4},{9,10},{10,9},{8,1... | collective-permute-start | bytes 196616 | tf_op jit(solution)/shard_map/ppermute | solution.py:28
  9.4 1.0 %collective-permute-start.2 = (bf16[64,512]{1,0:T(8,128)(2,1)S(1)}, bf16[64,512]{1,0:T(8,128)(2,1)S(1)}, u32[]{:S(2)}, u32[]{:S(2)}) collective-permute-start(bf16[64,512]{1,0:T(8,128)(2,1)S(1)} %get-tuple-element.86), channel_id=1, source_target_pairs={{0,1},{1,0},{2,3},{3,2},{4,5},{5,4},{6,7},{7,6},{8,9},{9,8},{10,11... | collective-permute-start | bytes 196616 | tf_op jit(solution)/shard_map/ppermute | solution.py:27
  10.3 2.7 %collective-permute-done.3 = bf16[64,512]{1,0:T(8,128)(2,1)S(1)} collective-permute-done((bf16[64,512]{1,0:T(8,128)(2,1)S(1)}, bf16[64,512]{1,0:T(8,128)(2,1)S(1)}, u32[]{:S(2)}, u32[]{:S(2)}) %collective-permute-start.3) | collective-permute-done | bytes 65568 | tf_op jit(solution)/shard_map/ppermute | solution.py:28
  13.0 0.0 collective-permute-done.2
  13.0 1.1 %first_image.1 = (bf16[64,2048]{1,0:T(8,128)(2,1)S(1)}, f32[272,128]{1,0:T(8,128)S(1)}) custom-call(f32[27,16,128]{2,1,0:T(8,128)S(1)} %coefficients.1.coef, bf16[192,2048]{1,0:T(8,128)(2,1)S(1)} %reshape.18.stack, f32[3,64,64]{2,1,0:T(8,128)S(1)} %get-tuple-element.37.sides, f32[64,64]{1,0:T(8,128)S(1)} %get-tuple-element.38.pair, ...), custom_call_target="tpu_custom_call" | custom-call | bytes 2408704 | tf_op jit(solution)/shard_map/first_image/pallas_call | solution.py:440
  14.2 0.2 collective-permute-start.4
  14.4 1.1 %collective-permute-done.4 = f32[136,128]{1,0:T(8,128)S(1)} collective-permute-done((f32[136,128]{1,0:T(8,128)S(1)}, f32[136,128]{1,0:T(8,128)S(1)}, u32[]{:S(2)}, u32[]{:S(2)}) %collective-permute-start.4) | collective-permute-done | bytes 69664 | tf_op jit(solution)/shard_map/ppermute | solution.py:409
  15.5 4.9 %collective-permute-start.7 = (f32[136,128]{1,0:T(8,128)S(1)}, f32[136,128]{1,0:T(8,128)S(1)}, u32[]{:S(2)}, u32[]{:S(2)}) collective-permute-start(f32[136,128]{1,0:T(8,128)S(1)} %select_add_fusion), channel_id=1, source_target_pairs={{0,6},{1,7},{2,4},{3,5},{4,2},{5,3},{6,0},{7,1},{8,14},{9,15},{10,... | collective-permute-start | bytes 208904 | tf_op jit(solution)/shard_map/ppermute | solution.py:409
  20.4 0.0 collective-permute-start.6
  20.4 0.4 collective-permute-start.5
  20.8 2.2 %collective-permute-done.7 = f32[136,128]{1,0:T(8,128)S(1)} collective-permute-done((f32[136,128]{1,0:T(8,128)S(1)}, f32[136,128]{1,0:T(8,128)S(1)}, u32[]{:S(2)}, u32[]{:S(2)}) %collective-permute-start.7) | collective-permute-done | bytes 69664 | tf_op jit(solution)/shard_map/ppermute | solution.py:409
  23.0 1.9 %collective-permute-done.6 = f32[136,128]{1,0:T(8,128)S(1)} collective-permute-done((f32[136,128]{1,0:T(8,128)S(1)}, f32[136,128]{1,0:T(8,128)S(1)}, u32[]{:S(2)}, u32[]{:S(2)}) %collective-permute-start.6) | collective-permute-done | bytes 69664 | tf_op jit(solution)/shard_map/ppermute | solution.py:409
  24.8 0.0 collective-permute-done.5
  24.9 4.9 %collective-permute-start.10 = (f32[136,128]{1,0:T(8,128)S(1)}, f32[136,128]{1,0:T(8,128)S(1)}, u32[]{:S(2)}, u32[]{:S(2)}) collective-permute-start(f32[136,128]{1,0:T(8,128)S(1)} %add_add_fusion.1), channel_id=1, source_target_pairs={{0,24},{1,25},{2,26},{3,27},{4,28},{5,29},{6,30},{7,31},{8,16},{9,... | collective-permute-start | bytes 208904 | tf_op jit(solution)/shard_map/ppermute | solution.py:409
  29.7 0.0 collective-permute-start.9
  29.7 0.4 collective-permute-start.8
  30.1 2.3 %collective-permute-done.10 = f32[136,128]{1,0:T(8,128)S(1)} collective-permute-done((f32[136,128]{1,0:T(8,128)S(1)}, f32[136,128]{1,0:T(8,128)S(1)}, u32[]{:S(2)}, u32[]{:S(2)}) %collective-permute-start.10) | collective-permute-done | bytes 69664 | tf_op jit(solution)/shard_map/ppermute | solution.py:409
  32.4 3.3 %collective-permute-done.9 = f32[136,128]{1,0:T(8,128)S(1)} collective-permute-done((f32[136,128]{1,0:T(8,128)S(1)}, f32[136,128]{1,0:T(8,128)S(1)}, u32[]{:S(2)}, u32[]{:S(2)}) %collective-permute-start.9) | collective-permute-done | bytes 69664 | tf_op jit(solution)/shard_map/ppermute | solution.py:409
  35.7 0.0 collective-permute-done.8
  35.7 0.2 collective-permute-start.11
  35.9 1.1 %collective-permute-done.11 = f32[136,128]{1,0:T(8,128)S(1)} collective-permute-done((f32[136,128]{1,0:T(8,128)S(1)}, f32[136,128]{1,0:T(8,128)S(1)}, u32[]{:S(2)}, u32[]{:S(2)}) %collective-permute-start.11) | collective-permute-done | bytes 69664 | tf_op jit(solution)/shard_map/ppermute | solution.py:409
  37.1 3.1 %first_solve.1 = (bf16[64,2048]{1,0:T(8,128)(2,1)S(1)}, f32[64,192]{1,0:T(8,128)S(1)}, f32[64,64]{1,0:T(8,128)S(1)}, f32[64,192]{1,0:T(8,128)S(1)}, f32[64,64]{1,0:T(8,128)S(1)}, /*index=5*/bf16[64,64]{1,0:T(8,128)(2,1)S(1)}) custom-call(f32[272,128]{1,0:T(8,128)S(1)} %pad_maximum_fusion.cross, bf16[192,2048]{1,0:T(8,128)(2,1)S(1)} %reshape.18.stack, ...), custom_call_target="tpu_custom_call" | custom-call | bytes 1589248 | tf_op jit(solution)/shard_map/first_solve/pallas_call | solution.py:440
  40.3 0.4 collective-permute-start.12
  40.7 0.7 collective-permute-start.13
  41.4 4.6 %collective-permute-done.12 = bf16[64,1024]{1,0:T(8,128)(2,1)S(1)} collective-permute-done((bf16[64,1024]{1,0:T(8,128)(2,1)S(1)}, bf16[64,1024]{1,0:T(8,128)(2,1)S(1)}, u32[]{:S(2)}, u32[]{:S(2)}) %collective-permute-start.12) | collective-permute-done | bytes 131104 | tf_op jit(solution)/shard_map/ppermute | solution.py:27
  45.9 0.0 collective-permute-done.13
  46.0 0.1 collective-permute-start.15
  46.1 1.1 %collective-permute-start.14 = (bf16[64,512]{1,0:T(8,128)(2,1)S(1)}, bf16[64,512]{1,0:T(8,128)(2,1)S(1)}, u32[]{:S(2)}, u32[]{:S(2)}) collective-permute-start(bf16[64,512]{1,0:T(8,128)(2,1)S(1)} %get-tuple-element.78), channel_id=1, source_target_pairs={{0,1},{1,0},{2,3},{3,2},{4,5},{5,4},{6,7},{7,6},{8,9},{9,8},{10,11... | collective-permute-start | bytes 196616 | tf_op jit(solution)/shard_map/ppermute | solution.py:27
  47.2 0.7 inner_image.3.partial
  47.9 2.2 %collective-permute-done.15 = bf16[64,512]{1,0:T(8,128)(2,1)S(1)} collective-permute-done((bf16[64,512]{1,0:T(8,128)(2,1)S(1)}, bf16[64,512]{1,0:T(8,128)(2,1)S(1)}, u32[]{:S(2)}, u32[]{:S(2)}) %collective-permute-start.15) | collective-permute-done | bytes 65568 | tf_op jit(solution)/shard_map/ppermute | solution.py:28
  50.1 0.0 collective-permute-done.14
  50.1 1.1 %second_image.1 = (bf16[64,2048]{1,0:T(8,128)(2,1)S(1)}, f32[64,256]{1,0:T(8,128)S(1)}) custom-call(f32[27,16,128]{2,1,0:T(8,128)S(1)} %coefficients.1.coef, bf16[192,2048]{1,0:T(8,128)(2,1)S(1)} %reshape.18.stack, bf16[64,2048]{1,0:T(8,128)(2,1)S(1)} %get-tuple-element.46.fields.block.last, f32[64,2048]{1,0:T(8,128)S(1)} %inner_image.3.partial, ...), custom_call_target="tpu_custom_call" | custom-call | bytes 2514944 | tf_op jit(solution)/shard_map/second_image/pallas_call | solution.py:440
  51.2 0.1 collective-permute-start.16
  51.3 1.2 %collective-permute-done.16 = f32[32,256]{1,0:T(8,128)S(1)} collective-permute-done((f32[32,256]{1,0:T(8,128)S(1)}, f32[32,256]{1,0:T(8,128)S(1)}, u32[]{:S(2)}, u32[]{:S(2)}) %collective-permute-start.16) | collective-permute-done | bytes 32800 | tf_op jit(solution)/shard_map/ppermute | solution.py:409
  52.5 5.0 %collective-permute-start.19 = (f32[32,256]{1,0:T(8,128)S(1)}, f32[32,256]{1,0:T(8,128)S(1)}, u32[]{:S(2)}, u32[]{:S(2)}) collective-permute-start(f32[32,256]{1,0:T(8,128)S(1)} %select_add_fusion.1), channel_id=1, source_target_pairs={{0,6},{1,7},{2,4},{3,5},{4,2},{5,3},{6,0},{7,1},{8,14},{9,15},{10,... | collective-permute-start | bytes 98312 | tf_op jit(solution)/shard_map/ppermute | solution.py:409
  57.5 0.5 collective-permute-start.17
  58.0 1.4 %collective-permute-done.19 = f32[32,256]{1,0:T(8,128)S(1)} collective-permute-done((f32[32,256]{1,0:T(8,128)S(1)}, f32[32,256]{1,0:T(8,128)S(1)}, u32[]{:S(2)}, u32[]{:S(2)}) %collective-permute-start.19) | collective-permute-done | bytes 32800 | tf_op jit(solution)/shard_map/ppermute | solution.py:409
  59.3 1.7 %collective-permute-done.18 = f32[32,256]{1,0:T(8,128)S(1)} collective-permute-done((f32[32,256]{1,0:T(8,128)S(1)}, f32[32,256]{1,0:T(8,128)S(1)}, u32[]{:S(2)}, u32[]{:S(2)}) %collective-permute-start.18) | collective-permute-done | bytes 32800 | tf_op jit(solution)/shard_map/ppermute | solution.py:409
  61.1 0.0 collective-permute-done.17
  61.1 2.2 %collective-permute-start.22 = (f32[32,256]{1,0:T(8,128)S(1)}, f32[32,256]{1,0:T(8,128)S(1)}, u32[]{:S(2)}, u32[]{:S(2)}) collective-permute-start(f32[32,256]{1,0:T(8,128)S(1)} %add_add_fusion.3), channel_id=1, source_target_pairs={{0,24},{1,25},{2,26},{3,27},{4,28},{5,29},{6,30},{7,31},{8,16},{9,... | collective-permute-start | bytes 98312 | tf_op jit(solution)/shard_map/ppermute | solution.py:409
  63.3 0.0 collective-permute-start.21
  63.3 2.0 %collective-permute-start.20 = (f32[32,256]{1,0:T(8,128)S(1)}, f32[32,256]{1,0:T(8,128)S(1)}, u32[]{:S(2)}, u32[]{:S(2)}) collective-permute-start(f32[32,256]{1,0:T(8,128)S(1)} %add_add_fusion.3), channel_id=1, source_target_pairs={{0,9},{1,8},{2,11},{3,10},{4,13},{5,12},{6,15},{7,14},{8,1},{9,0},... | collective-permute-start | bytes 98312 | tf_op jit(solution)/shard_map/ppermute | solution.py:409
  65.3 1.7 %collective-permute-done.22 = f32[32,256]{1,0:T(8,128)S(1)} collective-permute-done((f32[32,256]{1,0:T(8,128)S(1)}, f32[32,256]{1,0:T(8,128)S(1)}, u32[]{:S(2)}, u32[]{:S(2)}) %collective-permute-start.22) | collective-permute-done | bytes 32800 | tf_op jit(solution)/shard_map/ppermute | solution.py:409
  67.0 0.6 collective-permute-done.21
  67.6 0.5 collective-permute-done.20
  68.2 0.2 collective-permute-start.23
  68.3 0.4 next_gram.1
  68.8 0.7 collective-permute-done.23
  69.5 3.6 %second_solve.1 = (bf16[64,2,8,128]{3,2,1,0:T(8,128)(2,1)}, f32[2,64,192]{2,1,0:T(8,128)}, f32[2,64,64]{2,1,0:T(8,128)}) custom-call(f32[64,256]{1,0:T(8,128)S(1)} %pad_maximum_fusion.5.cross, bf16[192,192]{1,0:T(8,128)(2,1)S(1)} %get-tuple-element.53.own_high, bf16[192,192]{1,0:T(8,128)(2,1)S(1)} %get-tuple-element.54.own_low, ...), custom_call_target="tpu_custom_call" | custom-call | bytes 1982464 | tf_op jit(solution)/shard_map/second_solve/pallas_call | solution.py:440
  (30 shorter events, 0.4 us)
Async XLA Ops:
  0.6 1.0 %slice-start = ((bf16[3,64,2,8,128]{4,3,2,1,0:T(8,128)(2,1)}), bf16[1,64,2,8,128]{4,3,2,1,0:T(8,128)(2,1)S(1)}, s32[]{:S(2)}) async-start(bf16[3,64,2,8,128]{4,3,2,1,0:T(8,128)(2,1)} %param.3), calls=%async_computation | async-start | bytes 524288 | tf_op jit(solution)/shard_map/slice | solution.py:481
  1.6 3.8 %copy-start.2 = (bf16[3,64,2,8,128]{4,3,2,1,0:T(8,128)(2,1)S(1)}, bf16[3,64,2,8,128]{4,3,2,1,0:T(8,128)(2,1)}, u32[]{:S(2)}) copy-start(bf16[3,64,2,8,128]{4,3,2,1,0:T(8,128)(2,1)} %param.3) | copy-start | bytes 2359300
  1.7 6.8 %collective-permute-start = (bf16[64,1024]{1,0:T(8,128)(2,1)S(1)}, bf16[64,1024]{1,0:T(8,128)(2,1)S(1)}, u32[]{:S(2)}, u32[]{:S(2)}) collective-permute-start(bf16[64,1024]{1,0:T(8,128)(2,1)S(1)} %slice_select_fusion), channel_id=1, source_target_pairs={{0,4},{4,0},{8,12},{12,8},{16,20},{20,16},{24,28},{28,24},{1,5},{5... | collective-permute-start | bytes 393224 | tf_op jit(solution)/shard_map/ppermute | solution.py:27
  4.8 3.8 %collective-permute-start.1 = (bf16[64,1024]{1,0:T(8,128)(2,1)S(1)}, bf16[64,1024]{1,0:T(8,128)(2,1)S(1)}, u32[]{:S(2)}, u32[]{:S(2)}) collective-permute-start(bf16[64,1024]{1,0:T(8,128)(2,1)S(1)} %cut.2), channel_id=1, source_target_pairs={{4,8},{8,4},{12,16},{16,12},{20,24},{24,20},{5,9},{9,5},{13,17},{1... | collective-permute-start | bytes 393224 | tf_op jit(solution)/shard_map/ppermute | solution.py:28
  5.5 0.7 copy-start
  5.8 0.7 copy-start.1
  8.6 4.4 %collective-permute-start.3 = (bf16[64,512]{1,0:T(8,128)(2,1)S(1)}, bf16[64,512]{1,0:T(8,128)(2,1)S(1)}, u32[]{:S(2)}, u32[]{:S(2)}) collective-permute-start(bf16[64,512]{1,0:T(8,128)(2,1)S(1)} %get-tuple-element.85), channel_id=1, source_target_pairs={{1,2},{2,1},{0,3},{3,0},{5,6},{6,5},{4,7},{7,4},{9,10},{10,9},{8,1... | collective-permute-start | bytes 196616 | tf_op jit(solution)/shard_map/ppermute | solution.py:28
  9.4 3.6 %collective-permute-start.2 = (bf16[64,512]{1,0:T(8,128)(2,1)S(1)}, bf16[64,512]{1,0:T(8,128)(2,1)S(1)}, u32[]{:S(2)}, u32[]{:S(2)}) collective-permute-start(bf16[64,512]{1,0:T(8,128)(2,1)S(1)} %get-tuple-element.86), channel_id=1, source_target_pairs={{0,1},{1,0},{2,3},{3,2},{4,5},{5,4},{6,7},{7,6},{8,9},{9,8},{10,11... | collective-permute-start | bytes 196616 | tf_op jit(solution)/shard_map/ppermute | solution.py:27
  14.2 1.3 %collective-permute-start.4 = (f32[136,128]{1,0:T(8,128)S(1)}, f32[136,128]{1,0:T(8,128)S(1)}, u32[]{:S(2)}, u32[]{:S(2)}) collective-permute-start(f32[136,128]{1,0:T(8,128)S(1)} %slice_select_fusion.2), channel_id=1, source_target_pairs={{0,1},{1,0},{2,3},{3,2},{4,5},{5,4},{6,7},{7,6},{8,9},{9,8},{10,11... | collective-permute-start | bytes 208904 | tf_op jit(solution)/shard_map/ppermute | solution.py:409
  15.5 7.4 %collective-permute-start.7 = (f32[136,128]{1,0:T(8,128)S(1)}, f32[136,128]{1,0:T(8,128)S(1)}, u32[]{:S(2)}, u32[]{:S(2)}) collective-permute-start(f32[136,128]{1,0:T(8,128)S(1)} %select_add_fusion), channel_id=1, source_target_pairs={{0,6},{1,7},{2,4},{3,5},{4,2},{5,3},{6,0},{7,1},{8,14},{9,15},{10,... | collective-permute-start | bytes 208904 | tf_op jit(solution)/shard_map/ppermute | solution.py:409
  20.4 4.4 %collective-permute-start.6 = (f32[136,128]{1,0:T(8,128)S(1)}, f32[136,128]{1,0:T(8,128)S(1)}, u32[]{:S(2)}, u32[]{:S(2)}) collective-permute-start(f32[136,128]{1,0:T(8,128)S(1)} %select_add_fusion), channel_id=1, source_target_pairs={{0,5},{1,4},{2,7},{3,6},{4,1},{5,0},{6,3},{7,2},{8,13},{9,12},{10,... | collective-permute-start | bytes 208904 | tf_op jit(solution)/shard_map/ppermute | solution.py:409
  20.4 4.4 %collective-permute-start.5 = (f32[136,128]{1,0:T(8,128)S(1)}, f32[136,128]{1,0:T(8,128)S(1)}, u32[]{:S(2)}, u32[]{:S(2)}) collective-permute-start(f32[136,128]{1,0:T(8,128)S(1)} %select_add_fusion), channel_id=1, source_target_pairs={{0,3},{1,2},{2,1},{3,0},{4,7},{5,6},{6,5},{7,4},{8,11},{9,10},{10,... | collective-permute-start | bytes 208904 | tf_op jit(solution)/shard_map/ppermute | solution.py:409
  24.9 7.5 %collective-permute-start.10 = (f32[136,128]{1,0:T(8,128)S(1)}, f32[136,128]{1,0:T(8,128)S(1)}, u32[]{:S(2)}, u32[]{:S(2)}) collective-permute-start(f32[136,128]{1,0:T(8,128)S(1)} %add_add_fusion.1), channel_id=1, source_target_pairs={{0,24},{1,25},{2,26},{3,27},{4,28},{5,29},{6,30},{7,31},{8,16},{9,... | collective-permute-start | bytes 208904 | tf_op jit(solution)/shard_map/ppermute | solution.py:409
  29.7 6.0 %collective-permute-start.9 = (f32[136,128]{1,0:T(8,128)S(1)}, f32[136,128]{1,0:T(8,128)S(1)}, u32[]{:S(2)}, u32[]{:S(2)}) collective-permute-start(f32[136,128]{1,0:T(8,128)S(1)} %add_add_fusion.1), channel_id=1, source_target_pairs={{0,17},{1,16},{2,19},{3,18},{4,21},{5,20},{6,23},{7,22},{8,25},{9,... | collective-permute-start | bytes 208904 | tf_op jit(solution)/shard_map/ppermute | solution.py:409
  29.7 6.0 %collective-permute-start.8 = (f32[136,128]{1,0:T(8,128)S(1)}, f32[136,128]{1,0:T(8,128)S(1)}, u32[]{:S(2)}, u32[]{:S(2)}) collective-permute-start(f32[136,128]{1,0:T(8,128)S(1)} %add_add_fusion.1), channel_id=1, source_target_pairs={{0,9},{1,8},{2,11},{3,10},{4,13},{5,12},{6,15},{7,14},{8,1},{9,0},... | collective-permute-start | bytes 208904 | tf_op jit(solution)/shard_map/ppermute | solution.py:409
  35.7 1.3 %collective-permute-start.11 = (f32[136,128]{1,0:T(8,128)S(1)}, f32[136,128]{1,0:T(8,128)S(1)}, u32[]{:S(2)}, u32[]{:S(2)}) collective-permute-start(f32[136,128]{1,0:T(8,128)S(1)} %add_add_fusion), channel_id=1, source_target_pairs={{0,1},{1,0},{2,3},{3,2},{4,5},{5,4},{6,7},{7,6},{8,9},{9,8},{10,11... | collective-permute-start | bytes 208904 | tf_op jit(solution)/shard_map/ppermute | solution.py:409
  40.3 5.6 %collective-permute-start.12 = (bf16[64,1024]{1,0:T(8,128)(2,1)S(1)}, bf16[64,1024]{1,0:T(8,128)(2,1)S(1)}, u32[]{:S(2)}, u32[]{:S(2)}) collective-permute-start(bf16[64,1024]{1,0:T(8,128)(2,1)S(1)} %slice_select_fusion.1), channel_id=1, source_target_pairs={{0,4},{4,0},{8,12},{12,8},{16,20},{20,16},{24,28},{28,24},{1,5},{5... | collective-permute-start | bytes 393224 | tf_op jit(solution)/shard_map/ppermute | solution.py:27
  40.7 5.2 %collective-permute-start.13 = (bf16[64,1024]{1,0:T(8,128)(2,1)S(1)}, bf16[64,1024]{1,0:T(8,128)(2,1)S(1)}, u32[]{:S(2)}, u32[]{:S(2)}) collective-permute-start(bf16[64,1024]{1,0:T(8,128)(2,1)S(1)} %cut.3), channel_id=1, source_target_pairs={{4,8},{8,4},{12,16},{16,12},{20,24},{24,20},{5,9},{9,5},{13,17},{1... | collective-permute-start | bytes 393224 | tf_op jit(solution)/shard_map/ppermute | solution.py:28
  46.0 4.0 %collective-permute-start.15 = (bf16[64,512]{1,0:T(8,128)(2,1)S(1)}, bf16[64,512]{1,0:T(8,128)(2,1)S(1)}, u32[]{:S(2)}, u32[]{:S(2)}) collective-permute-start(bf16[64,512]{1,0:T(8,128)(2,1)S(1)} %get-tuple-element.77), channel_id=1, source_target_pairs={{1,2},{2,1},{0,3},{3,0},{5,6},{6,5},{4,7},{7,4},{9,10},{10,9},{8,1... | collective-permute-start | bytes 196616 | tf_op jit(solution)/shard_map/ppermute | solution.py:28
  46.1 4.0 %collective-permute-start.14 = (bf16[64,512]{1,0:T(8,128)(2,1)S(1)}, bf16[64,512]{1,0:T(8,128)(2,1)S(1)}, u32[]{:S(2)}, u32[]{:S(2)}) collective-permute-start(bf16[64,512]{1,0:T(8,128)(2,1)S(1)} %get-tuple-element.78), channel_id=1, source_target_pairs={{0,1},{1,0},{2,3},{3,2},{4,5},{5,4},{6,7},{7,6},{8,9},{9,8},{10,11... | collective-permute-start | bytes 196616 | tf_op jit(solution)/shard_map/ppermute | solution.py:27
  51.2 1.3 %collective-permute-start.16 = (f32[32,256]{1,0:T(8,128)S(1)}, f32[32,256]{1,0:T(8,128)S(1)}, u32[]{:S(2)}, u32[]{:S(2)}) collective-permute-start(f32[32,256]{1,0:T(8,128)S(1)} %slice_select_fusion.3), channel_id=1, source_target_pairs={{0,1},{1,0},{2,3},{3,2},{4,5},{5,4},{6,7},{7,6},{8,9},{9,8},{10,11... | collective-permute-start | bytes 98312 | tf_op jit(solution)/shard_map/ppermute | solution.py:409
  52.5 6.9 %collective-permute-start.19 = (f32[32,256]{1,0:T(8,128)S(1)}, f32[32,256]{1,0:T(8,128)S(1)}, u32[]{:S(2)}, u32[]{:S(2)}) collective-permute-start(f32[32,256]{1,0:T(8,128)S(1)} %select_add_fusion.1), channel_id=1, source_target_pairs={{0,6},{1,7},{2,4},{3,5},{4,2},{5,3},{6,0},{7,1},{8,14},{9,15},{10,... | collective-permute-start | bytes 98312 | tf_op jit(solution)/shard_map/ppermute | solution.py:409
  57.4 3.6 %collective-permute-start.18 = (f32[32,256]{1,0:T(8,128)S(1)}, f32[32,256]{1,0:T(8,128)S(1)}, u32[]{:S(2)}, u32[]{:S(2)}) collective-permute-start(f32[32,256]{1,0:T(8,128)S(1)} %select_add_fusion.1), channel_id=1, source_target_pairs={{0,5},{1,4},{2,7},{3,6},{4,1},{5,0},{6,3},{7,2},{8,13},{9,12},{10,... | collective-permute-start | bytes 98312 | tf_op jit(solution)/shard_map/ppermute | solution.py:409
  57.5 3.6 %collective-permute-start.17 = (f32[32,256]{1,0:T(8,128)S(1)}, f32[32,256]{1,0:T(8,128)S(1)}, u32[]{:S(2)}, u32[]{:S(2)}) collective-permute-start(f32[32,256]{1,0:T(8,128)S(1)} %select_add_fusion.1), channel_id=1, source_target_pairs={{0,3},{1,2},{2,1},{3,0},{4,7},{5,6},{6,5},{7,4},{8,11},{9,10},{10,... | collective-permute-start | bytes 98312 | tf_op jit(solution)/shard_map/ppermute | solution.py:409
  61.1 5.9 %collective-permute-start.22 = (f32[32,256]{1,0:T(8,128)S(1)}, f32[32,256]{1,0:T(8,128)S(1)}, u32[]{:S(2)}, u32[]{:S(2)}) collective-permute-start(f32[32,256]{1,0:T(8,128)S(1)} %add_add_fusion.3), channel_id=1, source_target_pairs={{0,24},{1,25},{2,26},{3,27},{4,28},{5,29},{6,30},{7,31},{8,16},{9,... | collective-permute-start | bytes 98312 | tf_op jit(solution)/shard_map/ppermute | solution.py:409
  63.3 4.3 %collective-permute-start.21 = (f32[32,256]{1,0:T(8,128)S(1)}, f32[32,256]{1,0:T(8,128)S(1)}, u32[]{:S(2)}, u32[]{:S(2)}) collective-permute-start(f32[32,256]{1,0:T(8,128)S(1)} %add_add_fusion.3), channel_id=1, source_target_pairs={{0,17},{1,16},{2,19},{3,18},{4,21},{5,20},{6,23},{7,22},{8,25},{9,... | collective-permute-start | bytes 98312 | tf_op jit(solution)/shard_map/ppermute | solution.py:409
  63.3 4.9 %collective-permute-start.20 = (f32[32,256]{1,0:T(8,128)S(1)}, f32[32,256]{1,0:T(8,128)S(1)}, u32[]{:S(2)}, u32[]{:S(2)}) collective-permute-start(f32[32,256]{1,0:T(8,128)S(1)} %add_add_fusion.3), channel_id=1, source_target_pairs={{0,9},{1,8},{2,11},{3,10},{4,13},{5,12},{6,15},{7,14},{8,1},{9,0},... | collective-permute-start | bytes 98312 | tf_op jit(solution)/shard_map/ppermute | solution.py:409
  68.2 1.3 %collective-permute-start.23 = (f32[32,256]{1,0:T(8,128)S(1)}, f32[32,256]{1,0:T(8,128)S(1)}, u32[]{:S(2)}, u32[]{:S(2)}) collective-permute-start(f32[32,256]{1,0:T(8,128)S(1)} %add_add_fusion.2), channel_id=1, source_target_pairs={{0,1},{1,0},{2,3},{3,2},{4,5},{5,4},{6,7},{7,6},{8,9},{9,8},{10,11... | collective-permute-start | bytes 98312 | tf_op jit(solution)/shard_map/ppermute | solution.py:409

commit v17 on v16

--- a/solution.py
+++ b/solution.py
@@ -213,7 +213,7 @@
     columns = image.shape[0]
     complete(image, partial, coef, spans, xlo, xhi, ylo, yhi)
     w = image[...]
-    first = dot(w, stack[...], NT)
+    first = dot(stack[...], w, NT).T
     corner, own_diagonal = two_in_one(last[...], dot(w, w, NT))
     rows = [
         first[:, : 2 * columns],
@@ -245,8 +245,8 @@
     fields = stack.shape[0]
     complete(image, partial, coef, spans, xlo, xhi, ylo, yhi)
     w = image[...]
-    cross[:, : fields - columns] = dot(w, stack[columns:], NT)
-    cross[:, fields - columns : fields] = dot(w, block[...], NT)
+    cross[:, : fields - columns] = dot(stack[columns:], w, NT).T
+    cross[:, fields - columns : fields] = dot(block[...], w, NT).T
     cross[:, fields:] = dot(w, w, NT)
 
 
@@ -425,7 +425,7 @@
     while bit < count:
         if 2 * bit < count:
             one, two, both = (partner(part, mask) for mask in (bit + 1, 2 * bit + 1, 3 * bit))
-            part = (part + one) + (two + both)
+            part = (part + both) + (two + one)
             bit *= 4
         else:
             part = part + partner(part, bit + 1)

time: 73.3 us -> 76.1 us (1.038)
  waiting for transfers between devices: 29.3 us -> 31.7 us
    ppermute x16, waiting for transfers between devices: 19.9 us -> 22.6 us  [partner(): return lax.ppermute(part, axes, [(i, i ^ mask) for i in range(count)])]
  transfers between devices with their start and end apart: 24 -> 24, of which waited for: 16 -> 15; matrix products, arithmetic and copies ran while one was open for 0% -> 0% of each run, Pallas kernels for 4% -> 4%
where the time goes in v17:
time: 76.1 us; the launch traced here: 75.9 us
  waiting for transfers between devices  31.7 us (42%)
  starting transfers between devices  28.7 us (38%)
  Pallas kernels  12.1 us (16%)
  local copies, waits for them, and re-layouts  2.13 us (3%)
  between operations  0.98 us (1%)
    ppermute x16, waiting for transfers between devices, partner(): return lax.ppermute(part, axes, [(i, i ^ mask) for i in range(count)])  22.6 us
    ppermute x16, starting transfers between devices, partner(): return lax.ppermute(part, axes, [(i, i ^ mask) for i in range(count)])  20.8 us
    pallas_call x8, Pallas kernels, call(): pl.pallas_call(kernel, out_shape=[jax.ShapeDtypeStruct(shape, dtype) for...  11.3 us
    ppermute x4, starting transfers between devices, swaps(): inner = lax.ppermute(near, axis, [(i, i ^ 1) for i in range(count)])  5.68 us
    ppermute x4, waiting for transfers between devices, swaps(): outer = lax.ppermute(far, axis, pairs)  4.9 us
    ppermute x4, waiting for transfers between devices, swaps(): inner = lax.ppermute(near, axis, [(i, i ^ 1) for i in range(count)])  4.22 us
    ppermute x4, starting transfers between devices, swaps(): outer = lax.ppermute(far, axis, pairs)  2.14 us
  transfers between devices with their start and end apart: 24, of which 15 were waited for; matrix products, arithmetic and copies ran while one was open for 0% of the time, Pallas kernels for 4%

profile of v17, /device:TPU:0, one launch (start us, length us, event | category | flops | bytes accessed | tf_op | source)
XLA Modules:
  0.0 75.9 jit_solution(7378131524264468747)
XLA Ops:
  0.6 0.0 slice-start
  0.7 0.9 %slice-done = bf16[1,64,2,8,128]{4,3,2,1,0:T(8,128)(2,1)S(1)} async-done(((bf16[3,64,2,8,128]{4,3,2,1,0:T(8,128)(2,1)}), bf16[1,64,2,8,128]{4,3,2,1,0:T(8,128)(2,1)S(1)}, s32[]{:S(2)}) %slice-start) | async-done | bytes 262168 | tf_op jit(solution)/shard_map/slice | solution.py:481
  1.6 0.1 reshape_squeeze.3.block.fields
  1.7 3.0 %collective-permute-start = (bf16[64,1024]{1,0:T(8,128)(2,1)S(1)}, bf16[64,1024]{1,0:T(8,128)(2,1)S(1)}, u32[]{:S(2)}, u32[]{:S(2)}) collective-permute-start(bf16[64,1024]{1,0:T(8,128)(2,1)S(1)} %slice_select_fusion), channel_id=1, source_target_pairs={{0,4},{4,0},{8,12},{12,8},{16,20},{20,16},{24,28},{28,24},{1,5},{5... | collective-permute-start | bytes 393224 | tf_op jit(solution)/shard_map/ppermute | solution.py:27
  4.8 0.7 collective-permute-start.1
  5.5 0.0 copy-start
  5.5 0.3 reshape.18.stack
  5.8 0.0 copy-start.1
  5.8 0.3 copy-done
  6.2 0.3 copy-done.1
  6.5 0.8 coefficients.1.coef
  7.3 0.7 inner_image.2.partial
  7.9 0.6 stack_gram.1
  8.5 0.0 collective-permute-done
  8.5 0.0 collective-permute-done.1
  8.6 0.7 collective-permute-start.3
  9.4 1.0 %collective-permute-start.2 = (bf16[64,512]{1,0:T(8,128)(2,1)S(1)}, bf16[64,512]{1,0:T(8,128)(2,1)S(1)}, u32[]{:S(2)}, u32[]{:S(2)}) collective-permute-start(bf16[64,512]{1,0:T(8,128)(2,1)S(1)} %get-tuple-element.86), channel_id=1, source_target_pairs={{0,1},{1,0},{2,3},{3,2},{4,5},{5,4},{6,7},{7,6},{8,9},{9,8},{10,11... | collective-permute-start | bytes 196616 | tf_op jit(solution)/shard_map/ppermute | solution.py:27
  10.3 2.7 %collective-permute-done.3 = bf16[64,512]{1,0:T(8,128)(2,1)S(1)} collective-permute-done((bf16[64,512]{1,0:T(8,128)(2,1)S(1)}, bf16[64,512]{1,0:T(8,128)(2,1)S(1)}, u32[]{:S(2)}, u32[]{:S(2)}) %collective-permute-start.3) | collective-permute-done | bytes 65568 | tf_op jit(solution)/shard_map/ppermute | solution.py:28
  13.0 0.0 collective-permute-done.2
  13.0 1.1 %first_image.1 = (bf16[64,2048]{1,0:T(8,128)(2,1)S(1)}, f32[272,128]{1,0:T(8,128)S(1)}) custom-call(f32[27,16,128]{2,1,0:T(8,128)S(1)} %coefficients.1.coef, bf16[192,2048]{1,0:T(8,128)(2,1)S(1)} %reshape.18.stack, f32[3,64,64]{2,1,0:T(8,128)S(1)} %get-tuple-element.37.sides, f32[64,64]{1,0:T(8,128)S(1)} %get-tuple-element.38.pair, ...), custom_call_target="tpu_custom_call" | custom-call | bytes 2408704 | tf_op jit(solution)/shard_map/first_image/pallas_call | solution.py:440
  14.2 0.2 collective-permute-start.4
  14.4 1.1 %collective-permute-done.4 = f32[136,128]{1,0:T(8,128)S(1)} collective-permute-done((f32[136,128]{1,0:T(8,128)S(1)}, f32[136,128]{1,0:T(8,128)S(1)}, u32[]{:S(2)}, u32[]{:S(2)}) %collective-permute-start.4) | collective-permute-done | bytes 69664 | tf_op jit(solution)/shard_map/ppermute | solution.py:409
  15.5 1.2 %collective-permute-start.7 = (f32[136,128]{1,0:T(8,128)S(1)}, f32[136,128]{1,0:T(8,128)S(1)}, u32[]{:S(2)}, u32[]{:S(2)}) collective-permute-start(f32[136,128]{1,0:T(8,128)S(1)} %select_add_fusion), channel_id=1, source_target_pairs={{0,3},{1,2},{2,1},{3,0},{4,7},{5,6},{6,5},{7,4},{8,11},{9,10},{10,... | collective-permute-start | bytes 208904 | tf_op jit(solution)/shard_map/ppermute | solution.py:409
  16.7 4.0 %collective-permute-start.6 = (f32[136,128]{1,0:T(8,128)S(1)}, f32[136,128]{1,0:T(8,128)S(1)}, u32[]{:S(2)}, u32[]{:S(2)}) collective-permute-start(f32[136,128]{1,0:T(8,128)S(1)} %select_add_fusion), channel_id=1, source_target_pairs={{0,5},{1,4},{2,7},{3,6},{4,1},{5,0},{6,3},{7,2},{8,13},{9,12},{10,... | collective-permute-start | bytes 208904 | tf_op jit(solution)/shard_map/ppermute | solution.py:409
  20.7 0.3 collective-permute-start.5
  21.1 0.0 collective-permute-done.7
  21.1 2.2 %collective-permute-done.6 = f32[136,128]{1,0:T(8,128)S(1)} collective-permute-done((f32[136,128]{1,0:T(8,128)S(1)}, f32[136,128]{1,0:T(8,128)S(1)}, u32[]{:S(2)}, u32[]{:S(2)}) %collective-permute-start.6) | collective-permute-done | bytes 69664 | tf_op jit(solution)/shard_map/ppermute | solution.py:409
  23.2 2.7 %collective-permute-done.5 = f32[136,128]{1,0:T(8,128)S(1)} collective-permute-done((f32[136,128]{1,0:T(8,128)S(1)}, f32[136,128]{1,0:T(8,128)S(1)}, u32[]{:S(2)}, u32[]{:S(2)}) %collective-permute-start.5) | collective-permute-done | bytes 69664 | tf_op jit(solution)/shard_map/ppermute | solution.py:409
  26.0 1.7 %collective-permute-start.10 = (f32[136,128]{1,0:T(8,128)S(1)}, f32[136,128]{1,0:T(8,128)S(1)}, u32[]{:S(2)}, u32[]{:S(2)}) collective-permute-start(f32[136,128]{1,0:T(8,128)S(1)} %add_add_fusion.1), channel_id=1, source_target_pairs={{0,9},{1,8},{2,11},{3,10},{4,13},{5,12},{6,15},{7,14},{8,1},{9,0},... | collective-permute-start | bytes 208904 | tf_op jit(solution)/shard_map/ppermute | solution.py:409
  27.7 3.1 %collective-permute-start.9 = (f32[136,128]{1,0:T(8,128)S(1)}, f32[136,128]{1,0:T(8,128)S(1)}, u32[]{:S(2)}, u32[]{:S(2)}) collective-permute-start(f32[136,128]{1,0:T(8,128)S(1)} %add_add_fusion.1), channel_id=1, source_target_pairs={{0,17},{1,16},{2,19},{3,18},{4,21},{5,20},{6,23},{7,22},{8,25},{9,... | collective-permute-start | bytes 208904 | tf_op jit(solution)/shard_map/ppermute | solution.py:409
  30.8 0.0 collective-permute-start.8
  30.8 0.0 collective-permute-done.10
  30.8 2.3 %collective-permute-done.9 = f32[136,128]{1,0:T(8,128)S(1)} collective-permute-done((f32[136,128]{1,0:T(8,128)S(1)}, f32[136,128]{1,0:T(8,128)S(1)}, u32[]{:S(2)}, u32[]{:S(2)}) %collective-permute-start.9) | collective-permute-done | bytes 69664 | tf_op jit(solution)/shard_map/ppermute | solution.py:409
  33.1 3.8 %collective-permute-done.8 = f32[136,128]{1,0:T(8,128)S(1)} collective-permute-done((f32[136,128]{1,0:T(8,128)S(1)}, f32[136,128]{1,0:T(8,128)S(1)}, u32[]{:S(2)}, u32[]{:S(2)}) %collective-permute-start.8) | collective-permute-done | bytes 69664 | tf_op jit(solution)/shard_map/ppermute | solution.py:409
  36.9 0.1 collective-permute-start.11
  37.0 1.2 %collective-permute-done.11 = f32[136,128]{1,0:T(8,128)S(1)} collective-permute-done((f32[136,128]{1,0:T(8,128)S(1)}, f32[136,128]{1,0:T(8,128)S(1)}, u32[]{:S(2)}, u32[]{:S(2)}) %collective-permute-start.11) | collective-permute-done | bytes 69664 | tf_op jit(solution)/shard_map/ppermute | solution.py:409
  38.3 3.1 %first_solve.1 = (bf16[64,2048]{1,0:T(8,128)(2,1)S(1)}, f32[64,192]{1,0:T(8,128)S(1)}, f32[64,64]{1,0:T(8,128)S(1)}, f32[64,192]{1,0:T(8,128)S(1)}, f32[64,64]{1,0:T(8,128)S(1)}, /*index=5*/bf16[64,64]{1,0:T(8,128)(2,1)S(1)}) custom-call(f32[272,128]{1,0:T(8,128)S(1)} %pad_maximum_fusion.cross, bf16[192,2048]{1,0:T(8,128)(2,1)S(1)} %reshape.18.stack, ...), custom_call_target="tpu_custom_call" | custom-call | bytes 1589248 | tf_op jit(solution)/shard_map/first_solve/pallas_call | solution.py:440
  41.5 0.7 collective-permute-start.12
  42.2 0.7 collective-permute-start.13
  42.9 4.2 %collective-permute-done.12 = bf16[64,1024]{1,0:T(8,128)(2,1)S(1)} collective-permute-done((bf16[64,1024]{1,0:T(8,128)(2,1)S(1)}, bf16[64,1024]{1,0:T(8,128)(2,1)S(1)}, u32[]{:S(2)}, u32[]{:S(2)}) %collective-permute-start.12) | collective-permute-done | bytes 131104 | tf_op jit(solution)/shard_map/ppermute | solution.py:27
  47.1 0.0 collective-permute-done.13
  47.2 0.1 collective-permute-start.15
  47.3 1.0 %collective-permute-start.14 = (bf16[64,512]{1,0:T(8,128)(2,1)S(1)}, bf16[64,512]{1,0:T(8,128)(2,1)S(1)}, u32[]{:S(2)}, u32[]{:S(2)}) collective-permute-start(bf16[64,512]{1,0:T(8,128)(2,1)S(1)} %get-tuple-element.78), channel_id=1, source_target_pairs={{0,1},{1,0},{2,3},{3,2},{4,5},{5,4},{6,7},{7,6},{8,9},{9,8},{10,11... | collective-permute-start | bytes 196616 | tf_op jit(solution)/shard_map/ppermute | solution.py:27
  48.3 0.7 inner_image.3.partial
  49.0 2.2 %collective-permute-done.15 = bf16[64,512]{1,0:T(8,128)(2,1)S(1)} collective-permute-done((bf16[64,512]{1,0:T(8,128)(2,1)S(1)}, bf16[64,512]{1,0:T(8,128)(2,1)S(1)}, u32[]{:S(2)}, u32[]{:S(2)}) %collective-permute-start.15) | collective-permute-done | bytes 65568 | tf_op jit(solution)/shard_map/ppermute | solution.py:28
  51.2 1.1 %second_image.1 = (bf16[64,2048]{1,0:T(8,128)(2,1)S(1)}, f32[64,256]{1,0:T(8,128)S(1)}) custom-call(f32[27,16,128]{2,1,0:T(8,128)S(1)} %coefficients.1.coef, bf16[192,2048]{1,0:T(8,128)(2,1)S(1)} %reshape.18.stack, bf16[64,2048]{1,0:T(8,128)(2,1)S(1)} %get-tuple-element.46.fields.block.last, f32[64,2048]{1,0:T(8,128)S(1)} %inner_image.3.partial, ...), custom_call_target="tpu_custom_call" | custom-call | bytes 2514944 | tf_op jit(solution)/shard_map/second_image/pallas_call | solution.py:440
  52.4 0.1 collective-permute-start.16
  52.4 1.2 %collective-permute-done.16 = f32[32,256]{1,0:T(8,128)S(1)} collective-permute-done((f32[32,256]{1,0:T(8,128)S(1)}, f32[32,256]{1,0:T(8,128)S(1)}, u32[]{:S(2)}, u32[]{:S(2)}) %collective-permute-start.16) | collective-permute-done | bytes 32800 | tf_op jit(solution)/shard_map/ppermute | solution.py:409
  53.6 0.8 %collective-permute-start.19 = (f32[32,256]{1,0:T(8,128)S(1)}, f32[32,256]{1,0:T(8,128)S(1)}, u32[]{:S(2)}, u32[]{:S(2)}) collective-permute-start(f32[32,256]{1,0:T(8,128)S(1)} %select_add_fusion.1), channel_id=1, source_target_pairs={{0,3},{1,2},{2,1},{3,0},{4,7},{5,6},{6,5},{7,4},{8,11},{9,10},{10,... | collective-permute-start | bytes 98312 | tf_op jit(solution)/shard_map/ppermute | solution.py:409
  54.5 4.5 %collective-permute-start.18 = (f32[32,256]{1,0:T(8,128)S(1)}, f32[32,256]{1,0:T(8,128)S(1)}, u32[]{:S(2)}, u32[]{:S(2)}) collective-permute-start(f32[32,256]{1,0:T(8,128)S(1)} %select_add_fusion.1), channel_id=1, source_target_pairs={{0,5},{1,4},{2,7},{3,6},{4,1},{5,0},{6,3},{7,2},{8,13},{9,12},{10,... | collective-permute-start | bytes 98312 | tf_op jit(solution)/shard_map/ppermute | solution.py:409
  59.0 0.4 collective-permute-start.17
  59.3 0.0 collective-permute-done.19
  59.3 1.2 %collective-permute-done.18 = f32[32,256]{1,0:T(8,128)S(1)} collective-permute-done((f32[32,256]{1,0:T(8,128)S(1)}, f32[32,256]{1,0:T(8,128)S(1)}, u32[]{:S(2)}, u32[]{:S(2)}) %collective-permute-start.18) | collective-permute-done | bytes 32800 | tf_op jit(solution)/shard_map/ppermute | solution.py:409
  60.6 3.2 %collective-permute-done.17 = f32[32,256]{1,0:T(8,128)S(1)} collective-permute-done((f32[32,256]{1,0:T(8,128)S(1)}, f32[32,256]{1,0:T(8,128)S(1)}, u32[]{:S(2)}, u32[]{:S(2)}) %collective-permute-start.17) | collective-permute-done | bytes 32800 | tf_op jit(solution)/shard_map/ppermute | solution.py:409
  63.8 0.3 collective-permute-start.22
  64.1 1.1 %collective-permute-start.21 = (f32[32,256]{1,0:T(8,128)S(1)}, f32[32,256]{1,0:T(8,128)S(1)}, u32[]{:S(2)}, u32[]{:S(2)}) collective-permute-start(f32[32,256]{1,0:T(8,128)S(1)} %add_add_fusion.3), channel_id=1, source_target_pairs={{0,17},{1,16},{2,19},{3,18},{4,21},{5,20},{6,23},{7,22},{8,25},{9,... | collective-permute-start | bytes 98312 | tf_op jit(solution)/shard_map/ppermute | solution.py:409
  65.1 2.8 %collective-permute-start.20 = (f32[32,256]{1,0:T(8,128)S(1)}, f32[32,256]{1,0:T(8,128)S(1)}, u32[]{:S(2)}, u32[]{:S(2)}) collective-permute-start(f32[32,256]{1,0:T(8,128)S(1)} %add_add_fusion.3), channel_id=1, source_target_pairs={{0,24},{1,25},{2,26},{3,27},{4,28},{5,29},{6,30},{7,31},{8,16},{9,... | collective-permute-start | bytes 98312 | tf_op jit(solution)/shard_map/ppermute | solution.py:409
  68.0 0.0 collective-permute-done.22
  68.0 0.4 collective-permute-done.21
  68.3 2.6 %collective-permute-done.20 = f32[32,256]{1,0:T(8,128)S(1)} collective-permute-done((f32[32,256]{1,0:T(8,128)S(1)}, f32[32,256]{1,0:T(8,128)S(1)}, u32[]{:S(2)}, u32[]{:S(2)}) %collective-permute-start.20) | collective-permute-done | bytes 32800 | tf_op jit(solution)/shard_map/ppermute | solution.py:409
  71.0 0.3 collective-permute-start.23
  71.3 0.4 next_gram.1
  71.7 0.5 collective-permute-done.23
  72.3 3.6 %second_solve.1 = (bf16[64,2,8,128]{3,2,1,0:T(8,128)(2,1)}, f32[2,64,192]{2,1,0:T(8,128)}, f32[2,64,64]{2,1,0:T(8,128)}) custom-call(f32[64,256]{1,0:T(8,128)S(1)} %pad_maximum_fusion.5.cross, bf16[192,192]{1,0:T(8,128)(2,1)S(1)} %get-tuple-element.53.own_high, bf16[192,192]{1,0:T(8,128)(2,1)S(1)} %get-tuple-element.54.own_low, ...), custom_call_target="tpu_custom_call" | custom-call | bytes 1982464 | tf_op jit(solution)/shard_map/second_solve/pallas_call | solution.py:440
  (30 shorter events, 0.4 us)
Async XLA Ops:
  0.6 1.0 %slice-start = ((bf16[3,64,2,8,128]{4,3,2,1,0:T(8,128)(2,1)}), bf16[1,64,2,8,128]{4,3,2,1,0:T(8,128)(2,1)S(1)}, s32[]{:S(2)}) async-start(bf16[3,64,2,8,128]{4,3,2,1,0:T(8,128)(2,1)} %param.3), calls=%async_computation | async-start | bytes 524288 | tf_op jit(solution)/shard_map/slice | solution.py:481
  1.6 3.8 %copy-start.2 = (bf16[3,64,2,8,128]{4,3,2,1,0:T(8,128)(2,1)S(1)}, bf16[3,64,2,8,128]{4,3,2,1,0:T(8,128)(2,1)}, u32[]{:S(2)}) copy-start(bf16[3,64,2,8,128]{4,3,2,1,0:T(8,128)(2,1)} %param.3) | copy-start | bytes 2359300
  1.7 6.8 %collective-permute-start = (bf16[64,1024]{1,0:T(8,128)(2,1)S(1)}, bf16[64,1024]{1,0:T(8,128)(2,1)S(1)}, u32[]{:S(2)}, u32[]{:S(2)}) collective-permute-start(bf16[64,1024]{1,0:T(8,128)(2,1)S(1)} %slice_select_fusion), channel_id=1, source_target_pairs={{0,4},{4,0},{8,12},{12,8},{16,20},{20,16},{24,28},{28,24},{1,5},{5... | collective-permute-start | bytes 393224 | tf_op jit(solution)/shard_map/ppermute | solution.py:27
  4.8 3.8 %collective-permute-start.1 = (bf16[64,1024]{1,0:T(8,128)(2,1)S(1)}, bf16[64,1024]{1,0:T(8,128)(2,1)S(1)}, u32[]{:S(2)}, u32[]{:S(2)}) collective-permute-start(bf16[64,1024]{1,0:T(8,128)(2,1)S(1)} %cut.2), channel_id=1, source_target_pairs={{4,8},{8,4},{12,16},{16,12},{20,24},{24,20},{5,9},{9,5},{13,17},{1... | collective-permute-start | bytes 393224 | tf_op jit(solution)/shard_map/ppermute | solution.py:28
  5.5 0.7 copy-start
  5.8 0.7 copy-start.1
  8.6 4.4 %collective-permute-start.3 = (bf16[64,512]{1,0:T(8,128)(2,1)S(1)}, bf16[64,512]{1,0:T(8,128)(2,1)S(1)}, u32[]{:S(2)}, u32[]{:S(2)}) collective-permute-start(bf16[64,512]{1,0:T(8,128)(2,1)S(1)} %get-tuple-element.85), channel_id=1, source_target_pairs={{1,2},{2,1},{0,3},{3,0},{5,6},{6,5},{4,7},{7,4},{9,10},{10,9},{8,1... | collective-permute-start | bytes 196616 | tf_op jit(solution)/shard_map/ppermute | solution.py:28
  9.4 3.6 %collective-permute-start.2 = (bf16[64,512]{1,0:T(8,128)(2,1)S(1)}, bf16[64,512]{1,0:T(8,128)(2,1)S(1)}, u32[]{:S(2)}, u32[]{:S(2)}) collective-permute-start(bf16[64,512]{1,0:T(8,128)(2,1)S(1)} %get-tuple-element.86), channel_id=1, source_target_pairs={{0,1},{1,0},{2,3},{3,2},{4,5},{5,4},{6,7},{7,6},{8,9},{9,8},{10,11... | collective-permute-start | bytes 196616 | tf_op jit(solution)/shard_map/ppermute | solution.py:27
  14.2 1.3 %collective-permute-start.4 = (f32[136,128]{1,0:T(8,128)S(1)}, f32[136,128]{1,0:T(8,128)S(1)}, u32[]{:S(2)}, u32[]{:S(2)}) collective-permute-start(f32[136,128]{1,0:T(8,128)S(1)} %slice_select_fusion.2), channel_id=1, source_target_pairs={{0,1},{1,0},{2,3},{3,2},{4,5},{5,4},{6,7},{7,6},{8,9},{9,8},{10,11... | collective-permute-start | bytes 208904 | tf_op jit(solution)/shard_map/ppermute | solution.py:409
  15.5 5.5 %collective-permute-start.7 = (f32[136,128]{1,0:T(8,128)S(1)}, f32[136,128]{1,0:T(8,128)S(1)}, u32[]{:S(2)}, u32[]{:S(2)}) collective-permute-start(f32[136,128]{1,0:T(8,128)S(1)} %select_add_fusion), channel_id=1, source_target_pairs={{0,3},{1,2},{2,1},{3,0},{4,7},{5,6},{6,5},{7,4},{8,11},{9,10},{10,... | collective-permute-start | bytes 208904 | tf_op jit(solution)/shard_map/ppermute | solution.py:409
  16.7 6.5 %collective-permute-start.6 = (f32[136,128]{1,0:T(8,128)S(1)}, f32[136,128]{1,0:T(8,128)S(1)}, u32[]{:S(2)}, u32[]{:S(2)}) collective-permute-start(f32[136,128]{1,0:T(8,128)S(1)} %select_add_fusion), channel_id=1, source_target_pairs={{0,5},{1,4},{2,7},{3,6},{4,1},{5,0},{6,3},{7,2},{8,13},{9,12},{10,... | collective-permute-start | bytes 208904 | tf_op jit(solution)/shard_map/ppermute | solution.py:409
  20.7 5.2 %collective-permute-start.5 = (f32[136,128]{1,0:T(8,128)S(1)}, f32[136,128]{1,0:T(8,128)S(1)}, u32[]{:S(2)}, u32[]{:S(2)}) collective-permute-start(f32[136,128]{1,0:T(8,128)S(1)} %select_add_fusion), channel_id=1, source_target_pairs={{0,6},{1,7},{2,4},{3,5},{4,2},{5,3},{6,0},{7,1},{8,14},{9,15},{10,... | collective-permute-start | bytes 208904 | tf_op jit(solution)/shard_map/ppermute | solution.py:409
  26.0 4.8 %collective-permute-start.10 = (f32[136,128]{1,0:T(8,128)S(1)}, f32[136,128]{1,0:T(8,128)S(1)}, u32[]{:S(2)}, u32[]{:S(2)}) collective-permute-start(f32[136,128]{1,0:T(8,128)S(1)} %add_add_fusion.1), channel_id=1, source_target_pairs={{0,9},{1,8},{2,11},{3,10},{4,13},{5,12},{6,15},{7,14},{8,1},{9,0},... | collective-permute-start | bytes 208904 | tf_op jit(solution)/shard_map/ppermute | solution.py:409
  27.7 5.4 %collective-permute-start.9 = (f32[136,128]{1,0:T(8,128)S(1)}, f32[136,128]{1,0:T(8,128)S(1)}, u32[]{:S(2)}, u32[]{:S(2)}) collective-permute-start(f32[136,128]{1,0:T(8,128)S(1)} %add_add_fusion.1), channel_id=1, source_target_pairs={{0,17},{1,16},{2,19},{3,18},{4,21},{5,20},{6,23},{7,22},{8,25},{9,... | collective-permute-start | bytes 208904 | tf_op jit(solution)/shard_map/ppermute | solution.py:409
  30.8 6.2 %collective-permute-start.8 = (f32[136,128]{1,0:T(8,128)S(1)}, f32[136,128]{1,0:T(8,128)S(1)}, u32[]{:S(2)}, u32[]{:S(2)}) collective-permute-start(f32[136,128]{1,0:T(8,128)S(1)} %add_add_fusion.1), channel_id=1, source_target_pairs={{0,24},{1,25},{2,26},{3,27},{4,28},{5,29},{6,30},{7,31},{8,16},{9,... | collective-permute-start | bytes 208904 | tf_op jit(solution)/shard_map/ppermute | solution.py:409
  36.9 1.3 %collective-permute-start.11 = (f32[136,128]{1,0:T(8,128)S(1)}, f32[136,128]{1,0:T(8,128)S(1)}, u32[]{:S(2)}, u32[]{:S(2)}) collective-permute-start(f32[136,128]{1,0:T(8,128)S(1)} %add_add_fusion), channel_id=1, source_target_pairs={{0,1},{1,0},{2,3},{3,2},{4,5},{5,4},{6,7},{7,6},{8,9},{9,8},{10,11... | collective-permute-start | bytes 208904 | tf_op jit(solution)/shard_map/ppermute | solution.py:409
  41.5 5.6 %collective-permute-start.12 = (bf16[64,1024]{1,0:T(8,128)(2,1)S(1)}, bf16[64,1024]{1,0:T(8,128)(2,1)S(1)}, u32[]{:S(2)}, u32[]{:S(2)}) collective-permute-start(bf16[64,1024]{1,0:T(8,128)(2,1)S(1)} %slice_select_fusion.1), channel_id=1, source_target_pairs={{0,4},{4,0},{8,12},{12,8},{16,20},{20,16},{24,28},{28,24},{1,5},{5... | collective-permute-start | bytes 393224 | tf_op jit(solution)/shard_map/ppermute | solution.py:27
  42.2 4.9 %collective-permute-start.13 = (bf16[64,1024]{1,0:T(8,128)(2,1)S(1)}, bf16[64,1024]{1,0:T(8,128)(2,1)S(1)}, u32[]{:S(2)}, u32[]{:S(2)}) collective-permute-start(bf16[64,1024]{1,0:T(8,128)(2,1)S(1)} %cut.3), channel_id=1, source_target_pairs={{4,8},{8,4},{12,16},{16,12},{20,24},{24,20},{5,9},{9,5},{13,17},{1... | collective-permute-start | bytes 393224 | tf_op jit(solution)/shard_map/ppermute | solution.py:28
  47.2 4.0 %collective-permute-start.15 = (bf16[64,512]{1,0:T(8,128)(2,1)S(1)}, bf16[64,512]{1,0:T(8,128)(2,1)S(1)}, u32[]{:S(2)}, u32[]{:S(2)}) collective-permute-start(bf16[64,512]{1,0:T(8,128)(2,1)S(1)} %get-tuple-element.77), channel_id=1, source_target_pairs={{1,2},{2,1},{0,3},{3,0},{5,6},{6,5},{4,7},{7,4},{9,10},{10,9},{8,1... | collective-permute-start | bytes 196616 | tf_op jit(solution)/shard_map/ppermute | solution.py:28
  47.3 3.9 %collective-permute-start.14 = (bf16[64,512]{1,0:T(8,128)(2,1)S(1)}, bf16[64,512]{1,0:T(8,128)(2,1)S(1)}, u32[]{:S(2)}, u32[]{:S(2)}) collective-permute-start(bf16[64,512]{1,0:T(8,128)(2,1)S(1)} %get-tuple-element.78), channel_id=1, source_target_pairs={{0,1},{1,0},{2,3},{3,2},{4,5},{5,4},{6,7},{7,6},{8,9},{9,8},{10,11... | collective-permute-start | bytes 196616 | tf_op jit(solution)/shard_map/ppermute | solution.py:27
  52.4 1.3 %collective-permute-start.16 = (f32[32,256]{1,0:T(8,128)S(1)}, f32[32,256]{1,0:T(8,128)S(1)}, u32[]{:S(2)}, u32[]{:S(2)}) collective-permute-start(f32[32,256]{1,0:T(8,128)S(1)} %slice_select_fusion.3), channel_id=1, source_target_pairs={{0,1},{1,0},{2,3},{3,2},{4,5},{5,4},{6,7},{7,6},{8,9},{9,8},{10,11... | collective-permute-start | bytes 98312 | tf_op jit(solution)/shard_map/ppermute | solution.py:409
  53.6 5.7 %collective-permute-start.19 = (f32[32,256]{1,0:T(8,128)S(1)}, f32[32,256]{1,0:T(8,128)S(1)}, u32[]{:S(2)}, u32[]{:S(2)}) collective-permute-start(f32[32,256]{1,0:T(8,128)S(1)} %select_add_fusion.1), channel_id=1, source_target_pairs={{0,3},{1,2},{2,1},{3,0},{4,7},{5,6},{6,5},{7,4},{8,11},{9,10},{10,... | collective-permute-start | bytes 98312 | tf_op jit(solution)/shard_map/ppermute | solution.py:409
  54.5 6.1 %collective-permute-start.18 = (f32[32,256]{1,0:T(8,128)S(1)}, f32[32,256]{1,0:T(8,128)S(1)}, u32[]{:S(2)}, u32[]{:S(2)}) collective-permute-start(f32[32,256]{1,0:T(8,128)S(1)} %select_add_fusion.1), channel_id=1, source_target_pairs={{0,5},{1,4},{2,7},{3,6},{4,1},{5,0},{6,3},{7,2},{8,13},{9,12},{10,... | collective-permute-start | bytes 98312 | tf_op jit(solution)/shard_map/ppermute | solution.py:409
  59.0 4.8 %collective-permute-start.17 = (f32[32,256]{1,0:T(8,128)S(1)}, f32[32,256]{1,0:T(8,128)S(1)}, u32[]{:S(2)}, u32[]{:S(2)}) collective-permute-start(f32[32,256]{1,0:T(8,128)S(1)} %select_add_fusion.1), channel_id=1, source_target_pairs={{0,6},{1,7},{2,4},{3,5},{4,2},{5,3},{6,0},{7,1},{8,14},{9,15},{10,... | collective-permute-start | bytes 98312 | tf_op jit(solution)/shard_map/ppermute | solution.py:409
  63.8 4.2 %collective-permute-start.22 = (f32[32,256]{1,0:T(8,128)S(1)}, f32[32,256]{1,0:T(8,128)S(1)}, u32[]{:S(2)}, u32[]{:S(2)}) collective-permute-start(f32[32,256]{1,0:T(8,128)S(1)} %add_add_fusion.3), channel_id=1, source_target_pairs={{0,9},{1,8},{2,11},{3,10},{4,13},{5,12},{6,15},{7,14},{8,1},{9,0},... | collective-permute-start | bytes 98312 | tf_op jit(solution)/shard_map/ppermute | solution.py:409
  64.1 4.2 %collective-permute-start.21 = (f32[32,256]{1,0:T(8,128)S(1)}, f32[32,256]{1,0:T(8,128)S(1)}, u32[]{:S(2)}, u32[]{:S(2)}) collective-permute-start(f32[32,256]{1,0:T(8,128)S(1)} %add_add_fusion.3), channel_id=1, source_target_pairs={{0,17},{1,16},{2,19},{3,18},{4,21},{5,20},{6,23},{7,22},{8,25},{9,... | collective-permute-start | bytes 98312 | tf_op jit(solution)/shard_map/ppermute | solution.py:409
  65.1 5.8 %collective-permute-start.20 = (f32[32,256]{1,0:T(8,128)S(1)}, f32[32,256]{1,0:T(8,128)S(1)}, u32[]{:S(2)}, u32[]{:S(2)}) collective-permute-start(f32[32,256]{1,0:T(8,128)S(1)} %add_add_fusion.3), channel_id=1, source_target_pairs={{0,24},{1,25},{2,26},{3,27},{4,28},{5,29},{6,30},{7,31},{8,16},{9,... | collective-permute-start | bytes 98312 | tf_op jit(solution)/shard_map/ppermute | solution.py:409
  71.0 1.3 %collective-permute-start.23 = (f32[32,256]{1,0:T(8,128)S(1)}, f32[32,256]{1,0:T(8,128)S(1)}, u32[]{:S(2)}, u32[]{:S(2)}) collective-permute-start(f32[32,256]{1,0:T(8,128)S(1)} %add_add_fusion.2), channel_id=1, source_target_pairs={{0,1},{1,0},{2,3},{3,2},{4,5},{5,4},{6,7},{7,6},{8,9},{9,8},{10,11... | collective-permute-start | bytes 98312 | tf_op jit(solution)/shard_map/ppermute | solution.py:409

commit v18 on v15

--- a/solution.py
+++ b/solution.py
@@ -17,38 +17,78 @@
     return lax.dot_general(left, right, dims, preferred_element_type=jnp.float32)
 
 
-def swaps(axis, upward, downward, closed, beside=None):
+def swap_pairs(axis, closed):
     count = lax.axis_size(axis)
-    me = lax.axis_index(axis)
-    odd = me % 2 == 1
-    pairs = [(i, (i - 1 ^ 1) + 1) for i in range(1, count - 1)]
+    near = [(i, i ^ 1) for i in range(count)]
+    far = [(i, (i - 1 ^ 1) + 1) for i in range(1, count - 1)]
     if closed:
-        pairs += [(0, count - 1), (count - 1, 0)]
-    near, far = jnp.where(odd, downward, upward), jnp.where(odd, upward, downward)
-    inner = lax.ppermute(near, axis, [(i, i ^ 1) for i in range(count)])
-    far, beside = lax.optimization_barrier((far, beside))
-    outer = lax.ppermute(far, axis, pairs)
-    if closed:
-        outer = jnp.where((me == 0) | (me == count - 1), 0, outer)
-    return jnp.where(odd, inner, outer), jnp.where(odd, outer, inner), beside
+        far += [(0, count - 1), (count - 1, 0)]
+    return near, far
+
+
+def cut_kernel(depth, start, block, ends, rest):
+    lines = rest.shape[1] // depth + 2
+    for ref, at, line in ((ends, 0, 0), (ends, 1, lines - 1), (rest, 0, 1)):
+        width = depth if ref is ends else rest.shape[1]
+        there = pl.ds(pl.multiple_of(start[0] + line * depth, 128), width)
+        ref[:, at * depth : at * depth + width] = block[:, there]
+
+
+def cut(block, start, lines, depth):
+    columns = block.shape[0]
+    return pl.pallas_call(
+        functools.partial(cut_kernel, depth),
+        out_shape=[
+            jax.ShapeDtypeStruct((columns, count * depth), block.dtype) for count in (2, lines - 2)
+        ],
+        in_specs=[
+            pl.BlockSpec(memory_space=pltpu.SMEM),
+            pl.BlockSpec(memory_space=pltpu.VMEM),
+        ],
+        out_specs=[pl.BlockSpec(memory_space=pltpu.VMEM)] * 2,
+        compiler_params=pltpu.CompilerParams(vmem_limit_bytes=4 * 1024 * 1024),
+        name="cut",
+    )(start.reshape(1), block)
 
 
 def neighbours(block, span_x, span_y, depth, beside=None, meanwhile=None):
     plane = span_y * depth
-    xlo, xhi, beside = swaps(
-        "slab", block[:, (span_x - 1) * plane :], block[:, :plane], False, beside
-    )
-    xlo, xhi, meanwhile = lax.optimization_barrier((xlo, xhi, meanwhile))
-
-    def edge(row):
-        at = row * depth
-        parts = [xlo[:, at : at + depth]]
+    top = (span_x - 1) * plane
+    odd = lax.axis_index("slab") % 2 == 1
+    near_pairs, far_pairs = swap_pairs("slab", False)
+    far_ends, far_rest = cut(block, jnp.where(odd, top, 0), span_y, depth)
+    near = lax.ppermute(
+        jnp.where(odd, block[:, :plane], block[:, top:]), "slab", near_pairs
+    )
+    far_ends = lax.ppermute(far_ends, "slab", far_pairs)
+    far_rest, beside = lax.optimization_barrier((far_rest, beside))
+    far_rest = lax.ppermute(far_rest, "slab", far_pairs)
+
+    def sort(near, far, odd):
+        return jnp.where(odd, near, far), jnp.where(odd, far, near)
+
+    far_ends, near = lax.optimization_barrier((far_ends, near))
+    near_ends = jnp.concatenate([near[:, :depth], near[:, plane - depth :]], axis=1)
+    xlo_ends, xhi_ends = sort(near_ends, far_ends, odd)
+    xlo_ends, xhi_ends, meanwhile = lax.optimization_barrier((xlo_ends, xhi_ends, meanwhile))
+
+    def edge(last):
+        at = (span_y - 1) * depth * last
+        parts = [xlo_ends[:, last * depth : (last + 1) * depth]]
         parts += [block[:, x * plane + at : x * plane + at + depth] for x in range(span_x)]
-        parts += [xhi[:, at : at + depth]]
+        parts += [xhi_ends[:, last * depth : (last + 1) * depth]]
         return jnp.concatenate(parts, axis=1)
 
-    ylo, yhi, _ = swaps("col", edge(span_y - 1), edge(0), True)
-    return (xlo, xhi, ylo, yhi), beside, meanwhile
+    me = lax.axis_index("col")
+    odd_col = me % 2 == 1
+    near_pairs, far_pairs = swap_pairs("col", True)
+    upward, downward = edge(1), edge(0)
+    near_y = lax.ppermute(jnp.where(odd_col, downward, upward), "col", near_pairs)
+    far_y = lax.ppermute(jnp.where(odd_col, upward, downward), "col", far_pairs)
+    far_y = jnp.where((me == 0) | (me == lax.axis_size("col") - 1), 0, far_y)
+    ylo, yhi = sort(near_y, far_y, odd_col)
+    xlo, xhi = sort(near[:, depth : plane - depth], far_rest, odd)
+    return (xlo_ends, xlo, xhi_ends, xhi, ylo, yhi), beside, meanwhile
 
 
 def coefficients_kernel(table, cells, coef):
@@ -135,7 +175,7 @@
     stencil(coef, spans, columns, line, True, write)
 
 
-def complete(image, partial, coef, spans, xlo, xhi, ylo, yhi):
+def complete(image, partial, coef, spans, xlo_ends, xlo, xhi_ends, xhi, ylo, yhi):
     span_x, span_y, depth = spans
 
     def line(rows, x, y):
@@ -143,8 +183,10 @@
             ref, at = ylo, x + 1
         elif y >= span_y:
             ref, at = yhi, x + 1
+        elif y in (0, span_y - 1):
+            ref, at = (xlo_ends if x < 0 else xhi_ends), int(y > 0)
         else:
-            ref, at = (xlo, y) if x < 0 else (xhi, y)
+            ref, at = (xlo if x < 0 else xhi), y - 1
         return ref[rows, at * depth : (at + 1) * depth].astype(jnp.float32)
 
     def write(rows, x, y, total):
@@ -186,10 +228,11 @@
 
 
 def first_image_kernel(
-    spans, coef, stack, sides, pair, last, diagonal, partial, xlo, xhi, ylo, yhi, image, cross
+    spans, coef, stack, sides, pair, last, diagonal, partial, *around_and_outs
 ):
+    *around, image, cross = around_and_outs
     columns = image.shape[0]
-    complete(image, partial, coef, spans, xlo, xhi, ylo, yhi)
+    complete(image, partial, coef, spans, *around)
     w = image[...]
     first = dot(w, stack[...], NT)
     corner, own_diagonal = two_in_one(last[...], dot(w, w, NT))
@@ -218,10 +261,11 @@
     return first, square, gram
 
 
-def second_image_kernel(spans, coef, stack, block, partial, xlo, xhi, ylo, yhi, image, cross):
+def second_image_kernel(spans, coef, stack, block, partial, *around_and_outs):
+    *around, image, cross = around_and_outs
     columns = image.shape[0]
     fields = stack.shape[0]
-    complete(image, partial, coef, spans, xlo, xhi, ylo, yhi)
+    complete(image, partial, coef, spans, *around)
     w = image[...]
     cross[:, : fields - columns] = dot(w, stack[columns:], NT)
     cross[:, fields - columns : fields] = dot(w, block[...], NT)

time: 76.7 us -> 76.7 us (level)
    ppermute x8 -> x10, starting transfers between devices: 11 us -> 14.5 us  [the longest x2 8.98 us: neighbours(): lax.ppermute(jnp.where(odd, block[:, :plane], block[:, top:]), 'slab', ne...]
    ppermute x16, starting transfers between devices: 21.1 us -> 18 us  [partner(): return lax.ppermute(part, axes, [(i, i ^ mask) for i in range(count)])]
    ppermute x8 -> x10, waiting for transfers between devices: 10.2 us -> 10.1 us  [the longest x2 5.45 us: neighbours(): far_y = lax.ppermute(jnp.where(odd_col, upward, downward), 'col', far_pairs)]
  transfers between devices with their start and end apart: 24 -> 26, of which waited for: 16 -> 16; matrix products, arithmetic and copies ran while one was open for 0% -> 1% of each run, Pallas kernels for 4% -> 4%
where the time goes in v18:
time: 76.7 us; the launch traced here: 76.5 us
  starting transfers between devices  32.5 us (42%)
  waiting for transfers between devices  28.9 us (38%)
  Pallas kernels  12.1 us (16%)
  local copies, waits for them, and re-layouts  1.48 us (2%)
  between operations  1.16 us (2%)
    ppermute x16, waiting for transfers between devices, partner(): return lax.ppermute(part, axes, [(i, i ^ mask) for i in range(count)])  18.8 us
    ppermute x16, starting transfers between devices, partner(): return lax.ppermute(part, axes, [(i, i ^ mask) for i in range(count)])  18 us
    pallas_call x8, Pallas kernels, call(): pl.pallas_call(kernel, out_shape=[jax.ShapeDtypeStruct(shape, dtype) for...  11.3 us
    ppermute x2, starting transfers between devices, neighbours(): lax.ppermute(jnp.where(odd, block[:, :plane], block[:, top:]), 'slab', ne...  8.98 us
    ppermute x2, waiting for transfers between devices, neighbours(): far_y = lax.ppermute(jnp.where(odd_col, upward, downward), 'col', far_pairs)  5.45 us
    ppermute x2, waiting for transfers between devices, neighbours(): lax.ppermute(jnp.where(odd, block[:, :plane], block[:, top:]), 'slab', ne...  4.67 us
    ppermute x2, starting transfers between devices, neighbours(): lax.ppermute(jnp.where(odd_col, downward, upward), 'col', near_pairs)  2.35 us
  transfers between devices with their start and end apart: 26, of which 16 were waited for; matrix products, arithmetic and copies ran while one was open for 1% of the time, Pallas kernels for 4%

profile of v18, /device:TPU:0, one launch (start us, length us, event | category | flops | bytes accessed | tf_op | source)
XLA Modules:
  0.0 76.5 jit_solution(2572284628641556638)
XLA Ops:
  0.6 0.0 slice-start
  0.7 0.9 %slice-done = bf16[1,64,2,8,128]{4,3,2,1,0:T(8,128)(2,1)S(1)} async-done(((bf16[3,64,2,8,128]{4,3,2,1,0:T(8,128)(2,1)}), bf16[1,64,2,8,128]{4,3,2,1,0:T(8,128)(2,1)S(1)}, s32[]{:S(2)}) %slice-start) | async-done | bytes 262168 | tf_op jit(solution)/shard_map/slice | solution.py:503
  1.6 0.1 reshape_squeeze.3.block.fields
  1.7 0.0 copy-start
  1.8 0.7 collective-permute-start
  2.4 0.0 copy-start.1
  2.5 0.0 copy-start.2
  2.5 5.8 %collective-permute-start.1 = (bf16[64,1024]{1,0:T(8,128)(2,1)S(1)}, bf16[64,1024]{1,0:T(8,128)(2,1)S(1)}, u32[]{:S(2)}, u32[]{:S(2)}) collective-permute-start(bf16[64,1024]{1,0:T(8,128)(2,1)S(1)} %slice_select_fusion), channel_id=1, source_target_pairs={{0,4},{4,0},{8,12},{12,8},{16,20},{20,16},{24,28},{28,24},{1,5},{5... | collective-permute-start | bytes 393224 | tf_op jit(solution)/shard_map/ppermute | solution.py:60
  8.3 0.8 coefficients.1.coef
  9.0 0.7 inner_image.2.partial
  9.7 0.7 collective-permute-start.2
  10.5 0.3 reshape.18.stack
  10.9 0.6 stack_gram.1
  11.5 0.0 collective-permute-done
  11.5 0.0 collective-permute-done.1
  11.6 0.5 collective-permute-start.4
  12.1 1.2 %collective-permute-start.3 = (bf16[64,512]{1,0:T(8,128)(2,1)S(1)}, bf16[64,512]{1,0:T(8,128)(2,1)S(1)}, u32[]{:S(2)}, u32[]{:S(2)}) collective-permute-start(bf16[64,512]{1,0:T(8,128)(2,1)S(1)} %get-tuple-element.102), channel_id=1, source_target_pairs={{0,1},{1,0},{2,3},{3,2},{4,5},{5,4},{6,7},{7,6},{8,9},{9,8},{10,11... | collective-permute-start | bytes 196616 | tf_op jit(solution)/shard_map/ppermute | solution.py:86
  13.3 0.0 collective-permute-done.2
  13.4 2.6 %collective-permute-done.4 = bf16[64,512]{1,0:T(8,128)(2,1)S(1)} collective-permute-done((bf16[64,512]{1,0:T(8,128)(2,1)S(1)}, bf16[64,512]{1,0:T(8,128)(2,1)S(1)}, u32[]{:S(2)}, u32[]{:S(2)}) %collective-permute-start.4) | collective-permute-done | bytes 65568 | tf_op jit(solution)/shard_map/ppermute | solution.py:87
  16.0 1.1 %first_image.1 = (bf16[64,2048]{1,0:T(8,128)(2,1)S(1)}, f32[272,128]{1,0:T(8,128)S(1)}) custom-call(f32[27,16,128]{2,1,0:T(8,128)S(1)} %coefficients.1.coef, bf16[192,2048]{1,0:T(8,128)(2,1)S(1)} %reshape.18.stack, f32[3,64,64]{2,1,0:T(8,128)S(1)} %get-tuple-element.49.sides, f32[64,64]{1,0:T(8,128)S(1)} %get-tuple-element.50.pair, ...), custom_call_target="tpu_custom_call" | custom-call | bytes 2408704 | tf_op jit(solution)/shard_map/first_image/pallas_call | solution.py:462
  17.2 0.2 collective-permute-start.5
  17.3 1.1 %collective-permute-done.5 = f32[136,128]{1,0:T(8,128)S(1)} collective-permute-done((f32[136,128]{1,0:T(8,128)S(1)}, f32[136,128]{1,0:T(8,128)S(1)}, u32[]{:S(2)}, u32[]{:S(2)}) %collective-permute-start.5) | collective-permute-done | bytes 69664 | tf_op jit(solution)/shard_map/ppermute | solution.py:431
  18.5 4.7 %collective-permute-start.8 = (f32[136,128]{1,0:T(8,128)S(1)}, f32[136,128]{1,0:T(8,128)S(1)}, u32[]{:S(2)}, u32[]{:S(2)}) collective-permute-start(f32[136,128]{1,0:T(8,128)S(1)} %select_add_fusion), channel_id=1, source_target_pairs={{0,6},{1,7},{2,4},{3,5},{4,2},{5,3},{6,0},{7,1},{8,14},{9,15},{10,... | collective-permute-start | bytes 208904 | tf_op jit(solution)/shard_map/ppermute | solution.py:431
  23.2 0.6 collective-permute-start.6
  23.8 1.9 %collective-permute-done.8 = f32[136,128]{1,0:T(8,128)S(1)} collective-permute-done((f32[136,128]{1,0:T(8,128)S(1)}, f32[136,128]{1,0:T(8,128)S(1)}, u32[]{:S(2)}, u32[]{:S(2)}) %collective-permute-start.8) | collective-permute-done | bytes 69664 | tf_op jit(solution)/shard_map/ppermute | solution.py:431
  25.7 1.9 %collective-permute-done.7 = f32[136,128]{1,0:T(8,128)S(1)} collective-permute-done((f32[136,128]{1,0:T(8,128)S(1)}, f32[136,128]{1,0:T(8,128)S(1)}, u32[]{:S(2)}, u32[]{:S(2)}) %collective-permute-start.7) | collective-permute-done | bytes 69664 | tf_op jit(solution)/shard_map/ppermute | solution.py:431
  27.6 0.0 collective-permute-done.6
  27.6 2.9 %collective-permute-start.11 = (f32[136,128]{1,0:T(8,128)S(1)}, f32[136,128]{1,0:T(8,128)S(1)}, u32[]{:S(2)}, u32[]{:S(2)}) collective-permute-start(f32[136,128]{1,0:T(8,128)S(1)} %add_add_fusion.1), channel_id=1, source_target_pairs={{0,24},{1,25},{2,26},{3,27},{4,28},{5,29},{6,30},{7,31},{8,16},{9,... | collective-permute-start | bytes 208904 | tf_op jit(solution)/shard_map/ppermute | solution.py:431
  30.5 0.0 collective-permute-start.10
  30.5 1.3 %collective-permute-start.9 = (f32[136,128]{1,0:T(8,128)S(1)}, f32[136,128]{1,0:T(8,128)S(1)}, u32[]{:S(2)}, u32[]{:S(2)}) collective-permute-start(f32[136,128]{1,0:T(8,128)S(1)} %add_add_fusion.1), channel_id=1, source_target_pairs={{0,9},{1,8},{2,11},{3,10},{4,13},{5,12},{6,15},{7,14},{8,1},{9,0},... | collective-permute-start | bytes 208904 | tf_op jit(solution)/shard_map/ppermute | solution.py:431
  31.8 2.6 %collective-permute-done.11 = f32[136,128]{1,0:T(8,128)S(1)} collective-permute-done((f32[136,128]{1,0:T(8,128)S(1)}, f32[136,128]{1,0:T(8,128)S(1)}, u32[]{:S(2)}, u32[]{:S(2)}) %collective-permute-start.11) | collective-permute-done | bytes 69664 | tf_op jit(solution)/shard_map/ppermute | solution.py:431
  34.4 2.4 %collective-permute-done.10 = f32[136,128]{1,0:T(8,128)S(1)} collective-permute-done((f32[136,128]{1,0:T(8,128)S(1)}, f32[136,128]{1,0:T(8,128)S(1)}, u32[]{:S(2)}, u32[]{:S(2)}) %collective-permute-start.10) | collective-permute-done | bytes 69664 | tf_op jit(solution)/shard_map/ppermute | solution.py:431
  36.8 0.0 collective-permute-done.9
  36.9 0.5 collective-permute-start.12
  37.3 0.9 %collective-permute-done.12 = f32[136,128]{1,0:T(8,128)S(1)} collective-permute-done((f32[136,128]{1,0:T(8,128)S(1)}, f32[136,128]{1,0:T(8,128)S(1)}, u32[]{:S(2)}, u32[]{:S(2)}) %collective-permute-start.12) | collective-permute-done | bytes 69664 | tf_op jit(solution)/shard_map/ppermute | solution.py:431
  38.3 3.1 %first_solve.1 = (bf16[64,2048]{1,0:T(8,128)(2,1)S(1)}, f32[64,192]{1,0:T(8,128)S(1)}, f32[64,64]{1,0:T(8,128)S(1)}, f32[64,192]{1,0:T(8,128)S(1)}, f32[64,64]{1,0:T(8,128)S(1)}, /*index=5*/bf16[64,64]{1,0:T(8,128)(2,1)S(1)}) custom-call(f32[272,128]{1,0:T(8,128)S(1)} %pad_maximum_fusion.cross, bf16[192,2048]{1,0:T(8,128)(2,1)S(1)} %reshape.18.stack, ...), custom_call_target="tpu_custom_call" | custom-call | bytes 1589248 | tf_op jit(solution)/shard_map/first_solve/pallas_call | solution.py:462
  41.5 0.7 collective-permute-start.13
  42.1 3.2 %collective-permute-start.14 = (bf16[64,1024]{1,0:T(8,128)(2,1)S(1)}, bf16[64,1024]{1,0:T(8,128)(2,1)S(1)}, u32[]{:S(2)}, u32[]{:S(2)}) collective-permute-start(bf16[64,1024]{1,0:T(8,128)(2,1)S(1)} %slice_select_fusion.1), channel_id=1, source_target_pairs={{0,4},{4,0},{8,12},{12,8},{16,20},{20,16},{24,28},{28,24},{1,5},{5... | collective-permute-start | bytes 393224 | tf_op jit(solution)/shard_map/ppermute | solution.py:60
  45.3 0.7 collective-permute-start.15
  46.0 0.7 inner_image.3.partial
  46.7 0.0 collective-permute-done.13
  46.7 4.7 %collective-permute-done.14 = bf16[64,1024]{1,0:T(8,128)(2,1)S(1)} collective-permute-done((bf16[64,1024]{1,0:T(8,128)(2,1)S(1)}, bf16[64,1024]{1,0:T(8,128)(2,1)S(1)}, u32[]{:S(2)}, u32[]{:S(2)}) %collective-permute-start.14) | collective-permute-done | bytes 131104 | tf_op jit(solution)/shard_map/ppermute | solution.py:60
  51.5 0.1 collective-permute-start.17
  51.6 1.1 %collective-permute-start.16 = (bf16[64,512]{1,0:T(8,128)(2,1)S(1)}, bf16[64,512]{1,0:T(8,128)(2,1)S(1)}, u32[]{:S(2)}, u32[]{:S(2)}) collective-permute-start(bf16[64,512]{1,0:T(8,128)(2,1)S(1)} %get-tuple-element.96), channel_id=1, source_target_pairs={{0,1},{1,0},{2,3},{3,2},{4,5},{5,4},{6,7},{7,6},{8,9},{9,8},{10,11... | collective-permute-start | bytes 196616 | tf_op jit(solution)/shard_map/ppermute | solution.py:86
  52.7 0.0 collective-permute-done.15
  52.7 2.8 %collective-permute-done.17 = bf16[64,512]{1,0:T(8,128)(2,1)S(1)} collective-permute-done((bf16[64,512]{1,0:T(8,128)(2,1)S(1)}, bf16[64,512]{1,0:T(8,128)(2,1)S(1)}, u32[]{:S(2)}, u32[]{:S(2)}) %collective-permute-start.17) | collective-permute-done | bytes 65568 | tf_op jit(solution)/shard_map/ppermute | solution.py:87
  55.5 0.0 collective-permute-done.16
  55.5 1.1 %second_image.1 = (bf16[64,2048]{1,0:T(8,128)(2,1)S(1)}, f32[64,256]{1,0:T(8,128)S(1)}) custom-call(f32[27,16,128]{2,1,0:T(8,128)S(1)} %coefficients.1.coef, bf16[192,2048]{1,0:T(8,128)(2,1)S(1)} %reshape.18.stack, bf16[64,2048]{1,0:T(8,128)(2,1)S(1)} %get-tuple-element.60.fields.block.last, f32[64,2048]{1,0:T(8,128)S(1)} %inner_image.3.partial, ...), custom_call_target="tpu_custom_call" | custom-call | bytes 2514944 | tf_op jit(solution)/shard_map/second_image/pallas_call | solution.py:462
  56.6 0.1 collective-permute-start.18
  56.7 1.2 %collective-permute-done.18 = f32[32,256]{1,0:T(8,128)S(1)} collective-permute-done((f32[32,256]{1,0:T(8,128)S(1)}, f32[32,256]{1,0:T(8,128)S(1)}, u32[]{:S(2)}, u32[]{:S(2)}) %collective-permute-start.18) | collective-permute-done | bytes 32800 | tf_op jit(solution)/shard_map/ppermute | solution.py:431
  57.9 2.9 %collective-permute-start.21 = (f32[32,256]{1,0:T(8,128)S(1)}, f32[32,256]{1,0:T(8,128)S(1)}, u32[]{:S(2)}, u32[]{:S(2)}) collective-permute-start(f32[32,256]{1,0:T(8,128)S(1)} %select_add_fusion.1), channel_id=1, source_target_pairs={{0,6},{1,7},{2,4},{3,5},{4,2},{5,3},{6,0},{7,1},{8,14},{9,15},{10,... | collective-permute-start | bytes 98312 | tf_op jit(solution)/shard_map/ppermute | solution.py:431
  60.8 0.0 collective-permute-start.20
  60.8 0.5 collective-permute-start.19
  61.3 1.4 %collective-permute-done.21 = f32[32,256]{1,0:T(8,128)S(1)} collective-permute-done((f32[32,256]{1,0:T(8,128)S(1)}, f32[32,256]{1,0:T(8,128)S(1)}, u32[]{:S(2)}, u32[]{:S(2)}) %collective-permute-start.21) | collective-permute-done | bytes 32800 | tf_op jit(solution)/shard_map/ppermute | solution.py:431
  62.7 1.7 %collective-permute-done.20 = f32[32,256]{1,0:T(8,128)S(1)} collective-permute-done((f32[32,256]{1,0:T(8,128)S(1)}, f32[32,256]{1,0:T(8,128)S(1)}, u32[]{:S(2)}, u32[]{:S(2)}) %collective-permute-start.20) | collective-permute-done | bytes 32800 | tf_op jit(solution)/shard_map/ppermute | solution.py:431
  64.5 2.0 %collective-permute-start.24 = (f32[32,256]{1,0:T(8,128)S(1)}, f32[32,256]{1,0:T(8,128)S(1)}, u32[]{:S(2)}, u32[]{:S(2)}) collective-permute-start(f32[32,256]{1,0:T(8,128)S(1)} %add_add_fusion.3), channel_id=1, source_target_pairs={{0,24},{1,25},{2,26},{3,27},{4,28},{5,29},{6,30},{7,31},{8,16},{9,... | collective-permute-start | bytes 98312 | tf_op jit(solution)/shard_map/ppermute | solution.py:431
  66.5 2.2 %collective-permute-start.22 = (f32[32,256]{1,0:T(8,128)S(1)}, f32[32,256]{1,0:T(8,128)S(1)}, u32[]{:S(2)}, u32[]{:S(2)}) collective-permute-start(f32[32,256]{1,0:T(8,128)S(1)} %add_add_fusion.3), channel_id=1, source_target_pairs={{0,9},{1,8},{2,11},{3,10},{4,13},{5,12},{6,15},{7,14},{8,1},{9,0},... | collective-permute-start | bytes 98312 | tf_op jit(solution)/shard_map/ppermute | solution.py:431
  68.6 1.7 %collective-permute-done.24 = f32[32,256]{1,0:T(8,128)S(1)} collective-permute-done((f32[32,256]{1,0:T(8,128)S(1)}, f32[32,256]{1,0:T(8,128)S(1)}, u32[]{:S(2)}, u32[]{:S(2)}) %collective-permute-start.24) | collective-permute-done | bytes 32800 | tf_op jit(solution)/shard_map/ppermute | solution.py:431
  70.3 0.7 collective-permute-done.23
  71.0 0.5 collective-permute-done.22
  71.6 0.2 collective-permute-start.25
  71.7 0.4 next_gram.1
  72.2 0.7 collective-permute-done.25
  72.9 3.6 %second_solve.1 = (bf16[64,2,8,128]{3,2,1,0:T(8,128)(2,1)}, f32[2,64,192]{2,1,0:T(8,128)}, f32[2,64,64]{2,1,0:T(8,128)}) custom-call(f32[64,256]{1,0:T(8,128)S(1)} %pad_maximum_fusion.5.cross, bf16[192,192]{1,0:T(8,128)(2,1)S(1)} %get-tuple-element.71.own_high, bf16[192,192]{1,0:T(8,128)(2,1)S(1)} %get-tuple-element.72.own_low, ...), custom_call_target="tpu_custom_call" | custom-call | bytes 1982464 | tf_op jit(solution)/shard_map/second_solve/pallas_call | solution.py:462
  (38 shorter events, 0.4 us)
Async XLA Ops:
  0.6 1.0 %slice-start = ((bf16[3,64,2,8,128]{4,3,2,1,0:T(8,128)(2,1)}), bf16[1,64,2,8,128]{4,3,2,1,0:T(8,128)(2,1)S(1)}, s32[]{:S(2)}) async-start(bf16[3,64,2,8,128]{4,3,2,1,0:T(8,128)(2,1)} %param.3), calls=%async_computation | async-start | bytes 524288 | tf_op jit(solution)/shard_map/slice | solution.py:503
  1.7 6.5 %copy-start = (s32[2,8,128]{2,1,0:T(8,128)S(1)}, s32[2,8,128]{2,1,0:T(8,128)}, u32[]{:S(2)}) copy-start(s32[2,8,128]{2,1,0:T(8,128)} %param.4) | copy-start | bytes 24580
  1.8 9.7 %collective-permute-start = (bf16[64,256]{1,0:T(8,128)(2,1)S(1)}, bf16[64,256]{1,0:T(8,128)(2,1)S(1)}, u32[]{:S(2)}, u32[]{:S(2)}) collective-permute-start(bf16[64,256]{1,0:T(8,128)(2,1)S(1)} %get-tuple-element.41), channel_id=1, source_target_pairs={{4,8},{8,4},{12,16},{16,12},{20,24},{24,20},{5,9},{9,5},{13,17},{1... | collective-permute-start | bytes 98312 | tf_op jit(solution)/shard_map/ppermute | solution.py:63
  2.4 5.9 %copy-start.1 = (f32[8,27]{1,0:T(8,128)S(1)}, f32[8,27]{1,0:T(8,128)}, u32[]{:S(2)}) copy-start(f32[8,27]{1,0:T(8,128)} %table.1) | copy-start | bytes 2596
  2.5 8.1 %copy-start.2 = (bf16[3,64,2,8,128]{4,3,2,1,0:T(8,128)(2,1)S(1)}, bf16[3,64,2,8,128]{4,3,2,1,0:T(8,128)(2,1)}, u32[]{:S(2)}) copy-start(bf16[3,64,2,8,128]{4,3,2,1,0:T(8,128)(2,1)} %param.3) | copy-start | bytes 2359300
  2.5 9.0 %collective-permute-start.1 = (bf16[64,1024]{1,0:T(8,128)(2,1)S(1)}, bf16[64,1024]{1,0:T(8,128)(2,1)S(1)}, u32[]{:S(2)}, u32[]{:S(2)}) collective-permute-start(bf16[64,1024]{1,0:T(8,128)(2,1)S(1)} %slice_select_fusion), channel_id=1, source_target_pairs={{0,4},{4,0},{8,12},{12,8},{16,20},{20,16},{24,28},{28,24},{1,5},{5... | collective-permute-start | bytes 393224 | tf_op jit(solution)/shard_map/ppermute | solution.py:60
  9.7 3.6 %collective-permute-start.2 = (bf16[64,768]{1,0:T(8,128)(2,1)S(1)}, bf16[64,768]{1,0:T(8,128)(2,1)S(1)}, u32[]{:S(2)}, u32[]{:S(2)}) collective-permute-start(bf16[64,768]{1,0:T(8,128)(2,1)S(1)} %get-tuple-element.56), channel_id=1, source_target_pairs={{4,8},{8,4},{12,16},{16,12},{20,24},{24,20},{5,9},{9,5},{13,17},{1... | collective-permute-start | bytes 294920 | tf_op jit(solution)/shard_map/ppermute | solution.py:65
  11.6 4.4 %collective-permute-start.4 = (bf16[64,512]{1,0:T(8,128)(2,1)S(1)}, bf16[64,512]{1,0:T(8,128)(2,1)S(1)}, u32[]{:S(2)}, u32[]{:S(2)}) collective-permute-start(bf16[64,512]{1,0:T(8,128)(2,1)S(1)} %get-tuple-element.101), channel_id=1, source_target_pairs={{1,2},{2,1},{0,3},{3,0},{5,6},{6,5},{4,7},{7,4},{9,10},{10,9},{8,1... | collective-permute-start | bytes 196616 | tf_op jit(solution)/shard_map/ppermute | solution.py:87
  12.1 3.9 %collective-permute-start.3 = (bf16[64,512]{1,0:T(8,128)(2,1)S(1)}, bf16[64,512]{1,0:T(8,128)(2,1)S(1)}, u32[]{:S(2)}, u32[]{:S(2)}) collective-permute-start(bf16[64,512]{1,0:T(8,128)(2,1)S(1)} %get-tuple-element.102), channel_id=1, source_target_pairs={{0,1},{1,0},{2,3},{3,2},{4,5},{5,4},{6,7},{7,6},{8,9},{9,8},{10,11... | collective-permute-start | bytes 196616 | tf_op jit(solution)/shard_map/ppermute | solution.py:86
  17.2 1.3 %collective-permute-start.5 = (f32[136,128]{1,0:T(8,128)S(1)}, f32[136,128]{1,0:T(8,128)S(1)}, u32[]{:S(2)}, u32[]{:S(2)}) collective-permute-start(f32[136,128]{1,0:T(8,128)S(1)} %slice_select_fusion.2), channel_id=1, source_target_pairs={{0,1},{1,0},{2,3},{3,2},{4,5},{5,4},{6,7},{7,6},{8,9},{9,8},{10,11... | collective-permute-start | bytes 208904 | tf_op jit(solution)/shard_map/ppermute | solution.py:431
  18.5 7.2 %collective-permute-start.8 = (f32[136,128]{1,0:T(8,128)S(1)}, f32[136,128]{1,0:T(8,128)S(1)}, u32[]{:S(2)}, u32[]{:S(2)}) collective-permute-start(f32[136,128]{1,0:T(8,128)S(1)} %select_add_fusion), channel_id=1, source_target_pairs={{0,6},{1,7},{2,4},{3,5},{4,2},{5,3},{6,0},{7,1},{8,14},{9,15},{10,... | collective-permute-start | bytes 208904 | tf_op jit(solution)/shard_map/ppermute | solution.py:431
  23.2 4.4 %collective-permute-start.7 = (f32[136,128]{1,0:T(8,128)S(1)}, f32[136,128]{1,0:T(8,128)S(1)}, u32[]{:S(2)}, u32[]{:S(2)}) collective-permute-start(f32[136,128]{1,0:T(8,128)S(1)} %select_add_fusion), channel_id=1, source_target_pairs={{0,5},{1,4},{2,7},{3,6},{4,1},{5,0},{6,3},{7,2},{8,13},{9,12},{10,... | collective-permute-start | bytes 208904 | tf_op jit(solution)/shard_map/ppermute | solution.py:431
  23.2 4.4 %collective-permute-start.6 = (f32[136,128]{1,0:T(8,128)S(1)}, f32[136,128]{1,0:T(8,128)S(1)}, u32[]{:S(2)}, u32[]{:S(2)}) collective-permute-start(f32[136,128]{1,0:T(8,128)S(1)} %select_add_fusion), channel_id=1, source_target_pairs={{0,3},{1,2},{2,1},{3,0},{4,7},{5,6},{6,5},{7,4},{8,11},{9,10},{10,... | collective-permute-start | bytes 208904 | tf_op jit(solution)/shard_map/ppermute | solution.py:431
  27.6 6.8 %collective-permute-start.11 = (f32[136,128]{1,0:T(8,128)S(1)}, f32[136,128]{1,0:T(8,128)S(1)}, u32[]{:S(2)}, u32[]{:S(2)}) collective-permute-start(f32[136,128]{1,0:T(8,128)S(1)} %add_add_fusion.1), channel_id=1, source_target_pairs={{0,24},{1,25},{2,26},{3,27},{4,28},{5,29},{6,30},{7,31},{8,16},{9,... | collective-permute-start | bytes 208904 | tf_op jit(solution)/shard_map/ppermute | solution.py:431
  30.5 6.3 %collective-permute-start.10 = (f32[136,128]{1,0:T(8,128)S(1)}, f32[136,128]{1,0:T(8,128)S(1)}, u32[]{:S(2)}, u32[]{:S(2)}) collective-permute-start(f32[136,128]{1,0:T(8,128)S(1)} %add_add_fusion.1), channel_id=1, source_target_pairs={{0,17},{1,16},{2,19},{3,18},{4,21},{5,20},{6,23},{7,22},{8,25},{9,... | collective-permute-start | bytes 208904 | tf_op jit(solution)/shard_map/ppermute | solution.py:431
  30.5 6.3 %collective-permute-start.9 = (f32[136,128]{1,0:T(8,128)S(1)}, f32[136,128]{1,0:T(8,128)S(1)}, u32[]{:S(2)}, u32[]{:S(2)}) collective-permute-start(f32[136,128]{1,0:T(8,128)S(1)} %add_add_fusion.1), channel_id=1, source_target_pairs={{0,9},{1,8},{2,11},{3,10},{4,13},{5,12},{6,15},{7,14},{8,1},{9,0},... | collective-permute-start | bytes 208904 | tf_op jit(solution)/shard_map/ppermute | solution.py:431
  36.9 1.4 %collective-permute-start.12 = (f32[136,128]{1,0:T(8,128)S(1)}, f32[136,128]{1,0:T(8,128)S(1)}, u32[]{:S(2)}, u32[]{:S(2)}) collective-permute-start(f32[136,128]{1,0:T(8,128)S(1)} %add_add_fusion), channel_id=1, source_target_pairs={{0,1},{1,0},{2,3},{3,2},{4,5},{5,4},{6,7},{7,6},{8,9},{9,8},{10,11... | collective-permute-start | bytes 208904 | tf_op jit(solution)/shard_map/ppermute | solution.py:431
  41.5 5.2 %collective-permute-start.13 = (bf16[64,256]{1,0:T(8,128)(2,1)S(1)}, bf16[64,256]{1,0:T(8,128)(2,1)S(1)}, u32[]{:S(2)}, u32[]{:S(2)}) collective-permute-start(bf16[64,256]{1,0:T(8,128)(2,1)S(1)} %get-tuple-element.61), channel_id=1, source_target_pairs={{4,8},{8,4},{12,16},{16,12},{20,24},{24,20},{5,9},{9,5},{13,17},{1... | collective-permute-start | bytes 98312 | tf_op jit(solution)/shard_map/ppermute | solution.py:63
  42.1 9.2 %collective-permute-start.14 = (bf16[64,1024]{1,0:T(8,128)(2,1)S(1)}, bf16[64,1024]{1,0:T(8,128)(2,1)S(1)}, u32[]{:S(2)}, u32[]{:S(2)}) collective-permute-start(bf16[64,1024]{1,0:T(8,128)(2,1)S(1)} %slice_select_fusion.1), channel_id=1, source_target_pairs={{0,4},{4,0},{8,12},{12,8},{16,20},{20,16},{24,28},{28,24},{1,5},{5... | collective-permute-start | bytes 393224 | tf_op jit(solution)/shard_map/ppermute | solution.py:60
  45.3 7.3 %collective-permute-start.15 = (bf16[64,768]{1,0:T(8,128)(2,1)S(1)}, bf16[64,768]{1,0:T(8,128)(2,1)S(1)}, u32[]{:S(2)}, u32[]{:S(2)}) collective-permute-start(bf16[64,768]{1,0:T(8,128)(2,1)S(1)} %get-tuple-element.65), channel_id=1, source_target_pairs={{4,8},{8,4},{12,16},{16,12},{20,24},{24,20},{5,9},{9,5},{13,17},{1... | collective-permute-start | bytes 294920 | tf_op jit(solution)/shard_map/ppermute | solution.py:65
  51.5 4.0 %collective-permute-start.17 = (bf16[64,512]{1,0:T(8,128)(2,1)S(1)}, bf16[64,512]{1,0:T(8,128)(2,1)S(1)}, u32[]{:S(2)}, u32[]{:S(2)}) collective-permute-start(bf16[64,512]{1,0:T(8,128)(2,1)S(1)} %get-tuple-element.95), channel_id=1, source_target_pairs={{1,2},{2,1},{0,3},{3,0},{5,6},{6,5},{4,7},{7,4},{9,10},{10,9},{8,1... | collective-permute-start | bytes 196616 | tf_op jit(solution)/shard_map/ppermute | solution.py:87
  51.6 3.9 %collective-permute-start.16 = (bf16[64,512]{1,0:T(8,128)(2,1)S(1)}, bf16[64,512]{1,0:T(8,128)(2,1)S(1)}, u32[]{:S(2)}, u32[]{:S(2)}) collective-permute-start(bf16[64,512]{1,0:T(8,128)(2,1)S(1)} %get-tuple-element.96), channel_id=1, source_target_pairs={{0,1},{1,0},{2,3},{3,2},{4,5},{5,4},{6,7},{7,6},{8,9},{9,8},{10,11... | collective-permute-start | bytes 196616 | tf_op jit(solution)/shard_map/ppermute | solution.py:86
  56.6 1.3 %collective-permute-start.18 = (f32[32,256]{1,0:T(8,128)S(1)}, f32[32,256]{1,0:T(8,128)S(1)}, u32[]{:S(2)}, u32[]{:S(2)}) collective-permute-start(f32[32,256]{1,0:T(8,128)S(1)} %slice_select_fusion.3), channel_id=1, source_target_pairs={{0,1},{1,0},{2,3},{3,2},{4,5},{5,4},{6,7},{7,6},{8,9},{9,8},{10,11... | collective-permute-start | bytes 98312 | tf_op jit(solution)/shard_map/ppermute | solution.py:431
  57.9 4.8 %collective-permute-start.21 = (f32[32,256]{1,0:T(8,128)S(1)}, f32[32,256]{1,0:T(8,128)S(1)}, u32[]{:S(2)}, u32[]{:S(2)}) collective-permute-start(f32[32,256]{1,0:T(8,128)S(1)} %select_add_fusion.1), channel_id=1, source_target_pairs={{0,6},{1,7},{2,4},{3,5},{4,2},{5,3},{6,0},{7,1},{8,14},{9,15},{10,... | collective-permute-start | bytes 98312 | tf_op jit(solution)/shard_map/ppermute | solution.py:431
  60.8 3.6 %collective-permute-start.20 = (f32[32,256]{1,0:T(8,128)S(1)}, f32[32,256]{1,0:T(8,128)S(1)}, u32[]{:S(2)}, u32[]{:S(2)}) collective-permute-start(f32[32,256]{1,0:T(8,128)S(1)} %select_add_fusion.1), channel_id=1, source_target_pairs={{0,5},{1,4},{2,7},{3,6},{4,1},{5,0},{6,3},{7,2},{8,13},{9,12},{10,... | collective-permute-start | bytes 98312 | tf_op jit(solution)/shard_map/ppermute | solution.py:431
  60.8 3.6 %collective-permute-start.19 = (f32[32,256]{1,0:T(8,128)S(1)}, f32[32,256]{1,0:T(8,128)S(1)}, u32[]{:S(2)}, u32[]{:S(2)}) collective-permute-start(f32[32,256]{1,0:T(8,128)S(1)} %select_add_fusion.1), channel_id=1, source_target_pairs={{0,3},{1,2},{2,1},{3,0},{4,7},{5,6},{6,5},{7,4},{8,11},{9,10},{10,... | collective-permute-start | bytes 98312 | tf_op jit(solution)/shard_map/ppermute | solution.py:431
  64.5 5.9 %collective-permute-start.24 = (f32[32,256]{1,0:T(8,128)S(1)}, f32[32,256]{1,0:T(8,128)S(1)}, u32[]{:S(2)}, u32[]{:S(2)}) collective-permute-start(f32[32,256]{1,0:T(8,128)S(1)} %add_add_fusion.3), channel_id=1, source_target_pairs={{0,24},{1,25},{2,26},{3,27},{4,28},{5,29},{6,30},{7,31},{8,16},{9,... | collective-permute-start | bytes 98312 | tf_op jit(solution)/shard_map/ppermute | solution.py:431
  66.5 4.6 %collective-permute-start.23 = (f32[32,256]{1,0:T(8,128)S(1)}, f32[32,256]{1,0:T(8,128)S(1)}, u32[]{:S(2)}, u32[]{:S(2)}) collective-permute-start(f32[32,256]{1,0:T(8,128)S(1)} %add_add_fusion.3), channel_id=1, source_target_pairs={{0,17},{1,16},{2,19},{3,18},{4,21},{5,20},{6,23},{7,22},{8,25},{9,... | collective-permute-start | bytes 98312 | tf_op jit(solution)/shard_map/ppermute | solution.py:431
  66.5 5.1 %collective-permute-start.22 = (f32[32,256]{1,0:T(8,128)S(1)}, f32[32,256]{1,0:T(8,128)S(1)}, u32[]{:S(2)}, u32[]{:S(2)}) collective-permute-start(f32[32,256]{1,0:T(8,128)S(1)} %add_add_fusion.3), channel_id=1, source_target_pairs={{0,9},{1,8},{2,11},{3,10},{4,13},{5,12},{6,15},{7,14},{8,1},{9,0},... | collective-permute-start | bytes 98312 | tf_op jit(solution)/shard_map/ppermute | solution.py:431
  71.6 1.3 %collective-permute-start.25 = (f32[32,256]{1,0:T(8,128)S(1)}, f32[32,256]{1,0:T(8,128)S(1)}, u32[]{:S(2)}, u32[]{:S(2)}) collective-permute-start(f32[32,256]{1,0:T(8,128)S(1)} %add_add_fusion.2), channel_id=1, source_target_pairs={{0,1},{1,0},{2,3},{3,2},{4,5},{5,4},{6,7},{7,6},{8,9},{9,8},{10,11... | collective-permute-start | bytes 98312 | tf_op jit(solution)/shard_map/ppermute | solution.py:431

commit v19 on v17

--- a/solution.py
+++ b/solution.py
@@ -20,15 +20,17 @@
 def swaps(axis, near, far, closed):
     count = lax.axis_size(axis)
     me = lax.axis_index(axis)
-    odd = me % 2 == 1
     pairs = [(i, (i - 1 ^ 1) + 1) for i in range(1, count - 1)]
     if closed:
         pairs += [(0, count - 1), (count - 1, 0)]
     inner = lax.ppermute(near, axis, [(i, i ^ 1) for i in range(count)])
     outer = lax.ppermute(far, axis, pairs)
     if closed:
-        outer = jnp.where((me == 0) | (me == count - 1), 0, outer)
-    return jnp.where(odd, inner, outer), jnp.where(odd, outer, inner)
+        odd = me % 2 == 1
+        low, high = jnp.where(odd, inner, outer), jnp.where(odd, outer, inner)
+        return jnp.where(me == 0, 0, low), jnp.where(me == count - 1, 0, high)
+    even = me % 2 == 0
+    return jnp.where(even, outer, inner), jnp.where(even, inner, outer)
 
 
 def cut_kernel(start, block, part):
@@ -70,7 +72,7 @@
     ylo, yhi = swaps(
         "col", jnp.where(odd, downward, upward), jnp.where(odd, upward, downward), True
     )
-    return (xlo, xhi, ylo, yhi), meanwhile
+    return (xlo, xhi), (ylo, yhi), meanwhile
 
 
 def coefficients_kernel(table, cells, coef):
@@ -110,71 +112,108 @@
     )(table, cell_map.reshape(lines, depth))
 
 
-def stencil(coef, spans, columns, line, inner, write):
-    span_x, span_y, depth = spans
+def stencil(coef, spans, columns, lines, line, wanted, write):
+    depth = spans[2]
 
     def tile(step, carry):
         rows = pl.ds(pl.multiple_of(step * ROWS, ROWS), ROWS)
         held = {}
-        for y in range(span_y):
-            for x in range(span_x):
-                sums = [None, None, None]
-                for pair in range(9):
-                    x_there, y_there = x + pair // 3 - 1, y + pair % 3 - 1
-                    inside = 0 <= x_there < span_x and 0 <= y_there < span_y
-                    if inside != inner:
-                        continue
-                    if (x_there, y_there) not in held:
-                        held[x_there, y_there] = line(rows, x_there, y_there)
-                    for dz in range(3):
-                        at = x * span_y + y
-                        term = coef[3 * pair + dz, at : at + 1, :] * held[x_there, y_there]
-                        sums[dz] = term if sums[dz] is None else sums[dz] + term
-                total = None
-                if sums[0] is not None:
-                    total = pltpu.roll(sums[0], 1, 1) + pltpu.roll(sums[2], depth - 1, 1)
-                    total = sums[1] + total
-                write(rows, x, y, total)
+        for x, y in lines:
+            at = x * spans[1] + y
+            sums = [None, None, None]
+            for pair in range(9):
+                there = x + pair // 3 - 1, y + pair % 3 - 1
+                if not wanted(there[1]):
+                    continue
+                if there not in held:
+                    held[there] = line(rows, *there)
+                for dz in range(3):
+                    term = coef[3 * pair + dz, at : at + 1, :] * held[there]
+                    sums[dz] = term if sums[dz] is None else sums[dz] + term
+            total = pltpu.roll(sums[0], 1, 1) + pltpu.roll(sums[2], depth - 1, 1)
+            write(rows, x, y, sums[1] + total)
         return carry
 
     lax.fori_loop(0, columns // ROWS, tile, 0)
 
 
-def inner_image_kernel(spans, coef, fields, partial):
+def middle_of(spans, x):
     _, span_y, depth = spans
-    columns = partial.shape[0]
-    block = fields.at[fields.shape[0] - columns :]
-
-    def here(x, y):
-        return pl.ds((x * span_y + y) * depth, depth)
+    inner = (span_y - 2) * depth
+    return pl.ds((x * span_y + 1) * depth, inner), pl.ds(x * inner, inner)
+
+
+def ends_of(spans, x, last):
+    _, span_y, depth = spans
+    return (
+        pl.ds((x * span_y + (span_y - 1) * last) * depth, depth),
+        pl.ds((2 * x + last) * depth, depth),
+    )
+
+
+def products(parts, fields):
+    total = 0
+    for w, cells in parts:
+        rows = [dot(w, ref[first:, cells], NT) for ref, first in fields]
+        total = total + jnp.concatenate(rows + [dot(w, w, NT)], axis=1)
+    return total
+
+
+def middle_image_kernel(spans, first, coef, stack, block, xlo, xhi, middle, partial, cross):
+    span_x, span_y, depth = spans
+
+    def line(rows, x, y):
+        ref, at = block, x * span_y + y
+        if x < 0 or x >= span_x:
+            ref, at = (xlo if x < 0 else xhi), y
+        return ref[rows, at * depth : (at + 1) * depth].astype(jnp.float32)
 
     def write(rows, x, y, total):
-        partial[rows, here(x, y)] = total
+        if 0 < y < span_y - 1:
+            at = x * (span_y - 2) + y - 1
+            middle[rows, at * depth : (at + 1) * depth] = total.astype(jnp.bfloat16)
+        else:
+            partial[rows, ends_of(spans, x, int(y > 0))[1]] = total
+
+    lines = [(x, y) for y in range(span_y) for x in range(span_x)]
+    stencil(coef, spans, block.shape[0], lines, line, lambda y: 0 <= y < span_y, write)
+    parts = [
+        (middle[:, own], there) for there, own in (middle_of(spans, x) for x in range(span_x))
+    ]
+    cross[...] = products(parts, [(stack, first)] + ([(block, 0)] if first else []))
+
+
+def end_lines(spans, coef, stack, block, partial, cross, ylo, yhi, ends):
+    span_x, span_y, depth = spans
 
     def line(rows, x, y):
-        return block[rows, here(x, y)].astype(jnp.float32)
-
-    stencil(coef, spans, columns, line, True, write)
-
-
-def complete(image, partial, coef, spans, xlo, xhi, ylo, yhi):
-    span_x, span_y, depth = spans
-
-    def line(rows, x, y):
-        if y < 0:
-            ref, at = ylo, x + 1
-        elif y >= span_y:
-            ref, at = yhi, x + 1
-        else:
-            ref, at = (xlo, y) if x < 0 else (xhi, y)
-        return ref[rows, at * depth : (at + 1) * depth].astype(jnp.float32)
+        return (ylo if y < 0 else yhi)[rows, (x + 1) * depth : (x + 2) * depth].astype(jnp.float32)
 
     def write(rows, x, y, total):
-        there = pl.ds((x * span_y + y) * depth, depth)
-        known = partial[rows, there]
-        image[rows, there] = (known if total is None else known + total).astype(jnp.bfloat16)
-
-    stencil(coef, spans, image.shape[0], line, False, write)
+        own = ends_of(spans, x, int(y > 0))[1]
+        ends[rows, own] = (partial[rows, own] + total).astype(jnp.bfloat16)
+
+    lines = [(x, y) for y in (0, span_y - 1) for x in range(span_x)]
+    stencil(coef, spans, ends.shape[0], lines, line, lambda y: not 0 <= y < span_y, write)
+    parts = []
+    for x in range(span_x):
+        for last in range(2):
+            there, own = ends_of(spans, x, last)
+            parts.append((ends[:, own], there))
+    fields = [(stack, 0)] if block is None else [(stack, ends.shape[0]), (block, 0)]
+    return cross[...] + products(parts, fields)
+
+
+def subtracted(spans, middle, ends, moved, block):
+    columns = ends.shape[0]
+    moved = moved[:columns] + moved[columns:]
+    pieces = []
+    for x in range(spans[0]):
+        pieces.append((middle, *middle_of(spans, x)))
+        pieces += [(ends, *ends_of(spans, x, last)) for last in range(2)]
+    for ref, there, own in pieces:
+        less = moved[:, there.start : there.start + there.size]
+        block[:, there] = (ref[:, own].astype(jnp.float32) - less).astype(jnp.bfloat16)
 
 
 def places(size):
@@ -208,13 +247,13 @@
 
 
 def first_image_kernel(
-    spans, coef, stack, sides, pair, last, diagonal, partial, xlo, xhi, ylo, yhi, image, cross
+    spans, coef, stack, sides, pair, last, diagonal, partial, known, ylo, yhi, ends, cross
 ):
-    columns = image.shape[0]
-    complete(image, partial, coef, spans, xlo, xhi, ylo, yhi)
-    w = image[...]
-    first = dot(stack[...], w, NT).T
-    corner, own_diagonal = two_in_one(last[...], dot(w, w, NT))
+    columns = ends.shape[0]
+    fields = stack.shape[0]
+    sums = end_lines(spans, coef, stack, None, partial, known, ylo, yhi, ends)
+    first, square = sums[:, :fields], sums[:, fields:]
+    corner, own_diagonal = two_in_one(last[...], square)
     rows = [
         first[:, : 2 * columns],
         jnp.concatenate([first[:, 2 * columns :], sides[0]], axis=1),
@@ -228,6 +267,10 @@
     cross[4 * columns :] = rest
 
 
+def second_image_kernel(spans, coef, stack, block, partial, known, ylo, yhi, ends, cross):
+    cross[...] = end_lines(spans, coef, stack, block, partial, known, ylo, yhi, ends)
+
+
 def opened(cross, columns, scale):
     parts = [cross[i * columns : (i + 1) * columns] * scale for i in range(4)]
     diagonals = cross[4 * columns : 4 * columns + 1] * scale
@@ -238,16 +281,6 @@
     gram = [[one, side[0], side[1]], [side[0].T, two, side[2]], [side[1].T, side[2].T, three]]
     gram = jnp.concatenate([jnp.concatenate(row, axis=1) for row in gram], axis=0)
     return first, square, gram
-
-
-def second_image_kernel(spans, coef, stack, block, partial, xlo, xhi, ylo, yhi, image, cross):
-    columns = image.shape[0]
-    fields = stack.shape[0]
-    complete(image, partial, coef, spans, xlo, xhi, ylo, yhi)
-    w = image[...]
-    cross[:, : fields - columns] = dot(stack[columns:], w, NT).T
-    cross[:, fields - columns : fields] = dot(block[...], w, NT).T
-    cross[:, fields:] = dot(w, w, NT)
 
 
 def split(values):
@@ -346,14 +379,15 @@
     return used, first + second, rest, square, sizes
 
 
-def first_solve_kernel(scale, cross, stack, image, block, proj, low, rest, square, inverse):
-    columns = image.shape[0]
+def first_solve_kernel(
+    scale, spans, cross, stack, middle, ends, block, proj, low, rest, square, inverse
+):
+    columns = ends.shape[0]
     first, own_square, gram = opened(cross, columns, scale)
     used, proj[...], rest[...], square_here, sizes = project(first, own_square, split(gram))
     square[...] = square_here
     moved = dot(jnp.concatenate(used, axis=0), stack[...])
-    w = image[...].astype(jnp.float32) - moved[:columns] - moved[columns:]
-    block[...] = w.astype(jnp.bfloat16)
+    subtracted(spans, middle, ends, moved, block)
     upper, inverse_here = factor(square_here, *sizes)
     low[...] = upper.T
     inverse_here = inverse_here.astype(jnp.bfloat16)
@@ -378,9 +412,10 @@
 
 
 def second_solve_kernel(
-    scale, cross, own_high, own_low, stack, last, image, proj_in, low_in, result, proj, low, block
+    scale, cross, own_high, own_low, stack, last, middle, ends, proj_in, low_in, result, proj, low,
+    block,
 ):
-    columns = image.shape[0]
+    columns = ends.shape[0]
     kept = stack.shape[0] - columns
     fields = stack.shape[0]
     sums = cross[...] * scale
@@ -389,14 +424,13 @@
     )
     proj[0] = proj_in[...]
     low[0] = low_in[...]
+    _, span_x, span_y, depth = result.shape
     both = jnp.concatenate(used, axis=0)
     moved = dot(both[:, :kept], stack[columns:]) + dot(both[:, kept:], last[...])
-    w = image[...].astype(jnp.float32) - moved[:columns] - moved[columns:]
-    block[...] = w.astype(jnp.bfloat16)
+    subtracted((span_x, span_y, depth), middle, ends, moved, block)
     upper, inverse = factor(square, *sizes)
     low[1] = upper.T
     inverse = inverse.astype(jnp.bfloat16)
-    _, span_x, span_y, depth = result.shape
     plane = span_y * depth
     for x in range(span_x):
         part = dot(inverse, block[:, x * plane : (x + 1) * plane])
@@ -425,7 +459,7 @@
     while bit < count:
         if 2 * bit < count:
             one, two, both = (partner(part, mask) for mask in (bit + 1, 2 * bit + 1, 3 * bit))
-            part = (part + both) + (two + one)
+            part = (part + one) + (both + two)
             bit *= 4
         else:
             part = part + partner(part, bit + 1)
@@ -469,30 +503,34 @@
         flops=2 * fields * fields * cells,
     )
 
-    def inner_image(block):
+    end_cells = 2 * span_x * depth
+
+    def middle_image(first, stack, block, planes):
         return call(
-            functools.partial(inner_image_kernel, spans),
-            "inner_image",
-            [((columns, cells), f32)],
-            coef, block,
+            functools.partial(middle_image_kernel, spans, first),
+            "middle_image",
+            [((columns, cells - end_cells), bf16), ((columns, end_cells), f32),
+             ((columns, fields + columns), f32)],
+            coef, stack, block, *planes,
             flops=2 * 27 * columns * cells,
-        )[0]
+        )
 
     last = basis[blocks - 1].reshape(columns, cells)
-    around, (stack, own, partial) = neighbours(last, *spans, (stack, own, inner_image(last)))
-    image, cross = call(
+    planes, lines, (coef, stack, own) = neighbours(last, *spans, (coef, stack, own))
+    middle, partial, known = middle_image(0, stack, last, planes)
+    ends, cross = call(
         functools.partial(first_image_kernel, spans),
         "first_image",
-        [((columns, cells), bf16), ((4 * columns + 16, 2 * columns), f32)],
-        coef, stack, *own, partial, *around,
+        [((columns, end_cells), bf16), ((4 * columns + 16, 2 * columns), f32)],
+        coef, stack, *own, partial, known, *lines,
     )
     cross = whole_sum(cross)
     block, proj, low, rest, square, inverse = call(
-        functools.partial(first_solve_kernel, scale),
+        functools.partial(first_solve_kernel, scale, spans),
         "first_solve",
         [((columns, cells), bf16), ((columns, fields), f32), ((columns, columns), f32),
          ((columns, fields), f32), ((columns, columns), f32), ((columns, columns), bf16)],
-        cross, stack, image,
+        cross, stack, middle, ends,
     )
     own = call(
         functools.partial(next_gram_kernel, scale),
@@ -500,18 +538,19 @@
         [((fields, fields), bf16)] * 2,
         cross, rest, square, inverse,
     )
-    around, _ = neighbours(block, *spans)
-    image, cross = call(
+    planes, lines, _ = neighbours(block, *spans)
+    middle, partial, known = middle_image(columns, stack, block, planes)
+    ends, cross = call(
         functools.partial(second_image_kernel, spans),
         "second_image",
-        [((columns, cells), bf16), ((columns, fields + columns), f32)],
-        coef, stack, block, inner_image(block), *around,
+        [((columns, end_cells), bf16), ((columns, fields + columns), f32)],
+        coef, stack, block, partial, known, *lines,
     )
     block, proj, low = call(
         functools.partial(second_solve_kernel, scale),
         "second_solve",
         [((columns, *spans), bf16), ((2, columns, fields), f32), ((2, columns, columns), f32)],
-        whole_sum(cross), *own, stack, block, image, proj, low,
+        whole_sum(cross), *own, stack, block, middle, ends, proj, low,
         scratch=[pltpu.VMEM((columns, cells), bf16)],
     )
     return block, jnp.swapaxes(proj, 1, 2), low

time: 76.1 us -> 72.7 us (0.955)
  waiting for transfers between devices: 31.7 us -> 27.1 us
    ppermute x16, waiting for transfers between devices: 22.6 us -> 19.8 us  [partner(): return lax.ppermute(part, axes, [(i, i ^ mask) for i in range(count)])]
    ppermute x4, waiting for transfers between devices: 4.9 us -> 2.34 us  [swaps(): outer = lax.ppermute(far, axis, pairs)]
  transfers between devices with their start and end apart: 24 -> 24, of which waited for: 15 -> 17; matrix products, arithmetic and copies ran while one was open for 0% -> 1% of each run, Pallas kernels for 4% -> 6%
where the time goes in v19:
time: 72.7 us; the launch traced here: 72.4 us
  starting transfers between devices  29.2 us (40%)
  waiting for transfers between devices  27.1 us (37%)
  Pallas kernels  12.7 us (17%)
  local copies, waits for them, and re-layouts  2.13 us (3%)
  between operations  0.98 us (1%)
    ppermute x16, starting transfers between devices, partner(): return lax.ppermute(part, axes, [(i, i ^ mask) for i in range(count)])  21.3 us
    ppermute x16, waiting for transfers between devices, partner(): return lax.ppermute(part, axes, [(i, i ^ mask) for i in range(count)])  19.8 us
    pallas_call x8, Pallas kernels, call(): pl.pallas_call(kernel, out_shape=[jax.ShapeDtypeStruct(shape, dtype) for...  12 us
    ppermute x4, starting transfers between devices, swaps(): inner = lax.ppermute(near, axis, [(i, i ^ 1) for i in range(count)])  6.07 us
    ppermute x4, waiting for transfers between devices, swaps(): inner = lax.ppermute(near, axis, [(i, i ^ 1) for i in range(count)])  4.93 us
    ppermute x4, waiting for transfers between devices, swaps(): outer = lax.ppermute(far, axis, pairs)  2.34 us
    ppermute x4, starting transfers between devices, swaps(): outer = lax.ppermute(far, axis, pairs)  1.8 us
  transfers between devices with their start and end apart: 24, of which 17 were waited for; matrix products, arithmetic and copies ran while one was open for 1% of the time, Pallas kernels for 6%

profile of v19, /device:TPU:0, one launch (start us, length us, event | category | flops | bytes accessed | tf_op | source)
XLA Modules:
  0.0 72.4 jit_solution(5212537391791514490)
XLA Ops:
  0.6 0.0 slice-start
  0.6 0.9 %slice-done = bf16[1,64,2,8,128]{4,3,2,1,0:T(8,128)(2,1)S(1)} async-done(((bf16[3,64,2,8,128]{4,3,2,1,0:T(8,128)(2,1)}), bf16[1,64,2,8,128]{4,3,2,1,0:T(8,128)(2,1)S(1)}, s32[]{:S(2)}) %slice-start) | async-done | bytes 262168 | tf_op jit(solution)/shard_map/slice | solution.py:518
  1.6 0.1 reshape_squeeze.3.block
  1.7 3.0 %collective-permute-start.1 = (bf16[64,1024]{1,0:T(8,128)(2,1)S(1)}, bf16[64,1024]{1,0:T(8,128)(2,1)S(1)}, u32[]{:S(2)}, u32[]{:S(2)}) collective-permute-start(bf16[64,1024]{1,0:T(8,128)(2,1)S(1)} %slice_select_fusion), channel_id=1, source_target_pairs={{0,4},{4,0},{8,12},{12,8},{16,20},{20,16},{24,28},{28,24},{1,5},{5... | collective-permute-start | bytes 393224 | tf_op jit(solution)/shard_map/ppermute | solution.py:26
  4.8 0.7 collective-permute-start
  5.5 0.3 reshape.18.stack
  5.8 0.0 copy-start
  5.8 0.6 stack_gram.1
  6.4 0.0 copy-start.1
  6.4 0.1 copy-done
  6.5 0.6 copy-done.1
  7.1 0.8 %coefficients.1.coef = f32[27,16,128]{2,1,0:T(8,128)S(1)} custom-call(f32[8,27]{1,0:T(8,128)S(1)} %copy-done.1, s32[16,128]{1,0:T(8,128)S(1)} %bitcast.7), custom_call_target="tpu_custom_call" | custom-call | tf_op jit(solution)/shard_map/coefficients/pallas_call | solution.py:102
  7.9 0.4 collective-permute-done.1
  8.2 0.0 collective-permute-done
  8.3 0.4 collective-permute-start.3
  8.7 1.5 %collective-permute-start.2 = (bf16[64,512]{1,0:T(8,128)(2,1)S(1)}, bf16[64,512]{1,0:T(8,128)(2,1)S(1)}, u32[]{:S(2)}, u32[]{:S(2)}) collective-permute-start(bf16[64,512]{1,0:T(8,128)(2,1)S(1)} %get-tuple-element.98), channel_id=1, source_target_pairs={{0,1},{1,0},{2,3},{3,2},{4,5},{5,4},{6,7},{7,6},{8,9},{9,8},{10,11... | collective-permute-start | bytes 196616 | tf_op jit(solution)/shard_map/ppermute | solution.py:26
  10.3 1.3 %middle_image.2 = (bf16[64,1536]{1,0:T(8,128)(2,1)S(1)}, f32[64,512]{1,0:T(8,128)S(1)}, f32[64,256]{1,0:T(8,128)S(1)}) custom-call(f32[27,16,128]{2,1,0:T(8,128)S(1)} %coefficients.1.coef, bf16[192,2048]{1,0:T(8,128)(2,1)S(1)} %reshape.18.stack, bf16[64,2048]{1,0:T(8,128)(2,1)S(1)} %reshape_squeeze.3.block, bf16[64,1024]{1,0:T(8,128)(2,1)S(1)} %get-tuple-element.48.xlo, ...), custom_call_target="tpu_custom_call" | custom-call | flops 7077888 | bytes 1925120 | tf_op jit(solution)/shard_map/middle_image/pallas_call | solution.py:474
  11.6 0.8 %collective-permute-done.3 = bf16[64,512]{1,0:T(8,128)(2,1)S(1)} collective-permute-done((bf16[64,512]{1,0:T(8,128)(2,1)S(1)}, bf16[64,512]{1,0:T(8,128)(2,1)S(1)}, u32[]{:S(2)}, u32[]{:S(2)}) %collective-permute-start.3) | collective-permute-done | bytes 65568 | tf_op jit(solution)/shard_map/ppermute | solution.py:27
  12.5 0.0 collective-permute-done.2
  12.5 0.9 %first_image.1 = (bf16[64,512]{1,0:T(8,128)(2,1)S(1)}, f32[272,128]{1,0:T(8,128)S(1)}) custom-call(f32[27,16,128]{2,1,0:T(8,128)S(1)} %coefficients.1.coef, bf16[192,2048]{1,0:T(8,128)(2,1)S(1)} %reshape.18.stack, f32[3,64,64]{2,1,0:T(8,128)S(1)} %get-tuple-element.44.sides, f32[64,64]{1,0:T(8,128)S(1)} %get-tuple-element.45.pair, ...), custom_call_target="tpu_custom_call" | custom-call | bytes 1622272 | tf_op jit(solution)/shard_map/first_image/pallas_call | solution.py:474
  13.4 0.2 collective-permute-start.4
  13.6 1.1 %collective-permute-done.4 = f32[136,128]{1,0:T(8,128)S(1)} collective-permute-done((f32[136,128]{1,0:T(8,128)S(1)}, f32[136,128]{1,0:T(8,128)S(1)}, u32[]{:S(2)}, u32[]{:S(2)}) %collective-permute-start.4) | collective-permute-done | bytes 69664 | tf_op jit(solution)/shard_map/ppermute | solution.py:443
  14.7 5.5 %collective-permute-start.6 = (f32[136,128]{1,0:T(8,128)S(1)}, f32[136,128]{1,0:T(8,128)S(1)}, u32[]{:S(2)}, u32[]{:S(2)}) collective-permute-start(f32[136,128]{1,0:T(8,128)S(1)} %select_add_fusion), channel_id=1, source_target_pairs={{0,6},{1,7},{2,4},{3,5},{4,2},{5,3},{6,0},{7,1},{8,14},{9,15},{10,... | collective-permute-start | bytes 208904 | tf_op jit(solution)/shard_map/ppermute | solution.py:443
  20.2 0.0 collective-permute-start.7
  20.2 0.4 collective-permute-start.5
  20.5 2.2 %collective-permute-done.6 = f32[136,128]{1,0:T(8,128)S(1)} collective-permute-done((f32[136,128]{1,0:T(8,128)S(1)}, f32[136,128]{1,0:T(8,128)S(1)}, u32[]{:S(2)}, u32[]{:S(2)}) %collective-permute-start.6) | collective-permute-done | bytes 69664 | tf_op jit(solution)/shard_map/ppermute | solution.py:443
  22.7 1.9 %collective-permute-done.7 = f32[136,128]{1,0:T(8,128)S(1)} collective-permute-done((f32[136,128]{1,0:T(8,128)S(1)}, f32[136,128]{1,0:T(8,128)S(1)}, u32[]{:S(2)}, u32[]{:S(2)}) %collective-permute-start.7) | collective-permute-done | bytes 69664 | tf_op jit(solution)/shard_map/ppermute | solution.py:443
  24.6 0.0 collective-permute-done.5
  24.6 4.9 %collective-permute-start.9 = (f32[136,128]{1,0:T(8,128)S(1)}, f32[136,128]{1,0:T(8,128)S(1)}, u32[]{:S(2)}, u32[]{:S(2)}) collective-permute-start(f32[136,128]{1,0:T(8,128)S(1)} %add_add_fusion.1), channel_id=1, source_target_pairs={{0,24},{1,25},{2,26},{3,27},{4,28},{5,29},{6,30},{7,31},{8,16},{9,... | collective-permute-start | bytes 208904 | tf_op jit(solution)/shard_map/ppermute | solution.py:443
  29.5 0.0 collective-permute-start.10
  29.5 0.4 collective-permute-start.8
  29.8 2.3 %collective-permute-done.9 = f32[136,128]{1,0:T(8,128)S(1)} collective-permute-done((f32[136,128]{1,0:T(8,128)S(1)}, f32[136,128]{1,0:T(8,128)S(1)}, u32[]{:S(2)}, u32[]{:S(2)}) %collective-permute-start.9) | collective-permute-done | bytes 69664 | tf_op jit(solution)/shard_map/ppermute | solution.py:443
  32.1 3.3 %collective-permute-done.10 = f32[136,128]{1,0:T(8,128)S(1)} collective-permute-done((f32[136,128]{1,0:T(8,128)S(1)}, f32[136,128]{1,0:T(8,128)S(1)}, u32[]{:S(2)}, u32[]{:S(2)}) %collective-permute-start.10) | collective-permute-done | bytes 69664 | tf_op jit(solution)/shard_map/ppermute | solution.py:443
  35.5 0.0 collective-permute-done.8
  35.5 0.2 collective-permute-start.11
  35.7 1.1 %collective-permute-done.11 = f32[136,128]{1,0:T(8,128)S(1)} collective-permute-done((f32[136,128]{1,0:T(8,128)S(1)}, f32[136,128]{1,0:T(8,128)S(1)}, u32[]{:S(2)}, u32[]{:S(2)}) %collective-permute-start.11) | collective-permute-done | bytes 69664 | tf_op jit(solution)/shard_map/ppermute | solution.py:443
  36.9 3.1 %first_solve.1 = (bf16[64,2048]{1,0:T(8,128)(2,1)S(1)}, f32[64,192]{1,0:T(8,128)S(1)}, f32[64,64]{1,0:T(8,128)S(1)}, f32[64,192]{1,0:T(8,128)S(1)}, f32[64,64]{1,0:T(8,128)S(1)}, /*index=5*/bf16[64,64]{1,0:T(8,128)(2,1)S(1)}) custom-call(f32[272,128]{1,0:T(8,128)S(1)} %pad_maximum_fusion.cross, bf16[192,2048]{1,0:T(8,128)(2,1)S(1)} %reshape.18.stack, ...), custom_call_target="tpu_custom_call" | custom-call | bytes 1589248 | tf_op jit(solution)/shard_map/first_solve/pallas_call | solution.py:474
  40.0 0.4 collective-permute-start.13
  40.4 0.7 collective-permute-start.12
  41.1 4.5 %collective-permute-done.13 = bf16[64,1024]{1,0:T(8,128)(2,1)S(1)} collective-permute-done((bf16[64,1024]{1,0:T(8,128)(2,1)S(1)}, bf16[64,1024]{1,0:T(8,128)(2,1)S(1)}, u32[]{:S(2)}, u32[]{:S(2)}) %collective-permute-start.13) | collective-permute-done | bytes 131104 | tf_op jit(solution)/shard_map/ppermute | solution.py:26
  45.7 0.0 collective-permute-done.12
  45.8 0.1 collective-permute-start.15
  45.8 1.1 %collective-permute-start.14 = (bf16[64,512]{1,0:T(8,128)(2,1)S(1)}, bf16[64,512]{1,0:T(8,128)(2,1)S(1)}, u32[]{:S(2)}, u32[]{:S(2)}) collective-permute-start(bf16[64,512]{1,0:T(8,128)(2,1)S(1)} %get-tuple-element.90), channel_id=1, source_target_pairs={{0,1},{1,0},{2,3},{3,2},{4,5},{5,4},{6,7},{7,6},{8,9},{9,8},{10,11... | collective-permute-start | bytes 196616 | tf_op jit(solution)/shard_map/ppermute | solution.py:26
  47.0 1.3 %middle_image.3 = (bf16[64,1536]{1,0:T(8,128)(2,1)S(1)}, f32[64,512]{1,0:T(8,128)S(1)}, f32[64,256]{1,0:T(8,128)S(1)}) custom-call(f32[27,16,128]{2,1,0:T(8,128)S(1)} %coefficients.1.coef, bf16[192,2048]{1,0:T(8,128)(2,1)S(1)} %reshape.18.stack, bf16[64,2048]{1,0:T(8,128)(2,1)S(1)} %get-tuple-element.55.block.last, ...), custom_call_target="tpu_custom_call" | custom-call | flops 7077888 | bytes 1925120 | tf_op jit(solution)/shard_map/middle_image/pallas_call | solution.py:474
  48.3 1.5 %collective-permute-done.15 = bf16[64,512]{1,0:T(8,128)(2,1)S(1)} collective-permute-done((bf16[64,512]{1,0:T(8,128)(2,1)S(1)}, bf16[64,512]{1,0:T(8,128)(2,1)S(1)}, u32[]{:S(2)}, u32[]{:S(2)}) %collective-permute-start.15) | collective-permute-done | bytes 65568 | tf_op jit(solution)/shard_map/ppermute | solution.py:27
  49.8 0.0 collective-permute-done.14
  49.8 0.7 second_image.1
  50.6 0.1 collective-permute-start.16
  50.6 1.2 %collective-permute-done.16 = f32[32,256]{1,0:T(8,128)S(1)} collective-permute-done((f32[32,256]{1,0:T(8,128)S(1)}, f32[32,256]{1,0:T(8,128)S(1)}, u32[]{:S(2)}, u32[]{:S(2)}) %collective-permute-start.16) | collective-permute-done | bytes 32800 | tf_op jit(solution)/shard_map/ppermute | solution.py:443
  51.8 5.0 %collective-permute-start.18 = (f32[32,256]{1,0:T(8,128)S(1)}, f32[32,256]{1,0:T(8,128)S(1)}, u32[]{:S(2)}, u32[]{:S(2)}) collective-permute-start(f32[32,256]{1,0:T(8,128)S(1)} %select_add_fusion.1), channel_id=1, source_target_pairs={{0,6},{1,7},{2,4},{3,5},{4,2},{5,3},{6,0},{7,1},{8,14},{9,15},{10,... | collective-permute-start | bytes 98312 | tf_op jit(solution)/shard_map/ppermute | solution.py:443
  56.8 0.0 collective-permute-start.19
  56.8 0.5 collective-permute-start.17
  57.3 1.4 %collective-permute-done.18 = f32[32,256]{1,0:T(8,128)S(1)} collective-permute-done((f32[32,256]{1,0:T(8,128)S(1)}, f32[32,256]{1,0:T(8,128)S(1)}, u32[]{:S(2)}, u32[]{:S(2)}) %collective-permute-start.18) | collective-permute-done | bytes 32800 | tf_op jit(solution)/shard_map/ppermute | solution.py:443
  58.7 1.7 %collective-permute-done.19 = f32[32,256]{1,0:T(8,128)S(1)} collective-permute-done((f32[32,256]{1,0:T(8,128)S(1)}, f32[32,256]{1,0:T(8,128)S(1)}, u32[]{:S(2)}, u32[]{:S(2)}) %collective-permute-start.19) | collective-permute-done | bytes 32800 | tf_op jit(solution)/shard_map/ppermute | solution.py:443
  60.4 2.2 %collective-permute-start.21 = (f32[32,256]{1,0:T(8,128)S(1)}, f32[32,256]{1,0:T(8,128)S(1)}, u32[]{:S(2)}, u32[]{:S(2)}) collective-permute-start(f32[32,256]{1,0:T(8,128)S(1)} %add_add_fusion.3), channel_id=1, source_target_pairs={{0,24},{1,25},{2,26},{3,27},{4,28},{5,29},{6,30},{7,31},{8,16},{9,... | collective-permute-start | bytes 98312 | tf_op jit(solution)/shard_map/ppermute | solution.py:443
  62.6 0.0 collective-permute-start.22
  62.6 2.0 %collective-permute-start.20 = (f32[32,256]{1,0:T(8,128)S(1)}, f32[32,256]{1,0:T(8,128)S(1)}, u32[]{:S(2)}, u32[]{:S(2)}) collective-permute-start(f32[32,256]{1,0:T(8,128)S(1)} %add_add_fusion.3), channel_id=1, source_target_pairs={{0,9},{1,8},{2,11},{3,10},{4,13},{5,12},{6,15},{7,14},{8,1},{9,0},... | collective-permute-start | bytes 98312 | tf_op jit(solution)/shard_map/ppermute | solution.py:443
  64.6 1.7 %collective-permute-done.21 = f32[32,256]{1,0:T(8,128)S(1)} collective-permute-done((f32[32,256]{1,0:T(8,128)S(1)}, f32[32,256]{1,0:T(8,128)S(1)}, u32[]{:S(2)}, u32[]{:S(2)}) %collective-permute-start.21) | collective-permute-done | bytes 32800 | tf_op jit(solution)/shard_map/ppermute | solution.py:443
  66.3 0.6 collective-permute-done.22
  67.0 0.5 collective-permute-done.20
  67.5 0.2 collective-permute-start.23
  67.7 0.4 next_gram.1
  68.1 0.7 collective-permute-done.23
  68.8 3.6 %second_solve.1 = (bf16[64,2,8,128]{3,2,1,0:T(8,128)(2,1)}, f32[2,64,192]{2,1,0:T(8,128)}, f32[2,64,64]{2,1,0:T(8,128)}) custom-call(f32[64,256]{1,0:T(8,128)S(1)} %pad_maximum_fusion.5.cross, bf16[192,192]{1,0:T(8,128)(2,1)S(1)} %get-tuple-element.64.own_high, bf16[192,192]{1,0:T(8,128)(2,1)S(1)} %get-tuple-element.65.own_low, ...), custom_call_target="tpu_custom_call" | custom-call | bytes 1982464 | tf_op jit(solution)/shard_map/second_solve/pallas_call | solution.py:474
  (30 shorter events, 0.4 us)
Async XLA Ops:
  0.6 1.0 %slice-start = ((bf16[3,64,2,8,128]{4,3,2,1,0:T(8,128)(2,1)}), bf16[1,64,2,8,128]{4,3,2,1,0:T(8,128)(2,1)S(1)}, s32[]{:S(2)}) async-start(bf16[3,64,2,8,128]{4,3,2,1,0:T(8,128)(2,1)} %param.3), calls=%async_computation | async-start | bytes 524288 | tf_op jit(solution)/shard_map/slice | solution.py:518
  1.6 3.9 %copy-start.2 = (bf16[3,64,2,8,128]{4,3,2,1,0:T(8,128)(2,1)S(1)}, bf16[3,64,2,8,128]{4,3,2,1,0:T(8,128)(2,1)}, u32[]{:S(2)}) copy-start(bf16[3,64,2,8,128]{4,3,2,1,0:T(8,128)(2,1)} %param.3) | copy-start | bytes 2359300
  1.7 6.5 %collective-permute-start.1 = (bf16[64,1024]{1,0:T(8,128)(2,1)S(1)}, bf16[64,1024]{1,0:T(8,128)(2,1)S(1)}, u32[]{:S(2)}, u32[]{:S(2)}) collective-permute-start(bf16[64,1024]{1,0:T(8,128)(2,1)S(1)} %slice_select_fusion), channel_id=1, source_target_pairs={{0,4},{4,0},{8,12},{12,8},{16,20},{20,16},{24,28},{28,24},{1,5},{5... | collective-permute-start | bytes 393224 | tf_op jit(solution)/shard_map/ppermute | solution.py:26
  4.8 3.5 %collective-permute-start = (bf16[64,1024]{1,0:T(8,128)(2,1)S(1)}, bf16[64,1024]{1,0:T(8,128)(2,1)S(1)}, u32[]{:S(2)}, u32[]{:S(2)}) collective-permute-start(bf16[64,1024]{1,0:T(8,128)(2,1)S(1)} %cut.2), channel_id=1, source_target_pairs={{4,8},{8,4},{12,16},{16,12},{20,24},{24,20},{5,9},{9,5},{13,17},{1... | collective-permute-start | bytes 393224 | tf_op jit(solution)/shard_map/ppermute | solution.py:27
  5.8 0.7 copy-start
  6.4 0.7 copy-start.1
  8.3 4.1 %collective-permute-start.3 = (bf16[64,512]{1,0:T(8,128)(2,1)S(1)}, bf16[64,512]{1,0:T(8,128)(2,1)S(1)}, u32[]{:S(2)}, u32[]{:S(2)}) collective-permute-start(bf16[64,512]{1,0:T(8,128)(2,1)S(1)} %get-tuple-element.97), channel_id=1, source_target_pairs={{1,2},{2,1},{0,3},{3,0},{5,6},{6,5},{4,7},{7,4},{9,10},{10,9},{8,1... | collective-permute-start | bytes 196616 | tf_op jit(solution)/shard_map/ppermute | solution.py:27
  8.7 3.7 %collective-permute-start.2 = (bf16[64,512]{1,0:T(8,128)(2,1)S(1)}, bf16[64,512]{1,0:T(8,128)(2,1)S(1)}, u32[]{:S(2)}, u32[]{:S(2)}) collective-permute-start(bf16[64,512]{1,0:T(8,128)(2,1)S(1)} %get-tuple-element.98), channel_id=1, source_target_pairs={{0,1},{1,0},{2,3},{3,2},{4,5},{5,4},{6,7},{7,6},{8,9},{9,8},{10,11... | collective-permute-start | bytes 196616 | tf_op jit(solution)/shard_map/ppermute | solution.py:26
  13.4 1.3 %collective-permute-start.4 = (f32[136,128]{1,0:T(8,128)S(1)}, f32[136,128]{1,0:T(8,128)S(1)}, u32[]{:S(2)}, u32[]{:S(2)}) collective-permute-start(f32[136,128]{1,0:T(8,128)S(1)} %slice_select_fusion.2), channel_id=1, source_target_pairs={{0,1},{1,0},{2,3},{3,2},{4,5},{5,4},{6,7},{7,6},{8,9},{9,8},{10,11... | collective-permute-start | bytes 208904 | tf_op jit(solution)/shard_map/ppermute | solution.py:443
  14.7 8.0 %collective-permute-start.6 = (f32[136,128]{1,0:T(8,128)S(1)}, f32[136,128]{1,0:T(8,128)S(1)}, u32[]{:S(2)}, u32[]{:S(2)}) collective-permute-start(f32[136,128]{1,0:T(8,128)S(1)} %select_add_fusion), channel_id=1, source_target_pairs={{0,6},{1,7},{2,4},{3,5},{4,2},{5,3},{6,0},{7,1},{8,14},{9,15},{10,... | collective-permute-start | bytes 208904 | tf_op jit(solution)/shard_map/ppermute | solution.py:443
  20.2 4.4 %collective-permute-start.7 = (f32[136,128]{1,0:T(8,128)S(1)}, f32[136,128]{1,0:T(8,128)S(1)}, u32[]{:S(2)}, u32[]{:S(2)}) collective-permute-start(f32[136,128]{1,0:T(8,128)S(1)} %select_add_fusion), channel_id=1, source_target_pairs={{0,5},{1,4},{2,7},{3,6},{4,1},{5,0},{6,3},{7,2},{8,13},{9,12},{10,... | collective-permute-start | bytes 208904 | tf_op jit(solution)/shard_map/ppermute | solution.py:443
  20.2 4.4 %collective-permute-start.5 = (f32[136,128]{1,0:T(8,128)S(1)}, f32[136,128]{1,0:T(8,128)S(1)}, u32[]{:S(2)}, u32[]{:S(2)}) collective-permute-start(f32[136,128]{1,0:T(8,128)S(1)} %select_add_fusion), channel_id=1, source_target_pairs={{0,3},{1,2},{2,1},{3,0},{4,7},{5,6},{6,5},{7,4},{8,11},{9,10},{10,... | collective-permute-start | bytes 208904 | tf_op jit(solution)/shard_map/ppermute | solution.py:443
  24.6 7.5 %collective-permute-start.9 = (f32[136,128]{1,0:T(8,128)S(1)}, f32[136,128]{1,0:T(8,128)S(1)}, u32[]{:S(2)}, u32[]{:S(2)}) collective-permute-start(f32[136,128]{1,0:T(8,128)S(1)} %add_add_fusion.1), channel_id=1, source_target_pairs={{0,24},{1,25},{2,26},{3,27},{4,28},{5,29},{6,30},{7,31},{8,16},{9,... | collective-permute-start | bytes 208904 | tf_op jit(solution)/shard_map/ppermute | solution.py:443
  29.5 6.0 %collective-permute-start.10 = (f32[136,128]{1,0:T(8,128)S(1)}, f32[136,128]{1,0:T(8,128)S(1)}, u32[]{:S(2)}, u32[]{:S(2)}) collective-permute-start(f32[136,128]{1,0:T(8,128)S(1)} %add_add_fusion.1), channel_id=1, source_target_pairs={{0,17},{1,16},{2,19},{3,18},{4,21},{5,20},{6,23},{7,22},{8,25},{9,... | collective-permute-start | bytes 208904 | tf_op jit(solution)/shard_map/ppermute | solution.py:443
  29.5 6.0 %collective-permute-start.8 = (f32[136,128]{1,0:T(8,128)S(1)}, f32[136,128]{1,0:T(8,128)S(1)}, u32[]{:S(2)}, u32[]{:S(2)}) collective-permute-start(f32[136,128]{1,0:T(8,128)S(1)} %add_add_fusion.1), channel_id=1, source_target_pairs={{0,9},{1,8},{2,11},{3,10},{4,13},{5,12},{6,15},{7,14},{8,1},{9,0},... | collective-permute-start | bytes 208904 | tf_op jit(solution)/shard_map/ppermute | solution.py:443
  35.5 1.3 %collective-permute-start.11 = (f32[136,128]{1,0:T(8,128)S(1)}, f32[136,128]{1,0:T(8,128)S(1)}, u32[]{:S(2)}, u32[]{:S(2)}) collective-permute-start(f32[136,128]{1,0:T(8,128)S(1)} %add_add_fusion), channel_id=1, source_target_pairs={{0,1},{1,0},{2,3},{3,2},{4,5},{5,4},{6,7},{7,6},{8,9},{9,8},{10,11... | collective-permute-start | bytes 208904 | tf_op jit(solution)/shard_map/ppermute | solution.py:443
  40.0 5.6 %collective-permute-start.13 = (bf16[64,1024]{1,0:T(8,128)(2,1)S(1)}, bf16[64,1024]{1,0:T(8,128)(2,1)S(1)}, u32[]{:S(2)}, u32[]{:S(2)}) collective-permute-start(bf16[64,1024]{1,0:T(8,128)(2,1)S(1)} %slice_select_fusion.1), channel_id=1, source_target_pairs={{0,4},{4,0},{8,12},{12,8},{16,20},{20,16},{24,28},{28,24},{1,5},{5... | collective-permute-start | bytes 393224 | tf_op jit(solution)/shard_map/ppermute | solution.py:26
  40.4 5.2 %collective-permute-start.12 = (bf16[64,1024]{1,0:T(8,128)(2,1)S(1)}, bf16[64,1024]{1,0:T(8,128)(2,1)S(1)}, u32[]{:S(2)}, u32[]{:S(2)}) collective-permute-start(bf16[64,1024]{1,0:T(8,128)(2,1)S(1)} %cut.3), channel_id=1, source_target_pairs={{4,8},{8,4},{12,16},{16,12},{20,24},{24,20},{5,9},{9,5},{13,17},{1... | collective-permute-start | bytes 393224 | tf_op jit(solution)/shard_map/ppermute | solution.py:27
  45.8 4.0 %collective-permute-start.15 = (bf16[64,512]{1,0:T(8,128)(2,1)S(1)}, bf16[64,512]{1,0:T(8,128)(2,1)S(1)}, u32[]{:S(2)}, u32[]{:S(2)}) collective-permute-start(bf16[64,512]{1,0:T(8,128)(2,1)S(1)} %get-tuple-element.89), channel_id=1, source_target_pairs={{1,2},{2,1},{0,3},{3,0},{5,6},{6,5},{4,7},{7,4},{9,10},{10,9},{8,1... | collective-permute-start | bytes 196616 | tf_op jit(solution)/shard_map/ppermute | solution.py:27
  45.8 4.0 %collective-permute-start.14 = (bf16[64,512]{1,0:T(8,128)(2,1)S(1)}, bf16[64,512]{1,0:T(8,128)(2,1)S(1)}, u32[]{:S(2)}, u32[]{:S(2)}) collective-permute-start(bf16[64,512]{1,0:T(8,128)(2,1)S(1)} %get-tuple-element.90), channel_id=1, source_target_pairs={{0,1},{1,0},{2,3},{3,2},{4,5},{5,4},{6,7},{7,6},{8,9},{9,8},{10,11... | collective-permute-start | bytes 196616 | tf_op jit(solution)/shard_map/ppermute | solution.py:26
  50.6 1.3 %collective-permute-start.16 = (f32[32,256]{1,0:T(8,128)S(1)}, f32[32,256]{1,0:T(8,128)S(1)}, u32[]{:S(2)}, u32[]{:S(2)}) collective-permute-start(f32[32,256]{1,0:T(8,128)S(1)} %slice_select_fusion.3), channel_id=1, source_target_pairs={{0,1},{1,0},{2,3},{3,2},{4,5},{5,4},{6,7},{7,6},{8,9},{9,8},{10,11... | collective-permute-start | bytes 98312 | tf_op jit(solution)/shard_map/ppermute | solution.py:443
  51.8 6.9 %collective-permute-start.18 = (f32[32,256]{1,0:T(8,128)S(1)}, f32[32,256]{1,0:T(8,128)S(1)}, u32[]{:S(2)}, u32[]{:S(2)}) collective-permute-start(f32[32,256]{1,0:T(8,128)S(1)} %select_add_fusion.1), channel_id=1, source_target_pairs={{0,6},{1,7},{2,4},{3,5},{4,2},{5,3},{6,0},{7,1},{8,14},{9,15},{10,... | collective-permute-start | bytes 98312 | tf_op jit(solution)/shard_map/ppermute | solution.py:443
  56.8 3.6 %collective-permute-start.19 = (f32[32,256]{1,0:T(8,128)S(1)}, f32[32,256]{1,0:T(8,128)S(1)}, u32[]{:S(2)}, u32[]{:S(2)}) collective-permute-start(f32[32,256]{1,0:T(8,128)S(1)} %select_add_fusion.1), channel_id=1, source_target_pairs={{0,5},{1,4},{2,7},{3,6},{4,1},{5,0},{6,3},{7,2},{8,13},{9,12},{10,... | collective-permute-start | bytes 98312 | tf_op jit(solution)/shard_map/ppermute | solution.py:443
  56.8 3.6 %collective-permute-start.17 = (f32[32,256]{1,0:T(8,128)S(1)}, f32[32,256]{1,0:T(8,128)S(1)}, u32[]{:S(2)}, u32[]{:S(2)}) collective-permute-start(f32[32,256]{1,0:T(8,128)S(1)} %select_add_fusion.1), channel_id=1, source_target_pairs={{0,3},{1,2},{2,1},{3,0},{4,7},{5,6},{6,5},{7,4},{8,11},{9,10},{10,... | collective-permute-start | bytes 98312 | tf_op jit(solution)/shard_map/ppermute | solution.py:443
  60.4 5.9 %collective-permute-start.21 = (f32[32,256]{1,0:T(8,128)S(1)}, f32[32,256]{1,0:T(8,128)S(1)}, u32[]{:S(2)}, u32[]{:S(2)}) collective-permute-start(f32[32,256]{1,0:T(8,128)S(1)} %add_add_fusion.3), channel_id=1, source_target_pairs={{0,24},{1,25},{2,26},{3,27},{4,28},{5,29},{6,30},{7,31},{8,16},{9,... | collective-permute-start | bytes 98312 | tf_op jit(solution)/shard_map/ppermute | solution.py:443
  62.6 4.3 %collective-permute-start.22 = (f32[32,256]{1,0:T(8,128)S(1)}, f32[32,256]{1,0:T(8,128)S(1)}, u32[]{:S(2)}, u32[]{:S(2)}) collective-permute-start(f32[32,256]{1,0:T(8,128)S(1)} %add_add_fusion.3), channel_id=1, source_target_pairs={{0,17},{1,16},{2,19},{3,18},{4,21},{5,20},{6,23},{7,22},{8,25},{9,... | collective-permute-start | bytes 98312 | tf_op jit(solution)/shard_map/ppermute | solution.py:443
  62.6 4.9 %collective-permute-start.20 = (f32[32,256]{1,0:T(8,128)S(1)}, f32[32,256]{1,0:T(8,128)S(1)}, u32[]{:S(2)}, u32[]{:S(2)}) collective-permute-start(f32[32,256]{1,0:T(8,128)S(1)} %add_add_fusion.3), channel_id=1, source_target_pairs={{0,9},{1,8},{2,11},{3,10},{4,13},{5,12},{6,15},{7,14},{8,1},{9,0},... | collective-permute-start | bytes 98312 | tf_op jit(solution)/shard_map/ppermute | solution.py:443
  67.5 1.3 %collective-permute-start.23 = (f32[32,256]{1,0:T(8,128)S(1)}, f32[32,256]{1,0:T(8,128)S(1)}, u32[]{:S(2)}, u32[]{:S(2)}) collective-permute-start(f32[32,256]{1,0:T(8,128)S(1)} %add_add_fusion.2), channel_id=1, source_target_pairs={{0,1},{1,0},{2,3},{3,2},{4,5},{5,4},{6,7},{7,6},{8,9},{9,8},{10,11... | collective-permute-start | bytes 98312 | tf_op jit(solution)/shard_map/ppermute | solution.py:443

commit v20 on v19

--- a/solution.py
+++ b/solution.py
@@ -151,12 +151,10 @@
     )
 
 
-def products(parts, fields):
-    total = 0
-    for w, cells in parts:
-        rows = [dot(w, ref[first:, cells], NT) for ref, first in fields]
-        total = total + jnp.concatenate(rows + [dot(w, w, NT)], axis=1)
-    return total
+def products(image, cells, fields):
+    w = image[...]
+    rows = [jnp.concatenate([ref[first:, there] for there in cells], axis=1) for ref, first in fields]
+    return dot(w, jnp.concatenate(rows + [w], axis=0), NT)
 
 
 def middle_image_kernel(spans, first, coef, stack, block, xlo, xhi, middle, partial, cross):
@@ -177,10 +175,8 @@
 
     lines = [(x, y) for y in range(span_y) for x in range(span_x)]
     stencil(coef, spans, block.shape[0], lines, line, lambda y: 0 <= y < span_y, write)
-    parts = [
-        (middle[:, own], there) for there, own in (middle_of(spans, x) for x in range(span_x))
-    ]
-    cross[...] = products(parts, [(stack, first)] + ([(block, 0)] if first else []))
+    cells = [middle_of(spans, x)[0] for x in range(span_x)]
+    cross[...] = products(middle, cells, [(stack, first)] + ([(block, 0)] if first else []))
 
 
 def end_lines(spans, coef, stack, block, partial, cross, ylo, yhi, ends):
@@ -195,13 +191,9 @@
 
     lines = [(x, y) for y in (0, span_y - 1) for x in range(span_x)]
     stencil(coef, spans, ends.shape[0], lines, line, lambda y: not 0 <= y < span_y, write)
-    parts = []
-    for x in range(span_x):
-        for last in range(2):
-            there, own = ends_of(spans, x, last)
-            parts.append((ends[:, own], there))
+    cells = [ends_of(spans, x, last)[0] for x in range(span_x) for last in range(2)]
     fields = [(stack, 0)] if block is None else [(stack, ends.shape[0]), (block, 0)]
-    return cross[...] + products(parts, fields)
+    return cross[...] + products(ends, cells, fields)
 
 
 def subtracted(spans, middle, ends, moved, block):
@@ -225,11 +217,6 @@
     return jnp.sum(jnp.where(row == column, square, 0.0), axis=axis, keepdims=True)
 
 
-def two_in_one(one, two):
-    row, column = places(one.shape[0])
-    return jnp.where(row >= column, one, two), diagonal_of(two, 0)
-
-
 def both_of(packed, diagonal):
     row, column = places(packed.shape[0])
     turned = packed.T
@@ -237,34 +224,37 @@
     return jnp.where(row >= column, packed, turned), jnp.where(row == column, diagonal, two)
 
 
-def stack_gram_kernel(columns, stack, sides, pair, last, diagonal):
+def stack_gram_kernel(columns, stack, sides, right, diagonal):
     parts = [stack[b * columns : (b + 1) * columns] for b in range(3)]
-    sides[0] = dot(parts[0], parts[1], NT)
-    sides[1] = dot(parts[0], parts[2], NT)
-    sides[2] = dot(parts[1], parts[2], NT)
-    pair[...], diagonal[...] = two_in_one(dot(parts[0], parts[0], NT), dot(parts[1], parts[1], NT))
-    last[...] = dot(parts[2], parts[2], NT)
+    row, column = places(columns)
+    second = dot(parts[1], parts[1], NT)
+    pair = jnp.where(row >= column, dot(parts[0], parts[0], NT), second)
+    sides[0] = jnp.concatenate(
+        [dot(parts[0], parts[2], NT), dot(parts[1], parts[2], NT)], axis=1
+    )
+    sides[1] = jnp.concatenate([pair, dot(parts[0], parts[1], NT)], axis=1)
+    nothing = jnp.zeros((columns, columns), jnp.float32)
+    right[...] = jnp.concatenate([nothing, dot(parts[2], parts[2], NT)], axis=1)
+    diagonal[...] = jnp.concatenate([diagonal_of(second, 0), nothing[:1]], axis=1)
 
 
 def first_image_kernel(
-    spans, coef, stack, sides, pair, last, diagonal, partial, known, ylo, yhi, ends, cross
+    spans, coef, stack, sides, right, diagonal, partial, known, ylo, yhi, ends, cross
 ):
     columns = ends.shape[0]
-    fields = stack.shape[0]
     sums = end_lines(spans, coef, stack, None, partial, known, ylo, yhi, ends)
-    first, square = sums[:, :fields], sums[:, fields:]
-    corner, own_diagonal = two_in_one(last[...], square)
-    rows = [
-        first[:, : 2 * columns],
-        jnp.concatenate([first[:, 2 * columns :], sides[0]], axis=1),
-        jnp.concatenate([sides[1], sides[2]], axis=1),
-        jnp.concatenate([pair[...], corner], axis=1),
-    ]
-    for i, row in enumerate(rows):
-        cross[i * columns : (i + 1) * columns] = row
-    rest = jnp.concatenate([diagonal[...], own_diagonal], axis=1)
-    rest = jnp.broadcast_to(rest, (cross.shape[0] - 4 * columns, 2 * columns))
-    cross[4 * columns :] = rest
+    cross[:columns] = sums[:, : 2 * columns]
+    sums = sums[:, 2 * columns :]
+    row, lane = (lax.broadcasted_iota(jnp.int32, sums.shape, dim) for dim in (0, 1))
+    cross[columns : 2 * columns] = jnp.where(
+        (lane >= columns) & (row >= lane - columns), right[...], sums
+    )
+    for i in range(2):
+        cross[(2 + i) * columns : (3 + i) * columns] = sides[i]
+    own = jnp.sum(jnp.where(row == lane - columns, sums, 0.0), axis=0, keepdims=True)
+    cross[4 * columns :] = jnp.broadcast_to(
+        diagonal[...] + own, (cross.shape[0] - 4 * columns, 2 * columns)
+    )
 
 
 def second_image_kernel(spans, coef, stack, block, partial, known, ylo, yhi, ends, cross):
@@ -273,12 +263,16 @@
 
 def opened(cross, columns, scale):
     parts = [cross[i * columns : (i + 1) * columns] * scale for i in range(4)]
+    left, right = ([part[:, at : at + columns] for part in parts] for at in (0, columns))
     diagonals = cross[4 * columns : 4 * columns + 1] * scale
-    first = jnp.concatenate([parts[0], parts[1][:, :columns]], axis=1)
-    side = parts[1][:, columns:], parts[2][:, :columns], parts[2][:, columns:]
-    one, two = both_of(parts[3][:, :columns], diagonals[:, :columns])
-    three, square = both_of(parts[3][:, columns:], diagonals[:, columns:])
-    gram = [[one, side[0], side[1]], [side[0].T, two, side[2]], [side[1].T, side[2].T, three]]
+    first = jnp.concatenate([parts[0], left[1]], axis=1)
+    one, two = both_of(left[3], diagonals[:, :columns])
+    three, square = both_of(right[1], diagonals[:, columns:])
+    gram = [
+        [one, right[3], left[2]],
+        [right[3].T, two, right[2]],
+        [left[2].T, right[2].T, three],
+    ]
     gram = jnp.concatenate([jnp.concatenate(row, axis=1) for row in gram], axis=0)
     return first, square, gram
 
@@ -497,8 +491,7 @@
     own = call(
         functools.partial(stack_gram_kernel, columns),
         "stack_gram",
-        [((blocks, columns, columns), f32), ((columns, columns), f32), ((columns, columns), f32),
-         ((1, columns), f32)],
+        [((2, columns, 2 * columns), f32), ((columns, 2 * columns), f32), ((1, 2 * columns), f32)],
         stack,
         flops=2 * fields * fields * cells,
     )

time: 72.7 us -> 72.3 us (level)
  no operation moved by 1% of the time
where the time goes in v20:
time: 72.3 us; the launch traced here: 72.1 us
  starting transfers between devices  29.2 us (40%)
  waiting for transfers between devices  27.2 us (38%)
  Pallas kernels  12.3 us (17%)
  local copies, waits for them, and re-layouts  2.13 us (3%)
  between operations  0.97 us (1%)
    ppermute x16, starting transfers between devices, partner(): return lax.ppermute(part, axes, [(i, i ^ mask) for i in range(count)])  21.3 us
    ppermute x16, waiting for transfers between devices, partner(): return lax.ppermute(part, axes, [(i, i ^ mask) for i in range(count)])  19.8 us
    pallas_call x8, Pallas kernels, call(): pl.pallas_call(kernel, out_shape=[jax.ShapeDtypeStruct(shape, dtype) for...  11.5 us
    ppermute x4, starting transfers between devices, swaps(): inner = lax.ppermute(near, axis, [(i, i ^ 1) for i in range(count)])  6.03 us
    ppermute x4, waiting for transfers between devices, swaps(): inner = lax.ppermute(near, axis, [(i, i ^ 1) for i in range(count)])  4.86 us
    ppermute x4, waiting for transfers between devices, swaps(): outer = lax.ppermute(far, axis, pairs)  2.49 us
    ppermute x4, starting transfers between devices, swaps(): outer = lax.ppermute(far, axis, pairs)  1.84 us
  transfers between devices with their start and end apart: 24, of which 17 were waited for; matrix products, arithmetic and copies ran while one was open for 1% of the time, Pallas kernels for 6%

profile of v20, /device:TPU:0, one launch (start us, length us, event | category | flops | bytes accessed | tf_op | source)
XLA Modules:
  0.0 72.1 jit_solution(11673209343804127468)
XLA Ops:
  0.6 0.0 slice-start
  0.6 0.9 %slice-done = bf16[1,64,2,8,128]{4,3,2,1,0:T(8,128)(2,1)S(1)} async-done(((bf16[3,64,2,8,128]{4,3,2,1,0:T(8,128)(2,1)}), bf16[1,64,2,8,128]{4,3,2,1,0:T(8,128)(2,1)S(1)}, s32[]{:S(2)}) %slice-start) | async-done | bytes 262168 | tf_op jit(solution)/shard_map/slice | solution.py:511
  1.6 0.1 reshape_squeeze.3.block
  1.7 3.0 %collective-permute-start.1 = (bf16[64,1024]{1,0:T(8,128)(2,1)S(1)}, bf16[64,1024]{1,0:T(8,128)(2,1)S(1)}, u32[]{:S(2)}, u32[]{:S(2)}) collective-permute-start(bf16[64,1024]{1,0:T(8,128)(2,1)S(1)} %slice_select_fusion), channel_id=1, source_target_pairs={{0,4},{4,0},{8,12},{12,8},{16,20},{20,16},{24,28},{28,24},{1,5},{5... | collective-permute-start | bytes 393224 | tf_op jit(solution)/shard_map/ppermute | solution.py:26
  4.8 0.7 collective-permute-start
  5.5 0.3 reshape.18.stack
  5.8 0.0 copy-start
  5.8 0.6 stack_gram.1
  6.5 0.0 copy-start.1
  6.5 0.0 copy-done
  6.5 0.6 copy-done.1
  7.1 0.8 %coefficients.1.coef = f32[27,16,128]{2,1,0:T(8,128)S(1)} custom-call(f32[8,27]{1,0:T(8,128)S(1)} %copy-done.1, s32[16,128]{1,0:T(8,128)S(1)} %bitcast.7), custom_call_target="tpu_custom_call" | custom-call | tf_op jit(solution)/shard_map/coefficients/pallas_call | solution.py:102
  7.9 0.3 collective-permute-done.1
  8.2 0.0 collective-permute-done
  8.3 0.4 collective-permute-start.3
  8.8 1.5 %collective-permute-start.2 = (bf16[64,512]{1,0:T(8,128)(2,1)S(1)}, bf16[64,512]{1,0:T(8,128)(2,1)S(1)}, u32[]{:S(2)}, u32[]{:S(2)}) collective-permute-start(bf16[64,512]{1,0:T(8,128)(2,1)S(1)} %get-tuple-element.94), channel_id=1, source_target_pairs={{0,1},{1,0},{2,3},{3,2},{4,5},{5,4},{6,7},{7,6},{8,9},{9,8},{10,11... | collective-permute-start | bytes 196616 | tf_op jit(solution)/shard_map/ppermute | solution.py:26
  10.3 1.3 %middle_image.2 = (bf16[64,1536]{1,0:T(8,128)(2,1)S(1)}, f32[64,512]{1,0:T(8,128)S(1)}, f32[64,256]{1,0:T(8,128)S(1)}) custom-call(f32[27,16,128]{2,1,0:T(8,128)S(1)} %coefficients.1.coef, bf16[192,2048]{1,0:T(8,128)(2,1)S(1)} %reshape.18.stack, bf16[64,2048]{1,0:T(8,128)(2,1)S(1)} %reshape_squeeze.3.block, bf16[64,1024]{1,0:T(8,128)(2,1)S(1)} %get-tuple-element.44.xlo, ...), custom_call_target="tpu_custom_call" | custom-call | flops 7077888 | bytes 1925120 | tf_op jit(solution)/shard_map/middle_image/pallas_call | solution.py:468
  11.6 0.9 %collective-permute-done.3 = bf16[64,512]{1,0:T(8,128)(2,1)S(1)} collective-permute-done((bf16[64,512]{1,0:T(8,128)(2,1)S(1)}, bf16[64,512]{1,0:T(8,128)(2,1)S(1)}, u32[]{:S(2)}, u32[]{:S(2)}) %collective-permute-start.3) | collective-permute-done | bytes 65568 | tf_op jit(solution)/shard_map/ppermute | solution.py:27
  12.5 0.0 collective-permute-done.2
  12.5 0.6 first_image.1
  13.1 0.2 collective-permute-start.4
  13.3 1.1 %collective-permute-done.4 = f32[136,128]{1,0:T(8,128)S(1)} collective-permute-done((f32[136,128]{1,0:T(8,128)S(1)}, f32[136,128]{1,0:T(8,128)S(1)}, u32[]{:S(2)}, u32[]{:S(2)}) %collective-permute-start.4) | collective-permute-done | bytes 69664 | tf_op jit(solution)/shard_map/ppermute | solution.py:437
  14.5 5.4 %collective-permute-start.6 = (f32[136,128]{1,0:T(8,128)S(1)}, f32[136,128]{1,0:T(8,128)S(1)}, u32[]{:S(2)}, u32[]{:S(2)}) collective-permute-start(f32[136,128]{1,0:T(8,128)S(1)} %select_add_fusion), channel_id=1, source_target_pairs={{0,6},{1,7},{2,4},{3,5},{4,2},{5,3},{6,0},{7,1},{8,14},{9,15},{10,... | collective-permute-start | bytes 208904 | tf_op jit(solution)/shard_map/ppermute | solution.py:437
  19.9 0.0 collective-permute-start.7
  19.9 0.4 collective-permute-start.5
  20.3 2.2 %collective-permute-done.6 = f32[136,128]{1,0:T(8,128)S(1)} collective-permute-done((f32[136,128]{1,0:T(8,128)S(1)}, f32[136,128]{1,0:T(8,128)S(1)}, u32[]{:S(2)}, u32[]{:S(2)}) %collective-permute-start.6) | collective-permute-done | bytes 69664 | tf_op jit(solution)/shard_map/ppermute | solution.py:437
  22.4 1.9 %collective-permute-done.7 = f32[136,128]{1,0:T(8,128)S(1)} collective-permute-done((f32[136,128]{1,0:T(8,128)S(1)}, f32[136,128]{1,0:T(8,128)S(1)}, u32[]{:S(2)}, u32[]{:S(2)}) %collective-permute-start.7) | collective-permute-done | bytes 69664 | tf_op jit(solution)/shard_map/ppermute | solution.py:437
  24.3 0.0 collective-permute-done.5
  24.4 4.9 %collective-permute-start.9 = (f32[136,128]{1,0:T(8,128)S(1)}, f32[136,128]{1,0:T(8,128)S(1)}, u32[]{:S(2)}, u32[]{:S(2)}) collective-permute-start(f32[136,128]{1,0:T(8,128)S(1)} %add_add_fusion.1), channel_id=1, source_target_pairs={{0,24},{1,25},{2,26},{3,27},{4,28},{5,29},{6,30},{7,31},{8,16},{9,... | collective-permute-start | bytes 208904 | tf_op jit(solution)/shard_map/ppermute | solution.py:437
  29.2 0.0 collective-permute-start.10
  29.2 0.4 collective-permute-start.8
  29.6 2.3 %collective-permute-done.9 = f32[136,128]{1,0:T(8,128)S(1)} collective-permute-done((f32[136,128]{1,0:T(8,128)S(1)}, f32[136,128]{1,0:T(8,128)S(1)}, u32[]{:S(2)}, u32[]{:S(2)}) %collective-permute-start.9) | collective-permute-done | bytes 69664 | tf_op jit(solution)/shard_map/ppermute | solution.py:437
  31.9 3.3 %collective-permute-done.10 = f32[136,128]{1,0:T(8,128)S(1)} collective-permute-done((f32[136,128]{1,0:T(8,128)S(1)}, f32[136,128]{1,0:T(8,128)S(1)}, u32[]{:S(2)}, u32[]{:S(2)}) %collective-permute-start.10) | collective-permute-done | bytes 69664 | tf_op jit(solution)/shard_map/ppermute | solution.py:437
  35.2 0.2 collective-permute-start.11
  35.4 1.1 %collective-permute-done.11 = f32[136,128]{1,0:T(8,128)S(1)} collective-permute-done((f32[136,128]{1,0:T(8,128)S(1)}, f32[136,128]{1,0:T(8,128)S(1)}, u32[]{:S(2)}, u32[]{:S(2)}) %collective-permute-start.11) | collective-permute-done | bytes 69664 | tf_op jit(solution)/shard_map/ppermute | solution.py:437
  36.6 3.1 %first_solve.1 = (bf16[64,2048]{1,0:T(8,128)(2,1)S(1)}, f32[64,192]{1,0:T(8,128)S(1)}, f32[64,64]{1,0:T(8,128)S(1)}, f32[64,192]{1,0:T(8,128)S(1)}, f32[64,64]{1,0:T(8,128)S(1)}, /*index=5*/bf16[64,64]{1,0:T(8,128)(2,1)S(1)}) custom-call(f32[272,128]{1,0:T(8,128)S(1)} %pad_maximum_fusion.cross, bf16[192,2048]{1,0:T(8,128)(2,1)S(1)} %reshape.18.stack, ...), custom_call_target="tpu_custom_call" | custom-call | bytes 1589248 | tf_op jit(solution)/shard_map/first_solve/pallas_call | solution.py:468
  39.8 0.4 collective-permute-start.13
  40.2 0.7 collective-permute-start.12
  40.9 4.5 %collective-permute-done.13 = bf16[64,1024]{1,0:T(8,128)(2,1)S(1)} collective-permute-done((bf16[64,1024]{1,0:T(8,128)(2,1)S(1)}, bf16[64,1024]{1,0:T(8,128)(2,1)S(1)}, u32[]{:S(2)}, u32[]{:S(2)}) %collective-permute-start.13) | collective-permute-done | bytes 131104 | tf_op jit(solution)/shard_map/ppermute | solution.py:26
  45.4 0.0 collective-permute-done.12
  45.5 0.1 collective-permute-start.15
  45.6 1.1 %collective-permute-start.14 = (bf16[64,512]{1,0:T(8,128)(2,1)S(1)}, bf16[64,512]{1,0:T(8,128)(2,1)S(1)}, u32[]{:S(2)}, u32[]{:S(2)}) collective-permute-start(bf16[64,512]{1,0:T(8,128)(2,1)S(1)} %get-tuple-element.86), channel_id=1, source_target_pairs={{0,1},{1,0},{2,3},{3,2},{4,5},{5,4},{6,7},{7,6},{8,9},{9,8},{10,11... | collective-permute-start | bytes 196616 | tf_op jit(solution)/shard_map/ppermute | solution.py:26
  46.7 1.3 %middle_image.3 = (bf16[64,1536]{1,0:T(8,128)(2,1)S(1)}, f32[64,512]{1,0:T(8,128)S(1)}, f32[64,256]{1,0:T(8,128)S(1)}) custom-call(f32[27,16,128]{2,1,0:T(8,128)S(1)} %coefficients.1.coef, bf16[192,2048]{1,0:T(8,128)(2,1)S(1)} %reshape.18.stack, bf16[64,2048]{1,0:T(8,128)(2,1)S(1)} %get-tuple-element.51.block.last, ...), custom_call_target="tpu_custom_call" | custom-call | flops 7077888 | bytes 1925120 | tf_op jit(solution)/shard_map/middle_image/pallas_call | solution.py:468
  48.0 1.6 %collective-permute-done.15 = bf16[64,512]{1,0:T(8,128)(2,1)S(1)} collective-permute-done((bf16[64,512]{1,0:T(8,128)(2,1)S(1)}, bf16[64,512]{1,0:T(8,128)(2,1)S(1)}, u32[]{:S(2)}, u32[]{:S(2)}) %collective-permute-start.15) | collective-permute-done | bytes 65568 | tf_op jit(solution)/shard_map/ppermute | solution.py:27
  49.5 0.0 collective-permute-done.14
  49.6 0.6 second_image.1
  50.2 0.1 collective-permute-start.16
  50.3 1.2 %collective-permute-done.16 = f32[32,256]{1,0:T(8,128)S(1)} collective-permute-done((f32[32,256]{1,0:T(8,128)S(1)}, f32[32,256]{1,0:T(8,128)S(1)}, u32[]{:S(2)}, u32[]{:S(2)}) %collective-permute-start.16) | collective-permute-done | bytes 32800 | tf_op jit(solution)/shard_map/ppermute | solution.py:437
  51.5 5.0 %collective-permute-start.18 = (f32[32,256]{1,0:T(8,128)S(1)}, f32[32,256]{1,0:T(8,128)S(1)}, u32[]{:S(2)}, u32[]{:S(2)}) collective-permute-start(f32[32,256]{1,0:T(8,128)S(1)} %select_add_fusion.1), channel_id=1, source_target_pairs={{0,6},{1,7},{2,4},{3,5},{4,2},{5,3},{6,0},{7,1},{8,14},{9,15},{10,... | collective-permute-start | bytes 98312 | tf_op jit(solution)/shard_map/ppermute | solution.py:437
  56.4 0.0 collective-permute-start.19
  56.4 0.5 collective-permute-start.17
  56.9 1.4 %collective-permute-done.18 = f32[32,256]{1,0:T(8,128)S(1)} collective-permute-done((f32[32,256]{1,0:T(8,128)S(1)}, f32[32,256]{1,0:T(8,128)S(1)}, u32[]{:S(2)}, u32[]{:S(2)}) %collective-permute-start.18) | collective-permute-done | bytes 32800 | tf_op jit(solution)/shard_map/ppermute | solution.py:437
  58.3 1.7 %collective-permute-done.19 = f32[32,256]{1,0:T(8,128)S(1)} collective-permute-done((f32[32,256]{1,0:T(8,128)S(1)}, f32[32,256]{1,0:T(8,128)S(1)}, u32[]{:S(2)}, u32[]{:S(2)}) %collective-permute-start.19) | collective-permute-done | bytes 32800 | tf_op jit(solution)/shard_map/ppermute | solution.py:437
  60.0 0.0 collective-permute-done.17
  60.1 2.2 %collective-permute-start.21 = (f32[32,256]{1,0:T(8,128)S(1)}, f32[32,256]{1,0:T(8,128)S(1)}, u32[]{:S(2)}, u32[]{:S(2)}) collective-permute-start(f32[32,256]{1,0:T(8,128)S(1)} %add_add_fusion.3), channel_id=1, source_target_pairs={{0,24},{1,25},{2,26},{3,27},{4,28},{5,29},{6,30},{7,31},{8,16},{9,... | collective-permute-start | bytes 98312 | tf_op jit(solution)/shard_map/ppermute | solution.py:437
  62.2 0.0 collective-permute-start.22
  62.2 2.0 %collective-permute-start.20 = (f32[32,256]{1,0:T(8,128)S(1)}, f32[32,256]{1,0:T(8,128)S(1)}, u32[]{:S(2)}, u32[]{:S(2)}) collective-permute-start(f32[32,256]{1,0:T(8,128)S(1)} %add_add_fusion.3), channel_id=1, source_target_pairs={{0,9},{1,8},{2,11},{3,10},{4,13},{5,12},{6,15},{7,14},{8,1},{9,0},... | collective-permute-start | bytes 98312 | tf_op jit(solution)/shard_map/ppermute | solution.py:437
  64.2 1.7 %collective-permute-done.21 = f32[32,256]{1,0:T(8,128)S(1)} collective-permute-done((f32[32,256]{1,0:T(8,128)S(1)}, f32[32,256]{1,0:T(8,128)S(1)}, u32[]{:S(2)}, u32[]{:S(2)}) %collective-permute-start.21) | collective-permute-done | bytes 32800 | tf_op jit(solution)/shard_map/ppermute | solution.py:437
  66.0 0.6 collective-permute-done.22
  66.6 0.5 collective-permute-done.20
  67.1 0.2 collective-permute-start.23
  67.3 0.4 next_gram.1
  67.7 0.7 collective-permute-done.23
  68.4 3.6 %second_solve.1 = (bf16[64,2,8,128]{3,2,1,0:T(8,128)(2,1)}, f32[2,64,192]{2,1,0:T(8,128)}, f32[2,64,64]{2,1,0:T(8,128)}) custom-call(f32[64,256]{1,0:T(8,128)S(1)} %pad_maximum_fusion.5.cross, bf16[192,192]{1,0:T(8,128)(2,1)S(1)} %get-tuple-element.60.own_high, bf16[192,192]{1,0:T(8,128)(2,1)S(1)} %get-tuple-element.61.own_low, ...), custom_call_target="tpu_custom_call" | custom-call | bytes 1982464 | tf_op jit(solution)/shard_map/second_solve/pallas_call | solution.py:468
  (30 shorter events, 0.4 us)
Async XLA Ops:
  0.6 1.0 %slice-start = ((bf16[3,64,2,8,128]{4,3,2,1,0:T(8,128)(2,1)}), bf16[1,64,2,8,128]{4,3,2,1,0:T(8,128)(2,1)S(1)}, s32[]{:S(2)}) async-start(bf16[3,64,2,8,128]{4,3,2,1,0:T(8,128)(2,1)} %param.3), calls=%async_computation | async-start | bytes 524288 | tf_op jit(solution)/shard_map/slice | solution.py:511
  1.6 3.9 %copy-start.2 = (bf16[3,64,2,8,128]{4,3,2,1,0:T(8,128)(2,1)S(1)}, bf16[3,64,2,8,128]{4,3,2,1,0:T(8,128)(2,1)}, u32[]{:S(2)}) copy-start(bf16[3,64,2,8,128]{4,3,2,1,0:T(8,128)(2,1)} %param.3) | copy-start | bytes 2359300
  1.7 6.5 %collective-permute-start.1 = (bf16[64,1024]{1,0:T(8,128)(2,1)S(1)}, bf16[64,1024]{1,0:T(8,128)(2,1)S(1)}, u32[]{:S(2)}, u32[]{:S(2)}) collective-permute-start(bf16[64,1024]{1,0:T(8,128)(2,1)S(1)} %slice_select_fusion), channel_id=1, source_target_pairs={{0,4},{4,0},{8,12},{12,8},{16,20},{20,16},{24,28},{28,24},{1,5},{5... | collective-permute-start | bytes 393224 | tf_op jit(solution)/shard_map/ppermute | solution.py:26
  4.8 3.5 %collective-permute-start = (bf16[64,1024]{1,0:T(8,128)(2,1)S(1)}, bf16[64,1024]{1,0:T(8,128)(2,1)S(1)}, u32[]{:S(2)}, u32[]{:S(2)}) collective-permute-start(bf16[64,1024]{1,0:T(8,128)(2,1)S(1)} %cut.2), channel_id=1, source_target_pairs={{4,8},{8,4},{12,16},{16,12},{20,24},{24,20},{5,9},{9,5},{13,17},{1... | collective-permute-start | bytes 393224 | tf_op jit(solution)/shard_map/ppermute | solution.py:27
  5.8 0.7 copy-start
  6.5 0.7 copy-start.1
  8.3 4.1 %collective-permute-start.3 = (bf16[64,512]{1,0:T(8,128)(2,1)S(1)}, bf16[64,512]{1,0:T(8,128)(2,1)S(1)}, u32[]{:S(2)}, u32[]{:S(2)}) collective-permute-start(bf16[64,512]{1,0:T(8,128)(2,1)S(1)} %get-tuple-element.93), channel_id=1, source_target_pairs={{1,2},{2,1},{0,3},{3,0},{5,6},{6,5},{4,7},{7,4},{9,10},{10,9},{8,1... | collective-permute-start | bytes 196616 | tf_op jit(solution)/shard_map/ppermute | solution.py:27
  8.8 3.7 %collective-permute-start.2 = (bf16[64,512]{1,0:T(8,128)(2,1)S(1)}, bf16[64,512]{1,0:T(8,128)(2,1)S(1)}, u32[]{:S(2)}, u32[]{:S(2)}) collective-permute-start(bf16[64,512]{1,0:T(8,128)(2,1)S(1)} %get-tuple-element.94), channel_id=1, source_target_pairs={{0,1},{1,0},{2,3},{3,2},{4,5},{5,4},{6,7},{7,6},{8,9},{9,8},{10,11... | collective-permute-start | bytes 196616 | tf_op jit(solution)/shard_map/ppermute | solution.py:26
  13.1 1.3 %collective-permute-start.4 = (f32[136,128]{1,0:T(8,128)S(1)}, f32[136,128]{1,0:T(8,128)S(1)}, u32[]{:S(2)}, u32[]{:S(2)}) collective-permute-start(f32[136,128]{1,0:T(8,128)S(1)} %slice_select_fusion.2), channel_id=1, source_target_pairs={{0,1},{1,0},{2,3},{3,2},{4,5},{5,4},{6,7},{7,6},{8,9},{9,8},{10,11... | collective-permute-start | bytes 208904 | tf_op jit(solution)/shard_map/ppermute | solution.py:437
  14.5 8.0 %collective-permute-start.6 = (f32[136,128]{1,0:T(8,128)S(1)}, f32[136,128]{1,0:T(8,128)S(1)}, u32[]{:S(2)}, u32[]{:S(2)}) collective-permute-start(f32[136,128]{1,0:T(8,128)S(1)} %select_add_fusion), channel_id=1, source_target_pairs={{0,6},{1,7},{2,4},{3,5},{4,2},{5,3},{6,0},{7,1},{8,14},{9,15},{10,... | collective-permute-start | bytes 208904 | tf_op jit(solution)/shard_map/ppermute | solution.py:437
  19.9 4.4 %collective-permute-start.7 = (f32[136,128]{1,0:T(8,128)S(1)}, f32[136,128]{1,0:T(8,128)S(1)}, u32[]{:S(2)}, u32[]{:S(2)}) collective-permute-start(f32[136,128]{1,0:T(8,128)S(1)} %select_add_fusion), channel_id=1, source_target_pairs={{0,5},{1,4},{2,7},{3,6},{4,1},{5,0},{6,3},{7,2},{8,13},{9,12},{10,... | collective-permute-start | bytes 208904 | tf_op jit(solution)/shard_map/ppermute | solution.py:437
  19.9 4.4 %collective-permute-start.5 = (f32[136,128]{1,0:T(8,128)S(1)}, f32[136,128]{1,0:T(8,128)S(1)}, u32[]{:S(2)}, u32[]{:S(2)}) collective-permute-start(f32[136,128]{1,0:T(8,128)S(1)} %select_add_fusion), channel_id=1, source_target_pairs={{0,3},{1,2},{2,1},{3,0},{4,7},{5,6},{6,5},{7,4},{8,11},{9,10},{10,... | collective-permute-start | bytes 208904 | tf_op jit(solution)/shard_map/ppermute | solution.py:437
  24.4 7.5 %collective-permute-start.9 = (f32[136,128]{1,0:T(8,128)S(1)}, f32[136,128]{1,0:T(8,128)S(1)}, u32[]{:S(2)}, u32[]{:S(2)}) collective-permute-start(f32[136,128]{1,0:T(8,128)S(1)} %add_add_fusion.1), channel_id=1, source_target_pairs={{0,24},{1,25},{2,26},{3,27},{4,28},{5,29},{6,30},{7,31},{8,16},{9,... | collective-permute-start | bytes 208904 | tf_op jit(solution)/shard_map/ppermute | solution.py:437
  29.2 6.0 %collective-permute-start.10 = (f32[136,128]{1,0:T(8,128)S(1)}, f32[136,128]{1,0:T(8,128)S(1)}, u32[]{:S(2)}, u32[]{:S(2)}) collective-permute-start(f32[136,128]{1,0:T(8,128)S(1)} %add_add_fusion.1), channel_id=1, source_target_pairs={{0,17},{1,16},{2,19},{3,18},{4,21},{5,20},{6,23},{7,22},{8,25},{9,... | collective-permute-start | bytes 208904 | tf_op jit(solution)/shard_map/ppermute | solution.py:437
  29.2 6.0 %collective-permute-start.8 = (f32[136,128]{1,0:T(8,128)S(1)}, f32[136,128]{1,0:T(8,128)S(1)}, u32[]{:S(2)}, u32[]{:S(2)}) collective-permute-start(f32[136,128]{1,0:T(8,128)S(1)} %add_add_fusion.1), channel_id=1, source_target_pairs={{0,9},{1,8},{2,11},{3,10},{4,13},{5,12},{6,15},{7,14},{8,1},{9,0},... | collective-permute-start | bytes 208904 | tf_op jit(solution)/shard_map/ppermute | solution.py:437
  35.2 1.3 %collective-permute-start.11 = (f32[136,128]{1,0:T(8,128)S(1)}, f32[136,128]{1,0:T(8,128)S(1)}, u32[]{:S(2)}, u32[]{:S(2)}) collective-permute-start(f32[136,128]{1,0:T(8,128)S(1)} %add_add_fusion), channel_id=1, source_target_pairs={{0,1},{1,0},{2,3},{3,2},{4,5},{5,4},{6,7},{7,6},{8,9},{9,8},{10,11... | collective-permute-start | bytes 208904 | tf_op jit(solution)/shard_map/ppermute | solution.py:437
  39.8 5.6 %collective-permute-start.13 = (bf16[64,1024]{1,0:T(8,128)(2,1)S(1)}, bf16[64,1024]{1,0:T(8,128)(2,1)S(1)}, u32[]{:S(2)}, u32[]{:S(2)}) collective-permute-start(bf16[64,1024]{1,0:T(8,128)(2,1)S(1)} %slice_select_fusion.1), channel_id=1, source_target_pairs={{0,4},{4,0},{8,12},{12,8},{16,20},{20,16},{24,28},{28,24},{1,5},{5... | collective-permute-start | bytes 393224 | tf_op jit(solution)/shard_map/ppermute | solution.py:26
  40.2 5.2 %collective-permute-start.12 = (bf16[64,1024]{1,0:T(8,128)(2,1)S(1)}, bf16[64,1024]{1,0:T(8,128)(2,1)S(1)}, u32[]{:S(2)}, u32[]{:S(2)}) collective-permute-start(bf16[64,1024]{1,0:T(8,128)(2,1)S(1)} %cut.3), channel_id=1, source_target_pairs={{4,8},{8,4},{12,16},{16,12},{20,24},{24,20},{5,9},{9,5},{13,17},{1... | collective-permute-start | bytes 393224 | tf_op jit(solution)/shard_map/ppermute | solution.py:27
  45.5 4.0 %collective-permute-start.15 = (bf16[64,512]{1,0:T(8,128)(2,1)S(1)}, bf16[64,512]{1,0:T(8,128)(2,1)S(1)}, u32[]{:S(2)}, u32[]{:S(2)}) collective-permute-start(bf16[64,512]{1,0:T(8,128)(2,1)S(1)} %get-tuple-element.85), channel_id=1, source_target_pairs={{1,2},{2,1},{0,3},{3,0},{5,6},{6,5},{4,7},{7,4},{9,10},{10,9},{8,1... | collective-permute-start | bytes 196616 | tf_op jit(solution)/shard_map/ppermute | solution.py:27
  45.6 4.0 %collective-permute-start.14 = (bf16[64,512]{1,0:T(8,128)(2,1)S(1)}, bf16[64,512]{1,0:T(8,128)(2,1)S(1)}, u32[]{:S(2)}, u32[]{:S(2)}) collective-permute-start(bf16[64,512]{1,0:T(8,128)(2,1)S(1)} %get-tuple-element.86), channel_id=1, source_target_pairs={{0,1},{1,0},{2,3},{3,2},{4,5},{5,4},{6,7},{7,6},{8,9},{9,8},{10,11... | collective-permute-start | bytes 196616 | tf_op jit(solution)/shard_map/ppermute | solution.py:26
  50.2 1.3 %collective-permute-start.16 = (f32[32,256]{1,0:T(8,128)S(1)}, f32[32,256]{1,0:T(8,128)S(1)}, u32[]{:S(2)}, u32[]{:S(2)}) collective-permute-start(f32[32,256]{1,0:T(8,128)S(1)} %slice_select_fusion.3), channel_id=1, source_target_pairs={{0,1},{1,0},{2,3},{3,2},{4,5},{5,4},{6,7},{7,6},{8,9},{9,8},{10,11... | collective-permute-start | bytes 98312 | tf_op jit(solution)/shard_map/ppermute | solution.py:437
  51.5 6.9 %collective-permute-start.18 = (f32[32,256]{1,0:T(8,128)S(1)}, f32[32,256]{1,0:T(8,128)S(1)}, u32[]{:S(2)}, u32[]{:S(2)}) collective-permute-start(f32[32,256]{1,0:T(8,128)S(1)} %select_add_fusion.1), channel_id=1, source_target_pairs={{0,6},{1,7},{2,4},{3,5},{4,2},{5,3},{6,0},{7,1},{8,14},{9,15},{10,... | collective-permute-start | bytes 98312 | tf_op jit(solution)/shard_map/ppermute | solution.py:437
  56.4 3.6 %collective-permute-start.19 = (f32[32,256]{1,0:T(8,128)S(1)}, f32[32,256]{1,0:T(8,128)S(1)}, u32[]{:S(2)}, u32[]{:S(2)}) collective-permute-start(f32[32,256]{1,0:T(8,128)S(1)} %select_add_fusion.1), channel_id=1, source_target_pairs={{0,5},{1,4},{2,7},{3,6},{4,1},{5,0},{6,3},{7,2},{8,13},{9,12},{10,... | collective-permute-start | bytes 98312 | tf_op jit(solution)/shard_map/ppermute | solution.py:437
  56.4 3.6 %collective-permute-start.17 = (f32[32,256]{1,0:T(8,128)S(1)}, f32[32,256]{1,0:T(8,128)S(1)}, u32[]{:S(2)}, u32[]{:S(2)}) collective-permute-start(f32[32,256]{1,0:T(8,128)S(1)} %select_add_fusion.1), channel_id=1, source_target_pairs={{0,3},{1,2},{2,1},{3,0},{4,7},{5,6},{6,5},{7,4},{8,11},{9,10},{10,... | collective-permute-start | bytes 98312 | tf_op jit(solution)/shard_map/ppermute | solution.py:437
  60.1 5.9 %collective-permute-start.21 = (f32[32,256]{1,0:T(8,128)S(1)}, f32[32,256]{1,0:T(8,128)S(1)}, u32[]{:S(2)}, u32[]{:S(2)}) collective-permute-start(f32[32,256]{1,0:T(8,128)S(1)} %add_add_fusion.3), channel_id=1, source_target_pairs={{0,24},{1,25},{2,26},{3,27},{4,28},{5,29},{6,30},{7,31},{8,16},{9,... | collective-permute-start | bytes 98312 | tf_op jit(solution)/shard_map/ppermute | solution.py:437
  62.2 4.3 %collective-permute-start.22 = (f32[32,256]{1,0:T(8,128)S(1)}, f32[32,256]{1,0:T(8,128)S(1)}, u32[]{:S(2)}, u32[]{:S(2)}) collective-permute-start(f32[32,256]{1,0:T(8,128)S(1)} %add_add_fusion.3), channel_id=1, source_target_pairs={{0,17},{1,16},{2,19},{3,18},{4,21},{5,20},{6,23},{7,22},{8,25},{9,... | collective-permute-start | bytes 98312 | tf_op jit(solution)/shard_map/ppermute | solution.py:437
  62.2 4.9 %collective-permute-start.20 = (f32[32,256]{1,0:T(8,128)S(1)}, f32[32,256]{1,0:T(8,128)S(1)}, u32[]{:S(2)}, u32[]{:S(2)}) collective-permute-start(f32[32,256]{1,0:T(8,128)S(1)} %add_add_fusion.3), channel_id=1, source_target_pairs={{0,9},{1,8},{2,11},{3,10},{4,13},{5,12},{6,15},{7,14},{8,1},{9,0},... | collective-permute-start | bytes 98312 | tf_op jit(solution)/shard_map/ppermute | solution.py:437
  67.1 1.3 %collective-permute-start.23 = (f32[32,256]{1,0:T(8,128)S(1)}, f32[32,256]{1,0:T(8,128)S(1)}, u32[]{:S(2)}, u32[]{:S(2)}) collective-permute-start(f32[32,256]{1,0:T(8,128)S(1)} %add_add_fusion.2), channel_id=1, source_target_pairs={{0,1},{1,0},{2,3},{3,2},{4,5},{5,4},{6,7},{7,6},{8,9},{9,8},{10,11... | collective-permute-start | bytes 98312 | tf_op jit(solution)/shard_map/ppermute | solution.py:437

commit v21 on v20

--- a/solution.py
+++ b/solution.py
@@ -318,7 +318,7 @@
         for p in range(0, 8, 2):
             q = p + 1
             first, mixed, last = entry[p, p], entry[p, q], entry[q, q]
-            inverse = 1.0 / (first * last - mixed * mixed)
+            inverse = pltpu.reciprocal(first * last - mixed * mixed, approx=True)
 
             def solve(one, two):
                 return (
@@ -453,7 +453,7 @@
     while bit < count:
         if 2 * bit < count:
             one, two, both = (partner(part, mask) for mask in (bit + 1, 2 * bit + 1, 3 * bit))
-            part = (part + one) + (both + two)
+            part = (part + one) + (two + both)
             bit *= 4
         else:
             part = part + partner(part, bit + 1)

time: 72.3 us -> 75.9 us (1.050)
  waiting for transfers between devices: 27.2 us -> 31 us
    ppermute x16, waiting for transfers between devices: 19.8 us -> 24.2 us  [partner(): return lax.ppermute(part, axes, [(i, i ^ mask) for i in range(count)])]
    ppermute x16, starting transfers between devices: 21.3 us -> 20.4 us  [partner(): return lax.ppermute(part, axes, [(i, i ^ mask) for i in range(count)])]
  transfers between devices with their start and end apart: 24 -> 24, of which waited for: 17 -> 19; matrix products, arithmetic and copies ran while one was open for 1% -> 0% of each run, Pallas kernels for 6% -> 6%
where the time goes in v21:
time: 75.9 us; the launch traced here: 75.6 us
  waiting for transfers between devices  31 us (41%)
  starting transfers between devices  28.9 us (38%)
  Pallas kernels  12.3 us (16%)
  local copies, waits for them, and re-layouts  2.13 us (3%)
  between operations  0.97 us (1%)
    ppermute x16, waiting for transfers between devices, partner(): return lax.ppermute(part, axes, [(i, i ^ mask) for i in range(count)])  24.2 us
    ppermute x16, starting transfers between devices, partner(): return lax.ppermute(part, axes, [(i, i ^ mask) for i in range(count)])  20.4 us
    pallas_call x8, Pallas kernels, call(): pl.pallas_call(kernel, out_shape=[jax.ShapeDtypeStruct(shape, dtype) for...  11.5 us
    ppermute x4, starting transfers between devices, swaps(): inner = lax.ppermute(near, axis, [(i, i ^ 1) for i in range(count)])  6.6 us
    ppermute x4, waiting for transfers between devices, swaps(): inner = lax.ppermute(near, axis, [(i, i ^ 1) for i in range(count)])  4.35 us
    ppermute x4, waiting for transfers between devices, swaps(): outer = lax.ppermute(far, axis, pairs)  2.49 us
    ppermute x4, starting transfers between devices, swaps(): outer = lax.ppermute(far, axis, pairs)  1.9 us
  transfers between devices with their start and end apart: 24, of which 19 were waited for; matrix products, arithmetic and copies ran while one was open for 0% of the time, Pallas kernels for 6%

profile of v21, /device:TPU:0, one launch (start us, length us, event | category | flops | bytes accessed | tf_op | source)
XLA Modules:
  0.0 75.6 jit_solution(14318580226384512780)
XLA Ops:
  0.6 0.0 slice-start
  0.6 0.9 %slice-done = bf16[1,64,2,8,128]{4,3,2,1,0:T(8,128)(2,1)S(1)} async-done(((bf16[3,64,2,8,128]{4,3,2,1,0:T(8,128)(2,1)}), bf16[1,64,2,8,128]{4,3,2,1,0:T(8,128)(2,1)S(1)}, s32[]{:S(2)}) %slice-start) | async-done | bytes 262168 | tf_op jit(solution)/shard_map/slice | solution.py:511
  1.6 0.1 reshape_squeeze.3.block
  1.7 3.0 %collective-permute-start.1 = (bf16[64,1024]{1,0:T(8,128)(2,1)S(1)}, bf16[64,1024]{1,0:T(8,128)(2,1)S(1)}, u32[]{:S(2)}, u32[]{:S(2)}) collective-permute-start(bf16[64,1024]{1,0:T(8,128)(2,1)S(1)} %slice_select_fusion), channel_id=1, source_target_pairs={{0,4},{4,0},{8,12},{12,8},{16,20},{20,16},{24,28},{28,24},{1,5},{5... | collective-permute-start | bytes 393224 | tf_op jit(solution)/shard_map/ppermute | solution.py:26
  4.8 0.7 collective-permute-start
  5.5 0.3 reshape.18.stack
  5.8 0.0 copy-start
  5.8 0.6 stack_gram.1
  6.5 0.0 copy-start.1
  6.5 0.0 copy-done
  6.5 0.6 copy-done.1
  7.1 0.8 %coefficients.1.coef = f32[27,16,128]{2,1,0:T(8,128)S(1)} custom-call(f32[8,27]{1,0:T(8,128)S(1)} %copy-done.1, s32[16,128]{1,0:T(8,128)S(1)} %bitcast.7), custom_call_target="tpu_custom_call" | custom-call | tf_op jit(solution)/shard_map/coefficients/pallas_call | solution.py:102
  7.9 0.3 collective-permute-done.1
  8.2 0.0 collective-permute-done
  8.3 0.4 collective-permute-start.3
  8.8 1.5 %collective-permute-start.2 = (bf16[64,512]{1,0:T(8,128)(2,1)S(1)}, bf16[64,512]{1,0:T(8,128)(2,1)S(1)}, u32[]{:S(2)}, u32[]{:S(2)}) collective-permute-start(bf16[64,512]{1,0:T(8,128)(2,1)S(1)} %get-tuple-element.94), channel_id=1, source_target_pairs={{0,1},{1,0},{2,3},{3,2},{4,5},{5,4},{6,7},{7,6},{8,9},{9,8},{10,11... | collective-permute-start | bytes 196616 | tf_op jit(solution)/shard_map/ppermute | solution.py:26
  10.3 1.3 %middle_image.2 = (bf16[64,1536]{1,0:T(8,128)(2,1)S(1)}, f32[64,512]{1,0:T(8,128)S(1)}, f32[64,256]{1,0:T(8,128)S(1)}) custom-call(f32[27,16,128]{2,1,0:T(8,128)S(1)} %coefficients.1.coef, bf16[192,2048]{1,0:T(8,128)(2,1)S(1)} %reshape.18.stack, bf16[64,2048]{1,0:T(8,128)(2,1)S(1)} %reshape_squeeze.3.block, bf16[64,1024]{1,0:T(8,128)(2,1)S(1)} %get-tuple-element.44.xlo, ...), custom_call_target="tpu_custom_call" | custom-call | flops 7077888 | bytes 1925120 | tf_op jit(solution)/shard_map/middle_image/pallas_call | solution.py:468
  11.6 0.9 %collective-permute-done.3 = bf16[64,512]{1,0:T(8,128)(2,1)S(1)} collective-permute-done((bf16[64,512]{1,0:T(8,128)(2,1)S(1)}, bf16[64,512]{1,0:T(8,128)(2,1)S(1)}, u32[]{:S(2)}, u32[]{:S(2)}) %collective-permute-start.3) | collective-permute-done | bytes 65568 | tf_op jit(solution)/shard_map/ppermute | solution.py:27
  12.5 0.0 collective-permute-done.2
  12.5 0.6 first_image.1
  13.1 0.2 collective-permute-start.4
  13.3 1.1 %collective-permute-done.4 = f32[136,128]{1,0:T(8,128)S(1)} collective-permute-done((f32[136,128]{1,0:T(8,128)S(1)}, f32[136,128]{1,0:T(8,128)S(1)}, u32[]{:S(2)}, u32[]{:S(2)}) %collective-permute-start.4) | collective-permute-done | bytes 69664 | tf_op jit(solution)/shard_map/ppermute | solution.py:437
  14.5 4.6 %collective-permute-start.6 = (f32[136,128]{1,0:T(8,128)S(1)}, f32[136,128]{1,0:T(8,128)S(1)}, u32[]{:S(2)}, u32[]{:S(2)}) collective-permute-start(f32[136,128]{1,0:T(8,128)S(1)} %select_add_fusion), channel_id=1, source_target_pairs={{0,5},{1,4},{2,7},{3,6},{4,1},{5,0},{6,3},{7,2},{8,13},{9,12},{10,... | collective-permute-start | bytes 208904 | tf_op jit(solution)/shard_map/ppermute | solution.py:437
  19.1 0.9 %collective-permute-start.7 = (f32[136,128]{1,0:T(8,128)S(1)}, f32[136,128]{1,0:T(8,128)S(1)}, u32[]{:S(2)}, u32[]{:S(2)}) collective-permute-start(f32[136,128]{1,0:T(8,128)S(1)} %select_add_fusion), channel_id=1, source_target_pairs={{0,6},{1,7},{2,4},{3,5},{4,2},{5,3},{6,0},{7,1},{8,14},{9,15},{10,... | collective-permute-start | bytes 208904 | tf_op jit(solution)/shard_map/ppermute | solution.py:437
  20.0 0.3 collective-permute-start.5
  20.3 1.3 %collective-permute-done.6 = f32[136,128]{1,0:T(8,128)S(1)} collective-permute-done((f32[136,128]{1,0:T(8,128)S(1)}, f32[136,128]{1,0:T(8,128)S(1)}, u32[]{:S(2)}, u32[]{:S(2)}) %collective-permute-start.6) | collective-permute-done | bytes 69664 | tf_op jit(solution)/shard_map/ppermute | solution.py:437
  21.6 2.9 %collective-permute-done.7 = f32[136,128]{1,0:T(8,128)S(1)} collective-permute-done((f32[136,128]{1,0:T(8,128)S(1)}, f32[136,128]{1,0:T(8,128)S(1)}, u32[]{:S(2)}, u32[]{:S(2)}) %collective-permute-start.7) | collective-permute-done | bytes 69664 | tf_op jit(solution)/shard_map/ppermute | solution.py:437
  24.5 1.4 %collective-permute-done.5 = f32[136,128]{1,0:T(8,128)S(1)} collective-permute-done((f32[136,128]{1,0:T(8,128)S(1)}, f32[136,128]{1,0:T(8,128)S(1)}, u32[]{:S(2)}, u32[]{:S(2)}) %collective-permute-start.5) | collective-permute-done | bytes 69664 | tf_op jit(solution)/shard_map/ppermute | solution.py:437
  25.9 3.2 %collective-permute-start.9 = (f32[136,128]{1,0:T(8,128)S(1)}, f32[136,128]{1,0:T(8,128)S(1)}, u32[]{:S(2)}, u32[]{:S(2)}) collective-permute-start(f32[136,128]{1,0:T(8,128)S(1)} %add_add_fusion.1), channel_id=1, source_target_pairs={{0,17},{1,16},{2,19},{3,18},{4,21},{5,20},{6,23},{7,22},{8,25},{9,... | collective-permute-start | bytes 208904 | tf_op jit(solution)/shard_map/ppermute | solution.py:437
  29.1 1.4 %collective-permute-start.10 = (f32[136,128]{1,0:T(8,128)S(1)}, f32[136,128]{1,0:T(8,128)S(1)}, u32[]{:S(2)}, u32[]{:S(2)}) collective-permute-start(f32[136,128]{1,0:T(8,128)S(1)} %add_add_fusion.1), channel_id=1, source_target_pairs={{0,24},{1,25},{2,26},{3,27},{4,28},{5,29},{6,30},{7,31},{8,16},{9,... | collective-permute-start | bytes 208904 | tf_op jit(solution)/shard_map/ppermute | solution.py:437
  30.5 0.2 collective-permute-start.8
  30.7 1.0 %collective-permute-done.9 = f32[136,128]{1,0:T(8,128)S(1)} collective-permute-done((f32[136,128]{1,0:T(8,128)S(1)}, f32[136,128]{1,0:T(8,128)S(1)}, u32[]{:S(2)}, u32[]{:S(2)}) %collective-permute-start.9) | collective-permute-done | bytes 69664 | tf_op jit(solution)/shard_map/ppermute | solution.py:437
  31.7 4.3 %collective-permute-done.10 = f32[136,128]{1,0:T(8,128)S(1)} collective-permute-done((f32[136,128]{1,0:T(8,128)S(1)}, f32[136,128]{1,0:T(8,128)S(1)}, u32[]{:S(2)}, u32[]{:S(2)}) %collective-permute-start.10) | collective-permute-done | bytes 69664 | tf_op jit(solution)/shard_map/ppermute | solution.py:437
  35.9 0.3 collective-permute-done.8
  36.2 0.2 collective-permute-start.11
  36.4 1.1 %collective-permute-done.11 = f32[136,128]{1,0:T(8,128)S(1)} collective-permute-done((f32[136,128]{1,0:T(8,128)S(1)}, f32[136,128]{1,0:T(8,128)S(1)}, u32[]{:S(2)}, u32[]{:S(2)}) %collective-permute-start.11) | collective-permute-done | bytes 69664 | tf_op jit(solution)/shard_map/ppermute | solution.py:437
  37.6 3.1 %first_solve.1 = (bf16[64,2048]{1,0:T(8,128)(2,1)S(1)}, f32[64,192]{1,0:T(8,128)S(1)}, f32[64,64]{1,0:T(8,128)S(1)}, f32[64,192]{1,0:T(8,128)S(1)}, f32[64,64]{1,0:T(8,128)S(1)}, /*index=5*/bf16[64,64]{1,0:T(8,128)(2,1)S(1)}) custom-call(f32[272,128]{1,0:T(8,128)S(1)} %pad_maximum_fusion.cross, bf16[192,2048]{1,0:T(8,128)(2,1)S(1)} %reshape.18.stack, ...), custom_call_target="tpu_custom_call" | custom-call | bytes 1589248 | tf_op jit(solution)/shard_map/first_solve/pallas_call | solution.py:468
  40.8 0.9 %collective-permute-start.13 = (bf16[64,1024]{1,0:T(8,128)(2,1)S(1)}, bf16[64,1024]{1,0:T(8,128)(2,1)S(1)}, u32[]{:S(2)}, u32[]{:S(2)}) collective-permute-start(bf16[64,1024]{1,0:T(8,128)(2,1)S(1)} %slice_select_fusion.1), channel_id=1, source_target_pairs={{0,4},{4,0},{8,12},{12,8},{16,20},{20,16},{24,28},{28,24},{1,5},{5... | collective-permute-start | bytes 393224 | tf_op jit(solution)/shard_map/ppermute | solution.py:26
  41.7 0.7 collective-permute-start.12
  42.4 4.0 %collective-permute-done.13 = bf16[64,1024]{1,0:T(8,128)(2,1)S(1)} collective-permute-done((bf16[64,1024]{1,0:T(8,128)(2,1)S(1)}, bf16[64,1024]{1,0:T(8,128)(2,1)S(1)}, u32[]{:S(2)}, u32[]{:S(2)}) %collective-permute-start.13) | collective-permute-done | bytes 131104 | tf_op jit(solution)/shard_map/ppermute | solution.py:26
  46.4 0.0 collective-permute-done.12
  46.5 0.1 collective-permute-start.15
  46.6 1.2 %collective-permute-start.14 = (bf16[64,512]{1,0:T(8,128)(2,1)S(1)}, bf16[64,512]{1,0:T(8,128)(2,1)S(1)}, u32[]{:S(2)}, u32[]{:S(2)}) collective-permute-start(bf16[64,512]{1,0:T(8,128)(2,1)S(1)} %get-tuple-element.86), channel_id=1, source_target_pairs={{0,1},{1,0},{2,3},{3,2},{4,5},{5,4},{6,7},{7,6},{8,9},{9,8},{10,11... | collective-permute-start | bytes 196616 | tf_op jit(solution)/shard_map/ppermute | solution.py:26
  47.8 1.3 %middle_image.3 = (bf16[64,1536]{1,0:T(8,128)(2,1)S(1)}, f32[64,512]{1,0:T(8,128)S(1)}, f32[64,256]{1,0:T(8,128)S(1)}) custom-call(f32[27,16,128]{2,1,0:T(8,128)S(1)} %coefficients.1.coef, bf16[192,2048]{1,0:T(8,128)(2,1)S(1)} %reshape.18.stack, bf16[64,2048]{1,0:T(8,128)(2,1)S(1)} %get-tuple-element.51.block.last, ...), custom_call_target="tpu_custom_call" | custom-call | flops 7077888 | bytes 1925120 | tf_op jit(solution)/shard_map/middle_image/pallas_call | solution.py:468
  49.1 1.6 %collective-permute-done.15 = bf16[64,512]{1,0:T(8,128)(2,1)S(1)} collective-permute-done((bf16[64,512]{1,0:T(8,128)(2,1)S(1)}, bf16[64,512]{1,0:T(8,128)(2,1)S(1)}, u32[]{:S(2)}, u32[]{:S(2)}) %collective-permute-start.15) | collective-permute-done | bytes 65568 | tf_op jit(solution)/shard_map/ppermute | solution.py:27
  50.6 0.0 collective-permute-done.14
  50.7 0.6 second_image.1
  51.3 0.1 collective-permute-start.16
  51.3 1.2 %collective-permute-done.16 = f32[32,256]{1,0:T(8,128)S(1)} collective-permute-done((f32[32,256]{1,0:T(8,128)S(1)}, f32[32,256]{1,0:T(8,128)S(1)}, u32[]{:S(2)}, u32[]{:S(2)}) %collective-permute-start.16) | collective-permute-done | bytes 32800 | tf_op jit(solution)/shard_map/ppermute | solution.py:437
  52.5 4.3 %collective-permute-start.18 = (f32[32,256]{1,0:T(8,128)S(1)}, f32[32,256]{1,0:T(8,128)S(1)}, u32[]{:S(2)}, u32[]{:S(2)}) collective-permute-start(f32[32,256]{1,0:T(8,128)S(1)} %select_add_fusion.1), channel_id=1, source_target_pairs={{0,5},{1,4},{2,7},{3,6},{4,1},{5,0},{6,3},{7,2},{8,13},{9,12},{10,... | collective-permute-start | bytes 98312 | tf_op jit(solution)/shard_map/ppermute | solution.py:437
  56.8 0.6 collective-permute-start.19
  57.5 0.6 collective-permute-start.17
  58.1 0.5 collective-permute-done.18
  58.6 3.1 %collective-permute-done.19 = f32[32,256]{1,0:T(8,128)S(1)} collective-permute-done((f32[32,256]{1,0:T(8,128)S(1)}, f32[32,256]{1,0:T(8,128)S(1)}, u32[]{:S(2)}, u32[]{:S(2)}) %collective-permute-start.19) | collective-permute-done | bytes 32800 | tf_op jit(solution)/shard_map/ppermute | solution.py:437
  61.7 0.1 collective-permute-done.17
  61.8 3.0 %collective-permute-start.21 = (f32[32,256]{1,0:T(8,128)S(1)}, f32[32,256]{1,0:T(8,128)S(1)}, u32[]{:S(2)}, u32[]{:S(2)}) collective-permute-start(f32[32,256]{1,0:T(8,128)S(1)} %add_add_fusion.3), channel_id=1, source_target_pairs={{0,17},{1,16},{2,19},{3,18},{4,21},{5,20},{6,23},{7,22},{8,25},{9,... | collective-permute-start | bytes 98312 | tf_op jit(solution)/shard_map/ppermute | solution.py:437
  64.8 0.5 collective-permute-start.22
  65.3 0.2 collective-permute-start.20
  65.5 1.1 %collective-permute-done.21 = f32[32,256]{1,0:T(8,128)S(1)} collective-permute-done((f32[32,256]{1,0:T(8,128)S(1)}, f32[32,256]{1,0:T(8,128)S(1)}, u32[]{:S(2)}, u32[]{:S(2)}) %collective-permute-start.21) | collective-permute-done | bytes 32800 | tf_op jit(solution)/shard_map/ppermute | solution.py:437
  66.6 4.1 %collective-permute-done.22 = f32[32,256]{1,0:T(8,128)S(1)} collective-permute-done((f32[32,256]{1,0:T(8,128)S(1)}, f32[32,256]{1,0:T(8,128)S(1)}, u32[]{:S(2)}, u32[]{:S(2)}) %collective-permute-start.22) | collective-permute-done | bytes 32800 | tf_op jit(solution)/shard_map/ppermute | solution.py:437
  70.7 0.1 collective-permute-start.23
  70.8 0.4 next_gram.1
  71.2 0.8 %collective-permute-done.23 = f32[32,256]{1,0:T(8,128)S(1)} collective-permute-done((f32[32,256]{1,0:T(8,128)S(1)}, f32[32,256]{1,0:T(8,128)S(1)}, u32[]{:S(2)}, u32[]{:S(2)}) %collective-permute-start.23) | collective-permute-done | bytes 32800 | tf_op jit(solution)/shard_map/ppermute | solution.py:437
  72.0 3.6 %second_solve.1 = (bf16[64,2,8,128]{3,2,1,0:T(8,128)(2,1)}, f32[2,64,192]{2,1,0:T(8,128)}, f32[2,64,64]{2,1,0:T(8,128)}) custom-call(f32[64,256]{1,0:T(8,128)S(1)} %pad_maximum_fusion.5.cross, bf16[192,192]{1,0:T(8,128)(2,1)S(1)} %get-tuple-element.60.own_high, bf16[192,192]{1,0:T(8,128)(2,1)S(1)} %get-tuple-element.61.own_low, ...), custom_call_target="tpu_custom_call" | custom-call | bytes 1982464 | tf_op jit(solution)/shard_map/second_solve/pallas_call | solution.py:468
  (30 shorter events, 0.4 us)
Async XLA Ops:
  0.6 1.0 %slice-start = ((bf16[3,64,2,8,128]{4,3,2,1,0:T(8,128)(2,1)}), bf16[1,64,2,8,128]{4,3,2,1,0:T(8,128)(2,1)S(1)}, s32[]{:S(2)}) async-start(bf16[3,64,2,8,128]{4,3,2,1,0:T(8,128)(2,1)} %param.3), calls=%async_computation | async-start | bytes 524288 | tf_op jit(solution)/shard_map/slice | solution.py:511
  1.6 3.9 %copy-start.2 = (bf16[3,64,2,8,128]{4,3,2,1,0:T(8,128)(2,1)S(1)}, bf16[3,64,2,8,128]{4,3,2,1,0:T(8,128)(2,1)}, u32[]{:S(2)}) copy-start(bf16[3,64,2,8,128]{4,3,2,1,0:T(8,128)(2,1)} %param.3) | copy-start | bytes 2359300
  1.7 6.5 %collective-permute-start.1 = (bf16[64,1024]{1,0:T(8,128)(2,1)S(1)}, bf16[64,1024]{1,0:T(8,128)(2,1)S(1)}, u32[]{:S(2)}, u32[]{:S(2)}) collective-permute-start(bf16[64,1024]{1,0:T(8,128)(2,1)S(1)} %slice_select_fusion), channel_id=1, source_target_pairs={{0,4},{4,0},{8,12},{12,8},{16,20},{20,16},{24,28},{28,24},{1,5},{5... | collective-permute-start | bytes 393224 | tf_op jit(solution)/shard_map/ppermute | solution.py:26
  4.8 3.5 %collective-permute-start = (bf16[64,1024]{1,0:T(8,128)(2,1)S(1)}, bf16[64,1024]{1,0:T(8,128)(2,1)S(1)}, u32[]{:S(2)}, u32[]{:S(2)}) collective-permute-start(bf16[64,1024]{1,0:T(8,128)(2,1)S(1)} %cut.2), channel_id=1, source_target_pairs={{4,8},{8,4},{12,16},{16,12},{20,24},{24,20},{5,9},{9,5},{13,17},{1... | collective-permute-start | bytes 393224 | tf_op jit(solution)/shard_map/ppermute | solution.py:27
  5.8 0.7 copy-start
  6.5 0.7 copy-start.1
  8.3 4.1 %collective-permute-start.3 = (bf16[64,512]{1,0:T(8,128)(2,1)S(1)}, bf16[64,512]{1,0:T(8,128)(2,1)S(1)}, u32[]{:S(2)}, u32[]{:S(2)}) collective-permute-start(bf16[64,512]{1,0:T(8,128)(2,1)S(1)} %get-tuple-element.93), channel_id=1, source_target_pairs={{1,2},{2,1},{0,3},{3,0},{5,6},{6,5},{4,7},{7,4},{9,10},{10,9},{8,1... | collective-permute-start | bytes 196616 | tf_op jit(solution)/shard_map/ppermute | solution.py:27
  8.8 3.7 %collective-permute-start.2 = (bf16[64,512]{1,0:T(8,128)(2,1)S(1)}, bf16[64,512]{1,0:T(8,128)(2,1)S(1)}, u32[]{:S(2)}, u32[]{:S(2)}) collective-permute-start(bf16[64,512]{1,0:T(8,128)(2,1)S(1)} %get-tuple-element.94), channel_id=1, source_target_pairs={{0,1},{1,0},{2,3},{3,2},{4,5},{5,4},{6,7},{7,6},{8,9},{9,8},{10,11... | collective-permute-start | bytes 196616 | tf_op jit(solution)/shard_map/ppermute | solution.py:26
  13.1 1.3 %collective-permute-start.4 = (f32[136,128]{1,0:T(8,128)S(1)}, f32[136,128]{1,0:T(8,128)S(1)}, u32[]{:S(2)}, u32[]{:S(2)}) collective-permute-start(f32[136,128]{1,0:T(8,128)S(1)} %slice_select_fusion.2), channel_id=1, source_target_pairs={{0,1},{1,0},{2,3},{3,2},{4,5},{5,4},{6,7},{7,6},{8,9},{9,8},{10,11... | collective-permute-start | bytes 208904 | tf_op jit(solution)/shard_map/ppermute | solution.py:437
  14.5 7.2 %collective-permute-start.6 = (f32[136,128]{1,0:T(8,128)S(1)}, f32[136,128]{1,0:T(8,128)S(1)}, u32[]{:S(2)}, u32[]{:S(2)}) collective-permute-start(f32[136,128]{1,0:T(8,128)S(1)} %select_add_fusion), channel_id=1, source_target_pairs={{0,5},{1,4},{2,7},{3,6},{4,1},{5,0},{6,3},{7,2},{8,13},{9,12},{10,... | collective-permute-start | bytes 208904 | tf_op jit(solution)/shard_map/ppermute | solution.py:437
  19.1 5.4 %collective-permute-start.7 = (f32[136,128]{1,0:T(8,128)S(1)}, f32[136,128]{1,0:T(8,128)S(1)}, u32[]{:S(2)}, u32[]{:S(2)}) collective-permute-start(f32[136,128]{1,0:T(8,128)S(1)} %select_add_fusion), channel_id=1, source_target_pairs={{0,6},{1,7},{2,4},{3,5},{4,2},{5,3},{6,0},{7,1},{8,14},{9,15},{10,... | collective-permute-start | bytes 208904 | tf_op jit(solution)/shard_map/ppermute | solution.py:437
  20.0 5.9 %collective-permute-start.5 = (f32[136,128]{1,0:T(8,128)S(1)}, f32[136,128]{1,0:T(8,128)S(1)}, u32[]{:S(2)}, u32[]{:S(2)}) collective-permute-start(f32[136,128]{1,0:T(8,128)S(1)} %select_add_fusion), channel_id=1, source_target_pairs={{0,3},{1,2},{2,1},{3,0},{4,7},{5,6},{6,5},{7,4},{8,11},{9,10},{10,... | collective-permute-start | bytes 208904 | tf_op jit(solution)/shard_map/ppermute | solution.py:437
  25.9 5.8 %collective-permute-start.9 = (f32[136,128]{1,0:T(8,128)S(1)}, f32[136,128]{1,0:T(8,128)S(1)}, u32[]{:S(2)}, u32[]{:S(2)}) collective-permute-start(f32[136,128]{1,0:T(8,128)S(1)} %add_add_fusion.1), channel_id=1, source_target_pairs={{0,17},{1,16},{2,19},{3,18},{4,21},{5,20},{6,23},{7,22},{8,25},{9,... | collective-permute-start | bytes 208904 | tf_op jit(solution)/shard_map/ppermute | solution.py:437
  29.1 6.8 %collective-permute-start.10 = (f32[136,128]{1,0:T(8,128)S(1)}, f32[136,128]{1,0:T(8,128)S(1)}, u32[]{:S(2)}, u32[]{:S(2)}) collective-permute-start(f32[136,128]{1,0:T(8,128)S(1)} %add_add_fusion.1), channel_id=1, source_target_pairs={{0,24},{1,25},{2,26},{3,27},{4,28},{5,29},{6,30},{7,31},{8,16},{9,... | collective-permute-start | bytes 208904 | tf_op jit(solution)/shard_map/ppermute | solution.py:437
  30.5 5.7 %collective-permute-start.8 = (f32[136,128]{1,0:T(8,128)S(1)}, f32[136,128]{1,0:T(8,128)S(1)}, u32[]{:S(2)}, u32[]{:S(2)}) collective-permute-start(f32[136,128]{1,0:T(8,128)S(1)} %add_add_fusion.1), channel_id=1, source_target_pairs={{0,9},{1,8},{2,11},{3,10},{4,13},{5,12},{6,15},{7,14},{8,1},{9,0},... | collective-permute-start | bytes 208904 | tf_op jit(solution)/shard_map/ppermute | solution.py:437
  36.2 1.3 %collective-permute-start.11 = (f32[136,128]{1,0:T(8,128)S(1)}, f32[136,128]{1,0:T(8,128)S(1)}, u32[]{:S(2)}, u32[]{:S(2)}) collective-permute-start(f32[136,128]{1,0:T(8,128)S(1)} %add_add_fusion), channel_id=1, source_target_pairs={{0,1},{1,0},{2,3},{3,2},{4,5},{5,4},{6,7},{7,6},{8,9},{9,8},{10,11... | collective-permute-start | bytes 208904 | tf_op jit(solution)/shard_map/ppermute | solution.py:437
  40.8 5.6 %collective-permute-start.13 = (bf16[64,1024]{1,0:T(8,128)(2,1)S(1)}, bf16[64,1024]{1,0:T(8,128)(2,1)S(1)}, u32[]{:S(2)}, u32[]{:S(2)}) collective-permute-start(bf16[64,1024]{1,0:T(8,128)(2,1)S(1)} %slice_select_fusion.1), channel_id=1, source_target_pairs={{0,4},{4,0},{8,12},{12,8},{16,20},{20,16},{24,28},{28,24},{1,5},{5... | collective-permute-start | bytes 393224 | tf_op jit(solution)/shard_map/ppermute | solution.py:26
  41.7 4.7 %collective-permute-start.12 = (bf16[64,1024]{1,0:T(8,128)(2,1)S(1)}, bf16[64,1024]{1,0:T(8,128)(2,1)S(1)}, u32[]{:S(2)}, u32[]{:S(2)}) collective-permute-start(bf16[64,1024]{1,0:T(8,128)(2,1)S(1)} %cut.3), channel_id=1, source_target_pairs={{4,8},{8,4},{12,16},{16,12},{20,24},{24,20},{5,9},{9,5},{13,17},{1... | collective-permute-start | bytes 393224 | tf_op jit(solution)/shard_map/ppermute | solution.py:27
  46.5 4.1 %collective-permute-start.15 = (bf16[64,512]{1,0:T(8,128)(2,1)S(1)}, bf16[64,512]{1,0:T(8,128)(2,1)S(1)}, u32[]{:S(2)}, u32[]{:S(2)}) collective-permute-start(bf16[64,512]{1,0:T(8,128)(2,1)S(1)} %get-tuple-element.85), channel_id=1, source_target_pairs={{1,2},{2,1},{0,3},{3,0},{5,6},{6,5},{4,7},{7,4},{9,10},{10,9},{8,1... | collective-permute-start | bytes 196616 | tf_op jit(solution)/shard_map/ppermute | solution.py:27
  46.6 4.0 %collective-permute-start.14 = (bf16[64,512]{1,0:T(8,128)(2,1)S(1)}, bf16[64,512]{1,0:T(8,128)(2,1)S(1)}, u32[]{:S(2)}, u32[]{:S(2)}) collective-permute-start(bf16[64,512]{1,0:T(8,128)(2,1)S(1)} %get-tuple-element.86), channel_id=1, source_target_pairs={{0,1},{1,0},{2,3},{3,2},{4,5},{5,4},{6,7},{7,6},{8,9},{9,8},{10,11... | collective-permute-start | bytes 196616 | tf_op jit(solution)/shard_map/ppermute | solution.py:26
  51.3 1.3 %collective-permute-start.16 = (f32[32,256]{1,0:T(8,128)S(1)}, f32[32,256]{1,0:T(8,128)S(1)}, u32[]{:S(2)}, u32[]{:S(2)}) collective-permute-start(f32[32,256]{1,0:T(8,128)S(1)} %slice_select_fusion.3), channel_id=1, source_target_pairs={{0,1},{1,0},{2,3},{3,2},{4,5},{5,4},{6,7},{7,6},{8,9},{9,8},{10,11... | collective-permute-start | bytes 98312 | tf_op jit(solution)/shard_map/ppermute | solution.py:437
  52.5 6.1 %collective-permute-start.18 = (f32[32,256]{1,0:T(8,128)S(1)}, f32[32,256]{1,0:T(8,128)S(1)}, u32[]{:S(2)}, u32[]{:S(2)}) collective-permute-start(f32[32,256]{1,0:T(8,128)S(1)} %select_add_fusion.1), channel_id=1, source_target_pairs={{0,5},{1,4},{2,7},{3,6},{4,1},{5,0},{6,3},{7,2},{8,13},{9,12},{10,... | collective-permute-start | bytes 98312 | tf_op jit(solution)/shard_map/ppermute | solution.py:437
  56.8 4.9 %collective-permute-start.19 = (f32[32,256]{1,0:T(8,128)S(1)}, f32[32,256]{1,0:T(8,128)S(1)}, u32[]{:S(2)}, u32[]{:S(2)}) collective-permute-start(f32[32,256]{1,0:T(8,128)S(1)} %select_add_fusion.1), channel_id=1, source_target_pairs={{0,6},{1,7},{2,4},{3,5},{4,2},{5,3},{6,0},{7,1},{8,14},{9,15},{10,... | collective-permute-start | bytes 98312 | tf_op jit(solution)/shard_map/ppermute | solution.py:437
  57.5 4.3 %collective-permute-start.17 = (f32[32,256]{1,0:T(8,128)S(1)}, f32[32,256]{1,0:T(8,128)S(1)}, u32[]{:S(2)}, u32[]{:S(2)}) collective-permute-start(f32[32,256]{1,0:T(8,128)S(1)} %select_add_fusion.1), channel_id=1, source_target_pairs={{0,3},{1,2},{2,1},{3,0},{4,7},{5,6},{6,5},{7,4},{8,11},{9,10},{10,... | collective-permute-start | bytes 98312 | tf_op jit(solution)/shard_map/ppermute | solution.py:437
  61.8 4.8 %collective-permute-start.21 = (f32[32,256]{1,0:T(8,128)S(1)}, f32[32,256]{1,0:T(8,128)S(1)}, u32[]{:S(2)}, u32[]{:S(2)}) collective-permute-start(f32[32,256]{1,0:T(8,128)S(1)} %add_add_fusion.3), channel_id=1, source_target_pairs={{0,17},{1,16},{2,19},{3,18},{4,21},{5,20},{6,23},{7,22},{8,25},{9,... | collective-permute-start | bytes 98312 | tf_op jit(solution)/shard_map/ppermute | solution.py:437
  64.8 5.9 %collective-permute-start.22 = (f32[32,256]{1,0:T(8,128)S(1)}, f32[32,256]{1,0:T(8,128)S(1)}, u32[]{:S(2)}, u32[]{:S(2)}) collective-permute-start(f32[32,256]{1,0:T(8,128)S(1)} %add_add_fusion.3), channel_id=1, source_target_pairs={{0,24},{1,25},{2,26},{3,27},{4,28},{5,29},{6,30},{7,31},{8,16},{9,... | collective-permute-start | bytes 98312 | tf_op jit(solution)/shard_map/ppermute | solution.py:437
  65.3 5.4 %collective-permute-start.20 = (f32[32,256]{1,0:T(8,128)S(1)}, f32[32,256]{1,0:T(8,128)S(1)}, u32[]{:S(2)}, u32[]{:S(2)}) collective-permute-start(f32[32,256]{1,0:T(8,128)S(1)} %add_add_fusion.3), channel_id=1, source_target_pairs={{0,9},{1,8},{2,11},{3,10},{4,13},{5,12},{6,15},{7,14},{8,1},{9,0},... | collective-permute-start | bytes 98312 | tf_op jit(solution)/shard_map/ppermute | solution.py:437
  70.7 1.3 %collective-permute-start.23 = (f32[32,256]{1,0:T(8,128)S(1)}, f32[32,256]{1,0:T(8,128)S(1)}, u32[]{:S(2)}, u32[]{:S(2)}) collective-permute-start(f32[32,256]{1,0:T(8,128)S(1)} %add_add_fusion.2), channel_id=1, source_target_pairs={{0,1},{1,0},{2,3},{3,2},{4,5},{5,4},{6,7},{7,6},{8,9},{9,8},{10,11... | collective-permute-start | bytes 98312 | tf_op jit(solution)/shard_map/ppermute | solution.py:437

commit v22 on v20

--- a/solution.py
+++ b/solution.py
@@ -444,7 +444,7 @@
     bit, upper = 1, 0
     while bit < count:
         upper = upper ^ (index // bit % 2)
-        bit *= 2
+        bit *= 4
     upper = upper == 1
     half = part.shape[0] // 2
     low, high = part[:half], part[half:]
@@ -452,11 +452,11 @@
     bit = 2
     while bit < count:
         if 2 * bit < count:
-            one, two, both = (partner(part, mask) for mask in (bit + 1, 2 * bit + 1, 3 * bit))
+            one, two, both = (partner(part, mask) for mask in (bit, 2 * bit + 1, 3 * bit + 1))
             part = (part + one) + (both + two)
             bit *= 4
         else:
-            part = part + partner(part, bit + 1)
+            part = part + partner(part, bit)
             bit *= 2
     other = partner(part, 1)
     return jnp.concatenate([jnp.where(upper, other, part), jnp.where(upper, part, other)], axis=0)

time: 72.3 us -> 73.1 us (1.011)
  starting transfers between devices: 29.2 us -> 30.5 us
    ppermute x16, starting transfers between devices: 21.3 us -> 22.5 us  [partner(): return lax.ppermute(part, axes, [(i, i ^ mask) for i in range(count)])]
  transfers between devices with their start and end apart: 24 -> 24, of which waited for: 17 -> 19; matrix products, arithmetic and copies ran while one was open for 1% -> 0% of each run, Pallas kernels for 6% -> 6%
where the time goes in v22:
time: 73.1 us; the launch traced here: 72.8 us
  starting transfers between devices  30.5 us (42%)
  waiting for transfers between devices  26.7 us (37%)
  Pallas kernels  12.3 us (17%)
  local copies, waits for them, and re-layouts  2.13 us (3%)
  between operations  0.96 us (1%)
    ppermute x16, starting transfers between devices, partner(): return lax.ppermute(part, axes, [(i, i ^ mask) for i in range(count)])  22.5 us
    ppermute x16, waiting for transfers between devices, partner(): return lax.ppermute(part, axes, [(i, i ^ mask) for i in range(count)])  19.5 us
    pallas_call x8, Pallas kernels, call(): pl.pallas_call(kernel, out_shape=[jax.ShapeDtypeStruct(shape, dtype) for...  11.5 us
    ppermute x4, starting transfers between devices, swaps(): inner = lax.ppermute(near, axis, [(i, i ^ 1) for i in range(count)])  6.1 us
    ppermute x4, waiting for transfers between devices, swaps(): inner = lax.ppermute(near, axis, [(i, i ^ 1) for i in range(count)])  4.67 us
    ppermute x4, waiting for transfers between devices, swaps(): outer = lax.ppermute(far, axis, pairs)  2.53 us
    ppermute x4, starting transfers between devices, swaps(): outer = lax.ppermute(far, axis, pairs)  1.84 us
  transfers between devices with their start and end apart: 24, of which 19 were waited for; matrix products, arithmetic and copies ran while one was open for 0% of the time, Pallas kernels for 6%

profile of v22, /device:TPU:0, one launch (start us, length us, event | category | flops | bytes accessed | tf_op | source)
XLA Modules:
  0.0 72.8 jit_solution(16580513217120384163)
XLA Ops:
  0.6 0.0 slice-start
  0.6 0.9 %slice-done = bf16[1,64,2,8,128]{4,3,2,1,0:T(8,128)(2,1)S(1)} async-done(((bf16[3,64,2,8,128]{4,3,2,1,0:T(8,128)(2,1)}), bf16[1,64,2,8,128]{4,3,2,1,0:T(8,128)(2,1)S(1)}, s32[]{:S(2)}) %slice-start) | async-done | bytes 262168 | tf_op jit(solution)/shard_map/slice | solution.py:511
  1.6 0.1 reshape_squeeze.3.block
  1.7 3.0 %collective-permute-start.1 = (bf16[64,1024]{1,0:T(8,128)(2,1)S(1)}, bf16[64,1024]{1,0:T(8,128)(2,1)S(1)}, u32[]{:S(2)}, u32[]{:S(2)}) collective-permute-start(bf16[64,1024]{1,0:T(8,128)(2,1)S(1)} %slice_select_fusion), channel_id=1, source_target_pairs={{0,4},{4,0},{8,12},{12,8},{16,20},{20,16},{24,28},{28,24},{1,5},{5... | collective-permute-start | bytes 393224 | tf_op jit(solution)/shard_map/ppermute | solution.py:26
  4.8 0.7 collective-permute-start
  5.5 0.3 reshape.18.stack
  5.8 0.0 copy-start
  5.8 0.6 stack_gram.1
  6.5 0.0 copy-start.1
  6.5 0.0 copy-done
  6.5 0.6 copy-done.1
  7.1 0.8 %coefficients.1.coef = f32[27,16,128]{2,1,0:T(8,128)S(1)} custom-call(f32[8,27]{1,0:T(8,128)S(1)} %copy-done.1, s32[16,128]{1,0:T(8,128)S(1)} %bitcast.7), custom_call_target="tpu_custom_call" | custom-call | tf_op jit(solution)/shard_map/coefficients/pallas_call | solution.py:102
  7.9 0.3 collective-permute-done.1
  8.2 0.0 collective-permute-done
  8.3 0.4 collective-permute-start.3
  8.8 1.5 %collective-permute-start.2 = (bf16[64,512]{1,0:T(8,128)(2,1)S(1)}, bf16[64,512]{1,0:T(8,128)(2,1)S(1)}, u32[]{:S(2)}, u32[]{:S(2)}) collective-permute-start(bf16[64,512]{1,0:T(8,128)(2,1)S(1)} %get-tuple-element.94), channel_id=1, source_target_pairs={{0,1},{1,0},{2,3},{3,2},{4,5},{5,4},{6,7},{7,6},{8,9},{9,8},{10,11... | collective-permute-start | bytes 196616 | tf_op jit(solution)/shard_map/ppermute | solution.py:26
  10.3 1.3 %middle_image.2 = (bf16[64,1536]{1,0:T(8,128)(2,1)S(1)}, f32[64,512]{1,0:T(8,128)S(1)}, f32[64,256]{1,0:T(8,128)S(1)}) custom-call(f32[27,16,128]{2,1,0:T(8,128)S(1)} %coefficients.1.coef, bf16[192,2048]{1,0:T(8,128)(2,1)S(1)} %reshape.18.stack, bf16[64,2048]{1,0:T(8,128)(2,1)S(1)} %reshape_squeeze.3.block, bf16[64,1024]{1,0:T(8,128)(2,1)S(1)} %get-tuple-element.44.xlo, ...), custom_call_target="tpu_custom_call" | custom-call | flops 7077888 | bytes 1925120 | tf_op jit(solution)/shard_map/middle_image/pallas_call | solution.py:468
  11.6 0.9 %collective-permute-done.3 = bf16[64,512]{1,0:T(8,128)(2,1)S(1)} collective-permute-done((bf16[64,512]{1,0:T(8,128)(2,1)S(1)}, bf16[64,512]{1,0:T(8,128)(2,1)S(1)}, u32[]{:S(2)}, u32[]{:S(2)}) %collective-permute-start.3) | collective-permute-done | bytes 65568 | tf_op jit(solution)/shard_map/ppermute | solution.py:27
  12.5 0.0 collective-permute-done.2
  12.5 0.6 first_image.1
  13.1 0.2 collective-permute-start.4
  13.3 1.1 %collective-permute-done.4 = f32[136,128]{1,0:T(8,128)S(1)} collective-permute-done((f32[136,128]{1,0:T(8,128)S(1)}, f32[136,128]{1,0:T(8,128)S(1)}, u32[]{:S(2)}, u32[]{:S(2)}) %collective-permute-start.4) | collective-permute-done | bytes 69664 | tf_op jit(solution)/shard_map/ppermute | solution.py:437
  14.5 5.2 %collective-permute-start.6 = (f32[136,128]{1,0:T(8,128)S(1)}, f32[136,128]{1,0:T(8,128)S(1)}, u32[]{:S(2)}, u32[]{:S(2)}) collective-permute-start(f32[136,128]{1,0:T(8,128)S(1)} %select_add_fusion), channel_id=1, source_target_pairs={{0,7},{1,6},{2,5},{3,4},{4,3},{5,2},{6,1},{7,0},{8,15},{9,14},{10,... | collective-permute-start | bytes 208904 | tf_op jit(solution)/shard_map/ppermute | solution.py:437
  19.7 0.0 collective-permute-start.7
  19.7 0.9 %collective-permute-start.5 = (f32[136,128]{1,0:T(8,128)S(1)}, f32[136,128]{1,0:T(8,128)S(1)}, u32[]{:S(2)}, u32[]{:S(2)}) collective-permute-start(f32[136,128]{1,0:T(8,128)S(1)} %select_add_fusion), channel_id=1, source_target_pairs={{0,2},{1,3},{2,0},{3,1},{4,6},{5,7},{6,4},{7,5},{8,10},{9,11},{10,... | collective-permute-start | bytes 208904 | tf_op jit(solution)/shard_map/ppermute | solution.py:437
  20.5 1.7 %collective-permute-done.6 = f32[136,128]{1,0:T(8,128)S(1)} collective-permute-done((f32[136,128]{1,0:T(8,128)S(1)}, f32[136,128]{1,0:T(8,128)S(1)}, u32[]{:S(2)}, u32[]{:S(2)}) %collective-permute-start.6) | collective-permute-done | bytes 69664 | tf_op jit(solution)/shard_map/ppermute | solution.py:437
  22.2 1.4 %collective-permute-done.7 = f32[136,128]{1,0:T(8,128)S(1)} collective-permute-done((f32[136,128]{1,0:T(8,128)S(1)}, f32[136,128]{1,0:T(8,128)S(1)}, u32[]{:S(2)}, u32[]{:S(2)}) %collective-permute-start.7) | collective-permute-done | bytes 69664 | tf_op jit(solution)/shard_map/ppermute | solution.py:437
  23.7 0.4 collective-permute-done.5
  24.1 4.9 %collective-permute-start.9 = (f32[136,128]{1,0:T(8,128)S(1)}, f32[136,128]{1,0:T(8,128)S(1)}, u32[]{:S(2)}, u32[]{:S(2)}) collective-permute-start(f32[136,128]{1,0:T(8,128)S(1)} %add_add_fusion.1), channel_id=1, source_target_pairs={{0,25},{1,24},{2,27},{3,26},{4,29},{5,28},{6,31},{7,30},{8,17},{9,... | collective-permute-start | bytes 208904 | tf_op jit(solution)/shard_map/ppermute | solution.py:437
  29.0 0.0 collective-permute-start.10
  29.0 0.6 collective-permute-start.8
  29.7 2.0 %collective-permute-done.9 = f32[136,128]{1,0:T(8,128)S(1)} collective-permute-done((f32[136,128]{1,0:T(8,128)S(1)}, f32[136,128]{1,0:T(8,128)S(1)}, u32[]{:S(2)}, u32[]{:S(2)}) %collective-permute-start.9) | collective-permute-done | bytes 69664 | tf_op jit(solution)/shard_map/ppermute | solution.py:437
  31.6 4.2 %collective-permute-done.10 = f32[136,128]{1,0:T(8,128)S(1)} collective-permute-done((f32[136,128]{1,0:T(8,128)S(1)}, f32[136,128]{1,0:T(8,128)S(1)}, u32[]{:S(2)}, u32[]{:S(2)}) %collective-permute-start.10) | collective-permute-done | bytes 69664 | tf_op jit(solution)/shard_map/ppermute | solution.py:437
  35.8 0.0 collective-permute-done.8
  35.9 0.2 collective-permute-start.11
  36.1 1.1 %collective-permute-done.11 = f32[136,128]{1,0:T(8,128)S(1)} collective-permute-done((f32[136,128]{1,0:T(8,128)S(1)}, f32[136,128]{1,0:T(8,128)S(1)}, u32[]{:S(2)}, u32[]{:S(2)}) %collective-permute-start.11) | collective-permute-done | bytes 69664 | tf_op jit(solution)/shard_map/ppermute | solution.py:437
  37.2 3.1 %first_solve.1 = (bf16[64,2048]{1,0:T(8,128)(2,1)S(1)}, f32[64,192]{1,0:T(8,128)S(1)}, f32[64,64]{1,0:T(8,128)S(1)}, f32[64,192]{1,0:T(8,128)S(1)}, f32[64,64]{1,0:T(8,128)S(1)}, /*index=5*/bf16[64,64]{1,0:T(8,128)(2,1)S(1)}) custom-call(f32[272,128]{1,0:T(8,128)S(1)} %pad_maximum_fusion.cross, bf16[192,2048]{1,0:T(8,128)(2,1)S(1)} %reshape.18.stack, ...), custom_call_target="tpu_custom_call" | custom-call | bytes 1589248 | tf_op jit(solution)/shard_map/first_solve/pallas_call | solution.py:468
  40.4 0.6 collective-permute-start.13
  41.0 0.7 collective-permute-start.12
  41.7 4.3 %collective-permute-done.13 = bf16[64,1024]{1,0:T(8,128)(2,1)S(1)} collective-permute-done((bf16[64,1024]{1,0:T(8,128)(2,1)S(1)}, bf16[64,1024]{1,0:T(8,128)(2,1)S(1)}, u32[]{:S(2)}, u32[]{:S(2)}) %collective-permute-start.13) | collective-permute-done | bytes 131104 | tf_op jit(solution)/shard_map/ppermute | solution.py:26
  46.1 0.0 collective-permute-done.12
  46.2 0.1 collective-permute-start.15
  46.2 1.0 %collective-permute-start.14 = (bf16[64,512]{1,0:T(8,128)(2,1)S(1)}, bf16[64,512]{1,0:T(8,128)(2,1)S(1)}, u32[]{:S(2)}, u32[]{:S(2)}) collective-permute-start(bf16[64,512]{1,0:T(8,128)(2,1)S(1)} %get-tuple-element.86), channel_id=1, source_target_pairs={{0,1},{1,0},{2,3},{3,2},{4,5},{5,4},{6,7},{7,6},{8,9},{9,8},{10,11... | collective-permute-start | bytes 196616 | tf_op jit(solution)/shard_map/ppermute | solution.py:26
  47.2 1.3 %middle_image.3 = (bf16[64,1536]{1,0:T(8,128)(2,1)S(1)}, f32[64,512]{1,0:T(8,128)S(1)}, f32[64,256]{1,0:T(8,128)S(1)}) custom-call(f32[27,16,128]{2,1,0:T(8,128)S(1)} %coefficients.1.coef, bf16[192,2048]{1,0:T(8,128)(2,1)S(1)} %reshape.18.stack, bf16[64,2048]{1,0:T(8,128)(2,1)S(1)} %get-tuple-element.51.block.last, ...), custom_call_target="tpu_custom_call" | custom-call | flops 7077888 | bytes 1925120 | tf_op jit(solution)/shard_map/middle_image/pallas_call | solution.py:468
  48.5 1.6 %collective-permute-done.15 = bf16[64,512]{1,0:T(8,128)(2,1)S(1)} collective-permute-done((bf16[64,512]{1,0:T(8,128)(2,1)S(1)}, bf16[64,512]{1,0:T(8,128)(2,1)S(1)}, u32[]{:S(2)}, u32[]{:S(2)}) %collective-permute-start.15) | collective-permute-done | bytes 65568 | tf_op jit(solution)/shard_map/ppermute | solution.py:27
  50.1 0.0 collective-permute-done.14
  50.1 0.6 second_image.1
  50.7 0.1 collective-permute-start.16
  50.8 1.2 %collective-permute-done.16 = f32[32,256]{1,0:T(8,128)S(1)} collective-permute-done((f32[32,256]{1,0:T(8,128)S(1)}, f32[32,256]{1,0:T(8,128)S(1)}, u32[]{:S(2)}, u32[]{:S(2)}) %collective-permute-start.16) | collective-permute-done | bytes 32800 | tf_op jit(solution)/shard_map/ppermute | solution.py:437
  52.0 4.8 %collective-permute-start.18 = (f32[32,256]{1,0:T(8,128)S(1)}, f32[32,256]{1,0:T(8,128)S(1)}, u32[]{:S(2)}, u32[]{:S(2)}) collective-permute-start(f32[32,256]{1,0:T(8,128)S(1)} %select_add_fusion.1), channel_id=1, source_target_pairs={{0,7},{1,6},{2,5},{3,4},{4,3},{5,2},{6,1},{7,0},{8,15},{9,14},{10,... | collective-permute-start | bytes 98312 | tf_op jit(solution)/shard_map/ppermute | solution.py:437
  56.8 0.9 %collective-permute-start.17 = (f32[32,256]{1,0:T(8,128)S(1)}, f32[32,256]{1,0:T(8,128)S(1)}, u32[]{:S(2)}, u32[]{:S(2)}) collective-permute-start(f32[32,256]{1,0:T(8,128)S(1)} %select_add_fusion.1), channel_id=1, source_target_pairs={{0,2},{1,3},{2,0},{3,1},{4,6},{5,7},{6,4},{7,5},{8,10},{9,11},{10,... | collective-permute-start | bytes 98312 | tf_op jit(solution)/shard_map/ppermute | solution.py:437
  57.7 0.9 %collective-permute-done.18 = f32[32,256]{1,0:T(8,128)S(1)} collective-permute-done((f32[32,256]{1,0:T(8,128)S(1)}, f32[32,256]{1,0:T(8,128)S(1)}, u32[]{:S(2)}, u32[]{:S(2)}) %collective-permute-start.18) | collective-permute-done | bytes 32800 | tf_op jit(solution)/shard_map/ppermute | solution.py:437
  58.6 1.6 %collective-permute-done.19 = f32[32,256]{1,0:T(8,128)S(1)} collective-permute-done((f32[32,256]{1,0:T(8,128)S(1)}, f32[32,256]{1,0:T(8,128)S(1)}, u32[]{:S(2)}, u32[]{:S(2)}) %collective-permute-start.19) | collective-permute-done | bytes 32800 | tf_op jit(solution)/shard_map/ppermute | solution.py:437
  60.2 0.6 collective-permute-done.17
  60.8 1.7 %collective-permute-start.21 = (f32[32,256]{1,0:T(8,128)S(1)}, f32[32,256]{1,0:T(8,128)S(1)}, u32[]{:S(2)}, u32[]{:S(2)}) collective-permute-start(f32[32,256]{1,0:T(8,128)S(1)} %add_add_fusion.3), channel_id=1, source_target_pairs={{0,25},{1,24},{2,27},{3,26},{4,29},{5,28},{6,31},{7,30},{8,17},{9,... | collective-permute-start | bytes 98312 | tf_op jit(solution)/shard_map/ppermute | solution.py:437
  62.5 1.0 %collective-permute-start.22 = (f32[32,256]{1,0:T(8,128)S(1)}, f32[32,256]{1,0:T(8,128)S(1)}, u32[]{:S(2)}, u32[]{:S(2)}) collective-permute-start(f32[32,256]{1,0:T(8,128)S(1)} %add_add_fusion.3), channel_id=1, source_target_pairs={{0,17},{1,16},{2,19},{3,18},{4,21},{5,20},{6,23},{7,22},{8,25},{9,... | collective-permute-start | bytes 98312 | tf_op jit(solution)/shard_map/ppermute | solution.py:437
  63.5 1.4 %collective-permute-start.20 = (f32[32,256]{1,0:T(8,128)S(1)}, f32[32,256]{1,0:T(8,128)S(1)}, u32[]{:S(2)}, u32[]{:S(2)}) collective-permute-start(f32[32,256]{1,0:T(8,128)S(1)} %add_add_fusion.3), channel_id=1, source_target_pairs={{0,8},{1,9},{2,10},{3,11},{4,12},{5,13},{6,14},{7,15},{8,0},{9,1},... | collective-permute-start | bytes 98312 | tf_op jit(solution)/shard_map/ppermute | solution.py:437
  64.9 1.1 %collective-permute-done.21 = f32[32,256]{1,0:T(8,128)S(1)} collective-permute-done((f32[32,256]{1,0:T(8,128)S(1)}, f32[32,256]{1,0:T(8,128)S(1)}, u32[]{:S(2)}, u32[]{:S(2)}) %collective-permute-start.21) | collective-permute-done | bytes 32800 | tf_op jit(solution)/shard_map/ppermute | solution.py:437
  66.1 1.3 %collective-permute-done.22 = f32[32,256]{1,0:T(8,128)S(1)} collective-permute-done((f32[32,256]{1,0:T(8,128)S(1)}, f32[32,256]{1,0:T(8,128)S(1)}, u32[]{:S(2)}, u32[]{:S(2)}) %collective-permute-start.22) | collective-permute-done | bytes 32800 | tf_op jit(solution)/shard_map/ppermute | solution.py:437
  67.4 0.3 collective-permute-done.20
  67.7 0.6 collective-permute-start.23
  68.3 0.4 next_gram.1
  68.7 0.4 collective-permute-done.23
  69.2 3.6 %second_solve.1 = (bf16[64,2,8,128]{3,2,1,0:T(8,128)(2,1)}, f32[2,64,192]{2,1,0:T(8,128)}, f32[2,64,64]{2,1,0:T(8,128)}) custom-call(f32[64,256]{1,0:T(8,128)S(1)} %pad_maximum_fusion.5.cross, bf16[192,192]{1,0:T(8,128)(2,1)S(1)} %get-tuple-element.60.own_high, bf16[192,192]{1,0:T(8,128)(2,1)S(1)} %get-tuple-element.61.own_low, ...), custom_call_target="tpu_custom_call" | custom-call | bytes 1982464 | tf_op jit(solution)/shard_map/second_solve/pallas_call | solution.py:468
  (30 shorter events, 0.4 us)
Async XLA Ops:
  0.6 1.0 %slice-start = ((bf16[3,64,2,8,128]{4,3,2,1,0:T(8,128)(2,1)}), bf16[1,64,2,8,128]{4,3,2,1,0:T(8,128)(2,1)S(1)}, s32[]{:S(2)}) async-start(bf16[3,64,2,8,128]{4,3,2,1,0:T(8,128)(2,1)} %param.3), calls=%async_computation | async-start | bytes 524288 | tf_op jit(solution)/shard_map/slice | solution.py:511
  1.6 3.9 %copy-start.2 = (bf16[3,64,2,8,128]{4,3,2,1,0:T(8,128)(2,1)S(1)}, bf16[3,64,2,8,128]{4,3,2,1,0:T(8,128)(2,1)}, u32[]{:S(2)}) copy-start(bf16[3,64,2,8,128]{4,3,2,1,0:T(8,128)(2,1)} %param.3) | copy-start | bytes 2359300
  1.7 6.5 %collective-permute-start.1 = (bf16[64,1024]{1,0:T(8,128)(2,1)S(1)}, bf16[64,1024]{1,0:T(8,128)(2,1)S(1)}, u32[]{:S(2)}, u32[]{:S(2)}) collective-permute-start(bf16[64,1024]{1,0:T(8,128)(2,1)S(1)} %slice_select_fusion), channel_id=1, source_target_pairs={{0,4},{4,0},{8,12},{12,8},{16,20},{20,16},{24,28},{28,24},{1,5},{5... | collective-permute-start | bytes 393224 | tf_op jit(solution)/shard_map/ppermute | solution.py:26
  4.8 3.5 %collective-permute-start = (bf16[64,1024]{1,0:T(8,128)(2,1)S(1)}, bf16[64,1024]{1,0:T(8,128)(2,1)S(1)}, u32[]{:S(2)}, u32[]{:S(2)}) collective-permute-start(bf16[64,1024]{1,0:T(8,128)(2,1)S(1)} %cut.2), channel_id=1, source_target_pairs={{4,8},{8,4},{12,16},{16,12},{20,24},{24,20},{5,9},{9,5},{13,17},{1... | collective-permute-start | bytes 393224 | tf_op jit(solution)/shard_map/ppermute | solution.py:27
  5.8 0.7 copy-start
  6.5 0.7 copy-start.1
  8.3 4.1 %collective-permute-start.3 = (bf16[64,512]{1,0:T(8,128)(2,1)S(1)}, bf16[64,512]{1,0:T(8,128)(2,1)S(1)}, u32[]{:S(2)}, u32[]{:S(2)}) collective-permute-start(bf16[64,512]{1,0:T(8,128)(2,1)S(1)} %get-tuple-element.93), channel_id=1, source_target_pairs={{1,2},{2,1},{0,3},{3,0},{5,6},{6,5},{4,7},{7,4},{9,10},{10,9},{8,1... | collective-permute-start | bytes 196616 | tf_op jit(solution)/shard_map/ppermute | solution.py:27
  8.8 3.7 %collective-permute-start.2 = (bf16[64,512]{1,0:T(8,128)(2,1)S(1)}, bf16[64,512]{1,0:T(8,128)(2,1)S(1)}, u32[]{:S(2)}, u32[]{:S(2)}) collective-permute-start(bf16[64,512]{1,0:T(8,128)(2,1)S(1)} %get-tuple-element.94), channel_id=1, source_target_pairs={{0,1},{1,0},{2,3},{3,2},{4,5},{5,4},{6,7},{7,6},{8,9},{9,8},{10,11... | collective-permute-start | bytes 196616 | tf_op jit(solution)/shard_map/ppermute | solution.py:26
  13.1 1.3 %collective-permute-start.4 = (f32[136,128]{1,0:T(8,128)S(1)}, f32[136,128]{1,0:T(8,128)S(1)}, u32[]{:S(2)}, u32[]{:S(2)}) collective-permute-start(f32[136,128]{1,0:T(8,128)S(1)} %slice_select_fusion.2), channel_id=1, source_target_pairs={{0,1},{1,0},{2,3},{3,2},{4,5},{5,4},{6,7},{7,6},{8,9},{9,8},{10,11... | collective-permute-start | bytes 208904 | tf_op jit(solution)/shard_map/ppermute | solution.py:437
  14.5 7.8 %collective-permute-start.6 = (f32[136,128]{1,0:T(8,128)S(1)}, f32[136,128]{1,0:T(8,128)S(1)}, u32[]{:S(2)}, u32[]{:S(2)}) collective-permute-start(f32[136,128]{1,0:T(8,128)S(1)} %select_add_fusion), channel_id=1, source_target_pairs={{0,7},{1,6},{2,5},{3,4},{4,3},{5,2},{6,1},{7,0},{8,15},{9,14},{10,... | collective-permute-start | bytes 208904 | tf_op jit(solution)/shard_map/ppermute | solution.py:437
  19.7 4.0 %collective-permute-start.7 = (f32[136,128]{1,0:T(8,128)S(1)}, f32[136,128]{1,0:T(8,128)S(1)}, u32[]{:S(2)}, u32[]{:S(2)}) collective-permute-start(f32[136,128]{1,0:T(8,128)S(1)} %select_add_fusion), channel_id=1, source_target_pairs={{0,5},{1,4},{2,7},{3,6},{4,1},{5,0},{6,3},{7,2},{8,13},{9,12},{10,... | collective-permute-start | bytes 208904 | tf_op jit(solution)/shard_map/ppermute | solution.py:437
  19.7 4.4 %collective-permute-start.5 = (f32[136,128]{1,0:T(8,128)S(1)}, f32[136,128]{1,0:T(8,128)S(1)}, u32[]{:S(2)}, u32[]{:S(2)}) collective-permute-start(f32[136,128]{1,0:T(8,128)S(1)} %select_add_fusion), channel_id=1, source_target_pairs={{0,2},{1,3},{2,0},{3,1},{4,6},{5,7},{6,4},{7,5},{8,10},{9,11},{10,... | collective-permute-start | bytes 208904 | tf_op jit(solution)/shard_map/ppermute | solution.py:437
  24.1 7.5 %collective-permute-start.9 = (f32[136,128]{1,0:T(8,128)S(1)}, f32[136,128]{1,0:T(8,128)S(1)}, u32[]{:S(2)}, u32[]{:S(2)}) collective-permute-start(f32[136,128]{1,0:T(8,128)S(1)} %add_add_fusion.1), channel_id=1, source_target_pairs={{0,25},{1,24},{2,27},{3,26},{4,29},{5,28},{6,31},{7,30},{8,17},{9,... | collective-permute-start | bytes 208904 | tf_op jit(solution)/shard_map/ppermute | solution.py:437
  29.0 6.8 %collective-permute-start.10 = (f32[136,128]{1,0:T(8,128)S(1)}, f32[136,128]{1,0:T(8,128)S(1)}, u32[]{:S(2)}, u32[]{:S(2)}) collective-permute-start(f32[136,128]{1,0:T(8,128)S(1)} %add_add_fusion.1), channel_id=1, source_target_pairs={{0,17},{1,16},{2,19},{3,18},{4,21},{5,20},{6,23},{7,22},{8,25},{9,... | collective-permute-start | bytes 208904 | tf_op jit(solution)/shard_map/ppermute | solution.py:437
  29.0 6.8 %collective-permute-start.8 = (f32[136,128]{1,0:T(8,128)S(1)}, f32[136,128]{1,0:T(8,128)S(1)}, u32[]{:S(2)}, u32[]{:S(2)}) collective-permute-start(f32[136,128]{1,0:T(8,128)S(1)} %add_add_fusion.1), channel_id=1, source_target_pairs={{0,8},{1,9},{2,10},{3,11},{4,12},{5,13},{6,14},{7,15},{8,0},{9,1},... | collective-permute-start | bytes 208904 | tf_op jit(solution)/shard_map/ppermute | solution.py:437
  35.9 1.3 %collective-permute-start.11 = (f32[136,128]{1,0:T(8,128)S(1)}, f32[136,128]{1,0:T(8,128)S(1)}, u32[]{:S(2)}, u32[]{:S(2)}) collective-permute-start(f32[136,128]{1,0:T(8,128)S(1)} %add_add_fusion), channel_id=1, source_target_pairs={{0,1},{1,0},{2,3},{3,2},{4,5},{5,4},{6,7},{7,6},{8,9},{9,8},{10,11... | collective-permute-start | bytes 208904 | tf_op jit(solution)/shard_map/ppermute | solution.py:437
  40.4 5.6 %collective-permute-start.13 = (bf16[64,1024]{1,0:T(8,128)(2,1)S(1)}, bf16[64,1024]{1,0:T(8,128)(2,1)S(1)}, u32[]{:S(2)}, u32[]{:S(2)}) collective-permute-start(bf16[64,1024]{1,0:T(8,128)(2,1)S(1)} %slice_select_fusion.1), channel_id=1, source_target_pairs={{0,4},{4,0},{8,12},{12,8},{16,20},{20,16},{24,28},{28,24},{1,5},{5... | collective-permute-start | bytes 393224 | tf_op jit(solution)/shard_map/ppermute | solution.py:26
  41.0 5.0 %collective-permute-start.12 = (bf16[64,1024]{1,0:T(8,128)(2,1)S(1)}, bf16[64,1024]{1,0:T(8,128)(2,1)S(1)}, u32[]{:S(2)}, u32[]{:S(2)}) collective-permute-start(bf16[64,1024]{1,0:T(8,128)(2,1)S(1)} %cut.3), channel_id=1, source_target_pairs={{4,8},{8,4},{12,16},{16,12},{20,24},{24,20},{5,9},{9,5},{13,17},{1... | collective-permute-start | bytes 393224 | tf_op jit(solution)/shard_map/ppermute | solution.py:27
  46.2 4.0 %collective-permute-start.15 = (bf16[64,512]{1,0:T(8,128)(2,1)S(1)}, bf16[64,512]{1,0:T(8,128)(2,1)S(1)}, u32[]{:S(2)}, u32[]{:S(2)}) collective-permute-start(bf16[64,512]{1,0:T(8,128)(2,1)S(1)} %get-tuple-element.85), channel_id=1, source_target_pairs={{1,2},{2,1},{0,3},{3,0},{5,6},{6,5},{4,7},{7,4},{9,10},{10,9},{8,1... | collective-permute-start | bytes 196616 | tf_op jit(solution)/shard_map/ppermute | solution.py:27
  46.2 3.9 %collective-permute-start.14 = (bf16[64,512]{1,0:T(8,128)(2,1)S(1)}, bf16[64,512]{1,0:T(8,128)(2,1)S(1)}, u32[]{:S(2)}, u32[]{:S(2)}) collective-permute-start(bf16[64,512]{1,0:T(8,128)(2,1)S(1)} %get-tuple-element.86), channel_id=1, source_target_pairs={{0,1},{1,0},{2,3},{3,2},{4,5},{5,4},{6,7},{7,6},{8,9},{9,8},{10,11... | collective-permute-start | bytes 196616 | tf_op jit(solution)/shard_map/ppermute | solution.py:26
  50.7 1.3 %collective-permute-start.16 = (f32[32,256]{1,0:T(8,128)S(1)}, f32[32,256]{1,0:T(8,128)S(1)}, u32[]{:S(2)}, u32[]{:S(2)}) collective-permute-start(f32[32,256]{1,0:T(8,128)S(1)} %slice_select_fusion.3), channel_id=1, source_target_pairs={{0,1},{1,0},{2,3},{3,2},{4,5},{5,4},{6,7},{7,6},{8,9},{9,8},{10,11... | collective-permute-start | bytes 98312 | tf_op jit(solution)/shard_map/ppermute | solution.py:437
  52.0 6.6 %collective-permute-start.18 = (f32[32,256]{1,0:T(8,128)S(1)}, f32[32,256]{1,0:T(8,128)S(1)}, u32[]{:S(2)}, u32[]{:S(2)}) collective-permute-start(f32[32,256]{1,0:T(8,128)S(1)} %select_add_fusion.1), channel_id=1, source_target_pairs={{0,7},{1,6},{2,5},{3,4},{4,3},{5,2},{6,1},{7,0},{8,15},{9,14},{10,... | collective-permute-start | bytes 98312 | tf_op jit(solution)/shard_map/ppermute | solution.py:437
  56.8 3.3 %collective-permute-start.19 = (f32[32,256]{1,0:T(8,128)S(1)}, f32[32,256]{1,0:T(8,128)S(1)}, u32[]{:S(2)}, u32[]{:S(2)}) collective-permute-start(f32[32,256]{1,0:T(8,128)S(1)} %select_add_fusion.1), channel_id=1, source_target_pairs={{0,5},{1,4},{2,7},{3,6},{4,1},{5,0},{6,3},{7,2},{8,13},{9,12},{10,... | collective-permute-start | bytes 98312 | tf_op jit(solution)/shard_map/ppermute | solution.py:437
  56.8 3.9 %collective-permute-start.17 = (f32[32,256]{1,0:T(8,128)S(1)}, f32[32,256]{1,0:T(8,128)S(1)}, u32[]{:S(2)}, u32[]{:S(2)}) collective-permute-start(f32[32,256]{1,0:T(8,128)S(1)} %select_add_fusion.1), channel_id=1, source_target_pairs={{0,2},{1,3},{2,0},{3,1},{4,6},{5,7},{6,4},{7,5},{8,10},{9,11},{10,... | collective-permute-start | bytes 98312 | tf_op jit(solution)/shard_map/ppermute | solution.py:437
  60.8 5.3 %collective-permute-start.21 = (f32[32,256]{1,0:T(8,128)S(1)}, f32[32,256]{1,0:T(8,128)S(1)}, u32[]{:S(2)}, u32[]{:S(2)}) collective-permute-start(f32[32,256]{1,0:T(8,128)S(1)} %add_add_fusion.3), channel_id=1, source_target_pairs={{0,25},{1,24},{2,27},{3,26},{4,29},{5,28},{6,31},{7,30},{8,17},{9,... | collective-permute-start | bytes 98312 | tf_op jit(solution)/shard_map/ppermute | solution.py:437
  62.5 4.9 %collective-permute-start.22 = (f32[32,256]{1,0:T(8,128)S(1)}, f32[32,256]{1,0:T(8,128)S(1)}, u32[]{:S(2)}, u32[]{:S(2)}) collective-permute-start(f32[32,256]{1,0:T(8,128)S(1)} %add_add_fusion.3), channel_id=1, source_target_pairs={{0,17},{1,16},{2,19},{3,18},{4,21},{5,20},{6,23},{7,22},{8,25},{9,... | collective-permute-start | bytes 98312 | tf_op jit(solution)/shard_map/ppermute | solution.py:437
  63.5 4.2 %collective-permute-start.20 = (f32[32,256]{1,0:T(8,128)S(1)}, f32[32,256]{1,0:T(8,128)S(1)}, u32[]{:S(2)}, u32[]{:S(2)}) collective-permute-start(f32[32,256]{1,0:T(8,128)S(1)} %add_add_fusion.3), channel_id=1, source_target_pairs={{0,8},{1,9},{2,10},{3,11},{4,12},{5,13},{6,14},{7,15},{8,0},{9,1},... | collective-permute-start | bytes 98312 | tf_op jit(solution)/shard_map/ppermute | solution.py:437
  67.7 1.4 %collective-permute-start.23 = (f32[32,256]{1,0:T(8,128)S(1)}, f32[32,256]{1,0:T(8,128)S(1)}, u32[]{:S(2)}, u32[]{:S(2)}) collective-permute-start(f32[32,256]{1,0:T(8,128)S(1)} %add_add_fusion.2), channel_id=1, source_target_pairs={{0,1},{1,0},{2,3},{3,2},{4,5},{5,4},{6,7},{7,6},{8,9},{9,8},{10,11... | collective-permute-start | bytes 98312 | tf_op jit(solution)/shard_map/ppermute | solution.py:437

commit v23 on v20

--- a/solution.py
+++ b/solution.py
@@ -17,20 +17,19 @@
     return lax.dot_general(left, right, dims, preferred_element_type=jnp.float32)
 
 
-def swaps(axis, near, far, closed):
+def swaps(axis, near, far):
     count = lax.axis_size(axis)
     me = lax.axis_index(axis)
     pairs = [(i, (i - 1 ^ 1) + 1) for i in range(1, count - 1)]
-    if closed:
-        pairs += [(0, count - 1), (count - 1, 0)]
     inner = lax.ppermute(near, axis, [(i, i ^ 1) for i in range(count)])
-    outer = lax.ppermute(far, axis, pairs)
-    if closed:
+    outer = lax.ppermute(far, axis, pairs + [(0, count - 1), (count - 1, 0)])
+    if axis == "slab":
+        even = me % 2 == 0
+        low, high = jnp.where(even, outer, inner), jnp.where(even, inner, outer)
+    else:
         odd = me % 2 == 1
         low, high = jnp.where(odd, inner, outer), jnp.where(odd, outer, inner)
-        return jnp.where(me == 0, 0, low), jnp.where(me == count - 1, 0, high)
-    even = me % 2 == 0
-    return jnp.where(even, outer, inner), jnp.where(even, inner, outer)
+    return jnp.where(me == 0, 0, low), jnp.where(me == count - 1, 0, high)
 
 
 def cut_kernel(start, block, part):
@@ -57,7 +56,7 @@
     odd = lax.axis_index("slab") % 2 == 1
     near = jnp.where(odd, block[:, :plane], block[:, top:])
     far = cut(block, jnp.where(odd, top, 0), plane)
-    xlo, xhi = swaps("slab", near, far, False)
+    xlo, xhi = swaps("slab", near, far)
     xlo, xhi, meanwhile = lax.optimization_barrier((xlo, xhi, meanwhile))
 
     def edge(row):
@@ -70,7 +69,7 @@
     odd = lax.axis_index("col") % 2 == 1
     upward, downward = edge(span_y - 1), edge(0)
     ylo, yhi = swaps(
-        "col", jnp.where(odd, downward, upward), jnp.where(odd, upward, downward), True
+        "col", jnp.where(odd, downward, upward), jnp.where(odd, upward, downward)
     )
     return (xlo, xhi), (ylo, yhi), meanwhile
 

time: 72.3 us -> 71.8 us (level)
    ppermute x16, starting transfers between devices: 21.3 us -> 15.4 us  [partner(): return lax.ppermute(part, axes, [(i, i ^ mask) for i in range(count)])]
    ppermute x4, starting transfers between devices: 1.84 us -> 6.81 us  [swaps(): outer = lax.ppermute(far, axis, pairs + [(0, count - 1), (count - 1, 0)])]
    ppermute x4, waiting for transfers between devices: 2.49 us -> 6.67 us  [swaps(): outer = lax.ppermute(far, axis, pairs + [(0, count - 1), (count - 1, 0)])]
    ppermute x16, waiting for transfers between devices: 19.8 us -> 17.6 us  [partner(): return lax.ppermute(part, axes, [(i, i ^ mask) for i in range(count)])]
    ppermute x4, waiting for transfers between devices: 4.86 us -> 2.85 us  [swaps(): inner = lax.ppermute(near, axis, [(i, i ^ 1) for i in range(count)])]
where the time goes in v23:
time: 71.8 us; the launch traced here: 71.6 us
  starting transfers between devices  28.8 us (40%)
  waiting for transfers between devices  27.1 us (38%)
  Pallas kernels  12.3 us (17%)
  local copies, waits for them, and re-layouts  2.13 us (3%)
  between operations  0.95 us (1%)
    ppermute x16, waiting for transfers between devices, partner(): return lax.ppermute(part, axes, [(i, i ^ mask) for i in range(count)])  17.6 us
    ppermute x16, starting transfers between devices, partner(): return lax.ppermute(part, axes, [(i, i ^ mask) for i in range(count)])  15.4 us
    pallas_call x8, Pallas kernels, call(): pl.pallas_call(kernel, out_shape=[jax.ShapeDtypeStruct(shape, dtype) for...  11.5 us
    ppermute x4, starting transfers between devices, swaps(): outer = lax.ppermute(far, axis, pairs + [(0, count - 1), (count - 1, 0)])  6.81 us
    ppermute x4, waiting for transfers between devices, swaps(): outer = lax.ppermute(far, axis, pairs + [(0, count - 1), (count - 1, 0)])  6.67 us
    ppermute x4, starting transfers between devices, swaps(): inner = lax.ppermute(near, axis, [(i, i ^ 1) for i in range(count)])  6.61 us
    ppermute x4, waiting for transfers between devices, swaps(): inner = lax.ppermute(near, axis, [(i, i ^ 1) for i in range(count)])  2.85 us
  transfers between devices with their start and end apart: 24, of which 17 were waited for; matrix products, arithmetic and copies ran while one was open for 1% of the time, Pallas kernels for 6%

profile of v23, /device:TPU:0, one launch (start us, length us, event | category | flops | bytes accessed | tf_op | source)
XLA Modules:
  0.0 71.6 jit_solution(6800867931095297022)
XLA Ops:
  0.6 0.0 slice-start
  0.6 0.9 %slice-done = bf16[1,64,2,8,128]{4,3,2,1,0:T(8,128)(2,1)S(1)} async-done(((bf16[3,64,2,8,128]{4,3,2,1,0:T(8,128)(2,1)}), bf16[1,64,2,8,128]{4,3,2,1,0:T(8,128)(2,1)S(1)}, s32[]{:S(2)}) %slice-start) | async-done | bytes 262168 | tf_op jit(solution)/shard_map/slice | solution.py:510
  1.6 0.1 reshape_squeeze.3.block
  1.7 3.0 %collective-permute-start.1 = (bf16[64,1024]{1,0:T(8,128)(2,1)S(1)}, bf16[64,1024]{1,0:T(8,128)(2,1)S(1)}, u32[]{:S(2)}, u32[]{:S(2)}) collective-permute-start(bf16[64,1024]{1,0:T(8,128)(2,1)S(1)} %slice_select_fusion), channel_id=1, source_target_pairs={{0,4},{4,0},{8,12},{12,8},{16,20},{20,16},{24,28},{28,24},{1,5},{5... | collective-permute-start | bytes 393224 | tf_op jit(solution)/shard_map/ppermute | solution.py:24
  4.8 3.6 %collective-permute-start = (bf16[64,1024]{1,0:T(8,128)(2,1)S(1)}, bf16[64,1024]{1,0:T(8,128)(2,1)S(1)}, u32[]{:S(2)}, u32[]{:S(2)}) collective-permute-start(bf16[64,1024]{1,0:T(8,128)(2,1)S(1)} %cut.2), channel_id=1, source_target_pairs={{4,8},{8,4},{12,16},{16,12},{20,24},{24,20},{0,28},{28,0},{5,9},{9... | collective-permute-start | bytes 393224 | tf_op jit(solution)/shard_map/ppermute | solution.py:25
  8.4 0.3 reshape.18.stack
  8.8 0.0 copy-start
  8.8 0.6 stack_gram.1
  9.4 0.0 copy-start.1
  9.4 0.0 copy-done
  9.5 0.6 copy-done.1
  10.1 0.8 %coefficients.1.coef = f32[27,16,128]{2,1,0:T(8,128)S(1)} custom-call(f32[8,27]{1,0:T(8,128)S(1)} %copy-done.1, s32[16,128]{1,0:T(8,128)S(1)} %bitcast.7), custom_call_target="tpu_custom_call" | custom-call | tf_op jit(solution)/shard_map/coefficients/pallas_call | solution.py:101
  10.9 0.0 collective-permute-done.1
  10.9 1.6 %collective-permute-done = bf16[64,1024]{1,0:T(8,128)(2,1)S(1)} collective-permute-done((bf16[64,1024]{1,0:T(8,128)(2,1)S(1)}, bf16[64,1024]{1,0:T(8,128)(2,1)S(1)}, u32[]{:S(2)}, u32[]{:S(2)}) %collective-permute-start) | collective-permute-done | bytes 131104 | tf_op jit(solution)/shard_map/ppermute | solution.py:25
  12.6 0.1 collective-permute-start.3
  12.7 1.6 %collective-permute-start.2 = (bf16[64,512]{1,0:T(8,128)(2,1)S(1)}, bf16[64,512]{1,0:T(8,128)(2,1)S(1)}, u32[]{:S(2)}, u32[]{:S(2)}) collective-permute-start(bf16[64,512]{1,0:T(8,128)(2,1)S(1)} %get-tuple-element.94), channel_id=1, source_target_pairs={{0,1},{1,0},{2,3},{3,2},{4,5},{5,4},{6,7},{7,6},{8,9},{9,8},{10,11... | collective-permute-start | bytes 196616 | tf_op jit(solution)/shard_map/ppermute | solution.py:24
  14.3 1.3 %middle_image.2 = (bf16[64,1536]{1,0:T(8,128)(2,1)S(1)}, f32[64,512]{1,0:T(8,128)S(1)}, f32[64,256]{1,0:T(8,128)S(1)}) custom-call(f32[27,16,128]{2,1,0:T(8,128)S(1)} %coefficients.1.coef, bf16[192,2048]{1,0:T(8,128)(2,1)S(1)} %reshape.18.stack, bf16[64,2048]{1,0:T(8,128)(2,1)S(1)} %reshape_squeeze.3.block, bf16[64,1024]{1,0:T(8,128)(2,1)S(1)} %get-tuple-element.44.xlo, ...), custom_call_target="tpu_custom_call" | custom-call | flops 7077888 | bytes 1925120 | tf_op jit(solution)/shard_map/middle_image/pallas_call | solution.py:467
  15.6 1.4 %collective-permute-done.3 = bf16[64,512]{1,0:T(8,128)(2,1)S(1)} collective-permute-done((bf16[64,512]{1,0:T(8,128)(2,1)S(1)}, bf16[64,512]{1,0:T(8,128)(2,1)S(1)}, u32[]{:S(2)}, u32[]{:S(2)}) %collective-permute-start.3) | collective-permute-done | bytes 65568 | tf_op jit(solution)/shard_map/ppermute | solution.py:25
  17.0 0.0 collective-permute-done.2
  17.0 0.6 first_image.1
  17.6 0.2 collective-permute-start.4
  17.8 1.1 %collective-permute-done.4 = f32[136,128]{1,0:T(8,128)S(1)} collective-permute-done((f32[136,128]{1,0:T(8,128)S(1)}, f32[136,128]{1,0:T(8,128)S(1)}, u32[]{:S(2)}, u32[]{:S(2)}) %collective-permute-start.4) | collective-permute-done | bytes 69664 | tf_op jit(solution)/shard_map/ppermute | solution.py:436
  19.0 0.7 collective-permute-start.6
  19.7 1.2 %collective-permute-start.7 = (f32[136,128]{1,0:T(8,128)S(1)}, f32[136,128]{1,0:T(8,128)S(1)}, u32[]{:S(2)}, u32[]{:S(2)}) collective-permute-start(f32[136,128]{1,0:T(8,128)S(1)} %select_add_fusion), channel_id=1, source_target_pairs={{0,5},{1,4},{2,7},{3,6},{4,1},{5,0},{6,3},{7,2},{8,13},{9,12},{10,... | collective-permute-start | bytes 208904 | tf_op jit(solution)/shard_map/ppermute | solution.py:436
  20.9 1.4 %collective-permute-start.5 = (f32[136,128]{1,0:T(8,128)S(1)}, f32[136,128]{1,0:T(8,128)S(1)}, u32[]{:S(2)}, u32[]{:S(2)}) collective-permute-start(f32[136,128]{1,0:T(8,128)S(1)} %select_add_fusion), channel_id=1, source_target_pairs={{0,3},{1,2},{2,1},{3,0},{4,7},{5,6},{6,5},{7,4},{8,11},{9,10},{10,... | collective-permute-start | bytes 208904 | tf_op jit(solution)/shard_map/ppermute | solution.py:436
  22.2 2.8 %collective-permute-done.6 = f32[136,128]{1,0:T(8,128)S(1)} collective-permute-done((f32[136,128]{1,0:T(8,128)S(1)}, f32[136,128]{1,0:T(8,128)S(1)}, u32[]{:S(2)}, u32[]{:S(2)}) %collective-permute-start.6) | collective-permute-done | bytes 69664 | tf_op jit(solution)/shard_map/ppermute | solution.py:436
  25.0 0.0 collective-permute-done.7
  25.0 0.5 collective-permute-done.5
  25.5 2.5 %collective-permute-start.9 = (f32[136,128]{1,0:T(8,128)S(1)}, f32[136,128]{1,0:T(8,128)S(1)}, u32[]{:S(2)}, u32[]{:S(2)}) collective-permute-start(f32[136,128]{1,0:T(8,128)S(1)} %add_add_fusion.1), channel_id=1, source_target_pairs={{0,24},{1,25},{2,26},{3,27},{4,28},{5,29},{6,30},{7,31},{8,16},{9,... | collective-permute-start | bytes 208904 | tf_op jit(solution)/shard_map/ppermute | solution.py:436
  28.0 0.0 collective-permute-start.10
  28.0 1.7 %collective-permute-start.8 = (f32[136,128]{1,0:T(8,128)S(1)}, f32[136,128]{1,0:T(8,128)S(1)}, u32[]{:S(2)}, u32[]{:S(2)}) collective-permute-start(f32[136,128]{1,0:T(8,128)S(1)} %add_add_fusion.1), channel_id=1, source_target_pairs={{0,9},{1,8},{2,11},{3,10},{4,13},{5,12},{6,15},{7,14},{8,1},{9,0},... | collective-permute-start | bytes 208904 | tf_op jit(solution)/shard_map/ppermute | solution.py:436
  29.7 2.8 %collective-permute-done.9 = f32[136,128]{1,0:T(8,128)S(1)} collective-permute-done((f32[136,128]{1,0:T(8,128)S(1)}, f32[136,128]{1,0:T(8,128)S(1)}, u32[]{:S(2)}, u32[]{:S(2)}) %collective-permute-start.9) | collective-permute-done | bytes 69664 | tf_op jit(solution)/shard_map/ppermute | solution.py:436
  32.5 2.2 %collective-permute-done.10 = f32[136,128]{1,0:T(8,128)S(1)} collective-permute-done((f32[136,128]{1,0:T(8,128)S(1)}, f32[136,128]{1,0:T(8,128)S(1)}, u32[]{:S(2)}, u32[]{:S(2)}) %collective-permute-start.10) | collective-permute-done | bytes 69664 | tf_op jit(solution)/shard_map/ppermute | solution.py:436
  34.7 0.0 collective-permute-done.8
  34.7 0.2 collective-permute-start.11
  34.9 1.2 %collective-permute-done.11 = f32[136,128]{1,0:T(8,128)S(1)} collective-permute-done((f32[136,128]{1,0:T(8,128)S(1)}, f32[136,128]{1,0:T(8,128)S(1)}, u32[]{:S(2)}, u32[]{:S(2)}) %collective-permute-start.11) | collective-permute-done | bytes 69664 | tf_op jit(solution)/shard_map/ppermute | solution.py:436
  36.1 3.1 %first_solve.1 = (bf16[64,2048]{1,0:T(8,128)(2,1)S(1)}, f32[64,192]{1,0:T(8,128)S(1)}, f32[64,64]{1,0:T(8,128)S(1)}, f32[64,192]{1,0:T(8,128)S(1)}, f32[64,64]{1,0:T(8,128)S(1)}, /*index=5*/bf16[64,64]{1,0:T(8,128)(2,1)S(1)}) custom-call(f32[272,128]{1,0:T(8,128)S(1)} %pad_maximum_fusion.cross, bf16[192,2048]{1,0:T(8,128)(2,1)S(1)} %reshape.18.stack, ...), custom_call_target="tpu_custom_call" | custom-call | bytes 1589248 | tf_op jit(solution)/shard_map/first_solve/pallas_call | solution.py:467
  39.3 0.9 %collective-permute-start.13 = (bf16[64,1024]{1,0:T(8,128)(2,1)S(1)}, bf16[64,1024]{1,0:T(8,128)(2,1)S(1)}, u32[]{:S(2)}, u32[]{:S(2)}) collective-permute-start(bf16[64,1024]{1,0:T(8,128)(2,1)S(1)} %slice_select_fusion.1), channel_id=1, source_target_pairs={{0,4},{4,0},{8,12},{12,8},{16,20},{20,16},{24,28},{28,24},{1,5},{5... | collective-permute-start | bytes 393224 | tf_op jit(solution)/shard_map/ppermute | solution.py:24
  40.1 3.0 %collective-permute-start.12 = (bf16[64,1024]{1,0:T(8,128)(2,1)S(1)}, bf16[64,1024]{1,0:T(8,128)(2,1)S(1)}, u32[]{:S(2)}, u32[]{:S(2)}) collective-permute-start(bf16[64,1024]{1,0:T(8,128)(2,1)S(1)} %cut.3), channel_id=1, source_target_pairs={{4,8},{8,4},{12,16},{16,12},{20,24},{24,20},{0,28},{28,0},{5,9},{9... | collective-permute-start | bytes 393224 | tf_op jit(solution)/shard_map/ppermute | solution.py:25
  43.2 2.8 %collective-permute-done.13 = bf16[64,1024]{1,0:T(8,128)(2,1)S(1)} collective-permute-done((bf16[64,1024]{1,0:T(8,128)(2,1)S(1)}, bf16[64,1024]{1,0:T(8,128)(2,1)S(1)}, u32[]{:S(2)}, u32[]{:S(2)}) %collective-permute-start.13) | collective-permute-done | bytes 131104 | tf_op jit(solution)/shard_map/ppermute | solution.py:24
  46.0 2.1 %collective-permute-done.12 = bf16[64,1024]{1,0:T(8,128)(2,1)S(1)} collective-permute-done((bf16[64,1024]{1,0:T(8,128)(2,1)S(1)}, bf16[64,1024]{1,0:T(8,128)(2,1)S(1)}, u32[]{:S(2)}, u32[]{:S(2)}) %collective-permute-start.12) | collective-permute-done | bytes 131104 | tf_op jit(solution)/shard_map/ppermute | solution.py:25
  48.2 0.1 collective-permute-start.15
  48.3 1.1 %collective-permute-start.14 = (bf16[64,512]{1,0:T(8,128)(2,1)S(1)}, bf16[64,512]{1,0:T(8,128)(2,1)S(1)}, u32[]{:S(2)}, u32[]{:S(2)}) collective-permute-start(bf16[64,512]{1,0:T(8,128)(2,1)S(1)} %get-tuple-element.86), channel_id=1, source_target_pairs={{0,1},{1,0},{2,3},{3,2},{4,5},{5,4},{6,7},{7,6},{8,9},{9,8},{10,11... | collective-permute-start | bytes 196616 | tf_op jit(solution)/shard_map/ppermute | solution.py:24
  49.4 1.3 %middle_image.3 = (bf16[64,1536]{1,0:T(8,128)(2,1)S(1)}, f32[64,512]{1,0:T(8,128)S(1)}, f32[64,256]{1,0:T(8,128)S(1)}) custom-call(f32[27,16,128]{2,1,0:T(8,128)S(1)} %coefficients.1.coef, bf16[192,2048]{1,0:T(8,128)(2,1)S(1)} %reshape.18.stack, bf16[64,2048]{1,0:T(8,128)(2,1)S(1)} %get-tuple-element.51.block.last, ...), custom_call_target="tpu_custom_call" | custom-call | flops 7077888 | bytes 1925120 | tf_op jit(solution)/shard_map/middle_image/pallas_call | solution.py:467
  50.7 1.6 %collective-permute-done.15 = bf16[64,512]{1,0:T(8,128)(2,1)S(1)} collective-permute-done((bf16[64,512]{1,0:T(8,128)(2,1)S(1)}, bf16[64,512]{1,0:T(8,128)(2,1)S(1)}, u32[]{:S(2)}, u32[]{:S(2)}) %collective-permute-start.15) | collective-permute-done | bytes 65568 | tf_op jit(solution)/shard_map/ppermute | solution.py:25
  52.2 0.0 collective-permute-done.14
  52.3 0.6 second_image.1
  52.9 0.1 collective-permute-start.16
  52.9 1.2 %collective-permute-done.16 = f32[32,256]{1,0:T(8,128)S(1)} collective-permute-done((f32[32,256]{1,0:T(8,128)S(1)}, f32[32,256]{1,0:T(8,128)S(1)}, u32[]{:S(2)}, u32[]{:S(2)}) %collective-permute-start.16) | collective-permute-done | bytes 32800 | tf_op jit(solution)/shard_map/ppermute | solution.py:436
  54.1 0.8 %collective-permute-start.18 = (f32[32,256]{1,0:T(8,128)S(1)}, f32[32,256]{1,0:T(8,128)S(1)}, u32[]{:S(2)}, u32[]{:S(2)}) collective-permute-start(f32[32,256]{1,0:T(8,128)S(1)} %select_add_fusion.1), channel_id=1, source_target_pairs={{0,6},{1,7},{2,4},{3,5},{4,2},{5,3},{6,0},{7,1},{8,14},{9,15},{10,... | collective-permute-start | bytes 98312 | tf_op jit(solution)/shard_map/ppermute | solution.py:436
  55.0 1.1 %collective-permute-start.19 = (f32[32,256]{1,0:T(8,128)S(1)}, f32[32,256]{1,0:T(8,128)S(1)}, u32[]{:S(2)}, u32[]{:S(2)}) collective-permute-start(f32[32,256]{1,0:T(8,128)S(1)} %select_add_fusion.1), channel_id=1, source_target_pairs={{0,5},{1,4},{2,7},{3,6},{4,1},{5,0},{6,3},{7,2},{8,13},{9,12},{10,... | collective-permute-start | bytes 98312 | tf_op jit(solution)/shard_map/ppermute | solution.py:436
  56.1 1.2 %collective-permute-start.17 = (f32[32,256]{1,0:T(8,128)S(1)}, f32[32,256]{1,0:T(8,128)S(1)}, u32[]{:S(2)}, u32[]{:S(2)}) collective-permute-start(f32[32,256]{1,0:T(8,128)S(1)} %select_add_fusion.1), channel_id=1, source_target_pairs={{0,3},{1,2},{2,1},{3,0},{4,7},{5,6},{6,5},{7,4},{8,11},{9,10},{10,... | collective-permute-start | bytes 98312 | tf_op jit(solution)/shard_map/ppermute | solution.py:436
  57.4 1.8 %collective-permute-done.18 = f32[32,256]{1,0:T(8,128)S(1)} collective-permute-done((f32[32,256]{1,0:T(8,128)S(1)}, f32[32,256]{1,0:T(8,128)S(1)}, u32[]{:S(2)}, u32[]{:S(2)}) %collective-permute-start.18) | collective-permute-done | bytes 32800 | tf_op jit(solution)/shard_map/ppermute | solution.py:436
  59.1 0.0 collective-permute-done.19
  59.1 0.3 collective-permute-done.17
  59.5 2.4 %collective-permute-start.21 = (f32[32,256]{1,0:T(8,128)S(1)}, f32[32,256]{1,0:T(8,128)S(1)}, u32[]{:S(2)}, u32[]{:S(2)}) collective-permute-start(f32[32,256]{1,0:T(8,128)S(1)} %add_add_fusion.3), channel_id=1, source_target_pairs={{0,24},{1,25},{2,26},{3,27},{4,28},{5,29},{6,30},{7,31},{8,16},{9,... | collective-permute-start | bytes 98312 | tf_op jit(solution)/shard_map/ppermute | solution.py:436
  61.9 0.0 collective-permute-start.22
  61.9 1.8 %collective-permute-start.20 = (f32[32,256]{1,0:T(8,128)S(1)}, f32[32,256]{1,0:T(8,128)S(1)}, u32[]{:S(2)}, u32[]{:S(2)}) collective-permute-start(f32[32,256]{1,0:T(8,128)S(1)} %add_add_fusion.3), channel_id=1, source_target_pairs={{0,9},{1,8},{2,11},{3,10},{4,13},{5,12},{6,15},{7,14},{8,1},{9,0},... | collective-permute-start | bytes 98312 | tf_op jit(solution)/shard_map/ppermute | solution.py:436
  63.7 1.9 %collective-permute-done.21 = f32[32,256]{1,0:T(8,128)S(1)} collective-permute-done((f32[32,256]{1,0:T(8,128)S(1)}, f32[32,256]{1,0:T(8,128)S(1)}, u32[]{:S(2)}, u32[]{:S(2)}) %collective-permute-start.21) | collective-permute-done | bytes 32800 | tf_op jit(solution)/shard_map/ppermute | solution.py:436
  65.5 1.1 %collective-permute-done.22 = f32[32,256]{1,0:T(8,128)S(1)} collective-permute-done((f32[32,256]{1,0:T(8,128)S(1)}, f32[32,256]{1,0:T(8,128)S(1)}, u32[]{:S(2)}, u32[]{:S(2)}) %collective-permute-start.22) | collective-permute-done | bytes 32800 | tf_op jit(solution)/shard_map/ppermute | solution.py:436
  66.7 0.2 collective-permute-start.23
  66.8 0.4 next_gram.1
  67.2 0.7 collective-permute-done.23
  68.0 3.6 %second_solve.1 = (bf16[64,2,8,128]{3,2,1,0:T(8,128)(2,1)}, f32[2,64,192]{2,1,0:T(8,128)}, f32[2,64,64]{2,1,0:T(8,128)}) custom-call(f32[64,256]{1,0:T(8,128)S(1)} %pad_maximum_fusion.5.cross, bf16[192,192]{1,0:T(8,128)(2,1)S(1)} %get-tuple-element.60.own_high, bf16[192,192]{1,0:T(8,128)(2,1)S(1)} %get-tuple-element.61.own_low, ...), custom_call_target="tpu_custom_call" | custom-call | bytes 1982464 | tf_op jit(solution)/shard_map/second_solve/pallas_call | solution.py:467
  (30 shorter events, 0.4 us)
Async XLA Ops:
  0.6 1.0 %slice-start = ((bf16[3,64,2,8,128]{4,3,2,1,0:T(8,128)(2,1)}), bf16[1,64,2,8,128]{4,3,2,1,0:T(8,128)(2,1)S(1)}, s32[]{:S(2)}) async-start(bf16[3,64,2,8,128]{4,3,2,1,0:T(8,128)(2,1)} %param.3), calls=%async_computation | async-start | bytes 524288 | tf_op jit(solution)/shard_map/slice | solution.py:510
  1.6 6.8 %copy-start.2 = (bf16[3,64,2,8,128]{4,3,2,1,0:T(8,128)(2,1)S(1)}, bf16[3,64,2,8,128]{4,3,2,1,0:T(8,128)(2,1)}, u32[]{:S(2)}) copy-start(bf16[3,64,2,8,128]{4,3,2,1,0:T(8,128)(2,1)} %param.3) | copy-start | bytes 2359300
  1.7 9.1 %collective-permute-start.1 = (bf16[64,1024]{1,0:T(8,128)(2,1)S(1)}, bf16[64,1024]{1,0:T(8,128)(2,1)S(1)}, u32[]{:S(2)}, u32[]{:S(2)}) collective-permute-start(bf16[64,1024]{1,0:T(8,128)(2,1)S(1)} %slice_select_fusion), channel_id=1, source_target_pairs={{0,4},{4,0},{8,12},{12,8},{16,20},{20,16},{24,28},{28,24},{1,5},{5... | collective-permute-start | bytes 393224 | tf_op jit(solution)/shard_map/ppermute | solution.py:24
  4.8 7.7 %collective-permute-start = (bf16[64,1024]{1,0:T(8,128)(2,1)S(1)}, bf16[64,1024]{1,0:T(8,128)(2,1)S(1)}, u32[]{:S(2)}, u32[]{:S(2)}) collective-permute-start(bf16[64,1024]{1,0:T(8,128)(2,1)S(1)} %cut.2), channel_id=1, source_target_pairs={{4,8},{8,4},{12,16},{16,12},{20,24},{24,20},{0,28},{28,0},{5,9},{9... | collective-permute-start | bytes 393224 | tf_op jit(solution)/shard_map/ppermute | solution.py:25
  8.8 0.7 copy-start
  9.4 0.7 copy-start.1
  12.6 4.4 %collective-permute-start.3 = (bf16[64,512]{1,0:T(8,128)(2,1)S(1)}, bf16[64,512]{1,0:T(8,128)(2,1)S(1)}, u32[]{:S(2)}, u32[]{:S(2)}) collective-permute-start(bf16[64,512]{1,0:T(8,128)(2,1)S(1)} %get-tuple-element.93), channel_id=1, source_target_pairs={{1,2},{2,1},{0,3},{3,0},{5,6},{6,5},{4,7},{7,4},{9,10},{10,9},{8,1... | collective-permute-start | bytes 196616 | tf_op jit(solution)/shard_map/ppermute | solution.py:25
  12.7 4.3 %collective-permute-start.2 = (bf16[64,512]{1,0:T(8,128)(2,1)S(1)}, bf16[64,512]{1,0:T(8,128)(2,1)S(1)}, u32[]{:S(2)}, u32[]{:S(2)}) collective-permute-start(bf16[64,512]{1,0:T(8,128)(2,1)S(1)} %get-tuple-element.94), channel_id=1, source_target_pairs={{0,1},{1,0},{2,3},{3,2},{4,5},{5,4},{6,7},{7,6},{8,9},{9,8},{10,11... | collective-permute-start | bytes 196616 | tf_op jit(solution)/shard_map/ppermute | solution.py:24
  17.6 1.3 %collective-permute-start.4 = (f32[136,128]{1,0:T(8,128)S(1)}, f32[136,128]{1,0:T(8,128)S(1)}, u32[]{:S(2)}, u32[]{:S(2)}) collective-permute-start(f32[136,128]{1,0:T(8,128)S(1)} %slice_select_fusion.2), channel_id=1, source_target_pairs={{0,1},{1,0},{2,3},{3,2},{4,5},{5,4},{6,7},{7,6},{8,9},{9,8},{10,11... | collective-permute-start | bytes 208904 | tf_op jit(solution)/shard_map/ppermute | solution.py:436
  19.0 6.1 %collective-permute-start.6 = (f32[136,128]{1,0:T(8,128)S(1)}, f32[136,128]{1,0:T(8,128)S(1)}, u32[]{:S(2)}, u32[]{:S(2)}) collective-permute-start(f32[136,128]{1,0:T(8,128)S(1)} %select_add_fusion), channel_id=1, source_target_pairs={{0,6},{1,7},{2,4},{3,5},{4,2},{5,3},{6,0},{7,1},{8,14},{9,15},{10,... | collective-permute-start | bytes 208904 | tf_op jit(solution)/shard_map/ppermute | solution.py:436
  19.7 5.4 %collective-permute-start.7 = (f32[136,128]{1,0:T(8,128)S(1)}, f32[136,128]{1,0:T(8,128)S(1)}, u32[]{:S(2)}, u32[]{:S(2)}) collective-permute-start(f32[136,128]{1,0:T(8,128)S(1)} %select_add_fusion), channel_id=1, source_target_pairs={{0,5},{1,4},{2,7},{3,6},{4,1},{5,0},{6,3},{7,2},{8,13},{9,12},{10,... | collective-permute-start | bytes 208904 | tf_op jit(solution)/shard_map/ppermute | solution.py:436
  20.9 4.6 %collective-permute-start.5 = (f32[136,128]{1,0:T(8,128)S(1)}, f32[136,128]{1,0:T(8,128)S(1)}, u32[]{:S(2)}, u32[]{:S(2)}) collective-permute-start(f32[136,128]{1,0:T(8,128)S(1)} %select_add_fusion), channel_id=1, source_target_pairs={{0,3},{1,2},{2,1},{3,0},{4,7},{5,6},{6,5},{7,4},{8,11},{9,10},{10,... | collective-permute-start | bytes 208904 | tf_op jit(solution)/shard_map/ppermute | solution.py:436
  25.5 6.9 %collective-permute-start.9 = (f32[136,128]{1,0:T(8,128)S(1)}, f32[136,128]{1,0:T(8,128)S(1)}, u32[]{:S(2)}, u32[]{:S(2)}) collective-permute-start(f32[136,128]{1,0:T(8,128)S(1)} %add_add_fusion.1), channel_id=1, source_target_pairs={{0,24},{1,25},{2,26},{3,27},{4,28},{5,29},{6,30},{7,31},{8,16},{9,... | collective-permute-start | bytes 208904 | tf_op jit(solution)/shard_map/ppermute | solution.py:436
  28.0 6.7 %collective-permute-start.10 = (f32[136,128]{1,0:T(8,128)S(1)}, f32[136,128]{1,0:T(8,128)S(1)}, u32[]{:S(2)}, u32[]{:S(2)}) collective-permute-start(f32[136,128]{1,0:T(8,128)S(1)} %add_add_fusion.1), channel_id=1, source_target_pairs={{0,17},{1,16},{2,19},{3,18},{4,21},{5,20},{6,23},{7,22},{8,25},{9,... | collective-permute-start | bytes 208904 | tf_op jit(solution)/shard_map/ppermute | solution.py:436
  28.0 6.7 %collective-permute-start.8 = (f32[136,128]{1,0:T(8,128)S(1)}, f32[136,128]{1,0:T(8,128)S(1)}, u32[]{:S(2)}, u32[]{:S(2)}) collective-permute-start(f32[136,128]{1,0:T(8,128)S(1)} %add_add_fusion.1), channel_id=1, source_target_pairs={{0,9},{1,8},{2,11},{3,10},{4,13},{5,12},{6,15},{7,14},{8,1},{9,0},... | collective-permute-start | bytes 208904 | tf_op jit(solution)/shard_map/ppermute | solution.py:436
  34.7 1.3 %collective-permute-start.11 = (f32[136,128]{1,0:T(8,128)S(1)}, f32[136,128]{1,0:T(8,128)S(1)}, u32[]{:S(2)}, u32[]{:S(2)}) collective-permute-start(f32[136,128]{1,0:T(8,128)S(1)} %add_add_fusion), channel_id=1, source_target_pairs={{0,1},{1,0},{2,3},{3,2},{4,5},{5,4},{6,7},{7,6},{8,9},{9,8},{10,11... | collective-permute-start | bytes 208904 | tf_op jit(solution)/shard_map/ppermute | solution.py:436
  39.3 6.8 %collective-permute-start.13 = (bf16[64,1024]{1,0:T(8,128)(2,1)S(1)}, bf16[64,1024]{1,0:T(8,128)(2,1)S(1)}, u32[]{:S(2)}, u32[]{:S(2)}) collective-permute-start(bf16[64,1024]{1,0:T(8,128)(2,1)S(1)} %slice_select_fusion.1), channel_id=1, source_target_pairs={{0,4},{4,0},{8,12},{12,8},{16,20},{20,16},{24,28},{28,24},{1,5},{5... | collective-permute-start | bytes 393224 | tf_op jit(solution)/shard_map/ppermute | solution.py:24
  40.1 8.0 %collective-permute-start.12 = (bf16[64,1024]{1,0:T(8,128)(2,1)S(1)}, bf16[64,1024]{1,0:T(8,128)(2,1)S(1)}, u32[]{:S(2)}, u32[]{:S(2)}) collective-permute-start(bf16[64,1024]{1,0:T(8,128)(2,1)S(1)} %cut.3), channel_id=1, source_target_pairs={{4,8},{8,4},{12,16},{16,12},{20,24},{24,20},{0,28},{28,0},{5,9},{9... | collective-permute-start | bytes 393224 | tf_op jit(solution)/shard_map/ppermute | solution.py:25
  48.2 4.0 %collective-permute-start.15 = (bf16[64,512]{1,0:T(8,128)(2,1)S(1)}, bf16[64,512]{1,0:T(8,128)(2,1)S(1)}, u32[]{:S(2)}, u32[]{:S(2)}) collective-permute-start(bf16[64,512]{1,0:T(8,128)(2,1)S(1)} %get-tuple-element.85), channel_id=1, source_target_pairs={{1,2},{2,1},{0,3},{3,0},{5,6},{6,5},{4,7},{7,4},{9,10},{10,9},{8,1... | collective-permute-start | bytes 196616 | tf_op jit(solution)/shard_map/ppermute | solution.py:25
  48.3 4.0 %collective-permute-start.14 = (bf16[64,512]{1,0:T(8,128)(2,1)S(1)}, bf16[64,512]{1,0:T(8,128)(2,1)S(1)}, u32[]{:S(2)}, u32[]{:S(2)}) collective-permute-start(bf16[64,512]{1,0:T(8,128)(2,1)S(1)} %get-tuple-element.86), channel_id=1, source_target_pairs={{0,1},{1,0},{2,3},{3,2},{4,5},{5,4},{6,7},{7,6},{8,9},{9,8},{10,11... | collective-permute-start | bytes 196616 | tf_op jit(solution)/shard_map/ppermute | solution.py:24
  52.9 1.3 %collective-permute-start.16 = (f32[32,256]{1,0:T(8,128)S(1)}, f32[32,256]{1,0:T(8,128)S(1)}, u32[]{:S(2)}, u32[]{:S(2)}) collective-permute-start(f32[32,256]{1,0:T(8,128)S(1)} %slice_select_fusion.3), channel_id=1, source_target_pairs={{0,1},{1,0},{2,3},{3,2},{4,5},{5,4},{6,7},{7,6},{8,9},{9,8},{10,11... | collective-permute-start | bytes 98312 | tf_op jit(solution)/shard_map/ppermute | solution.py:436
  54.1 5.0 %collective-permute-start.18 = (f32[32,256]{1,0:T(8,128)S(1)}, f32[32,256]{1,0:T(8,128)S(1)}, u32[]{:S(2)}, u32[]{:S(2)}) collective-permute-start(f32[32,256]{1,0:T(8,128)S(1)} %select_add_fusion.1), channel_id=1, source_target_pairs={{0,6},{1,7},{2,4},{3,5},{4,2},{5,3},{6,0},{7,1},{8,14},{9,15},{10,... | collective-permute-start | bytes 98312 | tf_op jit(solution)/shard_map/ppermute | solution.py:436
  55.0 4.1 %collective-permute-start.19 = (f32[32,256]{1,0:T(8,128)S(1)}, f32[32,256]{1,0:T(8,128)S(1)}, u32[]{:S(2)}, u32[]{:S(2)}) collective-permute-start(f32[32,256]{1,0:T(8,128)S(1)} %select_add_fusion.1), channel_id=1, source_target_pairs={{0,5},{1,4},{2,7},{3,6},{4,1},{5,0},{6,3},{7,2},{8,13},{9,12},{10,... | collective-permute-start | bytes 98312 | tf_op jit(solution)/shard_map/ppermute | solution.py:436
  56.1 3.4 %collective-permute-start.17 = (f32[32,256]{1,0:T(8,128)S(1)}, f32[32,256]{1,0:T(8,128)S(1)}, u32[]{:S(2)}, u32[]{:S(2)}) collective-permute-start(f32[32,256]{1,0:T(8,128)S(1)} %select_add_fusion.1), channel_id=1, source_target_pairs={{0,3},{1,2},{2,1},{3,0},{4,7},{5,6},{6,5},{7,4},{8,11},{9,10},{10,... | collective-permute-start | bytes 98312 | tf_op jit(solution)/shard_map/ppermute | solution.py:436
  59.5 6.0 %collective-permute-start.21 = (f32[32,256]{1,0:T(8,128)S(1)}, f32[32,256]{1,0:T(8,128)S(1)}, u32[]{:S(2)}, u32[]{:S(2)}) collective-permute-start(f32[32,256]{1,0:T(8,128)S(1)} %add_add_fusion.3), channel_id=1, source_target_pairs={{0,24},{1,25},{2,26},{3,27},{4,28},{5,29},{6,30},{7,31},{8,16},{9,... | collective-permute-start | bytes 98312 | tf_op jit(solution)/shard_map/ppermute | solution.py:436
  61.9 4.8 %collective-permute-start.22 = (f32[32,256]{1,0:T(8,128)S(1)}, f32[32,256]{1,0:T(8,128)S(1)}, u32[]{:S(2)}, u32[]{:S(2)}) collective-permute-start(f32[32,256]{1,0:T(8,128)S(1)} %add_add_fusion.3), channel_id=1, source_target_pairs={{0,17},{1,16},{2,19},{3,18},{4,21},{5,20},{6,23},{7,22},{8,25},{9,... | collective-permute-start | bytes 98312 | tf_op jit(solution)/shard_map/ppermute | solution.py:436
  61.9 4.8 %collective-permute-start.20 = (f32[32,256]{1,0:T(8,128)S(1)}, f32[32,256]{1,0:T(8,128)S(1)}, u32[]{:S(2)}, u32[]{:S(2)}) collective-permute-start(f32[32,256]{1,0:T(8,128)S(1)} %add_add_fusion.3), channel_id=1, source_target_pairs={{0,9},{1,8},{2,11},{3,10},{4,13},{5,12},{6,15},{7,14},{8,1},{9,0},... | collective-permute-start | bytes 98312 | tf_op jit(solution)/shard_map/ppermute | solution.py:436
  66.7 1.3 %collective-permute-start.23 = (f32[32,256]{1,0:T(8,128)S(1)}, f32[32,256]{1,0:T(8,128)S(1)}, u32[]{:S(2)}, u32[]{:S(2)}) collective-permute-start(f32[32,256]{1,0:T(8,128)S(1)} %add_add_fusion.2), channel_id=1, source_target_pairs={{0,1},{1,0},{2,3},{3,2},{4,5},{5,4},{6,7},{7,6},{8,9},{9,8},{10,11... | collective-permute-start | bytes 98312 | tf_op jit(solution)/shard_map/ppermute | solution.py:436

commit v24 on v23

--- a/solution.py
+++ b/solution.py
@@ -24,8 +24,8 @@
     inner = lax.ppermute(near, axis, [(i, i ^ 1) for i in range(count)])
     outer = lax.ppermute(far, axis, pairs + [(0, count - 1), (count - 1, 0)])
     if axis == "slab":
-        even = me % 2 == 0
-        low, high = jnp.where(even, outer, inner), jnp.where(even, inner, outer)
+        odd = me % 2 == 1
+        low, high = jnp.where(odd, inner, outer), jnp.where(odd, outer, inner)
     else:
         odd = me % 2 == 1
         low, high = jnp.where(odd, inner, outer), jnp.where(odd, outer, inner)

time: 71.8 us -> 74.8 us (1.042)
  waiting for transfers between devices: 27.1 us -> 32.7 us
  starting transfers between devices: 28.8 us -> 26.2 us
    ppermute x4, starting transfers between devices: 6.61 us -> 1.74 us  [swaps(): inner = lax.ppermute(near, axis, [(i, i ^ 1) for i in range(count)])]
    ppermute x4, waiting for transfers between devices: 6.67 us -> 10.5 us  [swaps(): outer = lax.ppermute(far, axis, pairs + [(0, count - 1), (count - 1, 0)])]
    ppermute x4, starting transfers between devices: 6.81 us -> 9.07 us  [swaps(): outer = lax.ppermute(far, axis, pairs + [(0, count - 1), (count - 1, 0)])]
    ppermute x4, waiting for transfers between devices: 2.85 us -> 4.31 us  [swaps(): inner = lax.ppermute(near, axis, [(i, i ^ 1) for i in range(count)])]
  transfers between devices with their start and end apart: 24 -> 24, of which waited for: 17 -> 18; matrix products, arithmetic and copies ran while one was open for 1% -> 1% of each run, Pallas kernels for 6% -> 6%
where the time goes in v24:
time: 74.8 us; the launch traced here: 74.6 us
  waiting for transfers between devices  32.7 us (44%)
  starting transfers between devices  26.2 us (35%)
  Pallas kernels  12.3 us (16%)
  local copies, waits for them, and re-layouts  2.13 us (3%)
  between operations  0.96 us (1%)
    ppermute x16, waiting for transfers between devices, partner(): return lax.ppermute(part, axes, [(i, i ^ mask) for i in range(count)])  17.9 us
    ppermute x16, starting transfers between devices, partner(): return lax.ppermute(part, axes, [(i, i ^ mask) for i in range(count)])  15.4 us
    pallas_call x8, Pallas kernels, call(): pl.pallas_call(kernel, out_shape=[jax.ShapeDtypeStruct(shape, dtype) for...  11.5 us
    ppermute x4, waiting for transfers between devices, swaps(): outer = lax.ppermute(far, axis, pairs + [(0, count - 1), (count - 1, 0)])  10.5 us
    ppermute x4, starting transfers between devices, swaps(): outer = lax.ppermute(far, axis, pairs + [(0, count - 1), (count - 1, 0)])  9.07 us
    ppermute x4, waiting for transfers between devices, swaps(): inner = lax.ppermute(near, axis, [(i, i ^ 1) for i in range(count)])  4.31 us
    ppermute x4, starting transfers between devices, swaps(): inner = lax.ppermute(near, axis, [(i, i ^ 1) for i in range(count)])  1.74 us
  transfers between devices with their start and end apart: 24, of which 18 were waited for; matrix products, arithmetic and copies ran while one was open for 1% of the time, Pallas kernels for 6%

profile of v24, /device:TPU:0, one launch (start us, length us, event | category | flops | bytes accessed | tf_op | source)
XLA Modules:
  0.0 74.6 jit_solution(16140037306500898086)
XLA Ops:
  0.6 0.0 slice-start
  0.7 0.9 %slice-done = bf16[1,64,2,8,128]{4,3,2,1,0:T(8,128)(2,1)S(1)} async-done(((bf16[3,64,2,8,128]{4,3,2,1,0:T(8,128)(2,1)}), bf16[1,64,2,8,128]{4,3,2,1,0:T(8,128)(2,1)S(1)}, s32[]{:S(2)}) %slice-start) | async-done | bytes 262168 | tf_op jit(solution)/shard_map/slice | solution.py:510
  1.6 0.1 reshape_squeeze.3.block
  1.7 6.0 %collective-permute-start.1 = (bf16[64,1024]{1,0:T(8,128)(2,1)S(1)}, bf16[64,1024]{1,0:T(8,128)(2,1)S(1)}, u32[]{:S(2)}, u32[]{:S(2)}) collective-permute-start(bf16[64,1024]{1,0:T(8,128)(2,1)S(1)} %cut.2), channel_id=1, source_target_pairs={{4,8},{8,4},{12,16},{16,12},{20,24},{24,20},{0,28},{28,0},{5,9},{9... | collective-permute-start | bytes 393224 | tf_op jit(solution)/shard_map/ppermute | solution.py:25
  7.8 0.1 collective-permute-start
  7.9 0.3 reshape.18.stack
  8.3 0.0 copy-start
  8.3 0.6 stack_gram.1
  8.9 0.0 copy-start.1
  8.9 0.0 copy-done
  9.0 0.6 copy-done.1
  9.6 0.8 %coefficients.1.coef = f32[27,16,128]{2,1,0:T(8,128)S(1)} custom-call(f32[8,27]{1,0:T(8,128)S(1)} %copy-done.1, s32[16,128]{1,0:T(8,128)S(1)} %bitcast.7), custom_call_target="tpu_custom_call" | custom-call | tf_op jit(solution)/shard_map/coefficients/pallas_call | solution.py:101
  10.4 1.0 %collective-permute-done.1 = bf16[64,1024]{1,0:T(8,128)(2,1)S(1)} collective-permute-done((bf16[64,1024]{1,0:T(8,128)(2,1)S(1)}, bf16[64,1024]{1,0:T(8,128)(2,1)S(1)}, u32[]{:S(2)}, u32[]{:S(2)}) %collective-permute-start.1) | collective-permute-done | bytes 131104 | tf_op jit(solution)/shard_map/ppermute | solution.py:25
  11.4 2.7 %collective-permute-done = bf16[64,1024]{1,0:T(8,128)(2,1)S(1)} collective-permute-done((bf16[64,1024]{1,0:T(8,128)(2,1)S(1)}, bf16[64,1024]{1,0:T(8,128)(2,1)S(1)}, u32[]{:S(2)}, u32[]{:S(2)}) %collective-permute-start) | collective-permute-done | bytes 131104 | tf_op jit(solution)/shard_map/ppermute | solution.py:24
  14.2 1.2 %collective-permute-start.3 = (bf16[64,512]{1,0:T(8,128)(2,1)S(1)}, bf16[64,512]{1,0:T(8,128)(2,1)S(1)}, u32[]{:S(2)}, u32[]{:S(2)}) collective-permute-start(bf16[64,512]{1,0:T(8,128)(2,1)S(1)} %get-tuple-element.93), channel_id=1, source_target_pairs={{1,2},{2,1},{0,3},{3,0},{5,6},{6,5},{4,7},{7,4},{9,10},{10,9},{8,1... | collective-permute-start | bytes 196616 | tf_op jit(solution)/shard_map/ppermute | solution.py:25
  15.3 0.5 collective-permute-start.2
  15.9 1.3 %middle_image.2 = (bf16[64,1536]{1,0:T(8,128)(2,1)S(1)}, f32[64,512]{1,0:T(8,128)S(1)}, f32[64,256]{1,0:T(8,128)S(1)}) custom-call(f32[27,16,128]{2,1,0:T(8,128)S(1)} %coefficients.1.coef, bf16[192,2048]{1,0:T(8,128)(2,1)S(1)} %reshape.18.stack, bf16[64,2048]{1,0:T(8,128)(2,1)S(1)} %reshape_squeeze.3.block, bf16[64,1024]{1,0:T(8,128)(2,1)S(1)} %get-tuple-element.44.xlo, ...), custom_call_target="tpu_custom_call" | custom-call | flops 7077888 | bytes 1925120 | tf_op jit(solution)/shard_map/middle_image/pallas_call | solution.py:467
  17.1 1.3 %collective-permute-done.3 = bf16[64,512]{1,0:T(8,128)(2,1)S(1)} collective-permute-done((bf16[64,512]{1,0:T(8,128)(2,1)S(1)}, bf16[64,512]{1,0:T(8,128)(2,1)S(1)}, u32[]{:S(2)}, u32[]{:S(2)}) %collective-permute-start.3) | collective-permute-done | bytes 65568 | tf_op jit(solution)/shard_map/ppermute | solution.py:25
  18.5 0.0 collective-permute-done.2
  18.5 0.6 first_image.1
  19.1 0.2 collective-permute-start.4
  19.3 1.1 %collective-permute-done.4 = f32[136,128]{1,0:T(8,128)S(1)} collective-permute-done((f32[136,128]{1,0:T(8,128)S(1)}, f32[136,128]{1,0:T(8,128)S(1)}, u32[]{:S(2)}, u32[]{:S(2)}) %collective-permute-start.4) | collective-permute-done | bytes 69664 | tf_op jit(solution)/shard_map/ppermute | solution.py:436
  20.5 0.7 collective-permute-start.6
  21.2 1.9 %collective-permute-start.7 = (f32[136,128]{1,0:T(8,128)S(1)}, f32[136,128]{1,0:T(8,128)S(1)}, u32[]{:S(2)}, u32[]{:S(2)}) collective-permute-start(f32[136,128]{1,0:T(8,128)S(1)} %select_add_fusion), channel_id=1, source_target_pairs={{0,5},{1,4},{2,7},{3,6},{4,1},{5,0},{6,3},{7,2},{8,13},{9,12},{10,... | collective-permute-start | bytes 208904 | tf_op jit(solution)/shard_map/ppermute | solution.py:436
  23.0 0.7 collective-permute-start.5
  23.8 2.8 %collective-permute-done.6 = f32[136,128]{1,0:T(8,128)S(1)} collective-permute-done((f32[136,128]{1,0:T(8,128)S(1)}, f32[136,128]{1,0:T(8,128)S(1)}, u32[]{:S(2)}, u32[]{:S(2)}) %collective-permute-start.6) | collective-permute-done | bytes 69664 | tf_op jit(solution)/shard_map/ppermute | solution.py:436
  26.5 0.0 collective-permute-done.7
  26.5 0.6 collective-permute-done.5
  27.2 1.5 %collective-permute-start.9 = (f32[136,128]{1,0:T(8,128)S(1)}, f32[136,128]{1,0:T(8,128)S(1)}, u32[]{:S(2)}, u32[]{:S(2)}) collective-permute-start(f32[136,128]{1,0:T(8,128)S(1)} %add_add_fusion.1), channel_id=1, source_target_pairs={{0,24},{1,25},{2,26},{3,27},{4,28},{5,29},{6,30},{7,31},{8,16},{9,... | collective-permute-start | bytes 208904 | tf_op jit(solution)/shard_map/ppermute | solution.py:436
  28.7 0.0 collective-permute-start.10
  28.7 2.7 %collective-permute-start.8 = (f32[136,128]{1,0:T(8,128)S(1)}, f32[136,128]{1,0:T(8,128)S(1)}, u32[]{:S(2)}, u32[]{:S(2)}) collective-permute-start(f32[136,128]{1,0:T(8,128)S(1)} %add_add_fusion.1), channel_id=1, source_target_pairs={{0,9},{1,8},{2,11},{3,10},{4,13},{5,12},{6,15},{7,14},{8,1},{9,0},... | collective-permute-start | bytes 208904 | tf_op jit(solution)/shard_map/ppermute | solution.py:436
  31.4 2.8 %collective-permute-done.9 = f32[136,128]{1,0:T(8,128)S(1)} collective-permute-done((f32[136,128]{1,0:T(8,128)S(1)}, f32[136,128]{1,0:T(8,128)S(1)}, u32[]{:S(2)}, u32[]{:S(2)}) %collective-permute-start.9) | collective-permute-done | bytes 69664 | tf_op jit(solution)/shard_map/ppermute | solution.py:436
  34.2 2.3 %collective-permute-done.10 = f32[136,128]{1,0:T(8,128)S(1)} collective-permute-done((f32[136,128]{1,0:T(8,128)S(1)}, f32[136,128]{1,0:T(8,128)S(1)}, u32[]{:S(2)}, u32[]{:S(2)}) %collective-permute-start.10) | collective-permute-done | bytes 69664 | tf_op jit(solution)/shard_map/ppermute | solution.py:436
  36.5 0.0 collective-permute-done.8
  36.5 0.2 collective-permute-start.11
  36.7 1.1 %collective-permute-done.11 = f32[136,128]{1,0:T(8,128)S(1)} collective-permute-done((f32[136,128]{1,0:T(8,128)S(1)}, f32[136,128]{1,0:T(8,128)S(1)}, u32[]{:S(2)}, u32[]{:S(2)}) %collective-permute-start.11) | collective-permute-done | bytes 69664 | tf_op jit(solution)/shard_map/ppermute | solution.py:436
  37.9 3.1 %first_solve.1 = (bf16[64,2048]{1,0:T(8,128)(2,1)S(1)}, f32[64,192]{1,0:T(8,128)S(1)}, f32[64,64]{1,0:T(8,128)S(1)}, f32[64,192]{1,0:T(8,128)S(1)}, f32[64,64]{1,0:T(8,128)S(1)}, /*index=5*/bf16[64,64]{1,0:T(8,128)(2,1)S(1)}) custom-call(f32[272,128]{1,0:T(8,128)S(1)} %pad_maximum_fusion.cross, bf16[192,2048]{1,0:T(8,128)(2,1)S(1)} %reshape.18.stack, ...), custom_call_target="tpu_custom_call" | custom-call | bytes 1589248 | tf_op jit(solution)/shard_map/first_solve/pallas_call | solution.py:467
  41.1 1.8 %collective-permute-start.13 = (bf16[64,1024]{1,0:T(8,128)(2,1)S(1)}, bf16[64,1024]{1,0:T(8,128)(2,1)S(1)}, u32[]{:S(2)}, u32[]{:S(2)}) collective-permute-start(bf16[64,1024]{1,0:T(8,128)(2,1)S(1)} %cut.3), channel_id=1, source_target_pairs={{4,8},{8,4},{12,16},{16,12},{20,24},{24,20},{0,28},{28,0},{5,9},{9... | collective-permute-start | bytes 393224 | tf_op jit(solution)/shard_map/ppermute | solution.py:25
  42.9 0.0 collective-permute-start.12
  42.9 6.6 %collective-permute-done.13 = bf16[64,1024]{1,0:T(8,128)(2,1)S(1)} collective-permute-done((bf16[64,1024]{1,0:T(8,128)(2,1)S(1)}, bf16[64,1024]{1,0:T(8,128)(2,1)S(1)}, u32[]{:S(2)}, u32[]{:S(2)}) %collective-permute-start.13) | collective-permute-done | bytes 131104 | tf_op jit(solution)/shard_map/ppermute | solution.py:25
  49.5 1.6 %collective-permute-done.12 = bf16[64,1024]{1,0:T(8,128)(2,1)S(1)} collective-permute-done((bf16[64,1024]{1,0:T(8,128)(2,1)S(1)}, bf16[64,1024]{1,0:T(8,128)(2,1)S(1)}, u32[]{:S(2)}, u32[]{:S(2)}) %collective-permute-start.12) | collective-permute-done | bytes 131104 | tf_op jit(solution)/shard_map/ppermute | solution.py:24
  51.2 0.1 collective-permute-start.15
  51.3 1.1 %collective-permute-start.14 = (bf16[64,512]{1,0:T(8,128)(2,1)S(1)}, bf16[64,512]{1,0:T(8,128)(2,1)S(1)}, u32[]{:S(2)}, u32[]{:S(2)}) collective-permute-start(bf16[64,512]{1,0:T(8,128)(2,1)S(1)} %get-tuple-element.86), channel_id=1, source_target_pairs={{0,1},{1,0},{2,3},{3,2},{4,5},{5,4},{6,7},{7,6},{8,9},{9,8},{10,11... | collective-permute-start | bytes 196616 | tf_op jit(solution)/shard_map/ppermute | solution.py:24
  52.4 1.3 %middle_image.3 = (bf16[64,1536]{1,0:T(8,128)(2,1)S(1)}, f32[64,512]{1,0:T(8,128)S(1)}, f32[64,256]{1,0:T(8,128)S(1)}) custom-call(f32[27,16,128]{2,1,0:T(8,128)S(1)} %coefficients.1.coef, bf16[192,2048]{1,0:T(8,128)(2,1)S(1)} %reshape.18.stack, bf16[64,2048]{1,0:T(8,128)(2,1)S(1)} %get-tuple-element.51.block.last, ...), custom_call_target="tpu_custom_call" | custom-call | flops 7077888 | bytes 1925120 | tf_op jit(solution)/shard_map/middle_image/pallas_call | solution.py:467
  53.6 1.6 %collective-permute-done.15 = bf16[64,512]{1,0:T(8,128)(2,1)S(1)} collective-permute-done((bf16[64,512]{1,0:T(8,128)(2,1)S(1)}, bf16[64,512]{1,0:T(8,128)(2,1)S(1)}, u32[]{:S(2)}, u32[]{:S(2)}) %collective-permute-start.15) | collective-permute-done | bytes 65568 | tf_op jit(solution)/shard_map/ppermute | solution.py:25
  55.2 0.0 collective-permute-done.14
  55.2 0.6 second_image.1
  55.8 0.1 collective-permute-start.16
  55.9 1.2 %collective-permute-done.16 = f32[32,256]{1,0:T(8,128)S(1)} collective-permute-done((f32[32,256]{1,0:T(8,128)S(1)}, f32[32,256]{1,0:T(8,128)S(1)}, u32[]{:S(2)}, u32[]{:S(2)}) %collective-permute-start.16) | collective-permute-done | bytes 32800 | tf_op jit(solution)/shard_map/ppermute | solution.py:436
  57.1 0.2 collective-permute-start.18
  57.3 1.8 %collective-permute-start.19 = (f32[32,256]{1,0:T(8,128)S(1)}, f32[32,256]{1,0:T(8,128)S(1)}, u32[]{:S(2)}, u32[]{:S(2)}) collective-permute-start(f32[32,256]{1,0:T(8,128)S(1)} %select_add_fusion.1), channel_id=1, source_target_pairs={{0,5},{1,4},{2,7},{3,6},{4,1},{5,0},{6,3},{7,2},{8,13},{9,12},{10,... | collective-permute-start | bytes 98312 | tf_op jit(solution)/shard_map/ppermute | solution.py:436
  59.1 1.2 %collective-permute-start.17 = (f32[32,256]{1,0:T(8,128)S(1)}, f32[32,256]{1,0:T(8,128)S(1)}, u32[]{:S(2)}, u32[]{:S(2)}) collective-permute-start(f32[32,256]{1,0:T(8,128)S(1)} %select_add_fusion.1), channel_id=1, source_target_pairs={{0,3},{1,2},{2,1},{3,0},{4,7},{5,6},{6,5},{7,4},{8,11},{9,10},{10,... | collective-permute-start | bytes 98312 | tf_op jit(solution)/shard_map/ppermute | solution.py:436
  60.3 1.6 %collective-permute-done.18 = f32[32,256]{1,0:T(8,128)S(1)} collective-permute-done((f32[32,256]{1,0:T(8,128)S(1)}, f32[32,256]{1,0:T(8,128)S(1)}, u32[]{:S(2)}, u32[]{:S(2)}) %collective-permute-start.18) | collective-permute-done | bytes 32800 | tf_op jit(solution)/shard_map/ppermute | solution.py:436
  61.9 0.0 collective-permute-done.19
  61.9 0.5 collective-permute-done.17
  62.4 2.6 %collective-permute-start.21 = (f32[32,256]{1,0:T(8,128)S(1)}, f32[32,256]{1,0:T(8,128)S(1)}, u32[]{:S(2)}, u32[]{:S(2)}) collective-permute-start(f32[32,256]{1,0:T(8,128)S(1)} %add_add_fusion.3), channel_id=1, source_target_pairs={{0,24},{1,25},{2,26},{3,27},{4,28},{5,29},{6,30},{7,31},{8,16},{9,... | collective-permute-start | bytes 98312 | tf_op jit(solution)/shard_map/ppermute | solution.py:436
  65.1 1.5 %collective-permute-start.20 = (f32[32,256]{1,0:T(8,128)S(1)}, f32[32,256]{1,0:T(8,128)S(1)}, u32[]{:S(2)}, u32[]{:S(2)}) collective-permute-start(f32[32,256]{1,0:T(8,128)S(1)} %add_add_fusion.3), channel_id=1, source_target_pairs={{0,9},{1,8},{2,11},{3,10},{4,13},{5,12},{6,15},{7,14},{8,1},{9,0},... | collective-permute-start | bytes 98312 | tf_op jit(solution)/shard_map/ppermute | solution.py:436
  66.6 2.0 %collective-permute-done.21 = f32[32,256]{1,0:T(8,128)S(1)} collective-permute-done((f32[32,256]{1,0:T(8,128)S(1)}, f32[32,256]{1,0:T(8,128)S(1)}, u32[]{:S(2)}, u32[]{:S(2)}) %collective-permute-start.21) | collective-permute-done | bytes 32800 | tf_op jit(solution)/shard_map/ppermute | solution.py:436
  68.6 1.1 %collective-permute-done.22 = f32[32,256]{1,0:T(8,128)S(1)} collective-permute-done((f32[32,256]{1,0:T(8,128)S(1)}, f32[32,256]{1,0:T(8,128)S(1)}, u32[]{:S(2)}, u32[]{:S(2)}) %collective-permute-start.22) | collective-permute-done | bytes 32800 | tf_op jit(solution)/shard_map/ppermute | solution.py:436
  69.7 0.0 collective-permute-done.20
  69.7 0.1 collective-permute-start.23
  69.8 0.4 next_gram.1
  70.2 0.7 collective-permute-done.23
  71.0 3.6 %second_solve.1 = (bf16[64,2,8,128]{3,2,1,0:T(8,128)(2,1)}, f32[2,64,192]{2,1,0:T(8,128)}, f32[2,64,64]{2,1,0:T(8,128)}) custom-call(f32[64,256]{1,0:T(8,128)S(1)} %pad_maximum_fusion.5.cross, bf16[192,192]{1,0:T(8,128)(2,1)S(1)} %get-tuple-element.60.own_high, bf16[192,192]{1,0:T(8,128)(2,1)S(1)} %get-tuple-element.61.own_low, ...), custom_call_target="tpu_custom_call" | custom-call | bytes 1982464 | tf_op jit(solution)/shard_map/second_solve/pallas_call | solution.py:467
  (30 shorter events, 0.4 us)
Async XLA Ops:
  0.6 1.0 %slice-start = ((bf16[3,64,2,8,128]{4,3,2,1,0:T(8,128)(2,1)}), bf16[1,64,2,8,128]{4,3,2,1,0:T(8,128)(2,1)S(1)}, s32[]{:S(2)}) async-start(bf16[3,64,2,8,128]{4,3,2,1,0:T(8,128)(2,1)} %param.3), calls=%async_computation | async-start | bytes 524288 | tf_op jit(solution)/shard_map/slice | solution.py:510
  1.6 6.3 %copy-start.2 = (bf16[3,64,2,8,128]{4,3,2,1,0:T(8,128)(2,1)S(1)}, bf16[3,64,2,8,128]{4,3,2,1,0:T(8,128)(2,1)}, u32[]{:S(2)}) copy-start(bf16[3,64,2,8,128]{4,3,2,1,0:T(8,128)(2,1)} %param.3) | copy-start | bytes 2359300
  1.7 9.6 %collective-permute-start.1 = (bf16[64,1024]{1,0:T(8,128)(2,1)S(1)}, bf16[64,1024]{1,0:T(8,128)(2,1)S(1)}, u32[]{:S(2)}, u32[]{:S(2)}) collective-permute-start(bf16[64,1024]{1,0:T(8,128)(2,1)S(1)} %cut.2), channel_id=1, source_target_pairs={{4,8},{8,4},{12,16},{16,12},{20,24},{24,20},{0,28},{28,0},{5,9},{9... | collective-permute-start | bytes 393224 | tf_op jit(solution)/shard_map/ppermute | solution.py:25
  7.8 6.3 %collective-permute-start = (bf16[64,1024]{1,0:T(8,128)(2,1)S(1)}, bf16[64,1024]{1,0:T(8,128)(2,1)S(1)}, u32[]{:S(2)}, u32[]{:S(2)}) collective-permute-start(bf16[64,1024]{1,0:T(8,128)(2,1)S(1)} %slice_select_fusion), channel_id=1, source_target_pairs={{0,4},{4,0},{8,12},{12,8},{16,20},{20,16},{24,28},{28,24},{1,5},{5... | collective-permute-start | bytes 393224 | tf_op jit(solution)/shard_map/ppermute | solution.py:24
  8.3 0.7 copy-start
  8.9 0.7 copy-start.1
  14.2 4.3 %collective-permute-start.3 = (bf16[64,512]{1,0:T(8,128)(2,1)S(1)}, bf16[64,512]{1,0:T(8,128)(2,1)S(1)}, u32[]{:S(2)}, u32[]{:S(2)}) collective-permute-start(bf16[64,512]{1,0:T(8,128)(2,1)S(1)} %get-tuple-element.93), channel_id=1, source_target_pairs={{1,2},{2,1},{0,3},{3,0},{5,6},{6,5},{4,7},{7,4},{9,10},{10,9},{8,1... | collective-permute-start | bytes 196616 | tf_op jit(solution)/shard_map/ppermute | solution.py:25
  15.3 3.2 %collective-permute-start.2 = (bf16[64,512]{1,0:T(8,128)(2,1)S(1)}, bf16[64,512]{1,0:T(8,128)(2,1)S(1)}, u32[]{:S(2)}, u32[]{:S(2)}) collective-permute-start(bf16[64,512]{1,0:T(8,128)(2,1)S(1)} %get-tuple-element.94), channel_id=1, source_target_pairs={{0,1},{1,0},{2,3},{3,2},{4,5},{5,4},{6,7},{7,6},{8,9},{9,8},{10,11... | collective-permute-start | bytes 196616 | tf_op jit(solution)/shard_map/ppermute | solution.py:24
  19.1 1.3 %collective-permute-start.4 = (f32[136,128]{1,0:T(8,128)S(1)}, f32[136,128]{1,0:T(8,128)S(1)}, u32[]{:S(2)}, u32[]{:S(2)}) collective-permute-start(f32[136,128]{1,0:T(8,128)S(1)} %slice_select_fusion.2), channel_id=1, source_target_pairs={{0,1},{1,0},{2,3},{3,2},{4,5},{5,4},{6,7},{7,6},{8,9},{9,8},{10,11... | collective-permute-start | bytes 208904 | tf_op jit(solution)/shard_map/ppermute | solution.py:436
  20.5 6.1 %collective-permute-start.6 = (f32[136,128]{1,0:T(8,128)S(1)}, f32[136,128]{1,0:T(8,128)S(1)}, u32[]{:S(2)}, u32[]{:S(2)}) collective-permute-start(f32[136,128]{1,0:T(8,128)S(1)} %select_add_fusion), channel_id=1, source_target_pairs={{0,6},{1,7},{2,4},{3,5},{4,2},{5,3},{6,0},{7,1},{8,14},{9,15},{10,... | collective-permute-start | bytes 208904 | tf_op jit(solution)/shard_map/ppermute | solution.py:436
  21.2 5.4 %collective-permute-start.7 = (f32[136,128]{1,0:T(8,128)S(1)}, f32[136,128]{1,0:T(8,128)S(1)}, u32[]{:S(2)}, u32[]{:S(2)}) collective-permute-start(f32[136,128]{1,0:T(8,128)S(1)} %select_add_fusion), channel_id=1, source_target_pairs={{0,5},{1,4},{2,7},{3,6},{4,1},{5,0},{6,3},{7,2},{8,13},{9,12},{10,... | collective-permute-start | bytes 208904 | tf_op jit(solution)/shard_map/ppermute | solution.py:436
  23.0 4.2 %collective-permute-start.5 = (f32[136,128]{1,0:T(8,128)S(1)}, f32[136,128]{1,0:T(8,128)S(1)}, u32[]{:S(2)}, u32[]{:S(2)}) collective-permute-start(f32[136,128]{1,0:T(8,128)S(1)} %select_add_fusion), channel_id=1, source_target_pairs={{0,3},{1,2},{2,1},{3,0},{4,7},{5,6},{6,5},{7,4},{8,11},{9,10},{10,... | collective-permute-start | bytes 208904 | tf_op jit(solution)/shard_map/ppermute | solution.py:436
  27.2 7.0 %collective-permute-start.9 = (f32[136,128]{1,0:T(8,128)S(1)}, f32[136,128]{1,0:T(8,128)S(1)}, u32[]{:S(2)}, u32[]{:S(2)}) collective-permute-start(f32[136,128]{1,0:T(8,128)S(1)} %add_add_fusion.1), channel_id=1, source_target_pairs={{0,24},{1,25},{2,26},{3,27},{4,28},{5,29},{6,30},{7,31},{8,16},{9,... | collective-permute-start | bytes 208904 | tf_op jit(solution)/shard_map/ppermute | solution.py:436
  28.7 7.8 %collective-permute-start.10 = (f32[136,128]{1,0:T(8,128)S(1)}, f32[136,128]{1,0:T(8,128)S(1)}, u32[]{:S(2)}, u32[]{:S(2)}) collective-permute-start(f32[136,128]{1,0:T(8,128)S(1)} %add_add_fusion.1), channel_id=1, source_target_pairs={{0,17},{1,16},{2,19},{3,18},{4,21},{5,20},{6,23},{7,22},{8,25},{9,... | collective-permute-start | bytes 208904 | tf_op jit(solution)/shard_map/ppermute | solution.py:436
  28.7 7.8 %collective-permute-start.8 = (f32[136,128]{1,0:T(8,128)S(1)}, f32[136,128]{1,0:T(8,128)S(1)}, u32[]{:S(2)}, u32[]{:S(2)}) collective-permute-start(f32[136,128]{1,0:T(8,128)S(1)} %add_add_fusion.1), channel_id=1, source_target_pairs={{0,9},{1,8},{2,11},{3,10},{4,13},{5,12},{6,15},{7,14},{8,1},{9,0},... | collective-permute-start | bytes 208904 | tf_op jit(solution)/shard_map/ppermute | solution.py:436
  36.5 1.3 %collective-permute-start.11 = (f32[136,128]{1,0:T(8,128)S(1)}, f32[136,128]{1,0:T(8,128)S(1)}, u32[]{:S(2)}, u32[]{:S(2)}) collective-permute-start(f32[136,128]{1,0:T(8,128)S(1)} %add_add_fusion), channel_id=1, source_target_pairs={{0,1},{1,0},{2,3},{3,2},{4,5},{5,4},{6,7},{7,6},{8,9},{9,8},{10,11... | collective-permute-start | bytes 208904 | tf_op jit(solution)/shard_map/ppermute | solution.py:436
  41.1 8.4 %collective-permute-start.13 = (bf16[64,1024]{1,0:T(8,128)(2,1)S(1)}, bf16[64,1024]{1,0:T(8,128)(2,1)S(1)}, u32[]{:S(2)}, u32[]{:S(2)}) collective-permute-start(bf16[64,1024]{1,0:T(8,128)(2,1)S(1)} %cut.3), channel_id=1, source_target_pairs={{4,8},{8,4},{12,16},{16,12},{20,24},{24,20},{0,28},{28,0},{5,9},{9... | collective-permute-start | bytes 393224 | tf_op jit(solution)/shard_map/ppermute | solution.py:25
  42.9 8.2 %collective-permute-start.12 = (bf16[64,1024]{1,0:T(8,128)(2,1)S(1)}, bf16[64,1024]{1,0:T(8,128)(2,1)S(1)}, u32[]{:S(2)}, u32[]{:S(2)}) collective-permute-start(bf16[64,1024]{1,0:T(8,128)(2,1)S(1)} %slice_select_fusion.1), channel_id=1, source_target_pairs={{0,4},{4,0},{8,12},{12,8},{16,20},{20,16},{24,28},{28,24},{1,5},{5... | collective-permute-start | bytes 393224 | tf_op jit(solution)/shard_map/ppermute | solution.py:24
  51.2 4.0 %collective-permute-start.15 = (bf16[64,512]{1,0:T(8,128)(2,1)S(1)}, bf16[64,512]{1,0:T(8,128)(2,1)S(1)}, u32[]{:S(2)}, u32[]{:S(2)}) collective-permute-start(bf16[64,512]{1,0:T(8,128)(2,1)S(1)} %get-tuple-element.85), channel_id=1, source_target_pairs={{1,2},{2,1},{0,3},{3,0},{5,6},{6,5},{4,7},{7,4},{9,10},{10,9},{8,1... | collective-permute-start | bytes 196616 | tf_op jit(solution)/shard_map/ppermute | solution.py:25
  51.3 4.0 %collective-permute-start.14 = (bf16[64,512]{1,0:T(8,128)(2,1)S(1)}, bf16[64,512]{1,0:T(8,128)(2,1)S(1)}, u32[]{:S(2)}, u32[]{:S(2)}) collective-permute-start(bf16[64,512]{1,0:T(8,128)(2,1)S(1)} %get-tuple-element.86), channel_id=1, source_target_pairs={{0,1},{1,0},{2,3},{3,2},{4,5},{5,4},{6,7},{7,6},{8,9},{9,8},{10,11... | collective-permute-start | bytes 196616 | tf_op jit(solution)/shard_map/ppermute | solution.py:24
  55.8 1.3 %collective-permute-start.16 = (f32[32,256]{1,0:T(8,128)S(1)}, f32[32,256]{1,0:T(8,128)S(1)}, u32[]{:S(2)}, u32[]{:S(2)}) collective-permute-start(f32[32,256]{1,0:T(8,128)S(1)} %slice_select_fusion.3), channel_id=1, source_target_pairs={{0,1},{1,0},{2,3},{3,2},{4,5},{5,4},{6,7},{7,6},{8,9},{9,8},{10,11... | collective-permute-start | bytes 98312 | tf_op jit(solution)/shard_map/ppermute | solution.py:436
  57.1 4.8 %collective-permute-start.18 = (f32[32,256]{1,0:T(8,128)S(1)}, f32[32,256]{1,0:T(8,128)S(1)}, u32[]{:S(2)}, u32[]{:S(2)}) collective-permute-start(f32[32,256]{1,0:T(8,128)S(1)} %select_add_fusion.1), channel_id=1, source_target_pairs={{0,6},{1,7},{2,4},{3,5},{4,2},{5,3},{6,0},{7,1},{8,14},{9,15},{10,... | collective-permute-start | bytes 98312 | tf_op jit(solution)/shard_map/ppermute | solution.py:436
  57.3 4.6 %collective-permute-start.19 = (f32[32,256]{1,0:T(8,128)S(1)}, f32[32,256]{1,0:T(8,128)S(1)}, u32[]{:S(2)}, u32[]{:S(2)}) collective-permute-start(f32[32,256]{1,0:T(8,128)S(1)} %select_add_fusion.1), channel_id=1, source_target_pairs={{0,5},{1,4},{2,7},{3,6},{4,1},{5,0},{6,3},{7,2},{8,13},{9,12},{10,... | collective-permute-start | bytes 98312 | tf_op jit(solution)/shard_map/ppermute | solution.py:436
  59.1 3.3 %collective-permute-start.17 = (f32[32,256]{1,0:T(8,128)S(1)}, f32[32,256]{1,0:T(8,128)S(1)}, u32[]{:S(2)}, u32[]{:S(2)}) collective-permute-start(f32[32,256]{1,0:T(8,128)S(1)} %select_add_fusion.1), channel_id=1, source_target_pairs={{0,3},{1,2},{2,1},{3,0},{4,7},{5,6},{6,5},{7,4},{8,11},{9,10},{10,... | collective-permute-start | bytes 98312 | tf_op jit(solution)/shard_map/ppermute | solution.py:436
  62.4 6.1 %collective-permute-start.21 = (f32[32,256]{1,0:T(8,128)S(1)}, f32[32,256]{1,0:T(8,128)S(1)}, u32[]{:S(2)}, u32[]{:S(2)}) collective-permute-start(f32[32,256]{1,0:T(8,128)S(1)} %add_add_fusion.3), channel_id=1, source_target_pairs={{0,24},{1,25},{2,26},{3,27},{4,28},{5,29},{6,30},{7,31},{8,16},{9,... | collective-permute-start | bytes 98312 | tf_op jit(solution)/shard_map/ppermute | solution.py:436
  65.0 4.6 %collective-permute-start.22 = (f32[32,256]{1,0:T(8,128)S(1)}, f32[32,256]{1,0:T(8,128)S(1)}, u32[]{:S(2)}, u32[]{:S(2)}) collective-permute-start(f32[32,256]{1,0:T(8,128)S(1)} %add_add_fusion.3), channel_id=1, source_target_pairs={{0,17},{1,16},{2,19},{3,18},{4,21},{5,20},{6,23},{7,22},{8,25},{9,... | collective-permute-start | bytes 98312 | tf_op jit(solution)/shard_map/ppermute | solution.py:436
  65.1 4.6 %collective-permute-start.20 = (f32[32,256]{1,0:T(8,128)S(1)}, f32[32,256]{1,0:T(8,128)S(1)}, u32[]{:S(2)}, u32[]{:S(2)}) collective-permute-start(f32[32,256]{1,0:T(8,128)S(1)} %add_add_fusion.3), channel_id=1, source_target_pairs={{0,9},{1,8},{2,11},{3,10},{4,13},{5,12},{6,15},{7,14},{8,1},{9,0},... | collective-permute-start | bytes 98312 | tf_op jit(solution)/shard_map/ppermute | solution.py:436
  69.7 1.3 %collective-permute-start.23 = (f32[32,256]{1,0:T(8,128)S(1)}, f32[32,256]{1,0:T(8,128)S(1)}, u32[]{:S(2)}, u32[]{:S(2)}) collective-permute-start(f32[32,256]{1,0:T(8,128)S(1)} %add_add_fusion.2), channel_id=1, source_target_pairs={{0,1},{1,0},{2,3},{3,2},{4,5},{5,4},{6,7},{7,6},{8,9},{9,8},{10,11... | collective-permute-start | bytes 98312 | tf_op jit(solution)/shard_map/ppermute | solution.py:436

commit v25 on v23

--- a/solution.py
+++ b/solution.py
@@ -365,10 +365,10 @@
     second = first - dots((first_low,), own)
     second_low = second.astype(jnp.bfloat16)
     used = (first_low, second_low)
-    sizes = [diagonal_of(square, axis) for axis in (1, 0)]
     square = square - dots(used, first_parts, NT)
     rest = second - dots((second_low,), own)
     square = square - dots(split(rest), used, NT)
+    sizes = [diagonal_of(square, axis) for axis in (1, 0)]
     return used, first + second, rest, square, sizes
 
 

time: 71.8 us -> 72.1 us (level)
  no operation moved by 1% of the time
where the time goes in v25:
time: 72.1 us; the launch traced here: 71.9 us
  starting transfers between devices  28.8 us (40%)
  waiting for transfers between devices  27.1 us (38%)
  Pallas kernels  12.6 us (17%)
  local copies, waits for them, and re-layouts  2.13 us (3%)
  between operations  0.95 us (1%)
    ppermute x16, waiting for transfers between devices, partner(): return lax.ppermute(part, axes, [(i, i ^ mask) for i in range(count)])  17.6 us
    ppermute x16, starting transfers between devices, partner(): return lax.ppermute(part, axes, [(i, i ^ mask) for i in range(count)])  15.4 us
    pallas_call x8, Pallas kernels, call(): pl.pallas_call(kernel, out_shape=[jax.ShapeDtypeStruct(shape, dtype) for...  11.8 us
    ppermute x4, starting transfers between devices, swaps(): outer = lax.ppermute(far, axis, pairs + [(0, count - 1), (count - 1, 0)])  6.81 us
    ppermute x4, waiting for transfers between devices, swaps(): outer = lax.ppermute(far, axis, pairs + [(0, count - 1), (count - 1, 0)])  6.67 us
    ppermute x4, starting transfers between devices, swaps(): inner = lax.ppermute(near, axis, [(i, i ^ 1) for i in range(count)])  6.61 us
    ppermute x4, waiting for transfers between devices, swaps(): inner = lax.ppermute(near, axis, [(i, i ^ 1) for i in range(count)])  2.85 us
  transfers between devices with their start and end apart: 24, of which 17 were waited for; matrix products, arithmetic and copies ran while one was open for 1% of the time, Pallas kernels for 6%

profile of v25, /device:TPU:0, one launch (start us, length us, event | category | flops | bytes accessed | tf_op | source)
XLA Modules:
  0.0 71.9 jit_solution(4975114367421907333)
XLA Ops:
  0.6 0.0 slice-start
  0.6 0.9 %slice-done = bf16[1,64,2,8,128]{4,3,2,1,0:T(8,128)(2,1)S(1)} async-done(((bf16[3,64,2,8,128]{4,3,2,1,0:T(8,128)(2,1)}), bf16[1,64,2,8,128]{4,3,2,1,0:T(8,128)(2,1)S(1)}, s32[]{:S(2)}) %slice-start) | async-done | bytes 262168 | tf_op jit(solution)/shard_map/slice | solution.py:510
  1.6 0.1 reshape_squeeze.3.block
  1.7 3.0 %collective-permute-start.1 = (bf16[64,1024]{1,0:T(8,128)(2,1)S(1)}, bf16[64,1024]{1,0:T(8,128)(2,1)S(1)}, u32[]{:S(2)}, u32[]{:S(2)}) collective-permute-start(bf16[64,1024]{1,0:T(8,128)(2,1)S(1)} %slice_select_fusion), channel_id=1, source_target_pairs={{0,4},{4,0},{8,12},{12,8},{16,20},{20,16},{24,28},{28,24},{1,5},{5... | collective-permute-start | bytes 393224 | tf_op jit(solution)/shard_map/ppermute | solution.py:24
  4.8 3.6 %collective-permute-start = (bf16[64,1024]{1,0:T(8,128)(2,1)S(1)}, bf16[64,1024]{1,0:T(8,128)(2,1)S(1)}, u32[]{:S(2)}, u32[]{:S(2)}) collective-permute-start(bf16[64,1024]{1,0:T(8,128)(2,1)S(1)} %cut.2), channel_id=1, source_target_pairs={{4,8},{8,4},{12,16},{16,12},{20,24},{24,20},{0,28},{28,0},{5,9},{9... | collective-permute-start | bytes 393224 | tf_op jit(solution)/shard_map/ppermute | solution.py:25
  8.4 0.3 reshape.18.stack
  8.8 0.0 copy-start
  8.8 0.6 stack_gram.1
  9.4 0.0 copy-start.1
  9.4 0.0 copy-done
  9.5 0.6 copy-done.1
  10.1 0.8 %coefficients.1.coef = f32[27,16,128]{2,1,0:T(8,128)S(1)} custom-call(f32[8,27]{1,0:T(8,128)S(1)} %copy-done.1, s32[16,128]{1,0:T(8,128)S(1)} %bitcast.7), custom_call_target="tpu_custom_call" | custom-call | tf_op jit(solution)/shard_map/coefficients/pallas_call | solution.py:101
  10.9 0.0 collective-permute-done.1
  10.9 1.6 %collective-permute-done = bf16[64,1024]{1,0:T(8,128)(2,1)S(1)} collective-permute-done((bf16[64,1024]{1,0:T(8,128)(2,1)S(1)}, bf16[64,1024]{1,0:T(8,128)(2,1)S(1)}, u32[]{:S(2)}, u32[]{:S(2)}) %collective-permute-start) | collective-permute-done | bytes 131104 | tf_op jit(solution)/shard_map/ppermute | solution.py:25
  12.6 0.1 collective-permute-start.3
  12.7 1.6 %collective-permute-start.2 = (bf16[64,512]{1,0:T(8,128)(2,1)S(1)}, bf16[64,512]{1,0:T(8,128)(2,1)S(1)}, u32[]{:S(2)}, u32[]{:S(2)}) collective-permute-start(bf16[64,512]{1,0:T(8,128)(2,1)S(1)} %get-tuple-element.94), channel_id=1, source_target_pairs={{0,1},{1,0},{2,3},{3,2},{4,5},{5,4},{6,7},{7,6},{8,9},{9,8},{10,11... | collective-permute-start | bytes 196616 | tf_op jit(solution)/shard_map/ppermute | solution.py:24
  14.3 1.3 %middle_image.2 = (bf16[64,1536]{1,0:T(8,128)(2,1)S(1)}, f32[64,512]{1,0:T(8,128)S(1)}, f32[64,256]{1,0:T(8,128)S(1)}) custom-call(f32[27,16,128]{2,1,0:T(8,128)S(1)} %coefficients.1.coef, bf16[192,2048]{1,0:T(8,128)(2,1)S(1)} %reshape.18.stack, bf16[64,2048]{1,0:T(8,128)(2,1)S(1)} %reshape_squeeze.3.block, bf16[64,1024]{1,0:T(8,128)(2,1)S(1)} %get-tuple-element.44.xlo, ...), custom_call_target="tpu_custom_call" | custom-call | flops 7077888 | bytes 1925120 | tf_op jit(solution)/shard_map/middle_image/pallas_call | solution.py:467
  15.6 1.4 %collective-permute-done.3 = bf16[64,512]{1,0:T(8,128)(2,1)S(1)} collective-permute-done((bf16[64,512]{1,0:T(8,128)(2,1)S(1)}, bf16[64,512]{1,0:T(8,128)(2,1)S(1)}, u32[]{:S(2)}, u32[]{:S(2)}) %collective-permute-start.3) | collective-permute-done | bytes 65568 | tf_op jit(solution)/shard_map/ppermute | solution.py:25
  17.0 0.0 collective-permute-done.2
  17.0 0.6 first_image.1
  17.6 0.2 collective-permute-start.4
  17.8 1.1 %collective-permute-done.4 = f32[136,128]{1,0:T(8,128)S(1)} collective-permute-done((f32[136,128]{1,0:T(8,128)S(1)}, f32[136,128]{1,0:T(8,128)S(1)}, u32[]{:S(2)}, u32[]{:S(2)}) %collective-permute-start.4) | collective-permute-done | bytes 69664 | tf_op jit(solution)/shard_map/ppermute | solution.py:436
  19.0 0.7 collective-permute-start.6
  19.7 1.2 %collective-permute-start.7 = (f32[136,128]{1,0:T(8,128)S(1)}, f32[136,128]{1,0:T(8,128)S(1)}, u32[]{:S(2)}, u32[]{:S(2)}) collective-permute-start(f32[136,128]{1,0:T(8,128)S(1)} %select_add_fusion), channel_id=1, source_target_pairs={{0,5},{1,4},{2,7},{3,6},{4,1},{5,0},{6,3},{7,2},{8,13},{9,12},{10,... | collective-permute-start | bytes 208904 | tf_op jit(solution)/shard_map/ppermute | solution.py:436
  20.9 1.4 %collective-permute-start.5 = (f32[136,128]{1,0:T(8,128)S(1)}, f32[136,128]{1,0:T(8,128)S(1)}, u32[]{:S(2)}, u32[]{:S(2)}) collective-permute-start(f32[136,128]{1,0:T(8,128)S(1)} %select_add_fusion), channel_id=1, source_target_pairs={{0,3},{1,2},{2,1},{3,0},{4,7},{5,6},{6,5},{7,4},{8,11},{9,10},{10,... | collective-permute-start | bytes 208904 | tf_op jit(solution)/shard_map/ppermute | solution.py:436
  22.2 2.8 %collective-permute-done.6 = f32[136,128]{1,0:T(8,128)S(1)} collective-permute-done((f32[136,128]{1,0:T(8,128)S(1)}, f32[136,128]{1,0:T(8,128)S(1)}, u32[]{:S(2)}, u32[]{:S(2)}) %collective-permute-start.6) | collective-permute-done | bytes 69664 | tf_op jit(solution)/shard_map/ppermute | solution.py:436
  25.0 0.0 collective-permute-done.7
  25.0 0.5 collective-permute-done.5
  25.5 2.5 %collective-permute-start.9 = (f32[136,128]{1,0:T(8,128)S(1)}, f32[136,128]{1,0:T(8,128)S(1)}, u32[]{:S(2)}, u32[]{:S(2)}) collective-permute-start(f32[136,128]{1,0:T(8,128)S(1)} %add_add_fusion.1), channel_id=1, source_target_pairs={{0,24},{1,25},{2,26},{3,27},{4,28},{5,29},{6,30},{7,31},{8,16},{9,... | collective-permute-start | bytes 208904 | tf_op jit(solution)/shard_map/ppermute | solution.py:436
  28.0 0.0 collective-permute-start.10
  28.0 1.7 %collective-permute-start.8 = (f32[136,128]{1,0:T(8,128)S(1)}, f32[136,128]{1,0:T(8,128)S(1)}, u32[]{:S(2)}, u32[]{:S(2)}) collective-permute-start(f32[136,128]{1,0:T(8,128)S(1)} %add_add_fusion.1), channel_id=1, source_target_pairs={{0,9},{1,8},{2,11},{3,10},{4,13},{5,12},{6,15},{7,14},{8,1},{9,0},... | collective-permute-start | bytes 208904 | tf_op jit(solution)/shard_map/ppermute | solution.py:436
  29.7 2.8 %collective-permute-done.9 = f32[136,128]{1,0:T(8,128)S(1)} collective-permute-done((f32[136,128]{1,0:T(8,128)S(1)}, f32[136,128]{1,0:T(8,128)S(1)}, u32[]{:S(2)}, u32[]{:S(2)}) %collective-permute-start.9) | collective-permute-done | bytes 69664 | tf_op jit(solution)/shard_map/ppermute | solution.py:436
  32.5 2.2 %collective-permute-done.10 = f32[136,128]{1,0:T(8,128)S(1)} collective-permute-done((f32[136,128]{1,0:T(8,128)S(1)}, f32[136,128]{1,0:T(8,128)S(1)}, u32[]{:S(2)}, u32[]{:S(2)}) %collective-permute-start.10) | collective-permute-done | bytes 69664 | tf_op jit(solution)/shard_map/ppermute | solution.py:436
  34.7 0.0 collective-permute-done.8
  34.7 0.2 collective-permute-start.11
  34.9 1.2 %collective-permute-done.11 = f32[136,128]{1,0:T(8,128)S(1)} collective-permute-done((f32[136,128]{1,0:T(8,128)S(1)}, f32[136,128]{1,0:T(8,128)S(1)}, u32[]{:S(2)}, u32[]{:S(2)}) %collective-permute-start.11) | collective-permute-done | bytes 69664 | tf_op jit(solution)/shard_map/ppermute | solution.py:436
  36.1 3.2 %first_solve.1 = (bf16[64,2048]{1,0:T(8,128)(2,1)S(1)}, f32[64,192]{1,0:T(8,128)S(1)}, f32[64,64]{1,0:T(8,128)S(1)}, f32[64,192]{1,0:T(8,128)S(1)}, f32[64,64]{1,0:T(8,128)S(1)}, /*index=5*/bf16[64,64]{1,0:T(8,128)(2,1)S(1)}) custom-call(f32[272,128]{1,0:T(8,128)S(1)} %pad_maximum_fusion.cross, bf16[192,2048]{1,0:T(8,128)(2,1)S(1)} %reshape.18.stack, ...), custom_call_target="tpu_custom_call" | custom-call | bytes 1589248 | tf_op jit(solution)/shard_map/first_solve/pallas_call | solution.py:467
  39.3 0.9 %collective-permute-start.13 = (bf16[64,1024]{1,0:T(8,128)(2,1)S(1)}, bf16[64,1024]{1,0:T(8,128)(2,1)S(1)}, u32[]{:S(2)}, u32[]{:S(2)}) collective-permute-start(bf16[64,1024]{1,0:T(8,128)(2,1)S(1)} %slice_select_fusion.1), channel_id=1, source_target_pairs={{0,4},{4,0},{8,12},{12,8},{16,20},{20,16},{24,28},{28,24},{1,5},{5... | collective-permute-start | bytes 393224 | tf_op jit(solution)/shard_map/ppermute | solution.py:24
  40.2 3.0 %collective-permute-start.12 = (bf16[64,1024]{1,0:T(8,128)(2,1)S(1)}, bf16[64,1024]{1,0:T(8,128)(2,1)S(1)}, u32[]{:S(2)}, u32[]{:S(2)}) collective-permute-start(bf16[64,1024]{1,0:T(8,128)(2,1)S(1)} %cut.3), channel_id=1, source_target_pairs={{4,8},{8,4},{12,16},{16,12},{20,24},{24,20},{0,28},{28,0},{5,9},{9... | collective-permute-start | bytes 393224 | tf_op jit(solution)/shard_map/ppermute | solution.py:25
  43.3 2.8 %collective-permute-done.13 = bf16[64,1024]{1,0:T(8,128)(2,1)S(1)} collective-permute-done((bf16[64,1024]{1,0:T(8,128)(2,1)S(1)}, bf16[64,1024]{1,0:T(8,128)(2,1)S(1)}, u32[]{:S(2)}, u32[]{:S(2)}) %collective-permute-start.13) | collective-permute-done | bytes 131104 | tf_op jit(solution)/shard_map/ppermute | solution.py:24
  46.1 2.1 %collective-permute-done.12 = bf16[64,1024]{1,0:T(8,128)(2,1)S(1)} collective-permute-done((bf16[64,1024]{1,0:T(8,128)(2,1)S(1)}, bf16[64,1024]{1,0:T(8,128)(2,1)S(1)}, u32[]{:S(2)}, u32[]{:S(2)}) %collective-permute-start.12) | collective-permute-done | bytes 131104 | tf_op jit(solution)/shard_map/ppermute | solution.py:25
  48.3 0.1 collective-permute-start.15
  48.4 1.1 %collective-permute-start.14 = (bf16[64,512]{1,0:T(8,128)(2,1)S(1)}, bf16[64,512]{1,0:T(8,128)(2,1)S(1)}, u32[]{:S(2)}, u32[]{:S(2)}) collective-permute-start(bf16[64,512]{1,0:T(8,128)(2,1)S(1)} %get-tuple-element.86), channel_id=1, source_target_pairs={{0,1},{1,0},{2,3},{3,2},{4,5},{5,4},{6,7},{7,6},{8,9},{9,8},{10,11... | collective-permute-start | bytes 196616 | tf_op jit(solution)/shard_map/ppermute | solution.py:24
  49.5 1.3 %middle_image.3 = (bf16[64,1536]{1,0:T(8,128)(2,1)S(1)}, f32[64,512]{1,0:T(8,128)S(1)}, f32[64,256]{1,0:T(8,128)S(1)}) custom-call(f32[27,16,128]{2,1,0:T(8,128)S(1)} %coefficients.1.coef, bf16[192,2048]{1,0:T(8,128)(2,1)S(1)} %reshape.18.stack, bf16[64,2048]{1,0:T(8,128)(2,1)S(1)} %get-tuple-element.51.block.last, ...), custom_call_target="tpu_custom_call" | custom-call | flops 7077888 | bytes 1925120 | tf_op jit(solution)/shard_map/middle_image/pallas_call | solution.py:467
  50.8 1.6 %collective-permute-done.15 = bf16[64,512]{1,0:T(8,128)(2,1)S(1)} collective-permute-done((bf16[64,512]{1,0:T(8,128)(2,1)S(1)}, bf16[64,512]{1,0:T(8,128)(2,1)S(1)}, u32[]{:S(2)}, u32[]{:S(2)}) %collective-permute-start.15) | collective-permute-done | bytes 65568 | tf_op jit(solution)/shard_map/ppermute | solution.py:25
  52.3 0.0 collective-permute-done.14
  52.3 0.6 second_image.1
  52.9 0.1 collective-permute-start.16
  53.0 1.2 %collective-permute-done.16 = f32[32,256]{1,0:T(8,128)S(1)} collective-permute-done((f32[32,256]{1,0:T(8,128)S(1)}, f32[32,256]{1,0:T(8,128)S(1)}, u32[]{:S(2)}, u32[]{:S(2)}) %collective-permute-start.16) | collective-permute-done | bytes 32800 | tf_op jit(solution)/shard_map/ppermute | solution.py:436
  54.2 0.8 %collective-permute-start.18 = (f32[32,256]{1,0:T(8,128)S(1)}, f32[32,256]{1,0:T(8,128)S(1)}, u32[]{:S(2)}, u32[]{:S(2)}) collective-permute-start(f32[32,256]{1,0:T(8,128)S(1)} %select_add_fusion.1), channel_id=1, source_target_pairs={{0,6},{1,7},{2,4},{3,5},{4,2},{5,3},{6,0},{7,1},{8,14},{9,15},{10,... | collective-permute-start | bytes 98312 | tf_op jit(solution)/shard_map/ppermute | solution.py:436
  55.1 1.1 %collective-permute-start.19 = (f32[32,256]{1,0:T(8,128)S(1)}, f32[32,256]{1,0:T(8,128)S(1)}, u32[]{:S(2)}, u32[]{:S(2)}) collective-permute-start(f32[32,256]{1,0:T(8,128)S(1)} %select_add_fusion.1), channel_id=1, source_target_pairs={{0,5},{1,4},{2,7},{3,6},{4,1},{5,0},{6,3},{7,2},{8,13},{9,12},{10,... | collective-permute-start | bytes 98312 | tf_op jit(solution)/shard_map/ppermute | solution.py:436
  56.2 1.2 %collective-permute-start.17 = (f32[32,256]{1,0:T(8,128)S(1)}, f32[32,256]{1,0:T(8,128)S(1)}, u32[]{:S(2)}, u32[]{:S(2)}) collective-permute-start(f32[32,256]{1,0:T(8,128)S(1)} %select_add_fusion.1), channel_id=1, source_target_pairs={{0,3},{1,2},{2,1},{3,0},{4,7},{5,6},{6,5},{7,4},{8,11},{9,10},{10,... | collective-permute-start | bytes 98312 | tf_op jit(solution)/shard_map/ppermute | solution.py:436
  57.4 1.8 %collective-permute-done.18 = f32[32,256]{1,0:T(8,128)S(1)} collective-permute-done((f32[32,256]{1,0:T(8,128)S(1)}, f32[32,256]{1,0:T(8,128)S(1)}, u32[]{:S(2)}, u32[]{:S(2)}) %collective-permute-start.18) | collective-permute-done | bytes 32800 | tf_op jit(solution)/shard_map/ppermute | solution.py:436
  59.2 0.0 collective-permute-done.19
  59.2 0.3 collective-permute-done.17
  59.6 2.4 %collective-permute-start.21 = (f32[32,256]{1,0:T(8,128)S(1)}, f32[32,256]{1,0:T(8,128)S(1)}, u32[]{:S(2)}, u32[]{:S(2)}) collective-permute-start(f32[32,256]{1,0:T(8,128)S(1)} %add_add_fusion.3), channel_id=1, source_target_pairs={{0,24},{1,25},{2,26},{3,27},{4,28},{5,29},{6,30},{7,31},{8,16},{9,... | collective-permute-start | bytes 98312 | tf_op jit(solution)/shard_map/ppermute | solution.py:436
  62.0 0.0 collective-permute-start.22
  62.0 1.8 %collective-permute-start.20 = (f32[32,256]{1,0:T(8,128)S(1)}, f32[32,256]{1,0:T(8,128)S(1)}, u32[]{:S(2)}, u32[]{:S(2)}) collective-permute-start(f32[32,256]{1,0:T(8,128)S(1)} %add_add_fusion.3), channel_id=1, source_target_pairs={{0,9},{1,8},{2,11},{3,10},{4,13},{5,12},{6,15},{7,14},{8,1},{9,0},... | collective-permute-start | bytes 98312 | tf_op jit(solution)/shard_map/ppermute | solution.py:436
  63.7 1.9 %collective-permute-done.21 = f32[32,256]{1,0:T(8,128)S(1)} collective-permute-done((f32[32,256]{1,0:T(8,128)S(1)}, f32[32,256]{1,0:T(8,128)S(1)}, u32[]{:S(2)}, u32[]{:S(2)}) %collective-permute-start.21) | collective-permute-done | bytes 32800 | tf_op jit(solution)/shard_map/ppermute | solution.py:436
  65.6 1.1 %collective-permute-done.22 = f32[32,256]{1,0:T(8,128)S(1)} collective-permute-done((f32[32,256]{1,0:T(8,128)S(1)}, f32[32,256]{1,0:T(8,128)S(1)}, u32[]{:S(2)}, u32[]{:S(2)}) %collective-permute-start.22) | collective-permute-done | bytes 32800 | tf_op jit(solution)/shard_map/ppermute | solution.py:436
  66.8 0.2 collective-permute-start.23
  66.9 0.4 next_gram.1
  67.3 0.7 collective-permute-done.23
  68.1 3.9 %second_solve.1 = (bf16[64,2,8,128]{3,2,1,0:T(8,128)(2,1)}, f32[2,64,192]{2,1,0:T(8,128)}, f32[2,64,64]{2,1,0:T(8,128)}) custom-call(f32[64,256]{1,0:T(8,128)S(1)} %pad_maximum_fusion.5.cross, bf16[192,192]{1,0:T(8,128)(2,1)S(1)} %get-tuple-element.60.own_high, bf16[192,192]{1,0:T(8,128)(2,1)S(1)} %get-tuple-element.61.own_low, ...), custom_call_target="tpu_custom_call" | custom-call | bytes 1982464 | tf_op jit(solution)/shard_map/second_solve/pallas_call | solution.py:467
  (30 shorter events, 0.4 us)
Async XLA Ops:
  0.6 1.0 %slice-start = ((bf16[3,64,2,8,128]{4,3,2,1,0:T(8,128)(2,1)}), bf16[1,64,2,8,128]{4,3,2,1,0:T(8,128)(2,1)S(1)}, s32[]{:S(2)}) async-start(bf16[3,64,2,8,128]{4,3,2,1,0:T(8,128)(2,1)} %param.3), calls=%async_computation | async-start | bytes 524288 | tf_op jit(solution)/shard_map/slice | solution.py:510
  1.6 6.8 %copy-start.2 = (bf16[3,64,2,8,128]{4,3,2,1,0:T(8,128)(2,1)S(1)}, bf16[3,64,2,8,128]{4,3,2,1,0:T(8,128)(2,1)}, u32[]{:S(2)}) copy-start(bf16[3,64,2,8,128]{4,3,2,1,0:T(8,128)(2,1)} %param.3) | copy-start | bytes 2359300
  1.7 9.1 %collective-permute-start.1 = (bf16[64,1024]{1,0:T(8,128)(2,1)S(1)}, bf16[64,1024]{1,0:T(8,128)(2,1)S(1)}, u32[]{:S(2)}, u32[]{:S(2)}) collective-permute-start(bf16[64,1024]{1,0:T(8,128)(2,1)S(1)} %slice_select_fusion), channel_id=1, source_target_pairs={{0,4},{4,0},{8,12},{12,8},{16,20},{20,16},{24,28},{28,24},{1,5},{5... | collective-permute-start | bytes 393224 | tf_op jit(solution)/shard_map/ppermute | solution.py:24
  4.8 7.7 %collective-permute-start = (bf16[64,1024]{1,0:T(8,128)(2,1)S(1)}, bf16[64,1024]{1,0:T(8,128)(2,1)S(1)}, u32[]{:S(2)}, u32[]{:S(2)}) collective-permute-start(bf16[64,1024]{1,0:T(8,128)(2,1)S(1)} %cut.2), channel_id=1, source_target_pairs={{4,8},{8,4},{12,16},{16,12},{20,24},{24,20},{0,28},{28,0},{5,9},{9... | collective-permute-start | bytes 393224 | tf_op jit(solution)/shard_map/ppermute | solution.py:25
  8.8 0.7 copy-start
  9.4 0.7 copy-start.1
  12.6 4.4 %collective-permute-start.3 = (bf16[64,512]{1,0:T(8,128)(2,1)S(1)}, bf16[64,512]{1,0:T(8,128)(2,1)S(1)}, u32[]{:S(2)}, u32[]{:S(2)}) collective-permute-start(bf16[64,512]{1,0:T(8,128)(2,1)S(1)} %get-tuple-element.93), channel_id=1, source_target_pairs={{1,2},{2,1},{0,3},{3,0},{5,6},{6,5},{4,7},{7,4},{9,10},{10,9},{8,1... | collective-permute-start | bytes 196616 | tf_op jit(solution)/shard_map/ppermute | solution.py:25
  12.7 4.3 %collective-permute-start.2 = (bf16[64,512]{1,0:T(8,128)(2,1)S(1)}, bf16[64,512]{1,0:T(8,128)(2,1)S(1)}, u32[]{:S(2)}, u32[]{:S(2)}) collective-permute-start(bf16[64,512]{1,0:T(8,128)(2,1)S(1)} %get-tuple-element.94), channel_id=1, source_target_pairs={{0,1},{1,0},{2,3},{3,2},{4,5},{5,4},{6,7},{7,6},{8,9},{9,8},{10,11... | collective-permute-start | bytes 196616 | tf_op jit(solution)/shard_map/ppermute | solution.py:24
  17.6 1.3 %collective-permute-start.4 = (f32[136,128]{1,0:T(8,128)S(1)}, f32[136,128]{1,0:T(8,128)S(1)}, u32[]{:S(2)}, u32[]{:S(2)}) collective-permute-start(f32[136,128]{1,0:T(8,128)S(1)} %slice_select_fusion.2), channel_id=1, source_target_pairs={{0,1},{1,0},{2,3},{3,2},{4,5},{5,4},{6,7},{7,6},{8,9},{9,8},{10,11... | collective-permute-start | bytes 208904 | tf_op jit(solution)/shard_map/ppermute | solution.py:436
  19.0 6.1 %collective-permute-start.6 = (f32[136,128]{1,0:T(8,128)S(1)}, f32[136,128]{1,0:T(8,128)S(1)}, u32[]{:S(2)}, u32[]{:S(2)}) collective-permute-start(f32[136,128]{1,0:T(8,128)S(1)} %select_add_fusion), channel_id=1, source_target_pairs={{0,6},{1,7},{2,4},{3,5},{4,2},{5,3},{6,0},{7,1},{8,14},{9,15},{10,... | collective-permute-start | bytes 208904 | tf_op jit(solution)/shard_map/ppermute | solution.py:436
  19.7 5.4 %collective-permute-start.7 = (f32[136,128]{1,0:T(8,128)S(1)}, f32[136,128]{1,0:T(8,128)S(1)}, u32[]{:S(2)}, u32[]{:S(2)}) collective-permute-start(f32[136,128]{1,0:T(8,128)S(1)} %select_add_fusion), channel_id=1, source_target_pairs={{0,5},{1,4},{2,7},{3,6},{4,1},{5,0},{6,3},{7,2},{8,13},{9,12},{10,... | collective-permute-start | bytes 208904 | tf_op jit(solution)/shard_map/ppermute | solution.py:436
  20.9 4.6 %collective-permute-start.5 = (f32[136,128]{1,0:T(8,128)S(1)}, f32[136,128]{1,0:T(8,128)S(1)}, u32[]{:S(2)}, u32[]{:S(2)}) collective-permute-start(f32[136,128]{1,0:T(8,128)S(1)} %select_add_fusion), channel_id=1, source_target_pairs={{0,3},{1,2},{2,1},{3,0},{4,7},{5,6},{6,5},{7,4},{8,11},{9,10},{10,... | collective-permute-start | bytes 208904 | tf_op jit(solution)/shard_map/ppermute | solution.py:436
  25.5 6.9 %collective-permute-start.9 = (f32[136,128]{1,0:T(8,128)S(1)}, f32[136,128]{1,0:T(8,128)S(1)}, u32[]{:S(2)}, u32[]{:S(2)}) collective-permute-start(f32[136,128]{1,0:T(8,128)S(1)} %add_add_fusion.1), channel_id=1, source_target_pairs={{0,24},{1,25},{2,26},{3,27},{4,28},{5,29},{6,30},{7,31},{8,16},{9,... | collective-permute-start | bytes 208904 | tf_op jit(solution)/shard_map/ppermute | solution.py:436
  28.0 6.7 %collective-permute-start.10 = (f32[136,128]{1,0:T(8,128)S(1)}, f32[136,128]{1,0:T(8,128)S(1)}, u32[]{:S(2)}, u32[]{:S(2)}) collective-permute-start(f32[136,128]{1,0:T(8,128)S(1)} %add_add_fusion.1), channel_id=1, source_target_pairs={{0,17},{1,16},{2,19},{3,18},{4,21},{5,20},{6,23},{7,22},{8,25},{9,... | collective-permute-start | bytes 208904 | tf_op jit(solution)/shard_map/ppermute | solution.py:436
  28.0 6.7 %collective-permute-start.8 = (f32[136,128]{1,0:T(8,128)S(1)}, f32[136,128]{1,0:T(8,128)S(1)}, u32[]{:S(2)}, u32[]{:S(2)}) collective-permute-start(f32[136,128]{1,0:T(8,128)S(1)} %add_add_fusion.1), channel_id=1, source_target_pairs={{0,9},{1,8},{2,11},{3,10},{4,13},{5,12},{6,15},{7,14},{8,1},{9,0},... | collective-permute-start | bytes 208904 | tf_op jit(solution)/shard_map/ppermute | solution.py:436
  34.7 1.3 %collective-permute-start.11 = (f32[136,128]{1,0:T(8,128)S(1)}, f32[136,128]{1,0:T(8,128)S(1)}, u32[]{:S(2)}, u32[]{:S(2)}) collective-permute-start(f32[136,128]{1,0:T(8,128)S(1)} %add_add_fusion), channel_id=1, source_target_pairs={{0,1},{1,0},{2,3},{3,2},{4,5},{5,4},{6,7},{7,6},{8,9},{9,8},{10,11... | collective-permute-start | bytes 208904 | tf_op jit(solution)/shard_map/ppermute | solution.py:436
  39.3 6.8 %collective-permute-start.13 = (bf16[64,1024]{1,0:T(8,128)(2,1)S(1)}, bf16[64,1024]{1,0:T(8,128)(2,1)S(1)}, u32[]{:S(2)}, u32[]{:S(2)}) collective-permute-start(bf16[64,1024]{1,0:T(8,128)(2,1)S(1)} %slice_select_fusion.1), channel_id=1, source_target_pairs={{0,4},{4,0},{8,12},{12,8},{16,20},{20,16},{24,28},{28,24},{1,5},{5... | collective-permute-start | bytes 393224 | tf_op jit(solution)/shard_map/ppermute | solution.py:24
  40.2 8.0 %collective-permute-start.12 = (bf16[64,1024]{1,0:T(8,128)(2,1)S(1)}, bf16[64,1024]{1,0:T(8,128)(2,1)S(1)}, u32[]{:S(2)}, u32[]{:S(2)}) collective-permute-start(bf16[64,1024]{1,0:T(8,128)(2,1)S(1)} %cut.3), channel_id=1, source_target_pairs={{4,8},{8,4},{12,16},{16,12},{20,24},{24,20},{0,28},{28,0},{5,9},{9... | collective-permute-start | bytes 393224 | tf_op jit(solution)/shard_map/ppermute | solution.py:25
  48.3 4.0 %collective-permute-start.15 = (bf16[64,512]{1,0:T(8,128)(2,1)S(1)}, bf16[64,512]{1,0:T(8,128)(2,1)S(1)}, u32[]{:S(2)}, u32[]{:S(2)}) collective-permute-start(bf16[64,512]{1,0:T(8,128)(2,1)S(1)} %get-tuple-element.85), channel_id=1, source_target_pairs={{1,2},{2,1},{0,3},{3,0},{5,6},{6,5},{4,7},{7,4},{9,10},{10,9},{8,1... | collective-permute-start | bytes 196616 | tf_op jit(solution)/shard_map/ppermute | solution.py:25
  48.4 3.9 %collective-permute-start.14 = (bf16[64,512]{1,0:T(8,128)(2,1)S(1)}, bf16[64,512]{1,0:T(8,128)(2,1)S(1)}, u32[]{:S(2)}, u32[]{:S(2)}) collective-permute-start(bf16[64,512]{1,0:T(8,128)(2,1)S(1)} %get-tuple-element.86), channel_id=1, source_target_pairs={{0,1},{1,0},{2,3},{3,2},{4,5},{5,4},{6,7},{7,6},{8,9},{9,8},{10,11... | collective-permute-start | bytes 196616 | tf_op jit(solution)/shard_map/ppermute | solution.py:24
  52.9 1.3 %collective-permute-start.16 = (f32[32,256]{1,0:T(8,128)S(1)}, f32[32,256]{1,0:T(8,128)S(1)}, u32[]{:S(2)}, u32[]{:S(2)}) collective-permute-start(f32[32,256]{1,0:T(8,128)S(1)} %slice_select_fusion.3), channel_id=1, source_target_pairs={{0,1},{1,0},{2,3},{3,2},{4,5},{5,4},{6,7},{7,6},{8,9},{9,8},{10,11... | collective-permute-start | bytes 98312 | tf_op jit(solution)/shard_map/ppermute | solution.py:436
  54.2 5.0 %collective-permute-start.18 = (f32[32,256]{1,0:T(8,128)S(1)}, f32[32,256]{1,0:T(8,128)S(1)}, u32[]{:S(2)}, u32[]{:S(2)}) collective-permute-start(f32[32,256]{1,0:T(8,128)S(1)} %select_add_fusion.1), channel_id=1, source_target_pairs={{0,6},{1,7},{2,4},{3,5},{4,2},{5,3},{6,0},{7,1},{8,14},{9,15},{10,... | collective-permute-start | bytes 98312 | tf_op jit(solution)/shard_map/ppermute | solution.py:436
  55.1 4.1 %collective-permute-start.19 = (f32[32,256]{1,0:T(8,128)S(1)}, f32[32,256]{1,0:T(8,128)S(1)}, u32[]{:S(2)}, u32[]{:S(2)}) collective-permute-start(f32[32,256]{1,0:T(8,128)S(1)} %select_add_fusion.1), channel_id=1, source_target_pairs={{0,5},{1,4},{2,7},{3,6},{4,1},{5,0},{6,3},{7,2},{8,13},{9,12},{10,... | collective-permute-start | bytes 98312 | tf_op jit(solution)/shard_map/ppermute | solution.py:436
  56.2 3.4 %collective-permute-start.17 = (f32[32,256]{1,0:T(8,128)S(1)}, f32[32,256]{1,0:T(8,128)S(1)}, u32[]{:S(2)}, u32[]{:S(2)}) collective-permute-start(f32[32,256]{1,0:T(8,128)S(1)} %select_add_fusion.1), channel_id=1, source_target_pairs={{0,3},{1,2},{2,1},{3,0},{4,7},{5,6},{6,5},{7,4},{8,11},{9,10},{10,... | collective-permute-start | bytes 98312 | tf_op jit(solution)/shard_map/ppermute | solution.py:436
  59.6 6.0 %collective-permute-start.21 = (f32[32,256]{1,0:T(8,128)S(1)}, f32[32,256]{1,0:T(8,128)S(1)}, u32[]{:S(2)}, u32[]{:S(2)}) collective-permute-start(f32[32,256]{1,0:T(8,128)S(1)} %add_add_fusion.3), channel_id=1, source_target_pairs={{0,24},{1,25},{2,26},{3,27},{4,28},{5,29},{6,30},{7,31},{8,16},{9,... | collective-permute-start | bytes 98312 | tf_op jit(solution)/shard_map/ppermute | solution.py:436
  62.0 4.8 %collective-permute-start.22 = (f32[32,256]{1,0:T(8,128)S(1)}, f32[32,256]{1,0:T(8,128)S(1)}, u32[]{:S(2)}, u32[]{:S(2)}) collective-permute-start(f32[32,256]{1,0:T(8,128)S(1)} %add_add_fusion.3), channel_id=1, source_target_pairs={{0,17},{1,16},{2,19},{3,18},{4,21},{5,20},{6,23},{7,22},{8,25},{9,... | collective-permute-start | bytes 98312 | tf_op jit(solution)/shard_map/ppermute | solution.py:436
  62.0 4.8 %collective-permute-start.20 = (f32[32,256]{1,0:T(8,128)S(1)}, f32[32,256]{1,0:T(8,128)S(1)}, u32[]{:S(2)}, u32[]{:S(2)}) collective-permute-start(f32[32,256]{1,0:T(8,128)S(1)} %add_add_fusion.3), channel_id=1, source_target_pairs={{0,9},{1,8},{2,11},{3,10},{4,13},{5,12},{6,15},{7,14},{8,1},{9,0},... | collective-permute-start | bytes 98312 | tf_op jit(solution)/shard_map/ppermute | solution.py:436
  66.8 1.3 %collective-permute-start.23 = (f32[32,256]{1,0:T(8,128)S(1)}, f32[32,256]{1,0:T(8,128)S(1)}, u32[]{:S(2)}, u32[]{:S(2)}) collective-permute-start(f32[32,256]{1,0:T(8,128)S(1)} %add_add_fusion.2), channel_id=1, source_target_pairs={{0,1},{1,0},{2,3},{3,2},{4,5},{5,4},{6,7},{7,6},{8,9},{9,8},{10,11... | collective-permute-start | bytes 98312 | tf_op jit(solution)/shard_map/ppermute | solution.py:436

commit v26 on v25

--- a/solution.py
+++ b/solution.py
@@ -282,7 +282,10 @@
 
 
 def dots(lefts, rights, dims=NN):
-    return sum(dot(left, right, dims) for left in lefts for right in rights)
+    stacked = lefts[0] if len(lefts) == 1 else jnp.concatenate(lefts, axis=0)
+    total = sum(dot(stacked, right, dims) for right in rights)
+    rows = lefts[0].shape[0]
+    return sum(total[i * rows : (i + 1) * rows] for i in range(len(lefts)))
 
 
 def factor(square, sizes, across):

time: 72.1 us -> 72.1 us (level)
  no operation moved by 1% of the time
where the time goes in v26:
time: 72.1 us; the launch traced here: 71.9 us
  starting transfers between devices  28.8 us (40%)
  waiting for transfers between devices  27.1 us (38%)
  Pallas kernels  12.6 us (17%)
  local copies, waits for them, and re-layouts  2.13 us (3%)
  between operations  0.95 us (1%)
    ppermute x16, waiting for transfers between devices, partner(): return lax.ppermute(part, axes, [(i, i ^ mask) for i in range(count)])  17.6 us
    ppermute x16, starting transfers between devices, partner(): return lax.ppermute(part, axes, [(i, i ^ mask) for i in range(count)])  15.4 us
    pallas_call x8, Pallas kernels, call(): pl.pallas_call(kernel, out_shape=[jax.ShapeDtypeStruct(shape, dtype) for...  11.8 us
    ppermute x4, starting transfers between devices, swaps(): outer = lax.ppermute(far, axis, pairs + [(0, count - 1), (count - 1, 0)])  6.81 us
    ppermute x4, waiting for transfers between devices, swaps(): outer = lax.ppermute(far, axis, pairs + [(0, count - 1), (count - 1, 0)])  6.67 us
    ppermute x4, starting transfers between devices, swaps(): inner = lax.ppermute(near, axis, [(i, i ^ 1) for i in range(count)])  6.61 us
    ppermute x4, waiting for transfers between devices, swaps(): inner = lax.ppermute(near, axis, [(i, i ^ 1) for i in range(count)])  2.85 us
  transfers between devices with their start and end apart: 24, of which 17 were waited for; matrix products, arithmetic and copies ran while one was open for 1% of the time, Pallas kernels for 6%

profile of v26, /device:TPU:0, one launch (start us, length us, event | category | flops | bytes accessed | tf_op | source)
XLA Modules:
  0.0 71.9 jit_solution(8824776393983509933)
XLA Ops:
  0.6 0.0 slice-start
  0.6 0.9 %slice-done = bf16[1,64,2,8,128]{4,3,2,1,0:T(8,128)(2,1)S(1)} async-done(((bf16[3,64,2,8,128]{4,3,2,1,0:T(8,128)(2,1)}), bf16[1,64,2,8,128]{4,3,2,1,0:T(8,128)(2,1)S(1)}, s32[]{:S(2)}) %slice-start) | async-done | bytes 262168 | tf_op jit(solution)/shard_map/slice | solution.py:513
  1.6 0.1 reshape_squeeze.3.block
  1.7 3.0 %collective-permute-start.1 = (bf16[64,1024]{1,0:T(8,128)(2,1)S(1)}, bf16[64,1024]{1,0:T(8,128)(2,1)S(1)}, u32[]{:S(2)}, u32[]{:S(2)}) collective-permute-start(bf16[64,1024]{1,0:T(8,128)(2,1)S(1)} %slice_select_fusion), channel_id=1, source_target_pairs={{0,4},{4,0},{8,12},{12,8},{16,20},{20,16},{24,28},{28,24},{1,5},{5... | collective-permute-start | bytes 393224 | tf_op jit(solution)/shard_map/ppermute | solution.py:24
  4.8 3.6 %collective-permute-start = (bf16[64,1024]{1,0:T(8,128)(2,1)S(1)}, bf16[64,1024]{1,0:T(8,128)(2,1)S(1)}, u32[]{:S(2)}, u32[]{:S(2)}) collective-permute-start(bf16[64,1024]{1,0:T(8,128)(2,1)S(1)} %cut.2), channel_id=1, source_target_pairs={{4,8},{8,4},{12,16},{16,12},{20,24},{24,20},{0,28},{28,0},{5,9},{9... | collective-permute-start | bytes 393224 | tf_op jit(solution)/shard_map/ppermute | solution.py:25
  8.4 0.3 reshape.18.stack
  8.8 0.0 copy-start
  8.8 0.6 stack_gram.1
  9.4 0.0 copy-start.1
  9.4 0.0 copy-done
  9.5 0.6 copy-done.1
  10.1 0.8 %coefficients.1.coef = f32[27,16,128]{2,1,0:T(8,128)S(1)} custom-call(f32[8,27]{1,0:T(8,128)S(1)} %copy-done.1, s32[16,128]{1,0:T(8,128)S(1)} %bitcast.7), custom_call_target="tpu_custom_call" | custom-call | tf_op jit(solution)/shard_map/coefficients/pallas_call | solution.py:101
  10.9 0.0 collective-permute-done.1
  10.9 1.6 %collective-permute-done = bf16[64,1024]{1,0:T(8,128)(2,1)S(1)} collective-permute-done((bf16[64,1024]{1,0:T(8,128)(2,1)S(1)}, bf16[64,1024]{1,0:T(8,128)(2,1)S(1)}, u32[]{:S(2)}, u32[]{:S(2)}) %collective-permute-start) | collective-permute-done | bytes 131104 | tf_op jit(solution)/shard_map/ppermute | solution.py:25
  12.6 0.1 collective-permute-start.3
  12.7 1.6 %collective-permute-start.2 = (bf16[64,512]{1,0:T(8,128)(2,1)S(1)}, bf16[64,512]{1,0:T(8,128)(2,1)S(1)}, u32[]{:S(2)}, u32[]{:S(2)}) collective-permute-start(bf16[64,512]{1,0:T(8,128)(2,1)S(1)} %get-tuple-element.94), channel_id=1, source_target_pairs={{0,1},{1,0},{2,3},{3,2},{4,5},{5,4},{6,7},{7,6},{8,9},{9,8},{10,11... | collective-permute-start | bytes 196616 | tf_op jit(solution)/shard_map/ppermute | solution.py:24
  14.3 1.3 %middle_image.2 = (bf16[64,1536]{1,0:T(8,128)(2,1)S(1)}, f32[64,512]{1,0:T(8,128)S(1)}, f32[64,256]{1,0:T(8,128)S(1)}) custom-call(f32[27,16,128]{2,1,0:T(8,128)S(1)} %coefficients.1.coef, bf16[192,2048]{1,0:T(8,128)(2,1)S(1)} %reshape.18.stack, bf16[64,2048]{1,0:T(8,128)(2,1)S(1)} %reshape_squeeze.3.block, bf16[64,1024]{1,0:T(8,128)(2,1)S(1)} %get-tuple-element.44.xlo, ...), custom_call_target="tpu_custom_call" | custom-call | flops 7077888 | bytes 1925120 | tf_op jit(solution)/shard_map/middle_image/pallas_call | solution.py:470
  15.6 1.4 %collective-permute-done.3 = bf16[64,512]{1,0:T(8,128)(2,1)S(1)} collective-permute-done((bf16[64,512]{1,0:T(8,128)(2,1)S(1)}, bf16[64,512]{1,0:T(8,128)(2,1)S(1)}, u32[]{:S(2)}, u32[]{:S(2)}) %collective-permute-start.3) | collective-permute-done | bytes 65568 | tf_op jit(solution)/shard_map/ppermute | solution.py:25
  17.0 0.0 collective-permute-done.2
  17.0 0.6 first_image.1
  17.6 0.2 collective-permute-start.4
  17.8 1.1 %collective-permute-done.4 = f32[136,128]{1,0:T(8,128)S(1)} collective-permute-done((f32[136,128]{1,0:T(8,128)S(1)}, f32[136,128]{1,0:T(8,128)S(1)}, u32[]{:S(2)}, u32[]{:S(2)}) %collective-permute-start.4) | collective-permute-done | bytes 69664 | tf_op jit(solution)/shard_map/ppermute | solution.py:439
  19.0 0.7 collective-permute-start.6
  19.7 1.2 %collective-permute-start.7 = (f32[136,128]{1,0:T(8,128)S(1)}, f32[136,128]{1,0:T(8,128)S(1)}, u32[]{:S(2)}, u32[]{:S(2)}) collective-permute-start(f32[136,128]{1,0:T(8,128)S(1)} %select_add_fusion), channel_id=1, source_target_pairs={{0,5},{1,4},{2,7},{3,6},{4,1},{5,0},{6,3},{7,2},{8,13},{9,12},{10,... | collective-permute-start | bytes 208904 | tf_op jit(solution)/shard_map/ppermute | solution.py:439
  20.9 1.4 %collective-permute-start.5 = (f32[136,128]{1,0:T(8,128)S(1)}, f32[136,128]{1,0:T(8,128)S(1)}, u32[]{:S(2)}, u32[]{:S(2)}) collective-permute-start(f32[136,128]{1,0:T(8,128)S(1)} %select_add_fusion), channel_id=1, source_target_pairs={{0,3},{1,2},{2,1},{3,0},{4,7},{5,6},{6,5},{7,4},{8,11},{9,10},{10,... | collective-permute-start | bytes 208904 | tf_op jit(solution)/shard_map/ppermute | solution.py:439
  22.2 2.8 %collective-permute-done.6 = f32[136,128]{1,0:T(8,128)S(1)} collective-permute-done((f32[136,128]{1,0:T(8,128)S(1)}, f32[136,128]{1,0:T(8,128)S(1)}, u32[]{:S(2)}, u32[]{:S(2)}) %collective-permute-start.6) | collective-permute-done | bytes 69664 | tf_op jit(solution)/shard_map/ppermute | solution.py:439
  25.0 0.0 collective-permute-done.7
  25.0 0.5 collective-permute-done.5
  25.5 2.5 %collective-permute-start.9 = (f32[136,128]{1,0:T(8,128)S(1)}, f32[136,128]{1,0:T(8,128)S(1)}, u32[]{:S(2)}, u32[]{:S(2)}) collective-permute-start(f32[136,128]{1,0:T(8,128)S(1)} %add_add_fusion.1), channel_id=1, source_target_pairs={{0,24},{1,25},{2,26},{3,27},{4,28},{5,29},{6,30},{7,31},{8,16},{9,... | collective-permute-start | bytes 208904 | tf_op jit(solution)/shard_map/ppermute | solution.py:439
  28.0 0.0 collective-permute-start.10
  28.0 1.7 %collective-permute-start.8 = (f32[136,128]{1,0:T(8,128)S(1)}, f32[136,128]{1,0:T(8,128)S(1)}, u32[]{:S(2)}, u32[]{:S(2)}) collective-permute-start(f32[136,128]{1,0:T(8,128)S(1)} %add_add_fusion.1), channel_id=1, source_target_pairs={{0,9},{1,8},{2,11},{3,10},{4,13},{5,12},{6,15},{7,14},{8,1},{9,0},... | collective-permute-start | bytes 208904 | tf_op jit(solution)/shard_map/ppermute | solution.py:439
  29.7 2.8 %collective-permute-done.9 = f32[136,128]{1,0:T(8,128)S(1)} collective-permute-done((f32[136,128]{1,0:T(8,128)S(1)}, f32[136,128]{1,0:T(8,128)S(1)}, u32[]{:S(2)}, u32[]{:S(2)}) %collective-permute-start.9) | collective-permute-done | bytes 69664 | tf_op jit(solution)/shard_map/ppermute | solution.py:439
  32.5 2.2 %collective-permute-done.10 = f32[136,128]{1,0:T(8,128)S(1)} collective-permute-done((f32[136,128]{1,0:T(8,128)S(1)}, f32[136,128]{1,0:T(8,128)S(1)}, u32[]{:S(2)}, u32[]{:S(2)}) %collective-permute-start.10) | collective-permute-done | bytes 69664 | tf_op jit(solution)/shard_map/ppermute | solution.py:439
  34.7 0.0 collective-permute-done.8
  34.7 0.2 collective-permute-start.11
  34.9 1.2 %collective-permute-done.11 = f32[136,128]{1,0:T(8,128)S(1)} collective-permute-done((f32[136,128]{1,0:T(8,128)S(1)}, f32[136,128]{1,0:T(8,128)S(1)}, u32[]{:S(2)}, u32[]{:S(2)}) %collective-permute-start.11) | collective-permute-done | bytes 69664 | tf_op jit(solution)/shard_map/ppermute | solution.py:439
  36.1 3.2 %first_solve.1 = (bf16[64,2048]{1,0:T(8,128)(2,1)S(1)}, f32[64,192]{1,0:T(8,128)S(1)}, f32[64,64]{1,0:T(8,128)S(1)}, f32[64,192]{1,0:T(8,128)S(1)}, f32[64,64]{1,0:T(8,128)S(1)}, /*index=5*/bf16[64,64]{1,0:T(8,128)(2,1)S(1)}) custom-call(f32[272,128]{1,0:T(8,128)S(1)} %pad_maximum_fusion.cross, bf16[192,2048]{1,0:T(8,128)(2,1)S(1)} %reshape.18.stack, ...), custom_call_target="tpu_custom_call" | custom-call | bytes 1589248 | tf_op jit(solution)/shard_map/first_solve/pallas_call | solution.py:470
  39.3 0.9 %collective-permute-start.13 = (bf16[64,1024]{1,0:T(8,128)(2,1)S(1)}, bf16[64,1024]{1,0:T(8,128)(2,1)S(1)}, u32[]{:S(2)}, u32[]{:S(2)}) collective-permute-start(bf16[64,1024]{1,0:T(8,128)(2,1)S(1)} %slice_select_fusion.1), channel_id=1, source_target_pairs={{0,4},{4,0},{8,12},{12,8},{16,20},{20,16},{24,28},{28,24},{1,5},{5... | collective-permute-start | bytes 393224 | tf_op jit(solution)/shard_map/ppermute | solution.py:24
  40.2 3.0 %collective-permute-start.12 = (bf16[64,1024]{1,0:T(8,128)(2,1)S(1)}, bf16[64,1024]{1,0:T(8,128)(2,1)S(1)}, u32[]{:S(2)}, u32[]{:S(2)}) collective-permute-start(bf16[64,1024]{1,0:T(8,128)(2,1)S(1)} %cut.3), channel_id=1, source_target_pairs={{4,8},{8,4},{12,16},{16,12},{20,24},{24,20},{0,28},{28,0},{5,9},{9... | collective-permute-start | bytes 393224 | tf_op jit(solution)/shard_map/ppermute | solution.py:25
  43.3 2.8 %collective-permute-done.13 = bf16[64,1024]{1,0:T(8,128)(2,1)S(1)} collective-permute-done((bf16[64,1024]{1,0:T(8,128)(2,1)S(1)}, bf16[64,1024]{1,0:T(8,128)(2,1)S(1)}, u32[]{:S(2)}, u32[]{:S(2)}) %collective-permute-start.13) | collective-permute-done | bytes 131104 | tf_op jit(solution)/shard_map/ppermute | solution.py:24
  46.1 2.1 %collective-permute-done.12 = bf16[64,1024]{1,0:T(8,128)(2,1)S(1)} collective-permute-done((bf16[64,1024]{1,0:T(8,128)(2,1)S(1)}, bf16[64,1024]{1,0:T(8,128)(2,1)S(1)}, u32[]{:S(2)}, u32[]{:S(2)}) %collective-permute-start.12) | collective-permute-done | bytes 131104 | tf_op jit(solution)/shard_map/ppermute | solution.py:25
  48.3 0.1 collective-permute-start.15
  48.4 1.1 %collective-permute-start.14 = (bf16[64,512]{1,0:T(8,128)(2,1)S(1)}, bf16[64,512]{1,0:T(8,128)(2,1)S(1)}, u32[]{:S(2)}, u32[]{:S(2)}) collective-permute-start(bf16[64,512]{1,0:T(8,128)(2,1)S(1)} %get-tuple-element.86), channel_id=1, source_target_pairs={{0,1},{1,0},{2,3},{3,2},{4,5},{5,4},{6,7},{7,6},{8,9},{9,8},{10,11... | collective-permute-start | bytes 196616 | tf_op jit(solution)/shard_map/ppermute | solution.py:24
  49.5 1.3 %middle_image.3 = (bf16[64,1536]{1,0:T(8,128)(2,1)S(1)}, f32[64,512]{1,0:T(8,128)S(1)}, f32[64,256]{1,0:T(8,128)S(1)}) custom-call(f32[27,16,128]{2,1,0:T(8,128)S(1)} %coefficients.1.coef, bf16[192,2048]{1,0:T(8,128)(2,1)S(1)} %reshape.18.stack, bf16[64,2048]{1,0:T(8,128)(2,1)S(1)} %get-tuple-element.51.block.last, ...), custom_call_target="tpu_custom_call" | custom-call | flops 7077888 | bytes 1925120 | tf_op jit(solution)/shard_map/middle_image/pallas_call | solution.py:470
  50.7 1.6 %collective-permute-done.15 = bf16[64,512]{1,0:T(8,128)(2,1)S(1)} collective-permute-done((bf16[64,512]{1,0:T(8,128)(2,1)S(1)}, bf16[64,512]{1,0:T(8,128)(2,1)S(1)}, u32[]{:S(2)}, u32[]{:S(2)}) %collective-permute-start.15) | collective-permute-done | bytes 65568 | tf_op jit(solution)/shard_map/ppermute | solution.py:25
  52.3 0.0 collective-permute-done.14
  52.3 0.6 second_image.1
  52.9 0.1 collective-permute-start.16
  53.0 1.2 %collective-permute-done.16 = f32[32,256]{1,0:T(8,128)S(1)} collective-permute-done((f32[32,256]{1,0:T(8,128)S(1)}, f32[32,256]{1,0:T(8,128)S(1)}, u32[]{:S(2)}, u32[]{:S(2)}) %collective-permute-start.16) | collective-permute-done | bytes 32800 | tf_op jit(solution)/shard_map/ppermute | solution.py:439
  54.2 0.9 %collective-permute-start.18 = (f32[32,256]{1,0:T(8,128)S(1)}, f32[32,256]{1,0:T(8,128)S(1)}, u32[]{:S(2)}, u32[]{:S(2)}) collective-permute-start(f32[32,256]{1,0:T(8,128)S(1)} %select_add_fusion.1), channel_id=1, source_target_pairs={{0,6},{1,7},{2,4},{3,5},{4,2},{5,3},{6,0},{7,1},{8,14},{9,15},{10,... | collective-permute-start | bytes 98312 | tf_op jit(solution)/shard_map/ppermute | solution.py:439
  55.1 1.1 %collective-permute-start.19 = (f32[32,256]{1,0:T(8,128)S(1)}, f32[32,256]{1,0:T(8,128)S(1)}, u32[]{:S(2)}, u32[]{:S(2)}) collective-permute-start(f32[32,256]{1,0:T(8,128)S(1)} %select_add_fusion.1), channel_id=1, source_target_pairs={{0,5},{1,4},{2,7},{3,6},{4,1},{5,0},{6,3},{7,2},{8,13},{9,12},{10,... | collective-permute-start | bytes 98312 | tf_op jit(solution)/shard_map/ppermute | solution.py:439
  56.2 1.2 %collective-permute-start.17 = (f32[32,256]{1,0:T(8,128)S(1)}, f32[32,256]{1,0:T(8,128)S(1)}, u32[]{:S(2)}, u32[]{:S(2)}) collective-permute-start(f32[32,256]{1,0:T(8,128)S(1)} %select_add_fusion.1), channel_id=1, source_target_pairs={{0,3},{1,2},{2,1},{3,0},{4,7},{5,6},{6,5},{7,4},{8,11},{9,10},{10,... | collective-permute-start | bytes 98312 | tf_op jit(solution)/shard_map/ppermute | solution.py:439
  57.4 1.8 %collective-permute-done.18 = f32[32,256]{1,0:T(8,128)S(1)} collective-permute-done((f32[32,256]{1,0:T(8,128)S(1)}, f32[32,256]{1,0:T(8,128)S(1)}, u32[]{:S(2)}, u32[]{:S(2)}) %collective-permute-start.18) | collective-permute-done | bytes 32800 | tf_op jit(solution)/shard_map/ppermute | solution.py:439
  59.2 0.0 collective-permute-done.19
  59.2 0.3 collective-permute-done.17
  59.6 2.4 %collective-permute-start.21 = (f32[32,256]{1,0:T(8,128)S(1)}, f32[32,256]{1,0:T(8,128)S(1)}, u32[]{:S(2)}, u32[]{:S(2)}) collective-permute-start(f32[32,256]{1,0:T(8,128)S(1)} %add_add_fusion.3), channel_id=1, source_target_pairs={{0,24},{1,25},{2,26},{3,27},{4,28},{5,29},{6,30},{7,31},{8,16},{9,... | collective-permute-start | bytes 98312 | tf_op jit(solution)/shard_map/ppermute | solution.py:439
  62.0 0.0 collective-permute-start.22
  62.0 1.8 %collective-permute-start.20 = (f32[32,256]{1,0:T(8,128)S(1)}, f32[32,256]{1,0:T(8,128)S(1)}, u32[]{:S(2)}, u32[]{:S(2)}) collective-permute-start(f32[32,256]{1,0:T(8,128)S(1)} %add_add_fusion.3), channel_id=1, source_target_pairs={{0,9},{1,8},{2,11},{3,10},{4,13},{5,12},{6,15},{7,14},{8,1},{9,0},... | collective-permute-start | bytes 98312 | tf_op jit(solution)/shard_map/ppermute | solution.py:439
  63.7 1.9 %collective-permute-done.21 = f32[32,256]{1,0:T(8,128)S(1)} collective-permute-done((f32[32,256]{1,0:T(8,128)S(1)}, f32[32,256]{1,0:T(8,128)S(1)}, u32[]{:S(2)}, u32[]{:S(2)}) %collective-permute-start.21) | collective-permute-done | bytes 32800 | tf_op jit(solution)/shard_map/ppermute | solution.py:439
  65.6 1.1 %collective-permute-done.22 = f32[32,256]{1,0:T(8,128)S(1)} collective-permute-done((f32[32,256]{1,0:T(8,128)S(1)}, f32[32,256]{1,0:T(8,128)S(1)}, u32[]{:S(2)}, u32[]{:S(2)}) %collective-permute-start.22) | collective-permute-done | bytes 32800 | tf_op jit(solution)/shard_map/ppermute | solution.py:439
  66.7 0.2 collective-permute-start.23
  66.9 0.4 next_gram.1
  67.3 0.7 collective-permute-done.23
  68.0 3.9 %second_solve.1 = (bf16[64,2,8,128]{3,2,1,0:T(8,128)(2,1)}, f32[2,64,192]{2,1,0:T(8,128)}, f32[2,64,64]{2,1,0:T(8,128)}) custom-call(f32[64,256]{1,0:T(8,128)S(1)} %pad_maximum_fusion.5.cross, bf16[192,192]{1,0:T(8,128)(2,1)S(1)} %get-tuple-element.60.own_high, bf16[192,192]{1,0:T(8,128)(2,1)S(1)} %get-tuple-element.61.own_low, ...), custom_call_target="tpu_custom_call" | custom-call | bytes 1982464 | tf_op jit(solution)/shard_map/second_solve/pallas_call | solution.py:470
  (30 shorter events, 0.4 us)
Async XLA Ops:
  0.6 1.0 %slice-start = ((bf16[3,64,2,8,128]{4,3,2,1,0:T(8,128)(2,1)}), bf16[1,64,2,8,128]{4,3,2,1,0:T(8,128)(2,1)S(1)}, s32[]{:S(2)}) async-start(bf16[3,64,2,8,128]{4,3,2,1,0:T(8,128)(2,1)} %param.3), calls=%async_computation | async-start | bytes 524288 | tf_op jit(solution)/shard_map/slice | solution.py:513
  1.6 6.8 %copy-start.2 = (bf16[3,64,2,8,128]{4,3,2,1,0:T(8,128)(2,1)S(1)}, bf16[3,64,2,8,128]{4,3,2,1,0:T(8,128)(2,1)}, u32[]{:S(2)}) copy-start(bf16[3,64,2,8,128]{4,3,2,1,0:T(8,128)(2,1)} %param.3) | copy-start | bytes 2359300
  1.7 9.1 %collective-permute-start.1 = (bf16[64,1024]{1,0:T(8,128)(2,1)S(1)}, bf16[64,1024]{1,0:T(8,128)(2,1)S(1)}, u32[]{:S(2)}, u32[]{:S(2)}) collective-permute-start(bf16[64,1024]{1,0:T(8,128)(2,1)S(1)} %slice_select_fusion), channel_id=1, source_target_pairs={{0,4},{4,0},{8,12},{12,8},{16,20},{20,16},{24,28},{28,24},{1,5},{5... | collective-permute-start | bytes 393224 | tf_op jit(solution)/shard_map/ppermute | solution.py:24
  4.8 7.7 %collective-permute-start = (bf16[64,1024]{1,0:T(8,128)(2,1)S(1)}, bf16[64,1024]{1,0:T(8,128)(2,1)S(1)}, u32[]{:S(2)}, u32[]{:S(2)}) collective-permute-start(bf16[64,1024]{1,0:T(8,128)(2,1)S(1)} %cut.2), channel_id=1, source_target_pairs={{4,8},{8,4},{12,16},{16,12},{20,24},{24,20},{0,28},{28,0},{5,9},{9... | collective-permute-start | bytes 393224 | tf_op jit(solution)/shard_map/ppermute | solution.py:25
  8.8 0.7 copy-start
  9.4 0.7 copy-start.1
  12.6 4.4 %collective-permute-start.3 = (bf16[64,512]{1,0:T(8,128)(2,1)S(1)}, bf16[64,512]{1,0:T(8,128)(2,1)S(1)}, u32[]{:S(2)}, u32[]{:S(2)}) collective-permute-start(bf16[64,512]{1,0:T(8,128)(2,1)S(1)} %get-tuple-element.93), channel_id=1, source_target_pairs={{1,2},{2,1},{0,3},{3,0},{5,6},{6,5},{4,7},{7,4},{9,10},{10,9},{8,1... | collective-permute-start | bytes 196616 | tf_op jit(solution)/shard_map/ppermute | solution.py:25
  12.7 4.3 %collective-permute-start.2 = (bf16[64,512]{1,0:T(8,128)(2,1)S(1)}, bf16[64,512]{1,0:T(8,128)(2,1)S(1)}, u32[]{:S(2)}, u32[]{:S(2)}) collective-permute-start(bf16[64,512]{1,0:T(8,128)(2,1)S(1)} %get-tuple-element.94), channel_id=1, source_target_pairs={{0,1},{1,0},{2,3},{3,2},{4,5},{5,4},{6,7},{7,6},{8,9},{9,8},{10,11... | collective-permute-start | bytes 196616 | tf_op jit(solution)/shard_map/ppermute | solution.py:24
  17.6 1.3 %collective-permute-start.4 = (f32[136,128]{1,0:T(8,128)S(1)}, f32[136,128]{1,0:T(8,128)S(1)}, u32[]{:S(2)}, u32[]{:S(2)}) collective-permute-start(f32[136,128]{1,0:T(8,128)S(1)} %slice_select_fusion.2), channel_id=1, source_target_pairs={{0,1},{1,0},{2,3},{3,2},{4,5},{5,4},{6,7},{7,6},{8,9},{9,8},{10,11... | collective-permute-start | bytes 208904 | tf_op jit(solution)/shard_map/ppermute | solution.py:439
  19.0 6.1 %collective-permute-start.6 = (f32[136,128]{1,0:T(8,128)S(1)}, f32[136,128]{1,0:T(8,128)S(1)}, u32[]{:S(2)}, u32[]{:S(2)}) collective-permute-start(f32[136,128]{1,0:T(8,128)S(1)} %select_add_fusion), channel_id=1, source_target_pairs={{0,6},{1,7},{2,4},{3,5},{4,2},{5,3},{6,0},{7,1},{8,14},{9,15},{10,... | collective-permute-start | bytes 208904 | tf_op jit(solution)/shard_map/ppermute | solution.py:439
  19.7 5.4 %collective-permute-start.7 = (f32[136,128]{1,0:T(8,128)S(1)}, f32[136,128]{1,0:T(8,128)S(1)}, u32[]{:S(2)}, u32[]{:S(2)}) collective-permute-start(f32[136,128]{1,0:T(8,128)S(1)} %select_add_fusion), channel_id=1, source_target_pairs={{0,5},{1,4},{2,7},{3,6},{4,1},{5,0},{6,3},{7,2},{8,13},{9,12},{10,... | collective-permute-start | bytes 208904 | tf_op jit(solution)/shard_map/ppermute | solution.py:439
  20.9 4.6 %collective-permute-start.5 = (f32[136,128]{1,0:T(8,128)S(1)}, f32[136,128]{1,0:T(8,128)S(1)}, u32[]{:S(2)}, u32[]{:S(2)}) collective-permute-start(f32[136,128]{1,0:T(8,128)S(1)} %select_add_fusion), channel_id=1, source_target_pairs={{0,3},{1,2},{2,1},{3,0},{4,7},{5,6},{6,5},{7,4},{8,11},{9,10},{10,... | collective-permute-start | bytes 208904 | tf_op jit(solution)/shard_map/ppermute | solution.py:439
  25.5 6.9 %collective-permute-start.9 = (f32[136,128]{1,0:T(8,128)S(1)}, f32[136,128]{1,0:T(8,128)S(1)}, u32[]{:S(2)}, u32[]{:S(2)}) collective-permute-start(f32[136,128]{1,0:T(8,128)S(1)} %add_add_fusion.1), channel_id=1, source_target_pairs={{0,24},{1,25},{2,26},{3,27},{4,28},{5,29},{6,30},{7,31},{8,16},{9,... | collective-permute-start | bytes 208904 | tf_op jit(solution)/shard_map/ppermute | solution.py:439
  28.0 6.7 %collective-permute-start.10 = (f32[136,128]{1,0:T(8,128)S(1)}, f32[136,128]{1,0:T(8,128)S(1)}, u32[]{:S(2)}, u32[]{:S(2)}) collective-permute-start(f32[136,128]{1,0:T(8,128)S(1)} %add_add_fusion.1), channel_id=1, source_target_pairs={{0,17},{1,16},{2,19},{3,18},{4,21},{5,20},{6,23},{7,22},{8,25},{9,... | collective-permute-start | bytes 208904 | tf_op jit(solution)/shard_map/ppermute | solution.py:439
  28.0 6.7 %collective-permute-start.8 = (f32[136,128]{1,0:T(8,128)S(1)}, f32[136,128]{1,0:T(8,128)S(1)}, u32[]{:S(2)}, u32[]{:S(2)}) collective-permute-start(f32[136,128]{1,0:T(8,128)S(1)} %add_add_fusion.1), channel_id=1, source_target_pairs={{0,9},{1,8},{2,11},{3,10},{4,13},{5,12},{6,15},{7,14},{8,1},{9,0},... | collective-permute-start | bytes 208904 | tf_op jit(solution)/shard_map/ppermute | solution.py:439
  34.7 1.3 %collective-permute-start.11 = (f32[136,128]{1,0:T(8,128)S(1)}, f32[136,128]{1,0:T(8,128)S(1)}, u32[]{:S(2)}, u32[]{:S(2)}) collective-permute-start(f32[136,128]{1,0:T(8,128)S(1)} %add_add_fusion), channel_id=1, source_target_pairs={{0,1},{1,0},{2,3},{3,2},{4,5},{5,4},{6,7},{7,6},{8,9},{9,8},{10,11... | collective-permute-start | bytes 208904 | tf_op jit(solution)/shard_map/ppermute | solution.py:439
  39.3 6.8 %collective-permute-start.13 = (bf16[64,1024]{1,0:T(8,128)(2,1)S(1)}, bf16[64,1024]{1,0:T(8,128)(2,1)S(1)}, u32[]{:S(2)}, u32[]{:S(2)}) collective-permute-start(bf16[64,1024]{1,0:T(8,128)(2,1)S(1)} %slice_select_fusion.1), channel_id=1, source_target_pairs={{0,4},{4,0},{8,12},{12,8},{16,20},{20,16},{24,28},{28,24},{1,5},{5... | collective-permute-start | bytes 393224 | tf_op jit(solution)/shard_map/ppermute | solution.py:24
  40.2 8.0 %collective-permute-start.12 = (bf16[64,1024]{1,0:T(8,128)(2,1)S(1)}, bf16[64,1024]{1,0:T(8,128)(2,1)S(1)}, u32[]{:S(2)}, u32[]{:S(2)}) collective-permute-start(bf16[64,1024]{1,0:T(8,128)(2,1)S(1)} %cut.3), channel_id=1, source_target_pairs={{4,8},{8,4},{12,16},{16,12},{20,24},{24,20},{0,28},{28,0},{5,9},{9... | collective-permute-start | bytes 393224 | tf_op jit(solution)/shard_map/ppermute | solution.py:25
  48.3 4.0 %collective-permute-start.15 = (bf16[64,512]{1,0:T(8,128)(2,1)S(1)}, bf16[64,512]{1,0:T(8,128)(2,1)S(1)}, u32[]{:S(2)}, u32[]{:S(2)}) collective-permute-start(bf16[64,512]{1,0:T(8,128)(2,1)S(1)} %get-tuple-element.85), channel_id=1, source_target_pairs={{1,2},{2,1},{0,3},{3,0},{5,6},{6,5},{4,7},{7,4},{9,10},{10,9},{8,1... | collective-permute-start | bytes 196616 | tf_op jit(solution)/shard_map/ppermute | solution.py:25
  48.4 3.9 %collective-permute-start.14 = (bf16[64,512]{1,0:T(8,128)(2,1)S(1)}, bf16[64,512]{1,0:T(8,128)(2,1)S(1)}, u32[]{:S(2)}, u32[]{:S(2)}) collective-permute-start(bf16[64,512]{1,0:T(8,128)(2,1)S(1)} %get-tuple-element.86), channel_id=1, source_target_pairs={{0,1},{1,0},{2,3},{3,2},{4,5},{5,4},{6,7},{7,6},{8,9},{9,8},{10,11... | collective-permute-start | bytes 196616 | tf_op jit(solution)/shard_map/ppermute | solution.py:24
  52.9 1.3 %collective-permute-start.16 = (f32[32,256]{1,0:T(8,128)S(1)}, f32[32,256]{1,0:T(8,128)S(1)}, u32[]{:S(2)}, u32[]{:S(2)}) collective-permute-start(f32[32,256]{1,0:T(8,128)S(1)} %slice_select_fusion.3), channel_id=1, source_target_pairs={{0,1},{1,0},{2,3},{3,2},{4,5},{5,4},{6,7},{7,6},{8,9},{9,8},{10,11... | collective-permute-start | bytes 98312 | tf_op jit(solution)/shard_map/ppermute | solution.py:439
  54.2 5.0 %collective-permute-start.18 = (f32[32,256]{1,0:T(8,128)S(1)}, f32[32,256]{1,0:T(8,128)S(1)}, u32[]{:S(2)}, u32[]{:S(2)}) collective-permute-start(f32[32,256]{1,0:T(8,128)S(1)} %select_add_fusion.1), channel_id=1, source_target_pairs={{0,6},{1,7},{2,4},{3,5},{4,2},{5,3},{6,0},{7,1},{8,14},{9,15},{10,... | collective-permute-start | bytes 98312 | tf_op jit(solution)/shard_map/ppermute | solution.py:439
  55.1 4.1 %collective-permute-start.19 = (f32[32,256]{1,0:T(8,128)S(1)}, f32[32,256]{1,0:T(8,128)S(1)}, u32[]{:S(2)}, u32[]{:S(2)}) collective-permute-start(f32[32,256]{1,0:T(8,128)S(1)} %select_add_fusion.1), channel_id=1, source_target_pairs={{0,5},{1,4},{2,7},{3,6},{4,1},{5,0},{6,3},{7,2},{8,13},{9,12},{10,... | collective-permute-start | bytes 98312 | tf_op jit(solution)/shard_map/ppermute | solution.py:439
  56.2 3.4 %collective-permute-start.17 = (f32[32,256]{1,0:T(8,128)S(1)}, f32[32,256]{1,0:T(8,128)S(1)}, u32[]{:S(2)}, u32[]{:S(2)}) collective-permute-start(f32[32,256]{1,0:T(8,128)S(1)} %select_add_fusion.1), channel_id=1, source_target_pairs={{0,3},{1,2},{2,1},{3,0},{4,7},{5,6},{6,5},{7,4},{8,11},{9,10},{10,... | collective-permute-start | bytes 98312 | tf_op jit(solution)/shard_map/ppermute | solution.py:439
  59.6 6.0 %collective-permute-start.21 = (f32[32,256]{1,0:T(8,128)S(1)}, f32[32,256]{1,0:T(8,128)S(1)}, u32[]{:S(2)}, u32[]{:S(2)}) collective-permute-start(f32[32,256]{1,0:T(8,128)S(1)} %add_add_fusion.3), channel_id=1, source_target_pairs={{0,24},{1,25},{2,26},{3,27},{4,28},{5,29},{6,30},{7,31},{8,16},{9,... | collective-permute-start | bytes 98312 | tf_op jit(solution)/shard_map/ppermute | solution.py:439
  62.0 4.8 %collective-permute-start.22 = (f32[32,256]{1,0:T(8,128)S(1)}, f32[32,256]{1,0:T(8,128)S(1)}, u32[]{:S(2)}, u32[]{:S(2)}) collective-permute-start(f32[32,256]{1,0:T(8,128)S(1)} %add_add_fusion.3), channel_id=1, source_target_pairs={{0,17},{1,16},{2,19},{3,18},{4,21},{5,20},{6,23},{7,22},{8,25},{9,... | collective-permute-start | bytes 98312 | tf_op jit(solution)/shard_map/ppermute | solution.py:439
  62.0 4.8 %collective-permute-start.20 = (f32[32,256]{1,0:T(8,128)S(1)}, f32[32,256]{1,0:T(8,128)S(1)}, u32[]{:S(2)}, u32[]{:S(2)}) collective-permute-start(f32[32,256]{1,0:T(8,128)S(1)} %add_add_fusion.3), channel_id=1, source_target_pairs={{0,9},{1,8},{2,11},{3,10},{4,13},{5,12},{6,15},{7,14},{8,1},{9,0},... | collective-permute-start | bytes 98312 | tf_op jit(solution)/shard_map/ppermute | solution.py:439
  66.7 1.3 %collective-permute-start.23 = (f32[32,256]{1,0:T(8,128)S(1)}, f32[32,256]{1,0:T(8,128)S(1)}, u32[]{:S(2)}, u32[]{:S(2)}) collective-permute-start(f32[32,256]{1,0:T(8,128)S(1)} %add_add_fusion.2), channel_id=1, source_target_pairs={{0,1},{1,0},{2,3},{3,2},{4,5},{5,4},{6,7},{7,6},{8,9},{9,8},{10,11... | collective-permute-start | bytes 98312 | tf_op jit(solution)/shard_map/ppermute | solution.py:439

commit v27 on v26

--- a/solution.py
+++ b/solution.py
@@ -412,7 +412,6 @@
     block,
 ):
     columns = ends.shape[0]
-    kept = stack.shape[0] - columns
     fields = stack.shape[0]
     sums = cross[...] * scale
     used, proj[1], _, square, sizes = project(
@@ -422,7 +421,7 @@
     low[0] = low_in[...]
     _, span_x, span_y, depth = result.shape
     both = jnp.concatenate(used, axis=0)
-    moved = dot(both[:, :kept], stack[columns:]) + dot(both[:, kept:], last[...])
+    moved = dot(both, jnp.concatenate([stack[columns:], last[...]], axis=0))
     subtracted((span_x, span_y, depth), middle, ends, moved, block)
     upper, inverse = factor(square, *sizes)
     low[1] = upper.T

time: 72.1 us -> 72.1 us (level)
  no operation moved by 1% of the time
where the time goes in v27:
time: 72.1 us; the launch traced here: 71.9 us
  starting transfers between devices  28.8 us (40%)
  waiting for transfers between devices  27.1 us (38%)
  Pallas kernels  12.6 us (17%)
  local copies, waits for them, and re-layouts  2.13 us (3%)
  between operations  0.95 us (1%)
    ppermute x16, waiting for transfers between devices, partner(): return lax.ppermute(part, axes, [(i, i ^ mask) for i in range(count)])  17.6 us
    ppermute x16, starting transfers between devices, partner(): return lax.ppermute(part, axes, [(i, i ^ mask) for i in range(count)])  15.4 us
    pallas_call x8, Pallas kernels, call(): pl.pallas_call(kernel, out_shape=[jax.ShapeDtypeStruct(shape, dtype) for...  11.8 us
    ppermute x4, starting transfers between devices, swaps(): outer = lax.ppermute(far, axis, pairs + [(0, count - 1), (count - 1, 0)])  6.81 us
    ppermute x4, waiting for transfers between devices, swaps(): outer = lax.ppermute(far, axis, pairs + [(0, count - 1), (count - 1, 0)])  6.67 us
    ppermute x4, starting transfers between devices, swaps(): inner = lax.ppermute(near, axis, [(i, i ^ 1) for i in range(count)])  6.61 us
    ppermute x4, waiting for transfers between devices, swaps(): inner = lax.ppermute(near, axis, [(i, i ^ 1) for i in range(count)])  2.85 us
  transfers between devices with their start and end apart: 24, of which 17 were waited for; matrix products, arithmetic and copies ran while one was open for 1% of the time, Pallas kernels for 6%

profile of v27, /device:TPU:0, one launch (start us, length us, event | category | flops | bytes accessed | tf_op | source)
XLA Modules:
  0.0 71.9 jit_solution(1228738574146767243)
XLA Ops:
  0.6 0.0 slice-start
  0.6 0.9 %slice-done = bf16[1,64,2,8,128]{4,3,2,1,0:T(8,128)(2,1)S(1)} async-done(((bf16[3,64,2,8,128]{4,3,2,1,0:T(8,128)(2,1)}), bf16[1,64,2,8,128]{4,3,2,1,0:T(8,128)(2,1)S(1)}, s32[]{:S(2)}) %slice-start) | async-done | bytes 262168 | tf_op jit(solution)/shard_map/slice | solution.py:512
  1.6 0.1 reshape_squeeze.3.block
  1.7 3.0 %collective-permute-start.1 = (bf16[64,1024]{1,0:T(8,128)(2,1)S(1)}, bf16[64,1024]{1,0:T(8,128)(2,1)S(1)}, u32[]{:S(2)}, u32[]{:S(2)}) collective-permute-start(bf16[64,1024]{1,0:T(8,128)(2,1)S(1)} %slice_select_fusion), channel_id=1, source_target_pairs={{0,4},{4,0},{8,12},{12,8},{16,20},{20,16},{24,28},{28,24},{1,5},{5... | collective-permute-start | bytes 393224 | tf_op jit(solution)/shard_map/ppermute | solution.py:24
  4.8 3.6 %collective-permute-start = (bf16[64,1024]{1,0:T(8,128)(2,1)S(1)}, bf16[64,1024]{1,0:T(8,128)(2,1)S(1)}, u32[]{:S(2)}, u32[]{:S(2)}) collective-permute-start(bf16[64,1024]{1,0:T(8,128)(2,1)S(1)} %cut.2), channel_id=1, source_target_pairs={{4,8},{8,4},{12,16},{16,12},{20,24},{24,20},{0,28},{28,0},{5,9},{9... | collective-permute-start | bytes 393224 | tf_op jit(solution)/shard_map/ppermute | solution.py:25
  8.4 0.3 reshape.18.stack
  8.8 0.0 copy-start
  8.8 0.6 stack_gram.1
  9.4 0.0 copy-start.1
  9.4 0.0 copy-done
  9.5 0.6 copy-done.1
  10.1 0.8 %coefficients.1.coef = f32[27,16,128]{2,1,0:T(8,128)S(1)} custom-call(f32[8,27]{1,0:T(8,128)S(1)} %copy-done.1, s32[16,128]{1,0:T(8,128)S(1)} %bitcast.7), custom_call_target="tpu_custom_call" | custom-call | tf_op jit(solution)/shard_map/coefficients/pallas_call | solution.py:101
  10.9 0.0 collective-permute-done.1
  10.9 1.6 %collective-permute-done = bf16[64,1024]{1,0:T(8,128)(2,1)S(1)} collective-permute-done((bf16[64,1024]{1,0:T(8,128)(2,1)S(1)}, bf16[64,1024]{1,0:T(8,128)(2,1)S(1)}, u32[]{:S(2)}, u32[]{:S(2)}) %collective-permute-start) | collective-permute-done | bytes 131104 | tf_op jit(solution)/shard_map/ppermute | solution.py:25
  12.6 0.1 collective-permute-start.3
  12.7 1.6 %collective-permute-start.2 = (bf16[64,512]{1,0:T(8,128)(2,1)S(1)}, bf16[64,512]{1,0:T(8,128)(2,1)S(1)}, u32[]{:S(2)}, u32[]{:S(2)}) collective-permute-start(bf16[64,512]{1,0:T(8,128)(2,1)S(1)} %get-tuple-element.94), channel_id=1, source_target_pairs={{0,1},{1,0},{2,3},{3,2},{4,5},{5,4},{6,7},{7,6},{8,9},{9,8},{10,11... | collective-permute-start | bytes 196616 | tf_op jit(solution)/shard_map/ppermute | solution.py:24
  14.3 1.3 %middle_image.2 = (bf16[64,1536]{1,0:T(8,128)(2,1)S(1)}, f32[64,512]{1,0:T(8,128)S(1)}, f32[64,256]{1,0:T(8,128)S(1)}) custom-call(f32[27,16,128]{2,1,0:T(8,128)S(1)} %coefficients.1.coef, bf16[192,2048]{1,0:T(8,128)(2,1)S(1)} %reshape.18.stack, bf16[64,2048]{1,0:T(8,128)(2,1)S(1)} %reshape_squeeze.3.block, bf16[64,1024]{1,0:T(8,128)(2,1)S(1)} %get-tuple-element.44.xlo, ...), custom_call_target="tpu_custom_call" | custom-call | flops 7077888 | bytes 1925120 | tf_op jit(solution)/shard_map/middle_image/pallas_call | solution.py:469
  15.6 1.4 %collective-permute-done.3 = bf16[64,512]{1,0:T(8,128)(2,1)S(1)} collective-permute-done((bf16[64,512]{1,0:T(8,128)(2,1)S(1)}, bf16[64,512]{1,0:T(8,128)(2,1)S(1)}, u32[]{:S(2)}, u32[]{:S(2)}) %collective-permute-start.3) | collective-permute-done | bytes 65568 | tf_op jit(solution)/shard_map/ppermute | solution.py:25
  17.0 0.0 collective-permute-done.2
  17.0 0.6 first_image.1
  17.6 0.2 collective-permute-start.4
  17.8 1.1 %collective-permute-done.4 = f32[136,128]{1,0:T(8,128)S(1)} collective-permute-done((f32[136,128]{1,0:T(8,128)S(1)}, f32[136,128]{1,0:T(8,128)S(1)}, u32[]{:S(2)}, u32[]{:S(2)}) %collective-permute-start.4) | collective-permute-done | bytes 69664 | tf_op jit(solution)/shard_map/ppermute | solution.py:438
  19.0 0.7 collective-permute-start.6
  19.7 1.2 %collective-permute-start.7 = (f32[136,128]{1,0:T(8,128)S(1)}, f32[136,128]{1,0:T(8,128)S(1)}, u32[]{:S(2)}, u32[]{:S(2)}) collective-permute-start(f32[136,128]{1,0:T(8,128)S(1)} %select_add_fusion), channel_id=1, source_target_pairs={{0,5},{1,4},{2,7},{3,6},{4,1},{5,0},{6,3},{7,2},{8,13},{9,12},{10,... | collective-permute-start | bytes 208904 | tf_op jit(solution)/shard_map/ppermute | solution.py:438
  20.9 1.4 %collective-permute-start.5 = (f32[136,128]{1,0:T(8,128)S(1)}, f32[136,128]{1,0:T(8,128)S(1)}, u32[]{:S(2)}, u32[]{:S(2)}) collective-permute-start(f32[136,128]{1,0:T(8,128)S(1)} %select_add_fusion), channel_id=1, source_target_pairs={{0,3},{1,2},{2,1},{3,0},{4,7},{5,6},{6,5},{7,4},{8,11},{9,10},{10,... | collective-permute-start | bytes 208904 | tf_op jit(solution)/shard_map/ppermute | solution.py:438
  22.2 2.8 %collective-permute-done.6 = f32[136,128]{1,0:T(8,128)S(1)} collective-permute-done((f32[136,128]{1,0:T(8,128)S(1)}, f32[136,128]{1,0:T(8,128)S(1)}, u32[]{:S(2)}, u32[]{:S(2)}) %collective-permute-start.6) | collective-permute-done | bytes 69664 | tf_op jit(solution)/shard_map/ppermute | solution.py:438
  25.0 0.0 collective-permute-done.7
  25.0 0.5 collective-permute-done.5
  25.5 2.5 %collective-permute-start.9 = (f32[136,128]{1,0:T(8,128)S(1)}, f32[136,128]{1,0:T(8,128)S(1)}, u32[]{:S(2)}, u32[]{:S(2)}) collective-permute-start(f32[136,128]{1,0:T(8,128)S(1)} %add_add_fusion.1), channel_id=1, source_target_pairs={{0,24},{1,25},{2,26},{3,27},{4,28},{5,29},{6,30},{7,31},{8,16},{9,... | collective-permute-start | bytes 208904 | tf_op jit(solution)/shard_map/ppermute | solution.py:438
  28.0 0.0 collective-permute-start.10
  28.0 1.7 %collective-permute-start.8 = (f32[136,128]{1,0:T(8,128)S(1)}, f32[136,128]{1,0:T(8,128)S(1)}, u32[]{:S(2)}, u32[]{:S(2)}) collective-permute-start(f32[136,128]{1,0:T(8,128)S(1)} %add_add_fusion.1), channel_id=1, source_target_pairs={{0,9},{1,8},{2,11},{3,10},{4,13},{5,12},{6,15},{7,14},{8,1},{9,0},... | collective-permute-start | bytes 208904 | tf_op jit(solution)/shard_map/ppermute | solution.py:438
  29.7 2.8 %collective-permute-done.9 = f32[136,128]{1,0:T(8,128)S(1)} collective-permute-done((f32[136,128]{1,0:T(8,128)S(1)}, f32[136,128]{1,0:T(8,128)S(1)}, u32[]{:S(2)}, u32[]{:S(2)}) %collective-permute-start.9) | collective-permute-done | bytes 69664 | tf_op jit(solution)/shard_map/ppermute | solution.py:438
  32.5 2.2 %collective-permute-done.10 = f32[136,128]{1,0:T(8,128)S(1)} collective-permute-done((f32[136,128]{1,0:T(8,128)S(1)}, f32[136,128]{1,0:T(8,128)S(1)}, u32[]{:S(2)}, u32[]{:S(2)}) %collective-permute-start.10) | collective-permute-done | bytes 69664 | tf_op jit(solution)/shard_map/ppermute | solution.py:438
  34.7 0.0 collective-permute-done.8
  34.7 0.2 collective-permute-start.11
  34.9 1.2 %collective-permute-done.11 = f32[136,128]{1,0:T(8,128)S(1)} collective-permute-done((f32[136,128]{1,0:T(8,128)S(1)}, f32[136,128]{1,0:T(8,128)S(1)}, u32[]{:S(2)}, u32[]{:S(2)}) %collective-permute-start.11) | collective-permute-done | bytes 69664 | tf_op jit(solution)/shard_map/ppermute | solution.py:438
  36.1 3.2 %first_solve.1 = (bf16[64,2048]{1,0:T(8,128)(2,1)S(1)}, f32[64,192]{1,0:T(8,128)S(1)}, f32[64,64]{1,0:T(8,128)S(1)}, f32[64,192]{1,0:T(8,128)S(1)}, f32[64,64]{1,0:T(8,128)S(1)}, /*index=5*/bf16[64,64]{1,0:T(8,128)(2,1)S(1)}) custom-call(f32[272,128]{1,0:T(8,128)S(1)} %pad_maximum_fusion.cross, bf16[192,2048]{1,0:T(8,128)(2,1)S(1)} %reshape.18.stack, ...), custom_call_target="tpu_custom_call" | custom-call | bytes 1589248 | tf_op jit(solution)/shard_map/first_solve/pallas_call | solution.py:469
  39.3 0.9 %collective-permute-start.13 = (bf16[64,1024]{1,0:T(8,128)(2,1)S(1)}, bf16[64,1024]{1,0:T(8,128)(2,1)S(1)}, u32[]{:S(2)}, u32[]{:S(2)}) collective-permute-start(bf16[64,1024]{1,0:T(8,128)(2,1)S(1)} %slice_select_fusion.1), channel_id=1, source_target_pairs={{0,4},{4,0},{8,12},{12,8},{16,20},{20,16},{24,28},{28,24},{1,5},{5... | collective-permute-start | bytes 393224 | tf_op jit(solution)/shard_map/ppermute | solution.py:24
  40.2 3.0 %collective-permute-start.12 = (bf16[64,1024]{1,0:T(8,128)(2,1)S(1)}, bf16[64,1024]{1,0:T(8,128)(2,1)S(1)}, u32[]{:S(2)}, u32[]{:S(2)}) collective-permute-start(bf16[64,1024]{1,0:T(8,128)(2,1)S(1)} %cut.3), channel_id=1, source_target_pairs={{4,8},{8,4},{12,16},{16,12},{20,24},{24,20},{0,28},{28,0},{5,9},{9... | collective-permute-start | bytes 393224 | tf_op jit(solution)/shard_map/ppermute | solution.py:25
  43.3 2.8 %collective-permute-done.13 = bf16[64,1024]{1,0:T(8,128)(2,1)S(1)} collective-permute-done((bf16[64,1024]{1,0:T(8,128)(2,1)S(1)}, bf16[64,1024]{1,0:T(8,128)(2,1)S(1)}, u32[]{:S(2)}, u32[]{:S(2)}) %collective-permute-start.13) | collective-permute-done | bytes 131104 | tf_op jit(solution)/shard_map/ppermute | solution.py:24
  46.1 2.1 %collective-permute-done.12 = bf16[64,1024]{1,0:T(8,128)(2,1)S(1)} collective-permute-done((bf16[64,1024]{1,0:T(8,128)(2,1)S(1)}, bf16[64,1024]{1,0:T(8,128)(2,1)S(1)}, u32[]{:S(2)}, u32[]{:S(2)}) %collective-permute-start.12) | collective-permute-done | bytes 131104 | tf_op jit(solution)/shard_map/ppermute | solution.py:25
  48.3 0.1 collective-permute-start.15
  48.4 1.1 %collective-permute-start.14 = (bf16[64,512]{1,0:T(8,128)(2,1)S(1)}, bf16[64,512]{1,0:T(8,128)(2,1)S(1)}, u32[]{:S(2)}, u32[]{:S(2)}) collective-permute-start(bf16[64,512]{1,0:T(8,128)(2,1)S(1)} %get-tuple-element.86), channel_id=1, source_target_pairs={{0,1},{1,0},{2,3},{3,2},{4,5},{5,4},{6,7},{7,6},{8,9},{9,8},{10,11... | collective-permute-start | bytes 196616 | tf_op jit(solution)/shard_map/ppermute | solution.py:24
  49.5 1.3 %middle_image.3 = (bf16[64,1536]{1,0:T(8,128)(2,1)S(1)}, f32[64,512]{1,0:T(8,128)S(1)}, f32[64,256]{1,0:T(8,128)S(1)}) custom-call(f32[27,16,128]{2,1,0:T(8,128)S(1)} %coefficients.1.coef, bf16[192,2048]{1,0:T(8,128)(2,1)S(1)} %reshape.18.stack, bf16[64,2048]{1,0:T(8,128)(2,1)S(1)} %get-tuple-element.51.block.last, ...), custom_call_target="tpu_custom_call" | custom-call | flops 7077888 | bytes 1925120 | tf_op jit(solution)/shard_map/middle_image/pallas_call | solution.py:469
  50.7 1.6 %collective-permute-done.15 = bf16[64,512]{1,0:T(8,128)(2,1)S(1)} collective-permute-done((bf16[64,512]{1,0:T(8,128)(2,1)S(1)}, bf16[64,512]{1,0:T(8,128)(2,1)S(1)}, u32[]{:S(2)}, u32[]{:S(2)}) %collective-permute-start.15) | collective-permute-done | bytes 65568 | tf_op jit(solution)/shard_map/ppermute | solution.py:25
  52.3 0.0 collective-permute-done.14
  52.3 0.6 second_image.1
  52.9 0.1 collective-permute-start.16
  53.0 1.2 %collective-permute-done.16 = f32[32,256]{1,0:T(8,128)S(1)} collective-permute-done((f32[32,256]{1,0:T(8,128)S(1)}, f32[32,256]{1,0:T(8,128)S(1)}, u32[]{:S(2)}, u32[]{:S(2)}) %collective-permute-start.16) | collective-permute-done | bytes 32800 | tf_op jit(solution)/shard_map/ppermute | solution.py:438
  54.2 0.9 %collective-permute-start.18 = (f32[32,256]{1,0:T(8,128)S(1)}, f32[32,256]{1,0:T(8,128)S(1)}, u32[]{:S(2)}, u32[]{:S(2)}) collective-permute-start(f32[32,256]{1,0:T(8,128)S(1)} %select_add_fusion.1), channel_id=1, source_target_pairs={{0,6},{1,7},{2,4},{3,5},{4,2},{5,3},{6,0},{7,1},{8,14},{9,15},{10,... | collective-permute-start | bytes 98312 | tf_op jit(solution)/shard_map/ppermute | solution.py:438
  55.1 1.1 %collective-permute-start.19 = (f32[32,256]{1,0:T(8,128)S(1)}, f32[32,256]{1,0:T(8,128)S(1)}, u32[]{:S(2)}, u32[]{:S(2)}) collective-permute-start(f32[32,256]{1,0:T(8,128)S(1)} %select_add_fusion.1), channel_id=1, source_target_pairs={{0,5},{1,4},{2,7},{3,6},{4,1},{5,0},{6,3},{7,2},{8,13},{9,12},{10,... | collective-permute-start | bytes 98312 | tf_op jit(solution)/shard_map/ppermute | solution.py:438
  56.2 1.2 %collective-permute-start.17 = (f32[32,256]{1,0:T(8,128)S(1)}, f32[32,256]{1,0:T(8,128)S(1)}, u32[]{:S(2)}, u32[]{:S(2)}) collective-permute-start(f32[32,256]{1,0:T(8,128)S(1)} %select_add_fusion.1), channel_id=1, source_target_pairs={{0,3},{1,2},{2,1},{3,0},{4,7},{5,6},{6,5},{7,4},{8,11},{9,10},{10,... | collective-permute-start | bytes 98312 | tf_op jit(solution)/shard_map/ppermute | solution.py:438
  57.4 1.8 %collective-permute-done.18 = f32[32,256]{1,0:T(8,128)S(1)} collective-permute-done((f32[32,256]{1,0:T(8,128)S(1)}, f32[32,256]{1,0:T(8,128)S(1)}, u32[]{:S(2)}, u32[]{:S(2)}) %collective-permute-start.18) | collective-permute-done | bytes 32800 | tf_op jit(solution)/shard_map/ppermute | solution.py:438
  59.2 0.0 collective-permute-done.19
  59.2 0.3 collective-permute-done.17
  59.6 2.4 %collective-permute-start.21 = (f32[32,256]{1,0:T(8,128)S(1)}, f32[32,256]{1,0:T(8,128)S(1)}, u32[]{:S(2)}, u32[]{:S(2)}) collective-permute-start(f32[32,256]{1,0:T(8,128)S(1)} %add_add_fusion.3), channel_id=1, source_target_pairs={{0,24},{1,25},{2,26},{3,27},{4,28},{5,29},{6,30},{7,31},{8,16},{9,... | collective-permute-start | bytes 98312 | tf_op jit(solution)/shard_map/ppermute | solution.py:438
  62.0 0.0 collective-permute-start.22
  62.0 1.8 %collective-permute-start.20 = (f32[32,256]{1,0:T(8,128)S(1)}, f32[32,256]{1,0:T(8,128)S(1)}, u32[]{:S(2)}, u32[]{:S(2)}) collective-permute-start(f32[32,256]{1,0:T(8,128)S(1)} %add_add_fusion.3), channel_id=1, source_target_pairs={{0,9},{1,8},{2,11},{3,10},{4,13},{5,12},{6,15},{7,14},{8,1},{9,0},... | collective-permute-start | bytes 98312 | tf_op jit(solution)/shard_map/ppermute | solution.py:438
  63.7 1.9 %collective-permute-done.21 = f32[32,256]{1,0:T(8,128)S(1)} collective-permute-done((f32[32,256]{1,0:T(8,128)S(1)}, f32[32,256]{1,0:T(8,128)S(1)}, u32[]{:S(2)}, u32[]{:S(2)}) %collective-permute-start.21) | collective-permute-done | bytes 32800 | tf_op jit(solution)/shard_map/ppermute | solution.py:438
  65.6 1.1 %collective-permute-done.22 = f32[32,256]{1,0:T(8,128)S(1)} collective-permute-done((f32[32,256]{1,0:T(8,128)S(1)}, f32[32,256]{1,0:T(8,128)S(1)}, u32[]{:S(2)}, u32[]{:S(2)}) %collective-permute-start.22) | collective-permute-done | bytes 32800 | tf_op jit(solution)/shard_map/ppermute | solution.py:438
  66.7 0.2 collective-permute-start.23
  66.9 0.4 next_gram.1
  67.3 0.7 collective-permute-done.23
  68.0 3.9 %second_solve.1 = (bf16[64,2,8,128]{3,2,1,0:T(8,128)(2,1)}, f32[2,64,192]{2,1,0:T(8,128)}, f32[2,64,64]{2,1,0:T(8,128)}) custom-call(f32[64,256]{1,0:T(8,128)S(1)} %pad_maximum_fusion.5.cross, bf16[192,192]{1,0:T(8,128)(2,1)S(1)} %get-tuple-element.60.own_high, bf16[192,192]{1,0:T(8,128)(2,1)S(1)} %get-tuple-element.61.own_low, ...), custom_call_target="tpu_custom_call" | custom-call | bytes 1982464 | tf_op jit(solution)/shard_map/second_solve/pallas_call | solution.py:469
  (30 shorter events, 0.4 us)
Async XLA Ops:
  0.6 1.0 %slice-start = ((bf16[3,64,2,8,128]{4,3,2,1,0:T(8,128)(2,1)}), bf16[1,64,2,8,128]{4,3,2,1,0:T(8,128)(2,1)S(1)}, s32[]{:S(2)}) async-start(bf16[3,64,2,8,128]{4,3,2,1,0:T(8,128)(2,1)} %param.3), calls=%async_computation | async-start | bytes 524288 | tf_op jit(solution)/shard_map/slice | solution.py:512
  1.6 6.8 %copy-start.2 = (bf16[3,64,2,8,128]{4,3,2,1,0:T(8,128)(2,1)S(1)}, bf16[3,64,2,8,128]{4,3,2,1,0:T(8,128)(2,1)}, u32[]{:S(2)}) copy-start(bf16[3,64,2,8,128]{4,3,2,1,0:T(8,128)(2,1)} %param.3) | copy-start | bytes 2359300
  1.7 9.1 %collective-permute-start.1 = (bf16[64,1024]{1,0:T(8,128)(2,1)S(1)}, bf16[64,1024]{1,0:T(8,128)(2,1)S(1)}, u32[]{:S(2)}, u32[]{:S(2)}) collective-permute-start(bf16[64,1024]{1,0:T(8,128)(2,1)S(1)} %slice_select_fusion), channel_id=1, source_target_pairs={{0,4},{4,0},{8,12},{12,8},{16,20},{20,16},{24,28},{28,24},{1,5},{5... | collective-permute-start | bytes 393224 | tf_op jit(solution)/shard_map/ppermute | solution.py:24
  4.8 7.7 %collective-permute-start = (bf16[64,1024]{1,0:T(8,128)(2,1)S(1)}, bf16[64,1024]{1,0:T(8,128)(2,1)S(1)}, u32[]{:S(2)}, u32[]{:S(2)}) collective-permute-start(bf16[64,1024]{1,0:T(8,128)(2,1)S(1)} %cut.2), channel_id=1, source_target_pairs={{4,8},{8,4},{12,16},{16,12},{20,24},{24,20},{0,28},{28,0},{5,9},{9... | collective-permute-start | bytes 393224 | tf_op jit(solution)/shard_map/ppermute | solution.py:25
  8.8 0.7 copy-start
  9.4 0.7 copy-start.1
  12.6 4.4 %collective-permute-start.3 = (bf16[64,512]{1,0:T(8,128)(2,1)S(1)}, bf16[64,512]{1,0:T(8,128)(2,1)S(1)}, u32[]{:S(2)}, u32[]{:S(2)}) collective-permute-start(bf16[64,512]{1,0:T(8,128)(2,1)S(1)} %get-tuple-element.93), channel_id=1, source_target_pairs={{1,2},{2,1},{0,3},{3,0},{5,6},{6,5},{4,7},{7,4},{9,10},{10,9},{8,1... | collective-permute-start | bytes 196616 | tf_op jit(solution)/shard_map/ppermute | solution.py:25
  12.7 4.3 %collective-permute-start.2 = (bf16[64,512]{1,0:T(8,128)(2,1)S(1)}, bf16[64,512]{1,0:T(8,128)(2,1)S(1)}, u32[]{:S(2)}, u32[]{:S(2)}) collective-permute-start(bf16[64,512]{1,0:T(8,128)(2,1)S(1)} %get-tuple-element.94), channel_id=1, source_target_pairs={{0,1},{1,0},{2,3},{3,2},{4,5},{5,4},{6,7},{7,6},{8,9},{9,8},{10,11... | collective-permute-start | bytes 196616 | tf_op jit(solution)/shard_map/ppermute | solution.py:24
  17.6 1.3 %collective-permute-start.4 = (f32[136,128]{1,0:T(8,128)S(1)}, f32[136,128]{1,0:T(8,128)S(1)}, u32[]{:S(2)}, u32[]{:S(2)}) collective-permute-start(f32[136,128]{1,0:T(8,128)S(1)} %slice_select_fusion.2), channel_id=1, source_target_pairs={{0,1},{1,0},{2,3},{3,2},{4,5},{5,4},{6,7},{7,6},{8,9},{9,8},{10,11... | collective-permute-start | bytes 208904 | tf_op jit(solution)/shard_map/ppermute | solution.py:438
  19.0 6.1 %collective-permute-start.6 = (f32[136,128]{1,0:T(8,128)S(1)}, f32[136,128]{1,0:T(8,128)S(1)}, u32[]{:S(2)}, u32[]{:S(2)}) collective-permute-start(f32[136,128]{1,0:T(8,128)S(1)} %select_add_fusion), channel_id=1, source_target_pairs={{0,6},{1,7},{2,4},{3,5},{4,2},{5,3},{6,0},{7,1},{8,14},{9,15},{10,... | collective-permute-start | bytes 208904 | tf_op jit(solution)/shard_map/ppermute | solution.py:438
  19.7 5.4 %collective-permute-start.7 = (f32[136,128]{1,0:T(8,128)S(1)}, f32[136,128]{1,0:T(8,128)S(1)}, u32[]{:S(2)}, u32[]{:S(2)}) collective-permute-start(f32[136,128]{1,0:T(8,128)S(1)} %select_add_fusion), channel_id=1, source_target_pairs={{0,5},{1,4},{2,7},{3,6},{4,1},{5,0},{6,3},{7,2},{8,13},{9,12},{10,... | collective-permute-start | bytes 208904 | tf_op jit(solution)/shard_map/ppermute | solution.py:438
  20.9 4.6 %collective-permute-start.5 = (f32[136,128]{1,0:T(8,128)S(1)}, f32[136,128]{1,0:T(8,128)S(1)}, u32[]{:S(2)}, u32[]{:S(2)}) collective-permute-start(f32[136,128]{1,0:T(8,128)S(1)} %select_add_fusion), channel_id=1, source_target_pairs={{0,3},{1,2},{2,1},{3,0},{4,7},{5,6},{6,5},{7,4},{8,11},{9,10},{10,... | collective-permute-start | bytes 208904 | tf_op jit(solution)/shard_map/ppermute | solution.py:438
  25.5 6.9 %collective-permute-start.9 = (f32[136,128]{1,0:T(8,128)S(1)}, f32[136,128]{1,0:T(8,128)S(1)}, u32[]{:S(2)}, u32[]{:S(2)}) collective-permute-start(f32[136,128]{1,0:T(8,128)S(1)} %add_add_fusion.1), channel_id=1, source_target_pairs={{0,24},{1,25},{2,26},{3,27},{4,28},{5,29},{6,30},{7,31},{8,16},{9,... | collective-permute-start | bytes 208904 | tf_op jit(solution)/shard_map/ppermute | solution.py:438
  28.0 6.7 %collective-permute-start.10 = (f32[136,128]{1,0:T(8,128)S(1)}, f32[136,128]{1,0:T(8,128)S(1)}, u32[]{:S(2)}, u32[]{:S(2)}) collective-permute-start(f32[136,128]{1,0:T(8,128)S(1)} %add_add_fusion.1), channel_id=1, source_target_pairs={{0,17},{1,16},{2,19},{3,18},{4,21},{5,20},{6,23},{7,22},{8,25},{9,... | collective-permute-start | bytes 208904 | tf_op jit(solution)/shard_map/ppermute | solution.py:438
  28.0 6.7 %collective-permute-start.8 = (f32[136,128]{1,0:T(8,128)S(1)}, f32[136,128]{1,0:T(8,128)S(1)}, u32[]{:S(2)}, u32[]{:S(2)}) collective-permute-start(f32[136,128]{1,0:T(8,128)S(1)} %add_add_fusion.1), channel_id=1, source_target_pairs={{0,9},{1,8},{2,11},{3,10},{4,13},{5,12},{6,15},{7,14},{8,1},{9,0},... | collective-permute-start | bytes 208904 | tf_op jit(solution)/shard_map/ppermute | solution.py:438
  34.7 1.3 %collective-permute-start.11 = (f32[136,128]{1,0:T(8,128)S(1)}, f32[136,128]{1,0:T(8,128)S(1)}, u32[]{:S(2)}, u32[]{:S(2)}) collective-permute-start(f32[136,128]{1,0:T(8,128)S(1)} %add_add_fusion), channel_id=1, source_target_pairs={{0,1},{1,0},{2,3},{3,2},{4,5},{5,4},{6,7},{7,6},{8,9},{9,8},{10,11... | collective-permute-start | bytes 208904 | tf_op jit(solution)/shard_map/ppermute | solution.py:438
  39.3 6.8 %collective-permute-start.13 = (bf16[64,1024]{1,0:T(8,128)(2,1)S(1)}, bf16[64,1024]{1,0:T(8,128)(2,1)S(1)}, u32[]{:S(2)}, u32[]{:S(2)}) collective-permute-start(bf16[64,1024]{1,0:T(8,128)(2,1)S(1)} %slice_select_fusion.1), channel_id=1, source_target_pairs={{0,4},{4,0},{8,12},{12,8},{16,20},{20,16},{24,28},{28,24},{1,5},{5... | collective-permute-start | bytes 393224 | tf_op jit(solution)/shard_map/ppermute | solution.py:24
  40.2 8.0 %collective-permute-start.12 = (bf16[64,1024]{1,0:T(8,128)(2,1)S(1)}, bf16[64,1024]{1,0:T(8,128)(2,1)S(1)}, u32[]{:S(2)}, u32[]{:S(2)}) collective-permute-start(bf16[64,1024]{1,0:T(8,128)(2,1)S(1)} %cut.3), channel_id=1, source_target_pairs={{4,8},{8,4},{12,16},{16,12},{20,24},{24,20},{0,28},{28,0},{5,9},{9... | collective-permute-start | bytes 393224 | tf_op jit(solution)/shard_map/ppermute | solution.py:25
  48.3 4.0 %collective-permute-start.15 = (bf16[64,512]{1,0:T(8,128)(2,1)S(1)}, bf16[64,512]{1,0:T(8,128)(2,1)S(1)}, u32[]{:S(2)}, u32[]{:S(2)}) collective-permute-start(bf16[64,512]{1,0:T(8,128)(2,1)S(1)} %get-tuple-element.85), channel_id=1, source_target_pairs={{1,2},{2,1},{0,3},{3,0},{5,6},{6,5},{4,7},{7,4},{9,10},{10,9},{8,1... | collective-permute-start | bytes 196616 | tf_op jit(solution)/shard_map/ppermute | solution.py:25
  48.4 3.9 %collective-permute-start.14 = (bf16[64,512]{1,0:T(8,128)(2,1)S(1)}, bf16[64,512]{1,0:T(8,128)(2,1)S(1)}, u32[]{:S(2)}, u32[]{:S(2)}) collective-permute-start(bf16[64,512]{1,0:T(8,128)(2,1)S(1)} %get-tuple-element.86), channel_id=1, source_target_pairs={{0,1},{1,0},{2,3},{3,2},{4,5},{5,4},{6,7},{7,6},{8,9},{9,8},{10,11... | collective-permute-start | bytes 196616 | tf_op jit(solution)/shard_map/ppermute | solution.py:24
  52.9 1.3 %collective-permute-start.16 = (f32[32,256]{1,0:T(8,128)S(1)}, f32[32,256]{1,0:T(8,128)S(1)}, u32[]{:S(2)}, u32[]{:S(2)}) collective-permute-start(f32[32,256]{1,0:T(8,128)S(1)} %slice_select_fusion.3), channel_id=1, source_target_pairs={{0,1},{1,0},{2,3},{3,2},{4,5},{5,4},{6,7},{7,6},{8,9},{9,8},{10,11... | collective-permute-start | bytes 98312 | tf_op jit(solution)/shard_map/ppermute | solution.py:438
  54.2 5.0 %collective-permute-start.18 = (f32[32,256]{1,0:T(8,128)S(1)}, f32[32,256]{1,0:T(8,128)S(1)}, u32[]{:S(2)}, u32[]{:S(2)}) collective-permute-start(f32[32,256]{1,0:T(8,128)S(1)} %select_add_fusion.1), channel_id=1, source_target_pairs={{0,6},{1,7},{2,4},{3,5},{4,2},{5,3},{6,0},{7,1},{8,14},{9,15},{10,... | collective-permute-start | bytes 98312 | tf_op jit(solution)/shard_map/ppermute | solution.py:438
  55.1 4.1 %collective-permute-start.19 = (f32[32,256]{1,0:T(8,128)S(1)}, f32[32,256]{1,0:T(8,128)S(1)}, u32[]{:S(2)}, u32[]{:S(2)}) collective-permute-start(f32[32,256]{1,0:T(8,128)S(1)} %select_add_fusion.1), channel_id=1, source_target_pairs={{0,5},{1,4},{2,7},{3,6},{4,1},{5,0},{6,3},{7,2},{8,13},{9,12},{10,... | collective-permute-start | bytes 98312 | tf_op jit(solution)/shard_map/ppermute | solution.py:438
  56.2 3.4 %collective-permute-start.17 = (f32[32,256]{1,0:T(8,128)S(1)}, f32[32,256]{1,0:T(8,128)S(1)}, u32[]{:S(2)}, u32[]{:S(2)}) collective-permute-start(f32[32,256]{1,0:T(8,128)S(1)} %select_add_fusion.1), channel_id=1, source_target_pairs={{0,3},{1,2},{2,1},{3,0},{4,7},{5,6},{6,5},{7,4},{8,11},{9,10},{10,... | collective-permute-start | bytes 98312 | tf_op jit(solution)/shard_map/ppermute | solution.py:438
  59.6 6.0 %collective-permute-start.21 = (f32[32,256]{1,0:T(8,128)S(1)}, f32[32,256]{1,0:T(8,128)S(1)}, u32[]{:S(2)}, u32[]{:S(2)}) collective-permute-start(f32[32,256]{1,0:T(8,128)S(1)} %add_add_fusion.3), channel_id=1, source_target_pairs={{0,24},{1,25},{2,26},{3,27},{4,28},{5,29},{6,30},{7,31},{8,16},{9,... | collective-permute-start | bytes 98312 | tf_op jit(solution)/shard_map/ppermute | solution.py:438
  62.0 4.8 %collective-permute-start.22 = (f32[32,256]{1,0:T(8,128)S(1)}, f32[32,256]{1,0:T(8,128)S(1)}, u32[]{:S(2)}, u32[]{:S(2)}) collective-permute-start(f32[32,256]{1,0:T(8,128)S(1)} %add_add_fusion.3), channel_id=1, source_target_pairs={{0,17},{1,16},{2,19},{3,18},{4,21},{5,20},{6,23},{7,22},{8,25},{9,... | collective-permute-start | bytes 98312 | tf_op jit(solution)/shard_map/ppermute | solution.py:438
  62.0 4.8 %collective-permute-start.20 = (f32[32,256]{1,0:T(8,128)S(1)}, f32[32,256]{1,0:T(8,128)S(1)}, u32[]{:S(2)}, u32[]{:S(2)}) collective-permute-start(f32[32,256]{1,0:T(8,128)S(1)} %add_add_fusion.3), channel_id=1, source_target_pairs={{0,9},{1,8},{2,11},{3,10},{4,13},{5,12},{6,15},{7,14},{8,1},{9,0},... | collective-permute-start | bytes 98312 | tf_op jit(solution)/shard_map/ppermute | solution.py:438
  66.7 1.3 %collective-permute-start.23 = (f32[32,256]{1,0:T(8,128)S(1)}, f32[32,256]{1,0:T(8,128)S(1)}, u32[]{:S(2)}, u32[]{:S(2)}) collective-permute-start(f32[32,256]{1,0:T(8,128)S(1)} %add_add_fusion.2), channel_id=1, source_target_pairs={{0,1},{1,0},{2,3},{3,2},{4,5},{5,4},{6,7},{7,6},{8,9},{9,8},{10,11... | collective-permute-start | bytes 98312 | tf_op jit(solution)/shard_map/ppermute | solution.py:438

commit v28 on v26

--- a/solution.py
+++ b/solution.py
@@ -27,8 +27,8 @@
         even = me % 2 == 0
         low, high = jnp.where(even, outer, inner), jnp.where(even, inner, outer)
     else:
-        odd = me % 2 == 1
-        low, high = jnp.where(odd, inner, outer), jnp.where(odd, outer, inner)
+        even = me % 2 == 0
+        low, high = jnp.where(even, outer, inner), jnp.where(even, inner, outer)
     return jnp.where(me == 0, 0, low), jnp.where(me == count - 1, 0, high)
 
 

time: 72.1 us -> 72.2 us (level)
  starting transfers between devices: 28.8 us -> 29.8 us
  waiting for transfers between devices: 27.1 us -> 26.2 us
    ppermute x4, starting transfers between devices: 6.81 us -> 9.78 us  [swaps(): outer = lax.ppermute(far, axis, pairs + [(0, count - 1), (count - 1, 0)])]
    ppermute x4, starting transfers between devices: 6.61 us -> 3.97 us  [swaps(): inner = lax.ppermute(near, axis, [(i, i ^ 1) for i in range(count)])]
    ppermute x4, waiting for transfers between devices: 6.67 us -> 5.88 us  [swaps(): outer = lax.ppermute(far, axis, pairs + [(0, count - 1), (count - 1, 0)])]
  transfers between devices with their start and end apart: 24 -> 24, of which waited for: 17 -> 18; matrix products, arithmetic and copies ran while one was open for 1% -> 0% of each run, Pallas kernels for 6% -> 6%
where the time goes in v28:
time: 72.2 us; the launch traced here: 72 us
  starting transfers between devices  29.8 us (41%)
  waiting for transfers between devices  26.2 us (36%)
  Pallas kernels  12.6 us (17%)
  local copies, waits for them, and re-layouts  2.13 us (3%)
  between operations  0.95 us (1%)
    ppermute x16, waiting for transfers between devices, partner(): return lax.ppermute(part, axes, [(i, i ^ mask) for i in range(count)])  17.5 us
    ppermute x16, starting transfers between devices, partner(): return lax.ppermute(part, axes, [(i, i ^ mask) for i in range(count)])  16.1 us
    pallas_call x8, Pallas kernels, call(): pl.pallas_call(kernel, out_shape=[jax.ShapeDtypeStruct(shape, dtype) for...  11.8 us
    ppermute x4, starting transfers between devices, swaps(): outer = lax.ppermute(far, axis, pairs + [(0, count - 1), (count - 1, 0)])  9.78 us
    ppermute x4, waiting for transfers between devices, swaps(): outer = lax.ppermute(far, axis, pairs + [(0, count - 1), (count - 1, 0)])  5.88 us
    ppermute x4, starting transfers between devices, swaps(): inner = lax.ppermute(near, axis, [(i, i ^ 1) for i in range(count)])  3.97 us
    ppermute x4, waiting for transfers between devices, swaps(): inner = lax.ppermute(near, axis, [(i, i ^ 1) for i in range(count)])  2.76 us
  transfers between devices with their start and end apart: 24, of which 18 were waited for; matrix products, arithmetic and copies ran while one was open for 0% of the time, Pallas kernels for 6%

profile of v28, /device:TPU:0, one launch (start us, length us, event | category | flops | bytes accessed | tf_op | source)
XLA Modules:
  0.0 72.0 jit_solution(10930513215049147671)
XLA Ops:
  0.6 0.0 slice-start
  0.6 0.9 %slice-done = bf16[1,64,2,8,128]{4,3,2,1,0:T(8,128)(2,1)S(1)} async-done(((bf16[3,64,2,8,128]{4,3,2,1,0:T(8,128)(2,1)}), bf16[1,64,2,8,128]{4,3,2,1,0:T(8,128)(2,1)S(1)}, s32[]{:S(2)}) %slice-start) | async-done | bytes 262168 | tf_op jit(solution)/shard_map/slice | solution.py:513
  1.6 0.1 reshape_squeeze.3.block
  1.7 3.0 %collective-permute-start.1 = (bf16[64,1024]{1,0:T(8,128)(2,1)S(1)}, bf16[64,1024]{1,0:T(8,128)(2,1)S(1)}, u32[]{:S(2)}, u32[]{:S(2)}) collective-permute-start(bf16[64,1024]{1,0:T(8,128)(2,1)S(1)} %slice_select_fusion), channel_id=1, source_target_pairs={{0,4},{4,0},{8,12},{12,8},{16,20},{20,16},{24,28},{28,24},{1,5},{5... | collective-permute-start | bytes 393224 | tf_op jit(solution)/shard_map/ppermute | solution.py:24
  4.8 3.6 %collective-permute-start = (bf16[64,1024]{1,0:T(8,128)(2,1)S(1)}, bf16[64,1024]{1,0:T(8,128)(2,1)S(1)}, u32[]{:S(2)}, u32[]{:S(2)}) collective-permute-start(bf16[64,1024]{1,0:T(8,128)(2,1)S(1)} %cut.2), channel_id=1, source_target_pairs={{4,8},{8,4},{12,16},{16,12},{20,24},{24,20},{0,28},{28,0},{5,9},{9... | collective-permute-start | bytes 393224 | tf_op jit(solution)/shard_map/ppermute | solution.py:25
  8.4 0.3 reshape.18.stack
  8.8 0.0 copy-start
  8.8 0.6 stack_gram.1
  9.4 0.0 copy-start.1
  9.4 0.0 copy-done
  9.5 0.6 copy-done.1
  10.1 0.8 %coefficients.1.coef = f32[27,16,128]{2,1,0:T(8,128)S(1)} custom-call(f32[8,27]{1,0:T(8,128)S(1)} %copy-done.1, s32[16,128]{1,0:T(8,128)S(1)} %bitcast.7), custom_call_target="tpu_custom_call" | custom-call | tf_op jit(solution)/shard_map/coefficients/pallas_call | solution.py:101
  10.9 0.0 collective-permute-done.1
  10.9 1.6 %collective-permute-done = bf16[64,1024]{1,0:T(8,128)(2,1)S(1)} collective-permute-done((bf16[64,1024]{1,0:T(8,128)(2,1)S(1)}, bf16[64,1024]{1,0:T(8,128)(2,1)S(1)}, u32[]{:S(2)}, u32[]{:S(2)}) %collective-permute-start) | collective-permute-done | bytes 131104 | tf_op jit(solution)/shard_map/ppermute | solution.py:25
  12.6 0.1 collective-permute-start.3
  12.7 1.6 %collective-permute-start.2 = (bf16[64,512]{1,0:T(8,128)(2,1)S(1)}, bf16[64,512]{1,0:T(8,128)(2,1)S(1)}, u32[]{:S(2)}, u32[]{:S(2)}) collective-permute-start(bf16[64,512]{1,0:T(8,128)(2,1)S(1)} %get-tuple-element.94), channel_id=1, source_target_pairs={{1,2},{2,1},{0,3},{3,0},{5,6},{6,5},{4,7},{7,4},{9,10},{10,9},{8,1... | collective-permute-start | bytes 196616 | tf_op jit(solution)/shard_map/ppermute | solution.py:25
  14.3 1.3 %middle_image.2 = (bf16[64,1536]{1,0:T(8,128)(2,1)S(1)}, f32[64,512]{1,0:T(8,128)S(1)}, f32[64,256]{1,0:T(8,128)S(1)}) custom-call(f32[27,16,128]{2,1,0:T(8,128)S(1)} %coefficients.1.coef, bf16[192,2048]{1,0:T(8,128)(2,1)S(1)} %reshape.18.stack, bf16[64,2048]{1,0:T(8,128)(2,1)S(1)} %reshape_squeeze.3.block, bf16[64,1024]{1,0:T(8,128)(2,1)S(1)} %get-tuple-element.44.xlo, ...), custom_call_target="tpu_custom_call" | custom-call | flops 7077888 | bytes 1925120 | tf_op jit(solution)/shard_map/middle_image/pallas_call | solution.py:470
  15.6 0.0 collective-permute-done.3
  15.6 1.0 %collective-permute-done.2 = bf16[64,512]{1,0:T(8,128)(2,1)S(1)} collective-permute-done((bf16[64,512]{1,0:T(8,128)(2,1)S(1)}, bf16[64,512]{1,0:T(8,128)(2,1)S(1)}, u32[]{:S(2)}, u32[]{:S(2)}) %collective-permute-start.2) | collective-permute-done | bytes 65568 | tf_op jit(solution)/shard_map/ppermute | solution.py:25
  16.6 0.6 first_image.1
  17.2 0.5 collective-permute-start.4
  17.6 0.9 %collective-permute-done.4 = f32[136,128]{1,0:T(8,128)S(1)} collective-permute-done((f32[136,128]{1,0:T(8,128)S(1)}, f32[136,128]{1,0:T(8,128)S(1)}, u32[]{:S(2)}, u32[]{:S(2)}) %collective-permute-start.4) | collective-permute-done | bytes 69664 | tf_op jit(solution)/shard_map/ppermute | solution.py:439
  18.6 1.3 %collective-permute-start.6 = (f32[136,128]{1,0:T(8,128)S(1)}, f32[136,128]{1,0:T(8,128)S(1)}, u32[]{:S(2)}, u32[]{:S(2)}) collective-permute-start(f32[136,128]{1,0:T(8,128)S(1)} %select_add_fusion), channel_id=1, source_target_pairs={{0,6},{1,7},{2,4},{3,5},{4,2},{5,3},{6,0},{7,1},{8,14},{9,15},{10,... | collective-permute-start | bytes 208904 | tf_op jit(solution)/shard_map/ppermute | solution.py:439
  19.9 1.4 %collective-permute-start.7 = (f32[136,128]{1,0:T(8,128)S(1)}, f32[136,128]{1,0:T(8,128)S(1)}, u32[]{:S(2)}, u32[]{:S(2)}) collective-permute-start(f32[136,128]{1,0:T(8,128)S(1)} %select_add_fusion), channel_id=1, source_target_pairs={{0,5},{1,4},{2,7},{3,6},{4,1},{5,0},{6,3},{7,2},{8,13},{9,12},{10,... | collective-permute-start | bytes 208904 | tf_op jit(solution)/shard_map/ppermute | solution.py:439
  21.3 0.5 collective-permute-start.5
  21.8 2.7 %collective-permute-done.6 = f32[136,128]{1,0:T(8,128)S(1)} collective-permute-done((f32[136,128]{1,0:T(8,128)S(1)}, f32[136,128]{1,0:T(8,128)S(1)}, u32[]{:S(2)}, u32[]{:S(2)}) %collective-permute-start.6) | collective-permute-done | bytes 69664 | tf_op jit(solution)/shard_map/ppermute | solution.py:439
  24.5 0.4 collective-permute-done.7
  25.0 0.5 collective-permute-done.5
  25.5 2.6 %collective-permute-start.9 = (f32[136,128]{1,0:T(8,128)S(1)}, f32[136,128]{1,0:T(8,128)S(1)}, u32[]{:S(2)}, u32[]{:S(2)}) collective-permute-start(f32[136,128]{1,0:T(8,128)S(1)} %add_add_fusion.1), channel_id=1, source_target_pairs={{0,24},{1,25},{2,26},{3,27},{4,28},{5,29},{6,30},{7,31},{8,16},{9,... | collective-permute-start | bytes 208904 | tf_op jit(solution)/shard_map/ppermute | solution.py:439
  28.0 0.0 collective-permute-start.10
  28.0 1.6 %collective-permute-start.8 = (f32[136,128]{1,0:T(8,128)S(1)}, f32[136,128]{1,0:T(8,128)S(1)}, u32[]{:S(2)}, u32[]{:S(2)}) collective-permute-start(f32[136,128]{1,0:T(8,128)S(1)} %add_add_fusion.1), channel_id=1, source_target_pairs={{0,9},{1,8},{2,11},{3,10},{4,13},{5,12},{6,15},{7,14},{8,1},{9,0},... | collective-permute-start | bytes 208904 | tf_op jit(solution)/shard_map/ppermute | solution.py:439
  29.7 2.7 %collective-permute-done.9 = f32[136,128]{1,0:T(8,128)S(1)} collective-permute-done((f32[136,128]{1,0:T(8,128)S(1)}, f32[136,128]{1,0:T(8,128)S(1)}, u32[]{:S(2)}, u32[]{:S(2)}) %collective-permute-start.9) | collective-permute-done | bytes 69664 | tf_op jit(solution)/shard_map/ppermute | solution.py:439
  32.4 2.3 %collective-permute-done.10 = f32[136,128]{1,0:T(8,128)S(1)} collective-permute-done((f32[136,128]{1,0:T(8,128)S(1)}, f32[136,128]{1,0:T(8,128)S(1)}, u32[]{:S(2)}, u32[]{:S(2)}) %collective-permute-start.10) | collective-permute-done | bytes 69664 | tf_op jit(solution)/shard_map/ppermute | solution.py:439
  34.7 0.0 collective-permute-done.8
  34.7 0.2 collective-permute-start.11
  34.9 1.2 %collective-permute-done.11 = f32[136,128]{1,0:T(8,128)S(1)} collective-permute-done((f32[136,128]{1,0:T(8,128)S(1)}, f32[136,128]{1,0:T(8,128)S(1)}, u32[]{:S(2)}, u32[]{:S(2)}) %collective-permute-start.11) | collective-permute-done | bytes 69664 | tf_op jit(solution)/shard_map/ppermute | solution.py:439
  36.1 3.2 %first_solve.1 = (bf16[64,2048]{1,0:T(8,128)(2,1)S(1)}, f32[64,192]{1,0:T(8,128)S(1)}, f32[64,64]{1,0:T(8,128)S(1)}, f32[64,192]{1,0:T(8,128)S(1)}, f32[64,64]{1,0:T(8,128)S(1)}, /*index=5*/bf16[64,64]{1,0:T(8,128)(2,1)S(1)}) custom-call(f32[272,128]{1,0:T(8,128)S(1)} %pad_maximum_fusion.cross, bf16[192,2048]{1,0:T(8,128)(2,1)S(1)} %reshape.18.stack, ...), custom_call_target="tpu_custom_call" | custom-call | bytes 1589248 | tf_op jit(solution)/shard_map/first_solve/pallas_call | solution.py:470
  39.3 0.8 %collective-permute-start.13 = (bf16[64,1024]{1,0:T(8,128)(2,1)S(1)}, bf16[64,1024]{1,0:T(8,128)(2,1)S(1)}, u32[]{:S(2)}, u32[]{:S(2)}) collective-permute-start(bf16[64,1024]{1,0:T(8,128)(2,1)S(1)} %slice_select_fusion.1), channel_id=1, source_target_pairs={{0,4},{4,0},{8,12},{12,8},{16,20},{20,16},{24,28},{28,24},{1,5},{5... | collective-permute-start | bytes 393224 | tf_op jit(solution)/shard_map/ppermute | solution.py:24
  40.2 3.1 %collective-permute-start.12 = (bf16[64,1024]{1,0:T(8,128)(2,1)S(1)}, bf16[64,1024]{1,0:T(8,128)(2,1)S(1)}, u32[]{:S(2)}, u32[]{:S(2)}) collective-permute-start(bf16[64,1024]{1,0:T(8,128)(2,1)S(1)} %cut.3), channel_id=1, source_target_pairs={{4,8},{8,4},{12,16},{16,12},{20,24},{24,20},{0,28},{28,0},{5,9},{9... | collective-permute-start | bytes 393224 | tf_op jit(solution)/shard_map/ppermute | solution.py:25
  43.3 2.8 %collective-permute-done.13 = bf16[64,1024]{1,0:T(8,128)(2,1)S(1)} collective-permute-done((bf16[64,1024]{1,0:T(8,128)(2,1)S(1)}, bf16[64,1024]{1,0:T(8,128)(2,1)S(1)}, u32[]{:S(2)}, u32[]{:S(2)}) %collective-permute-start.13) | collective-permute-done | bytes 131104 | tf_op jit(solution)/shard_map/ppermute | solution.py:24
  46.1 2.1 %collective-permute-done.12 = bf16[64,1024]{1,0:T(8,128)(2,1)S(1)} collective-permute-done((bf16[64,1024]{1,0:T(8,128)(2,1)S(1)}, bf16[64,1024]{1,0:T(8,128)(2,1)S(1)}, u32[]{:S(2)}, u32[]{:S(2)}) %collective-permute-start.12) | collective-permute-done | bytes 131104 | tf_op jit(solution)/shard_map/ppermute | solution.py:25
  48.2 0.1 collective-permute-start.15
  48.3 1.4 %collective-permute-start.14 = (bf16[64,512]{1,0:T(8,128)(2,1)S(1)}, bf16[64,512]{1,0:T(8,128)(2,1)S(1)}, u32[]{:S(2)}, u32[]{:S(2)}) collective-permute-start(bf16[64,512]{1,0:T(8,128)(2,1)S(1)} %get-tuple-element.86), channel_id=1, source_target_pairs={{1,2},{2,1},{0,3},{3,0},{5,6},{6,5},{4,7},{7,4},{9,10},{10,9},{8,1... | collective-permute-start | bytes 196616 | tf_op jit(solution)/shard_map/ppermute | solution.py:25
  49.7 1.3 %middle_image.3 = (bf16[64,1536]{1,0:T(8,128)(2,1)S(1)}, f32[64,512]{1,0:T(8,128)S(1)}, f32[64,256]{1,0:T(8,128)S(1)}) custom-call(f32[27,16,128]{2,1,0:T(8,128)S(1)} %coefficients.1.coef, bf16[192,2048]{1,0:T(8,128)(2,1)S(1)} %reshape.18.stack, bf16[64,2048]{1,0:T(8,128)(2,1)S(1)} %get-tuple-element.51.block.last, ...), custom_call_target="tpu_custom_call" | custom-call | flops 7077888 | bytes 1925120 | tf_op jit(solution)/shard_map/middle_image/pallas_call | solution.py:470
  51.0 0.0 collective-permute-done.15
  51.0 1.2 %collective-permute-done.14 = bf16[64,512]{1,0:T(8,128)(2,1)S(1)} collective-permute-done((bf16[64,512]{1,0:T(8,128)(2,1)S(1)}, bf16[64,512]{1,0:T(8,128)(2,1)S(1)}, u32[]{:S(2)}, u32[]{:S(2)}) %collective-permute-start.14) | collective-permute-done | bytes 65568 | tf_op jit(solution)/shard_map/ppermute | solution.py:25
  52.2 0.6 second_image.1
  52.8 0.5 collective-permute-start.16
  53.3 0.9 %collective-permute-done.16 = f32[32,256]{1,0:T(8,128)S(1)} collective-permute-done((f32[32,256]{1,0:T(8,128)S(1)}, f32[32,256]{1,0:T(8,128)S(1)}, u32[]{:S(2)}, u32[]{:S(2)}) %collective-permute-start.16) | collective-permute-done | bytes 32800 | tf_op jit(solution)/shard_map/ppermute | solution.py:439
  54.2 1.1 %collective-permute-start.18 = (f32[32,256]{1,0:T(8,128)S(1)}, f32[32,256]{1,0:T(8,128)S(1)}, u32[]{:S(2)}, u32[]{:S(2)}) collective-permute-start(f32[32,256]{1,0:T(8,128)S(1)} %select_add_fusion.1), channel_id=1, source_target_pairs={{0,6},{1,7},{2,4},{3,5},{4,2},{5,3},{6,0},{7,1},{8,14},{9,15},{10,... | collective-permute-start | bytes 98312 | tf_op jit(solution)/shard_map/ppermute | solution.py:439
  55.3 1.3 %collective-permute-start.19 = (f32[32,256]{1,0:T(8,128)S(1)}, f32[32,256]{1,0:T(8,128)S(1)}, u32[]{:S(2)}, u32[]{:S(2)}) collective-permute-start(f32[32,256]{1,0:T(8,128)S(1)} %select_add_fusion.1), channel_id=1, source_target_pairs={{0,5},{1,4},{2,7},{3,6},{4,1},{5,0},{6,3},{7,2},{8,13},{9,12},{10,... | collective-permute-start | bytes 98312 | tf_op jit(solution)/shard_map/ppermute | solution.py:439
  56.6 0.8 %collective-permute-start.17 = (f32[32,256]{1,0:T(8,128)S(1)}, f32[32,256]{1,0:T(8,128)S(1)}, u32[]{:S(2)}, u32[]{:S(2)}) collective-permute-start(f32[32,256]{1,0:T(8,128)S(1)} %select_add_fusion.1), channel_id=1, source_target_pairs={{0,3},{1,2},{2,1},{3,0},{4,7},{5,6},{6,5},{7,4},{8,11},{9,10},{10,... | collective-permute-start | bytes 98312 | tf_op jit(solution)/shard_map/ppermute | solution.py:439
  57.4 1.8 %collective-permute-done.18 = f32[32,256]{1,0:T(8,128)S(1)} collective-permute-done((f32[32,256]{1,0:T(8,128)S(1)}, f32[32,256]{1,0:T(8,128)S(1)}, u32[]{:S(2)}, u32[]{:S(2)}) %collective-permute-start.18) | collective-permute-done | bytes 32800 | tf_op jit(solution)/shard_map/ppermute | solution.py:439
  59.1 0.0 collective-permute-done.19
  59.1 0.8 %collective-permute-done.17 = f32[32,256]{1,0:T(8,128)S(1)} collective-permute-done((f32[32,256]{1,0:T(8,128)S(1)}, f32[32,256]{1,0:T(8,128)S(1)}, u32[]{:S(2)}, u32[]{:S(2)}) %collective-permute-start.17) | collective-permute-done | bytes 32800 | tf_op jit(solution)/shard_map/ppermute | solution.py:439
  59.9 2.3 %collective-permute-start.21 = (f32[32,256]{1,0:T(8,128)S(1)}, f32[32,256]{1,0:T(8,128)S(1)}, u32[]{:S(2)}, u32[]{:S(2)}) collective-permute-start(f32[32,256]{1,0:T(8,128)S(1)} %add_add_fusion.3), channel_id=1, source_target_pairs={{0,24},{1,25},{2,26},{3,27},{4,28},{5,29},{6,30},{7,31},{8,16},{9,... | collective-permute-start | bytes 98312 | tf_op jit(solution)/shard_map/ppermute | solution.py:439
  62.2 0.0 collective-permute-start.22
  62.2 1.9 %collective-permute-start.20 = (f32[32,256]{1,0:T(8,128)S(1)}, f32[32,256]{1,0:T(8,128)S(1)}, u32[]{:S(2)}, u32[]{:S(2)}) collective-permute-start(f32[32,256]{1,0:T(8,128)S(1)} %add_add_fusion.3), channel_id=1, source_target_pairs={{0,9},{1,8},{2,11},{3,10},{4,13},{5,12},{6,15},{7,14},{8,1},{9,0},... | collective-permute-start | bytes 98312 | tf_op jit(solution)/shard_map/ppermute | solution.py:439
  64.1 1.8 %collective-permute-done.21 = f32[32,256]{1,0:T(8,128)S(1)} collective-permute-done((f32[32,256]{1,0:T(8,128)S(1)}, f32[32,256]{1,0:T(8,128)S(1)}, u32[]{:S(2)}, u32[]{:S(2)}) %collective-permute-start.21) | collective-permute-done | bytes 32800 | tf_op jit(solution)/shard_map/ppermute | solution.py:439
  65.9 0.9 %collective-permute-done.22 = f32[32,256]{1,0:T(8,128)S(1)} collective-permute-done((f32[32,256]{1,0:T(8,128)S(1)}, f32[32,256]{1,0:T(8,128)S(1)}, u32[]{:S(2)}, u32[]{:S(2)}) %collective-permute-start.22) | collective-permute-done | bytes 32800 | tf_op jit(solution)/shard_map/ppermute | solution.py:439
  66.8 0.2 collective-permute-start.23
  67.0 0.4 next_gram.1
  67.4 0.7 collective-permute-done.23
  68.1 3.9 %second_solve.1 = (bf16[64,2,8,128]{3,2,1,0:T(8,128)(2,1)}, f32[2,64,192]{2,1,0:T(8,128)}, f32[2,64,64]{2,1,0:T(8,128)}) custom-call(f32[64,256]{1,0:T(8,128)S(1)} %pad_maximum_fusion.5.cross, bf16[192,192]{1,0:T(8,128)(2,1)S(1)} %get-tuple-element.60.own_high, bf16[192,192]{1,0:T(8,128)(2,1)S(1)} %get-tuple-element.61.own_low, ...), custom_call_target="tpu_custom_call" | custom-call | bytes 1982464 | tf_op jit(solution)/shard_map/second_solve/pallas_call | solution.py:470
  (30 shorter events, 0.4 us)
Async XLA Ops:
  0.6 1.0 %slice-start = ((bf16[3,64,2,8,128]{4,3,2,1,0:T(8,128)(2,1)}), bf16[1,64,2,8,128]{4,3,2,1,0:T(8,128)(2,1)S(1)}, s32[]{:S(2)}) async-start(bf16[3,64,2,8,128]{4,3,2,1,0:T(8,128)(2,1)} %param.3), calls=%async_computation | async-start | bytes 524288 | tf_op jit(solution)/shard_map/slice | solution.py:513
  1.6 6.8 %copy-start.2 = (bf16[3,64,2,8,128]{4,3,2,1,0:T(8,128)(2,1)S(1)}, bf16[3,64,2,8,128]{4,3,2,1,0:T(8,128)(2,1)}, u32[]{:S(2)}) copy-start(bf16[3,64,2,8,128]{4,3,2,1,0:T(8,128)(2,1)} %param.3) | copy-start | bytes 2359300
  1.7 9.1 %collective-permute-start.1 = (bf16[64,1024]{1,0:T(8,128)(2,1)S(1)}, bf16[64,1024]{1,0:T(8,128)(2,1)S(1)}, u32[]{:S(2)}, u32[]{:S(2)}) collective-permute-start(bf16[64,1024]{1,0:T(8,128)(2,1)S(1)} %slice_select_fusion), channel_id=1, source_target_pairs={{0,4},{4,0},{8,12},{12,8},{16,20},{20,16},{24,28},{28,24},{1,5},{5... | collective-permute-start | bytes 393224 | tf_op jit(solution)/shard_map/ppermute | solution.py:24
  4.8 7.7 %collective-permute-start = (bf16[64,1024]{1,0:T(8,128)(2,1)S(1)}, bf16[64,1024]{1,0:T(8,128)(2,1)S(1)}, u32[]{:S(2)}, u32[]{:S(2)}) collective-permute-start(bf16[64,1024]{1,0:T(8,128)(2,1)S(1)} %cut.2), channel_id=1, source_target_pairs={{4,8},{8,4},{12,16},{16,12},{20,24},{24,20},{0,28},{28,0},{5,9},{9... | collective-permute-start | bytes 393224 | tf_op jit(solution)/shard_map/ppermute | solution.py:25
  8.8 0.7 copy-start
  9.4 0.7 copy-start.1
  12.6 3.0 %collective-permute-start.3 = (bf16[64,512]{1,0:T(8,128)(2,1)S(1)}, bf16[64,512]{1,0:T(8,128)(2,1)S(1)}, u32[]{:S(2)}, u32[]{:S(2)}) collective-permute-start(bf16[64,512]{1,0:T(8,128)(2,1)S(1)} %get-tuple-element.93), channel_id=1, source_target_pairs={{0,1},{1,0},{2,3},{3,2},{4,5},{5,4},{6,7},{7,6},{8,9},{9,8},{10,11... | collective-permute-start | bytes 196616 | tf_op jit(solution)/shard_map/ppermute | solution.py:24
  12.7 3.9 %collective-permute-start.2 = (bf16[64,512]{1,0:T(8,128)(2,1)S(1)}, bf16[64,512]{1,0:T(8,128)(2,1)S(1)}, u32[]{:S(2)}, u32[]{:S(2)}) collective-permute-start(bf16[64,512]{1,0:T(8,128)(2,1)S(1)} %get-tuple-element.94), channel_id=1, source_target_pairs={{1,2},{2,1},{0,3},{3,0},{5,6},{6,5},{4,7},{7,4},{9,10},{10,9},{8,1... | collective-permute-start | bytes 196616 | tf_op jit(solution)/shard_map/ppermute | solution.py:25
  17.2 1.4 %collective-permute-start.4 = (f32[136,128]{1,0:T(8,128)S(1)}, f32[136,128]{1,0:T(8,128)S(1)}, u32[]{:S(2)}, u32[]{:S(2)}) collective-permute-start(f32[136,128]{1,0:T(8,128)S(1)} %slice_select_fusion.2), channel_id=1, source_target_pairs={{0,1},{1,0},{2,3},{3,2},{4,5},{5,4},{6,7},{7,6},{8,9},{9,8},{10,11... | collective-permute-start | bytes 208904 | tf_op jit(solution)/shard_map/ppermute | solution.py:439
  18.6 6.0 %collective-permute-start.6 = (f32[136,128]{1,0:T(8,128)S(1)}, f32[136,128]{1,0:T(8,128)S(1)}, u32[]{:S(2)}, u32[]{:S(2)}) collective-permute-start(f32[136,128]{1,0:T(8,128)S(1)} %select_add_fusion), channel_id=1, source_target_pairs={{0,6},{1,7},{2,4},{3,5},{4,2},{5,3},{6,0},{7,1},{8,14},{9,15},{10,... | collective-permute-start | bytes 208904 | tf_op jit(solution)/shard_map/ppermute | solution.py:439
  19.9 5.1 %collective-permute-start.7 = (f32[136,128]{1,0:T(8,128)S(1)}, f32[136,128]{1,0:T(8,128)S(1)}, u32[]{:S(2)}, u32[]{:S(2)}) collective-permute-start(f32[136,128]{1,0:T(8,128)S(1)} %select_add_fusion), channel_id=1, source_target_pairs={{0,5},{1,4},{2,7},{3,6},{4,1},{5,0},{6,3},{7,2},{8,13},{9,12},{10,... | collective-permute-start | bytes 208904 | tf_op jit(solution)/shard_map/ppermute | solution.py:439
  21.3 4.2 %collective-permute-start.5 = (f32[136,128]{1,0:T(8,128)S(1)}, f32[136,128]{1,0:T(8,128)S(1)}, u32[]{:S(2)}, u32[]{:S(2)}) collective-permute-start(f32[136,128]{1,0:T(8,128)S(1)} %select_add_fusion), channel_id=1, source_target_pairs={{0,3},{1,2},{2,1},{3,0},{4,7},{5,6},{6,5},{7,4},{8,11},{9,10},{10,... | collective-permute-start | bytes 208904 | tf_op jit(solution)/shard_map/ppermute | solution.py:439
  25.5 6.9 %collective-permute-start.9 = (f32[136,128]{1,0:T(8,128)S(1)}, f32[136,128]{1,0:T(8,128)S(1)}, u32[]{:S(2)}, u32[]{:S(2)}) collective-permute-start(f32[136,128]{1,0:T(8,128)S(1)} %add_add_fusion.1), channel_id=1, source_target_pairs={{0,24},{1,25},{2,26},{3,27},{4,28},{5,29},{6,30},{7,31},{8,16},{9,... | collective-permute-start | bytes 208904 | tf_op jit(solution)/shard_map/ppermute | solution.py:439
  28.0 6.6 %collective-permute-start.10 = (f32[136,128]{1,0:T(8,128)S(1)}, f32[136,128]{1,0:T(8,128)S(1)}, u32[]{:S(2)}, u32[]{:S(2)}) collective-permute-start(f32[136,128]{1,0:T(8,128)S(1)} %add_add_fusion.1), channel_id=1, source_target_pairs={{0,17},{1,16},{2,19},{3,18},{4,21},{5,20},{6,23},{7,22},{8,25},{9,... | collective-permute-start | bytes 208904 | tf_op jit(solution)/shard_map/ppermute | solution.py:439
  28.0 6.6 %collective-permute-start.8 = (f32[136,128]{1,0:T(8,128)S(1)}, f32[136,128]{1,0:T(8,128)S(1)}, u32[]{:S(2)}, u32[]{:S(2)}) collective-permute-start(f32[136,128]{1,0:T(8,128)S(1)} %add_add_fusion.1), channel_id=1, source_target_pairs={{0,9},{1,8},{2,11},{3,10},{4,13},{5,12},{6,15},{7,14},{8,1},{9,0},... | collective-permute-start | bytes 208904 | tf_op jit(solution)/shard_map/ppermute | solution.py:439
  34.7 1.3 %collective-permute-start.11 = (f32[136,128]{1,0:T(8,128)S(1)}, f32[136,128]{1,0:T(8,128)S(1)}, u32[]{:S(2)}, u32[]{:S(2)}) collective-permute-start(f32[136,128]{1,0:T(8,128)S(1)} %add_add_fusion), channel_id=1, source_target_pairs={{0,1},{1,0},{2,3},{3,2},{4,5},{5,4},{6,7},{7,6},{8,9},{9,8},{10,11... | collective-permute-start | bytes 208904 | tf_op jit(solution)/shard_map/ppermute | solution.py:439
  39.3 6.7 %collective-permute-start.13 = (bf16[64,1024]{1,0:T(8,128)(2,1)S(1)}, bf16[64,1024]{1,0:T(8,128)(2,1)S(1)}, u32[]{:S(2)}, u32[]{:S(2)}) collective-permute-start(bf16[64,1024]{1,0:T(8,128)(2,1)S(1)} %slice_select_fusion.1), channel_id=1, source_target_pairs={{0,4},{4,0},{8,12},{12,8},{16,20},{20,16},{24,28},{28,24},{1,5},{5... | collective-permute-start | bytes 393224 | tf_op jit(solution)/shard_map/ppermute | solution.py:24
  40.2 8.0 %collective-permute-start.12 = (bf16[64,1024]{1,0:T(8,128)(2,1)S(1)}, bf16[64,1024]{1,0:T(8,128)(2,1)S(1)}, u32[]{:S(2)}, u32[]{:S(2)}) collective-permute-start(bf16[64,1024]{1,0:T(8,128)(2,1)S(1)} %cut.3), channel_id=1, source_target_pairs={{4,8},{8,4},{12,16},{16,12},{20,24},{24,20},{0,28},{28,0},{5,9},{9... | collective-permute-start | bytes 393224 | tf_op jit(solution)/shard_map/ppermute | solution.py:25
  48.2 2.7 %collective-permute-start.15 = (bf16[64,512]{1,0:T(8,128)(2,1)S(1)}, bf16[64,512]{1,0:T(8,128)(2,1)S(1)}, u32[]{:S(2)}, u32[]{:S(2)}) collective-permute-start(bf16[64,512]{1,0:T(8,128)(2,1)S(1)} %get-tuple-element.85), channel_id=1, source_target_pairs={{0,1},{1,0},{2,3},{3,2},{4,5},{5,4},{6,7},{7,6},{8,9},{9,8},{10,11... | collective-permute-start | bytes 196616 | tf_op jit(solution)/shard_map/ppermute | solution.py:24
  48.3 3.9 %collective-permute-start.14 = (bf16[64,512]{1,0:T(8,128)(2,1)S(1)}, bf16[64,512]{1,0:T(8,128)(2,1)S(1)}, u32[]{:S(2)}, u32[]{:S(2)}) collective-permute-start(bf16[64,512]{1,0:T(8,128)(2,1)S(1)} %get-tuple-element.86), channel_id=1, source_target_pairs={{1,2},{2,1},{0,3},{3,0},{5,6},{6,5},{4,7},{7,4},{9,10},{10,9},{8,1... | collective-permute-start | bytes 196616 | tf_op jit(solution)/shard_map/ppermute | solution.py:25
  52.8 1.3 %collective-permute-start.16 = (f32[32,256]{1,0:T(8,128)S(1)}, f32[32,256]{1,0:T(8,128)S(1)}, u32[]{:S(2)}, u32[]{:S(2)}) collective-permute-start(f32[32,256]{1,0:T(8,128)S(1)} %slice_select_fusion.3), channel_id=1, source_target_pairs={{0,1},{1,0},{2,3},{3,2},{4,5},{5,4},{6,7},{7,6},{8,9},{9,8},{10,11... | collective-permute-start | bytes 98312 | tf_op jit(solution)/shard_map/ppermute | solution.py:439
  54.2 5.0 %collective-permute-start.18 = (f32[32,256]{1,0:T(8,128)S(1)}, f32[32,256]{1,0:T(8,128)S(1)}, u32[]{:S(2)}, u32[]{:S(2)}) collective-permute-start(f32[32,256]{1,0:T(8,128)S(1)} %select_add_fusion.1), channel_id=1, source_target_pairs={{0,6},{1,7},{2,4},{3,5},{4,2},{5,3},{6,0},{7,1},{8,14},{9,15},{10,... | collective-permute-start | bytes 98312 | tf_op jit(solution)/shard_map/ppermute | solution.py:439
  55.3 3.9 %collective-permute-start.19 = (f32[32,256]{1,0:T(8,128)S(1)}, f32[32,256]{1,0:T(8,128)S(1)}, u32[]{:S(2)}, u32[]{:S(2)}) collective-permute-start(f32[32,256]{1,0:T(8,128)S(1)} %select_add_fusion.1), channel_id=1, source_target_pairs={{0,5},{1,4},{2,7},{3,6},{4,1},{5,0},{6,3},{7,2},{8,13},{9,12},{10,... | collective-permute-start | bytes 98312 | tf_op jit(solution)/shard_map/ppermute | solution.py:439
  56.6 3.3 %collective-permute-start.17 = (f32[32,256]{1,0:T(8,128)S(1)}, f32[32,256]{1,0:T(8,128)S(1)}, u32[]{:S(2)}, u32[]{:S(2)}) collective-permute-start(f32[32,256]{1,0:T(8,128)S(1)} %select_add_fusion.1), channel_id=1, source_target_pairs={{0,3},{1,2},{2,1},{3,0},{4,7},{5,6},{6,5},{7,4},{8,11},{9,10},{10,... | collective-permute-start | bytes 98312 | tf_op jit(solution)/shard_map/ppermute | solution.py:439
  59.9 6.0 %collective-permute-start.21 = (f32[32,256]{1,0:T(8,128)S(1)}, f32[32,256]{1,0:T(8,128)S(1)}, u32[]{:S(2)}, u32[]{:S(2)}) collective-permute-start(f32[32,256]{1,0:T(8,128)S(1)} %add_add_fusion.3), channel_id=1, source_target_pairs={{0,24},{1,25},{2,26},{3,27},{4,28},{5,29},{6,30},{7,31},{8,16},{9,... | collective-permute-start | bytes 98312 | tf_op jit(solution)/shard_map/ppermute | solution.py:439
  62.2 4.6 %collective-permute-start.22 = (f32[32,256]{1,0:T(8,128)S(1)}, f32[32,256]{1,0:T(8,128)S(1)}, u32[]{:S(2)}, u32[]{:S(2)}) collective-permute-start(f32[32,256]{1,0:T(8,128)S(1)} %add_add_fusion.3), channel_id=1, source_target_pairs={{0,17},{1,16},{2,19},{3,18},{4,21},{5,20},{6,23},{7,22},{8,25},{9,... | collective-permute-start | bytes 98312 | tf_op jit(solution)/shard_map/ppermute | solution.py:439
  62.2 4.6 %collective-permute-start.20 = (f32[32,256]{1,0:T(8,128)S(1)}, f32[32,256]{1,0:T(8,128)S(1)}, u32[]{:S(2)}, u32[]{:S(2)}) collective-permute-start(f32[32,256]{1,0:T(8,128)S(1)} %add_add_fusion.3), channel_id=1, source_target_pairs={{0,9},{1,8},{2,11},{3,10},{4,13},{5,12},{6,15},{7,14},{8,1},{9,0},... | collective-permute-start | bytes 98312 | tf_op jit(solution)/shard_map/ppermute | solution.py:439
  66.8 1.3 %collective-permute-start.23 = (f32[32,256]{1,0:T(8,128)S(1)}, f32[32,256]{1,0:T(8,128)S(1)}, u32[]{:S(2)}, u32[]{:S(2)}) collective-permute-start(f32[32,256]{1,0:T(8,128)S(1)} %add_add_fusion.2), channel_id=1, source_target_pairs={{0,1},{1,0},{2,3},{3,2},{4,5},{5,4},{6,7},{7,6},{8,9},{9,8},{10,11... | collective-permute-start | bytes 98312 | tf_op jit(solution)/shard_map/ppermute | solution.py:439
